TPU v7x, 32 devices: a whole 2x2x4 slice. The times are simulated.
32 devices in a mesh: rep: 2 (over x), tp: 16 (over z, y, core).
Axes of the slice: x: 2, y: 2, z: 4, core: 2. Of those that a mesh axis runs over, the one named last changes fastest.
Arguments:
- tokens: bfloat16 [512, 8192], P(('rep', 'tp')), parts along dimension 0, may hold values from -6 to 6
- gate_matrix: bfloat16 [8192, 14336], P(None, 'tp'), may hold values from -0.0625 to 0.0625
- up_matrix: bfloat16 [8192, 14336], P(None, 'tp'), may hold values from -0.0625 to 0.0625
- down_matrix: bfloat16 [14336, 8192], P('tp'), may hold values from -0.046875 to 0.046875
- shrink_matrices: bfloat16 [16, 8192, 128], P('rep', None, 'tp'), parts along dimension 0, may hold values from -0.0625 to 0.0625
- expand_matrices: bfloat16 [16, 128, 14336], P('rep', None, 'tp'), parts along dimension 0, may hold values from -0.75 to 0.75
- adapter_per_block: int32 [4], P('rep'), parts along dimension 0, may hold values from 0 to 7
- block_token_count: int32 [4], P('rep'), parts along dimension 0, may hold values from 32 to 128, as said below
Outputs:
- mixed_out: bfloat16 [512, 8192], P(('rep', 'tp')), parts along dimension 0
There are 2 independent parts, one for each index of `rep`. A program takes and returns all parts, laid end to end along the dimension named above; an argument that names none is the same for every part. Nothing has to cross between parts.
Inputs may be any that keep to these rules, and one draw needn't show every extreme that they name: `block_token_count`: every block holds at least a quarter of 128 live rows, and some block is full.
All inputs are finite; a program needn't handle non-finite values.
Results may differ from a plain program's by a relative error of at most 0.014.
Values may be sent and summed in bfloat16 or wider, within the bound.
No kernel may reach another device: no remote copies, remote signals or barrier semaphores. Data moves between devices by JAX's collectives and lax.ppermute only.
A program may use at most 128 MiB of HBM per device.

v0:
```python
import jax
import jax.numpy as jnp
from jax import lax
from jax.sharding import PartitionSpec as P


def per_device(
    tokens,
    gate_matrix,
    up_matrix,
    down_matrix,
    shrink_matrices,
    expand_matrices,
    adapter_per_block,
    block_token_count,
):
    group_count = lax.axis_size("tp")
    position = lax.axis_index("tp")
    tok_dev = tokens.shape[0]
    ff_dev = gate_matrix.shape[1]
    adapter_table = shrink_matrices.shape[0]
    rank_column_span = shrink_matrices.shape[2]
    blocks = adapter_per_block.shape[0]
    total_rows = tok_dev * group_count
    block_rows = total_rows // blocks
    rank_width = rank_column_span * group_count
    half_rank = rank_width // 2
    adapter_ids = jnp.arange(adapter_table, dtype=jnp.int32)
    block_ids = jnp.arange(blocks, dtype=jnp.int32)
    selected_expand = expand_matrices[adapter_per_block]
    local_row_slice = lax.all_gather(tokens, "tp", axis=0, tiled=True)
    row_ids = jnp.arange(local_row_slice.shape[0], dtype=jnp.int32)
    owner_block = row_ids // block_rows
    pick_block = (owner_block[:, None] == block_ids[None, :]).astype(jnp.int32)
    row_adapter = jnp.sum(pick_block * adapter_per_block[None, :], axis=1)
    gate_part = jnp.dot(local_row_slice, gate_matrix, preferred_element_type=jnp.float32)
    up_part = jnp.dot(local_row_slice, up_matrix, preferred_element_type=jnp.float32)
    shrink_every_block = jnp.einsum(
        "fz,czs->fcs", local_row_slice, shrink_matrices, preferred_element_type=jnp.float32
    )
    chosen = (row_adapter[:, None] == adapter_ids[None, :]).astype(jnp.float32)
    shrink = jnp.sum(shrink_every_block * chosen[:, :, None], axis=1)
    joined = jnp.concatenate([gate_part, up_part, shrink], axis=1)
    base_gate = joined[:, :ff_dev]
    base_up = joined[:, ff_dev : 2 * ff_dev]
    rank_local = joined[:, 2 * ff_dev :].astype(jnp.bfloat16)
    rank_full = lax.all_gather(rank_local, "tp", axis=1, tiled=True)
    ranks_blocked = rank_full.reshape(blocks, block_rows, rank_width)
    gate_delta = jnp.einsum(
        "bkr,brf->bkf",
        ranks_blocked[:, :, :half_rank],
        selected_expand[:, :half_rank, :],
        preferred_element_type=jnp.float32,
    ).reshape(total_rows, ff_dev)
    up_delta = jnp.einsum(
        "bkr,brf->bkf",
        ranks_blocked[:, :, half_rank:],
        selected_expand[:, half_rank:, :],
        preferred_element_type=jnp.float32,
    ).reshape(total_rows, ff_dev)
    hidden = (jax.nn.silu(base_gate + gate_delta) * (base_up + up_delta)).astype(jnp.bfloat16)
    summed = lax.psum_scatter(
        jnp.dot(hidden, down_matrix, preferred_element_type=jnp.float32).astype(jnp.bfloat16),
        "tp",
        scatter_dimension=0,
        tiled=True,
    ).astype(jnp.float32)
    own_rows = position * tok_dev + jnp.arange(tok_dev, dtype=jnp.int32)
    own_block = own_rows // block_rows
    match_block = (own_block[:, None] == block_ids[None, :]).astype(jnp.int32)
    live_rows = jnp.sum(match_block * block_token_count[None, :], axis=1)
    live_mask = own_rows % block_rows < live_rows
    return jnp.where(live_mask[:, None], summed, jnp.zeros_like(summed)).astype(jnp.bfloat16)


def solution(mesh):
    return jax.shard_map(
        per_device,
        mesh=mesh,
        in_specs=(
            P(("rep", "tp"), None),
            P(None, "tp"),
            P(None, "tp"),
            P("tp", None),
            P("rep", None, "tp"),
            P("rep", None, "tp"),
            P("rep"),
            P("rep"),
        ),
        out_specs=P(("rep", "tp"), None),
        check_vma=False,
    )
```

profile of v0, /device:TPU:0, one launch (start us, length us, event | category | flops | bytes accessed | tf_op | source)
XLA Modules:
  0.0 198.6 jit_solution(2734734838332084296)
XLA Ops:
  6.5 0.0 copy-start
  6.5 0.0 all-gather.2.cloned.1.call-start
  6.5 0.7 all-gather.2.cloned.1.call-update
  7.3 0.0 reduce-scatter.2.cloned.1.call-start
  7.3 0.7 compare_select_fusion.1
  8.0 0.1 copy-done
  8.0 0.6 gather_fusion
  8.7 0.7 fusion.12
  9.4 53.4 %all-gather.2.cloned.1.call-done = bf16[256,8192]{1,0:T(8,128)(2,1)} async-done(((bf16[16,8192]{1,0:T(8,128)(2,1)}), bf16[256,8192]{1,0:T(8,128)(2,1)}) %all-gather.2.cloned.1.call-update) | async-done | bytes 4194320 | tf_op jit(solution)/shard_map/all_gather | solution.py:31
  62.8 3.9 %fusion.3 = bf16[256,8]{0,1:T(8,128)(2,1)S(1)} fusion(bf16[256,8192]{1,0:T(8,128)(2,1)} %all-gather.2.cloned.1.call-done, bf16[8,8192,8]{1,2,0:T(8,128)(2,1)} %param.12, f32[256,8]{0,1:T(8,128)S(1)} %fusion.11), kind=kOutput, calls=%fused_computation.8 | convolution fusion | flops 268466176 | bytes 5255168
  66.7 19.1 %all_gather.7 = bf16[256,128]{0,1:T(8,128)(2,1)S(1)} all-gather(bf16[256,8]{0,1:T(8,128)(2,1)S(1)} %fusion.3), channel_id=1, replica_groups=mesh['rep'=2,'tp'=16] {'tp'}, dimensions={1}, use_global_device_ids=true | all-gather | bytes 69632 | tf_op jit(solution)/shard_map/all_gather | solution.py:47
  85.8 0.1 copy.14
  85.9 0.3 fusion.7
  86.1 0.3 fusion.5
  86.5 12.0 %convolution_add_fusion.1 = f32[256,896]{1,0:T(8,128)} fusion(f32[256,896]{1,0:T(8,128)S(1)} %bitcast.21, bf16[256,8192]{1,0:T(8,128)(2,1)} %all-gather.2.cloned.1.call-done, bf16[8192,896]{1,0:T(8,128)(2,1)} %param.9), kind=kOutput, calls=%fused_computation.4 | convolution fusion | flops 3758325760 | bytes 20709376 | tf_op jit(solution)/shard_map/dot_general | solution.py:36
  98.4 21.6 %convolution_convert_fusion = bf16[256,8192]{1,0:T(8,128)(2,1)} fusion(bf16[896,8192]{1,0:T(8,128)(2,1)} %param.11, f32[256,896]{1,0:T(8,128)S(1)} %bitcast.20, bf16[256,8192]{1,0:T(8,128)(2,1)} %all-gather.2.cloned.1.call-done, bf16[8192,896]{1,0:T(8,128)(2,1)} %param.10, f32[256,896]{1,0:T(8,128)} %convolution_add_fusion.1), kind=kOutput, calls=%fused_computation.1 | convolution fusion | flops 7519895552 | bytes 39583744 | tf_op jit(solution)/shard_map/dot_general | solution.py:63
  120.1 0.0 copy-start.1
  120.1 0.0 reduce-scatter.2.cloned.1.call-update
  120.1 0.6 copy-done.1
  120.7 0.1 fusion.13
  120.8 69.2 %reduce-scatter.2.cloned.1.call-done = bf16[16,8192]{1,0:T(8,128)(2,1)} async-done(((bf16[256,8192]{1,0:T(8,128)(2,1)}), bf16[16,8192]{1,0:T(8,128)(2,1)}) %reduce-scatter.2.cloned.1.call-update) | async-done | bytes 262160 | tf_op jit(solution)/shard_map/reduce_scatter | solution.py:62
  190.0 1.8 select_convert_fusion
  (5 shorter events, 0.0 us)
Async XLA Ops:
  6.5 1.5 copy-start
  6.5 56.3 %all-gather.2.cloned.1.call-start = ((), (), s32[]{:S(2)}) async-start(), calls=%async_computation.1 | async-start | bytes 4456448 | tf_op jit(solution)/shard_map/all_gather | solution.py:31
  7.3 182.7 %reduce-scatter.2.cloned.1.call-start = ((), (), s32[]{:S(2)}) async-start(), calls=%async_computation.2 | async-start | bytes 4456448 | tf_op jit(solution)/shard_map/reduce_scatter | solution.py:62
  120.1 0.7 copy-start.1
Sparse Core Ops, SparseCore 0:
  9.5 53.2 all-gather.1
  120.2 69.7 reduce-scatter.1
where the time goes:
time: 199 us
  waiting for transfers between devices  123 us (62%)
  matrix products  38.1 us (19%)
  blocking collectives  19.1 us (10%)
  between operations  13.4 us (7%)
  other arithmetic  3.3 us (2%)
    reduce_scatter x1, waiting for transfers between devices, per_device(): lax.psum_scatter(jnp.dot(hidden, down_matrix, preferred_element_type=jnp....  69.2 us
    all_gather x1, waiting for transfers between devices, per_device(): local_row_slice = lax.all_gather(tokens, 'tp', axis=0, tiled=True)  53.4 us
    dot_general x1, matrix products, per_device(): jnp.dot(hidden, down_matrix, preferred_element_type=jnp.float32)  21.6 us
    all_gather x1, blocking collectives, per_device(): rank_full = lax.all_gather(rank_local, 'tp', axis=1, tiled=True)  19.1 us
    dot_general x1, matrix products, per_device(): jnp.dot(local_row_slice, gate_matrix, preferred_element_type=jnp.float32)  12 us
  transfers between devices with their start and end apart: 2, of which 2 were waited for; matrix products, arithmetic and copies ran while one was open for 1% of the time, Pallas kernels for 0%

commit v1 on v0

v1 whole, which is shorter than its diff:
```python
import functools

import jax
import jax.numpy as jnp
import numpy as np
from jax import lax
from jax.experimental import pallas as pl
from jax.experimental.pallas import tpu as pltpu
from jax.sharding import Mesh, PartitionSpec as P

F32 = jnp.float32
BF16 = jnp.bfloat16
VMEM_LIMIT = 56 * 1024 * 1024
SWAP = [(0, 1), (1, 0)]


def largest_tile(size, limit):
    tile = limit
    while size % tile:
        tile //= 2
    return tile


def gate_up_kernel(own_ref, sib_ref, wg_ref, wu_ref, g_ref, u_ref):
    @pl.when(pl.program_id(0) == 0)
    def _():
        g_ref[...] = jnp.zeros_like(g_ref)
        u_ref[...] = jnp.zeros_like(u_ref)

    half = own_ref.shape[0]
    rows = jnp.concatenate([own_ref[...], sib_ref[...]], axis=0)
    g_ref[...] += jnp.dot(rows, wg_ref[...], preferred_element_type=F32)
    u_ref[...] += jnp.dot(rows, wu_ref[...], preferred_element_type=F32)


def gate_up(own, sib, gate_matrix, up_matrix, first):
    half, depth = own.shape
    width = gate_matrix.shape[1]
    tile = largest_tile(depth, 1024)
    steps = depth // tile
    offset = first // tile
    out = jax.ShapeDtypeStruct((2 * half, width), F32)
    return pl.pallas_call(
        gate_up_kernel,
        grid=(steps,),
        in_specs=[
            pl.BlockSpec((half, tile), lambda k: (0, k)),
            pl.BlockSpec((half, tile), lambda k: (0, k)),
            pl.BlockSpec((tile, width), lambda k: (k + offset, 0)),
            pl.BlockSpec((tile, width), lambda k: (k + offset, 0)),
        ],
        out_specs=[pl.BlockSpec((2 * half, width), lambda k: (0, 0))] * 2,
        out_shape=[out, out],
        compiler_params=pltpu.CompilerParams(vmem_limit_bytes=VMEM_LIMIT),
        cost_estimate=pl.CostEstimate(
            flops=8 * half * depth * width,
            bytes_accessed=4 * depth * width + 4 * half * depth,
            transcendentals=0,
        ),
        name="gate_up",
    )(own, sib, gate_matrix, up_matrix)


def finish_kernel(parts, adapter_ref, *refs):
    g_refs, u_refs = refs[:parts], refs[parts : 2 * parts]
    rank_ref, expand_ref, hidden_ref = refs[2 * parts :]
    _, _, rows, width = hidden_ref.shape
    rank = rank_ref[...].reshape(2 * rows, rank_ref.shape[-1])
    half = rank.shape[1] // 2
    gate = jnp.dot(rank[:, :half], expand_ref[0, :half], preferred_element_type=F32)
    up = jnp.dot(rank[:, half:], expand_ref[0, half:], preferred_element_type=F32)
    for g_ref in g_refs:
        gate += g_ref[...].reshape(2 * rows, width)
    for u_ref in u_refs:
        up += u_ref[...].reshape(2 * rows, width)
    hidden = gate / (1.0 + jnp.exp(-gate)) * up
    hidden_ref[...] = hidden.astype(BF16).reshape(hidden_ref.shape)


def finish(gates, ups, rank, expand, adapters):
    blocks = adapters.shape[0]
    total, width = gates[0].shape
    rows = total // (2 * blocks)
    ranks = rank.shape[1]
    parts = len(gates)

    def by_block(x):
        return x.reshape(2, blocks, rows, x.shape[-1])

    wide = pl.BlockSpec((2, 1, rows, width), lambda b, ids: (0, b, 0, 0))
    hidden = pl.pallas_call(
        functools.partial(finish_kernel, parts),
        grid_spec=pltpu.PrefetchScalarGridSpec(
            num_scalar_prefetch=1,
            grid=(blocks,),
            in_specs=[wide] * (2 * parts)
            + [
                pl.BlockSpec((2, 1, rows, ranks), lambda b, ids: (0, b, 0, 0)),
                pl.BlockSpec((1, ranks, width), lambda b, ids: (ids[b], 0, 0)),
            ],
            out_specs=wide,
        ),
        out_shape=jax.ShapeDtypeStruct((2, blocks, rows, width), BF16),
        compiler_params=pltpu.CompilerParams(vmem_limit_bytes=VMEM_LIMIT),
        name="finish",
    )(adapters, *map(by_block, gates), *map(by_block, ups), by_block(rank), expand)
    return hidden.reshape(total, width)


def down_kernel(hidden_ref, w_ref, mine_ref, sib_ref):
    product = jnp.dot(hidden_ref[...], w_ref[...], preferred_element_type=F32).astype(BF16)
    half = product.shape[0] // 2
    mine_ref[...] = product[:half]
    sib_ref[...] = product[half:]


def down(hidden, down_matrix, first, columns):
    total, depth = hidden.shape
    tile = largest_tile(columns, 1024)
    offset = first // tile
    out = jax.ShapeDtypeStruct((total // 2, columns), BF16)
    return pl.pallas_call(
        down_kernel,
        grid=(columns // tile,),
        in_specs=[
            pl.BlockSpec((total, depth), lambda n: (0, 0)),
            pl.BlockSpec((depth, tile), lambda n: (0, n + offset)),
        ],
        out_specs=[pl.BlockSpec((total // 2, tile), lambda n: (0, n))] * 2,
        out_shape=[out, out],
        compiler_params=pltpu.CompilerParams(vmem_limit_bytes=VMEM_LIMIT),
        cost_estimate=pl.CostEstimate(
            flops=2 * total * depth * columns,
            bytes_accessed=2 * depth * columns + 2 * total * columns,
            transcendentals=0,
        ),
        name="down",
    )(hidden, down_matrix)


def ring_of(chips):
    return list(range(0, chips, 2)) + list(range(chips - 1, 0, -2))


def per_device(
    chips,
    tokens,
    gate_matrix,
    up_matrix,
    down_matrix,
    shrink_matrices,
    expand_matrices,
    adapter_per_block,
    block_token_count,
):
    chip, core = lax.axis_index("chip"), lax.axis_index("core")
    rows, model = tokens.shape
    blocks = adapter_per_block.shape[0]
    span = shrink_matrices.shape[2]
    half = chips * rows
    total = 2 * half
    block_rows = total // blocks
    ring = ring_of(chips)
    place = jnp.asarray(np.argsort(ring), jnp.int32)[chip]
    ring_table = jnp.asarray(ring, jnp.int32)
    rightward = [(ring[i], ring[(i + 1) % chips]) for i in range(chips)]
    leftward = [(b, a) for a, b in rightward]

    parts = 2
    depth = model // parts
    shrink = jnp.swapaxes(shrink_matrices, 1, 2)[adapter_per_block]
    gates, ups = [], []
    rank = jnp.zeros((total, blocks * span), F32)
    gathered = []
    for part in range(parts):
        piece = tokens[:, part * depth : (part + 1) * depth]
        own = lax.all_gather(piece, "chip", axis=0, tiled=True)
        sib = lax.ppermute(own, "core", SWAP)
        gathered.append((own, sib))
        pick = shrink[:, :, part * depth : (part + 1) * depth].reshape(blocks * span, depth)
        pair = [
            lax.dot_general(x, pick, (((1,), (1,)), ((), ())), preferred_element_type=F32)
            for x in (own, sib)
        ]
        rank = rank + jnp.concatenate(pair, axis=0)
    row_block = (jnp.arange(total) % half) * 2 // block_rows
    wanted = row_block[:, None] == jnp.arange(blocks)[None, :]
    rank = jnp.sum(
        jnp.where(wanted[:, :, None], rank.reshape(total, blocks, span), 0.0), axis=1
    ).astype(BF16).T

    other = lax.ppermute(rank, "core", SWAP)
    other = jnp.concatenate([other[:, half:], other[:, :half]], axis=1)
    pair = jnp.where(core == 0, jnp.stack([rank, other]), jnp.stack([other, rank]))
    pair = pair.reshape(2 * span, total)
    ranks = [pair]
    for shift in range(1, chips):
        ranks.append(lax.ppermute(pair, "chip", [(i, (i + shift) % chips) for i in range(chips)]))
    stacked = jnp.stack(ranks)
    order = (chip - jnp.arange(chips)) % chips
    rank_full = stacked[order].reshape(chips * 2 * span, total).T

    for part, (own, sib) in enumerate(gathered):
        g, u = gate_up(own, sib, gate_matrix, up_matrix, part * depth)
        gates.append(g)
        ups.append(u)
    hidden = finish(gates, ups, rank_full, expand_matrices, adapter_per_block)

    results = []
    columns = model // 2
    steps = chips // 2
    for side in range(2):
        mine, sib = down(hidden, down_matrix, side * columns, columns)
        came = lax.ppermute(sib, "core", SWAP)
        mine = mine.reshape(chips, rows, columns)
        came = came.reshape(chips, rows, columns)

        def take(offset):
            at = ring_table[(place + offset) % chips]
            return lax.dynamic_index_in_dim(mine, at, 0, False).astype(
                F32
            ) + lax.dynamic_index_in_dim(came, at, 0, False).astype(F32)

        result = take(0)
        for sign, links in ((1, rightward), (-1, leftward)):
            far = steps if (sign == 1) == (side == 0) else steps - 1
            carry = None
            for offset in range(far, 0, -1):
                value = take(sign * offset)
                if carry is not None:
                    value = value + carry.astype(F32)
                carry = lax.ppermute(value.astype(BF16), "chip", links)
            result = result + carry.astype(F32)
        results.append(result)
    summed = jnp.concatenate(results, axis=1)

    first = (2 * chip + core) * rows
    own_block = first // block_rows
    live = block_token_count[own_block]
    row_ids = first % block_rows + jnp.arange(rows, dtype=jnp.int32)
    return jnp.where((row_ids < live)[:, None], summed, 0.0).astype(BF16)


def solution(mesh):
    groups, members = mesh.devices.shape
    chips = members // 2
    fine = Mesh(mesh.devices.reshape(groups, chips, 2), ("rep", "chip", "core"))
    tp = ("chip", "core")
    return jax.shard_map(
        functools.partial(per_device, chips),
        mesh=fine,
        in_specs=(
            P(("rep", "chip", "core"), None),
            P(None, tp),
            P(None, tp),
            P(tp, None),
            P("rep", None, tp),
            P("rep", None, tp),
            P("rep"),
            P("rep"),
        ),
        out_specs=P(("rep", "chip", "core"), None),
        check_vma=False,
    )
```

time: 199 us -> 233 us (1.17)
  Pallas kernels: 0 us -> 35.8 us
  matrix products: 38.1 us -> 3.98 us
  between operations: 13.4 us -> 38 us
  starting transfers between devices: 0.04 us -> 23.4 us
  blocking collectives: 19.1 us -> 0 us
  waiting for transfers between devices: 123 us -> 111 us
  other arithmetic: 3.3 us -> 14 us
  local copies, waits for them, and re-layouts: 1.4 us -> 5.52 us
    reduce_scatter x1 -> x0, waiting for transfers between devices: 69.2 us -> none  [per_device(): lax.psum_scatter(jnp.dot(hidden, down_matrix, preferred_element_type=jnp....]
    pallas_call x0 -> x5, Pallas kernels: none -> 35.8 us  [the longest x2 19.1 us: gate_up(): pl.pallas_call(gate_up_kernel, grid=(steps,), in_specs=[pl.BlockSpec((hal...]
    dot_general x4, matrix products: 34.2 us -> 3.98 us  [per_device(): lax.dot_general(x, pick, (((1,), (1,)), ((), ())), preferred_element_type...]
    all_gather x1 -> x2, waiting for transfers between devices: 53.4 us -> 83.1 us  [per_device(): own = lax.all_gather(piece, 'chip', axis=0, tiled=True)]
    ppermute x0 -> x26, waiting for transfers between devices: none -> 27.5 us  [the longest x7 16.7 us: per_device(): lax.ppermute(pair, 'chip', [(i, (i + shift) % chips) for i in range(chips)])]
    ppermute x0 -> x26, starting transfers between devices: none -> 23.3 us  [the longest x14 15.3 us: per_device(): carry = lax.ppermute(value.astype(BF16), 'chip', links)]
    all_gather x1 -> x0, blocking collectives: 19.1 us -> none  [per_device(): rank_full = lax.all_gather(rank_local, 'tp', axis=1, tiled=True)]
    convert_element_type x2 -> x11, other arithmetic: 1.77 us -> 10.8 us  [the longest x10 9.97 us: per_device(): carry = lax.ppermute(value.astype(BF16), 'chip', links)]
  transfers between devices with their start and end apart: 2 -> 28, of which waited for: 2 -> 12; matrix products, arithmetic and copies ran while one was open for 1% -> 8% of each run, Pallas kernels for 0% -> 11%
where the time goes in v1:
time: 233 us; the launch traced here: 232 us
  waiting for transfers between devices  111 us (48%)
  between operations  38 us (16%)
  Pallas kernels  35.8 us (15%)
  starting transfers between devices  23.4 us (10%)
  other arithmetic  14 us (6%)
  local copies, waits for them, and re-layouts  5.52 us (2%)
  matrix products  3.98 us (2%)
    all_gather x2, waiting for transfers between devices, per_device(): own = lax.all_gather(piece, 'chip', axis=0, tiled=True)  83.1 us
    pallas_call x2, Pallas kernels, gate_up(): pl.pallas_call(gate_up_kernel, grid=(steps,), in_specs=[pl.BlockSpec((hal...  19.1 us
    ppermute x7, waiting for transfers between devices, per_device(): lax.ppermute(pair, 'chip', [(i, (i + shift) % chips) for i in range(chips)])  16.7 us
    ppermute x14, starting transfers between devices, per_device(): carry = lax.ppermute(value.astype(BF16), 'chip', links)  15.3 us
    pallas_call x2, Pallas kernels, down(): pl.pallas_call(down_kernel, grid=(columns // tile,), in_specs=[pl.BlockSp...  12.8 us
    ppermute x14, waiting for transfers between devices, per_device(): carry = lax.ppermute(value.astype(BF16), 'chip', links)  10.8 us
    convert_element_type x10, other arithmetic, per_device(): carry = lax.ppermute(value.astype(BF16), 'chip', links)  9.97 us
    ppermute x7, starting transfers between devices, per_device(): lax.ppermute(pair, 'chip', [(i, (i + shift) % chips) for i in range(chips)])  7.08 us
  transfers between devices with their start and end apart: 28, of which 12 were waited for; matrix products, arithmetic and copies ran while one was open for 8% of the time, Pallas kernels for 11%

profile of v1, /device:TPU:0, one launch (start us, length us, event | category | flops | bytes accessed | tf_op | source)
XLA Modules:
  0.0 232.0 jit_solution(168977256827063880)
XLA Ops:
  6.5 1.8 fusion.23
  8.4 0.7 all-gather.5.cloned.1.call-update
  9.1 43.3 %all-gather.3.cloned.1.call-done.own_ref = bf16[128,4096]{1,0:T(8,128)(2,1)} async-done(((bf16[16,4096]{1,0:T(8,128)(2,1)}), bf16[128,4096]{1,0:T(8,128)(2,1)}) %all-gather.3.cloned.1.call-update) | async-done | bytes 1048592 | tf_op jit(solution)/shard_map/all_gather | solution.py:177
  52.4 0.7 compare_select_fusion.1
  53.0 0.6 gather_fusion
  53.6 39.8 %all-gather.5.cloned.1.call-done.own_ref = bf16[128,4096]{1,0:T(8,128)(2,1)} async-done(((bf16[16,4096]{1,0:T(8,128)(2,1)}), bf16[128,4096]{1,0:T(8,128)(2,1)}) %all-gather.5.cloned.1.call-update) | async-done | bytes 1048592 | tf_op jit(solution)/shard_map/all_gather | solution.py:177
  93.5 1.6 convolution_bitcast_fusion.3
  95.1 1.6 convolution_bitcast_fusion.1
  96.7 0.4 convolution_bitcast_fusion.2
  97.1 0.4 convolution_bitcast_fusion
  97.5 0.6 collective-permute-start.2
  98.1 9.5 %gate_up.2 = (f32[256,896]{1,0:T(8,128)}, f32[256,896]{1,0:T(8,128)}) custom-call(bf16[128,4096]{1,0:T(8,128)(2,1)} %all-gather.3.cloned.1.call-done.own_ref, bf16[128,4096]{1,0:T(8,128)(2,1)} %copy-done.1, bf16[8192,896]{1,0:T(8,128)(2,1)} %wg_ref.3, bf16[8192,896]{1,0:T(8,128)(2,1)} %wu_ref.3), custom_call_target="tpu_custom_call" | custom-call | flops 3758096384 | bytes 16777216 | tf_op jit(solution)/shard_map/gate_up/pallas_call | solution.py:43
  107.6 9.5 %gate_up.3 = (f32[256,896]{1,0:T(8,128)}, f32[256,896]{1,0:T(8,128)}) custom-call(bf16[128,4096]{1,0:T(8,128)(2,1)} %all-gather.5.cloned.1.call-done.own_ref, bf16[128,4096]{1,0:T(8,128)(2,1)} %copy-done.2, bf16[8192,896]{1,0:T(8,128)(2,1)} %wg_ref.3, bf16[8192,896]{1,0:T(8,128)(2,1)} %wu_ref.3), custom_call_target="tpu_custom_call" | custom-call | flops 3758096384 | bytes 16777216 | tf_op jit(solution)/shard_map/gate_up/pallas_call | solution.py:43
  117.2 2.1 collective-permute-start.9
  119.3 0.1 collective-permute-start.8
  119.4 1.3 collective-permute-start.7
  120.7 3.0 %collective-permute-start.6 = (bf16[16,256]{1,0:T(8,128)(2,1)S(1)}, bf16[16,256]{1,0:T(8,128)(2,1)S(1)}, u32[]{:S(2)}, u32[]{:S(2)}) collective-permute-start(bf16[16,256]{1,0:T(8,128)(2,1)S(1)} %fusion.19), channel_id=1, source_target_pairs={{0,8},{2,10},{4,12},{6,14},{8,0},{10,2},{12,4},{14,6},{1,9},{3,11}... | collective-permute-start | bytes 24584 | tf_op jit(solution)/shard_map/ppermute | solution.py:198
  123.7 0.6 collective-permute-start.3
  124.3 5.8 %collective-permute-done.3 = bf16[16,256]{1,0:T(8,128)(2,1)S(1)} collective-permute-done((bf16[16,256]{1,0:T(8,128)(2,1)S(1)}, bf16[16,256]{1,0:T(8,128)(2,1)S(1)}, u32[]{:S(2)}, u32[]{:S(2)}) %collective-permute-start.3) | collective-permute-done | bytes 8224 | tf_op jit(solution)/shard_map/ppermute | solution.py:198
  130.1 5.4 %collective-permute-done.4 = bf16[16,256]{1,0:T(8,128)(2,1)S(1)} collective-permute-done((bf16[16,256]{1,0:T(8,128)(2,1)S(1)}, bf16[16,256]{1,0:T(8,128)(2,1)S(1)}, u32[]{:S(2)}, u32[]{:S(2)}) %collective-permute-start.4) | collective-permute-done | bytes 8224 | tf_op jit(solution)/shard_map/ppermute | solution.py:198
  135.5 5.4 %collective-permute-done.5 = bf16[16,256]{1,0:T(8,128)(2,1)S(1)} collective-permute-done((bf16[16,256]{1,0:T(8,128)(2,1)S(1)}, bf16[16,256]{1,0:T(8,128)(2,1)S(1)}, u32[]{:S(2)}, u32[]{:S(2)}) %collective-permute-start.5) | collective-permute-done | bytes 8224 | tf_op jit(solution)/shard_map/ppermute | solution.py:198
  141.0 0.6 gather_fusion.1
  141.6 0.7 copy.11
  142.3 3.9 %finish.1 = bf16[2,2,64,896]{3,2,1,0:T(8,128)(2,1)} custom-call(s32[2]{0:T(128)} %adapter_ref.1, f32[2,2,64,896]{3,2,1,0:T(8,128)} %bitcast.159, f32[2,2,64,896]{3,2,1,0:T(8,128)} %bitcast.161, f32[2,2,64,896]{3,2,1,0:T(8,128)} %bitcast.160, f32[2,2,64,896]{3,2,1,0:T(8,128)} %bitcast.162, bf16[2,2,64,128]{3,2,1,0:T(8,128)(2,1)} %bitcast.163, ...), custom_call_target="tpu_custom_call" | custom-call | tf_op jit(solution)/shard_map/finish/pallas_call | solution.py:91
  146.2 6.4 %down.3 = (bf16[128,4096]{1,0:T(8,128)(2,1)}, bf16[128,4096]{1,0:T(8,128)(2,1)}) custom-call(bf16[256,896]{1,0:T(8,128)(2,1)} %bitcast.139, bf16[896,8192]{1,0:T(8,128)(2,1)} %w_ref.3), custom_call_target="tpu_custom_call" | custom-call | flops 1879048192 | bytes 9437184 | tf_op jit(solution)/shard_map/down/pallas_call | solution.py:122
  152.6 6.4 %down.2 = (bf16[128,4096]{1,0:T(8,128)(2,1)}, bf16[128,4096]{1,0:T(8,128)(2,1)}) custom-call(bf16[256,896]{1,0:T(8,128)(2,1)} %bitcast.140, bf16[896,8192]{1,0:T(8,128)(2,1)} %w_ref.3), custom_call_target="tpu_custom_call" | custom-call | flops 1879048192 | bytes 9437184 | tf_op jit(solution)/shard_map/down/pallas_call | solution.py:122
  159.0 0.4 collective-permute-start.10
  159.5 0.6 dynamic_slice.138
  167.3 0.7 fusion.25
  179.4 0.6 dynamic_slice.137
  185.7 0.6 add_compare_fusion
  186.3 1.0 fusion.15
  187.3 0.1 collective-permute-start.19
  187.4 2.0 collective-permute-start.22
  189.4 1.0 fusion.13
  190.4 0.1 collective-permute-start.11
  190.5 2.0 collective-permute-start.15
  192.5 0.5 collective-permute-done.19
  193.0 1.0 fusion.4
  194.0 0.3 collective-permute-start.20
  194.3 1.4 collective-permute-done.11
  195.7 1.0 fusion.9
  196.6 0.3 collective-permute-start.12
  197.0 3.0 %collective-permute-done.20 = bf16[16,4096]{1,0:T(8,128)(2,1)S(1)} collective-permute-done((bf16[16,4096]{1,0:T(8,128)(2,1)S(1)}, bf16[16,4096]{1,0:T(8,128)(2,1)S(1)}, u32[]{:S(2)}, u32[]{:S(2)}) %collective-permute-start.20) | collective-permute-done | bytes 131104 | tf_op jit(solution)/shard_map/ppermute | solution.py:232
  200.0 1.1 fusion.5
  201.0 0.1 collective-permute-start.21
  201.1 2.0 collective-permute-start.23
  203.1 1.0 fusion.10
  204.1 0.1 collective-permute-start.13
  204.2 2.3 collective-permute-done.23
  206.5 1.0 fusion.2
  207.5 2.5 %collective-permute-start.24 = (bf16[16,4096]{1,0:T(8,128)(2,1)S(1)}, bf16[16,4096]{1,0:T(8,128)(2,1)S(1)}, u32[]{:S(2)}, u32[]{:S(2)}) collective-permute-start(bf16[16,4096]{1,0:T(8,128)(2,1)S(1)} %fusion.2), channel_id=1, source_target_pairs={{4,0},{8,4},{12,8},{14,12},{10,14},{6,10},{2,6},{0,2},{5,1},{9,5},... | collective-permute-start | bytes 393224 | tf_op jit(solution)/shard_map/ppermute | solution.py:232
  210.0 1.1 fusion.11
  211.1 2.0 collective-permute-start.16
  213.1 0.7 collective-permute-done.24
  213.9 1.0 fusion.3
  214.9 2.5 %collective-permute-start.25 = (bf16[16,4096]{1,0:T(8,128)(2,1)S(1)}, bf16[16,4096]{1,0:T(8,128)(2,1)S(1)}, u32[]{:S(2)}, u32[]{:S(2)}) collective-permute-start(bf16[16,4096]{1,0:T(8,128)(2,1)S(1)} %fusion.3), channel_id=1, source_target_pairs={{4,0},{8,4},{12,8},{14,12},{10,14},{6,10},{2,6},{0,2},{5,1},{9,5},... | collective-permute-start | bytes 393224 | tf_op jit(solution)/shard_map/ppermute | solution.py:232
  217.4 1.0 fusion.8
  218.4 1.2 collective-permute-start.17
  219.5 0.4 collective-permute-done.25
  219.9 1.0 fusion.6
  220.9 2.5 %collective-permute-done.17 = bf16[16,4096]{1,0:T(8,128)(2,1)S(1)} collective-permute-done((bf16[16,4096]{1,0:T(8,128)(2,1)S(1)}, bf16[16,4096]{1,0:T(8,128)(2,1)S(1)}, u32[]{:S(2)}, u32[]{:S(2)}) %collective-permute-start.17) | collective-permute-done | bytes 131104 | tf_op jit(solution)/shard_map/ppermute | solution.py:232
  223.4 1.0 fusion.12
  224.4 0.8 fusion
  (56 shorter events, 0.3 us)
Async XLA Ops:
  6.5 46.5 %copy-start = (bf16[8,8192,8]{1,2,0:T(8,128)(2,1)S(1)}, bf16[8,8192,8]{1,2,0:T(8,128)(2,1)}, u32[]{:S(2)}) copy-start(bf16[8,8192,8]{1,2,0:T(8,128)(2,1)} %param.14) | copy-start | bytes 3145732
  6.5 45.8 %all-gather.3.cloned.1.call-start = ((), (), s32[]{:S(2)}) async-start(), calls=%async_computation | async-start | bytes 1179648 | tf_op jit(solution)/shard_map/all_gather | solution.py:177
  8.3 85.1 %all-gather.5.cloned.1.call-start = ((), (), s32[]{:S(2)}) async-start(), calls=%async_computation.1 | async-start | bytes 1179648 | tf_op jit(solution)/shard_map/all_gather | solution.py:177
  52.4 44.3 %collective-permute-start = (bf16[128,4096]{1,0:T(8,128)(2,1)}, bf16[128,4096]{1,0:T(8,128)(2,1)S(1)}, u32[]{:S(2)}, u32[]{:S(2)}) collective-permute-start(bf16[128,4096]{1,0:T(8,128)(2,1)} %all-gather.3.cloned.1.call-done.own_ref), channel_id=1, source_target_pairs={{0,1},{1,0},{2,3},{3,2},{4,5},{5,4},{6,7},{7,6},{8,9},{9,8},{10,11... | collective-permute-start | bytes 3145736 | tf_op jit(solution)/shard_map/ppermute | solution.py:178
  93.4 3.7 %collective-permute-start.1 = (bf16[128,4096]{1,0:T(8,128)(2,1)}, bf16[128,4096]{1,0:T(8,128)(2,1)S(1)}, u32[]{:S(2)}, u32[]{:S(2)}) collective-permute-start(bf16[128,4096]{1,0:T(8,128)(2,1)} %all-gather.5.cloned.1.call-done.own_ref), channel_id=1, source_target_pairs={{0,1},{1,0},{2,3},{3,2},{4,5},{5,4},{6,7},{7,6},{8,9},{9,8},{10,11... | collective-permute-start | bytes 3145736 | tf_op jit(solution)/shard_map/ppermute | solution.py:178
  96.7 1.4 copy-start.1
  97.1 10.5 %copy-start.2 = (bf16[128,4096]{1,0:T(8,128)(2,1)}, bf16[128,4096]{1,0:T(8,128)(2,1)S(1)}, u32[]{:S(2)}) copy-start(bf16[128,4096]{1,0:T(8,128)(2,1)S(1)} %collective-permute-done.1.sib_ref) | copy-start | bytes 3145732
  97.5 19.6 %collective-permute-start.2 = (bf16[8,256]{1,0:T(8,128)(2,1)S(1)}, bf16[8,256]{1,0:T(8,128)(2,1)S(1)}, u32[]{:S(2)}, u32[]{:S(2)}) collective-permute-start(bf16[8,256]{1,0:T(8,128)(2,1)S(1)} %bitcast.165), channel_id=1, source_target_pairs={{0,1},{1,0},{2,3},{3,2},{4,5},{5,4},{6,7},{7,6},{8,9},{9,8},{10,11... | collective-permute-start | bytes 12296 | tf_op jit(solution)/shard_map/ppermute | solution.py:192
  117.2 23.8 %collective-permute-start.9 = (bf16[16,256]{1,0:T(8,128)(2,1)S(1)}, bf16[16,256]{1,0:T(8,128)(2,1)S(1)}, u32[]{:S(2)}, u32[]{:S(2)}) collective-permute-start(bf16[16,256]{1,0:T(8,128)(2,1)S(1)} %fusion.19), channel_id=1, source_target_pairs={{0,14},{2,0},{4,2},{6,4},{8,6},{10,8},{12,10},{14,12},{1,15},{3,1}... | collective-permute-start | bytes 24584 | tf_op jit(solution)/shard_map/ppermute | solution.py:198
  119.3 21.7 %collective-permute-start.8 = (bf16[16,256]{1,0:T(8,128)(2,1)S(1)}, bf16[16,256]{1,0:T(8,128)(2,1)S(1)}, u32[]{:S(2)}, u32[]{:S(2)}) collective-permute-start(bf16[16,256]{1,0:T(8,128)(2,1)S(1)} %fusion.19), channel_id=1, source_target_pairs={{0,12},{2,14},{4,0},{6,2},{8,4},{10,6},{12,8},{14,10},{1,13},{3,15... | collective-permute-start | bytes 24584 | tf_op jit(solution)/shard_map/ppermute | solution.py:198
  119.4 21.6 %collective-permute-start.7 = (bf16[16,256]{1,0:T(8,128)(2,1)S(1)}, bf16[16,256]{1,0:T(8,128)(2,1)S(1)}, u32[]{:S(2)}, u32[]{:S(2)}) collective-permute-start(bf16[16,256]{1,0:T(8,128)(2,1)S(1)} %fusion.19), channel_id=1, source_target_pairs={{0,10},{2,12},{4,14},{6,0},{8,2},{10,4},{12,6},{14,8},{1,11},{3,13... | collective-permute-start | bytes 24584 | tf_op jit(solution)/shard_map/ppermute | solution.py:198
  120.7 20.3 %collective-permute-start.6 = (bf16[16,256]{1,0:T(8,128)(2,1)S(1)}, bf16[16,256]{1,0:T(8,128)(2,1)S(1)}, u32[]{:S(2)}, u32[]{:S(2)}) collective-permute-start(bf16[16,256]{1,0:T(8,128)(2,1)S(1)} %fusion.19), channel_id=1, source_target_pairs={{0,8},{2,10},{4,12},{6,14},{8,0},{10,2},{12,4},{14,6},{1,9},{3,11}... | collective-permute-start | bytes 24584 | tf_op jit(solution)/shard_map/ppermute | solution.py:198
  123.7 6.3 %collective-permute-start.3 = (bf16[16,256]{1,0:T(8,128)(2,1)S(1)}, bf16[16,256]{1,0:T(8,128)(2,1)S(1)}, u32[]{:S(2)}, u32[]{:S(2)}) collective-permute-start(bf16[16,256]{1,0:T(8,128)(2,1)S(1)} %fusion.19), channel_id=1, source_target_pairs={{0,2},{2,4},{4,6},{6,8},{8,10},{10,12},{12,14},{14,0},{1,3},{3,5},... | collective-permute-start | bytes 24584 | tf_op jit(solution)/shard_map/ppermute | solution.py:198
  130.1 5.4 %collective-permute-start.4 = (bf16[16,256]{1,0:T(8,128)(2,1)S(1)}, bf16[16,256]{1,0:T(8,128)(2,1)S(1)}, u32[]{:S(2)}, u32[]{:S(2)}) collective-permute-start(bf16[16,256]{1,0:T(8,128)(2,1)S(1)} %fusion.19), channel_id=1, source_target_pairs={{0,4},{2,6},{4,8},{6,10},{8,12},{10,14},{12,0},{14,2},{1,5},{3,7},... | collective-permute-start | bytes 24584 | tf_op jit(solution)/shard_map/ppermute | solution.py:198
  135.5 5.4 %collective-permute-start.5 = (bf16[16,256]{1,0:T(8,128)(2,1)S(1)}, bf16[16,256]{1,0:T(8,128)(2,1)S(1)}, u32[]{:S(2)}, u32[]{:S(2)}) collective-permute-start(bf16[16,256]{1,0:T(8,128)(2,1)S(1)} %fusion.19), channel_id=1, source_target_pairs={{0,6},{2,8},{4,10},{6,12},{8,14},{10,0},{12,2},{14,4},{1,7},{3,9},... | collective-permute-start | bytes 24584 | tf_op jit(solution)/shard_map/ppermute | solution.py:198
  146.2 13.3 %copy-start.6 = (s32[8]{0:T(128)S(1)}, s32[8]{0:T(128)}, u32[]{:S(2)}) copy-start(s32[8]{0:T(128)} %constant.209.clone) | copy-start | bytes 100
  146.2 21.1 %copy-start.4 = (s32[8]{0:T(128)S(1)}, s32[8]{0:T(128)}, u32[]{:S(2)}) copy-start(s32[8]{0:T(128)} %constant.210.clone) | copy-start | bytes 100
  146.2 33.2 %copy-start.5 = (s32[2]{0:T(128)S(1)}, s32[2]{0:T(128)}, u32[]{:S(2)}) copy-start(s32[2]{0:T(128)} %param.17) | copy-start | bytes 28
  152.6 33.7 %copy-start.3 = (bf16[128,4096]{1,0:T(8,128)(2,1)S(1)}, bf16[128,4096]{1,0:T(8,128)(2,1)}, u32[]{:S(2)}) copy-start(bf16[128,4096]{1,0:T(8,128)(2,1)} %get-tuple-element.19) | copy-start | bytes 3145732
  152.6 33.7 %collective-permute-start.18 = (bf16[128,4096]{1,0:T(8,128)(2,1)}, bf16[128,4096]{1,0:T(8,128)(2,1)}, u32[]{:S(2)}, u32[]{:S(2)}) collective-permute-start(bf16[128,4096]{1,0:T(8,128)(2,1)} %get-tuple-element.20), channel_id=1, source_target_pairs={{0,1},{1,0},{2,3},{3,2},{4,5},{5,4},{6,7},{7,6},{8,9},{9,8},{10,11... | collective-permute-start | bytes 3145736 | tf_op jit(solution)/shard_map/ppermute | solution.py:214
  159.0 30.3 %collective-permute-start.10 = (bf16[128,4096]{1,0:T(8,128)(2,1)}, bf16[128,4096]{1,0:T(8,128)(2,1)S(1)}, u32[]{:S(2)}, u32[]{:S(2)}) collective-permute-start(bf16[128,4096]{1,0:T(8,128)(2,1)} %get-tuple-element.18), channel_id=1, source_target_pairs={{0,1},{1,0},{2,3},{3,2},{4,5},{5,4},{6,7},{7,6},{8,9},{9,8},{10,11... | collective-permute-start | bytes 3145736 | tf_op jit(solution)/shard_map/ppermute | solution.py:214
  187.3 5.7 %collective-permute-start.19 = (bf16[16,4096]{1,0:T(8,128)(2,1)S(1)}, bf16[16,4096]{1,0:T(8,128)(2,1)S(1)}, u32[]{:S(2)}, u32[]{:S(2)}) collective-permute-start(bf16[16,4096]{1,0:T(8,128)(2,1)S(1)} %get-tuple-element.27), channel_id=1, source_target_pairs={{0,4},{4,8},{8,12},{12,14},{14,10},{10,6},{6,2},{2,0},{1,5},{5,9},... | collective-permute-start | bytes 393224 | tf_op jit(solution)/shard_map/ppermute | solution.py:232
  187.4 9.6 %collective-permute-start.22 = (bf16[16,4096]{1,0:T(8,128)(2,1)S(1)}, bf16[16,4096]{1,0:T(8,128)(2,1)S(1)}, u32[]{:S(2)}, u32[]{:S(2)}) collective-permute-start(bf16[16,4096]{1,0:T(8,128)(2,1)S(1)} %get-tuple-element.28), channel_id=1, source_target_pairs={{4,0},{8,4},{12,8},{14,12},{10,14},{6,10},{2,6},{0,2},{5,1},{9,5},... | collective-permute-start | bytes 393224 | tf_op jit(solution)/shard_map/ppermute | solution.py:232
  190.4 5.2 %collective-permute-start.11 = (bf16[16,4096]{1,0:T(8,128)(2,1)S(1)}, bf16[16,4096]{1,0:T(8,128)(2,1)S(1)}, u32[]{:S(2)}, u32[]{:S(2)}) collective-permute-start(bf16[16,4096]{1,0:T(8,128)(2,1)S(1)} %get-tuple-element.23), channel_id=1, source_target_pairs={{0,4},{4,8},{8,12},{12,14},{14,10},{10,6},{6,2},{2,0},{1,5},{5,9},... | collective-permute-start | bytes 393224 | tf_op jit(solution)/shard_map/ppermute | solution.py:232
  190.5 19.4 %collective-permute-start.15 = (bf16[16,4096]{1,0:T(8,128)(2,1)S(1)}, bf16[16,4096]{1,0:T(8,128)(2,1)S(1)}, u32[]{:S(2)}, u32[]{:S(2)}) collective-permute-start(bf16[16,4096]{1,0:T(8,128)(2,1)S(1)} %get-tuple-element.24), channel_id=1, source_target_pairs={{4,0},{8,4},{12,8},{14,12},{10,14},{6,10},{2,6},{0,2},{5,1},{9,5},... | collective-permute-start | bytes 393224 | tf_op jit(solution)/shard_map/ppermute | solution.py:232
  194.0 6.0 %collective-permute-start.20 = (bf16[16,4096]{1,0:T(8,128)(2,1)S(1)}, bf16[16,4096]{1,0:T(8,128)(2,1)S(1)}, u32[]{:S(2)}, u32[]{:S(2)}) collective-permute-start(bf16[16,4096]{1,0:T(8,128)(2,1)S(1)} %fusion.4), channel_id=1, source_target_pairs={{0,4},{4,8},{8,12},{12,14},{14,10},{10,6},{6,2},{2,0},{1,5},{5,9},... | collective-permute-start | bytes 393224 | tf_op jit(solution)/shard_map/ppermute | solution.py:232
  196.6 6.5 %collective-permute-start.12 = (bf16[16,4096]{1,0:T(8,128)(2,1)S(1)}, bf16[16,4096]{1,0:T(8,128)(2,1)S(1)}, u32[]{:S(2)}, u32[]{:S(2)}) collective-permute-start(bf16[16,4096]{1,0:T(8,128)(2,1)S(1)} %fusion.9), channel_id=1, source_target_pairs={{0,4},{4,8},{8,12},{12,14},{14,10},{10,6},{6,2},{2,0},{1,5},{5,9},... | collective-permute-start | bytes 393224 | tf_op jit(solution)/shard_map/ppermute | solution.py:232
  201.0 18.5 %collective-permute-start.21 = (bf16[16,4096]{1,0:T(8,128)(2,1)S(1)}, bf16[16,4096]{1,0:T(8,128)(2,1)S(1)}, u32[]{:S(2)}, u32[]{:S(2)}) collective-permute-start(bf16[16,4096]{1,0:T(8,128)(2,1)S(1)} %get-tuple-element.25), channel_id=1, source_target_pairs={{0,4},{4,8},{8,12},{12,14},{14,10},{10,6},{6,2},{2,0},{1,5},{5,9},... | collective-permute-start | bytes 393224 | tf_op jit(solution)/shard_map/ppermute | solution.py:232
  201.1 5.4 %collective-permute-start.23 = (bf16[16,4096]{1,0:T(8,128)(2,1)S(1)}, bf16[16,4096]{1,0:T(8,128)(2,1)S(1)}, u32[]{:S(2)}, u32[]{:S(2)}) collective-permute-start(bf16[16,4096]{1,0:T(8,128)(2,1)S(1)} %get-tuple-element.26), channel_id=1, source_target_pairs={{4,0},{8,4},{12,8},{14,12},{10,14},{6,10},{2,6},{0,2},{5,1},{9,5},... | collective-permute-start | bytes 393224 | tf_op jit(solution)/shard_map/ppermute | solution.py:232
  204.1 5.9 %collective-permute-start.13 = (bf16[16,4096]{1,0:T(8,128)(2,1)S(1)}, bf16[16,4096]{1,0:T(8,128)(2,1)S(1)}, u32[]{:S(2)}, u32[]{:S(2)}) collective-permute-start(bf16[16,4096]{1,0:T(8,128)(2,1)S(1)} %fusion.10), channel_id=1, source_target_pairs={{0,4},{4,8},{8,12},{12,14},{14,10},{10,6},{6,2},{2,0},{1,5},{5,9},... | collective-permute-start | bytes 393224 | tf_op jit(solution)/shard_map/ppermute | solution.py:232
  207.5 6.4 %collective-permute-start.24 = (bf16[16,4096]{1,0:T(8,128)(2,1)S(1)}, bf16[16,4096]{1,0:T(8,128)(2,1)S(1)}, u32[]{:S(2)}, u32[]{:S(2)}) collective-permute-start(bf16[16,4096]{1,0:T(8,128)(2,1)S(1)} %fusion.2), channel_id=1, source_target_pairs={{4,0},{8,4},{12,8},{14,12},{10,14},{6,10},{2,6},{0,2},{5,1},{9,5},... | collective-permute-start | bytes 393224 | tf_op jit(solution)/shard_map/ppermute | solution.py:232
  211.1 9.9 %collective-permute-start.14 = (bf16[16,4096]{1,0:T(8,128)(2,1)S(1)}, bf16[16,4096]{1,0:T(8,128)(2,1)S(1)}, u32[]{:S(2)}, u32[]{:S(2)}) collective-permute-start(bf16[16,4096]{1,0:T(8,128)(2,1)S(1)} %get-tuple-element.21), channel_id=1, source_target_pairs={{0,4},{4,8},{8,12},{12,14},{14,10},{10,6},{6,2},{2,0},{1,5},{5,9},... | collective-permute-start | bytes 393224 | tf_op jit(solution)/shard_map/ppermute | solution.py:232
  211.1 6.3 %collective-permute-start.16 = (bf16[16,4096]{1,0:T(8,128)(2,1)S(1)}, bf16[16,4096]{1,0:T(8,128)(2,1)S(1)}, u32[]{:S(2)}, u32[]{:S(2)}) collective-permute-start(bf16[16,4096]{1,0:T(8,128)(2,1)S(1)} %get-tuple-element.22), channel_id=1, source_target_pairs={{4,0},{8,4},{12,8},{14,12},{10,14},{6,10},{2,6},{0,2},{5,1},{9,5},... | collective-permute-start | bytes 393224 | tf_op jit(solution)/shard_map/ppermute | solution.py:232
  214.9 5.1 %collective-permute-start.25 = (bf16[16,4096]{1,0:T(8,128)(2,1)S(1)}, bf16[16,4096]{1,0:T(8,128)(2,1)S(1)}, u32[]{:S(2)}, u32[]{:S(2)}) collective-permute-start(bf16[16,4096]{1,0:T(8,128)(2,1)S(1)} %fusion.3), channel_id=1, source_target_pairs={{4,0},{8,4},{12,8},{14,12},{10,14},{6,10},{2,6},{0,2},{5,1},{9,5},... | collective-permute-start | bytes 393224 | tf_op jit(solution)/shard_map/ppermute | solution.py:232
  218.4 5.0 %collective-permute-start.17 = (bf16[16,4096]{1,0:T(8,128)(2,1)S(1)}, bf16[16,4096]{1,0:T(8,128)(2,1)S(1)}, u32[]{:S(2)}, u32[]{:S(2)}) collective-permute-start(bf16[16,4096]{1,0:T(8,128)(2,1)S(1)} %fusion.8), channel_id=1, source_target_pairs={{4,0},{8,4},{12,8},{14,12},{10,14},{6,10},{2,6},{0,2},{5,1},{9,5},... | collective-permute-start | bytes 393224 | tf_op jit(solution)/shard_map/ppermute | solution.py:232
Sparse Core Ops, SparseCore 0:
  9.5 42.8 all-gather.2
  54.5 38.8 all-gather.4

commit v2 on v0

v2 whole, which is shorter than its diff:
```python
import functools

import jax
import jax.numpy as jnp
import numpy as np
from jax import lax
from jax.experimental import pallas as pl
from jax.experimental.pallas import tpu as pltpu
from jax.sharding import PartitionSpec as P

F32 = jnp.float32
BF16 = jnp.bfloat16
VMEM_LIMIT = 40 * 1024 * 1024


def largest_tile(size, limit):
    tile = limit
    while size % tile:
        tile //= 2
    return tile


def params():
    return pltpu.CompilerParams(vmem_limit_bytes=VMEM_LIMIT)


def cost(flops, moved):
    return pl.CostEstimate(flops=flops, bytes_accessed=moved, transcendentals=0)


def ring_of(chips):
    return list(range(0, chips, 2)) + list(range(chips - 1, 0, -2))


def layout(members, rows, block_rows):
    chips = members // 2
    ring = ring_of(chips)
    reach = chips // 2
    table = []
    for device in range(members):
        chip, core = divmod(device, 2)
        place = ring.index(chip)

        def row(side, distance, half):
            sign = 1 if side == 0 else -1
            return (2 * ring[(place + sign * distance) % chips] + half) * rows

        arrive = [row(core, 0, core), row(core, 0, 1 - core)]
        for side in (core, 1 - core):
            for step in range(1, reach + 1):
                arrive.append(row(1 - side, step, side))
                if step < reach:
                    arrive.append(row(1 - side, step, 1 - side))
        leave = []
        for side in (core, 1 - core):
            leave.append(row(side, reach, side))
            for step in range(reach - 1, 0, -1):
                leave += [row(side, step, side), row(side, step, 1 - side)]
            leave.append(row(side, 0, side))
        own = device * rows
        table.append(arrive + leave + [own // block_rows, own % block_rows, device])
    return np.asarray(table, np.int32)


def around(members):
    ring = ring_of(members // 2)
    size = len(ring)
    pairs = []
    for i in range(size):
        pairs.append((2 * ring[i], 2 * ring[(i + 1) % size]))
        pairs.append((2 * ring[i] + 1, 2 * ring[i - 1] + 1))
    return pairs


def crossing(members, bit):
    return [(i, i ^ bit) for i in range(members)]


def rank_kernel(members, blocks, table_ref, ids_ref, *refs):
    pieces, shrinks = refs[:members], refs[members : members + blocks]
    all_ref, rank_ref, total = refs[members + blocks :]
    step = pl.program_id(0)
    rows = pieces[0].shape[0]
    for index, piece in enumerate(pieces):
        start = pl.multiple_of(table_ref[index], rows)
        all_ref[pl.ds(start, rows), :] = piece[...]
    span = all_ref.shape[0] // blocks
    parts = [
        lax.dot_general(
            shrinks[b][0],
            all_ref[b * span : (b + 1) * span, :],
            (((1,), (1,)), ((), ())),
            preferred_element_type=F32,
        )
        for b in range(blocks)
    ]
    part = jnp.concatenate(parts, axis=1)

    @pl.when(step == 0)
    def _():
        total[...] = part

    @pl.when(step > 0)
    def _():
        total[...] += part

    rank_ref[...] = total[...].astype(BF16)


def rank_and_rows(table, adapters, pieces, shrink):
    members = len(pieces)
    rows, model = pieces[0].shape
    blocks = adapters.shape[0]
    span = shrink.shape[1]
    total = members * rows
    tile = largest_tile(model, 1024)

    def chosen(b):
        return pl.BlockSpec((1, span, tile), lambda k, table, ids: (ids[b], 0, k))

    return pl.pallas_call(
        functools.partial(rank_kernel, members, blocks),
        grid_spec=pltpu.PrefetchScalarGridSpec(
            num_scalar_prefetch=2,
            grid=(model // tile,),
            in_specs=[pl.BlockSpec((rows, tile), lambda k, table, ids: (0, k))] * members
            + [chosen(b) for b in range(blocks)],
            out_specs=[
                pl.BlockSpec((total, tile), lambda k, table, ids: (0, k)),
                pl.BlockSpec((span, total), lambda k, table, ids: (0, 0)),
            ],
            scratch_shapes=[pltpu.VMEM((span, total), F32)],
        ),
        out_shape=[
            jax.ShapeDtypeStruct((total, model), BF16),
            jax.ShapeDtypeStruct((span, total), BF16),
        ],
        compiler_params=params(),
        cost_estimate=cost(2 * total * model * span, 4 * total * model),
        name="rank",
    )(table, adapters, *pieces, *([shrink] * blocks))


def product_kernel(rows_ref, *refs):
    w_refs, out_ref = refs[:-1], refs[-1]
    depth = w_refs[0].shape[0]
    part = 0.0
    for index, w_ref in enumerate(w_refs):
        columns = rows_ref[:, index * depth : (index + 1) * depth]
        part += jnp.dot(columns, w_ref[...], preferred_element_type=F32)

    @pl.when(pl.program_id(0) == 0)
    def _():
        out_ref[...] = part

    @pl.when(pl.program_id(0) > 0)
    def _():
        out_ref[...] += part


def product(tokens, matrix, part, parts):
    total, model = tokens.shape
    width = matrix.shape[1]
    depth = model // parts
    tile = largest_tile(depth, 1024)
    steps = depth // tile
    split = 4

    def piece(index):
        return pl.BlockSpec(
            (tile // split, width), lambda k: ((k + part * steps) * split + index, 0)
        )

    return pl.pallas_call(
        product_kernel,
        grid=(steps,),
        in_specs=[pl.BlockSpec((total, tile), lambda k: (0, k + part * steps))]
        + [piece(index) for index in range(split)],
        out_specs=pl.BlockSpec((total, width), lambda k: (0, 0)),
        out_shape=jax.ShapeDtypeStruct((total, width), F32),
        compiler_params=params(),
        cost_estimate=cost(2 * total * depth * width, 2 * depth * (width + total)),
        name="product",
    )(tokens, *([matrix] * split))


def finish_kernel(parts, span, table_ref, ids_ref, *refs):
    g_refs, u_refs = refs[:parts], refs[parts : 2 * parts]
    rank_ref, expand_ref, hidden_ref = refs[2 * parts :]
    ranks = rank_ref.shape[0]
    device = table_ref[table_ref.shape[0] - 1]
    shape = (ranks, ranks)
    want = lax.broadcasted_iota(jnp.int32, shape, 0)
    have = lax.broadcasted_iota(jnp.int32, shape, 1)
    origin = ((have // span) ^ device) * span + have % span
    order = jnp.where(want == origin, 1.0, 0.0).astype(BF16)
    rank = jnp.dot(order, rank_ref[...], preferred_element_type=F32).T.astype(BF16)
    half = ranks // 2
    gate = jnp.dot(rank[:, :half], expand_ref[0, :half], preferred_element_type=F32)
    up = jnp.dot(rank[:, half:], expand_ref[0, half:], preferred_element_type=F32)
    for g_ref in g_refs:
        gate += g_ref[...]
    for u_ref in u_refs:
        up += u_ref[...]
    hidden_ref[...] = (gate / (1.0 + jnp.exp(-gate)) * up).astype(BF16)


def finish(table, adapters, gates, ups, rank, expand, span):
    blocks = adapters.shape[0]
    total, width = gates[0].shape
    rows = total // blocks
    ranks = rank.shape[0]
    parts = len(gates)
    wide = pl.BlockSpec((rows, width), lambda b, table, ids: (b, 0))
    return pl.pallas_call(
        functools.partial(finish_kernel, parts, span),
        grid_spec=pltpu.PrefetchScalarGridSpec(
            num_scalar_prefetch=2,
            grid=(blocks,),
            in_specs=[wide] * (2 * parts)
            + [
                pl.BlockSpec((ranks, rows), lambda b, table, ids: (0, b)),
                pl.BlockSpec((1, ranks, width), lambda b, table, ids: (ids[b], 0, 0)),
            ],
            out_specs=wide,
        ),
        out_shape=jax.ShapeDtypeStruct((total, width), BF16),
        compiler_params=params(),
        name="finish",
    )(table, adapters, *gates, *ups, rank, expand)


def down_kernel(first, groups, rows, split, table_ref, hidden_ref, *refs):
    w_refs, outs, product_ref = refs[:split], refs[split:-1], refs[-1]
    depth = w_refs[0].shape[0]
    part = 0.0
    for index, w_ref in enumerate(w_refs):
        columns = hidden_ref[:, index * depth : (index + 1) * depth]
        part += jnp.dot(columns, w_ref[...], preferred_element_type=F32)
    product_ref[...] = part.astype(BF16)
    at = first
    for out, group in zip(outs, groups, strict=True):
        for index in range(group):
            start = pl.multiple_of(table_ref[at], rows)
            out[index * rows : (index + 1) * rows, :] = product_ref[pl.ds(start, rows), :]
            at += 1


def down(table, first, hidden, down_matrix, groups, rows):
    total, depth = hidden.shape
    columns = down_matrix.shape[1]
    tile = largest_tile(columns, 1024)
    split = max(s for s in (1, 2, 4, 7) if depth % (s * 128) == 0 or s == 1)

    def piece(index):
        return pl.BlockSpec((depth // split, tile), lambda n, table: (index, n))

    return pl.pallas_call(
        functools.partial(down_kernel, first, groups, rows, split),
        grid_spec=pltpu.PrefetchScalarGridSpec(
            num_scalar_prefetch=1,
            grid=(columns // tile,),
            in_specs=[
                pl.BlockSpec((total, depth), lambda n, table: (0, 0)),
            ]
            + [piece(index) for index in range(split)],
            out_specs=[
                pl.BlockSpec((group * rows, tile), lambda n, table: (0, n)) for group in groups
            ],
            scratch_shapes=[pltpu.VMEM((total, tile), BF16)],
        ),
        out_shape=[jax.ShapeDtypeStruct((group * rows, columns), BF16) for group in groups],
        compiler_params=params(),
        cost_estimate=cost(
            2 * total * depth * columns, 2 * depth * columns + 2 * total * columns
        ),
        name="down",
    )(table, hidden, *([down_matrix] * split))


def last_kernel(table_ref, counts_ref, *refs):
    out_ref = refs[-1]
    summed = refs[0][...].astype(F32)
    for ref in refs[1:-1]:
        summed += ref[...].astype(F32)
    size = table_ref.shape[0]
    live = counts_ref[table_ref[size - 3]] - table_ref[size - 2]
    row = lax.broadcasted_iota(jnp.int32, summed.shape, 0)
    out_ref[...] = jnp.where(row < live, summed, 0.0).astype(BF16)


def last(table, counts, terms):
    shape = terms[0].shape
    return pl.pallas_call(
        last_kernel,
        grid_spec=pltpu.PrefetchScalarGridSpec(
            num_scalar_prefetch=2,
            grid=(1,),
            in_specs=[pl.BlockSpec(shape, lambda i, table, counts: (0, 0))] * len(terms),
            out_specs=pl.BlockSpec(shape, lambda i, table, counts: (0, 0)),
        ),
        out_shape=jax.ShapeDtypeStruct(shape, BF16),
        compiler_params=params(),
        name="last",
    )(table, counts, *terms)


def added(*terms):
    total = terms[0].astype(F32)
    for term in terms[1:]:
        total = total + term.astype(F32)
    return total.astype(BF16)


def per_device(
    members,
    tokens,
    gate_matrix,
    up_matrix,
    down_matrix,
    shrink_matrices,
    expand_matrices,
    adapter_per_block,
    block_token_count,
):
    rows, model = tokens.shape
    blocks = adapter_per_block.shape[0]
    span = shrink_matrices.shape[2]
    reach = members // 4
    block_rows = members * rows // blocks
    table = jnp.asarray(layout(members, rows, block_rows))[lax.axis_index("tp")]
    ring = around(members)
    swap = crossing(members, 1)

    def step(x):
        return lax.ppermute(x, "tp", ring)

    def cross(x, bit=1):
        return lax.ppermute(x, "tp", crossing(members, bit))

    first, second = tokens, cross(tokens)
    pieces, mine, theirs = [first, second], [], []
    for distance in range(1, reach + 1):
        first = step(first)
        mine.append(first)
        theirs.append(cross(first))
        if distance < reach:
            second = step(second)
            mine.append(second)
            theirs.append(cross(second))
    pieces = pieces + mine + theirs

    shrink = jnp.swapaxes(shrink_matrices, 1, 2)
    everyone, rank = rank_and_rows(table, adapter_per_block, pieces, shrink)
    bit = 1
    while bit < members:
        rank = jnp.concatenate([rank, cross(rank, bit)], axis=0)
        bit *= 2

    parts = 2
    gates = [product(everyone, gate_matrix, part, parts) for part in range(parts)]
    ups = [product(everyone, up_matrix, part, parts) for part in range(parts)]
    hidden = finish(table, adapter_per_block, gates, ups, rank, expand_matrices, span)

    slots = 2 * reach
    groups = [1] * slots + [1] + [2] * (reach - 1) + [1]
    outs = down(table, members, hidden, down_matrix, groups, rows)
    keep, give = outs[:slots], outs[slots:]
    came = [cross(x) for x in give]
    first = step(added(keep[0], came[0]))
    second = None
    for index in range(1, reach):
        pair = came[index]
        here = [keep[2 * index], pair[rows:]] + ([] if second is None else [second])
        second = step(added(*here))
        first = step(added(keep[2 * index - 1], pair[:rows], first))
    return last(table, block_token_count, [keep[-1], came[-1], first, cross(second)])


def solution(mesh):
    members = mesh.shape["tp"]
    return jax.shard_map(
        functools.partial(per_device, members),
        mesh=mesh,
        in_specs=(
            P(("rep", "tp"), None),
            P(None, "tp"),
            P(None, "tp"),
            P("tp", None),
            P("rep", None, "tp"),
            P("rep", None, "tp"),
            P("rep"),
            P("rep"),
        ),
        out_specs=P(("rep", "tp"), None),
        check_vma=False,
    )
```

time: 199 us -> 127 us (0.64)
  waiting for transfers between devices: 123 us -> 39.8 us
  Pallas kernels: 0 us -> 44.5 us
  matrix products: 38.1 us -> 0 us
  starting transfers between devices: 0.04 us -> 37.1 us
  blocking collectives: 19.1 us -> 0 us
  between operations: 13.4 us -> 0.15 us
  other arithmetic: 3.3 us -> 0.62 us
  local copies, waits for them, and re-layouts: 1.4 us -> 3.54 us
    reduce_scatter x1 -> x0, waiting for transfers between devices: 69.2 us -> none  [per_device(): lax.psum_scatter(jnp.dot(hidden, down_matrix, preferred_element_type=jnp....]
    all_gather x1 -> x0, waiting for transfers between devices: 53.4 us -> none  [per_device(): local_row_slice = lax.all_gather(tokens, 'tp', axis=0, tiled=True)]
    pallas_call x0 -> x8, Pallas kernels: none -> 44.5 us  [the longest x4 22.8 us: product(): pl.pallas_call(product_kernel, grid=(steps,), in_specs=[pl.BlockSpec((tot...]
    ppermute x0 -> x32, waiting for transfers between devices: none -> 39.8 us  [the longest x14 31.5 us: step(): return lax.ppermute(x, 'tp', ring)]
    ppermute x0 -> x32, starting transfers between devices: none -> 37.1 us  [the longest x14 27.4 us: step(): return lax.ppermute(x, 'tp', ring)]
    dot_general x4 -> x0, matrix products: 34.2 us -> none  [the longest x1 21.6 us: per_device(): jnp.dot(hidden, down_matrix, preferred_element_type=jnp.float32)]
    all_gather x1 -> x0, blocking collectives: 19.1 us -> none  [per_device(): rank_full = lax.all_gather(rank_local, 'tp', axis=1, tiled=True)]
    unnamed x1 -> x0, matrix products: 3.88 us -> none
  transfers between devices with their start and end apart: 2 -> 32, of which waited for: 2 -> 20; matrix products, arithmetic and copies ran while one was open for 1% -> 1% of each run, Pallas kernels for 0% -> 0%
where the time goes in v2:
time: 127 us; the launch traced here: 126 us
  Pallas kernels  44.5 us (35%)
  waiting for transfers between devices  39.8 us (31%)
  starting transfers between devices  37.1 us (29%)
  local copies, waits for them, and re-layouts  3.54 us (3%)
    ppermute x14, waiting for transfers between devices, step(): return lax.ppermute(x, 'tp', ring)  31.5 us
    ppermute x14, starting transfers between devices, step(): return lax.ppermute(x, 'tp', ring)  27.4 us
    pallas_call x4, Pallas kernels, product(): pl.pallas_call(product_kernel, grid=(steps,), in_specs=[pl.BlockSpec((tot...  22.8 us
    pallas_call x1, Pallas kernels, down(): pl.pallas_call(functools.partial(down_kernel, first, groups, rows, split)...  12.6 us
    ppermute x18, starting transfers between devices, cross(): return lax.ppermute(x, 'tp', crossing(members, bit))  9.77 us
    ppermute x18, waiting for transfers between devices, cross(): return lax.ppermute(x, 'tp', crossing(members, bit))  8.26 us
    pallas_call x1, Pallas kernels, rank_and_rows(): pl.pallas_call(functools.partial(rank_kernel, members, blocks), grid_spec...  5.95 us
    unnamed x14, local copies, waits for them, and re-layouts  2.85 us
  transfers between devices with their start and end apart: 32, of which 20 were waited for; matrix products, arithmetic and copies ran while one was open for 1% of the time, Pallas kernels for 0%

profile of v2, /device:TPU:0, one launch (start us, length us, event | category | flops | bytes accessed | tf_op | source)
XLA Modules:
  0.0 125.7 jit_solution(15892479963017024434)
XLA Ops:
  0.0 0.5 collective-permute-start
  0.5 2.6 %collective-permute-start.1 = (bf16[16,8192]{1,0:T(8,128)(2,1)}, bf16[16,8192]{1,0:T(8,128)(2,1)S(1)}, u32[]{:S(2)}, u32[]{:S(2)}) collective-permute-start(bf16[16,8192]{1,0:T(8,128)(2,1)} %refs_0_.6), channel_id=1, source_target_pairs={{0,4},{1,3},{4,8},{5,1},{8,12},{9,5},{12,14},{13,9},{14,10},{15,13... | collective-permute-start | bytes 786440 | tf_op jit(solution)/shard_map/ppermute | solution.py:336
  3.0 0.0 collective-permute-done.refs_1_
  3.0 1.7 %collective-permute-start.2 = (bf16[16,8192]{1,0:T(8,128)(2,1)S(1)}, bf16[16,8192]{1,0:T(8,128)(2,1)S(1)}, u32[]{:S(2)}, u32[]{:S(2)}) collective-permute-start(bf16[16,8192]{1,0:T(8,128)(2,1)S(1)} %collective-permute-done.refs_1_), channel_id=1, source_target_pairs={{0,4},{1,3},{4,8},{5,1},{8,12},{9,5},{12,14},{13,9},{14,10},{15,13... | collective-permute-start | bytes 786440 | tf_op jit(solution)/shard_map/ppermute | solution.py:336
  4.8 2.8 %collective-permute-done.1.refs_2_ = bf16[16,8192]{1,0:T(8,128)(2,1)S(1)} collective-permute-done((bf16[16,8192]{1,0:T(8,128)(2,1)}, bf16[16,8192]{1,0:T(8,128)(2,1)S(1)}, u32[]{:S(2)}, u32[]{:S(2)}) %collective-permute-start.1) | collective-permute-done | bytes 262176 | tf_op jit(solution)/shard_map/ppermute | solution.py:336
  7.5 2.1 %collective-permute-start.3 = (bf16[16,8192]{1,0:T(8,128)(2,1)S(1)}, bf16[16,8192]{1,0:T(8,128)(2,1)S(1)}, u32[]{:S(2)}, u32[]{:S(2)}) collective-permute-start(bf16[16,8192]{1,0:T(8,128)(2,1)S(1)} %collective-permute-done.1.refs_2_), channel_id=1, source_target_pairs={{0,4},{1,3},{4,8},{5,1},{8,12},{9,5},{12,14},{13,9},{14,10},{15,13... | collective-permute-start | bytes 786440 | tf_op jit(solution)/shard_map/ppermute | solution.py:336
  9.6 0.7 collective-permute-done.2.refs_3_
  10.3 2.1 %collective-permute-start.4 = (bf16[16,8192]{1,0:T(8,128)(2,1)S(1)}, bf16[16,8192]{1,0:T(8,128)(2,1)S(1)}, u32[]{:S(2)}, u32[]{:S(2)}) collective-permute-start(bf16[16,8192]{1,0:T(8,128)(2,1)S(1)} %collective-permute-done.2.refs_3_), channel_id=1, source_target_pairs={{0,4},{1,3},{4,8},{5,1},{8,12},{9,5},{12,14},{13,9},{14,10},{15,13... | collective-permute-start | bytes 786440 | tf_op jit(solution)/shard_map/ppermute | solution.py:336
  12.4 1.5 %collective-permute-done.3.refs_4_ = bf16[16,8192]{1,0:T(8,128)(2,1)S(1)} collective-permute-done((bf16[16,8192]{1,0:T(8,128)(2,1)S(1)}, bf16[16,8192]{1,0:T(8,128)(2,1)S(1)}, u32[]{:S(2)}, u32[]{:S(2)}) %collective-permute-start.3) | collective-permute-done | bytes 262176 | tf_op jit(solution)/shard_map/ppermute | solution.py:336
  13.9 2.1 %collective-permute-start.5 = (bf16[16,8192]{1,0:T(8,128)(2,1)S(1)}, bf16[16,8192]{1,0:T(8,128)(2,1)S(1)}, u32[]{:S(2)}, u32[]{:S(2)}) collective-permute-start(bf16[16,8192]{1,0:T(8,128)(2,1)S(1)} %collective-permute-done.3.refs_4_), channel_id=1, source_target_pairs={{0,4},{1,3},{4,8},{5,1},{8,12},{9,5},{12,14},{13,9},{14,10},{15,13... | collective-permute-start | bytes 786440 | tf_op jit(solution)/shard_map/ppermute | solution.py:336
  16.0 0.5 collective-permute-start.9
  16.5 0.2 collective-permute-done.4.refs_5_
  16.7 2.1 %collective-permute-start.6 = (bf16[16,8192]{1,0:T(8,128)(2,1)S(1)}, bf16[16,8192]{1,0:T(8,128)(2,1)S(1)}, u32[]{:S(2)}, u32[]{:S(2)}) collective-permute-start(bf16[16,8192]{1,0:T(8,128)(2,1)S(1)} %collective-permute-done.4.refs_5_), channel_id=1, source_target_pairs={{0,4},{1,3},{4,8},{5,1},{8,12},{9,5},{12,14},{13,9},{14,10},{15,13... | collective-permute-start | bytes 786440 | tf_op jit(solution)/shard_map/ppermute | solution.py:336
  18.8 1.5 %collective-permute-done.5.refs_6_ = bf16[16,8192]{1,0:T(8,128)(2,1)S(1)} collective-permute-done((bf16[16,8192]{1,0:T(8,128)(2,1)S(1)}, bf16[16,8192]{1,0:T(8,128)(2,1)S(1)}, u32[]{:S(2)}, u32[]{:S(2)}) %collective-permute-start.5) | collective-permute-done | bytes 262176 | tf_op jit(solution)/shard_map/ppermute | solution.py:336
  20.3 2.1 %collective-permute-start.7 = (bf16[16,8192]{1,0:T(8,128)(2,1)S(1)}, bf16[16,8192]{1,0:T(8,128)(2,1)S(1)}, u32[]{:S(2)}, u32[]{:S(2)}) collective-permute-start(bf16[16,8192]{1,0:T(8,128)(2,1)S(1)} %collective-permute-done.5.refs_6_), channel_id=1, source_target_pairs={{0,4},{1,3},{4,8},{5,1},{8,12},{9,5},{12,14},{13,9},{14,10},{15,13... | collective-permute-start | bytes 786440 | tf_op jit(solution)/shard_map/ppermute | solution.py:336
  22.4 0.5 collective-permute-start.11
  22.9 0.1 collective-permute-start.12
  22.9 0.1 collective-permute-done.6.refs_7_
  23.1 0.3 collective-permute-start.13
  23.4 3.3 %collective-permute-done.7.refs_8_ = bf16[16,8192]{1,0:T(8,128)(2,1)S(1)} collective-permute-done((bf16[16,8192]{1,0:T(8,128)(2,1)S(1)}, bf16[16,8192]{1,0:T(8,128)(2,1)S(1)}, u32[]{:S(2)}, u32[]{:S(2)}) %collective-permute-start.7) | collective-permute-done | bytes 262176 | tf_op jit(solution)/shard_map/ppermute | solution.py:336
  26.7 0.7 dynamic-slice_bitcast_fusion.table_ref
  27.4 0.9 collective-permute-done.14.refs_15_
  28.3 1.2 copy-done
  29.5 0.9 copy-done.2
  30.5 0.7 copy-done.3
  31.1 6.0 %rank.1 = (bf16[256,8192]{1,0:T(8,128)(2,1)S(1)}, bf16[8,256]{1,0:T(8,128)(2,1)S(1)}) custom-call(s32[35]{0:T(128)S(1)} %dynamic-slice_bitcast_fusion.table_ref, s32[2]{0:T(128)S(1)} %copy-done.3, bf16[16,8192]{1,0:T(8,128)(2,1)S(1)} %copy-done.2, bf16[16,8192]{1,0:T(8,128)(2,1)S(1)} %collective-permute-done.refs_1_, ...), custom_call_target="tpu_custom_call" | custom-call | flops 33554432 | bytes 8388608 | tf_op jit(solution)/shard_map/rank/pallas_call | solution.py:121
  37.1 5.7 %product.7.refs_3_ = f32[256,896]{1,0:T(8,128)S(1)} custom-call(bf16[256,8192]{1,0:T(8,128)(2,1)S(1)} %get-tuple-element.20.rows_ref, bf16[8192,896]{1,0:T(8,128)(2,1)} %refs_3_.8, bf16[8192,896]{1,0:T(8,128)(2,1)} %refs_3_.8, bf16[8192,896]{1,0:T(8,128)(2,1)} %refs_3_.8, bf16[8192,896]{1,0:T(8,128)(2,1)} %refs_3_.8), custom_call_target="tpu_custom_call" | custom-call | flops 1879048192 | bytes 9437184 | tf_op jit(solution)/shard_map/product/pallas_call | solution.py:174
  42.8 5.7 %product.6.refs_2_ = f32[256,896]{1,0:T(8,128)S(1)} custom-call(bf16[256,8192]{1,0:T(8,128)(2,1)S(1)} %get-tuple-element.20.rows_ref, bf16[8192,896]{1,0:T(8,128)(2,1)} %refs_3_.8, bf16[8192,896]{1,0:T(8,128)(2,1)} %refs_3_.8, bf16[8192,896]{1,0:T(8,128)(2,1)} %refs_3_.8, bf16[8192,896]{1,0:T(8,128)(2,1)} %refs_3_.8), custom_call_target="tpu_custom_call" | custom-call | flops 1879048192 | bytes 9437184 | tf_op jit(solution)/shard_map/product/pallas_call | solution.py:174
  48.5 5.7 %product.5.refs_1_ = f32[256,896]{1,0:T(8,128)S(1)} custom-call(bf16[256,8192]{1,0:T(8,128)(2,1)S(1)} %get-tuple-element.20.rows_ref, bf16[8192,896]{1,0:T(8,128)(2,1)} %refs_3_.6, bf16[8192,896]{1,0:T(8,128)(2,1)} %refs_3_.6, bf16[8192,896]{1,0:T(8,128)(2,1)} %refs_3_.6, bf16[8192,896]{1,0:T(8,128)(2,1)} %refs_3_.6), custom_call_target="tpu_custom_call" | custom-call | flops 1879048192 | bytes 9437184 | tf_op jit(solution)/shard_map/product/pallas_call | solution.py:174
  54.1 0.0 copy-start.1
  54.2 5.8 %product.4.refs_0_ = f32[256,896]{1,0:T(8,128)S(1)} custom-call(bf16[256,8192]{1,0:T(8,128)(2,1)S(1)} %get-tuple-element.20.rows_ref, bf16[8192,896]{1,0:T(8,128)(2,1)} %refs_3_.6, bf16[8192,896]{1,0:T(8,128)(2,1)} %refs_3_.6, bf16[8192,896]{1,0:T(8,128)(2,1)} %refs_3_.6, bf16[8192,896]{1,0:T(8,128)(2,1)} %refs_3_.6), custom_call_target="tpu_custom_call" | custom-call | flops 1879048192 | bytes 9437184 | tf_op jit(solution)/shard_map/product/pallas_call | solution.py:174
  60.0 0.2 collective-permute-start.15
  60.2 1.0 collective-permute-done.15
  61.2 2.0 %collective-permute-start.16 = (bf16[16,256]{1,0:T(8,128)(2,1)S(1)}, bf16[16,256]{1,0:T(8,128)(2,1)S(1)}, u32[]{:S(2)}, u32[]{:S(2)}) collective-permute-start(bf16[16,256]{1,0:T(8,128)(2,1)S(1)} %pad_maximum_fusion.2), channel_id=1, source_target_pairs={{0,2},{1,3},{2,0},{3,1},{4,6},{5,7},{6,4},{7,5},{8,10},{9,11},{10,... | collective-permute-start | bytes 24584 | tf_op jit(solution)/shard_map/ppermute | solution.py:339
  63.2 1.6 %collective-permute-done.16 = bf16[16,256]{1,0:T(8,128)(2,1)S(1)} collective-permute-done((bf16[16,256]{1,0:T(8,128)(2,1)S(1)}, bf16[16,256]{1,0:T(8,128)(2,1)S(1)}, u32[]{:S(2)}, u32[]{:S(2)}) %collective-permute-start.16) | collective-permute-done | bytes 8224 | tf_op jit(solution)/shard_map/ppermute | solution.py:339
  64.8 2.1 %collective-permute-start.17 = (bf16[32,256]{1,0:T(8,128)(2,1)S(1)}, bf16[32,256]{1,0:T(8,128)(2,1)S(1)}, u32[]{:S(2)}, u32[]{:S(2)}) collective-permute-start(bf16[32,256]{1,0:T(8,128)(2,1)S(1)} %pad_maximum_fusion.1), channel_id=1, source_target_pairs={{0,4},{1,5},{2,6},{3,7},{4,0},{5,1},{6,2},{7,3},{8,12},{9,13},{10,... | collective-permute-start | bytes 49160 | tf_op jit(solution)/shard_map/ppermute | solution.py:339
  66.9 1.7 %collective-permute-done.17 = bf16[32,256]{1,0:T(8,128)(2,1)S(1)} collective-permute-done((bf16[32,256]{1,0:T(8,128)(2,1)S(1)}, bf16[32,256]{1,0:T(8,128)(2,1)S(1)}, u32[]{:S(2)}, u32[]{:S(2)}) %collective-permute-start.17) | collective-permute-done | bytes 16416 | tf_op jit(solution)/shard_map/ppermute | solution.py:339
  68.6 3.0 %collective-permute-start.18 = (bf16[64,256]{1,0:T(8,128)(2,1)S(1)}, bf16[64,256]{1,0:T(8,128)(2,1)S(1)}, u32[]{:S(2)}, u32[]{:S(2)}) collective-permute-start(bf16[64,256]{1,0:T(8,128)(2,1)S(1)} %pad_maximum_fusion), channel_id=1, source_target_pairs={{0,8},{1,9},{2,10},{3,11},{4,12},{5,13},{6,14},{7,15},{8,0},{9,1},... | collective-permute-start | bytes 98312 | tf_op jit(solution)/shard_map/ppermute | solution.py:339
  71.7 1.9 %collective-permute-done.18 = bf16[64,256]{1,0:T(8,128)(2,1)S(1)} collective-permute-done((bf16[64,256]{1,0:T(8,128)(2,1)S(1)}, bf16[64,256]{1,0:T(8,128)(2,1)S(1)}, u32[]{:S(2)}, u32[]{:S(2)}) %collective-permute-start.18) | collective-permute-done | bytes 32800 | tf_op jit(solution)/shard_map/ppermute | solution.py:339
  73.6 1.7 %finish.1.hidden_ref = bf16[256,896]{1,0:T(8,128)(2,1)S(1)} custom-call(s32[35]{0:T(128)S(1)} %dynamic-slice_bitcast_fusion.table_ref, s32[2]{0:T(128)S(1)} %copy-done.3, f32[256,896]{1,0:T(8,128)S(1)} %product.4.refs_0_, f32[256,896]{1,0:T(8,128)S(1)} %product.5.refs_1_, f32[256,896]{1,0:T(8,128)S(1)} %product.6.refs_2_, f32[256,896]{1,0:T(8,128)S(1)} %product.7.refs_3_, ...), custom_call_target="tpu_custom_call" | custom-call | tf_op jit(solution)/shard_map/finish/pallas_call | solution.py:215
  75.3 0.0 copy-start.4
  75.3 12.6 %down.1 = (bf16[16,8192]{1,0:T(8,128)(2,1)S(1)}, bf16[16,8192]{1,0:T(8,128)(2,1)S(1)}, bf16[16,8192]{1,0:T(8,128)(2,1)S(1)}, bf16[16,8192]{1,0:T(8,128)(2,1)S(1)...) custom-call(s32[35]{0:T(128)S(1)} %dynamic-slice_bitcast_fusion.tabl, ...), custom_call_target="tpu_custom_call" | custom-call | flops 3758096384 | bytes 18874368 | tf_op jit(solution)/shard_map/down/pallas_call | solution.py:258
  87.9 0.1 collective-permute-start.23
  88.0 0.5 collective-permute-start.22
  88.5 1.0 collective-permute-done.23
  89.5 0.1 add_convert_fusion.6
  89.6 2.0 %collective-permute-start.24 = (bf16[16,8192]{1,0:T(8,128)(2,1)S(1)}, bf16[16,8192]{1,0:T(8,128)(2,1)S(1)}, u32[]{:S(2)}, u32[]{:S(2)}) collective-permute-start(bf16[16,8192]{1,0:T(8,128)(2,1)S(1)} %add_convert_fusion.6), channel_id=1, source_target_pairs={{0,4},{1,3},{4,8},{5,1},{8,12},{9,5},{12,14},{13,9},{14,10},{15,13... | collective-permute-start | bytes 786440 | tf_op jit(solution)/shard_map/ppermute | solution.py:336
  91.6 4.5 %collective-permute-done.24 = bf16[16,8192]{1,0:T(8,128)(2,1)S(1)} collective-permute-done((bf16[16,8192]{1,0:T(8,128)(2,1)S(1)}, bf16[16,8192]{1,0:T(8,128)(2,1)S(1)}, u32[]{:S(2)}, u32[]{:S(2)}) %collective-permute-start.24) | collective-permute-done | bytes 262176 | tf_op jit(solution)/shard_map/ppermute | solution.py:336
  96.0 0.2 add_convert_fusion.2
  96.2 2.0 %collective-permute-start.28 = (bf16[16,8192]{1,0:T(8,128)(2,1)S(1)}, bf16[16,8192]{1,0:T(8,128)(2,1)S(1)}, u32[]{:S(2)}, u32[]{:S(2)}) collective-permute-start(bf16[16,8192]{1,0:T(8,128)(2,1)S(1)} %get-tuple-element.39), channel_id=1, source_target_pairs={{0,4},{1,3},{4,8},{5,1},{8,12},{9,5},{12,14},{13,9},{14,10},{15,13... | collective-permute-start | bytes 786440 | tf_op jit(solution)/shard_map/ppermute | solution.py:336
  98.2 1.6 %collective-permute-start.25 = (bf16[16,8192]{1,0:T(8,128)(2,1)S(1)}, bf16[16,8192]{1,0:T(8,128)(2,1)S(1)}, u32[]{:S(2)}, u32[]{:S(2)}) collective-permute-start(bf16[16,8192]{1,0:T(8,128)(2,1)S(1)} %get-tuple-element.40), channel_id=1, source_target_pairs={{0,4},{1,3},{4,8},{5,1},{8,12},{9,5},{12,14},{13,9},{14,10},{15,13... | collective-permute-start | bytes 786440 | tf_op jit(solution)/shard_map/ppermute | solution.py:336
  99.8 2.9 %collective-permute-done.28 = bf16[16,8192]{1,0:T(8,128)(2,1)S(1)} collective-permute-done((bf16[16,8192]{1,0:T(8,128)(2,1)S(1)}, bf16[16,8192]{1,0:T(8,128)(2,1)S(1)}, u32[]{:S(2)}, u32[]{:S(2)}) %collective-permute-start.28) | collective-permute-done | bytes 262176 | tf_op jit(solution)/shard_map/ppermute | solution.py:336
  102.6 2.8 %collective-permute-done.25 = bf16[16,8192]{1,0:T(8,128)(2,1)S(1)} collective-permute-done((bf16[16,8192]{1,0:T(8,128)(2,1)S(1)}, bf16[16,8192]{1,0:T(8,128)(2,1)S(1)}, u32[]{:S(2)}, u32[]{:S(2)}) %collective-permute-start.25) | collective-permute-done | bytes 262176 | tf_op jit(solution)/shard_map/ppermute | solution.py:336
  105.4 0.2 add_convert_fusion.1
  105.6 2.0 %collective-permute-start.29 = (bf16[16,8192]{1,0:T(8,128)(2,1)S(1)}, bf16[16,8192]{1,0:T(8,128)(2,1)S(1)}, u32[]{:S(2)}, u32[]{:S(2)}) collective-permute-start(bf16[16,8192]{1,0:T(8,128)(2,1)S(1)} %get-tuple-element.37), channel_id=1, source_target_pairs={{0,4},{1,3},{4,8},{5,1},{8,12},{9,5},{12,14},{13,9},{14,10},{15,13... | collective-permute-start | bytes 786440 | tf_op jit(solution)/shard_map/ppermute | solution.py:336
  107.6 1.6 %collective-permute-start.26 = (bf16[16,8192]{1,0:T(8,128)(2,1)S(1)}, bf16[16,8192]{1,0:T(8,128)(2,1)S(1)}, u32[]{:S(2)}, u32[]{:S(2)}) collective-permute-start(bf16[16,8192]{1,0:T(8,128)(2,1)S(1)} %get-tuple-element.38), channel_id=1, source_target_pairs={{0,4},{1,3},{4,8},{5,1},{8,12},{9,5},{12,14},{13,9},{14,10},{15,13... | collective-permute-start | bytes 786440 | tf_op jit(solution)/shard_map/ppermute | solution.py:336
  109.2 2.9 %collective-permute-done.29 = bf16[16,8192]{1,0:T(8,128)(2,1)S(1)} collective-permute-done((bf16[16,8192]{1,0:T(8,128)(2,1)S(1)}, bf16[16,8192]{1,0:T(8,128)(2,1)S(1)}, u32[]{:S(2)}, u32[]{:S(2)}) %collective-permute-start.29) | collective-permute-done | bytes 262176 | tf_op jit(solution)/shard_map/ppermute | solution.py:336
  112.0 2.8 %collective-permute-done.26 = bf16[16,8192]{1,0:T(8,128)(2,1)S(1)} collective-permute-done((bf16[16,8192]{1,0:T(8,128)(2,1)S(1)}, bf16[16,8192]{1,0:T(8,128)(2,1)S(1)}, u32[]{:S(2)}, u32[]{:S(2)}) %collective-permute-start.26) | collective-permute-done | bytes 262176 | tf_op jit(solution)/shard_map/ppermute | solution.py:336
  114.9 0.2 add_convert_fusion
  115.1 2.0 %collective-permute-start.30 = (bf16[16,8192]{1,0:T(8,128)(2,1)S(1)}, bf16[16,8192]{1,0:T(8,128)(2,1)S(1)}, u32[]{:S(2)}, u32[]{:S(2)}) collective-permute-start(bf16[16,8192]{1,0:T(8,128)(2,1)S(1)} %get-tuple-element.35), channel_id=1, source_target_pairs={{0,4},{1,3},{4,8},{5,1},{8,12},{9,5},{12,14},{13,9},{14,10},{15,13... | collective-permute-start | bytes 786440 | tf_op jit(solution)/shard_map/ppermute | solution.py:336
  117.0 1.6 %collective-permute-start.27 = (bf16[16,8192]{1,0:T(8,128)(2,1)S(1)}, bf16[16,8192]{1,0:T(8,128)(2,1)S(1)}, u32[]{:S(2)}, u32[]{:S(2)}) collective-permute-start(bf16[16,8192]{1,0:T(8,128)(2,1)S(1)} %get-tuple-element.36), channel_id=1, source_target_pairs={{0,4},{1,3},{4,8},{5,1},{8,12},{9,5},{12,14},{13,9},{14,10},{15,13... | collective-permute-start | bytes 786440 | tf_op jit(solution)/shard_map/ppermute | solution.py:336
  118.6 2.9 %collective-permute-done.30 = bf16[16,8192]{1,0:T(8,128)(2,1)S(1)} collective-permute-done((bf16[16,8192]{1,0:T(8,128)(2,1)S(1)}, bf16[16,8192]{1,0:T(8,128)(2,1)S(1)}, u32[]{:S(2)}, u32[]{:S(2)}) %collective-permute-start.30) | collective-permute-done | bytes 262176 | tf_op jit(solution)/shard_map/ppermute | solution.py:336
  121.5 2.8 %collective-permute-done.27.refs_2_ = bf16[16,8192]{1,0:T(8,128)(2,1)S(1)} collective-permute-done((bf16[16,8192]{1,0:T(8,128)(2,1)S(1)}, bf16[16,8192]{1,0:T(8,128)(2,1)S(1)}, u32[]{:S(2)}, u32[]{:S(2)}) %collective-permute-start.27) | collective-permute-done | bytes 262176 | tf_op jit(solution)/shard_map/ppermute | solution.py:336
  124.3 1.4 %last.1 = bf16[16,8192]{1,0:T(8,128)(2,1)} custom-call(s32[35]{0:T(128)S(1)} %dynamic-slice_bitcast_fusion.table_ref, s32[2]{0:T(128)S(1)} %copy-done.4, bf16[16,8192]{1,0:T(8,128)(2,1)S(1)} %get-tuple-element.22.refs_0_, bf16[16,8192]{1,0:T(8,128)(2,1)S(1)} %collective-permute-done.19.refs_1_, bf16[16,8192]{1,0:T(8,128)(2,1)S(1)} %collective-permute-done.27.refs_2_, ...), custom_call_target="tpu_custom_call" | custom-call | tf_op jit(solution)/shard_map/last/pallas_call | solution.py:294
  (31 shorter events, 0.1 us)
Async XLA Ops:
  0.0 3.0 %collective-permute-start = (bf16[16,8192]{1,0:T(8,128)(2,1)}, bf16[16,8192]{1,0:T(8,128)(2,1)S(1)}, u32[]{:S(2)}, u32[]{:S(2)}) collective-permute-start(bf16[16,8192]{1,0:T(8,128)(2,1)} %refs_0_.6), channel_id=1, source_target_pairs={{0,1},{1,0},{2,3},{3,2},{4,5},{5,4},{6,7},{7,6},{8,9},{9,8},{10,11... | collective-permute-start | bytes 786440 | tf_op jit(solution)/shard_map/ppermute | solution.py:339
  0.5 7.1 %collective-permute-start.1 = (bf16[16,8192]{1,0:T(8,128)(2,1)}, bf16[16,8192]{1,0:T(8,128)(2,1)S(1)}, u32[]{:S(2)}, u32[]{:S(2)}) collective-permute-start(bf16[16,8192]{1,0:T(8,128)(2,1)} %refs_0_.6), channel_id=1, source_target_pairs={{0,4},{1,3},{4,8},{5,1},{8,12},{9,5},{12,14},{13,9},{14,10},{15,13... | collective-permute-start | bytes 786440 | tf_op jit(solution)/shard_map/ppermute | solution.py:336
  3.0 7.3 %collective-permute-start.2 = (bf16[16,8192]{1,0:T(8,128)(2,1)S(1)}, bf16[16,8192]{1,0:T(8,128)(2,1)S(1)}, u32[]{:S(2)}, u32[]{:S(2)}) collective-permute-start(bf16[16,8192]{1,0:T(8,128)(2,1)S(1)} %collective-permute-done.refs_1_), channel_id=1, source_target_pairs={{0,4},{1,3},{4,8},{5,1},{8,12},{9,5},{12,14},{13,9},{14,10},{15,13... | collective-permute-start | bytes 786440 | tf_op jit(solution)/shard_map/ppermute | solution.py:336
  7.5 6.4 %collective-permute-start.3 = (bf16[16,8192]{1,0:T(8,128)(2,1)S(1)}, bf16[16,8192]{1,0:T(8,128)(2,1)S(1)}, u32[]{:S(2)}, u32[]{:S(2)}) collective-permute-start(bf16[16,8192]{1,0:T(8,128)(2,1)S(1)} %collective-permute-done.1.refs_2_), channel_id=1, source_target_pairs={{0,4},{1,3},{4,8},{5,1},{8,12},{9,5},{12,14},{13,9},{14,10},{15,13... | collective-permute-start | bytes 786440 | tf_op jit(solution)/shard_map/ppermute | solution.py:336
  10.3 6.4 %collective-permute-start.4 = (bf16[16,8192]{1,0:T(8,128)(2,1)S(1)}, bf16[16,8192]{1,0:T(8,128)(2,1)S(1)}, u32[]{:S(2)}, u32[]{:S(2)}) collective-permute-start(bf16[16,8192]{1,0:T(8,128)(2,1)S(1)} %collective-permute-done.2.refs_3_), channel_id=1, source_target_pairs={{0,4},{1,3},{4,8},{5,1},{8,12},{9,5},{12,14},{13,9},{14,10},{15,13... | collective-permute-start | bytes 786440 | tf_op jit(solution)/shard_map/ppermute | solution.py:336
  13.9 6.4 %collective-permute-start.5 = (bf16[16,8192]{1,0:T(8,128)(2,1)S(1)}, bf16[16,8192]{1,0:T(8,128)(2,1)S(1)}, u32[]{:S(2)}, u32[]{:S(2)}) collective-permute-start(bf16[16,8192]{1,0:T(8,128)(2,1)S(1)} %collective-permute-done.3.refs_4_), channel_id=1, source_target_pairs={{0,4},{1,3},{4,8},{5,1},{8,12},{9,5},{12,14},{13,9},{14,10},{15,13... | collective-permute-start | bytes 786440 | tf_op jit(solution)/shard_map/ppermute | solution.py:336
  16.0 6.4 %collective-permute-start.8 = (bf16[16,8192]{1,0:T(8,128)(2,1)S(1)}, bf16[16,8192]{1,0:T(8,128)(2,1)S(1)}, u32[]{:S(2)}, u32[]{:S(2)}) collective-permute-start(bf16[16,8192]{1,0:T(8,128)(2,1)S(1)} %collective-permute-done.1.refs_2_), channel_id=1, source_target_pairs={{0,1},{1,0},{2,3},{3,2},{4,5},{5,4},{6,7},{7,6},{8,9},{9,8},{10,11... | collective-permute-start | bytes 786440 | tf_op jit(solution)/shard_map/ppermute | solution.py:339
  16.0 6.9 %collective-permute-start.9 = (bf16[16,8192]{1,0:T(8,128)(2,1)S(1)}, bf16[16,8192]{1,0:T(8,128)(2,1)S(1)}, u32[]{:S(2)}, u32[]{:S(2)}) collective-permute-start(bf16[16,8192]{1,0:T(8,128)(2,1)S(1)} %collective-permute-done.2.refs_3_), channel_id=1, source_target_pairs={{0,1},{1,0},{2,3},{3,2},{4,5},{5,4},{6,7},{7,6},{8,9},{9,8},{10,11... | collective-permute-start | bytes 786440 | tf_op jit(solution)/shard_map/ppermute | solution.py:339
  16.7 6.4 %collective-permute-start.6 = (bf16[16,8192]{1,0:T(8,128)(2,1)S(1)}, bf16[16,8192]{1,0:T(8,128)(2,1)S(1)}, u32[]{:S(2)}, u32[]{:S(2)}) collective-permute-start(bf16[16,8192]{1,0:T(8,128)(2,1)S(1)} %collective-permute-done.4.refs_5_), channel_id=1, source_target_pairs={{0,4},{1,3},{4,8},{5,1},{8,12},{9,5},{12,14},{13,9},{14,10},{15,13... | collective-permute-start | bytes 786440 | tf_op jit(solution)/shard_map/ppermute | solution.py:336
  20.3 6.4 %collective-permute-start.7 = (bf16[16,8192]{1,0:T(8,128)(2,1)S(1)}, bf16[16,8192]{1,0:T(8,128)(2,1)S(1)}, u32[]{:S(2)}, u32[]{:S(2)}) collective-permute-start(bf16[16,8192]{1,0:T(8,128)(2,1)S(1)} %collective-permute-done.5.refs_6_), channel_id=1, source_target_pairs={{0,4},{1,3},{4,8},{5,1},{8,12},{9,5},{12,14},{13,9},{14,10},{15,13... | collective-permute-start | bytes 786440 | tf_op jit(solution)/shard_map/ppermute | solution.py:336
  22.4 5.0 %collective-permute-start.10 = (bf16[16,8192]{1,0:T(8,128)(2,1)S(1)}, bf16[16,8192]{1,0:T(8,128)(2,1)S(1)}, u32[]{:S(2)}, u32[]{:S(2)}) collective-permute-start(bf16[16,8192]{1,0:T(8,128)(2,1)S(1)} %collective-permute-done.3.refs_4_), channel_id=1, source_target_pairs={{0,1},{1,0},{2,3},{3,2},{4,5},{5,4},{6,7},{7,6},{8,9},{9,8},{10,11... | collective-permute-start | bytes 786440 | tf_op jit(solution)/shard_map/ppermute | solution.py:339
  22.4 5.0 %collective-permute-start.11 = (bf16[16,8192]{1,0:T(8,128)(2,1)S(1)}, bf16[16,8192]{1,0:T(8,128)(2,1)S(1)}, u32[]{:S(2)}, u32[]{:S(2)}) collective-permute-start(bf16[16,8192]{1,0:T(8,128)(2,1)S(1)} %collective-permute-done.4.refs_5_), channel_id=1, source_target_pairs={{0,1},{1,0},{2,3},{3,2},{4,5},{5,4},{6,7},{7,6},{8,9},{9,8},{10,11... | collective-permute-start | bytes 786440 | tf_op jit(solution)/shard_map/ppermute | solution.py:339
  22.9 4.5 %collective-permute-start.12 = (bf16[16,8192]{1,0:T(8,128)(2,1)S(1)}, bf16[16,8192]{1,0:T(8,128)(2,1)S(1)}, u32[]{:S(2)}, u32[]{:S(2)}) collective-permute-start(bf16[16,8192]{1,0:T(8,128)(2,1)S(1)} %collective-permute-done.5.refs_6_), channel_id=1, source_target_pairs={{0,1},{1,0},{2,3},{3,2},{4,5},{5,4},{6,7},{7,6},{8,9},{9,8},{10,11... | collective-permute-start | bytes 786440 | tf_op jit(solution)/shard_map/ppermute | solution.py:339
  23.1 4.3 %collective-permute-start.13 = (bf16[16,8192]{1,0:T(8,128)(2,1)S(1)}, bf16[16,8192]{1,0:T(8,128)(2,1)}, u32[]{:S(2)}, u32[]{:S(2)}) collective-permute-start(bf16[16,8192]{1,0:T(8,128)(2,1)S(1)} %collective-permute-done.6.refs_7_), channel_id=1, source_target_pairs={{0,1},{1,0},{2,3},{3,2},{4,5},{5,4},{6,7},{7,6},{8,9},{9,8},{10,11... | collective-permute-start | bytes 786440 | tf_op jit(solution)/shard_map/ppermute | solution.py:339
  26.6 1.7 %collective-permute-start.14 = (bf16[16,8192]{1,0:T(8,128)(2,1)S(1)}, bf16[16,8192]{1,0:T(8,128)(2,1)}, u32[]{:S(2)}, u32[]{:S(2)}) collective-permute-start(bf16[16,8192]{1,0:T(8,128)(2,1)S(1)} %collective-permute-done.7.refs_8_), channel_id=1, source_target_pairs={{0,1},{1,0},{2,3},{3,2},{4,5},{5,4},{6,7},{7,6},{8,9},{9,8},{10,11... | collective-permute-start | bytes 786440 | tf_op jit(solution)/shard_map/ppermute | solution.py:339
  28.3 1.2 copy-start
  29.5 0.9 copy-start.2
  30.5 0.7 copy-start.3
  54.1 19.4 %copy-start.1 = (bf16[8,128,896]{2,1,0:T(8,128)(2,1)S(1)}, bf16[8,128,896]{2,1,0:T(8,128)(2,1)}, u32[]{:S(2)}) copy-start(bf16[8,128,896]{2,1,0:T(8,128)(2,1)} %refs_5_.2) | copy-start | bytes 5505028
  60.0 1.2 collective-permute-start.15
  61.2 3.7 %collective-permute-start.16 = (bf16[16,256]{1,0:T(8,128)(2,1)S(1)}, bf16[16,256]{1,0:T(8,128)(2,1)S(1)}, u32[]{:S(2)}, u32[]{:S(2)}) collective-permute-start(bf16[16,256]{1,0:T(8,128)(2,1)S(1)} %pad_maximum_fusion.2), channel_id=1, source_target_pairs={{0,2},{1,3},{2,0},{3,1},{4,6},{5,7},{6,4},{7,5},{8,10},{9,11},{10,... | collective-permute-start | bytes 24584 | tf_op jit(solution)/shard_map/ppermute | solution.py:339
  64.8 3.8 %collective-permute-start.17 = (bf16[32,256]{1,0:T(8,128)(2,1)S(1)}, bf16[32,256]{1,0:T(8,128)(2,1)S(1)}, u32[]{:S(2)}, u32[]{:S(2)}) collective-permute-start(bf16[32,256]{1,0:T(8,128)(2,1)S(1)} %pad_maximum_fusion.1), channel_id=1, source_target_pairs={{0,4},{1,5},{2,6},{3,7},{4,0},{5,1},{6,2},{7,3},{8,12},{9,13},{10,... | collective-permute-start | bytes 49160 | tf_op jit(solution)/shard_map/ppermute | solution.py:339
  68.6 4.9 %collective-permute-start.18 = (bf16[64,256]{1,0:T(8,128)(2,1)S(1)}, bf16[64,256]{1,0:T(8,128)(2,1)S(1)}, u32[]{:S(2)}, u32[]{:S(2)}) collective-permute-start(bf16[64,256]{1,0:T(8,128)(2,1)S(1)} %pad_maximum_fusion), channel_id=1, source_target_pairs={{0,8},{1,9},{2,10},{3,11},{4,12},{5,13},{6,14},{7,15},{8,0},{9,1},... | collective-permute-start | bytes 98312 | tf_op jit(solution)/shard_map/ppermute | solution.py:339
  75.3 49.0 %copy-start.4 = (s32[2]{0:T(128)S(1)}, s32[2]{0:T(128)}, u32[]{:S(2)}) copy-start(s32[2]{0:T(128)} %counts_ref.1) | copy-start | bytes 28
  87.9 1.6 %collective-permute-start.23 = (bf16[16,8192]{1,0:T(8,128)(2,1)S(1)}, bf16[16,8192]{1,0:T(8,128)(2,1)S(1)}, u32[]{:S(2)}, u32[]{:S(2)}) collective-permute-start(bf16[16,8192]{1,0:T(8,128)(2,1)S(1)} %get-tuple-element.31), channel_id=1, source_target_pairs={{0,1},{1,0},{2,3},{3,2},{4,5},{5,4},{6,7},{7,6},{8,9},{9,8},{10,11... | collective-permute-start | bytes 786440 | tf_op jit(solution)/shard_map/ppermute | solution.py:339
  88.0 8.0 %collective-permute-start.22 = (bf16[32,8192]{1,0:T(8,128)(2,1)S(1)}, bf16[32,8192]{1,0:T(8,128)(2,1)S(1)}, u32[]{:S(2)}, u32[]{:S(2)}) collective-permute-start(bf16[32,8192]{1,0:T(8,128)(2,1)S(1)} %get-tuple-element.29), channel_id=1, source_target_pairs={{0,1},{1,0},{2,3},{3,2},{4,5},{5,4},{6,7},{7,6},{8,9},{9,8},{10,11... | collective-permute-start | bytes 1572872 | tf_op jit(solution)/shard_map/ppermute | solution.py:339
  89.6 6.4 %collective-permute-start.24 = (bf16[16,8192]{1,0:T(8,128)(2,1)S(1)}, bf16[16,8192]{1,0:T(8,128)(2,1)S(1)}, u32[]{:S(2)}, u32[]{:S(2)}) collective-permute-start(bf16[16,8192]{1,0:T(8,128)(2,1)S(1)} %add_convert_fusion.6), channel_id=1, source_target_pairs={{0,4},{1,3},{4,8},{5,1},{8,12},{9,5},{12,14},{13,9},{14,10},{15,13... | collective-permute-start | bytes 786440 | tf_op jit(solution)/shard_map/ppermute | solution.py:336
  91.6 8.2 %collective-permute-start.21 = (bf16[32,8192]{1,0:T(8,128)(2,1)S(1)}, bf16[32,8192]{1,0:T(8,128)(2,1)S(1)}, u32[]{:S(2)}, u32[]{:S(2)}) collective-permute-start(bf16[32,8192]{1,0:T(8,128)(2,1)S(1)} %get-tuple-element.27), channel_id=1, source_target_pairs={{0,1},{1,0},{2,3},{3,2},{4,5},{5,4},{6,7},{7,6},{8,9},{9,8},{10,11... | collective-permute-start | bytes 1572872 | tf_op jit(solution)/shard_map/ppermute | solution.py:339
  96.2 6.4 %collective-permute-start.28 = (bf16[16,8192]{1,0:T(8,128)(2,1)S(1)}, bf16[16,8192]{1,0:T(8,128)(2,1)S(1)}, u32[]{:S(2)}, u32[]{:S(2)}) collective-permute-start(bf16[16,8192]{1,0:T(8,128)(2,1)S(1)} %get-tuple-element.39), channel_id=1, source_target_pairs={{0,4},{1,3},{4,8},{5,1},{8,12},{9,5},{12,14},{13,9},{14,10},{15,13... | collective-permute-start | bytes 786440 | tf_op jit(solution)/shard_map/ppermute | solution.py:336
  98.2 7.3 %collective-permute-start.25 = (bf16[16,8192]{1,0:T(8,128)(2,1)S(1)}, bf16[16,8192]{1,0:T(8,128)(2,1)S(1)}, u32[]{:S(2)}, u32[]{:S(2)}) collective-permute-start(bf16[16,8192]{1,0:T(8,128)(2,1)S(1)} %get-tuple-element.40), channel_id=1, source_target_pairs={{0,4},{1,3},{4,8},{5,1},{8,12},{9,5},{12,14},{13,9},{14,10},{15,13... | collective-permute-start | bytes 786440 | tf_op jit(solution)/shard_map/ppermute | solution.py:336
  99.8 9.4 %collective-permute-start.20 = (bf16[32,8192]{1,0:T(8,128)(2,1)S(1)}, bf16[32,8192]{1,0:T(8,128)(2,1)S(1)}, u32[]{:S(2)}, u32[]{:S(2)}) collective-permute-start(bf16[32,8192]{1,0:T(8,128)(2,1)S(1)} %get-tuple-element.25), channel_id=1, source_target_pairs={{0,1},{1,0},{2,3},{3,2},{4,5},{5,4},{6,7},{7,6},{8,9},{9,8},{10,11... | collective-permute-start | bytes 1572872 | tf_op jit(solution)/shard_map/ppermute | solution.py:339
  105.6 6.4 %collective-permute-start.29 = (bf16[16,8192]{1,0:T(8,128)(2,1)S(1)}, bf16[16,8192]{1,0:T(8,128)(2,1)S(1)}, u32[]{:S(2)}, u32[]{:S(2)}) collective-permute-start(bf16[16,8192]{1,0:T(8,128)(2,1)S(1)} %get-tuple-element.37), channel_id=1, source_target_pairs={{0,4},{1,3},{4,8},{5,1},{8,12},{9,5},{12,14},{13,9},{14,10},{15,13... | collective-permute-start | bytes 786440 | tf_op jit(solution)/shard_map/ppermute | solution.py:336
  107.6 7.3 %collective-permute-start.26 = (bf16[16,8192]{1,0:T(8,128)(2,1)S(1)}, bf16[16,8192]{1,0:T(8,128)(2,1)S(1)}, u32[]{:S(2)}, u32[]{:S(2)}) collective-permute-start(bf16[16,8192]{1,0:T(8,128)(2,1)S(1)} %get-tuple-element.38), channel_id=1, source_target_pairs={{0,4},{1,3},{4,8},{5,1},{8,12},{9,5},{12,14},{13,9},{14,10},{15,13... | collective-permute-start | bytes 786440 | tf_op jit(solution)/shard_map/ppermute | solution.py:336
  115.1 6.4 %collective-permute-start.30 = (bf16[16,8192]{1,0:T(8,128)(2,1)S(1)}, bf16[16,8192]{1,0:T(8,128)(2,1)S(1)}, u32[]{:S(2)}, u32[]{:S(2)}) collective-permute-start(bf16[16,8192]{1,0:T(8,128)(2,1)S(1)} %get-tuple-element.35), channel_id=1, source_target_pairs={{0,4},{1,3},{4,8},{5,1},{8,12},{9,5},{12,14},{13,9},{14,10},{15,13... | collective-permute-start | bytes 786440 | tf_op jit(solution)/shard_map/ppermute | solution.py:336
  117.0 4.5 %collective-permute-start.19 = (bf16[16,8192]{1,0:T(8,128)(2,1)S(1)}, bf16[16,8192]{1,0:T(8,128)(2,1)S(1)}, u32[]{:S(2)}, u32[]{:S(2)}) collective-permute-start(bf16[16,8192]{1,0:T(8,128)(2,1)S(1)} %get-tuple-element.23), channel_id=1, source_target_pairs={{0,1},{1,0},{2,3},{3,2},{4,5},{5,4},{6,7},{7,6},{8,9},{9,8},{10,11... | collective-permute-start | bytes 786440 | tf_op jit(solution)/shard_map/ppermute | solution.py:339
  117.0 7.3 %collective-permute-start.27 = (bf16[16,8192]{1,0:T(8,128)(2,1)S(1)}, bf16[16,8192]{1,0:T(8,128)(2,1)S(1)}, u32[]{:S(2)}, u32[]{:S(2)}) collective-permute-start(bf16[16,8192]{1,0:T(8,128)(2,1)S(1)} %get-tuple-element.36), channel_id=1, source_target_pairs={{0,4},{1,3},{4,8},{5,1},{8,12},{9,5},{12,14},{13,9},{14,10},{15,13... | collective-permute-start | bytes 786440 | tf_op jit(solution)/shard_map/ppermute | solution.py:336
  121.5 2.8 %collective-permute-start.31 = (bf16[16,8192]{1,0:T(8,128)(2,1)S(1)}, bf16[16,8192]{1,0:T(8,128)(2,1)S(1)}, u32[]{:S(2)}, u32[]{:S(2)}) collective-permute-start(bf16[16,8192]{1,0:T(8,128)(2,1)S(1)} %collective-permute-done.30), channel_id=1, source_target_pairs={{0,1},{1,0},{2,3},{3,2},{4,5},{5,4},{6,7},{7,6},{8,9},{9,8},{10,11... | collective-permute-start | bytes 786440 | tf_op jit(solution)/shard_map/ppermute | solution.py:339

commit v3 on v2

v3 whole, which is shorter than its diff:
```python
import functools

import jax
import jax.numpy as jnp
import numpy as np
from jax import lax
from jax.experimental import pallas as pl
from jax.experimental.pallas import tpu as pltpu
from jax.sharding import PartitionSpec as P

F32 = jnp.float32
BF16 = jnp.bfloat16
VMEM_LIMIT = 20 * 1024 * 1024


def largest_tile(size, limit):
    tile = limit
    while size % tile:
        tile //= 2
    return tile


def params():
    return pltpu.CompilerParams(vmem_limit_bytes=VMEM_LIMIT)


def cost(flops, moved):
    return pl.CostEstimate(flops=flops, bytes_accessed=moved, transcendentals=0)


def ring_of(chips):
    return list(range(0, chips, 2)) + list(range(chips - 1, 0, -2))


def layout(members, rows, block_rows):
    chips = members // 2
    ring = ring_of(chips)
    reach = chips // 2
    table = []
    for device in range(members):
        chip, core = divmod(device, 2)
        place = ring.index(chip)

        def row(side, distance, half):
            sign = 1 if side == 0 else -1
            return (2 * ring[(place + sign * distance) % chips] + half) * rows

        arrive = [row(core, 0, core), row(core, 0, 1 - core)]
        for side in (core, 1 - core):
            for step in range(1, reach + 1):
                arrive.append(row(1 - side, step, side))
                if step < reach:
                    arrive.append(row(1 - side, step, 1 - side))
        leave = []
        for side in (core, 1 - core):
            leave.append(row(side, reach, side))
            for step in range(reach - 1, 0, -1):
                leave += [row(side, step, side), row(side, step, 1 - side)]
            leave.append(row(side, 0, side))
        own = device * rows
        table.append(arrive + leave + [own // block_rows, own % block_rows, device])
    return np.asarray(table, np.int32)


def around(members):
    ring = ring_of(members // 2)
    size = len(ring)
    pairs = []
    for i in range(size):
        pairs.append((2 * ring[i], 2 * ring[(i + 1) % size]))
        pairs.append((2 * ring[i] + 1, 2 * ring[i - 1] + 1))
    return pairs


def crossing(members, bit):
    return [(i, i ^ bit) for i in range(members)]


def whole(count):
    return [pl.BlockSpec(memory_space=pltpu.VMEM)] * count


SCALARS = pl.BlockSpec(memory_space=pltpu.SMEM)
FAR = pl.BlockSpec(memory_space=pl.ANY)


def rank_kernel(numbers, block_rows, blocks, at, span, table_ref, shrink_ref, *refs):
    out_ref = refs[-1]
    pieces = refs[:-1]
    rows = pieces[0].shape[0]
    lhs = jnp.concatenate([piece[...] for piece in pieces], axis=0)
    found = [
        lax.dot_general(
            lhs, shrink_ref[table_ref[at + b]], (((1,), (1,)), ((), ())), preferred_element_type=F32
        )
        for b in range(blocks)
    ]
    for index, number in enumerate(numbers):
        block = table_ref[number] // block_rows
        part = slice(index * rows, (index + 1) * rows)
        value = found[0][part]
        for b in range(1, blocks):
            value = jnp.where(block == b, found[b][part], value)
        out_ref[part, :] = value


def rank_of(table, at, blocks, block_rows, numbers, pieces, shrink):
    rows, model = pieces[0].shape
    span = shrink.shape[1]
    total = rows * len(pieces)
    return pl.pallas_call(
        functools.partial(rank_kernel, numbers, block_rows, blocks, at, span),
        in_specs=[SCALARS] + whole(1 + len(pieces)),
        out_specs=whole(1)[0],
        out_shape=jax.ShapeDtypeStruct((total, span), F32),
        compiler_params=params(),
        cost_estimate=cost(2 * total * model * span * blocks, 2 * total * model),
        name="rank",
    )(table, shrink, *pieces)


def order_kernel(rows, groups, table_ref, *refs):
    parts, out_ref, scratch = refs[:-2], refs[-2], refs[-1]
    span = out_ref.shape[0]
    for numbers, part in zip(groups, parts, strict=True):
        for index, number in enumerate(numbers):
            start = pl.multiple_of(table_ref[number], rows)
            scratch[pl.ds(start, rows), :span] = part[index * rows : (index + 1) * rows, :]
    out_ref[...] = scratch[...].T[:span].astype(BF16)


def ordered(table, rows, groups, parts):
    span = parts[0].shape[1]
    total = sum(part.shape[0] for part in parts)
    return pl.pallas_call(
        functools.partial(order_kernel, rows, groups),
        in_specs=[SCALARS] + whole(len(parts)),
        out_specs=whole(1)[0],
        out_shape=jax.ShapeDtypeStruct((span, total), BF16),
        scratch_shapes=[pltpu.VMEM((total, 128), F32)],
        compiler_params=params(),
        name="ordered",
    )(table, *parts)


def product_kernel(first, chunks, slots, table_ref, w_ref, *refs):
    pieces = refs[: -4]
    out_ref, total, store, sems = refs[-4:]
    size = store.shape[1]
    rows = pieces[0].shape[0]

    def copy(chunk):
        return pltpu.make_async_copy(
            w_ref.at[pl.ds(first + chunk * size, size), :],
            store.at[chunk % slots],
            sems.at[chunk % slots],
        )

    for chunk in range(min(slots, chunks)):
        copy(chunk).start()
    for chunk in range(chunks):
        start = first + chunk * size
        lhs = jnp.concatenate([piece[:, start : start + size] for piece in pieces], axis=0)
        copy(chunk).wait()
        part = jnp.dot(lhs, store[chunk % slots], preferred_element_type=F32)
        if chunk + slots < chunks:
            copy(chunk + slots).start()
        if chunk == 0:
            total[...] = part
        elif chunk < chunks - 1:
            total[...] += part
        else:
            part += total[...]
            for index in range(len(pieces)):
                place = pl.multiple_of(table_ref[index], rows)
                out_ref[pl.ds(place, rows), :] = part[index * rows : (index + 1) * rows]


def product(table, pieces, matrix, part, parts):
    rows, model = pieces[0].shape
    total = rows * len(pieces)
    width = matrix.shape[1]
    depth = model // parts
    size = min(512, depth // 2)
    chunks = depth // size
    slots = min(4, chunks)
    return pl.pallas_call(
        functools.partial(product_kernel, part * depth, chunks, slots),
        in_specs=[SCALARS, FAR] + whole(len(pieces)),
        out_specs=whole(1)[0],
        out_shape=jax.ShapeDtypeStruct((total, width), F32),
        scratch_shapes=[
            pltpu.VMEM((total, width), F32),
            pltpu.VMEM((slots, size, width), BF16),
            pltpu.SemaphoreType.DMA((slots,)),
        ],
        compiler_params=params(),
        cost_estimate=cost(2 * total * depth * width, 2 * depth * (width + total)),
        name="product",
    )(table, matrix, *pieces)


def finish_kernel(parts, span, table_ref, ids_ref, *refs):
    g_refs, u_refs = refs[:parts], refs[parts : 2 * parts]
    rank_ref, expand_ref, hidden_ref = refs[2 * parts :]
    ranks = rank_ref.shape[0]
    device = table_ref[table_ref.shape[0] - 1]
    shape = (ranks, ranks)
    want = lax.broadcasted_iota(jnp.int32, shape, 0)
    have = lax.broadcasted_iota(jnp.int32, shape, 1)
    origin = ((have // span) ^ device) * span + have % span
    order = jnp.where(want == origin, 1.0, 0.0).astype(BF16)
    rank = jnp.dot(order, rank_ref[...], preferred_element_type=F32).T.astype(BF16)
    half = ranks // 2
    gate = jnp.dot(rank[:, :half], expand_ref[0, :half], preferred_element_type=F32)
    up = jnp.dot(rank[:, half:], expand_ref[0, half:], preferred_element_type=F32)
    for g_ref in g_refs:
        gate += g_ref[...]
    for u_ref in u_refs:
        up += u_ref[...]
    hidden_ref[...] = (gate / (1.0 + jnp.exp(-gate)) * up).astype(BF16)


def finish(table, at, blocks, gates, ups, rank, expand, span):
    total, width = gates[0].shape
    rows = total // blocks
    ranks = rank.shape[0]
    parts = len(gates)
    wide = pl.BlockSpec((rows, width), lambda b, table: (b, 0))

    def kernel(table_ref, *refs):
        finish_kernel(parts, span, table_ref, None, *refs)

    return pl.pallas_call(
        kernel,
        grid_spec=pltpu.PrefetchScalarGridSpec(
            num_scalar_prefetch=1,
            grid=(blocks,),
            in_specs=[wide] * (2 * parts)
            + [
                pl.BlockSpec((ranks, rows), lambda b, table: (0, b)),
                pl.BlockSpec((1, ranks, width), lambda b, table: (table[at + b], 0, 0)),
            ],
            out_specs=wide,
        ),
        out_shape=jax.ShapeDtypeStruct((total, width), BF16),
        compiler_params=params(),
        name="finish",
    )(table, *gates, *ups, rank, expand)


def down_kernel(first, groups, rows, chunks, slots, table_ref, w_ref, hidden_ref, *refs):
    outs, (product_ref, store, sems) = refs[:-3], refs[-3:]
    size = store.shape[2]

    def copy(chunk):
        return pltpu.make_async_copy(
            w_ref.at[:, pl.ds(chunk * size, size)],
            store.at[chunk % slots],
            sems.at[chunk % slots],
        )

    for chunk in range(min(slots, chunks)):
        copy(chunk).start()
    hidden = hidden_ref[...]
    for chunk in range(chunks):
        columns = slice(chunk * size, (chunk + 1) * size)
        copy(chunk).wait()
        part = jnp.dot(hidden, store[chunk % slots], preferred_element_type=F32)
        if chunk + slots < chunks:
            copy(chunk + slots).start()
        product_ref[...] = part.astype(BF16)
        at = first
        for out, group in zip(outs, groups, strict=True):
            for index in range(group):
                start = pl.multiple_of(table_ref[at], rows)
                out[index * rows : (index + 1) * rows, columns] = product_ref[pl.ds(start, rows), :]
                at += 1


def down(table, first, hidden, down_matrix, groups, rows):
    total, depth = hidden.shape
    columns = down_matrix.shape[1]
    size = min(512, columns // 2)
    chunks = columns // size
    slots = min(4, chunks)
    return pl.pallas_call(
        functools.partial(down_kernel, first, groups, rows, chunks, slots),
        in_specs=[SCALARS, FAR] + whole(1),
        out_specs=whole(len(groups)),
        out_shape=[jax.ShapeDtypeStruct((group * rows, columns), BF16) for group in groups],
        scratch_shapes=[
            pltpu.VMEM((total, size), BF16),
            pltpu.VMEM((slots, depth, size), BF16),
            pltpu.SemaphoreType.DMA((slots,)),
        ],
        compiler_params=params(),
        cost_estimate=cost(
            2 * total * depth * columns, 2 * depth * columns + 2 * total * columns
        ),
        name="down",
    )(table, down_matrix, hidden)


def last_kernel(at, table_ref, *refs):
    out_ref = refs[-1]
    summed = refs[0][...].astype(F32)
    for ref in refs[1:-1]:
        summed += ref[...].astype(F32)
    size = table_ref.shape[0]
    live = table_ref[at + table_ref[size - 3]] - table_ref[size - 2]
    row = lax.broadcasted_iota(jnp.int32, summed.shape, 0)
    out_ref[...] = jnp.where(row < live, summed, 0.0).astype(BF16)


def last(table, at, terms):
    shape = terms[0].shape
    return pl.pallas_call(
        functools.partial(last_kernel, at),
        in_specs=[SCALARS] + whole(len(terms)),
        out_specs=whole(1)[0],
        out_shape=jax.ShapeDtypeStruct(shape, BF16),
        compiler_params=params(),
        name="last",
    )(table, *terms)


def add_kernel(starts, *refs):
    out_ref = refs[-1]
    rows = out_ref.shape[0]
    total = 0.0
    for start, ref in zip(starts, refs[:-1], strict=True):
        total += ref[start : start + rows, :].astype(F32)
    out_ref[...] = total.astype(BF16)


def added(rows, *terms):
    starts = [start for start, _ in terms]
    columns = terms[0][1].shape[1]
    return pl.pallas_call(
        functools.partial(add_kernel, starts),
        in_specs=whole(len(terms)),
        out_specs=whole(1)[0],
        out_shape=jax.ShapeDtypeStruct((rows, columns), BF16),
        compiler_params=params(),
        cost_estimate=cost(len(terms) * rows * columns, 2 * rows * columns),
        name="added",
    )(*[term for _, term in terms])


def per_device(
    members,
    tokens,
    gate_matrix,
    up_matrix,
    down_matrix,
    shrink_matrices,
    expand_matrices,
    adapter_per_block,
    block_token_count,
):
    rows, model = tokens.shape
    blocks = adapter_per_block.shape[0]
    span = shrink_matrices.shape[2]
    reach = members // 4
    block_rows = members * rows // blocks
    where = layout(members, rows, block_rows)
    known = where.shape[1]
    here = jnp.asarray(where)[lax.axis_index("tp")]
    table = jnp.concatenate([here, adapter_per_block, block_token_count, here[-3:]])
    adapters_at, counts_at = known, known + blocks
    ring = around(members)

    def step(x):
        return lax.ppermute(x, "tp", ring)

    def cross(x, bit=1):
        return lax.ppermute(x, "tp", crossing(members, bit))

    first, second = tokens, cross(tokens)
    pieces, mine, theirs = [first, second], [], []
    for distance in range(1, reach + 1):
        first = step(first)
        mine.append(first)
        theirs.append(cross(first))
        if distance < reach:
            second = step(second)
            mine.append(second)
            theirs.append(cross(second))
    pieces = pieces + mine + theirs

    shrink = jnp.swapaxes(shrink_matrices, 1, 2)
    early = reach if reach > 1 else 1
    soon = [0, 1] + [2 + i for i in range(early)] + [2 + len(mine) + i for i in range(early - 2)]
    late = [i for i in range(members) if i not in soon]
    groups = [soon, late]
    found = [
        rank_of(
            table, adapters_at, blocks, block_rows, group, [pieces[i] for i in group], shrink
        )
        for group in groups
    ]
    rank = ordered(table, rows, groups, found)
    bit = 1
    while bit < members:
        rank = jnp.concatenate([rank, cross(rank, bit)], axis=0)
        bit *= 2

    parts = 2
    gates = [product(table, pieces, gate_matrix, part, parts) for part in range(parts)]
    ups = [product(table, pieces, up_matrix, part, parts) for part in range(parts)]
    hidden = finish(table, adapters_at, blocks, gates, ups, rank, expand_matrices, span)

    slots = 2 * reach
    groups = [1] * slots + [1] + [2] * (reach - 1) + [1]
    outs = down(table, members, hidden, down_matrix, groups, rows)
    keep, give = outs[:slots], outs[slots:]
    came = [cross(x) for x in give]
    first = step(added(rows, (0, keep[0]), (0, came[0])))
    second = None
    for index in range(1, reach):
        more = [] if second is None else [(0, second)]
        second = step(added(rows, (0, keep[2 * index]), (rows, came[index]), *more))
        first = step(added(rows, (0, keep[2 * index - 1]), (0, came[index]), (0, first)))
    return last(table, counts_at, [keep[-1], came[-1], first, cross(second)])


def solution(mesh):
    members = mesh.shape["tp"]
    return jax.shard_map(
        functools.partial(per_device, members),
        mesh=mesh,
        in_specs=(
            P(("rep", "tp"), None),
            P(None, "tp"),
            P(None, "tp"),
            P("tp", None),
            P("rep", None, "tp"),
            P("rep", None, "tp"),
            P("rep"),
            P("rep"),
        ),
        out_specs=P(("rep", "tp"), None),
        check_vma=False,
    )
```

time: 127 us -> 128 us (level); the launches traced: 126 us -> 128 us
  local copies, waits for them, and re-layouts: 3.54 us -> 14.3 us
  waiting for transfers between devices: 39.8 us -> 31.4 us
    unnamed x14 -> x24, local copies, waits for them, and re-layouts: 2.85 us -> 13.5 us
    ppermute x14, waiting for transfers between devices: 31.5 us -> 24.5 us  [step(): return lax.ppermute(x, 'tp', ring)]
    ppermute x18, waiting for transfers between devices: 8.26 us -> 6.96 us  [cross(): return lax.ppermute(x, 'tp', crossing(members, bit))]
    pallas_call x8 -> x17, Pallas kernels: 44.5 us -> 43.3 us  [the longest x4 25 us: product(): pl.pallas_call(functools.partial(product_kernel, part * depth, chunks, sl...]
  transfers between devices with their start and end apart: 32 -> 32, of which waited for: 20 -> 18; matrix products, arithmetic and copies ran while one was open for 1% -> 1% of each run, Pallas kernels for 0% -> 21%
where the time goes in v3:
time: 128 us
  Pallas kernels  43.3 us (34%)
  starting transfers between devices  38.1 us (30%)
  waiting for transfers between devices  31.4 us (25%)
  local copies, waits for them, and re-layouts  14.3 us (11%)
    ppermute x14, starting transfers between devices, step(): return lax.ppermute(x, 'tp', ring)  28.3 us
    pallas_call x4, Pallas kernels, product(): pl.pallas_call(functools.partial(product_kernel, part * depth, chunks, sl...  25 us
    ppermute x14, waiting for transfers between devices, step(): return lax.ppermute(x, 'tp', ring)  24.5 us
    unnamed x24, local copies, waits for them, and re-layouts  13.5 us
    pallas_call x1, Pallas kernels, down(): pl.pallas_call(functools.partial(down_kernel, first, groups, rows, chunks...  10.1 us
    ppermute x18, starting transfers between devices, cross(): return lax.ppermute(x, 'tp', crossing(members, bit))  9.73 us
    ppermute x18, waiting for transfers between devices, cross(): return lax.ppermute(x, 'tp', crossing(members, bit))  6.96 us
    pallas_call x2, Pallas kernels, rank_of(): pl.pallas_call(functools.partial(rank_kernel, numbers, block_rows, blocks...  3.54 us
  transfers between devices with their start and end apart: 32, of which 18 were waited for; matrix products, arithmetic and copies ran while one was open for 1% of the time, Pallas kernels for 21%

profile of v3, /device:TPU:0, one launch (start us, length us, event | category | flops | bytes accessed | tf_op | source)
XLA Modules:
  0.0 128.1 jit_solution(6005068413536175258)
XLA Ops:
  0.0 3.0 %collective-permute-start.1 = (bf16[16,8192]{1,0:T(8,128)(2,1)}, bf16[16,8192]{1,0:T(8,128)(2,1)S(1)}, u32[]{:S(2)}, u32[]{:S(2)}) collective-permute-start(bf16[16,8192]{1,0:T(8,128)(2,1)} %refs_0_.9), channel_id=1, source_target_pairs={{0,4},{1,3},{4,8},{5,1},{8,12},{9,5},{12,14},{13,9},{14,10},{15,13... | collective-permute-start | bytes 786440 | tf_op jit(solution)/shard_map/ppermute | solution.py:375
  3.0 4.5 %collective-permute-done.1.refs_2_ = bf16[16,8192]{1,0:T(8,128)(2,1)S(1)} collective-permute-done((bf16[16,8192]{1,0:T(8,128)(2,1)}, bf16[16,8192]{1,0:T(8,128)(2,1)S(1)}, u32[]{:S(2)}, u32[]{:S(2)}) %collective-permute-start.1) | collective-permute-done | bytes 262176 | tf_op jit(solution)/shard_map/ppermute | solution.py:375
  7.5 2.1 %collective-permute-start.3 = (bf16[16,8192]{1,0:T(8,128)(2,1)S(1)}, bf16[16,8192]{1,0:T(8,128)(2,1)S(1)}, u32[]{:S(2)}, u32[]{:S(2)}) collective-permute-start(bf16[16,8192]{1,0:T(8,128)(2,1)S(1)} %collective-permute-done.1.refs_2_), channel_id=1, source_target_pairs={{0,4},{1,3},{4,8},{5,1},{8,12},{9,5},{12,14},{13,9},{14,10},{15,13... | collective-permute-start | bytes 786440 | tf_op jit(solution)/shard_map/ppermute | solution.py:375
  9.6 1.6 %collective-permute-start.2 = (bf16[16,8192]{1,0:T(8,128)(2,1)S(1)}, bf16[16,8192]{1,0:T(8,128)(2,1)S(1)}, u32[]{:S(2)}, u32[]{:S(2)}) collective-permute-start(bf16[16,8192]{1,0:T(8,128)(2,1)S(1)} %collective-permute-done.refs_1_), channel_id=1, source_target_pairs={{0,4},{1,3},{4,8},{5,1},{8,12},{9,5},{12,14},{13,9},{14,10},{15,13... | collective-permute-start | bytes 786440 | tf_op jit(solution)/shard_map/ppermute | solution.py:375
  11.2 2.7 %collective-permute-done.3.refs_4_ = bf16[16,8192]{1,0:T(8,128)(2,1)S(1)} collective-permute-done((bf16[16,8192]{1,0:T(8,128)(2,1)S(1)}, bf16[16,8192]{1,0:T(8,128)(2,1)S(1)}, u32[]{:S(2)}, u32[]{:S(2)}) %collective-permute-start.3) | collective-permute-done | bytes 262176 | tf_op jit(solution)/shard_map/ppermute | solution.py:375
  13.9 2.1 %collective-permute-start.5 = (bf16[16,8192]{1,0:T(8,128)(2,1)S(1)}, bf16[16,8192]{1,0:T(8,128)(2,1)S(1)}, u32[]{:S(2)}, u32[]{:S(2)}) collective-permute-start(bf16[16,8192]{1,0:T(8,128)(2,1)S(1)} %collective-permute-done.3.refs_4_), channel_id=1, source_target_pairs={{0,4},{1,3},{4,8},{5,1},{8,12},{9,5},{12,14},{13,9},{14,10},{15,13... | collective-permute-start | bytes 786440 | tf_op jit(solution)/shard_map/ppermute | solution.py:375
  16.0 0.7 collective-permute-done.2.refs_3_
  16.7 2.1 %collective-permute-start.4 = (bf16[16,8192]{1,0:T(8,128)(2,1)S(1)}, bf16[16,8192]{1,0:T(8,128)(2,1)S(1)}, u32[]{:S(2)}, u32[]{:S(2)}) collective-permute-start(bf16[16,8192]{1,0:T(8,128)(2,1)S(1)} %collective-permute-done.2.refs_3_), channel_id=1, source_target_pairs={{0,4},{1,3},{4,8},{5,1},{8,12},{9,5},{12,14},{13,9},{14,10},{15,13... | collective-permute-start | bytes 786440 | tf_op jit(solution)/shard_map/ppermute | solution.py:375
  18.8 0.5 collective-permute-start.9
  19.3 1.0 collective-permute-done.5.refs_6_.refs_0_
  20.3 2.1 %collective-permute-start.7 = (bf16[16,8192]{1,0:T(8,128)(2,1)S(1)}, bf16[16,8192]{1,0:T(8,128)(2,1)S(1)}, u32[]{:S(2)}, u32[]{:S(2)}) collective-permute-start(bf16[16,8192]{1,0:T(8,128)(2,1)S(1)} %collective-permute-done.5.refs_6_.refs_0_), channel_id=1, source_target_pairs={{0,4},{1,3},{4,8},{5,1},{8,12},{9,5},{12,14},{13,9},{14,10},{15,13... | collective-permute-start | bytes 786440 | tf_op jit(solution)/shard_map/ppermute | solution.py:375
  22.4 0.7 collective-permute-done.4.refs_5_
  23.1 2.1 %collective-permute-start.6 = (bf16[16,8192]{1,0:T(8,128)(2,1)S(1)}, bf16[16,8192]{1,0:T(8,128)(2,1)S(1)}, u32[]{:S(2)}, u32[]{:S(2)}) collective-permute-start(bf16[16,8192]{1,0:T(8,128)(2,1)S(1)} %collective-permute-done.4.refs_5_), channel_id=1, source_target_pairs={{0,4},{1,3},{4,8},{5,1},{8,12},{9,5},{12,14},{13,9},{14,10},{15,13... | collective-permute-start | bytes 786440 | tf_op jit(solution)/shard_map/ppermute | solution.py:375
  25.2 0.7 fusion
  25.9 0.5 collective-permute-start.12
  26.4 0.2 collective-permute-done.7.refs_8_.refs_2_
  26.6 0.2 collective-permute-start.14
  26.9 2.6 %collective-permute-done.6.refs_7_.refs_1_ = bf16[16,8192]{1,0:T(8,128)(2,1)S(1)} collective-permute-done((bf16[16,8192]{1,0:T(8,128)(2,1)S(1)}, bf16[16,8192]{1,0:T(8,128)(2,1)S(1)}, u32[]{:S(2)}, u32[]{:S(2)}) %collective-permute-start.6) | collective-permute-done | bytes 262176 | tf_op jit(solution)/shard_map/ppermute | solution.py:375
  29.5 0.1 slice_bitcast_fusion
  29.5 0.7 pad_add_fusion.table_ref
  30.3 0.9 copy-done.2
  31.2 1.2 copy-done.4
  32.5 1.8 %rank.2.refs_0_ = f32[128,8]{1,0:T(8,128)S(1)} custom-call(s32[42]{0:T(128)S(1)} %pad_add_fusion.table_ref, bf16[8,8,8192]{2,1,0:T(8,128)(2,1)S(1)} %bitcast.7, bf16[16,8192]{1,0:T(8,128)(2,1)S(1)} %copy-done.2, bf16[16,8192]{1,0:T(8,128)(2,1)S(1)} %collective-permute-done.refs_1_, bf16[16,8192]{1,0:T(8,128)(2,1)S(1)} %collective-permute-done.1.refs_2_, ...), custom_call_target="tpu_custom_call" | custom-call | flops 33554432 | bytes 2097152 | tf_op jit(solution)/shard_map/rank/pallas_call | solution.py:111
  34.3 1.8 %rank.3.refs_1_ = f32[128,8]{1,0:T(8,128)S(1)} custom-call(s32[42]{0:T(128)S(1)} %pad_add_fusion.table_ref, bf16[8,8,8192]{2,1,0:T(8,128)(2,1)S(1)} %bitcast.8, bf16[16,8192]{1,0:T(8,128)(2,1)S(1)} %collective-permute-done.5.refs_6_.refs_0_, bf16[16,8192]{1,0:T(8,128)(2,1)S(1)} %collective-permute-done.6.refs_7_.refs_1_, ...), custom_call_target="tpu_custom_call" | custom-call | flops 33554432 | bytes 2097152 | tf_op jit(solution)/shard_map/rank/pallas_call | solution.py:111
  36.1 0.6 ordered.1
  36.7 0.5 collective-permute-start.15
  37.2 5.2 %copy-done = bf16[8192,896]{1,0:T(8,128)(2,1)S(1)} copy-done((bf16[8192,896]{1,0:T(8,128)(2,1)S(1)}, bf16[8192,896]{1,0:T(8,128)(2,1)}, u32[]{:S(2)}) %copy-start) | copy-done | bytes 14680088
  42.4 0.9 copy-done.3
  43.3 6.4 %product.7.refs_3_ = f32[256,896]{1,0:T(8,128)S(1)} custom-call(s32[42]{0:T(128)S(1)} %pad_add_fusion.table_ref, bf16[8192,896]{1,0:T(8,128)(2,1)S(1)} %copy-done, bf16[16,8192]{1,0:T(8,128)(2,1)S(1)} %copy-done.3, bf16[16,8192]{1,0:T(8,128)(2,1)S(1)} %collective-permute-done.refs_1_, bf16[16,8192]{1,0:T(8,128)(2,1)S(1)} %collective-permute-done.1.refs_2_, ...), custom_call_target="tpu_custom_call" | custom-call | flops 1879048192 | bytes 9437184 | tf_op jit(solution)/shard_map/product/pallas_call | solution.py:187
  49.8 6.2 %product.6.refs_2_ = f32[256,896]{1,0:T(8,128)S(1)} custom-call(s32[42]{0:T(128)S(1)} %pad_add_fusion.table_ref, bf16[8192,896]{1,0:T(8,128)(2,1)S(1)} %copy-done, bf16[16,8192]{1,0:T(8,128)(2,1)S(1)} %copy-done.3, bf16[16,8192]{1,0:T(8,128)(2,1)S(1)} %collective-permute-done.refs_1_, bf16[16,8192]{1,0:T(8,128)(2,1)S(1)} %collective-permute-done.1.refs_2_, ...), custom_call_target="tpu_custom_call" | custom-call | flops 1879048192 | bytes 9437184 | tf_op jit(solution)/shard_map/product/pallas_call | solution.py:187
  56.0 6.2 %product.5.refs_1_ = f32[256,896]{1,0:T(8,128)S(1)} custom-call(s32[42]{0:T(128)S(1)} %pad_add_fusion.table_ref, bf16[8192,896]{1,0:T(8,128)(2,1)S(1)} %bitcast.6, bf16[16,8192]{1,0:T(8,128)(2,1)S(1)} %copy-done.3, bf16[16,8192]{1,0:T(8,128)(2,1)S(1)} %collective-permute-done.refs_1_, bf16[16,8192]{1,0:T(8,128)(2,1)S(1)} %collective-permute-done.1.refs_2_, ...), custom_call_target="tpu_custom_call" | custom-call | flops 1879048192 | bytes 9437184 | tf_op jit(solution)/shard_map/product/pallas_call | solution.py:187
  62.3 6.2 %product.4.refs_0_ = f32[256,896]{1,0:T(8,128)S(1)} custom-call(s32[42]{0:T(128)S(1)} %pad_add_fusion.table_ref, bf16[8192,896]{1,0:T(8,128)(2,1)S(1)} %bitcast.6, bf16[16,8192]{1,0:T(8,128)(2,1)S(1)} %copy-done.3, bf16[16,8192]{1,0:T(8,128)(2,1)S(1)} %collective-permute-done.refs_1_, bf16[16,8192]{1,0:T(8,128)(2,1)S(1)} %collective-permute-done.1.refs_2_, ...), custom_call_target="tpu_custom_call" | custom-call | flops 1879048192 | bytes 9437184 | tf_op jit(solution)/shard_map/product/pallas_call | solution.py:187
  68.5 2.1 %collective-permute-start.16 = (bf16[16,256]{1,0:T(8,128)(2,1)S(1)}, bf16[16,256]{1,0:T(8,128)(2,1)S(1)}, u32[]{:S(2)}, u32[]{:S(2)}) collective-permute-start(bf16[16,256]{1,0:T(8,128)(2,1)S(1)} %pad_maximum_fusion.2), channel_id=1, source_target_pairs={{0,2},{1,3},{2,0},{3,1},{4,6},{5,7},{6,4},{7,5},{8,10},{9,11},{10,... | collective-permute-start | bytes 24584 | tf_op jit(solution)/shard_map/ppermute | solution.py:378
  70.6 1.6 %collective-permute-done.16 = bf16[16,256]{1,0:T(8,128)(2,1)S(1)} collective-permute-done((bf16[16,256]{1,0:T(8,128)(2,1)S(1)}, bf16[16,256]{1,0:T(8,128)(2,1)S(1)}, u32[]{:S(2)}, u32[]{:S(2)}) %collective-permute-start.16) | collective-permute-done | bytes 8224 | tf_op jit(solution)/shard_map/ppermute | solution.py:378
  72.2 2.1 %collective-permute-start.17 = (bf16[32,256]{1,0:T(8,128)(2,1)S(1)}, bf16[32,256]{1,0:T(8,128)(2,1)S(1)}, u32[]{:S(2)}, u32[]{:S(2)}) collective-permute-start(bf16[32,256]{1,0:T(8,128)(2,1)S(1)} %pad_maximum_fusion.1), channel_id=1, source_target_pairs={{0,4},{1,5},{2,6},{3,7},{4,0},{5,1},{6,2},{7,3},{8,12},{9,13},{10,... | collective-permute-start | bytes 49160 | tf_op jit(solution)/shard_map/ppermute | solution.py:378
  74.3 1.7 %collective-permute-done.17 = bf16[32,256]{1,0:T(8,128)(2,1)S(1)} collective-permute-done((bf16[32,256]{1,0:T(8,128)(2,1)S(1)}, bf16[32,256]{1,0:T(8,128)(2,1)S(1)}, u32[]{:S(2)}, u32[]{:S(2)}) %collective-permute-start.17) | collective-permute-done | bytes 16416 | tf_op jit(solution)/shard_map/ppermute | solution.py:378
  76.0 3.0 %collective-permute-start.18 = (bf16[64,256]{1,0:T(8,128)(2,1)S(1)}, bf16[64,256]{1,0:T(8,128)(2,1)S(1)}, u32[]{:S(2)}, u32[]{:S(2)}) collective-permute-start(bf16[64,256]{1,0:T(8,128)(2,1)S(1)} %pad_maximum_fusion), channel_id=1, source_target_pairs={{0,8},{1,9},{2,10},{3,11},{4,12},{5,13},{6,14},{7,15},{8,0},{9,1},... | collective-permute-start | bytes 98312 | tf_op jit(solution)/shard_map/ppermute | solution.py:378
  79.1 1.9 %collective-permute-done.18 = bf16[64,256]{1,0:T(8,128)(2,1)S(1)} collective-permute-done((bf16[64,256]{1,0:T(8,128)(2,1)S(1)}, bf16[64,256]{1,0:T(8,128)(2,1)S(1)}, u32[]{:S(2)}, u32[]{:S(2)}) %collective-permute-start.18) | collective-permute-done | bytes 32800 | tf_op jit(solution)/shard_map/ppermute | solution.py:378
  81.0 2.0 %finish.1.hidden_ref = bf16[256,896]{1,0:T(8,128)(2,1)S(1)} custom-call(s32[42]{0:T(128)S(1)} %pad_add_fusion.table_ref, f32[256,896]{1,0:T(8,128)S(1)} %product.4.refs_0_, f32[256,896]{1,0:T(8,128)S(1)} %product.5.refs_1_, f32[256,896]{1,0:T(8,128)S(1)} %product.6.refs_2_, f32[256,896]{1,0:T(8,128)S(1)} %product.7.refs_3_, ...), custom_call_target="tpu_custom_call" | custom-call | tf_op jit(solution)/shard_map/finish/pallas_call | solution.py:234
  83.0 5.2 %copy-done.1 = bf16[896,8192]{1,0:T(8,128)(2,1)S(1)} copy-done((bf16[896,8192]{1,0:T(8,128)(2,1)S(1)}, bf16[896,8192]{1,0:T(8,128)(2,1)}, u32[]{:S(2)}) %copy-start.1) | copy-done | bytes 14680088
  88.1 10.1 %down.1 = (bf16[16,8192]{1,0:T(8,128)(2,1)S(1)}, bf16[16,8192]{1,0:T(8,128)(2,1)S(1)}, bf16[16,8192]{1,0:T(8,128)(2,1)S(1)}, bf16[16,8192]{1,0:T(8,128)(2,1)S(1)...) custom-call(s32[42]{0:T(128)S(1)} %pad_add_fusion.table_ref, ...), custom_call_target="tpu_custom_call" | custom-call | flops 3758096384 | bytes 18874368 | tf_op jit(solution)/shard_map/down/pallas_call | solution.py:287
  98.3 0.5 collective-permute-start.23
  98.8 0.1 collective-permute-start.21
  98.9 1.7 %collective-permute-done.23.refs_1_ = bf16[16,8192]{1,0:T(8,128)(2,1)S(1)} collective-permute-done((bf16[16,8192]{1,0:T(8,128)(2,1)S(1)}, bf16[16,8192]{1,0:T(8,128)(2,1)S(1)}, u32[]{:S(2)}, u32[]{:S(2)}) %collective-permute-start.23) | collective-permute-done | bytes 262176 | tf_op jit(solution)/shard_map/ppermute | solution.py:378
  100.7 2.0 %collective-permute-start.24 = (bf16[16,8192]{1,0:T(8,128)(2,1)S(1)}, bf16[16,8192]{1,0:T(8,128)(2,1)S(1)}, u32[]{:S(2)}, u32[]{:S(2)}) collective-permute-start(bf16[16,8192]{1,0:T(8,128)(2,1)S(1)} %added.7), channel_id=1, source_target_pairs={{0,4},{1,3},{4,8},{5,1},{8,12},{9,5},{12,14},{13,9},{14,10},{15,13... | collective-permute-start | bytes 786440 | tf_op jit(solution)/shard_map/ppermute | solution.py:375
  102.7 1.6 %collective-permute-start.28 = (bf16[16,8192]{1,0:T(8,128)(2,1)S(1)}, bf16[16,8192]{1,0:T(8,128)(2,1)S(1)}, u32[]{:S(2)}, u32[]{:S(2)}) collective-permute-start(bf16[16,8192]{1,0:T(8,128)(2,1)S(1)} %added.11), channel_id=1, source_target_pairs={{0,4},{1,3},{4,8},{5,1},{8,12},{9,5},{12,14},{13,9},{14,10},{15,13... | collective-permute-start | bytes 786440 | tf_op jit(solution)/shard_map/ppermute | solution.py:375
  104.3 2.8 %collective-permute-done.24.refs_2_ = bf16[16,8192]{1,0:T(8,128)(2,1)S(1)} collective-permute-done((bf16[16,8192]{1,0:T(8,128)(2,1)S(1)}, bf16[16,8192]{1,0:T(8,128)(2,1)S(1)}, u32[]{:S(2)}, u32[]{:S(2)}) %collective-permute-start.24) | collective-permute-done | bytes 262176 | tf_op jit(solution)/shard_map/ppermute | solution.py:375
  107.1 0.1 added.8
  107.2 2.0 %collective-permute-start.25 = (bf16[16,8192]{1,0:T(8,128)(2,1)S(1)}, bf16[16,8192]{1,0:T(8,128)(2,1)S(1)}, u32[]{:S(2)}, u32[]{:S(2)}) collective-permute-start(bf16[16,8192]{1,0:T(8,128)(2,1)S(1)} %added.8), channel_id=1, source_target_pairs={{0,4},{1,3},{4,8},{5,1},{8,12},{9,5},{12,14},{13,9},{14,10},{15,13... | collective-permute-start | bytes 786440 | tf_op jit(solution)/shard_map/ppermute | solution.py:375
  109.1 0.8 collective-permute-done.28.refs_2_
  109.9 0.1 added.12
  110.0 2.0 %collective-permute-start.29 = (bf16[16,8192]{1,0:T(8,128)(2,1)S(1)}, bf16[16,8192]{1,0:T(8,128)(2,1)S(1)}, u32[]{:S(2)}, u32[]{:S(2)}) collective-permute-start(bf16[16,8192]{1,0:T(8,128)(2,1)S(1)} %added.12), channel_id=1, source_target_pairs={{0,4},{1,3},{4,8},{5,1},{8,12},{9,5},{12,14},{13,9},{14,10},{15,13... | collective-permute-start | bytes 786440 | tf_op jit(solution)/shard_map/ppermute | solution.py:375
  111.9 1.7 %collective-permute-done.25.refs_2_ = bf16[16,8192]{1,0:T(8,128)(2,1)S(1)} collective-permute-done((bf16[16,8192]{1,0:T(8,128)(2,1)S(1)}, bf16[16,8192]{1,0:T(8,128)(2,1)S(1)}, u32[]{:S(2)}, u32[]{:S(2)}) %collective-permute-start.25) | collective-permute-done | bytes 262176 | tf_op jit(solution)/shard_map/ppermute | solution.py:375
  113.6 0.1 added.9
  113.7 2.0 %collective-permute-start.26 = (bf16[16,8192]{1,0:T(8,128)(2,1)S(1)}, bf16[16,8192]{1,0:T(8,128)(2,1)S(1)}, u32[]{:S(2)}, u32[]{:S(2)}) collective-permute-start(bf16[16,8192]{1,0:T(8,128)(2,1)S(1)} %added.9), channel_id=1, source_target_pairs={{0,4},{1,3},{4,8},{5,1},{8,12},{9,5},{12,14},{13,9},{14,10},{15,13... | collective-permute-start | bytes 786440 | tf_op jit(solution)/shard_map/ppermute | solution.py:375
  115.7 0.8 collective-permute-done.29.refs_2_
  116.4 0.1 added.13
  116.5 2.0 %collective-permute-start.30 = (bf16[16,8192]{1,0:T(8,128)(2,1)S(1)}, bf16[16,8192]{1,0:T(8,128)(2,1)S(1)}, u32[]{:S(2)}, u32[]{:S(2)}) collective-permute-start(bf16[16,8192]{1,0:T(8,128)(2,1)S(1)} %added.13), channel_id=1, source_target_pairs={{0,4},{1,3},{4,8},{5,1},{8,12},{9,5},{12,14},{13,9},{14,10},{15,13... | collective-permute-start | bytes 786440 | tf_op jit(solution)/shard_map/ppermute | solution.py:375
  118.5 1.7 %collective-permute-done.26.refs_2_ = bf16[16,8192]{1,0:T(8,128)(2,1)S(1)} collective-permute-done((bf16[16,8192]{1,0:T(8,128)(2,1)S(1)}, bf16[16,8192]{1,0:T(8,128)(2,1)S(1)}, u32[]{:S(2)}, u32[]{:S(2)}) %collective-permute-start.26) | collective-permute-done | bytes 262176 | tf_op jit(solution)/shard_map/ppermute | solution.py:375
  120.1 0.1 added.10
  120.2 2.0 %collective-permute-start.27 = (bf16[16,8192]{1,0:T(8,128)(2,1)S(1)}, bf16[16,8192]{1,0:T(8,128)(2,1)S(1)}, u32[]{:S(2)}, u32[]{:S(2)}) collective-permute-start(bf16[16,8192]{1,0:T(8,128)(2,1)S(1)} %added.10), channel_id=1, source_target_pairs={{0,4},{1,3},{4,8},{5,1},{8,12},{9,5},{12,14},{13,9},{14,10},{15,13... | collective-permute-start | bytes 786440 | tf_op jit(solution)/shard_map/ppermute | solution.py:375
  122.2 0.8 collective-permute-done.30
  122.9 3.7 %collective-permute-done.27.refs_2_ = bf16[16,8192]{1,0:T(8,128)(2,1)S(1)} collective-permute-done((bf16[16,8192]{1,0:T(8,128)(2,1)S(1)}, bf16[16,8192]{1,0:T(8,128)(2,1)S(1)}, u32[]{:S(2)}, u32[]{:S(2)}) %collective-permute-start.27) | collective-permute-done | bytes 262176 | tf_op jit(solution)/shard_map/ppermute | solution.py:375
  126.7 1.4 %last.1 = bf16[16,8192]{1,0:T(8,128)(2,1)} custom-call(s32[42]{0:T(128)S(1)} %pad_add_fusion.table_ref, bf16[16,8192]{1,0:T(8,128)(2,1)S(1)} %get-tuple-element.18.refs_0_, bf16[16,8192]{1,0:T(8,128)(2,1)S(1)} %collective-permute-done.19.refs_1_, bf16[16,8192]{1,0:T(8,128)(2,1)S(1)} %collective-permute-done.27.refs_2_, ...), custom_call_target="tpu_custom_call" | custom-call | tf_op jit(solution)/shard_map/last/pallas_call | solution.py:318
  (49 shorter events, 0.4 us)
Async XLA Ops:
  0.0 7.5 %collective-permute-start.1 = (bf16[16,8192]{1,0:T(8,128)(2,1)}, bf16[16,8192]{1,0:T(8,128)(2,1)S(1)}, u32[]{:S(2)}, u32[]{:S(2)}) collective-permute-start(bf16[16,8192]{1,0:T(8,128)(2,1)} %refs_0_.9), channel_id=1, source_target_pairs={{0,4},{1,3},{4,8},{5,1},{8,12},{9,5},{12,14},{13,9},{14,10},{15,13... | collective-permute-start | bytes 786440 | tf_op jit(solution)/shard_map/ppermute | solution.py:375
  3.0 6.6 %collective-permute-start = (bf16[16,8192]{1,0:T(8,128)(2,1)}, bf16[16,8192]{1,0:T(8,128)(2,1)S(1)}, u32[]{:S(2)}, u32[]{:S(2)}) collective-permute-start(bf16[16,8192]{1,0:T(8,128)(2,1)} %refs_0_.9), channel_id=1, source_target_pairs={{0,1},{1,0},{2,3},{3,2},{4,5},{5,4},{6,7},{7,6},{8,9},{9,8},{10,11... | collective-permute-start | bytes 786440 | tf_op jit(solution)/shard_map/ppermute | solution.py:378
  7.5 6.4 %collective-permute-start.3 = (bf16[16,8192]{1,0:T(8,128)(2,1)S(1)}, bf16[16,8192]{1,0:T(8,128)(2,1)S(1)}, u32[]{:S(2)}, u32[]{:S(2)}) collective-permute-start(bf16[16,8192]{1,0:T(8,128)(2,1)S(1)} %collective-permute-done.1.refs_2_), channel_id=1, source_target_pairs={{0,4},{1,3},{4,8},{5,1},{8,12},{9,5},{12,14},{13,9},{14,10},{15,13... | collective-permute-start | bytes 786440 | tf_op jit(solution)/shard_map/ppermute | solution.py:375
  9.6 7.1 %collective-permute-start.2 = (bf16[16,8192]{1,0:T(8,128)(2,1)S(1)}, bf16[16,8192]{1,0:T(8,128)(2,1)S(1)}, u32[]{:S(2)}, u32[]{:S(2)}) collective-permute-start(bf16[16,8192]{1,0:T(8,128)(2,1)S(1)} %collective-permute-done.refs_1_), channel_id=1, source_target_pairs={{0,4},{1,3},{4,8},{5,1},{8,12},{9,5},{12,14},{13,9},{14,10},{15,13... | collective-permute-start | bytes 786440 | tf_op jit(solution)/shard_map/ppermute | solution.py:375
  13.9 6.4 %collective-permute-start.5 = (bf16[16,8192]{1,0:T(8,128)(2,1)S(1)}, bf16[16,8192]{1,0:T(8,128)(2,1)S(1)}, u32[]{:S(2)}, u32[]{:S(2)}) collective-permute-start(bf16[16,8192]{1,0:T(8,128)(2,1)S(1)} %collective-permute-done.3.refs_4_), channel_id=1, source_target_pairs={{0,4},{1,3},{4,8},{5,1},{8,12},{9,5},{12,14},{13,9},{14,10},{15,13... | collective-permute-start | bytes 786440 | tf_op jit(solution)/shard_map/ppermute | solution.py:375
  16.7 6.4 %collective-permute-start.4 = (bf16[16,8192]{1,0:T(8,128)(2,1)S(1)}, bf16[16,8192]{1,0:T(8,128)(2,1)S(1)}, u32[]{:S(2)}, u32[]{:S(2)}) collective-permute-start(bf16[16,8192]{1,0:T(8,128)(2,1)S(1)} %collective-permute-done.2.refs_3_), channel_id=1, source_target_pairs={{0,4},{1,3},{4,8},{5,1},{8,12},{9,5},{12,14},{13,9},{14,10},{15,13... | collective-permute-start | bytes 786440 | tf_op jit(solution)/shard_map/ppermute | solution.py:375
  18.8 7.1 %collective-permute-start.8 = (bf16[16,8192]{1,0:T(8,128)(2,1)S(1)}, bf16[16,8192]{1,0:T(8,128)(2,1)S(1)}, u32[]{:S(2)}, u32[]{:S(2)}) collective-permute-start(bf16[16,8192]{1,0:T(8,128)(2,1)S(1)} %collective-permute-done.1.refs_2_), channel_id=1, source_target_pairs={{0,1},{1,0},{2,3},{3,2},{4,5},{5,4},{6,7},{7,6},{8,9},{9,8},{10,11... | collective-permute-start | bytes 786440 | tf_op jit(solution)/shard_map/ppermute | solution.py:378
  18.8 7.6 %collective-permute-start.9 = (bf16[16,8192]{1,0:T(8,128)(2,1)S(1)}, bf16[16,8192]{1,0:T(8,128)(2,1)S(1)}, u32[]{:S(2)}, u32[]{:S(2)}) collective-permute-start(bf16[16,8192]{1,0:T(8,128)(2,1)S(1)} %collective-permute-done.2.refs_3_), channel_id=1, source_target_pairs={{0,1},{1,0},{2,3},{3,2},{4,5},{5,4},{6,7},{7,6},{8,9},{9,8},{10,11... | collective-permute-start | bytes 786440 | tf_op jit(solution)/shard_map/ppermute | solution.py:378
  20.3 6.4 %collective-permute-start.7 = (bf16[16,8192]{1,0:T(8,128)(2,1)S(1)}, bf16[16,8192]{1,0:T(8,128)(2,1)S(1)}, u32[]{:S(2)}, u32[]{:S(2)}) collective-permute-start(bf16[16,8192]{1,0:T(8,128)(2,1)S(1)} %collective-permute-done.5.refs_6_.refs_0_), channel_id=1, source_target_pairs={{0,4},{1,3},{4,8},{5,1},{8,12},{9,5},{12,14},{13,9},{14,10},{15,13... | collective-permute-start | bytes 786440 | tf_op jit(solution)/shard_map/ppermute | solution.py:375
  23.1 6.4 %collective-permute-start.6 = (bf16[16,8192]{1,0:T(8,128)(2,1)S(1)}, bf16[16,8192]{1,0:T(8,128)(2,1)S(1)}, u32[]{:S(2)}, u32[]{:S(2)}) collective-permute-start(bf16[16,8192]{1,0:T(8,128)(2,1)S(1)} %collective-permute-done.4.refs_5_), channel_id=1, source_target_pairs={{0,4},{1,3},{4,8},{5,1},{8,12},{9,5},{12,14},{13,9},{14,10},{15,13... | collective-permute-start | bytes 786440 | tf_op jit(solution)/shard_map/ppermute | solution.py:375
  25.9 8.4 %collective-permute-start.10 = (bf16[16,8192]{1,0:T(8,128)(2,1)S(1)}, bf16[16,8192]{1,0:T(8,128)(2,1)S(1)}, u32[]{:S(2)}, u32[]{:S(2)}) collective-permute-start(bf16[16,8192]{1,0:T(8,128)(2,1)S(1)} %collective-permute-done.3.refs_4_), channel_id=1, source_target_pairs={{0,1},{1,0},{2,3},{3,2},{4,5},{5,4},{6,7},{7,6},{8,9},{9,8},{10,11... | collective-permute-start | bytes 786440 | tf_op jit(solution)/shard_map/ppermute | solution.py:378
  25.9 8.4 %collective-permute-start.12 = (bf16[16,8192]{1,0:T(8,128)(2,1)S(1)}, bf16[16,8192]{1,0:T(8,128)(2,1)S(1)}, u32[]{:S(2)}, u32[]{:S(2)}) collective-permute-start(bf16[16,8192]{1,0:T(8,128)(2,1)S(1)} %collective-permute-done.5.refs_6_.refs_0_), channel_id=1, source_target_pairs={{0,1},{1,0},{2,3},{3,2},{4,5},{5,4},{6,7},{7,6},{8,9},{9,8},{10,11... | collective-permute-start | bytes 786440 | tf_op jit(solution)/shard_map/ppermute | solution.py:378
  26.4 7.9 %collective-permute-start.11 = (bf16[16,8192]{1,0:T(8,128)(2,1)S(1)}, bf16[16,8192]{1,0:T(8,128)(2,1)S(1)}, u32[]{:S(2)}, u32[]{:S(2)}) collective-permute-start(bf16[16,8192]{1,0:T(8,128)(2,1)S(1)} %collective-permute-done.4.refs_5_), channel_id=1, source_target_pairs={{0,1},{1,0},{2,3},{3,2},{4,5},{5,4},{6,7},{7,6},{8,9},{9,8},{10,11... | collective-permute-start | bytes 786440 | tf_op jit(solution)/shard_map/ppermute | solution.py:378
  26.6 7.6 %collective-permute-start.14 = (bf16[16,8192]{1,0:T(8,128)(2,1)S(1)}, bf16[16,8192]{1,0:T(8,128)(2,1)S(1)}, u32[]{:S(2)}, u32[]{:S(2)}) collective-permute-start(bf16[16,8192]{1,0:T(8,128)(2,1)S(1)} %collective-permute-done.7.refs_8_.refs_2_), channel_id=1, source_target_pairs={{0,1},{1,0},{2,3},{3,2},{4,5},{5,4},{6,7},{7,6},{8,9},{9,8},{10,11... | collective-permute-start | bytes 786440 | tf_op jit(solution)/shard_map/ppermute | solution.py:378
  29.5 4.8 %collective-permute-start.13 = (bf16[16,8192]{1,0:T(8,128)(2,1)S(1)}, bf16[16,8192]{1,0:T(8,128)(2,1)S(1)}, u32[]{:S(2)}, u32[]{:S(2)}) collective-permute-start(bf16[16,8192]{1,0:T(8,128)(2,1)S(1)} %collective-permute-done.6.refs_7_.refs_1_), channel_id=1, source_target_pairs={{0,1},{1,0},{2,3},{3,2},{4,5},{5,4},{6,7},{7,6},{8,9},{9,8},{10,11... | collective-permute-start | bytes 786440 | tf_op jit(solution)/shard_map/ppermute | solution.py:378
  30.3 1.0 copy-start.2
  31.2 1.2 copy-start.4
  36.7 31.8 %collective-permute-start.15 = (bf16[8,256]{1,0:T(8,128)(2,1)S(1)}, bf16[8,256]{1,0:T(8,128)(2,1)S(1)}, u32[]{:S(2)}, u32[]{:S(2)}) collective-permute-start(bf16[8,256]{1,0:T(8,128)(2,1)S(1)} %ordered.1), channel_id=1, source_target_pairs={{0,1},{1,0},{2,3},{3,2},{4,5},{5,4},{6,7},{7,6},{8,9},{9,8},{10,11... | collective-permute-start | bytes 12296 | tf_op jit(solution)/shard_map/ppermute | solution.py:378
  37.2 5.2 %copy-start = (bf16[8192,896]{1,0:T(8,128)(2,1)S(1)}, bf16[8192,896]{1,0:T(8,128)(2,1)}, u32[]{:S(2)}) copy-start(bf16[8192,896]{1,0:T(8,128)(2,1)} %w_ref.8) | copy-start | bytes 44040196
  42.4 0.9 copy-start.3
  43.3 12.6 %slice-start = ((s8[14680064]{0:T(1024)(128)(4,1)}), s8[4194304]{0:T(1024)(128)(4,1)S(1)}, s32[]{:S(2)}) async-start(s8[14680064]{0:T(1024)(128)(4,1)} %bitcast.5), calls=%async_computation | async-start | bytes 8388608
  43.3 12.7 %slice-start.1 = ((s8[14680064]{0:T(1024)(128)(4,1)}), s8[4194304]{0:T(1024)(128)(4,1)S(1)}, s32[]{:S(2)}) async-start(s8[14680064]{0:T(1024)(128)(4,1)} %bitcast.5), calls=%async_computation.1 | async-start | bytes 8388608
  49.7 6.3 %slice-start.2 = ((s8[14680064]{0:T(1024)(128)(4,1)}), s8[4194304]{0:T(1024)(128)(4,1)S(1)}, s32[]{:S(2)}) async-start(s8[14680064]{0:T(1024)(128)(4,1)} %bitcast.5), calls=%async_computation.2 | async-start | bytes 8388608
  49.7 6.3 %slice-start.3 = ((s8[14680064]{0:T(1024)(128)(4,1)}), s8[2097152]{0:T(1024)(128)(4,1)S(1)}, s32[]{:S(2)}) async-start(s8[14680064]{0:T(1024)(128)(4,1)} %bitcast.5), calls=%async_computation.3 | async-start | bytes 4194304
  62.2 18.7 %copy-start.5 = (bf16[8,128,896]{2,1,0:T(8,128)(2,1)S(1)}, bf16[8,128,896]{2,1,0:T(8,128)(2,1)}, u32[]{:S(2)}) copy-start(bf16[8,128,896]{2,1,0:T(8,128)(2,1)} %refs_5_.1) | copy-start | bytes 5505028
  68.5 3.7 %collective-permute-start.16 = (bf16[16,256]{1,0:T(8,128)(2,1)S(1)}, bf16[16,256]{1,0:T(8,128)(2,1)S(1)}, u32[]{:S(2)}, u32[]{:S(2)}) collective-permute-start(bf16[16,256]{1,0:T(8,128)(2,1)S(1)} %pad_maximum_fusion.2), channel_id=1, source_target_pairs={{0,2},{1,3},{2,0},{3,1},{4,6},{5,7},{6,4},{7,5},{8,10},{9,11},{10,... | collective-permute-start | bytes 24584 | tf_op jit(solution)/shard_map/ppermute | solution.py:378
  72.2 3.8 %collective-permute-start.17 = (bf16[32,256]{1,0:T(8,128)(2,1)S(1)}, bf16[32,256]{1,0:T(8,128)(2,1)S(1)}, u32[]{:S(2)}, u32[]{:S(2)}) collective-permute-start(bf16[32,256]{1,0:T(8,128)(2,1)S(1)} %pad_maximum_fusion.1), channel_id=1, source_target_pairs={{0,4},{1,5},{2,6},{3,7},{4,0},{5,1},{6,2},{7,3},{8,12},{9,13},{10,... | collective-permute-start | bytes 49160 | tf_op jit(solution)/shard_map/ppermute | solution.py:378
  76.0 4.9 %collective-permute-start.18 = (bf16[64,256]{1,0:T(8,128)(2,1)S(1)}, bf16[64,256]{1,0:T(8,128)(2,1)S(1)}, u32[]{:S(2)}, u32[]{:S(2)}) collective-permute-start(bf16[64,256]{1,0:T(8,128)(2,1)S(1)} %pad_maximum_fusion), channel_id=1, source_target_pairs={{0,8},{1,9},{2,10},{3,11},{4,12},{5,13},{6,14},{7,15},{8,0},{9,1},... | collective-permute-start | bytes 98312 | tf_op jit(solution)/shard_map/ppermute | solution.py:378
  83.0 5.2 %copy-start.1 = (bf16[896,8192]{1,0:T(8,128)(2,1)S(1)}, bf16[896,8192]{1,0:T(8,128)(2,1)}, u32[]{:S(2)}) copy-start(bf16[896,8192]{1,0:T(8,128)(2,1)} %w_ref.9) | copy-start | bytes 44040196
  98.2 4.4 %collective-permute-start.22 = (bf16[32,8192]{1,0:T(8,128)(2,1)S(1)}, bf16[32,8192]{1,0:T(8,128)(2,1)S(1)}, u32[]{:S(2)}, u32[]{:S(2)}) collective-permute-start(bf16[32,8192]{1,0:T(8,128)(2,1)S(1)} %get-tuple-element.25), channel_id=1, source_target_pairs={{0,1},{1,0},{2,3},{3,2},{4,5},{5,4},{6,7},{7,6},{8,9},{9,8},{10,11... | collective-permute-start | bytes 1572872 | tf_op jit(solution)/shard_map/ppermute | solution.py:378
  98.3 2.3 %collective-permute-start.23 = (bf16[16,8192]{1,0:T(8,128)(2,1)S(1)}, bf16[16,8192]{1,0:T(8,128)(2,1)S(1)}, u32[]{:S(2)}, u32[]{:S(2)}) collective-permute-start(bf16[16,8192]{1,0:T(8,128)(2,1)S(1)} %get-tuple-element.27), channel_id=1, source_target_pairs={{0,1},{1,0},{2,3},{3,2},{4,5},{5,4},{6,7},{7,6},{8,9},{9,8},{10,11... | collective-permute-start | bytes 786440 | tf_op jit(solution)/shard_map/ppermute | solution.py:378
  98.8 10.3 %collective-permute-start.21 = (bf16[32,8192]{1,0:T(8,128)(2,1)S(1)}, bf16[32,8192]{1,0:T(8,128)(2,1)S(1)}, u32[]{:S(2)}, u32[]{:S(2)}) collective-permute-start(bf16[32,8192]{1,0:T(8,128)(2,1)S(1)} %get-tuple-element.23), channel_id=1, source_target_pairs={{0,1},{1,0},{2,3},{3,2},{4,5},{5,4},{6,7},{7,6},{8,9},{9,8},{10,11... | collective-permute-start | bytes 1572872 | tf_op jit(solution)/shard_map/ppermute | solution.py:378
  100.7 6.4 %collective-permute-start.24 = (bf16[16,8192]{1,0:T(8,128)(2,1)S(1)}, bf16[16,8192]{1,0:T(8,128)(2,1)S(1)}, u32[]{:S(2)}, u32[]{:S(2)}) collective-permute-start(bf16[16,8192]{1,0:T(8,128)(2,1)S(1)} %added.7), channel_id=1, source_target_pairs={{0,4},{1,3},{4,8},{5,1},{8,12},{9,5},{12,14},{13,9},{14,10},{15,13... | collective-permute-start | bytes 786440 | tf_op jit(solution)/shard_map/ppermute | solution.py:375
  102.7 7.2 %collective-permute-start.28 = (bf16[16,8192]{1,0:T(8,128)(2,1)S(1)}, bf16[16,8192]{1,0:T(8,128)(2,1)S(1)}, u32[]{:S(2)}, u32[]{:S(2)}) collective-permute-start(bf16[16,8192]{1,0:T(8,128)(2,1)S(1)} %added.11), channel_id=1, source_target_pairs={{0,4},{1,3},{4,8},{5,1},{8,12},{9,5},{12,14},{13,9},{14,10},{15,13... | collective-permute-start | bytes 786440 | tf_op jit(solution)/shard_map/ppermute | solution.py:375
  104.3 11.3 %collective-permute-start.20 = (bf16[32,8192]{1,0:T(8,128)(2,1)S(1)}, bf16[32,8192]{1,0:T(8,128)(2,1)S(1)}, u32[]{:S(2)}, u32[]{:S(2)}) collective-permute-start(bf16[32,8192]{1,0:T(8,128)(2,1)S(1)} %get-tuple-element.21), channel_id=1, source_target_pairs={{0,1},{1,0},{2,3},{3,2},{4,5},{5,4},{6,7},{7,6},{8,9},{9,8},{10,11... | collective-permute-start | bytes 1572872 | tf_op jit(solution)/shard_map/ppermute | solution.py:378
  107.2 6.4 %collective-permute-start.25 = (bf16[16,8192]{1,0:T(8,128)(2,1)S(1)}, bf16[16,8192]{1,0:T(8,128)(2,1)S(1)}, u32[]{:S(2)}, u32[]{:S(2)}) collective-permute-start(bf16[16,8192]{1,0:T(8,128)(2,1)S(1)} %added.8), channel_id=1, source_target_pairs={{0,4},{1,3},{4,8},{5,1},{8,12},{9,5},{12,14},{13,9},{14,10},{15,13... | collective-permute-start | bytes 786440 | tf_op jit(solution)/shard_map/ppermute | solution.py:375
  110.0 6.4 %collective-permute-start.29 = (bf16[16,8192]{1,0:T(8,128)(2,1)S(1)}, bf16[16,8192]{1,0:T(8,128)(2,1)S(1)}, u32[]{:S(2)}, u32[]{:S(2)}) collective-permute-start(bf16[16,8192]{1,0:T(8,128)(2,1)S(1)} %added.12), channel_id=1, source_target_pairs={{0,4},{1,3},{4,8},{5,1},{8,12},{9,5},{12,14},{13,9},{14,10},{15,13... | collective-permute-start | bytes 786440 | tf_op jit(solution)/shard_map/ppermute | solution.py:375
  113.7 6.4 %collective-permute-start.26 = (bf16[16,8192]{1,0:T(8,128)(2,1)S(1)}, bf16[16,8192]{1,0:T(8,128)(2,1)S(1)}, u32[]{:S(2)}, u32[]{:S(2)}) collective-permute-start(bf16[16,8192]{1,0:T(8,128)(2,1)S(1)} %added.9), channel_id=1, source_target_pairs={{0,4},{1,3},{4,8},{5,1},{8,12},{9,5},{12,14},{13,9},{14,10},{15,13... | collective-permute-start | bytes 786440 | tf_op jit(solution)/shard_map/ppermute | solution.py:375
  116.5 6.4 %collective-permute-start.30 = (bf16[16,8192]{1,0:T(8,128)(2,1)S(1)}, bf16[16,8192]{1,0:T(8,128)(2,1)S(1)}, u32[]{:S(2)}, u32[]{:S(2)}) collective-permute-start(bf16[16,8192]{1,0:T(8,128)(2,1)S(1)} %added.13), channel_id=1, source_target_pairs={{0,4},{1,3},{4,8},{5,1},{8,12},{9,5},{12,14},{13,9},{14,10},{15,13... | collective-permute-start | bytes 786440 | tf_op jit(solution)/shard_map/ppermute | solution.py:375
  118.5 4.5 %collective-permute-start.19 = (bf16[16,8192]{1,0:T(8,128)(2,1)S(1)}, bf16[16,8192]{1,0:T(8,128)(2,1)S(1)}, u32[]{:S(2)}, u32[]{:S(2)}) collective-permute-start(bf16[16,8192]{1,0:T(8,128)(2,1)S(1)} %get-tuple-element.19), channel_id=1, source_target_pairs={{0,1},{1,0},{2,3},{3,2},{4,5},{5,4},{6,7},{7,6},{8,9},{9,8},{10,11... | collective-permute-start | bytes 786440 | tf_op jit(solution)/shard_map/ppermute | solution.py:378
  120.2 6.4 %collective-permute-start.27 = (bf16[16,8192]{1,0:T(8,128)(2,1)S(1)}, bf16[16,8192]{1,0:T(8,128)(2,1)S(1)}, u32[]{:S(2)}, u32[]{:S(2)}) collective-permute-start(bf16[16,8192]{1,0:T(8,128)(2,1)S(1)} %added.10), channel_id=1, source_target_pairs={{0,4},{1,3},{4,8},{5,1},{8,12},{9,5},{12,14},{13,9},{14,10},{15,13... | collective-permute-start | bytes 786440 | tf_op jit(solution)/shard_map/ppermute | solution.py:375
  122.9 3.7 %collective-permute-start.31 = (bf16[16,8192]{1,0:T(8,128)(2,1)S(1)}, bf16[16,8192]{1,0:T(8,128)(2,1)S(1)}, u32[]{:S(2)}, u32[]{:S(2)}) collective-permute-start(bf16[16,8192]{1,0:T(8,128)(2,1)S(1)} %collective-permute-done.30), channel_id=1, source_target_pairs={{0,1},{1,0},{2,3},{3,2},{4,5},{5,4},{6,7},{7,6},{8,9},{9,8},{10,11... | collective-permute-start | bytes 786440 | tf_op jit(solution)/shard_map/ppermute | solution.py:378

commit v4 on v3

v4 whole, which is shorter than its diff:
```python
import functools

import jax
import jax.numpy as jnp
from jax import lax
from jax.experimental import pallas as pl
from jax.experimental.pallas import tpu as pltpu
from jax.sharding import PartitionSpec as P

F32 = jnp.float32
BF16 = jnp.bfloat16
VMEM_LIMIT = 20 * 1024 * 1024


def largest_tile(size, limit):
    tile = limit
    while size % tile:
        tile //= 2
    return tile


def params():
    return pltpu.CompilerParams(vmem_limit_bytes=VMEM_LIMIT)


def cost(flops, moved):
    return pl.CostEstimate(flops=flops, bytes_accessed=moved, transcendentals=0)


def ring_of(chips):
    return list(range(0, chips, 2)) + list(range(chips - 1, 0, -2))


def piece_row(device, members, rows, side, distance, half):
    chips = members // 2
    chip = device // 2
    place = jnp.where(chip % 2 == 0, chip // 2, chips - (chip + 1) // 2)
    spot = (place + chips + jnp.where(side == 0, distance, -distance)) % chips
    there = jnp.where(spot < chips // 2, 2 * spot, 2 * (chips - spot) - 1)
    return pl.multiple_of((2 * there + half) * rows, rows)


def arrivals(device, members, rows):
    core, reach = device % 2, members // 4
    places = [(core, 0, core), (core, 0, 1 - core)]
    for side in (core, 1 - core):
        for step in range(1, reach + 1):
            places.append((1 - side, step, side))
            if step < reach:
                places.append((1 - side, step, 1 - side))
    return [piece_row(device, members, rows, *place) for place in places]


def departures(device, members, rows):
    core, reach = device % 2, members // 4
    places = []
    for side in (core, 1 - core):
        places.append((side, reach, side))
        for step in range(reach - 1, 0, -1):
            places += [(side, step, side), (side, step, 1 - side)]
        places.append((side, 0, side))
    return [piece_row(device, members, rows, *place) for place in places]


def around(members):
    ring = ring_of(members // 2)
    size = len(ring)
    pairs = []
    for i in range(size):
        pairs.append((2 * ring[i], 2 * ring[(i + 1) % size]))
        pairs.append((2 * ring[i] + 1, 2 * ring[i - 1] + 1))
    return pairs


def crossing(members, bit):
    return [(i, i ^ bit) for i in range(members)]


def whole(count):
    return [pl.BlockSpec(memory_space=pltpu.VMEM)] * count


SCALARS = pl.BlockSpec(memory_space=pltpu.SMEM)
FAR = pl.BlockSpec(memory_space=pl.ANY)


def far(x):
    return pltpu.with_memory_space_constraint(x, pltpu.HBM)


def prepare_kernel(blocks, ids_ref, tokens_ref, shrink_ref, expand_ref, passed_in, *refs):
    own_ref, weights_ref, chosen_ref, passed_out, sems = refs
    copies = [pltpu.make_async_copy(tokens_ref, own_ref, sems.at[0])]
    for b in range(blocks):
        copies.append(
            pltpu.make_async_copy(shrink_ref.at[ids_ref[b]], weights_ref.at[b], sems.at[1 + 2 * b])
        )
        copies.append(
            pltpu.make_async_copy(expand_ref.at[ids_ref[b]], chosen_ref.at[b], sems.at[2 + 2 * b])
        )
    for copy in copies:
        copy.start()
    for copy in copies:
        copy.wait()


def prepare(adapters, tokens, shrink, expand, passed):
    blocks = adapters.shape[0]

    def like(shape):
        return jax.ShapeDtypeStruct(shape, BF16)

    return pl.pallas_call(
        functools.partial(prepare_kernel, blocks),
        in_specs=[SCALARS, FAR, FAR, FAR, FAR],
        out_specs=whole(3) + [FAR],
        out_shape=[
            like(tokens.shape),
            like((blocks,) + shrink.shape[1:]),
            like((blocks,) + expand.shape[1:]),
            like(passed.shape),
        ],
        input_output_aliases={4: 3},
        scratch_shapes=[pltpu.SemaphoreType.DMA((1 + 2 * blocks,))],
        compiler_params=params(),
        name="prepare",
    )(adapters, far(tokens), far(shrink), far(expand), passed)


def rank_kernel(shrink_ref, *refs):
    pieces, out_ref, scratch = refs[:-2], refs[-2], refs[-1]
    members = len(pieces)
    rows = pieces[0].shape[0]
    blocks, span, _ = shrink_ref.shape
    block_rows = members * rows // blocks
    places = arrivals(lax.axis_index("tp"), members, rows)
    lhs = jnp.concatenate([piece[...] for piece in pieces], axis=0)
    weights = jnp.concatenate([shrink_ref[b] for b in range(blocks)], axis=0)
    found = lax.dot_general(
        lhs, weights, (((1,), (1,)), ((), ())), preferred_element_type=F32
    )
    for index, place in enumerate(places):
        part = found[index * rows : (index + 1) * rows]
        value = part[:, :span]
        for b in range(1, blocks):
            value = jnp.where(place // block_rows == b, part[:, b * span : (b + 1) * span], value)
        scratch[pl.ds(place, rows), :span] = value
    out_ref[...] = scratch[...].T[:span].astype(BF16)


def rank_of(pieces, shrink):
    rows, model = pieces[0].shape
    blocks, span, _ = shrink.shape
    total = rows * len(pieces)
    return pl.pallas_call(
        rank_kernel,
        in_specs=whole(1 + len(pieces)),
        out_specs=whole(1)[0],
        out_shape=jax.ShapeDtypeStruct((span, total), BF16),
        scratch_shapes=[pltpu.VMEM((total, 128), F32)],
        compiler_params=params(),
        cost_estimate=cost(2 * total * model * span * blocks, 2 * total * model),
        name="rank",
    )(shrink, *pieces)


def product_kernel(first, size, chunks, slots, w_ref, *refs):
    pieces = refs[:-5]
    out_ref, total, store, sems = refs[-4:]
    rows = pieces[0].shape[0]

    def copy(chunk):
        return pltpu.make_async_copy(
            w_ref.at[pl.ds(first + chunk * size, size), :],
            store.at[chunk % slots],
            sems.at[chunk % slots],
        )

    for chunk in range(slots):
        copy(chunk).start()
    places = arrivals(lax.axis_index("tp"), len(pieces), rows)
    for chunk in range(chunks):
        start = first + chunk * size
        lhs = jnp.concatenate([piece[:, start : start + size] for piece in pieces], axis=0)
        copy(chunk).wait()
        part = jnp.dot(lhs, store[chunk % slots], preferred_element_type=F32)
        if chunk + slots < chunks:
            copy(chunk + slots).start()
        if chunk > 0:
            part += total[...]
        if chunk < chunks - 1:
            total[...] = part
    for index, place in enumerate(places):
        out_ref[pl.ds(place, rows), :] = part[index * rows : (index + 1) * rows]


def product(pieces, matrix, part, parts, after):
    rows, model = pieces[0].shape
    total = rows * len(pieces)
    width = matrix.shape[1]
    depth = model // parts
    size = min(1024, depth)
    chunks = depth // size
    slots = min(4, chunks)
    return pl.pallas_call(
        functools.partial(product_kernel, part * depth, size, chunks, slots),
        in_specs=[FAR] + whole(len(pieces) + 1),
        out_specs=whole(1)[0],
        out_shape=jax.ShapeDtypeStruct((total, width), F32),
        scratch_shapes=[
            pltpu.VMEM((total, width), F32),
            pltpu.VMEM((slots, size, width), BF16),
            pltpu.SemaphoreType.DMA((slots,)),
        ],
        compiler_params=params(),
        cost_estimate=cost(2 * total * depth * width, 2 * depth * (width + total)),
        name="product",
    )(far(matrix), *pieces, after)


def finish_kernel(span, gate_a, gate_b, up_a, up_b, rank_ref, expand_ref, hidden_ref):
    ranks = rank_ref.shape[0]
    device = lax.axis_index("tp")
    shape = (ranks, ranks)
    want = lax.broadcasted_iota(jnp.int32, shape, 0)
    have = lax.broadcasted_iota(jnp.int32, shape, 1)
    origin = ((have // span) ^ device) * span + have % span
    order = jnp.where(want == origin, 1.0, 0.0).astype(BF16)
    rank = jnp.dot(order, rank_ref[...], preferred_element_type=F32).T.astype(BF16)
    half = ranks // 2
    blocks = expand_ref.shape[0]
    rows = hidden_ref.shape[0] // blocks
    for b in range(blocks):
        part = slice(b * rows, (b + 1) * rows)
        expand = expand_ref[b]
        gate = jnp.dot(rank[part, :half], expand[:half], preferred_element_type=F32)
        up = jnp.dot(rank[part, half:], expand[half:], preferred_element_type=F32)
        gate += gate_a[part] + gate_b[part]
        up += up_a[part] + up_b[part]
        hidden_ref[part] = (gate / (1.0 + jnp.exp(-gate)) * up).astype(BF16)


def finish(products, rank, expand, span):
    total, width = products[0].shape
    return pl.pallas_call(
        functools.partial(finish_kernel, span),
        in_specs=whole(6),
        out_specs=whole(1)[0],
        out_shape=jax.ShapeDtypeStruct((total, width), BF16),
        compiler_params=params(),
        name="finish",
    )(*products, rank, expand)


def down_kernel(members, groups, rows, chunks, slots, w_ref, hidden_ref, *refs):
    outs, (product_ref, store, sems) = refs[:-3], refs[-3:]
    size = store.shape[2]

    def copy(chunk):
        return pltpu.make_async_copy(
            w_ref.at[:, pl.ds(chunk * size, size)],
            store.at[chunk % slots],
            sems.at[chunk % slots],
        )

    for chunk in range(slots):
        copy(chunk).start()
    places = departures(lax.axis_index("tp"), members, rows)
    hidden = hidden_ref[...]
    for chunk in range(chunks):
        columns = slice(chunk * size, (chunk + 1) * size)
        copy(chunk).wait()
        part = jnp.dot(hidden, store[chunk % slots], preferred_element_type=F32)
        if chunk + slots < chunks:
            copy(chunk + slots).start()
        product_ref[...] = part.astype(BF16)
        at = 0
        for out, group in zip(outs, groups, strict=True):
            for index in range(group):
                out[index * rows : (index + 1) * rows, columns] = product_ref[
                    pl.ds(places[at], rows), :
                ]
                at += 1


def down(hidden, down_matrix, groups, rows):
    total, depth = hidden.shape
    columns = down_matrix.shape[1]
    size = min(1024, columns)
    chunks = columns // size
    slots = min(4, chunks)
    return pl.pallas_call(
        functools.partial(down_kernel, total // rows, groups, rows, chunks, slots),
        in_specs=[FAR] + whole(1),
        out_specs=whole(len(groups)),
        out_shape=[jax.ShapeDtypeStruct((group * rows, columns), BF16) for group in groups],
        scratch_shapes=[
            pltpu.VMEM((total, size), BF16),
            pltpu.VMEM((slots, depth, size), BF16),
            pltpu.SemaphoreType.DMA((slots,)),
        ],
        compiler_params=params(),
        cost_estimate=cost(
            2 * total * depth * columns, 2 * depth * columns + 2 * total * columns
        ),
        name="down",
    )(far(down_matrix), hidden)


def last_kernel(blocks, members, counts_ref, *refs):
    out_ref = refs[-1]
    rows = out_ref.shape[0]
    summed = refs[0][...].astype(F32)
    for ref in refs[1:-1]:
        summed += ref[...].astype(F32)
    first = lax.axis_index("tp") * rows
    block_rows = members * rows // blocks
    live = counts_ref[first // block_rows] - first % block_rows
    row = lax.broadcasted_iota(jnp.int32, summed.shape, 0)
    out_ref[...] = jnp.where(row < live, summed, 0.0).astype(BF16)


def last(members, counts, terms):
    return pl.pallas_call(
        functools.partial(last_kernel, counts.shape[0], members),
        in_specs=[SCALARS] + whole(len(terms)),
        out_specs=whole(1)[0],
        out_shape=jax.ShapeDtypeStruct(terms[0].shape, BF16),
        compiler_params=params(),
        name="last",
    )(counts, *terms)


def add_kernel(starts, *refs):
    out_ref = refs[-1]
    rows = out_ref.shape[0]
    total = 0.0
    for start, ref in zip(starts, refs[:-1], strict=True):
        total += ref[start : start + rows, :].astype(F32)
    out_ref[...] = total.astype(BF16)


def added(rows, *terms):
    starts = [start for start, _ in terms]
    columns = terms[0][1].shape[1]
    return pl.pallas_call(
        functools.partial(add_kernel, starts),
        in_specs=whole(len(terms)),
        out_specs=whole(1)[0],
        out_shape=jax.ShapeDtypeStruct((rows, columns), BF16),
        compiler_params=params(),
        cost_estimate=cost(len(terms) * rows * columns, 2 * rows * columns),
        name="added",
    )(*[term for _, term in terms])


def per_device(
    members,
    tokens,
    gate_matrix,
    up_matrix,
    down_matrix,
    shrink_matrices,
    expand_matrices,
    adapter_per_block,
    block_token_count,
):
    rows = tokens.shape[0]
    span = shrink_matrices.shape[2]
    reach = members // 4
    ring = around(members)

    def step(x):
        return lax.ppermute(x, "tp", ring)

    def cross(x, bit=1):
        return lax.ppermute(x, "tp", crossing(members, bit))

    first = tokens
    own, shrink, expand, second = prepare(
        adapter_per_block,
        tokens,
        jnp.swapaxes(shrink_matrices, 1, 2),
        expand_matrices,
        cross(tokens),
    )
    pieces, mine, theirs = [own, second], [], []
    for distance in range(1, reach + 1):
        first = step(first)
        mine.append(first)
        theirs.append(cross(first))
        if distance < reach:
            second = step(second)
            mine.append(second)
            theirs.append(cross(second))
    pieces = pieces + mine + theirs

    rank = rank_of(pieces, shrink)
    work = [(gate_matrix, 0), (gate_matrix, 1), (up_matrix, 0), (up_matrix, 1)]
    products, after = [], rank
    bit = 1
    while bit < members or work:
        if work:
            matrix, part = work.pop(0)
            products.append(product(pieces, matrix, part, 2, after))
        if bit < members:
            after = cross(rank, bit)
            rank = jnp.concatenate([rank, after], axis=0)
            bit *= 2
    hidden = finish(products, rank, expand, span)

    slots = 2 * reach
    groups = [1] * slots + [1] + [2] * (reach - 1) + [1]
    outs = down(hidden, down_matrix, groups, rows)
    keep, give = outs[:slots], outs[slots:]
    came = [cross(x) for x in give]
    first = step(added(rows, (0, keep[0]), (0, came[0])))
    second = None
    for index in range(1, reach):
        more = [] if second is None else [(0, second)]
        second = step(added(rows, (0, keep[2 * index]), (rows, came[index]), *more))
        first = step(added(rows, (0, keep[2 * index - 1]), (0, came[index]), (0, first)))
    return last(members, block_token_count, [keep[-1], came[-1], first, cross(second)])


def solution(mesh):
    members = mesh.shape["tp"]
    return jax.shard_map(
        functools.partial(per_device, members),
        mesh=mesh,
        in_specs=(
            P(("rep", "tp"), None),
            P(None, "tp"),
            P(None, "tp"),
            P("tp", None),
            P("rep", None, "tp"),
            P("rep", None, "tp"),
            P("rep"),
            P("rep"),
        ),
        out_specs=P(("rep", "tp"), None),
        check_vma=False,
    )
```

time: 128 us -> 93.1 us (0.73)
  local copies, waits for them, and re-layouts: 14.3 us -> 0.68 us
  starting transfers between devices: 38.1 us -> 25.3 us
  Pallas kernels: 43.3 us -> 31.5 us
  waiting for transfers between devices: 31.4 us -> 35.2 us
    unnamed x24 -> x8, local copies, waits for them, and re-layouts: 13.5 us -> 0.67 us
    pallas_call x10 -> x9, Pallas kernels: 42.6 us -> 30.9 us  [the longest x4 17.8 us: product(): pl.pallas_call(functools.partial(product_kernel, part * depth, size, chun...]
    ppermute x14, starting transfers between devices: 28.3 us -> 16.9 us  [step(): return lax.ppermute(x, 'tp', ring)]
    ppermute x14, waiting for transfers between devices: 24.5 us -> 31.9 us  [step(): return lax.ppermute(x, 'tp', ring)]
    ppermute x18, waiting for transfers between devices: 6.96 us -> 3.24 us  [cross(): return lax.ppermute(x, 'tp', crossing(members, bit))]
    ppermute x18, starting transfers between devices: 9.73 us -> 8.44 us  [cross(): return lax.ppermute(x, 'tp', crossing(members, bit))]
  transfers between devices with their start and end apart: 32 -> 32, of which waited for: 18 -> 16; matrix products, arithmetic and copies ran while one was open for 1% -> 0% of each run, Pallas kernels for 21% -> 22%
where the time goes in v4:
time: 93.1 us; the launch traced here: 92.9 us
  waiting for transfers between devices  35.2 us (38%)
  Pallas kernels  31.5 us (34%)
  starting transfers between devices  25.3 us (27%)
    ppermute x14, waiting for transfers between devices, step(): return lax.ppermute(x, 'tp', ring)  31.9 us
    pallas_call x4, Pallas kernels, product(): pl.pallas_call(functools.partial(product_kernel, part * depth, size, chun...  17.8 us
    ppermute x14, starting transfers between devices, step(): return lax.ppermute(x, 'tp', ring)  16.9 us
    ppermute x18, starting transfers between devices, cross(): return lax.ppermute(x, 'tp', crossing(members, bit))  8.44 us
    pallas_call x1, Pallas kernels, down(): pl.pallas_call(functools.partial(down_kernel, total // rows, groups, rows...  7.53 us
    ppermute x18, waiting for transfers between devices, cross(): return lax.ppermute(x, 'tp', crossing(members, bit))  3.24 us
  transfers between devices with their start and end apart: 32, of which 16 were waited for; matrix products, arithmetic and copies ran while one was open for 0% of the time, Pallas kernels for 22%

profile of v4, /device:TPU:0, one launch (start us, length us, event | category | flops | bytes accessed | tf_op | source)
XLA Modules:
  0.0 92.9 jit_solution(15995424538849656142)
XLA Ops:
  0.0 0.5 collective-permute-start
  0.5 2.6 %collective-permute-start.1 = (bf16[16,8192]{1,0:T(8,128)(2,1)}, bf16[16,8192]{1,0:T(8,128)(2,1)S(1)}, u32[]{:S(2)}, u32[]{:S(2)}) collective-permute-start(bf16[16,8192]{1,0:T(8,128)(2,1)} %tokens_ref.1), channel_id=1, source_target_pairs={{0,4},{1,3},{4,8},{5,1},{8,12},{9,5},{12,14},{13,9},{14,10},{15,13... | collective-permute-start | bytes 786440 | tf_op jit(solution)/shard_map/ppermute | solution.py:374
  3.0 0.0 collective-permute-done.passed_in
  3.0 0.7 copy-done
  3.7 1.8 %prepare.1 = (bf16[16,8192]{1,0:T(8,128)(2,1)S(1)}, bf16[2,8,8192]{2,1,0:T(8,128)(2,1)S(1)}, bf16[2,128,896]{2,1,0:T(8,128)(2,1)S(1)}, bf16[16,8192]{1,0:T(8,128)(2,1)S(1)}) custom-call(s32[2]{0:T(128)S(1)} %copy-done, bf16[16,8192]{1,0:T(8,128)(2,1)} %tokens_ref.1, bf16[8,8,8192]{2,1,0:T(8,128)(2,1)} %bitcast.1, ...), custom_call_target="tpu_custom_call", output_to_operand_aliasing={{3}: (4, {})} | custom-call | tf_op jit(solution)/shard_map/prepare/pallas_call | solution.py:113
  5.5 1.8 %collective-permute-start.2 = (bf16[16,8192]{1,0:T(8,128)(2,1)S(1)}, bf16[16,8192]{1,0:T(8,128)(2,1)S(1)}, u32[]{:S(2)}, u32[]{:S(2)}) collective-permute-start(bf16[16,8192]{1,0:T(8,128)(2,1)S(1)} %get-tuple-element.23.refs_1_), channel_id=1, source_target_pairs={{0,4},{1,3},{4,8},{5,1},{8,12},{9,5},{12,14},{13,9},{14,10},{15,13... | collective-permute-start | bytes 786440 | tf_op jit(solution)/shard_map/ppermute | solution.py:374
  7.3 0.2 collective-permute-done.1.refs_2_
  7.5 2.1 %collective-permute-start.3 = (bf16[16,8192]{1,0:T(8,128)(2,1)S(1)}, bf16[16,8192]{1,0:T(8,128)(2,1)S(1)}, u32[]{:S(2)}, u32[]{:S(2)}) collective-permute-start(bf16[16,8192]{1,0:T(8,128)(2,1)S(1)} %collective-permute-done.1.refs_2_), channel_id=1, source_target_pairs={{0,4},{1,3},{4,8},{5,1},{8,12},{9,5},{12,14},{13,9},{14,10},{15,13... | collective-permute-start | bytes 786440 | tf_op jit(solution)/shard_map/ppermute | solution.py:374
  9.6 2.3 %collective-permute-done.2.refs_3_ = bf16[16,8192]{1,0:T(8,128)(2,1)S(1)} collective-permute-done((bf16[16,8192]{1,0:T(8,128)(2,1)S(1)}, bf16[16,8192]{1,0:T(8,128)(2,1)S(1)}, u32[]{:S(2)}, u32[]{:S(2)}) %collective-permute-start.2) | collective-permute-done | bytes 262176 | tf_op jit(solution)/shard_map/ppermute | solution.py:374
  11.9 1.7 %collective-permute-start.4 = (bf16[16,8192]{1,0:T(8,128)(2,1)S(1)}, bf16[16,8192]{1,0:T(8,128)(2,1)S(1)}, u32[]{:S(2)}, u32[]{:S(2)}) collective-permute-start(bf16[16,8192]{1,0:T(8,128)(2,1)S(1)} %collective-permute-done.2.refs_3_), channel_id=1, source_target_pairs={{0,4},{1,3},{4,8},{5,1},{8,12},{9,5},{12,14},{13,9},{14,10},{15,13... | collective-permute-start | bytes 786440 | tf_op jit(solution)/shard_map/ppermute | solution.py:374
  13.7 1.1 %collective-permute-done.3.refs_4_ = bf16[16,8192]{1,0:T(8,128)(2,1)S(1)} collective-permute-done((bf16[16,8192]{1,0:T(8,128)(2,1)S(1)}, bf16[16,8192]{1,0:T(8,128)(2,1)S(1)}, u32[]{:S(2)}, u32[]{:S(2)}) %collective-permute-start.3) | collective-permute-done | bytes 262176 | tf_op jit(solution)/shard_map/ppermute | solution.py:374
  14.7 1.7 %collective-permute-start.5 = (bf16[16,8192]{1,0:T(8,128)(2,1)S(1)}, bf16[16,8192]{1,0:T(8,128)(2,1)S(1)}, u32[]{:S(2)}, u32[]{:S(2)}) collective-permute-start(bf16[16,8192]{1,0:T(8,128)(2,1)S(1)} %collective-permute-done.3.refs_4_), channel_id=1, source_target_pairs={{0,4},{1,3},{4,8},{5,1},{8,12},{9,5},{12,14},{13,9},{14,10},{15,13... | collective-permute-start | bytes 786440 | tf_op jit(solution)/shard_map/ppermute | solution.py:374
  16.5 0.5 collective-permute-start.9
  17.0 1.3 %collective-permute-done.4.refs_5_ = bf16[16,8192]{1,0:T(8,128)(2,1)S(1)} collective-permute-done((bf16[16,8192]{1,0:T(8,128)(2,1)S(1)}, bf16[16,8192]{1,0:T(8,128)(2,1)S(1)}, u32[]{:S(2)}, u32[]{:S(2)}) %collective-permute-start.4) | collective-permute-done | bytes 262176 | tf_op jit(solution)/shard_map/ppermute | solution.py:374
  18.3 1.7 %collective-permute-start.6 = (bf16[16,8192]{1,0:T(8,128)(2,1)S(1)}, bf16[16,8192]{1,0:T(8,128)(2,1)S(1)}, u32[]{:S(2)}, u32[]{:S(2)}) collective-permute-start(bf16[16,8192]{1,0:T(8,128)(2,1)S(1)} %collective-permute-done.4.refs_5_), channel_id=1, source_target_pairs={{0,4},{1,3},{4,8},{5,1},{8,12},{9,5},{12,14},{13,9},{14,10},{15,13... | collective-permute-start | bytes 786440 | tf_op jit(solution)/shard_map/ppermute | solution.py:374
  20.0 1.1 %collective-permute-done.5.refs_6_ = bf16[16,8192]{1,0:T(8,128)(2,1)S(1)} collective-permute-done((bf16[16,8192]{1,0:T(8,128)(2,1)S(1)}, bf16[16,8192]{1,0:T(8,128)(2,1)S(1)}, u32[]{:S(2)}, u32[]{:S(2)}) %collective-permute-start.5) | collective-permute-done | bytes 262176 | tf_op jit(solution)/shard_map/ppermute | solution.py:374
  21.1 1.7 %collective-permute-start.7 = (bf16[16,8192]{1,0:T(8,128)(2,1)S(1)}, bf16[16,8192]{1,0:T(8,128)(2,1)S(1)}, u32[]{:S(2)}, u32[]{:S(2)}) collective-permute-start(bf16[16,8192]{1,0:T(8,128)(2,1)S(1)} %collective-permute-done.5.refs_6_), channel_id=1, source_target_pairs={{0,4},{1,3},{4,8},{5,1},{8,12},{9,5},{12,14},{13,9},{14,10},{15,13... | collective-permute-start | bytes 786440 | tf_op jit(solution)/shard_map/ppermute | solution.py:374
  22.9 0.0 collective-permute-start.10
  22.9 0.0 collective-permute-done.8.refs_9_
  22.9 0.5 collective-permute-start.11
  23.4 0.0 collective-permute-done.9.refs_10_
  23.4 0.1 collective-permute-start.12
  23.4 1.2 %collective-permute-done.6.refs_7_ = bf16[16,8192]{1,0:T(8,128)(2,1)S(1)} collective-permute-done((bf16[16,8192]{1,0:T(8,128)(2,1)S(1)}, bf16[16,8192]{1,0:T(8,128)(2,1)S(1)}, u32[]{:S(2)}, u32[]{:S(2)}) %collective-permute-start.6) | collective-permute-done | bytes 262176 | tf_op jit(solution)/shard_map/ppermute | solution.py:374
  24.7 2.8 %collective-permute-done.7.refs_8_ = bf16[16,8192]{1,0:T(8,128)(2,1)S(1)} collective-permute-done((bf16[16,8192]{1,0:T(8,128)(2,1)S(1)}, bf16[16,8192]{1,0:T(8,128)(2,1)S(1)}, u32[]{:S(2)}, u32[]{:S(2)}) %collective-permute-start.7) | collective-permute-done | bytes 262176 | tf_op jit(solution)/shard_map/ppermute | solution.py:374
  27.5 0.0 collective-permute-start.14
  27.5 1.5 %collective-permute-done.14.refs_15_ = bf16[16,8192]{1,0:T(8,128)(2,1)S(1)} collective-permute-done((bf16[16,8192]{1,0:T(8,128)(2,1)S(1)}, bf16[16,8192]{1,0:T(8,128)(2,1)S(1)}, u32[]{:S(2)}, u32[]{:S(2)}) %collective-permute-start.14) | collective-permute-done | bytes 262176 | tf_op jit(solution)/shard_map/ppermute | solution.py:377
  29.0 1.4 %rank.1.refs_16_ = bf16[8,256]{1,0:T(8,128)(2,1)S(1)} custom-call(bf16[2,8,8192]{2,1,0:T(8,128)(2,1)S(1)} %get-tuple-element.24.shrink_ref, bf16[16,8192]{1,0:T(8,128)(2,1)S(1)} %get-tuple-element.22.refs_0_, bf16[16,8192]{1,0:T(8,128)(2,1)S(1)} %get-tuple-element.23.refs_1_, bf16[16,8192]{1,0:T(8,128)(2,1)S(1)} %collective-permute-done.1.refs_2_, ...), custom_call_target="tpu_custom_call" | custom-call | flops 67108864 | bytes 4194304 | tf_op jit(solution)/shard_map/rank/pallas_call | solution.py:155
  30.5 0.2 collective-permute-start.15
  30.6 4.4 %product.4.gate_a = f32[256,896]{1,0:T(8,128)S(1)} custom-call(bf16[8192,896]{1,0:T(8,128)(2,1)} %w_ref.6, bf16[16,8192]{1,0:T(8,128)(2,1)S(1)} %get-tuple-element.22.refs_0_, bf16[16,8192]{1,0:T(8,128)(2,1)S(1)} %get-tuple-element.23.refs_1_, bf16[16,8192]{1,0:T(8,128)(2,1)S(1)} %collective-permute-done.1.refs_2_, ...), custom_call_target="tpu_custom_call" | custom-call | flops 1879048192 | bytes 9437184 | tf_op jit(solution)/shard_map/product/pallas_call | solution.py:205
  35.1 1.8 %collective-permute-start.16 = (bf16[16,256]{1,0:T(8,128)(2,1)S(1)}, bf16[16,256]{1,0:T(8,128)(2,1)S(1)}, u32[]{:S(2)}, u32[]{:S(2)}) collective-permute-start(bf16[16,256]{1,0:T(8,128)(2,1)S(1)} %pad_maximum_fusion.2), channel_id=1, source_target_pairs={{0,2},{1,3},{2,0},{3,1},{4,6},{5,7},{6,4},{7,5},{8,10},{9,11},{10,... | collective-permute-start | bytes 24584 | tf_op jit(solution)/shard_map/ppermute | solution.py:377
  36.9 4.4 %product.5.gate_b = f32[256,896]{1,0:T(8,128)S(1)} custom-call(bf16[8192,896]{1,0:T(8,128)(2,1)} %w_ref.6, bf16[16,8192]{1,0:T(8,128)(2,1)S(1)} %get-tuple-element.22.refs_0_, bf16[16,8192]{1,0:T(8,128)(2,1)S(1)} %get-tuple-element.23.refs_1_, bf16[16,8192]{1,0:T(8,128)(2,1)S(1)} %collective-permute-done.1.refs_2_, ...), custom_call_target="tpu_custom_call" | custom-call | flops 1879048192 | bytes 9437184 | tf_op jit(solution)/shard_map/product/pallas_call | solution.py:205
  41.4 1.6 %collective-permute-start.17 = (bf16[32,256]{1,0:T(8,128)(2,1)S(1)}, bf16[32,256]{1,0:T(8,128)(2,1)S(1)}, u32[]{:S(2)}, u32[]{:S(2)}) collective-permute-start(bf16[32,256]{1,0:T(8,128)(2,1)S(1)} %pad_maximum_fusion.1), channel_id=1, source_target_pairs={{0,4},{1,5},{2,6},{3,7},{4,0},{5,1},{6,2},{7,3},{8,12},{9,13},{10,... | collective-permute-start | bytes 49160 | tf_op jit(solution)/shard_map/ppermute | solution.py:377
  43.0 4.4 %product.6.up_a = f32[256,896]{1,0:T(8,128)S(1)} custom-call(bf16[8192,896]{1,0:T(8,128)(2,1)} %w_ref.8, bf16[16,8192]{1,0:T(8,128)(2,1)S(1)} %get-tuple-element.22.refs_0_, bf16[16,8192]{1,0:T(8,128)(2,1)S(1)} %get-tuple-element.23.refs_1_, bf16[16,8192]{1,0:T(8,128)(2,1)S(1)} %collective-permute-done.1.refs_2_, ...), custom_call_target="tpu_custom_call" | custom-call | flops 1879048192 | bytes 9437184 | tf_op jit(solution)/shard_map/product/pallas_call | solution.py:205
  47.5 2.7 %collective-permute-start.18 = (bf16[64,256]{1,0:T(8,128)(2,1)S(1)}, bf16[64,256]{1,0:T(8,128)(2,1)S(1)}, u32[]{:S(2)}, u32[]{:S(2)}) collective-permute-start(bf16[64,256]{1,0:T(8,128)(2,1)S(1)} %pad_maximum_fusion), channel_id=1, source_target_pairs={{0,8},{1,9},{2,10},{3,11},{4,12},{5,13},{6,14},{7,15},{8,0},{9,1},... | collective-permute-start | bytes 98312 | tf_op jit(solution)/shard_map/ppermute | solution.py:377
  50.2 4.4 %product.7.up_b = f32[256,896]{1,0:T(8,128)S(1)} custom-call(bf16[8192,896]{1,0:T(8,128)(2,1)} %w_ref.8, bf16[16,8192]{1,0:T(8,128)(2,1)S(1)} %get-tuple-element.22.refs_0_, bf16[16,8192]{1,0:T(8,128)(2,1)S(1)} %get-tuple-element.23.refs_1_, bf16[16,8192]{1,0:T(8,128)(2,1)S(1)} %collective-permute-done.1.refs_2_, ...), custom_call_target="tpu_custom_call" | custom-call | flops 1879048192 | bytes 9437184 | tf_op jit(solution)/shard_map/product/pallas_call | solution.py:205
  54.6 0.0 copy-start.1
  54.7 0.9 finish.1.hidden_ref
  55.6 7.5 %down.1 = (bf16[16,8192]{1,0:T(8,128)(2,1)S(1)}, bf16[16,8192]{1,0:T(8,128)(2,1)S(1)}, bf16[16,8192]{1,0:T(8,128)(2,1)S(1)}, bf16[16,8192]{1,0:T(8,128)(2,1)S(1)...) custom-call(bf16[896,8192]{1,0:T(8,128)(2,1)} %w_ref.9, ...), custom_call_target="tpu_custom_call" | custom-call | flops 3758096384 | bytes 18874368 | tf_op jit(solution)/shard_map/down/pallas_call | solution.py:292
  63.1 0.1 collective-permute-start.22
  63.2 0.5 collective-permute-start.23
  63.7 0.1 collective-permute-start.21
  63.8 1.7 %collective-permute-done.23.refs_1_ = bf16[16,8192]{1,0:T(8,128)(2,1)S(1)} collective-permute-done((bf16[16,8192]{1,0:T(8,128)(2,1)S(1)}, bf16[16,8192]{1,0:T(8,128)(2,1)S(1)}, u32[]{:S(2)}, u32[]{:S(2)}) %collective-permute-start.23) | collective-permute-done | bytes 262176 | tf_op jit(solution)/shard_map/ppermute | solution.py:377
  65.5 0.1 added.7
  65.5 0.5 collective-permute-start.24
  66.0 0.1 added.11
  66.1 0.5 collective-permute-start.28
  66.6 5.3 %collective-permute-done.24.refs_2_ = bf16[16,8192]{1,0:T(8,128)(2,1)S(1)} collective-permute-done((bf16[16,8192]{1,0:T(8,128)(2,1)S(1)}, bf16[16,8192]{1,0:T(8,128)(2,1)S(1)}, u32[]{:S(2)}, u32[]{:S(2)}) %collective-permute-start.24) | collective-permute-done | bytes 262176 | tf_op jit(solution)/shard_map/ppermute | solution.py:374
  71.9 0.1 added.8
  72.0 0.5 collective-permute-start.25
  72.5 2.2 %collective-permute-done.28.refs_2_ = bf16[16,8192]{1,0:T(8,128)(2,1)S(1)} collective-permute-done((bf16[16,8192]{1,0:T(8,128)(2,1)S(1)}, bf16[16,8192]{1,0:T(8,128)(2,1)S(1)}, u32[]{:S(2)}, u32[]{:S(2)}) %collective-permute-start.28) | collective-permute-done | bytes 262176 | tf_op jit(solution)/shard_map/ppermute | solution.py:374
  74.8 0.1 added.12
  74.9 0.5 collective-permute-start.29
  75.3 3.1 %collective-permute-done.25.refs_2_ = bf16[16,8192]{1,0:T(8,128)(2,1)S(1)} collective-permute-done((bf16[16,8192]{1,0:T(8,128)(2,1)S(1)}, bf16[16,8192]{1,0:T(8,128)(2,1)S(1)}, u32[]{:S(2)}, u32[]{:S(2)}) %collective-permute-start.25) | collective-permute-done | bytes 262176 | tf_op jit(solution)/shard_map/ppermute | solution.py:374
  78.5 0.1 added.9
  78.6 0.5 collective-permute-start.26
  79.1 2.2 %collective-permute-done.29.refs_2_ = bf16[16,8192]{1,0:T(8,128)(2,1)S(1)} collective-permute-done((bf16[16,8192]{1,0:T(8,128)(2,1)S(1)}, bf16[16,8192]{1,0:T(8,128)(2,1)S(1)}, u32[]{:S(2)}, u32[]{:S(2)}) %collective-permute-start.29) | collective-permute-done | bytes 262176 | tf_op jit(solution)/shard_map/ppermute | solution.py:374
  81.3 0.1 added.13
  81.4 0.5 collective-permute-start.30
  81.9 3.1 %collective-permute-done.26.refs_2_ = bf16[16,8192]{1,0:T(8,128)(2,1)S(1)} collective-permute-done((bf16[16,8192]{1,0:T(8,128)(2,1)S(1)}, bf16[16,8192]{1,0:T(8,128)(2,1)S(1)}, u32[]{:S(2)}, u32[]{:S(2)}) %collective-permute-start.26) | collective-permute-done | bytes 262176 | tf_op jit(solution)/shard_map/ppermute | solution.py:374
  85.0 0.1 added.10
  85.1 0.5 collective-permute-start.27
  85.6 2.2 %collective-permute-done.30 = bf16[16,8192]{1,0:T(8,128)(2,1)S(1)} collective-permute-done((bf16[16,8192]{1,0:T(8,128)(2,1)S(1)}, bf16[16,8192]{1,0:T(8,128)(2,1)S(1)}, u32[]{:S(2)}, u32[]{:S(2)}) %collective-permute-start.30) | collective-permute-done | bytes 262176 | tf_op jit(solution)/shard_map/ppermute | solution.py:374
  87.8 3.7 %collective-permute-done.27.refs_2_ = bf16[16,8192]{1,0:T(8,128)(2,1)S(1)} collective-permute-done((bf16[16,8192]{1,0:T(8,128)(2,1)S(1)}, bf16[16,8192]{1,0:T(8,128)(2,1)S(1)}, u32[]{:S(2)}, u32[]{:S(2)}) %collective-permute-start.27) | collective-permute-done | bytes 262176 | tf_op jit(solution)/shard_map/ppermute | solution.py:374
  91.5 1.4 %last.1 = bf16[16,8192]{1,0:T(8,128)(2,1)} custom-call(s32[2]{0:T(128)S(1)} %copy-done.1, bf16[16,8192]{1,0:T(8,128)(2,1)S(1)} %get-tuple-element.26.refs_0_, bf16[16,8192]{1,0:T(8,128)(2,1)S(1)} %collective-permute-done.19.refs_1_, bf16[16,8192]{1,0:T(8,128)(2,1)S(1)} %collective-permute-done.27.refs_2_, bf16[16,8192]{1,0:T(8,128)(2,1)S(1)} %collective-permute-done.31.refs_3_), custom_call_target="tpu_custom_call" | custom-call | tf_op jit(solution)/shard_map/last/pallas_call | solution.py:324
  (28 shorter events, 0.1 us)
Async XLA Ops:
  0.0 3.0 %collective-permute-start = (bf16[16,8192]{1,0:T(8,128)(2,1)}, bf16[16,8192]{1,0:T(8,128)(2,1)S(1)}, u32[]{:S(2)}, u32[]{:S(2)}) collective-permute-start(bf16[16,8192]{1,0:T(8,128)(2,1)} %tokens_ref.1), channel_id=1, source_target_pairs={{0,1},{1,0},{2,3},{3,2},{4,5},{5,4},{6,7},{7,6},{8,9},{9,8},{10,11... | collective-permute-start | bytes 786440 | tf_op jit(solution)/shard_map/ppermute | solution.py:377
  0.5 7.1 %collective-permute-start.1 = (bf16[16,8192]{1,0:T(8,128)(2,1)}, bf16[16,8192]{1,0:T(8,128)(2,1)S(1)}, u32[]{:S(2)}, u32[]{:S(2)}) collective-permute-start(bf16[16,8192]{1,0:T(8,128)(2,1)} %tokens_ref.1), channel_id=1, source_target_pairs={{0,4},{1,3},{4,8},{5,1},{8,12},{9,5},{12,14},{13,9},{14,10},{15,13... | collective-permute-start | bytes 786440 | tf_op jit(solution)/shard_map/ppermute | solution.py:374
  3.0 0.7 copy-start
  5.5 6.4 %collective-permute-start.2 = (bf16[16,8192]{1,0:T(8,128)(2,1)S(1)}, bf16[16,8192]{1,0:T(8,128)(2,1)S(1)}, u32[]{:S(2)}, u32[]{:S(2)}) collective-permute-start(bf16[16,8192]{1,0:T(8,128)(2,1)S(1)} %get-tuple-element.23.refs_1_), channel_id=1, source_target_pairs={{0,4},{1,3},{4,8},{5,1},{8,12},{9,5},{12,14},{13,9},{14,10},{15,13... | collective-permute-start | bytes 786440 | tf_op jit(solution)/shard_map/ppermute | solution.py:374
  7.5 7.2 %collective-permute-start.3 = (bf16[16,8192]{1,0:T(8,128)(2,1)S(1)}, bf16[16,8192]{1,0:T(8,128)(2,1)S(1)}, u32[]{:S(2)}, u32[]{:S(2)}) collective-permute-start(bf16[16,8192]{1,0:T(8,128)(2,1)S(1)} %collective-permute-done.1.refs_2_), channel_id=1, source_target_pairs={{0,4},{1,3},{4,8},{5,1},{8,12},{9,5},{12,14},{13,9},{14,10},{15,13... | collective-permute-start | bytes 786440 | tf_op jit(solution)/shard_map/ppermute | solution.py:374
  11.9 6.4 %collective-permute-start.4 = (bf16[16,8192]{1,0:T(8,128)(2,1)S(1)}, bf16[16,8192]{1,0:T(8,128)(2,1)S(1)}, u32[]{:S(2)}, u32[]{:S(2)}) collective-permute-start(bf16[16,8192]{1,0:T(8,128)(2,1)S(1)} %collective-permute-done.2.refs_3_), channel_id=1, source_target_pairs={{0,4},{1,3},{4,8},{5,1},{8,12},{9,5},{12,14},{13,9},{14,10},{15,13... | collective-permute-start | bytes 786440 | tf_op jit(solution)/shard_map/ppermute | solution.py:374
  14.7 6.4 %collective-permute-start.5 = (bf16[16,8192]{1,0:T(8,128)(2,1)S(1)}, bf16[16,8192]{1,0:T(8,128)(2,1)S(1)}, u32[]{:S(2)}, u32[]{:S(2)}) collective-permute-start(bf16[16,8192]{1,0:T(8,128)(2,1)S(1)} %collective-permute-done.3.refs_4_), channel_id=1, source_target_pairs={{0,4},{1,3},{4,8},{5,1},{8,12},{9,5},{12,14},{13,9},{14,10},{15,13... | collective-permute-start | bytes 786440 | tf_op jit(solution)/shard_map/ppermute | solution.py:374
  16.5 6.4 %collective-permute-start.8 = (bf16[16,8192]{1,0:T(8,128)(2,1)S(1)}, bf16[16,8192]{1,0:T(8,128)(2,1)S(1)}, u32[]{:S(2)}, u32[]{:S(2)}) collective-permute-start(bf16[16,8192]{1,0:T(8,128)(2,1)S(1)} %collective-permute-done.1.refs_2_), channel_id=1, source_target_pairs={{0,1},{1,0},{2,3},{3,2},{4,5},{5,4},{6,7},{7,6},{8,9},{9,8},{10,11... | collective-permute-start | bytes 786440 | tf_op jit(solution)/shard_map/ppermute | solution.py:377
  16.5 6.9 %collective-permute-start.9 = (bf16[16,8192]{1,0:T(8,128)(2,1)S(1)}, bf16[16,8192]{1,0:T(8,128)(2,1)S(1)}, u32[]{:S(2)}, u32[]{:S(2)}) collective-permute-start(bf16[16,8192]{1,0:T(8,128)(2,1)S(1)} %collective-permute-done.2.refs_3_), channel_id=1, source_target_pairs={{0,1},{1,0},{2,3},{3,2},{4,5},{5,4},{6,7},{7,6},{8,9},{9,8},{10,11... | collective-permute-start | bytes 786440 | tf_op jit(solution)/shard_map/ppermute | solution.py:377
  18.3 6.4 %collective-permute-start.6 = (bf16[16,8192]{1,0:T(8,128)(2,1)S(1)}, bf16[16,8192]{1,0:T(8,128)(2,1)S(1)}, u32[]{:S(2)}, u32[]{:S(2)}) collective-permute-start(bf16[16,8192]{1,0:T(8,128)(2,1)S(1)} %collective-permute-done.4.refs_5_), channel_id=1, source_target_pairs={{0,4},{1,3},{4,8},{5,1},{8,12},{9,5},{12,14},{13,9},{14,10},{15,13... | collective-permute-start | bytes 786440 | tf_op jit(solution)/shard_map/ppermute | solution.py:374
  21.1 6.4 %collective-permute-start.7 = (bf16[16,8192]{1,0:T(8,128)(2,1)S(1)}, bf16[16,8192]{1,0:T(8,128)(2,1)S(1)}, u32[]{:S(2)}, u32[]{:S(2)}) collective-permute-start(bf16[16,8192]{1,0:T(8,128)(2,1)S(1)} %collective-permute-done.5.refs_6_), channel_id=1, source_target_pairs={{0,4},{1,3},{4,8},{5,1},{8,12},{9,5},{12,14},{13,9},{14,10},{15,13... | collective-permute-start | bytes 786440 | tf_op jit(solution)/shard_map/ppermute | solution.py:374
  22.9 4.6 %collective-permute-start.10 = (bf16[16,8192]{1,0:T(8,128)(2,1)S(1)}, bf16[16,8192]{1,0:T(8,128)(2,1)S(1)}, u32[]{:S(2)}, u32[]{:S(2)}) collective-permute-start(bf16[16,8192]{1,0:T(8,128)(2,1)S(1)} %collective-permute-done.3.refs_4_), channel_id=1, source_target_pairs={{0,1},{1,0},{2,3},{3,2},{4,5},{5,4},{6,7},{7,6},{8,9},{9,8},{10,11... | collective-permute-start | bytes 786440 | tf_op jit(solution)/shard_map/ppermute | solution.py:377
  22.9 4.6 %collective-permute-start.11 = (bf16[16,8192]{1,0:T(8,128)(2,1)S(1)}, bf16[16,8192]{1,0:T(8,128)(2,1)S(1)}, u32[]{:S(2)}, u32[]{:S(2)}) collective-permute-start(bf16[16,8192]{1,0:T(8,128)(2,1)S(1)} %collective-permute-done.4.refs_5_), channel_id=1, source_target_pairs={{0,1},{1,0},{2,3},{3,2},{4,5},{5,4},{6,7},{7,6},{8,9},{9,8},{10,11... | collective-permute-start | bytes 786440 | tf_op jit(solution)/shard_map/ppermute | solution.py:377
  23.4 4.1 %collective-permute-start.12 = (bf16[16,8192]{1,0:T(8,128)(2,1)S(1)}, bf16[16,8192]{1,0:T(8,128)(2,1)S(1)}, u32[]{:S(2)}, u32[]{:S(2)}) collective-permute-start(bf16[16,8192]{1,0:T(8,128)(2,1)S(1)} %collective-permute-done.5.refs_6_), channel_id=1, source_target_pairs={{0,1},{1,0},{2,3},{3,2},{4,5},{5,4},{6,7},{7,6},{8,9},{9,8},{10,11... | collective-permute-start | bytes 786440 | tf_op jit(solution)/shard_map/ppermute | solution.py:377
  24.7 2.8 %collective-permute-start.13 = (bf16[16,8192]{1,0:T(8,128)(2,1)S(1)}, bf16[16,8192]{1,0:T(8,128)(2,1)S(1)}, u32[]{:S(2)}, u32[]{:S(2)}) collective-permute-start(bf16[16,8192]{1,0:T(8,128)(2,1)S(1)} %collective-permute-done.6.refs_7_), channel_id=1, source_target_pairs={{0,1},{1,0},{2,3},{3,2},{4,5},{5,4},{6,7},{7,6},{8,9},{9,8},{10,11... | collective-permute-start | bytes 786440 | tf_op jit(solution)/shard_map/ppermute | solution.py:377
  27.5 1.5 %collective-permute-start.14 = (bf16[16,8192]{1,0:T(8,128)(2,1)S(1)}, bf16[16,8192]{1,0:T(8,128)(2,1)S(1)}, u32[]{:S(2)}, u32[]{:S(2)}) collective-permute-start(bf16[16,8192]{1,0:T(8,128)(2,1)S(1)} %collective-permute-done.7.refs_8_), channel_id=1, source_target_pairs={{0,1},{1,0},{2,3},{3,2},{4,5},{5,4},{6,7},{7,6},{8,9},{9,8},{10,11... | collective-permute-start | bytes 786440 | tf_op jit(solution)/shard_map/ppermute | solution.py:377
  30.5 4.6 %collective-permute-start.15 = (bf16[8,256]{1,0:T(8,128)(2,1)S(1)}, bf16[8,256]{1,0:T(8,128)(2,1)S(1)}, u32[]{:S(2)}, u32[]{:S(2)}) collective-permute-start(bf16[8,256]{1,0:T(8,128)(2,1)S(1)} %rank.1.refs_16_), channel_id=1, source_target_pairs={{0,1},{1,0},{2,3},{3,2},{4,5},{5,4},{6,7},{7,6},{8,9},{9,8},{10,11... | collective-permute-start | bytes 12296 | tf_op jit(solution)/shard_map/ppermute | solution.py:377
  35.1 6.2 %collective-permute-start.16 = (bf16[16,256]{1,0:T(8,128)(2,1)S(1)}, bf16[16,256]{1,0:T(8,128)(2,1)S(1)}, u32[]{:S(2)}, u32[]{:S(2)}) collective-permute-start(bf16[16,256]{1,0:T(8,128)(2,1)S(1)} %pad_maximum_fusion.2), channel_id=1, source_target_pairs={{0,2},{1,3},{2,0},{3,1},{4,6},{5,7},{6,4},{7,5},{8,10},{9,11},{10,... | collective-permute-start | bytes 24584 | tf_op jit(solution)/shard_map/ppermute | solution.py:377
  41.4 6.1 %collective-permute-start.17 = (bf16[32,256]{1,0:T(8,128)(2,1)S(1)}, bf16[32,256]{1,0:T(8,128)(2,1)S(1)}, u32[]{:S(2)}, u32[]{:S(2)}) collective-permute-start(bf16[32,256]{1,0:T(8,128)(2,1)S(1)} %pad_maximum_fusion.1), channel_id=1, source_target_pairs={{0,4},{1,5},{2,6},{3,7},{4,0},{5,1},{6,2},{7,3},{8,12},{9,13},{10,... | collective-permute-start | bytes 49160 | tf_op jit(solution)/shard_map/ppermute | solution.py:377
  47.5 7.1 %collective-permute-start.18 = (bf16[64,256]{1,0:T(8,128)(2,1)S(1)}, bf16[64,256]{1,0:T(8,128)(2,1)S(1)}, u32[]{:S(2)}, u32[]{:S(2)}) collective-permute-start(bf16[64,256]{1,0:T(8,128)(2,1)S(1)} %pad_maximum_fusion), channel_id=1, source_target_pairs={{0,8},{1,9},{2,10},{3,11},{4,12},{5,13},{6,14},{7,15},{8,0},{9,1},... | collective-permute-start | bytes 98312 | tf_op jit(solution)/shard_map/ppermute | solution.py:377
  54.6 36.9 %copy-start.1 = (s32[2]{0:T(128)S(1)}, s32[2]{0:T(128)}, u32[]{:S(2)}) copy-start(s32[2]{0:T(128)} %counts_ref.1) | copy-start | bytes 28
  63.1 2.9 %collective-permute-start.22 = (bf16[32,8192]{1,0:T(8,128)(2,1)S(1)}, bf16[32,8192]{1,0:T(8,128)(2,1)S(1)}, u32[]{:S(2)}, u32[]{:S(2)}) collective-permute-start(bf16[32,8192]{1,0:T(8,128)(2,1)S(1)} %get-tuple-element.33), channel_id=1, source_target_pairs={{0,1},{1,0},{2,3},{3,2},{4,5},{5,4},{6,7},{7,6},{8,9},{9,8},{10,11... | collective-permute-start | bytes 1572872 | tf_op jit(solution)/shard_map/ppermute | solution.py:377
  63.2 2.3 %collective-permute-start.23 = (bf16[16,8192]{1,0:T(8,128)(2,1)S(1)}, bf16[16,8192]{1,0:T(8,128)(2,1)S(1)}, u32[]{:S(2)}, u32[]{:S(2)}) collective-permute-start(bf16[16,8192]{1,0:T(8,128)(2,1)S(1)} %get-tuple-element.35), channel_id=1, source_target_pairs={{0,1},{1,0},{2,3},{3,2},{4,5},{5,4},{6,7},{7,6},{8,9},{9,8},{10,11... | collective-permute-start | bytes 786440 | tf_op jit(solution)/shard_map/ppermute | solution.py:377
  63.7 8.9 %collective-permute-start.21 = (bf16[32,8192]{1,0:T(8,128)(2,1)S(1)}, bf16[32,8192]{1,0:T(8,128)(2,1)S(1)}, u32[]{:S(2)}, u32[]{:S(2)}) collective-permute-start(bf16[32,8192]{1,0:T(8,128)(2,1)S(1)} %get-tuple-element.31), channel_id=1, source_target_pairs={{0,1},{1,0},{2,3},{3,2},{4,5},{5,4},{6,7},{7,6},{8,9},{9,8},{10,11... | collective-permute-start | bytes 1572872 | tf_op jit(solution)/shard_map/ppermute | solution.py:377
  65.5 6.4 %collective-permute-start.24 = (bf16[16,8192]{1,0:T(8,128)(2,1)S(1)}, bf16[16,8192]{1,0:T(8,128)(2,1)S(1)}, u32[]{:S(2)}, u32[]{:S(2)}) collective-permute-start(bf16[16,8192]{1,0:T(8,128)(2,1)S(1)} %added.7), channel_id=1, source_target_pairs={{0,4},{1,3},{4,8},{5,1},{8,12},{9,5},{12,14},{13,9},{14,10},{15,13... | collective-permute-start | bytes 786440 | tf_op jit(solution)/shard_map/ppermute | solution.py:374
  66.1 8.7 %collective-permute-start.28 = (bf16[16,8192]{1,0:T(8,128)(2,1)S(1)}, bf16[16,8192]{1,0:T(8,128)(2,1)S(1)}, u32[]{:S(2)}, u32[]{:S(2)}) collective-permute-start(bf16[16,8192]{1,0:T(8,128)(2,1)S(1)} %added.11), channel_id=1, source_target_pairs={{0,4},{1,3},{4,8},{5,1},{8,12},{9,5},{12,14},{13,9},{14,10},{15,13... | collective-permute-start | bytes 786440 | tf_op jit(solution)/shard_map/ppermute | solution.py:374
  66.6 12.5 %collective-permute-start.20 = (bf16[32,8192]{1,0:T(8,128)(2,1)S(1)}, bf16[32,8192]{1,0:T(8,128)(2,1)S(1)}, u32[]{:S(2)}, u32[]{:S(2)}) collective-permute-start(bf16[32,8192]{1,0:T(8,128)(2,1)S(1)} %get-tuple-element.29), channel_id=1, source_target_pairs={{0,1},{1,0},{2,3},{3,2},{4,5},{5,4},{6,7},{7,6},{8,9},{9,8},{10,11... | collective-permute-start | bytes 1572872 | tf_op jit(solution)/shard_map/ppermute | solution.py:377
  72.0 6.4 %collective-permute-start.25 = (bf16[16,8192]{1,0:T(8,128)(2,1)S(1)}, bf16[16,8192]{1,0:T(8,128)(2,1)S(1)}, u32[]{:S(2)}, u32[]{:S(2)}) collective-permute-start(bf16[16,8192]{1,0:T(8,128)(2,1)S(1)} %added.8), channel_id=1, source_target_pairs={{0,4},{1,3},{4,8},{5,1},{8,12},{9,5},{12,14},{13,9},{14,10},{15,13... | collective-permute-start | bytes 786440 | tf_op jit(solution)/shard_map/ppermute | solution.py:374
  74.9 6.4 %collective-permute-start.29 = (bf16[16,8192]{1,0:T(8,128)(2,1)S(1)}, bf16[16,8192]{1,0:T(8,128)(2,1)S(1)}, u32[]{:S(2)}, u32[]{:S(2)}) collective-permute-start(bf16[16,8192]{1,0:T(8,128)(2,1)S(1)} %added.12), channel_id=1, source_target_pairs={{0,4},{1,3},{4,8},{5,1},{8,12},{9,5},{12,14},{13,9},{14,10},{15,13... | collective-permute-start | bytes 786440 | tf_op jit(solution)/shard_map/ppermute | solution.py:374
  78.6 6.4 %collective-permute-start.26 = (bf16[16,8192]{1,0:T(8,128)(2,1)S(1)}, bf16[16,8192]{1,0:T(8,128)(2,1)S(1)}, u32[]{:S(2)}, u32[]{:S(2)}) collective-permute-start(bf16[16,8192]{1,0:T(8,128)(2,1)S(1)} %added.9), channel_id=1, source_target_pairs={{0,4},{1,3},{4,8},{5,1},{8,12},{9,5},{12,14},{13,9},{14,10},{15,13... | collective-permute-start | bytes 786440 | tf_op jit(solution)/shard_map/ppermute | solution.py:374
  81.4 6.4 %collective-permute-start.30 = (bf16[16,8192]{1,0:T(8,128)(2,1)S(1)}, bf16[16,8192]{1,0:T(8,128)(2,1)S(1)}, u32[]{:S(2)}, u32[]{:S(2)}) collective-permute-start(bf16[16,8192]{1,0:T(8,128)(2,1)S(1)} %added.13), channel_id=1, source_target_pairs={{0,4},{1,3},{4,8},{5,1},{8,12},{9,5},{12,14},{13,9},{14,10},{15,13... | collective-permute-start | bytes 786440 | tf_op jit(solution)/shard_map/ppermute | solution.py:374
  81.9 5.9 %collective-permute-start.19 = (bf16[16,8192]{1,0:T(8,128)(2,1)S(1)}, bf16[16,8192]{1,0:T(8,128)(2,1)S(1)}, u32[]{:S(2)}, u32[]{:S(2)}) collective-permute-start(bf16[16,8192]{1,0:T(8,128)(2,1)S(1)} %get-tuple-element.27), channel_id=1, source_target_pairs={{0,1},{1,0},{2,3},{3,2},{4,5},{5,4},{6,7},{7,6},{8,9},{9,8},{10,11... | collective-permute-start | bytes 786440 | tf_op jit(solution)/shard_map/ppermute | solution.py:377
  85.1 6.4 %collective-permute-start.27 = (bf16[16,8192]{1,0:T(8,128)(2,1)S(1)}, bf16[16,8192]{1,0:T(8,128)(2,1)S(1)}, u32[]{:S(2)}, u32[]{:S(2)}) collective-permute-start(bf16[16,8192]{1,0:T(8,128)(2,1)S(1)} %added.10), channel_id=1, source_target_pairs={{0,4},{1,3},{4,8},{5,1},{8,12},{9,5},{12,14},{13,9},{14,10},{15,13... | collective-permute-start | bytes 786440 | tf_op jit(solution)/shard_map/ppermute | solution.py:374
  87.8 3.7 %collective-permute-start.31 = (bf16[16,8192]{1,0:T(8,128)(2,1)S(1)}, bf16[16,8192]{1,0:T(8,128)(2,1)S(1)}, u32[]{:S(2)}, u32[]{:S(2)}) collective-permute-start(bf16[16,8192]{1,0:T(8,128)(2,1)S(1)} %collective-permute-done.30), channel_id=1, source_target_pairs={{0,1},{1,0},{2,3},{3,2},{4,5},{5,4},{6,7},{7,6},{8,9},{9,8},{10,11... | collective-permute-start | bytes 786440 | tf_op jit(solution)/shard_map/ppermute | solution.py:377

commit v5 on v4

--- a/solution.py
+++ b/solution.py
@@ -121,6 +121,7 @@
             like(passed.shape),
         ],
         input_output_aliases={4: 3},
+        cost_estimate=cost(30_000_000_000, 0),
         scratch_shapes=[pltpu.SemaphoreType.DMA((1 + 2 * blocks,))],
         compiler_params=params(),
         name="prepare",
@@ -164,32 +165,16 @@
     )(shrink, *pieces)
 
 
-def product_kernel(first, size, chunks, slots, w_ref, *refs):
-    pieces = refs[:-5]
-    out_ref, total, store, sems = refs[-4:]
+def product_kernel(first, w_ref, *refs):
+    pieces, out_ref = refs[:-2], refs[-1]
     rows = pieces[0].shape[0]
-
-    def copy(chunk):
-        return pltpu.make_async_copy(
-            w_ref.at[pl.ds(first + chunk * size, size), :],
-            store.at[chunk % slots],
-            sems.at[chunk % slots],
-        )
-
-    for chunk in range(slots):
-        copy(chunk).start()
+    depth = w_ref.shape[0] // 2
+    size = min(2048, depth)
     places = arrivals(lax.axis_index("tp"), len(pieces), rows)
-    for chunk in range(chunks):
-        start = first + chunk * size
+    part = 0.0
+    for start in range(first, first + depth, size):
         lhs = jnp.concatenate([piece[:, start : start + size] for piece in pieces], axis=0)
-        copy(chunk).wait()
-        part = jnp.dot(lhs, store[chunk % slots], preferred_element_type=F32)
-        if chunk + slots < chunks:
-            copy(chunk + slots).start()
-        if chunk > 0:
-            part += total[...]
-        if chunk < chunks - 1:
-            total[...] = part
+        part += jnp.dot(lhs, w_ref[start : start + size, :], preferred_element_type=F32)
     for index, place in enumerate(places):
         out_ref[pl.ds(place, rows), :] = part[index * rows : (index + 1) * rows]
 
@@ -199,23 +184,15 @@
     total = rows * len(pieces)
     width = matrix.shape[1]
     depth = model // parts
-    size = min(1024, depth)
-    chunks = depth // size
-    slots = min(4, chunks)
-    return pl.pallas_call(
-        functools.partial(product_kernel, part * depth, size, chunks, slots),
-        in_specs=[FAR] + whole(len(pieces) + 1),
+    return pl.pallas_call(
+        functools.partial(product_kernel, part * depth),
+        in_specs=whole(len(pieces) + 2),
         out_specs=whole(1)[0],
         out_shape=jax.ShapeDtypeStruct((total, width), F32),
-        scratch_shapes=[
-            pltpu.VMEM((total, width), F32),
-            pltpu.VMEM((slots, size, width), BF16),
-            pltpu.SemaphoreType.DMA((slots,)),
-        ],
         compiler_params=params(),
         cost_estimate=cost(2 * total * depth * width, 2 * depth * (width + total)),
         name="product",
-    )(far(matrix), *pieces, after)
+    )(matrix, *pieces, after)
 
 
 def finish_kernel(span, gate_a, gate_b, up_a, up_b, rank_ref, expand_ref, hidden_ref):
@@ -252,27 +229,13 @@
     )(*products, rank, expand)
 
 
-def down_kernel(members, groups, rows, chunks, slots, w_ref, hidden_ref, *refs):
-    outs, (product_ref, store, sems) = refs[:-3], refs[-3:]
-    size = store.shape[2]
-
-    def copy(chunk):
-        return pltpu.make_async_copy(
-            w_ref.at[:, pl.ds(chunk * size, size)],
-            store.at[chunk % slots],
-            sems.at[chunk % slots],
-        )
-
-    for chunk in range(slots):
-        copy(chunk).start()
+def down_kernel(members, groups, rows, size, w_ref, hidden_ref, *refs):
+    outs, product_ref = refs[:-1], refs[-1]
     places = departures(lax.axis_index("tp"), members, rows)
     hidden = hidden_ref[...]
-    for chunk in range(chunks):
-        columns = slice(chunk * size, (chunk + 1) * size)
-        copy(chunk).wait()
-        part = jnp.dot(hidden, store[chunk % slots], preferred_element_type=F32)
-        if chunk + slots < chunks:
-            copy(chunk + slots).start()
+    for start in range(0, w_ref.shape[1], size):
+        columns = slice(start, start + size)
+        part = jnp.dot(hidden, w_ref[:, columns], preferred_element_type=F32)
         product_ref[...] = part.astype(BF16)
         at = 0
         for out, group in zip(outs, groups, strict=True):
@@ -287,24 +250,18 @@
     total, depth = hidden.shape
     columns = down_matrix.shape[1]
     size = min(1024, columns)
-    chunks = columns // size
-    slots = min(4, chunks)
-    return pl.pallas_call(
-        functools.partial(down_kernel, total // rows, groups, rows, chunks, slots),
-        in_specs=[FAR] + whole(1),
+    return pl.pallas_call(
+        functools.partial(down_kernel, total // rows, groups, rows, size),
+        in_specs=whole(2),
         out_specs=whole(len(groups)),
         out_shape=[jax.ShapeDtypeStruct((group * rows, columns), BF16) for group in groups],
-        scratch_shapes=[
-            pltpu.VMEM((total, size), BF16),
-            pltpu.VMEM((slots, depth, size), BF16),
-            pltpu.SemaphoreType.DMA((slots,)),
-        ],
+        scratch_shapes=[pltpu.VMEM((total, size), BF16)],
         compiler_params=params(),
         cost_estimate=cost(
             2 * total * depth * columns, 2 * depth * columns + 2 * total * columns
         ),
         name="down",
-    )(far(down_matrix), hidden)
+    )(down_matrix, hidden)
 
 
 def last_kernel(blocks, members, counts_ref, *refs):

time: 93.1 us -> 82.2 us (0.88)
  Pallas kernels: 31.5 us -> 20.5 us
  waiting for transfers between devices: 35.2 us -> 28.8 us
  starting transfers between devices: 25.3 us -> 31.7 us
    pallas_call x4, Pallas kernels: 17.8 us -> 9.43 us  [product(): pl.pallas_call(functools.partial(product_kernel, part * depth), in_specs=...]
    ppermute x14, waiting for transfers between devices: 31.9 us -> 25.5 us  [step(): return lax.ppermute(x, 'tp', ring)]
    ppermute x14, starting transfers between devices: 16.9 us -> 23.3 us  [step(): return lax.ppermute(x, 'tp', ring)]
    pallas_call x1, Pallas kernels: 7.53 us -> 4.85 us  [down(): pl.pallas_call(functools.partial(down_kernel, total // rows, groups, rows...]
  transfers between devices with their start and end apart: 32 -> 32, of which waited for: 16 -> 15; matrix products, arithmetic and copies ran while one was open for 0% -> 0% of each run, Pallas kernels for 22% -> 15%
where the time goes in v5:
time: 82.2 us; the launch traced here: 82.1 us
  starting transfers between devices  31.7 us (39%)
  waiting for transfers between devices  28.8 us (35%)
  Pallas kernels  20.5 us (25%)
    ppermute x14, waiting for transfers between devices, step(): return lax.ppermute(x, 'tp', ring)  25.5 us
    ppermute x14, starting transfers between devices, step(): return lax.ppermute(x, 'tp', ring)  23.3 us
    pallas_call x4, Pallas kernels, product(): pl.pallas_call(functools.partial(product_kernel, part * depth), in_specs=...  9.43 us
    ppermute x18, starting transfers between devices, cross(): return lax.ppermute(x, 'tp', crossing(members, bit))  8.44 us
    pallas_call x1, Pallas kernels, down(): pl.pallas_call(functools.partial(down_kernel, total // rows, groups, rows...  4.85 us
    ppermute x18, waiting for transfers between devices, cross(): return lax.ppermute(x, 'tp', crossing(members, bit))  3.24 us
    pallas_call x1, Pallas kernels, prepare(): pl.pallas_call(functools.partial(prepare_kernel, blocks), in_specs=[SCALA...  2.04 us
  transfers between devices with their start and end apart: 32, of which 15 were waited for; matrix products, arithmetic and copies ran while one was open for 0% of the time, Pallas kernels for 15%

profile of v5, /device:TPU:0, one launch (start us, length us, event | category | flops | bytes accessed | tf_op | source)
XLA Modules:
  0.0 82.1 jit_solution(743288795568073750)
XLA Ops:
  0.0 0.5 collective-permute-start
  0.5 2.6 %collective-permute-start.1 = (bf16[16,8192]{1,0:T(8,128)(2,1)}, bf16[16,8192]{1,0:T(8,128)(2,1)S(1)}, u32[]{:S(2)}, u32[]{:S(2)}) collective-permute-start(bf16[16,8192]{1,0:T(8,128)(2,1)} %tokens_ref.1), channel_id=1, source_target_pairs={{0,4},{1,3},{4,8},{5,1},{8,12},{9,5},{12,14},{13,9},{14,10},{15,13... | collective-permute-start | bytes 786440 | tf_op jit(solution)/shard_map/ppermute | solution.py:331
  3.0 0.7 copy-done.2
  3.7 2.0 %prepare.1 = (bf16[16,8192]{1,0:T(8,128)(2,1)S(1)}, bf16[2,8,8192]{2,1,0:T(8,128)(2,1)S(1)}, bf16[2,128,896]{2,1,0:T(8,128)(2,1)S(1)}, bf16[16,8192]{1,0:T(8,128)(2,1)S(1)}) custom-call(s32[2]{0:T(128)S(1)} %copy-done.2, bf16[16,8192]{1,0:T(8,128)(2,1)} %tokens_ref.1, bf16[8,8,8192]{2,1,0:T(8,128)(2,1)} %bitcast.5, ...), custom_call_target="tpu_custom_call", output_to_operand_aliasing={{3}: (4, {})} | custom-call | flops 30000001024 | tf_op jit(solution)/shard_map/prepare/pallas_call | solution.py:113
  5.7 1.8 %collective-permute-start.2 = (bf16[16,8192]{1,0:T(8,128)(2,1)S(1)}, bf16[16,8192]{1,0:T(8,128)(2,1)S(1)}, u32[]{:S(2)}, u32[]{:S(2)}) collective-permute-start(bf16[16,8192]{1,0:T(8,128)(2,1)S(1)} %get-tuple-element.23.refs_1_), channel_id=1, source_target_pairs={{0,4},{1,3},{4,8},{5,1},{8,12},{9,5},{12,14},{13,9},{14,10},{15,13... | collective-permute-start | bytes 786440 | tf_op jit(solution)/shard_map/ppermute | solution.py:331
  7.5 0.0 collective-permute-done.1.refs_2_
  7.5 2.1 %collective-permute-start.3 = (bf16[16,8192]{1,0:T(8,128)(2,1)S(1)}, bf16[16,8192]{1,0:T(8,128)(2,1)S(1)}, u32[]{:S(2)}, u32[]{:S(2)}) collective-permute-start(bf16[16,8192]{1,0:T(8,128)(2,1)S(1)} %collective-permute-done.1.refs_2_), channel_id=1, source_target_pairs={{0,4},{1,3},{4,8},{5,1},{8,12},{9,5},{12,14},{13,9},{14,10},{15,13... | collective-permute-start | bytes 786440 | tf_op jit(solution)/shard_map/ppermute | solution.py:331
  9.6 2.5 %collective-permute-done.2.refs_3_ = bf16[16,8192]{1,0:T(8,128)(2,1)S(1)} collective-permute-done((bf16[16,8192]{1,0:T(8,128)(2,1)S(1)}, bf16[16,8192]{1,0:T(8,128)(2,1)S(1)}, u32[]{:S(2)}, u32[]{:S(2)}) %collective-permute-start.2) | collective-permute-done | bytes 262176 | tf_op jit(solution)/shard_map/ppermute | solution.py:331
  12.2 1.7 %collective-permute-start.4 = (bf16[16,8192]{1,0:T(8,128)(2,1)S(1)}, bf16[16,8192]{1,0:T(8,128)(2,1)S(1)}, u32[]{:S(2)}, u32[]{:S(2)}) collective-permute-start(bf16[16,8192]{1,0:T(8,128)(2,1)S(1)} %collective-permute-done.2.refs_3_), channel_id=1, source_target_pairs={{0,4},{1,3},{4,8},{5,1},{8,12},{9,5},{12,14},{13,9},{14,10},{15,13... | collective-permute-start | bytes 786440 | tf_op jit(solution)/shard_map/ppermute | solution.py:331
  13.9 1.1 %collective-permute-done.3.refs_4_ = bf16[16,8192]{1,0:T(8,128)(2,1)S(1)} collective-permute-done((bf16[16,8192]{1,0:T(8,128)(2,1)S(1)}, bf16[16,8192]{1,0:T(8,128)(2,1)S(1)}, u32[]{:S(2)}, u32[]{:S(2)}) %collective-permute-start.3) | collective-permute-done | bytes 262176 | tf_op jit(solution)/shard_map/ppermute | solution.py:331
  15.0 1.7 %collective-permute-start.5 = (bf16[16,8192]{1,0:T(8,128)(2,1)S(1)}, bf16[16,8192]{1,0:T(8,128)(2,1)S(1)}, u32[]{:S(2)}, u32[]{:S(2)}) collective-permute-start(bf16[16,8192]{1,0:T(8,128)(2,1)S(1)} %collective-permute-done.3.refs_4_), channel_id=1, source_target_pairs={{0,4},{1,3},{4,8},{5,1},{8,12},{9,5},{12,14},{13,9},{14,10},{15,13... | collective-permute-start | bytes 786440 | tf_op jit(solution)/shard_map/ppermute | solution.py:331
  16.7 0.0 collective-permute-start.8
  16.7 0.5 collective-permute-start.9
  17.2 1.3 %collective-permute-done.4.refs_5_ = bf16[16,8192]{1,0:T(8,128)(2,1)S(1)} collective-permute-done((bf16[16,8192]{1,0:T(8,128)(2,1)S(1)}, bf16[16,8192]{1,0:T(8,128)(2,1)S(1)}, u32[]{:S(2)}, u32[]{:S(2)}) %collective-permute-start.4) | collective-permute-done | bytes 262176 | tf_op jit(solution)/shard_map/ppermute | solution.py:331
  18.5 1.7 %collective-permute-start.6 = (bf16[16,8192]{1,0:T(8,128)(2,1)S(1)}, bf16[16,8192]{1,0:T(8,128)(2,1)S(1)}, u32[]{:S(2)}, u32[]{:S(2)}) collective-permute-start(bf16[16,8192]{1,0:T(8,128)(2,1)S(1)} %collective-permute-done.4.refs_5_), channel_id=1, source_target_pairs={{0,4},{1,3},{4,8},{5,1},{8,12},{9,5},{12,14},{13,9},{14,10},{15,13... | collective-permute-start | bytes 786440 | tf_op jit(solution)/shard_map/ppermute | solution.py:331
  20.3 1.1 %collective-permute-done.5.refs_6_ = bf16[16,8192]{1,0:T(8,128)(2,1)S(1)} collective-permute-done((bf16[16,8192]{1,0:T(8,128)(2,1)S(1)}, bf16[16,8192]{1,0:T(8,128)(2,1)S(1)}, u32[]{:S(2)}, u32[]{:S(2)}) %collective-permute-start.5) | collective-permute-done | bytes 262176 | tf_op jit(solution)/shard_map/ppermute | solution.py:331
  21.3 1.7 %collective-permute-start.7 = (bf16[16,8192]{1,0:T(8,128)(2,1)S(1)}, bf16[16,8192]{1,0:T(8,128)(2,1)S(1)}, u32[]{:S(2)}, u32[]{:S(2)}) collective-permute-start(bf16[16,8192]{1,0:T(8,128)(2,1)S(1)} %collective-permute-done.5.refs_6_), channel_id=1, source_target_pairs={{0,4},{1,3},{4,8},{5,1},{8,12},{9,5},{12,14},{13,9},{14,10},{15,13... | collective-permute-start | bytes 786440 | tf_op jit(solution)/shard_map/ppermute | solution.py:331
  23.1 0.5 collective-permute-start.11
  23.6 0.1 collective-permute-start.12
  23.7 1.2 %collective-permute-done.6.refs_7_ = bf16[16,8192]{1,0:T(8,128)(2,1)S(1)} collective-permute-done((bf16[16,8192]{1,0:T(8,128)(2,1)S(1)}, bf16[16,8192]{1,0:T(8,128)(2,1)S(1)}, u32[]{:S(2)}, u32[]{:S(2)}) %collective-permute-start.6) | collective-permute-done | bytes 262176 | tf_op jit(solution)/shard_map/ppermute | solution.py:331
  24.9 2.8 %collective-permute-done.7.refs_8_ = bf16[16,8192]{1,0:T(8,128)(2,1)S(1)} collective-permute-done((bf16[16,8192]{1,0:T(8,128)(2,1)S(1)}, bf16[16,8192]{1,0:T(8,128)(2,1)S(1)}, u32[]{:S(2)}, u32[]{:S(2)}) %collective-permute-start.7) | collective-permute-done | bytes 262176 | tf_op jit(solution)/shard_map/ppermute | solution.py:331
  27.7 1.5 %collective-permute-done.14.refs_15_ = bf16[16,8192]{1,0:T(8,128)(2,1)S(1)} collective-permute-done((bf16[16,8192]{1,0:T(8,128)(2,1)S(1)}, bf16[16,8192]{1,0:T(8,128)(2,1)S(1)}, u32[]{:S(2)}, u32[]{:S(2)}) %collective-permute-start.14) | collective-permute-done | bytes 262176 | tf_op jit(solution)/shard_map/ppermute | solution.py:334
  29.3 1.4 %rank.1.refs_16_ = bf16[8,256]{1,0:T(8,128)(2,1)S(1)} custom-call(bf16[2,8,8192]{2,1,0:T(8,128)(2,1)S(1)} %get-tuple-element.24.shrink_ref, bf16[16,8192]{1,0:T(8,128)(2,1)S(1)} %get-tuple-element.22.refs_0_, bf16[16,8192]{1,0:T(8,128)(2,1)S(1)} %get-tuple-element.23.refs_1_, bf16[16,8192]{1,0:T(8,128)(2,1)S(1)} %collective-permute-done.1.refs_2_, ...), custom_call_target="tpu_custom_call" | custom-call | flops 67108864 | bytes 4194304 | tf_op jit(solution)/shard_map/rank/pallas_call | solution.py:156
  30.7 0.2 collective-permute-start.15
  30.9 2.4 %product.4.gate_a = f32[256,896]{1,0:T(8,128)S(1)} custom-call(bf16[8192,896]{1,0:T(8,128)(2,1)S(1)} %copy-done, bf16[16,8192]{1,0:T(8,128)(2,1)S(1)} %get-tuple-element.22.refs_0_, bf16[16,8192]{1,0:T(8,128)(2,1)S(1)} %get-tuple-element.23.refs_1_, bf16[16,8192]{1,0:T(8,128)(2,1)S(1)} %collective-permute-done.1.refs_2_, ...), custom_call_target="tpu_custom_call" | custom-call | flops 1879048192 | bytes 9437184 | tf_op jit(solution)/shard_map/product/pallas_call | solution.py:187
  33.3 0.0 slice-start.2
  33.3 1.8 %collective-permute-start.16 = (bf16[16,256]{1,0:T(8,128)(2,1)S(1)}, bf16[16,256]{1,0:T(8,128)(2,1)S(1)}, u32[]{:S(2)}, u32[]{:S(2)}) collective-permute-start(bf16[16,256]{1,0:T(8,128)(2,1)S(1)} %pad_maximum_fusion.2), channel_id=1, source_target_pairs={{0,2},{1,3},{2,0},{3,1},{4,6},{5,7},{6,4},{7,5},{8,10},{9,11},{10,... | collective-permute-start | bytes 24584 | tf_op jit(solution)/shard_map/ppermute | solution.py:334
  35.1 2.4 %product.5.gate_b = f32[256,896]{1,0:T(8,128)S(1)} custom-call(bf16[8192,896]{1,0:T(8,128)(2,1)S(1)} %copy-done, bf16[16,8192]{1,0:T(8,128)(2,1)S(1)} %get-tuple-element.22.refs_0_, bf16[16,8192]{1,0:T(8,128)(2,1)S(1)} %get-tuple-element.23.refs_1_, bf16[16,8192]{1,0:T(8,128)(2,1)S(1)} %collective-permute-done.1.refs_2_, ...), custom_call_target="tpu_custom_call" | custom-call | flops 1879048192 | bytes 9437184 | tf_op jit(solution)/shard_map/product/pallas_call | solution.py:187
  37.5 1.6 %collective-permute-start.17 = (bf16[32,256]{1,0:T(8,128)(2,1)S(1)}, bf16[32,256]{1,0:T(8,128)(2,1)S(1)}, u32[]{:S(2)}, u32[]{:S(2)}) collective-permute-start(bf16[32,256]{1,0:T(8,128)(2,1)S(1)} %pad_maximum_fusion.1), channel_id=1, source_target_pairs={{0,4},{1,5},{2,6},{3,7},{4,0},{5,1},{6,2},{7,3},{8,12},{9,13},{10,... | collective-permute-start | bytes 49160 | tf_op jit(solution)/shard_map/ppermute | solution.py:334
  39.2 0.0 slice-start.4
  39.2 0.0 slice-start.5
  39.2 2.3 %product.6.up_a = f32[256,896]{1,0:T(8,128)S(1)} custom-call(bf16[8192,896]{1,0:T(8,128)(2,1)S(1)} %bitcast.2, bf16[16,8192]{1,0:T(8,128)(2,1)S(1)} %get-tuple-element.22.refs_0_, bf16[16,8192]{1,0:T(8,128)(2,1)S(1)} %get-tuple-element.23.refs_1_, bf16[16,8192]{1,0:T(8,128)(2,1)S(1)} %collective-permute-done.1.refs_2_, ...), custom_call_target="tpu_custom_call" | custom-call | flops 1879048192 | bytes 9437184 | tf_op jit(solution)/shard_map/product/pallas_call | solution.py:187
  41.6 0.0 slice-start.6
  41.6 2.7 %collective-permute-start.18 = (bf16[64,256]{1,0:T(8,128)(2,1)S(1)}, bf16[64,256]{1,0:T(8,128)(2,1)S(1)}, u32[]{:S(2)}, u32[]{:S(2)}) collective-permute-start(bf16[64,256]{1,0:T(8,128)(2,1)S(1)} %pad_maximum_fusion), channel_id=1, source_target_pairs={{0,8},{1,9},{2,10},{3,11},{4,12},{5,13},{6,14},{7,15},{8,0},{9,1},... | collective-permute-start | bytes 98312 | tf_op jit(solution)/shard_map/ppermute | solution.py:334
  44.2 2.3 %product.7.up_b = f32[256,896]{1,0:T(8,128)S(1)} custom-call(bf16[8192,896]{1,0:T(8,128)(2,1)S(1)} %bitcast.2, bf16[16,8192]{1,0:T(8,128)(2,1)S(1)} %get-tuple-element.22.refs_0_, bf16[16,8192]{1,0:T(8,128)(2,1)S(1)} %get-tuple-element.23.refs_1_, bf16[16,8192]{1,0:T(8,128)(2,1)S(1)} %collective-permute-done.1.refs_2_, ...), custom_call_target="tpu_custom_call" | custom-call | flops 1879048192 | bytes 9437184 | tf_op jit(solution)/shard_map/product/pallas_call | solution.py:187
  46.6 0.0 copy-start.1
  46.6 0.7 finish.1.hidden_ref
  47.4 4.8 %down.1 = (bf16[16,8192]{1,0:T(8,128)(2,1)S(1)}, bf16[16,8192]{1,0:T(8,128)(2,1)S(1)}, bf16[16,8192]{1,0:T(8,128)(2,1)S(1)}, bf16[16,8192]{1,0:T(8,128)(2,1)S(1)...) custom-call(bf16[896,8192]{1,0:T(8,128)(2,1)S(1)} %bitcast.4, ...), custom_call_target="tpu_custom_call" | custom-call | flops 3758096384 | bytes 18874368 | tf_op jit(solution)/shard_map/down/pallas_call | solution.py:253
  52.3 0.1 collective-permute-start.22
  52.4 0.5 collective-permute-start.23
  52.9 0.1 collective-permute-start.21
  52.9 1.7 %collective-permute-done.23.refs_1_ = bf16[16,8192]{1,0:T(8,128)(2,1)S(1)} collective-permute-done((bf16[16,8192]{1,0:T(8,128)(2,1)S(1)}, bf16[16,8192]{1,0:T(8,128)(2,1)S(1)}, u32[]{:S(2)}, u32[]{:S(2)}) %collective-permute-start.23) | collective-permute-done | bytes 262176 | tf_op jit(solution)/shard_map/ppermute | solution.py:334
  54.6 0.1 added.7
  54.7 1.3 %collective-permute-start.24 = (bf16[16,8192]{1,0:T(8,128)(2,1)S(1)}, bf16[16,8192]{1,0:T(8,128)(2,1)S(1)}, u32[]{:S(2)}, u32[]{:S(2)}) collective-permute-start(bf16[16,8192]{1,0:T(8,128)(2,1)S(1)} %added.7), channel_id=1, source_target_pairs={{0,4},{1,3},{4,8},{5,1},{8,12},{9,5},{12,14},{13,9},{14,10},{15,13... | collective-permute-start | bytes 786440 | tf_op jit(solution)/shard_map/ppermute | solution.py:331
  56.0 0.1 added.11
  56.1 1.9 %collective-permute-start.28 = (bf16[16,8192]{1,0:T(8,128)(2,1)S(1)}, bf16[16,8192]{1,0:T(8,128)(2,1)S(1)}, u32[]{:S(2)}, u32[]{:S(2)}) collective-permute-start(bf16[16,8192]{1,0:T(8,128)(2,1)S(1)} %added.11), channel_id=1, source_target_pairs={{0,4},{1,3},{4,8},{5,1},{8,12},{9,5},{12,14},{13,9},{14,10},{15,13... | collective-permute-start | bytes 786440 | tf_op jit(solution)/shard_map/ppermute | solution.py:331
  58.0 3.2 %collective-permute-done.24.refs_2_ = bf16[16,8192]{1,0:T(8,128)(2,1)S(1)} collective-permute-done((bf16[16,8192]{1,0:T(8,128)(2,1)S(1)}, bf16[16,8192]{1,0:T(8,128)(2,1)S(1)}, u32[]{:S(2)}, u32[]{:S(2)}) %collective-permute-start.24) | collective-permute-done | bytes 262176 | tf_op jit(solution)/shard_map/ppermute | solution.py:331
  61.1 0.1 added.8
  61.2 1.3 %collective-permute-start.25 = (bf16[16,8192]{1,0:T(8,128)(2,1)S(1)}, bf16[16,8192]{1,0:T(8,128)(2,1)S(1)}, u32[]{:S(2)}, u32[]{:S(2)}) collective-permute-start(bf16[16,8192]{1,0:T(8,128)(2,1)S(1)} %added.8), channel_id=1, source_target_pairs={{0,4},{1,3},{4,8},{5,1},{8,12},{9,5},{12,14},{13,9},{14,10},{15,13... | collective-permute-start | bytes 786440 | tf_op jit(solution)/shard_map/ppermute | solution.py:331
  62.6 1.4 %collective-permute-done.28.refs_2_ = bf16[16,8192]{1,0:T(8,128)(2,1)S(1)} collective-permute-done((bf16[16,8192]{1,0:T(8,128)(2,1)S(1)}, bf16[16,8192]{1,0:T(8,128)(2,1)S(1)}, u32[]{:S(2)}, u32[]{:S(2)}) %collective-permute-start.28) | collective-permute-done | bytes 262176 | tf_op jit(solution)/shard_map/ppermute | solution.py:331
  63.9 0.1 added.12
  64.0 1.3 %collective-permute-start.29 = (bf16[16,8192]{1,0:T(8,128)(2,1)S(1)}, bf16[16,8192]{1,0:T(8,128)(2,1)S(1)}, u32[]{:S(2)}, u32[]{:S(2)}) collective-permute-start(bf16[16,8192]{1,0:T(8,128)(2,1)S(1)} %added.12), channel_id=1, source_target_pairs={{0,4},{1,3},{4,8},{5,1},{8,12},{9,5},{12,14},{13,9},{14,10},{15,13... | collective-permute-start | bytes 786440 | tf_op jit(solution)/shard_map/ppermute | solution.py:331
  65.4 2.3 %collective-permute-done.25.refs_2_ = bf16[16,8192]{1,0:T(8,128)(2,1)S(1)} collective-permute-done((bf16[16,8192]{1,0:T(8,128)(2,1)S(1)}, bf16[16,8192]{1,0:T(8,128)(2,1)S(1)}, u32[]{:S(2)}, u32[]{:S(2)}) %collective-permute-start.25) | collective-permute-done | bytes 262176 | tf_op jit(solution)/shard_map/ppermute | solution.py:331
  67.6 0.1 added.9
  67.7 1.3 %collective-permute-start.26 = (bf16[16,8192]{1,0:T(8,128)(2,1)S(1)}, bf16[16,8192]{1,0:T(8,128)(2,1)S(1)}, u32[]{:S(2)}, u32[]{:S(2)}) collective-permute-start(bf16[16,8192]{1,0:T(8,128)(2,1)S(1)} %added.9), channel_id=1, source_target_pairs={{0,4},{1,3},{4,8},{5,1},{8,12},{9,5},{12,14},{13,9},{14,10},{15,13... | collective-permute-start | bytes 786440 | tf_op jit(solution)/shard_map/ppermute | solution.py:331
  69.1 1.4 %collective-permute-done.29.refs_2_ = bf16[16,8192]{1,0:T(8,128)(2,1)S(1)} collective-permute-done((bf16[16,8192]{1,0:T(8,128)(2,1)S(1)}, bf16[16,8192]{1,0:T(8,128)(2,1)S(1)}, u32[]{:S(2)}, u32[]{:S(2)}) %collective-permute-start.29) | collective-permute-done | bytes 262176 | tf_op jit(solution)/shard_map/ppermute | solution.py:331
  70.5 0.1 added.13
  70.6 1.3 %collective-permute-start.30 = (bf16[16,8192]{1,0:T(8,128)(2,1)S(1)}, bf16[16,8192]{1,0:T(8,128)(2,1)S(1)}, u32[]{:S(2)}, u32[]{:S(2)}) collective-permute-start(bf16[16,8192]{1,0:T(8,128)(2,1)S(1)} %added.13), channel_id=1, source_target_pairs={{0,4},{1,3},{4,8},{5,1},{8,12},{9,5},{12,14},{13,9},{14,10},{15,13... | collective-permute-start | bytes 786440 | tf_op jit(solution)/shard_map/ppermute | solution.py:331
  71.9 2.3 %collective-permute-done.26.refs_2_ = bf16[16,8192]{1,0:T(8,128)(2,1)S(1)} collective-permute-done((bf16[16,8192]{1,0:T(8,128)(2,1)S(1)}, bf16[16,8192]{1,0:T(8,128)(2,1)S(1)}, u32[]{:S(2)}, u32[]{:S(2)}) %collective-permute-start.26) | collective-permute-done | bytes 262176 | tf_op jit(solution)/shard_map/ppermute | solution.py:331
  74.2 0.1 added.10
  74.3 1.3 %collective-permute-start.27 = (bf16[16,8192]{1,0:T(8,128)(2,1)S(1)}, bf16[16,8192]{1,0:T(8,128)(2,1)S(1)}, u32[]{:S(2)}, u32[]{:S(2)}) collective-permute-start(bf16[16,8192]{1,0:T(8,128)(2,1)S(1)} %added.10), channel_id=1, source_target_pairs={{0,4},{1,3},{4,8},{5,1},{8,12},{9,5},{12,14},{13,9},{14,10},{15,13... | collective-permute-start | bytes 786440 | tf_op jit(solution)/shard_map/ppermute | solution.py:331
  75.6 1.4 %collective-permute-done.30 = bf16[16,8192]{1,0:T(8,128)(2,1)S(1)} collective-permute-done((bf16[16,8192]{1,0:T(8,128)(2,1)S(1)}, bf16[16,8192]{1,0:T(8,128)(2,1)S(1)}, u32[]{:S(2)}, u32[]{:S(2)}) %collective-permute-start.30) | collective-permute-done | bytes 262176 | tf_op jit(solution)/shard_map/ppermute | solution.py:331
  77.0 3.7 %collective-permute-done.27.refs_2_ = bf16[16,8192]{1,0:T(8,128)(2,1)S(1)} collective-permute-done((bf16[16,8192]{1,0:T(8,128)(2,1)S(1)}, bf16[16,8192]{1,0:T(8,128)(2,1)S(1)}, u32[]{:S(2)}, u32[]{:S(2)}) %collective-permute-start.27) | collective-permute-done | bytes 262176 | tf_op jit(solution)/shard_map/ppermute | solution.py:331
  80.7 1.4 %last.1 = bf16[16,8192]{1,0:T(8,128)(2,1)} custom-call(s32[2]{0:T(128)S(1)} %copy-done.1, bf16[16,8192]{1,0:T(8,128)(2,1)S(1)} %get-tuple-element.26.refs_0_, bf16[16,8192]{1,0:T(8,128)(2,1)S(1)} %collective-permute-done.19.refs_1_, bf16[16,8192]{1,0:T(8,128)(2,1)S(1)} %collective-permute-done.27.refs_2_, bf16[16,8192]{1,0:T(8,128)(2,1)S(1)} %collective-permute-done.31.refs_3_), custom_call_target="tpu_custom_call" | custom-call | tf_op jit(solution)/shard_map/last/pallas_call | solution.py:281
  (48 shorter events, 0.1 us)
Async XLA Ops:
  0.0 3.0 %collective-permute-start = (bf16[16,8192]{1,0:T(8,128)(2,1)}, bf16[16,8192]{1,0:T(8,128)(2,1)S(1)}, u32[]{:S(2)}, u32[]{:S(2)}) collective-permute-start(bf16[16,8192]{1,0:T(8,128)(2,1)} %tokens_ref.1), channel_id=1, source_target_pairs={{0,1},{1,0},{2,3},{3,2},{4,5},{5,4},{6,7},{7,6},{8,9},{9,8},{10,11... | collective-permute-start | bytes 786440 | tf_op jit(solution)/shard_map/ppermute | solution.py:334
  0.5 7.1 %collective-permute-start.1 = (bf16[16,8192]{1,0:T(8,128)(2,1)}, bf16[16,8192]{1,0:T(8,128)(2,1)S(1)}, u32[]{:S(2)}, u32[]{:S(2)}) collective-permute-start(bf16[16,8192]{1,0:T(8,128)(2,1)} %tokens_ref.1), channel_id=1, source_target_pairs={{0,4},{1,3},{4,8},{5,1},{8,12},{9,5},{12,14},{13,9},{14,10},{15,13... | collective-permute-start | bytes 786440 | tf_op jit(solution)/shard_map/ppermute | solution.py:331
  3.0 0.7 copy-start.2
  3.7 27.2 %copy-start = (bf16[8192,896]{1,0:T(8,128)(2,1)S(1)}, bf16[8192,896]{1,0:T(8,128)(2,1)}, u32[]{:S(2)}) copy-start(bf16[8192,896]{1,0:T(8,128)(2,1)} %w_ref.6) | copy-start | bytes 44040196
  5.7 6.4 %collective-permute-start.2 = (bf16[16,8192]{1,0:T(8,128)(2,1)S(1)}, bf16[16,8192]{1,0:T(8,128)(2,1)S(1)}, u32[]{:S(2)}, u32[]{:S(2)}) collective-permute-start(bf16[16,8192]{1,0:T(8,128)(2,1)S(1)} %get-tuple-element.23.refs_1_), channel_id=1, source_target_pairs={{0,4},{1,3},{4,8},{5,1},{8,12},{9,5},{12,14},{13,9},{14,10},{15,13... | collective-permute-start | bytes 786440 | tf_op jit(solution)/shard_map/ppermute | solution.py:331
  7.5 7.4 %collective-permute-start.3 = (bf16[16,8192]{1,0:T(8,128)(2,1)S(1)}, bf16[16,8192]{1,0:T(8,128)(2,1)S(1)}, u32[]{:S(2)}, u32[]{:S(2)}) collective-permute-start(bf16[16,8192]{1,0:T(8,128)(2,1)S(1)} %collective-permute-done.1.refs_2_), channel_id=1, source_target_pairs={{0,4},{1,3},{4,8},{5,1},{8,12},{9,5},{12,14},{13,9},{14,10},{15,13... | collective-permute-start | bytes 786440 | tf_op jit(solution)/shard_map/ppermute | solution.py:331
  12.2 6.4 %collective-permute-start.4 = (bf16[16,8192]{1,0:T(8,128)(2,1)S(1)}, bf16[16,8192]{1,0:T(8,128)(2,1)S(1)}, u32[]{:S(2)}, u32[]{:S(2)}) collective-permute-start(bf16[16,8192]{1,0:T(8,128)(2,1)S(1)} %collective-permute-done.2.refs_3_), channel_id=1, source_target_pairs={{0,4},{1,3},{4,8},{5,1},{8,12},{9,5},{12,14},{13,9},{14,10},{15,13... | collective-permute-start | bytes 786440 | tf_op jit(solution)/shard_map/ppermute | solution.py:331
  15.0 6.4 %collective-permute-start.5 = (bf16[16,8192]{1,0:T(8,128)(2,1)S(1)}, bf16[16,8192]{1,0:T(8,128)(2,1)S(1)}, u32[]{:S(2)}, u32[]{:S(2)}) collective-permute-start(bf16[16,8192]{1,0:T(8,128)(2,1)S(1)} %collective-permute-done.3.refs_4_), channel_id=1, source_target_pairs={{0,4},{1,3},{4,8},{5,1},{8,12},{9,5},{12,14},{13,9},{14,10},{15,13... | collective-permute-start | bytes 786440 | tf_op jit(solution)/shard_map/ppermute | solution.py:331
  16.7 6.4 %collective-permute-start.8 = (bf16[16,8192]{1,0:T(8,128)(2,1)S(1)}, bf16[16,8192]{1,0:T(8,128)(2,1)S(1)}, u32[]{:S(2)}, u32[]{:S(2)}) collective-permute-start(bf16[16,8192]{1,0:T(8,128)(2,1)S(1)} %collective-permute-done.1.refs_2_), channel_id=1, source_target_pairs={{0,1},{1,0},{2,3},{3,2},{4,5},{5,4},{6,7},{7,6},{8,9},{9,8},{10,11... | collective-permute-start | bytes 786440 | tf_op jit(solution)/shard_map/ppermute | solution.py:334
  16.7 6.9 %collective-permute-start.9 = (bf16[16,8192]{1,0:T(8,128)(2,1)S(1)}, bf16[16,8192]{1,0:T(8,128)(2,1)S(1)}, u32[]{:S(2)}, u32[]{:S(2)}) collective-permute-start(bf16[16,8192]{1,0:T(8,128)(2,1)S(1)} %collective-permute-done.2.refs_3_), channel_id=1, source_target_pairs={{0,1},{1,0},{2,3},{3,2},{4,5},{5,4},{6,7},{7,6},{8,9},{9,8},{10,11... | collective-permute-start | bytes 786440 | tf_op jit(solution)/shard_map/ppermute | solution.py:334
  18.5 6.4 %collective-permute-start.6 = (bf16[16,8192]{1,0:T(8,128)(2,1)S(1)}, bf16[16,8192]{1,0:T(8,128)(2,1)S(1)}, u32[]{:S(2)}, u32[]{:S(2)}) collective-permute-start(bf16[16,8192]{1,0:T(8,128)(2,1)S(1)} %collective-permute-done.4.refs_5_), channel_id=1, source_target_pairs={{0,4},{1,3},{4,8},{5,1},{8,12},{9,5},{12,14},{13,9},{14,10},{15,13... | collective-permute-start | bytes 786440 | tf_op jit(solution)/shard_map/ppermute | solution.py:331
  21.3 6.4 %collective-permute-start.7 = (bf16[16,8192]{1,0:T(8,128)(2,1)S(1)}, bf16[16,8192]{1,0:T(8,128)(2,1)S(1)}, u32[]{:S(2)}, u32[]{:S(2)}) collective-permute-start(bf16[16,8192]{1,0:T(8,128)(2,1)S(1)} %collective-permute-done.5.refs_6_), channel_id=1, source_target_pairs={{0,4},{1,3},{4,8},{5,1},{8,12},{9,5},{12,14},{13,9},{14,10},{15,13... | collective-permute-start | bytes 786440 | tf_op jit(solution)/shard_map/ppermute | solution.py:331
  23.1 4.6 %collective-permute-start.10 = (bf16[16,8192]{1,0:T(8,128)(2,1)S(1)}, bf16[16,8192]{1,0:T(8,128)(2,1)S(1)}, u32[]{:S(2)}, u32[]{:S(2)}) collective-permute-start(bf16[16,8192]{1,0:T(8,128)(2,1)S(1)} %collective-permute-done.3.refs_4_), channel_id=1, source_target_pairs={{0,1},{1,0},{2,3},{3,2},{4,5},{5,4},{6,7},{7,6},{8,9},{9,8},{10,11... | collective-permute-start | bytes 786440 | tf_op jit(solution)/shard_map/ppermute | solution.py:334
  23.1 4.6 %collective-permute-start.11 = (bf16[16,8192]{1,0:T(8,128)(2,1)S(1)}, bf16[16,8192]{1,0:T(8,128)(2,1)S(1)}, u32[]{:S(2)}, u32[]{:S(2)}) collective-permute-start(bf16[16,8192]{1,0:T(8,128)(2,1)S(1)} %collective-permute-done.4.refs_5_), channel_id=1, source_target_pairs={{0,1},{1,0},{2,3},{3,2},{4,5},{5,4},{6,7},{7,6},{8,9},{9,8},{10,11... | collective-permute-start | bytes 786440 | tf_op jit(solution)/shard_map/ppermute | solution.py:334
  23.6 4.1 %collective-permute-start.12 = (bf16[16,8192]{1,0:T(8,128)(2,1)S(1)}, bf16[16,8192]{1,0:T(8,128)(2,1)S(1)}, u32[]{:S(2)}, u32[]{:S(2)}) collective-permute-start(bf16[16,8192]{1,0:T(8,128)(2,1)S(1)} %collective-permute-done.5.refs_6_), channel_id=1, source_target_pairs={{0,1},{1,0},{2,3},{3,2},{4,5},{5,4},{6,7},{7,6},{8,9},{9,8},{10,11... | collective-permute-start | bytes 786440 | tf_op jit(solution)/shard_map/ppermute | solution.py:334
  24.9 2.8 %collective-permute-start.13 = (bf16[16,8192]{1,0:T(8,128)(2,1)S(1)}, bf16[16,8192]{1,0:T(8,128)(2,1)S(1)}, u32[]{:S(2)}, u32[]{:S(2)}) collective-permute-start(bf16[16,8192]{1,0:T(8,128)(2,1)S(1)} %collective-permute-done.6.refs_7_), channel_id=1, source_target_pairs={{0,1},{1,0},{2,3},{3,2},{4,5},{5,4},{6,7},{7,6},{8,9},{9,8},{10,11... | collective-permute-start | bytes 786440 | tf_op jit(solution)/shard_map/ppermute | solution.py:334
  27.7 1.5 %collective-permute-start.14 = (bf16[16,8192]{1,0:T(8,128)(2,1)S(1)}, bf16[16,8192]{1,0:T(8,128)(2,1)S(1)}, u32[]{:S(2)}, u32[]{:S(2)}) collective-permute-start(bf16[16,8192]{1,0:T(8,128)(2,1)S(1)} %collective-permute-done.7.refs_8_), channel_id=1, source_target_pairs={{0,1},{1,0},{2,3},{3,2},{4,5},{5,4},{6,7},{7,6},{8,9},{9,8},{10,11... | collective-permute-start | bytes 786440 | tf_op jit(solution)/shard_map/ppermute | solution.py:334
  30.7 2.6 %collective-permute-start.15 = (bf16[8,256]{1,0:T(8,128)(2,1)S(1)}, bf16[8,256]{1,0:T(8,128)(2,1)S(1)}, u32[]{:S(2)}, u32[]{:S(2)}) collective-permute-start(bf16[8,256]{1,0:T(8,128)(2,1)S(1)} %rank.1.refs_16_), channel_id=1, source_target_pairs={{0,1},{1,0},{2,3},{3,2},{4,5},{5,4},{6,7},{7,6},{8,9},{9,8},{10,11... | collective-permute-start | bytes 12296 | tf_op jit(solution)/shard_map/ppermute | solution.py:334
  30.9 8.3 %slice-start = ((s8[14680064]{0:T(1024)(128)(4,1)}), s8[2097152]{0:T(1024)(128)(4,1)S(1)}, s32[]{:S(2)}) async-start(s8[14680064]{0:T(1024)(128)(4,1)} %bitcast.1), calls=%async_computation | async-start | bytes 4194304
  30.9 8.3 %slice-start.1 = ((s8[14680064]{0:T(1024)(128)(4,1)}), s8[4194304]{0:T(1024)(128)(4,1)S(1)}, s32[]{:S(2)}) async-start(s8[14680064]{0:T(1024)(128)(4,1)} %bitcast.1), calls=%async_computation.1 | async-start | bytes 8388608
  33.3 5.9 %slice-start.2 = ((s8[14680064]{0:T(1024)(128)(4,1)}), s8[4194304]{0:T(1024)(128)(4,1)S(1)}, s32[]{:S(2)}) async-start(s8[14680064]{0:T(1024)(128)(4,1)} %bitcast.1), calls=%async_computation.2 | async-start | bytes 8388608
  33.3 5.8 %slice-start.3 = ((s8[14680064]{0:T(1024)(128)(4,1)}), s8[4194304]{0:T(1024)(128)(4,1)S(1)}, s32[]{:S(2)}) async-start(s8[14680064]{0:T(1024)(128)(4,1)} %bitcast.1), calls=%async_computation.3 | async-start | bytes 8388608
  33.3 4.2 %collective-permute-start.16 = (bf16[16,256]{1,0:T(8,128)(2,1)S(1)}, bf16[16,256]{1,0:T(8,128)(2,1)S(1)}, u32[]{:S(2)}, u32[]{:S(2)}) collective-permute-start(bf16[16,256]{1,0:T(8,128)(2,1)S(1)} %pad_maximum_fusion.2), channel_id=1, source_target_pairs={{0,2},{1,3},{2,0},{3,1},{4,6},{5,7},{6,4},{7,5},{8,10},{9,11},{10,... | collective-permute-start | bytes 24584 | tf_op jit(solution)/shard_map/ppermute | solution.py:334
  37.5 4.1 %collective-permute-start.17 = (bf16[32,256]{1,0:T(8,128)(2,1)S(1)}, bf16[32,256]{1,0:T(8,128)(2,1)S(1)}, u32[]{:S(2)}, u32[]{:S(2)}) collective-permute-start(bf16[32,256]{1,0:T(8,128)(2,1)S(1)} %pad_maximum_fusion.1), channel_id=1, source_target_pairs={{0,4},{1,5},{2,6},{3,7},{4,0},{5,1},{6,2},{7,3},{8,12},{9,13},{10,... | collective-permute-start | bytes 49160 | tf_op jit(solution)/shard_map/ppermute | solution.py:334
  39.2 8.2 %slice-start.4 = ((s8[14680064]{0:T(1024)(128)(4,1)}), s8[4194304]{0:T(1024)(128)(4,1)S(1)}, s32[]{:S(2)}) async-start(s8[14680064]{0:T(1024)(128)(4,1)} %bitcast.3), calls=%async_computation.4 | async-start | bytes 8388608
  39.2 8.2 %slice-start.5 = ((s8[14680064]{0:T(1024)(128)(4,1)}), s8[4194304]{0:T(1024)(128)(4,1)S(1)}, s32[]{:S(2)}) async-start(s8[14680064]{0:T(1024)(128)(4,1)} %bitcast.3), calls=%async_computation.5 | async-start | bytes 8388608
  41.6 5.8 %slice-start.6 = ((s8[14680064]{0:T(1024)(128)(4,1)}), s8[4194304]{0:T(1024)(128)(4,1)S(1)}, s32[]{:S(2)}) async-start(s8[14680064]{0:T(1024)(128)(4,1)} %bitcast.3), calls=%async_computation.6 | async-start | bytes 8388608
  41.6 5.8 %slice-start.7 = ((s8[14680064]{0:T(1024)(128)(4,1)}), s8[2097152]{0:T(1024)(128)(4,1)S(1)}, s32[]{:S(2)}) async-start(s8[14680064]{0:T(1024)(128)(4,1)} %bitcast.3), calls=%async_computation.7 | async-start | bytes 4194304
  41.6 5.0 %collective-permute-start.18 = (bf16[64,256]{1,0:T(8,128)(2,1)S(1)}, bf16[64,256]{1,0:T(8,128)(2,1)S(1)}, u32[]{:S(2)}, u32[]{:S(2)}) collective-permute-start(bf16[64,256]{1,0:T(8,128)(2,1)S(1)} %pad_maximum_fusion), channel_id=1, source_target_pairs={{0,8},{1,9},{2,10},{3,11},{4,12},{5,13},{6,14},{7,15},{8,0},{9,1},... | collective-permute-start | bytes 98312 | tf_op jit(solution)/shard_map/ppermute | solution.py:334
  46.6 34.1 %copy-start.1 = (s32[2]{0:T(128)S(1)}, s32[2]{0:T(128)}, u32[]{:S(2)}) copy-start(s32[2]{0:T(128)} %counts_ref.1) | copy-start | bytes 28
  52.3 3.8 %collective-permute-start.22 = (bf16[32,8192]{1,0:T(8,128)(2,1)S(1)}, bf16[32,8192]{1,0:T(8,128)(2,1)S(1)}, u32[]{:S(2)}, u32[]{:S(2)}) collective-permute-start(bf16[32,8192]{1,0:T(8,128)(2,1)S(1)} %get-tuple-element.33), channel_id=1, source_target_pairs={{0,1},{1,0},{2,3},{3,2},{4,5},{5,4},{6,7},{7,6},{8,9},{9,8},{10,11... | collective-permute-start | bytes 1572872 | tf_op jit(solution)/shard_map/ppermute | solution.py:334
  52.4 2.3 %collective-permute-start.23 = (bf16[16,8192]{1,0:T(8,128)(2,1)S(1)}, bf16[16,8192]{1,0:T(8,128)(2,1)S(1)}, u32[]{:S(2)}, u32[]{:S(2)}) collective-permute-start(bf16[16,8192]{1,0:T(8,128)(2,1)S(1)} %get-tuple-element.35), channel_id=1, source_target_pairs={{0,1},{1,0},{2,3},{3,2},{4,5},{5,4},{6,7},{7,6},{8,9},{9,8},{10,11... | collective-permute-start | bytes 786440 | tf_op jit(solution)/shard_map/ppermute | solution.py:334
  52.9 9.7 %collective-permute-start.21 = (bf16[32,8192]{1,0:T(8,128)(2,1)S(1)}, bf16[32,8192]{1,0:T(8,128)(2,1)S(1)}, u32[]{:S(2)}, u32[]{:S(2)}) collective-permute-start(bf16[32,8192]{1,0:T(8,128)(2,1)S(1)} %get-tuple-element.31), channel_id=1, source_target_pairs={{0,1},{1,0},{2,3},{3,2},{4,5},{5,4},{6,7},{7,6},{8,9},{9,8},{10,11... | collective-permute-start | bytes 1572872 | tf_op jit(solution)/shard_map/ppermute | solution.py:334
  54.7 6.4 %collective-permute-start.24 = (bf16[16,8192]{1,0:T(8,128)(2,1)S(1)}, bf16[16,8192]{1,0:T(8,128)(2,1)S(1)}, u32[]{:S(2)}, u32[]{:S(2)}) collective-permute-start(bf16[16,8192]{1,0:T(8,128)(2,1)S(1)} %added.7), channel_id=1, source_target_pairs={{0,4},{1,3},{4,8},{5,1},{8,12},{9,5},{12,14},{13,9},{14,10},{15,13... | collective-permute-start | bytes 786440 | tf_op jit(solution)/shard_map/ppermute | solution.py:331
  56.1 7.8 %collective-permute-start.28 = (bf16[16,8192]{1,0:T(8,128)(2,1)S(1)}, bf16[16,8192]{1,0:T(8,128)(2,1)S(1)}, u32[]{:S(2)}, u32[]{:S(2)}) collective-permute-start(bf16[16,8192]{1,0:T(8,128)(2,1)S(1)} %added.11), channel_id=1, source_target_pairs={{0,4},{1,3},{4,8},{5,1},{8,12},{9,5},{12,14},{13,9},{14,10},{15,13... | collective-permute-start | bytes 786440 | tf_op jit(solution)/shard_map/ppermute | solution.py:331
  58.0 11.1 %collective-permute-start.20 = (bf16[32,8192]{1,0:T(8,128)(2,1)S(1)}, bf16[32,8192]{1,0:T(8,128)(2,1)S(1)}, u32[]{:S(2)}, u32[]{:S(2)}) collective-permute-start(bf16[32,8192]{1,0:T(8,128)(2,1)S(1)} %get-tuple-element.29), channel_id=1, source_target_pairs={{0,1},{1,0},{2,3},{3,2},{4,5},{5,4},{6,7},{7,6},{8,9},{9,8},{10,11... | collective-permute-start | bytes 1572872 | tf_op jit(solution)/shard_map/ppermute | solution.py:334
  61.2 6.4 %collective-permute-start.25 = (bf16[16,8192]{1,0:T(8,128)(2,1)S(1)}, bf16[16,8192]{1,0:T(8,128)(2,1)S(1)}, u32[]{:S(2)}, u32[]{:S(2)}) collective-permute-start(bf16[16,8192]{1,0:T(8,128)(2,1)S(1)} %added.8), channel_id=1, source_target_pairs={{0,4},{1,3},{4,8},{5,1},{8,12},{9,5},{12,14},{13,9},{14,10},{15,13... | collective-permute-start | bytes 786440 | tf_op jit(solution)/shard_map/ppermute | solution.py:331
  64.0 6.4 %collective-permute-start.29 = (bf16[16,8192]{1,0:T(8,128)(2,1)S(1)}, bf16[16,8192]{1,0:T(8,128)(2,1)S(1)}, u32[]{:S(2)}, u32[]{:S(2)}) collective-permute-start(bf16[16,8192]{1,0:T(8,128)(2,1)S(1)} %added.12), channel_id=1, source_target_pairs={{0,4},{1,3},{4,8},{5,1},{8,12},{9,5},{12,14},{13,9},{14,10},{15,13... | collective-permute-start | bytes 786440 | tf_op jit(solution)/shard_map/ppermute | solution.py:331
  67.7 6.4 %collective-permute-start.26 = (bf16[16,8192]{1,0:T(8,128)(2,1)S(1)}, bf16[16,8192]{1,0:T(8,128)(2,1)S(1)}, u32[]{:S(2)}, u32[]{:S(2)}) collective-permute-start(bf16[16,8192]{1,0:T(8,128)(2,1)S(1)} %added.9), channel_id=1, source_target_pairs={{0,4},{1,3},{4,8},{5,1},{8,12},{9,5},{12,14},{13,9},{14,10},{15,13... | collective-permute-start | bytes 786440 | tf_op jit(solution)/shard_map/ppermute | solution.py:331
  70.6 6.4 %collective-permute-start.30 = (bf16[16,8192]{1,0:T(8,128)(2,1)S(1)}, bf16[16,8192]{1,0:T(8,128)(2,1)S(1)}, u32[]{:S(2)}, u32[]{:S(2)}) collective-permute-start(bf16[16,8192]{1,0:T(8,128)(2,1)S(1)} %added.13), channel_id=1, source_target_pairs={{0,4},{1,3},{4,8},{5,1},{8,12},{9,5},{12,14},{13,9},{14,10},{15,13... | collective-permute-start | bytes 786440 | tf_op jit(solution)/shard_map/ppermute | solution.py:331
  71.9 5.1 %collective-permute-start.19 = (bf16[16,8192]{1,0:T(8,128)(2,1)S(1)}, bf16[16,8192]{1,0:T(8,128)(2,1)S(1)}, u32[]{:S(2)}, u32[]{:S(2)}) collective-permute-start(bf16[16,8192]{1,0:T(8,128)(2,1)S(1)} %get-tuple-element.27), channel_id=1, source_target_pairs={{0,1},{1,0},{2,3},{3,2},{4,5},{5,4},{6,7},{7,6},{8,9},{9,8},{10,11... | collective-permute-start | bytes 786440 | tf_op jit(solution)/shard_map/ppermute | solution.py:334
  74.3 6.4 %collective-permute-start.27 = (bf16[16,8192]{1,0:T(8,128)(2,1)S(1)}, bf16[16,8192]{1,0:T(8,128)(2,1)S(1)}, u32[]{:S(2)}, u32[]{:S(2)}) collective-permute-start(bf16[16,8192]{1,0:T(8,128)(2,1)S(1)} %added.10), channel_id=1, source_target_pairs={{0,4},{1,3},{4,8},{5,1},{8,12},{9,5},{12,14},{13,9},{14,10},{15,13... | collective-permute-start | bytes 786440 | tf_op jit(solution)/shard_map/ppermute | solution.py:331
  77.0 3.7 %collective-permute-start.31 = (bf16[16,8192]{1,0:T(8,128)(2,1)S(1)}, bf16[16,8192]{1,0:T(8,128)(2,1)S(1)}, u32[]{:S(2)}, u32[]{:S(2)}) collective-permute-start(bf16[16,8192]{1,0:T(8,128)(2,1)S(1)} %collective-permute-done.30), channel_id=1, source_target_pairs={{0,1},{1,0},{2,3},{3,2},{4,5},{5,4},{6,7},{7,6},{8,9},{9,8},{10,11... | collective-permute-start | bytes 786440 | tf_op jit(solution)/shard_map/ppermute | solution.py:334

commit v6 on v5

--- a/solution.py
+++ b/solution.py
@@ -88,55 +88,35 @@
     return pltpu.with_memory_space_constraint(x, pltpu.HBM)
 
 
-def prepare_kernel(blocks, ids_ref, tokens_ref, shrink_ref, expand_ref, passed_in, *refs):
-    own_ref, weights_ref, chosen_ref, passed_out, sems = refs
-    copies = [pltpu.make_async_copy(tokens_ref, own_ref, sems.at[0])]
-    for b in range(blocks):
-        copies.append(
-            pltpu.make_async_copy(shrink_ref.at[ids_ref[b]], weights_ref.at[b], sems.at[1 + 2 * b])
-        )
-        copies.append(
-            pltpu.make_async_copy(expand_ref.at[ids_ref[b]], chosen_ref.at[b], sems.at[2 + 2 * b])
-        )
-    for copy in copies:
-        copy.start()
-    for copy in copies:
-        copy.wait()
-
-
-def prepare(adapters, tokens, shrink, expand, passed):
-    blocks = adapters.shape[0]
-
-    def like(shape):
-        return jax.ShapeDtypeStruct(shape, BF16)
-
-    return pl.pallas_call(
-        functools.partial(prepare_kernel, blocks),
-        in_specs=[SCALARS, FAR, FAR, FAR, FAR],
-        out_specs=whole(3) + [FAR],
-        out_shape=[
-            like(tokens.shape),
-            like((blocks,) + shrink.shape[1:]),
-            like((blocks,) + expand.shape[1:]),
-            like(passed.shape),
-        ],
-        input_output_aliases={4: 3},
+def anchor_kernel(tokens_ref, passed_in, own_ref, passed_out, sem):
+    copy = pltpu.make_async_copy(tokens_ref, own_ref, sem)
+    copy.start()
+    copy.wait()
+
+
+def anchor(tokens, passed):
+    return pl.pallas_call(
+        anchor_kernel,
+        in_specs=[FAR, FAR],
+        out_specs=whole(1) + [FAR],
+        out_shape=[jax.ShapeDtypeStruct(passed.shape, passed.dtype)] * 2,
+        input_output_aliases={1: 1},
+        scratch_shapes=[pltpu.SemaphoreType.DMA],
+        compiler_params=params(),
         cost_estimate=cost(30_000_000_000, 0),
-        scratch_shapes=[pltpu.SemaphoreType.DMA((1 + 2 * blocks,))],
-        compiler_params=params(),
-        name="prepare",
-    )(adapters, far(tokens), far(shrink), far(expand), passed)
-
-
-def rank_kernel(shrink_ref, *refs):
+        name="anchor",
+    )(far(tokens), passed)
+
+
+def rank_kernel(blocks, ids_ref, shrink_ref, *refs):
     pieces, out_ref, scratch = refs[:-2], refs[-2], refs[-1]
     members = len(pieces)
     rows = pieces[0].shape[0]
-    blocks, span, _ = shrink_ref.shape
+    span = shrink_ref.shape[1]
     block_rows = members * rows // blocks
     places = arrivals(lax.axis_index("tp"), members, rows)
     lhs = jnp.concatenate([piece[...] for piece in pieces], axis=0)
-    weights = jnp.concatenate([shrink_ref[b] for b in range(blocks)], axis=0)
+    weights = jnp.concatenate([shrink_ref[ids_ref[b]] for b in range(blocks)], axis=0)
     found = lax.dot_general(
         lhs, weights, (((1,), (1,)), ((), ())), preferred_element_type=F32
     )
@@ -149,20 +129,20 @@
     out_ref[...] = scratch[...].T[:span].astype(BF16)
 
 
-def rank_of(pieces, shrink):
+def rank_of(adapters, pieces, shrink):
     rows, model = pieces[0].shape
-    blocks, span, _ = shrink.shape
+    blocks, span = adapters.shape[0], shrink.shape[1]
     total = rows * len(pieces)
     return pl.pallas_call(
-        rank_kernel,
-        in_specs=whole(1 + len(pieces)),
+        functools.partial(rank_kernel, blocks),
+        in_specs=[SCALARS] + whole(1 + len(pieces)),
         out_specs=whole(1)[0],
         out_shape=jax.ShapeDtypeStruct((span, total), BF16),
         scratch_shapes=[pltpu.VMEM((total, 128), F32)],
         compiler_params=params(),
         cost_estimate=cost(2 * total * model * span * blocks, 2 * total * model),
         name="rank",
-    )(shrink, *pieces)
+    )(adapters, shrink, *pieces)
 
 
 def product_kernel(first, w_ref, *refs):
@@ -195,21 +175,14 @@
     )(matrix, *pieces, after)
 
 
-def finish_kernel(span, gate_a, gate_b, up_a, up_b, rank_ref, expand_ref, hidden_ref):
+def finish_kernel(blocks, ids_ref, gate_a, gate_b, up_a, up_b, rank_ref, expand_ref, hidden_ref):
     ranks = rank_ref.shape[0]
-    device = lax.axis_index("tp")
-    shape = (ranks, ranks)
-    want = lax.broadcasted_iota(jnp.int32, shape, 0)
-    have = lax.broadcasted_iota(jnp.int32, shape, 1)
-    origin = ((have // span) ^ device) * span + have % span
-    order = jnp.where(want == origin, 1.0, 0.0).astype(BF16)
-    rank = jnp.dot(order, rank_ref[...], preferred_element_type=F32).T.astype(BF16)
+    rank = rank_ref[...].astype(F32).T.astype(BF16)
     half = ranks // 2
-    blocks = expand_ref.shape[0]
     rows = hidden_ref.shape[0] // blocks
     for b in range(blocks):
         part = slice(b * rows, (b + 1) * rows)
-        expand = expand_ref[b]
+        expand = expand_ref[ids_ref[b]]
         gate = jnp.dot(rank[part, :half], expand[:half], preferred_element_type=F32)
         up = jnp.dot(rank[part, half:], expand[half:], preferred_element_type=F32)
         gate += gate_a[part] + gate_b[part]
@@ -217,16 +190,16 @@
         hidden_ref[part] = (gate / (1.0 + jnp.exp(-gate)) * up).astype(BF16)
 
 
-def finish(products, rank, expand, span):
+def finish(adapters, products, rank, expand):
     total, width = products[0].shape
     return pl.pallas_call(
-        functools.partial(finish_kernel, span),
-        in_specs=whole(6),
+        functools.partial(finish_kernel, adapters.shape[0]),
+        in_specs=[SCALARS] + whole(6),
         out_specs=whole(1)[0],
         out_shape=jax.ShapeDtypeStruct((total, width), BF16),
         compiler_params=params(),
         name="finish",
-    )(*products, rank, expand)
+    )(adapters, *products, rank, expand)
 
 
 def down_kernel(members, groups, rows, size, w_ref, hidden_ref, *refs):
@@ -334,13 +307,7 @@
         return lax.ppermute(x, "tp", crossing(members, bit))
 
     first = tokens
-    own, shrink, expand, second = prepare(
-        adapter_per_block,
-        tokens,
-        jnp.swapaxes(shrink_matrices, 1, 2),
-        expand_matrices,
-        cross(tokens),
-    )
+    own, second = anchor(tokens, cross(tokens))
     pieces, mine, theirs = [own, second], [], []
     for distance in range(1, reach + 1):
         first = step(first)
@@ -352,19 +319,16 @@
             theirs.append(cross(second))
     pieces = pieces + mine + theirs
 
-    rank = rank_of(pieces, shrink)
-    work = [(gate_matrix, 0), (gate_matrix, 1), (up_matrix, 0), (up_matrix, 1)]
-    products, after = [], rank
-    bit = 1
-    while bit < members or work:
-        if work:
-            matrix, part = work.pop(0)
-            products.append(product(pieces, matrix, part, 2, after))
-        if bit < members:
-            after = cross(rank, bit)
-            rank = jnp.concatenate([rank, after], axis=0)
-            bit *= 2
-    hidden = finish(products, rank, expand, span)
+    rank = rank_of(adapter_per_block, pieces, jnp.swapaxes(shrink_matrices, 1, 2))
+    everyone = lax.all_to_all(
+        jnp.broadcast_to(rank[None], (members,) + rank.shape), "tp", 0, 0, tiled=True
+    ).reshape(members * span, -1)
+    products = [
+        product(pieces, matrix, part, 2, rank)
+        for matrix in (gate_matrix, up_matrix)
+        for part in range(2)
+    ]
+    hidden = finish(adapter_per_block, products, everyone, expand_matrices)
 
     slots = 2 * reach
     groups = [1] * slots + [1] + [2] * (reach - 1) + [1]

time: 82.2 us -> 107 us (1.30)
  local copies, waits for them, and re-layouts: 0.73 us -> 24.5 us
  starting transfers between devices: 31.7 us -> 36 us
  waiting for transfers between devices: 28.8 us -> 25.6 us
    unnamed x26 -> x48, local copies, waits for them, and re-layouts: 0.72 us -> 23.9 us
    all_to_all x0 -> x1, starting transfers between devices: none -> 6.63 us  [per_device(): lax.all_to_all(jnp.broadcast_to(rank[None], (members,) + rank.shape), 'tp...]
    ppermute x18 -> x14, starting transfers between devices: 8.44 us -> 2.55 us  [cross(): return lax.ppermute(x, 'tp', crossing(members, bit))]
    ppermute x14, starting transfers between devices: 23.3 us -> 26.8 us  [step(): return lax.ppermute(x, 'tp', ring)]
    ppermute x14, waiting for transfers between devices: 25.5 us -> 22.5 us  [step(): return lax.ppermute(x, 'tp', ring)]
    ppermute x18 -> x14, waiting for transfers between devices: 3.24 us -> 3.07 us  [cross(): return lax.ppermute(x, 'tp', crossing(members, bit))]
  transfers between devices with their start and end apart: 32 -> 29, of which waited for: 15 -> 16; matrix products, arithmetic and copies ran while one was open for 0% -> 0% of each run, Pallas kernels for 15% -> 10%
where the time goes in v6:
time: 107 us
  starting transfers between devices  36 us (34%)
  waiting for transfers between devices  25.6 us (24%)
  local copies, waits for them, and re-layouts  24.5 us (23%)
  Pallas kernels  20.4 us (19%)
    ppermute x14, starting transfers between devices, step(): return lax.ppermute(x, 'tp', ring)  26.8 us
    unnamed x48, local copies, waits for them, and re-layouts  23.9 us
    ppermute x14, waiting for transfers between devices, step(): return lax.ppermute(x, 'tp', ring)  22.5 us
    pallas_call x4, Pallas kernels, product(): pl.pallas_call(functools.partial(product_kernel, part * depth), in_specs=...  9.52 us
    all_to_all x1, starting transfers between devices, per_device(): lax.all_to_all(jnp.broadcast_to(rank[None], (members,) + rank.shape), 'tp...  6.63 us
    pallas_call x1, Pallas kernels, down(): pl.pallas_call(functools.partial(down_kernel, total // rows, groups, rows...  4.63 us
    ppermute x14, waiting for transfers between devices, cross(): return lax.ppermute(x, 'tp', crossing(members, bit))  3.07 us
    ppermute x14, starting transfers between devices, cross(): return lax.ppermute(x, 'tp', crossing(members, bit))  2.55 us
  transfers between devices with their start and end apart: 29, of which 16 were waited for; matrix products, arithmetic and copies ran while one was open for 0% of the time, Pallas kernels for 10%

profile of v6, /device:TPU:0, one launch (start us, length us, event | category | flops | bytes accessed | tf_op | source)
XLA Modules:
  0.0 106.7 jit_solution(12984284680517380271)
XLA Ops:
  0.0 0.5 collective-permute-start
  0.5 2.6 %collective-permute-start.1 = (bf16[16,8192]{1,0:T(8,128)(2,1)}, bf16[16,8192]{1,0:T(8,128)(2,1)S(1)}, u32[]{:S(2)}, u32[]{:S(2)}) collective-permute-start(bf16[16,8192]{1,0:T(8,128)(2,1)} %tokens_ref.1), channel_id=1, source_target_pairs={{0,4},{1,3},{4,8},{5,1},{8,12},{9,5},{12,14},{13,9},{14,10},{15,13... | collective-permute-start | bytes 786440 | tf_op jit(solution)/shard_map/ppermute | solution.py:304
  3.1 1.0 anchor.1
  4.1 1.7 %collective-permute-start.2 = (bf16[16,8192]{1,0:T(8,128)(2,1)S(1)}, bf16[16,8192]{1,0:T(8,128)(2,1)S(1)}, u32[]{:S(2)}, u32[]{:S(2)}) collective-permute-start(bf16[16,8192]{1,0:T(8,128)(2,1)S(1)} %get-tuple-element.21.refs_1_), channel_id=1, source_target_pairs={{0,4},{1,3},{4,8},{5,1},{8,12},{9,5},{12,14},{13,9},{14,10},{15,13... | collective-permute-start | bytes 786440 | tf_op jit(solution)/shard_map/ppermute | solution.py:304
  5.8 1.8 %collective-permute-done.1.refs_2_ = bf16[16,8192]{1,0:T(8,128)(2,1)S(1)} collective-permute-done((bf16[16,8192]{1,0:T(8,128)(2,1)}, bf16[16,8192]{1,0:T(8,128)(2,1)S(1)}, u32[]{:S(2)}, u32[]{:S(2)}) %collective-permute-start.1) | collective-permute-done | bytes 262176 | tf_op jit(solution)/shard_map/ppermute | solution.py:304
  7.6 2.1 %collective-permute-start.3 = (bf16[16,8192]{1,0:T(8,128)(2,1)S(1)}, bf16[16,8192]{1,0:T(8,128)(2,1)S(1)}, u32[]{:S(2)}, u32[]{:S(2)}) collective-permute-start(bf16[16,8192]{1,0:T(8,128)(2,1)S(1)} %collective-permute-done.1.refs_2_), channel_id=1, source_target_pairs={{0,4},{1,3},{4,8},{5,1},{8,12},{9,5},{12,14},{13,9},{14,10},{15,13... | collective-permute-start | bytes 786440 | tf_op jit(solution)/shard_map/ppermute | solution.py:304
  9.7 0.9 collective-permute-done.2.refs_3_
  10.5 2.0 %collective-permute-start.4 = (bf16[16,8192]{1,0:T(8,128)(2,1)S(1)}, bf16[16,8192]{1,0:T(8,128)(2,1)S(1)}, u32[]{:S(2)}, u32[]{:S(2)}) collective-permute-start(bf16[16,8192]{1,0:T(8,128)(2,1)S(1)} %collective-permute-done.2.refs_3_), channel_id=1, source_target_pairs={{0,4},{1,3},{4,8},{5,1},{8,12},{9,5},{12,14},{13,9},{14,10},{15,13... | collective-permute-start | bytes 786440 | tf_op jit(solution)/shard_map/ppermute | solution.py:304
  12.5 1.5 %collective-permute-done.3.refs_4_ = bf16[16,8192]{1,0:T(8,128)(2,1)S(1)} collective-permute-done((bf16[16,8192]{1,0:T(8,128)(2,1)S(1)}, bf16[16,8192]{1,0:T(8,128)(2,1)S(1)}, u32[]{:S(2)}, u32[]{:S(2)}) %collective-permute-start.3) | collective-permute-done | bytes 262176 | tf_op jit(solution)/shard_map/ppermute | solution.py:304
  14.0 2.1 %collective-permute-start.5 = (bf16[16,8192]{1,0:T(8,128)(2,1)S(1)}, bf16[16,8192]{1,0:T(8,128)(2,1)S(1)}, u32[]{:S(2)}, u32[]{:S(2)}) collective-permute-start(bf16[16,8192]{1,0:T(8,128)(2,1)S(1)} %collective-permute-done.3.refs_4_), channel_id=1, source_target_pairs={{0,4},{1,3},{4,8},{5,1},{8,12},{9,5},{12,14},{13,9},{14,10},{15,13... | collective-permute-start | bytes 786440 | tf_op jit(solution)/shard_map/ppermute | solution.py:304
  16.0 0.5 collective-permute-start.9
  16.6 0.3 collective-permute-done.4.refs_5_
  16.9 2.0 %collective-permute-start.6 = (bf16[16,8192]{1,0:T(8,128)(2,1)S(1)}, bf16[16,8192]{1,0:T(8,128)(2,1)S(1)}, u32[]{:S(2)}, u32[]{:S(2)}) collective-permute-start(bf16[16,8192]{1,0:T(8,128)(2,1)S(1)} %collective-permute-done.4.refs_5_), channel_id=1, source_target_pairs={{0,4},{1,3},{4,8},{5,1},{8,12},{9,5},{12,14},{13,9},{14,10},{15,13... | collective-permute-start | bytes 786440 | tf_op jit(solution)/shard_map/ppermute | solution.py:304
  18.9 1.5 %collective-permute-done.5.refs_6_ = bf16[16,8192]{1,0:T(8,128)(2,1)S(1)} collective-permute-done((bf16[16,8192]{1,0:T(8,128)(2,1)S(1)}, bf16[16,8192]{1,0:T(8,128)(2,1)S(1)}, u32[]{:S(2)}, u32[]{:S(2)}) %collective-permute-start.5) | collective-permute-done | bytes 262176 | tf_op jit(solution)/shard_map/ppermute | solution.py:304
  20.3 2.1 %collective-permute-start.7 = (bf16[16,8192]{1,0:T(8,128)(2,1)S(1)}, bf16[16,8192]{1,0:T(8,128)(2,1)S(1)}, u32[]{:S(2)}, u32[]{:S(2)}) collective-permute-start(bf16[16,8192]{1,0:T(8,128)(2,1)S(1)} %collective-permute-done.5.refs_6_), channel_id=1, source_target_pairs={{0,4},{1,3},{4,8},{5,1},{8,12},{9,5},{12,14},{13,9},{14,10},{15,13... | collective-permute-start | bytes 786440 | tf_op jit(solution)/shard_map/ppermute | solution.py:304
  22.4 0.5 collective-permute-start.11
  23.0 0.3 collective-permute-done.6.refs_7_
  23.3 0.2 collective-permute-start.13
  23.5 3.3 %collective-permute-done.7.refs_8_ = bf16[16,8192]{1,0:T(8,128)(2,1)S(1)} collective-permute-done((bf16[16,8192]{1,0:T(8,128)(2,1)S(1)}, bf16[16,8192]{1,0:T(8,128)(2,1)S(1)}, u32[]{:S(2)}, u32[]{:S(2)}) %collective-permute-start.7) | collective-permute-done | bytes 262176 | tf_op jit(solution)/shard_map/ppermute | solution.py:304
  26.7 1.5 %collective-permute-done.14.refs_15_ = bf16[16,8192]{1,0:T(8,128)(2,1)S(1)} collective-permute-done((bf16[16,8192]{1,0:T(8,128)(2,1)S(1)}, bf16[16,8192]{1,0:T(8,128)(2,1)S(1)}, u32[]{:S(2)}, u32[]{:S(2)}) %collective-permute-start.14) | collective-permute-done | bytes 262176 | tf_op jit(solution)/shard_map/ppermute | solution.py:307
  28.3 2.0 %rank.1.refs_16_ = bf16[8,256]{1,0:T(8,128)(2,1)S(1)} custom-call(s32[2]{0:T(128)S(1)} %copy-done.18, bf16[8,8,8192]{2,1,0:T(8,128)(2,1)S(1)} %bitcast.4, bf16[16,8192]{1,0:T(8,128)(2,1)S(1)} %get-tuple-element.20.refs_0_, bf16[16,8192]{1,0:T(8,128)(2,1)S(1)} %get-tuple-element.21.refs_1_, bf16[16,8192]{1,0:T(8,128)(2,1)S(1)} %collective-permute-done.1.refs_2_, ...), custom_call_target="tpu_custom_call" | custom-call | flops 67108864 | bytes 4194304 | tf_op jit(solution)/shard_map/rank/pallas_call | solution.py:136
  30.3 0.7 copy-done.2
  31.0 0.6 broadcast_in_dim.2
  31.6 6.6 %all-to-all-start = ((bf16[16,8,256]{2,1,0:T(8,128)(2,1)}), bf16[16,8,256]{2,1,0:T(8,128)(2,1)S(1)}, u32[]{:S(2)}, u32[]{:S(2)}) async-start(bf16[16,8,256]{2,1,0:T(8,128)(2,1)} %broadcast_in_dim.2), calls=%async_computation | async-start | bytes 131072 | tf_op jit(solution)/shard_map/all_to_all | solution.py:323
  38.2 5.2 %copy-done = bf16[8192,896]{1,0:T(8,128)(2,1)S(1)} copy-done((bf16[8192,896]{1,0:T(8,128)(2,1)S(1)}, bf16[8192,896]{1,0:T(8,128)(2,1)}, u32[]{:S(2)}) %copy-start) | copy-done | bytes 14680088
  43.4 0.9 copy-done.3
  44.4 0.9 copy-done.5
  45.3 0.9 copy-done.7
  46.3 2.4 %product.7.up_b = f32[256,896]{1,0:T(8,128)S(1)} custom-call(bf16[8192,896]{1,0:T(8,128)(2,1)S(1)} %copy-done, bf16[16,8192]{1,0:T(8,128)(2,1)S(1)} %get-tuple-element.20.refs_0_, bf16[16,8192]{1,0:T(8,128)(2,1)S(1)} %copy-done.7, bf16[16,8192]{1,0:T(8,128)(2,1)S(1)} %collective-permute-done.1.refs_2_, bf16[16,8192]{1,0:T(8,128)(2,1)S(1)} %collective-permute-done.2.refs_3_, ...), custom_call_target="tpu_custom_call" | custom-call | flops 1879048192 | bytes 9437184 | tf_op jit(solution)/shard_map/product/pallas_call | solution.py:167
  48.7 0.9 copy-done.8
  49.6 2.4 %product.6.up_a = f32[256,896]{1,0:T(8,128)S(1)} custom-call(bf16[8192,896]{1,0:T(8,128)(2,1)S(1)} %copy-done, bf16[16,8192]{1,0:T(8,128)(2,1)S(1)} %get-tuple-element.20.refs_0_, bf16[16,8192]{1,0:T(8,128)(2,1)S(1)} %copy-done.7, bf16[16,8192]{1,0:T(8,128)(2,1)S(1)} %collective-permute-done.1.refs_2_, bf16[16,8192]{1,0:T(8,128)(2,1)S(1)} %collective-permute-done.2.refs_3_, ...), custom_call_target="tpu_custom_call" | custom-call | flops 1879048192 | bytes 9437184 | tf_op jit(solution)/shard_map/product/pallas_call | solution.py:167
  52.0 0.9 copy-done.10
  52.9 2.4 %product.5.gate_b = f32[256,896]{1,0:T(8,128)S(1)} custom-call(bf16[8192,896]{1,0:T(8,128)(2,1)S(1)} %bitcast.3, bf16[16,8192]{1,0:T(8,128)(2,1)S(1)} %get-tuple-element.20.refs_0_, bf16[16,8192]{1,0:T(8,128)(2,1)S(1)} %copy-done.7, bf16[16,8192]{1,0:T(8,128)(2,1)S(1)} %collective-permute-done.1.refs_2_, ...), custom_call_target="tpu_custom_call" | custom-call | flops 1879048192 | bytes 9437184 | tf_op jit(solution)/shard_map/product/pallas_call | solution.py:167
  55.3 0.9 copy-done.12
  56.2 2.4 %product.4.gate_a = f32[256,896]{1,0:T(8,128)S(1)} custom-call(bf16[8192,896]{1,0:T(8,128)(2,1)S(1)} %bitcast.3, bf16[16,8192]{1,0:T(8,128)(2,1)S(1)} %get-tuple-element.20.refs_0_, bf16[16,8192]{1,0:T(8,128)(2,1)S(1)} %copy-done.7, bf16[16,8192]{1,0:T(8,128)(2,1)S(1)} %collective-permute-done.1.refs_2_, ...), custom_call_target="tpu_custom_call" | custom-call | flops 1879048192 | bytes 9437184 | tf_op jit(solution)/shard_map/product/pallas_call | solution.py:167
  58.6 0.9 copy-done.14
  59.6 1.2 %copy-done.9 = f32[256,896]{1,0:T(8,128)S(1)} copy-done((f32[256,896]{1,0:T(8,128)S(1)}, f32[256,896]{1,0:T(8,128)}, u32[]{:S(2)}) %copy-start.9) | copy-done | bytes 917528
  60.8 1.2 %copy-done.11 = f32[256,896]{1,0:T(8,128)S(1)} copy-done((f32[256,896]{1,0:T(8,128)S(1)}, f32[256,896]{1,0:T(8,128)}, u32[]{:S(2)}) %copy-start.11) | copy-done | bytes 917528
  61.9 1.2 %copy-done.13 = f32[256,896]{1,0:T(8,128)S(1)} copy-done((f32[256,896]{1,0:T(8,128)S(1)}, f32[256,896]{1,0:T(8,128)}, u32[]{:S(2)}) %copy-start.13) | copy-done | bytes 917528
  63.1 1.2 %copy-done.15 = f32[256,896]{1,0:T(8,128)S(1)} copy-done((f32[256,896]{1,0:T(8,128)S(1)}, f32[256,896]{1,0:T(8,128)}, u32[]{:S(2)}) %copy-start.15) | copy-done | bytes 917528
  64.3 1.5 %copy-done.16 = bf16[8,128,896]{2,1,0:T(8,128)(2,1)S(1)} copy-done((bf16[8,128,896]{2,1,0:T(8,128)(2,1)S(1)}, bf16[8,128,896]{2,1,0:T(8,128)(2,1)}, u32[]{:S(2)}) %copy-start.16) | copy-done | bytes 1835032
  65.8 1.2 %finish.1.hidden_ref = bf16[256,896]{1,0:T(8,128)(2,1)S(1)} custom-call(s32[2]{0:T(128)S(1)} %copy-done.18, f32[256,896]{1,0:T(8,128)S(1)} %copy-done.15, f32[256,896]{1,0:T(8,128)S(1)} %copy-done.13, f32[256,896]{1,0:T(8,128)S(1)} %copy-done.11, f32[256,896]{1,0:T(8,128)S(1)} %copy-done.9, bf16[128,256]{1,0:T(8,128)(2,1)S(1)} %bitcast.5, ...), custom_call_target="tpu_custom_call" | custom-call | tf_op jit(solution)/shard_map/finish/pallas_call | solution.py:195
  67.1 5.2 %copy-done.1 = bf16[896,8192]{1,0:T(8,128)(2,1)S(1)} copy-done((bf16[896,8192]{1,0:T(8,128)(2,1)S(1)}, bf16[896,8192]{1,0:T(8,128)(2,1)}, u32[]{:S(2)}) %copy-start.1) | copy-done | bytes 14680088
  72.2 4.6 %down.1 = (bf16[16,8192]{1,0:T(8,128)(2,1)S(1)}, bf16[16,8192]{1,0:T(8,128)(2,1)S(1)}, bf16[16,8192]{1,0:T(8,128)(2,1)S(1)}, bf16[16,8192]{1,0:T(8,128)(2,1)S(1)...) custom-call(bf16[896,8192]{1,0:T(8,128)(2,1)S(1)} %copy-done.1, ...), custom_call_target="tpu_custom_call" | custom-call | flops 3758096384 | bytes 18874368 | tf_op jit(solution)/shard_map/down/pallas_call | solution.py:226
  76.9 0.3 collective-permute-start.18
  77.2 0.3 collective-permute-start.19
  77.4 0.2 collective-permute-start.17
  77.7 1.5 %collective-permute-done.19.refs_1_ = bf16[16,8192]{1,0:T(8,128)(2,1)S(1)} collective-permute-done((bf16[16,8192]{1,0:T(8,128)(2,1)S(1)}, bf16[16,8192]{1,0:T(8,128)(2,1)S(1)}, u32[]{:S(2)}, u32[]{:S(2)}) %collective-permute-start.19) | collective-permute-done | bytes 262176 | tf_op jit(solution)/shard_map/ppermute | solution.py:307
  79.3 1.8 %collective-permute-start.20 = (bf16[16,8192]{1,0:T(8,128)(2,1)S(1)}, bf16[16,8192]{1,0:T(8,128)(2,1)S(1)}, u32[]{:S(2)}, u32[]{:S(2)}) collective-permute-start(bf16[16,8192]{1,0:T(8,128)(2,1)S(1)} %added.7), channel_id=1, source_target_pairs={{0,4},{1,3},{4,8},{5,1},{8,12},{9,5},{12,14},{13,9},{14,10},{15,13... | collective-permute-start | bytes 786440 | tf_op jit(solution)/shard_map/ppermute | solution.py:304
  81.2 1.5 %collective-permute-start.24 = (bf16[16,8192]{1,0:T(8,128)(2,1)S(1)}, bf16[16,8192]{1,0:T(8,128)(2,1)S(1)}, u32[]{:S(2)}, u32[]{:S(2)}) collective-permute-start(bf16[16,8192]{1,0:T(8,128)(2,1)S(1)} %added.11), channel_id=1, source_target_pairs={{0,4},{1,3},{4,8},{5,1},{8,12},{9,5},{12,14},{13,9},{14,10},{15,13... | collective-permute-start | bytes 786440 | tf_op jit(solution)/shard_map/ppermute | solution.py:304
  82.7 3.0 %collective-permute-done.20.refs_2_ = bf16[16,8192]{1,0:T(8,128)(2,1)S(1)} collective-permute-done((bf16[16,8192]{1,0:T(8,128)(2,1)S(1)}, bf16[16,8192]{1,0:T(8,128)(2,1)S(1)}, u32[]{:S(2)}, u32[]{:S(2)}) %collective-permute-start.20) | collective-permute-done | bytes 262176 | tf_op jit(solution)/shard_map/ppermute | solution.py:304
  85.7 0.1 added.8
  85.8 1.8 %collective-permute-start.21 = (bf16[16,8192]{1,0:T(8,128)(2,1)S(1)}, bf16[16,8192]{1,0:T(8,128)(2,1)S(1)}, u32[]{:S(2)}, u32[]{:S(2)}) collective-permute-start(bf16[16,8192]{1,0:T(8,128)(2,1)S(1)} %added.8), channel_id=1, source_target_pairs={{0,4},{1,3},{4,8},{5,1},{8,12},{9,5},{12,14},{13,9},{14,10},{15,13... | collective-permute-start | bytes 786440 | tf_op jit(solution)/shard_map/ppermute | solution.py:304
  87.6 0.9 collective-permute-done.24.refs_2_
  88.6 1.8 %collective-permute-start.25 = (bf16[16,8192]{1,0:T(8,128)(2,1)S(1)}, bf16[16,8192]{1,0:T(8,128)(2,1)S(1)}, u32[]{:S(2)}, u32[]{:S(2)}) collective-permute-start(bf16[16,8192]{1,0:T(8,128)(2,1)S(1)} %added.12), channel_id=1, source_target_pairs={{0,4},{1,3},{4,8},{5,1},{8,12},{9,5},{12,14},{13,9},{14,10},{15,13... | collective-permute-start | bytes 786440 | tf_op jit(solution)/shard_map/ppermute | solution.py:304
  90.4 1.8 %collective-permute-done.21.refs_2_ = bf16[16,8192]{1,0:T(8,128)(2,1)S(1)} collective-permute-done((bf16[16,8192]{1,0:T(8,128)(2,1)S(1)}, bf16[16,8192]{1,0:T(8,128)(2,1)S(1)}, u32[]{:S(2)}, u32[]{:S(2)}) %collective-permute-start.21) | collective-permute-done | bytes 262176 | tf_op jit(solution)/shard_map/ppermute | solution.py:304
  92.3 1.8 %collective-permute-start.22 = (bf16[16,8192]{1,0:T(8,128)(2,1)S(1)}, bf16[16,8192]{1,0:T(8,128)(2,1)S(1)}, u32[]{:S(2)}, u32[]{:S(2)}) collective-permute-start(bf16[16,8192]{1,0:T(8,128)(2,1)S(1)} %added.9), channel_id=1, source_target_pairs={{0,4},{1,3},{4,8},{5,1},{8,12},{9,5},{12,14},{13,9},{14,10},{15,13... | collective-permute-start | bytes 786440 | tf_op jit(solution)/shard_map/ppermute | solution.py:304
  94.1 0.9 collective-permute-done.25.refs_2_
  95.1 1.8 %collective-permute-start.26 = (bf16[16,8192]{1,0:T(8,128)(2,1)S(1)}, bf16[16,8192]{1,0:T(8,128)(2,1)S(1)}, u32[]{:S(2)}, u32[]{:S(2)}) collective-permute-start(bf16[16,8192]{1,0:T(8,128)(2,1)S(1)} %added.13), channel_id=1, source_target_pairs={{0,4},{1,3},{4,8},{5,1},{8,12},{9,5},{12,14},{13,9},{14,10},{15,13... | collective-permute-start | bytes 786440 | tf_op jit(solution)/shard_map/ppermute | solution.py:304
  96.9 1.8 %collective-permute-done.22.refs_2_ = bf16[16,8192]{1,0:T(8,128)(2,1)S(1)} collective-permute-done((bf16[16,8192]{1,0:T(8,128)(2,1)S(1)}, bf16[16,8192]{1,0:T(8,128)(2,1)S(1)}, u32[]{:S(2)}, u32[]{:S(2)}) %collective-permute-start.22) | collective-permute-done | bytes 262176 | tf_op jit(solution)/shard_map/ppermute | solution.py:304
  98.9 1.8 %collective-permute-start.23 = (bf16[16,8192]{1,0:T(8,128)(2,1)S(1)}, bf16[16,8192]{1,0:T(8,128)(2,1)S(1)}, u32[]{:S(2)}, u32[]{:S(2)}) collective-permute-start(bf16[16,8192]{1,0:T(8,128)(2,1)S(1)} %added.10), channel_id=1, source_target_pairs={{0,4},{1,3},{4,8},{5,1},{8,12},{9,5},{12,14},{13,9},{14,10},{15,13... | collective-permute-start | bytes 786440 | tf_op jit(solution)/shard_map/ppermute | solution.py:304
  100.7 0.9 collective-permute-done.26
  101.6 3.7 %collective-permute-done.23.refs_2_ = bf16[16,8192]{1,0:T(8,128)(2,1)S(1)} collective-permute-done((bf16[16,8192]{1,0:T(8,128)(2,1)S(1)}, bf16[16,8192]{1,0:T(8,128)(2,1)S(1)}, u32[]{:S(2)}, u32[]{:S(2)}) %collective-permute-start.23) | collective-permute-done | bytes 262176 | tf_op jit(solution)/shard_map/ppermute | solution.py:304
  105.3 1.4 %last.1 = bf16[16,8192]{1,0:T(8,128)(2,1)} custom-call(s32[2]{0:T(128)S(1)} %copy-done.19, bf16[16,8192]{1,0:T(8,128)(2,1)S(1)} %get-tuple-element.22.refs_0_, bf16[16,8192]{1,0:T(8,128)(2,1)S(1)} %collective-permute-done.15.refs_1_, bf16[16,8192]{1,0:T(8,128)(2,1)S(1)} %collective-permute-done.23.refs_2_, bf16[16,8192]{1,0:T(8,128)(2,1)S(1)} %collective-permute-done.27.refs_3_), custom_call_target="tpu_custom_call" | custom-call | tf_op jit(solution)/shard_map/last/pallas_call | solution.py:254
  (60 shorter events, 0.7 us)
Async XLA Ops:
  0.0 28.3 %copy-start.17 = (bf16[8,8192,8]{1,2,0:T(8,128)(2,1)S(1)}, bf16[8,8192,8]{1,2,0:T(8,128)(2,1)}, u32[]{:S(2)}) copy-start(bf16[8,8192,8]{1,2,0:T(8,128)(2,1)} %param.12) | copy-start | bytes 3145732
  0.0 28.3 %copy-start.18 = (s32[2]{0:T(128)S(1)}, s32[2]{0:T(128)}, u32[]{:S(2)}) copy-start(s32[2]{0:T(128)} %ids_ref.3) | copy-start | bytes 28
  0.0 3.1 %collective-permute-start = (bf16[16,8192]{1,0:T(8,128)(2,1)}, bf16[16,8192]{1,0:T(8,128)(2,1)S(1)}, u32[]{:S(2)}, u32[]{:S(2)}) collective-permute-start(bf16[16,8192]{1,0:T(8,128)(2,1)} %tokens_ref.1), channel_id=1, source_target_pairs={{0,1},{1,0},{2,3},{3,2},{4,5},{5,4},{6,7},{7,6},{8,9},{9,8},{10,11... | collective-permute-start | bytes 786440 | tf_op jit(solution)/shard_map/ppermute | solution.py:307
  0.5 7.1 %collective-permute-start.1 = (bf16[16,8192]{1,0:T(8,128)(2,1)}, bf16[16,8192]{1,0:T(8,128)(2,1)S(1)}, u32[]{:S(2)}, u32[]{:S(2)}) collective-permute-start(bf16[16,8192]{1,0:T(8,128)(2,1)} %tokens_ref.1), channel_id=1, source_target_pairs={{0,4},{1,3},{4,8},{5,1},{8,12},{9,5},{12,14},{13,9},{14,10},{15,13... | collective-permute-start | bytes 786440 | tf_op jit(solution)/shard_map/ppermute | solution.py:304
  4.1 26.2 %copy-start.6 = (bf16[16,8192]{1,0:T(8,128)(2,1)}, bf16[16,8192]{1,0:T(8,128)(2,1)S(1)}, u32[]{:S(2)}) copy-start(bf16[16,8192]{1,0:T(8,128)(2,1)S(1)} %get-tuple-element.21.refs_1_) | copy-start | bytes 786436
  4.1 6.4 %collective-permute-start.2 = (bf16[16,8192]{1,0:T(8,128)(2,1)S(1)}, bf16[16,8192]{1,0:T(8,128)(2,1)S(1)}, u32[]{:S(2)}, u32[]{:S(2)}) collective-permute-start(bf16[16,8192]{1,0:T(8,128)(2,1)S(1)} %get-tuple-element.21.refs_1_), channel_id=1, source_target_pairs={{0,4},{1,3},{4,8},{5,1},{8,12},{9,5},{12,14},{13,9},{14,10},{15,13... | collective-permute-start | bytes 786440 | tf_op jit(solution)/shard_map/ppermute | solution.py:304
  7.6 6.4 %collective-permute-start.3 = (bf16[16,8192]{1,0:T(8,128)(2,1)S(1)}, bf16[16,8192]{1,0:T(8,128)(2,1)S(1)}, u32[]{:S(2)}, u32[]{:S(2)}) collective-permute-start(bf16[16,8192]{1,0:T(8,128)(2,1)S(1)} %collective-permute-done.1.refs_2_), channel_id=1, source_target_pairs={{0,4},{1,3},{4,8},{5,1},{8,12},{9,5},{12,14},{13,9},{14,10},{15,13... | collective-permute-start | bytes 786440 | tf_op jit(solution)/shard_map/ppermute | solution.py:304
  10.5 6.4 %collective-permute-start.4 = (bf16[16,8192]{1,0:T(8,128)(2,1)S(1)}, bf16[16,8192]{1,0:T(8,128)(2,1)S(1)}, u32[]{:S(2)}, u32[]{:S(2)}) collective-permute-start(bf16[16,8192]{1,0:T(8,128)(2,1)S(1)} %collective-permute-done.2.refs_3_), channel_id=1, source_target_pairs={{0,4},{1,3},{4,8},{5,1},{8,12},{9,5},{12,14},{13,9},{14,10},{15,13... | collective-permute-start | bytes 786440 | tf_op jit(solution)/shard_map/ppermute | solution.py:304
  14.0 6.4 %collective-permute-start.5 = (bf16[16,8192]{1,0:T(8,128)(2,1)S(1)}, bf16[16,8192]{1,0:T(8,128)(2,1)S(1)}, u32[]{:S(2)}, u32[]{:S(2)}) collective-permute-start(bf16[16,8192]{1,0:T(8,128)(2,1)S(1)} %collective-permute-done.3.refs_4_), channel_id=1, source_target_pairs={{0,4},{1,3},{4,8},{5,1},{8,12},{9,5},{12,14},{13,9},{14,10},{15,13... | collective-permute-start | bytes 786440 | tf_op jit(solution)/shard_map/ppermute | solution.py:304
  16.0 6.4 %collective-permute-start.8 = (bf16[16,8192]{1,0:T(8,128)(2,1)S(1)}, bf16[16,8192]{1,0:T(8,128)(2,1)S(1)}, u32[]{:S(2)}, u32[]{:S(2)}) collective-permute-start(bf16[16,8192]{1,0:T(8,128)(2,1)S(1)} %collective-permute-done.1.refs_2_), channel_id=1, source_target_pairs={{0,1},{1,0},{2,3},{3,2},{4,5},{5,4},{6,7},{7,6},{8,9},{9,8},{10,11... | collective-permute-start | bytes 786440 | tf_op jit(solution)/shard_map/ppermute | solution.py:307
  16.0 6.9 %collective-permute-start.9 = (bf16[16,8192]{1,0:T(8,128)(2,1)S(1)}, bf16[16,8192]{1,0:T(8,128)(2,1)S(1)}, u32[]{:S(2)}, u32[]{:S(2)}) collective-permute-start(bf16[16,8192]{1,0:T(8,128)(2,1)S(1)} %collective-permute-done.2.refs_3_), channel_id=1, source_target_pairs={{0,1},{1,0},{2,3},{3,2},{4,5},{5,4},{6,7},{7,6},{8,9},{9,8},{10,11... | collective-permute-start | bytes 786440 | tf_op jit(solution)/shard_map/ppermute | solution.py:307
  16.9 6.4 %collective-permute-start.6 = (bf16[16,8192]{1,0:T(8,128)(2,1)S(1)}, bf16[16,8192]{1,0:T(8,128)(2,1)S(1)}, u32[]{:S(2)}, u32[]{:S(2)}) collective-permute-start(bf16[16,8192]{1,0:T(8,128)(2,1)S(1)} %collective-permute-done.4.refs_5_), channel_id=1, source_target_pairs={{0,4},{1,3},{4,8},{5,1},{8,12},{9,5},{12,14},{13,9},{14,10},{15,13... | collective-permute-start | bytes 786440 | tf_op jit(solution)/shard_map/ppermute | solution.py:304
  20.3 6.4 %collective-permute-start.7 = (bf16[16,8192]{1,0:T(8,128)(2,1)S(1)}, bf16[16,8192]{1,0:T(8,128)(2,1)S(1)}, u32[]{:S(2)}, u32[]{:S(2)}) collective-permute-start(bf16[16,8192]{1,0:T(8,128)(2,1)S(1)} %collective-permute-done.5.refs_6_), channel_id=1, source_target_pairs={{0,4},{1,3},{4,8},{5,1},{8,12},{9,5},{12,14},{13,9},{14,10},{15,13... | collective-permute-start | bytes 786440 | tf_op jit(solution)/shard_map/ppermute | solution.py:304
  22.4 4.3 %collective-permute-start.10 = (bf16[16,8192]{1,0:T(8,128)(2,1)S(1)}, bf16[16,8192]{1,0:T(8,128)(2,1)S(1)}, u32[]{:S(2)}, u32[]{:S(2)}) collective-permute-start(bf16[16,8192]{1,0:T(8,128)(2,1)S(1)} %collective-permute-done.3.refs_4_), channel_id=1, source_target_pairs={{0,1},{1,0},{2,3},{3,2},{4,5},{5,4},{6,7},{7,6},{8,9},{9,8},{10,11... | collective-permute-start | bytes 786440 | tf_op jit(solution)/shard_map/ppermute | solution.py:307
  22.4 4.3 %collective-permute-start.11 = (bf16[16,8192]{1,0:T(8,128)(2,1)S(1)}, bf16[16,8192]{1,0:T(8,128)(2,1)S(1)}, u32[]{:S(2)}, u32[]{:S(2)}) collective-permute-start(bf16[16,8192]{1,0:T(8,128)(2,1)S(1)} %collective-permute-done.4.refs_5_), channel_id=1, source_target_pairs={{0,1},{1,0},{2,3},{3,2},{4,5},{5,4},{6,7},{7,6},{8,9},{9,8},{10,11... | collective-permute-start | bytes 786440 | tf_op jit(solution)/shard_map/ppermute | solution.py:307
  22.9 3.8 %collective-permute-start.12 = (bf16[16,8192]{1,0:T(8,128)(2,1)S(1)}, bf16[16,8192]{1,0:T(8,128)(2,1)S(1)}, u32[]{:S(2)}, u32[]{:S(2)}) collective-permute-start(bf16[16,8192]{1,0:T(8,128)(2,1)S(1)} %collective-permute-done.5.refs_6_), channel_id=1, source_target_pairs={{0,1},{1,0},{2,3},{3,2},{4,5},{5,4},{6,7},{7,6},{8,9},{9,8},{10,11... | collective-permute-start | bytes 786440 | tf_op jit(solution)/shard_map/ppermute | solution.py:307
  23.3 3.5 %collective-permute-start.13 = (bf16[16,8192]{1,0:T(8,128)(2,1)S(1)}, bf16[16,8192]{1,0:T(8,128)(2,1)S(1)}, u32[]{:S(2)}, u32[]{:S(2)}) collective-permute-start(bf16[16,8192]{1,0:T(8,128)(2,1)S(1)} %collective-permute-done.6.refs_7_), channel_id=1, source_target_pairs={{0,1},{1,0},{2,3},{3,2},{4,5},{5,4},{6,7},{7,6},{8,9},{9,8},{10,11... | collective-permute-start | bytes 786440 | tf_op jit(solution)/shard_map/ppermute | solution.py:307
  26.7 1.5 %collective-permute-start.14 = (bf16[16,8192]{1,0:T(8,128)(2,1)S(1)}, bf16[16,8192]{1,0:T(8,128)(2,1)S(1)}, u32[]{:S(2)}, u32[]{:S(2)}) collective-permute-start(bf16[16,8192]{1,0:T(8,128)(2,1)S(1)} %collective-permute-done.7.refs_8_), channel_id=1, source_target_pairs={{0,1},{1,0},{2,3},{3,2},{4,5},{5,4},{6,7},{7,6},{8,9},{9,8},{10,11... | collective-permute-start | bytes 786440 | tf_op jit(solution)/shard_map/ppermute | solution.py:307
  28.2 2.0 %copy-start.4 = (bf16[16,8192]{1,0:T(8,128)(2,1)}, bf16[16,8192]{1,0:T(8,128)(2,1)S(1)}, u32[]{:S(2)}) copy-start(bf16[16,8192]{1,0:T(8,128)(2,1)S(1)} %collective-permute-done.14.refs_15_) | copy-start | bytes 786436
  30.2 0.7 copy-start.2
  31.6 28.0 %all-to-all-start = ((bf16[16,8,256]{2,1,0:T(8,128)(2,1)}), bf16[16,8,256]{2,1,0:T(8,128)(2,1)S(1)}, u32[]{:S(2)}, u32[]{:S(2)}) async-start(bf16[16,8,256]{2,1,0:T(8,128)(2,1)} %broadcast_in_dim.2), calls=%async_computation | async-start | bytes 131072 | tf_op jit(solution)/shard_map/all_to_all | solution.py:323
  38.2 5.2 %copy-start = (bf16[8192,896]{1,0:T(8,128)(2,1)S(1)}, bf16[8192,896]{1,0:T(8,128)(2,1)}, u32[]{:S(2)}) copy-start(bf16[8192,896]{1,0:T(8,128)(2,1)} %w_ref.8) | copy-start | bytes 44040196
  43.4 0.9 copy-start.3
  44.4 0.9 copy-start.5
  45.3 0.9 copy-start.7
  46.3 6.6 %slice-start = ((s8[14680064]{0:T(1024)(128)(4,1)}), s8[4194304]{0:T(1024)(128)(4,1)S(1)}, s32[]{:S(2)}) async-start(s8[14680064]{0:T(1024)(128)(4,1)} %bitcast.2), calls=%async_computation.1 | async-start | bytes 8388608
  46.3 6.6 %slice-start.1 = ((s8[14680064]{0:T(1024)(128)(4,1)}), s8[4194304]{0:T(1024)(128)(4,1)S(1)}, s32[]{:S(2)}) async-start(s8[14680064]{0:T(1024)(128)(4,1)} %bitcast.2), calls=%async_computation.2 | async-start | bytes 8388608
  46.3 6.6 %slice-start.2 = ((s8[14680064]{0:T(1024)(128)(4,1)}), s8[4194304]{0:T(1024)(128)(4,1)S(1)}, s32[]{:S(2)}) async-start(s8[14680064]{0:T(1024)(128)(4,1)} %bitcast.2), calls=%async_computation.3 | async-start | bytes 8388608
  48.7 0.9 copy-start.8
  49.6 3.3 %slice-start.3 = ((s8[14680064]{0:T(1024)(128)(4,1)}), s8[2097152]{0:T(1024)(128)(4,1)S(1)}, s32[]{:S(2)}) async-start(s8[14680064]{0:T(1024)(128)(4,1)} %bitcast.2), calls=%async_computation.4 | async-start | bytes 4194304
  52.0 0.9 copy-start.10
  55.3 0.9 copy-start.12
  58.6 0.9 copy-start.14
  59.6 1.2 %copy-start.9 = (f32[256,896]{1,0:T(8,128)S(1)}, f32[256,896]{1,0:T(8,128)}, u32[]{:S(2)}) copy-start(f32[256,896]{1,0:T(8,128)} %copy-done.8) | copy-start | bytes 2752516
  60.8 1.2 %copy-start.11 = (f32[256,896]{1,0:T(8,128)S(1)}, f32[256,896]{1,0:T(8,128)}, u32[]{:S(2)}) copy-start(f32[256,896]{1,0:T(8,128)} %copy-done.10) | copy-start | bytes 2752516
  61.9 1.2 %copy-start.13 = (f32[256,896]{1,0:T(8,128)S(1)}, f32[256,896]{1,0:T(8,128)}, u32[]{:S(2)}) copy-start(f32[256,896]{1,0:T(8,128)} %copy-done.12) | copy-start | bytes 2752516
  63.1 1.2 %copy-start.15 = (f32[256,896]{1,0:T(8,128)S(1)}, f32[256,896]{1,0:T(8,128)}, u32[]{:S(2)}) copy-start(f32[256,896]{1,0:T(8,128)} %copy-done.14) | copy-start | bytes 2752516
  64.3 1.5 %copy-start.16 = (bf16[8,128,896]{2,1,0:T(8,128)(2,1)S(1)}, bf16[8,128,896]{2,1,0:T(8,128)(2,1)}, u32[]{:S(2)}) copy-start(bf16[8,128,896]{2,1,0:T(8,128)(2,1)} %expand_ref.1) | copy-start | bytes 5505028
  65.8 39.5 %copy-start.19 = (s32[2]{0:T(128)S(1)}, s32[2]{0:T(128)}, u32[]{:S(2)}) copy-start(s32[2]{0:T(128)} %counts_ref.1) | copy-start | bytes 28
  67.0 5.2 %copy-start.1 = (bf16[896,8192]{1,0:T(8,128)(2,1)S(1)}, bf16[896,8192]{1,0:T(8,128)(2,1)}, u32[]{:S(2)}) copy-start(bf16[896,8192]{1,0:T(8,128)(2,1)} %w_ref.9) | copy-start | bytes 44040196
  76.9 4.2 %collective-permute-start.18 = (bf16[32,8192]{1,0:T(8,128)(2,1)S(1)}, bf16[32,8192]{1,0:T(8,128)(2,1)S(1)}, u32[]{:S(2)}, u32[]{:S(2)}) collective-permute-start(bf16[32,8192]{1,0:T(8,128)(2,1)S(1)} %get-tuple-element.29), channel_id=1, source_target_pairs={{0,1},{1,0},{2,3},{3,2},{4,5},{5,4},{6,7},{7,6},{8,9},{9,8},{10,11... | collective-permute-start | bytes 1572872 | tf_op jit(solution)/shard_map/ppermute | solution.py:307
  77.2 2.0 %collective-permute-start.19 = (bf16[16,8192]{1,0:T(8,128)(2,1)S(1)}, bf16[16,8192]{1,0:T(8,128)(2,1)S(1)}, u32[]{:S(2)}, u32[]{:S(2)}) collective-permute-start(bf16[16,8192]{1,0:T(8,128)(2,1)S(1)} %get-tuple-element.31), channel_id=1, source_target_pairs={{0,1},{1,0},{2,3},{3,2},{4,5},{5,4},{6,7},{7,6},{8,9},{9,8},{10,11... | collective-permute-start | bytes 786440 | tf_op jit(solution)/shard_map/ppermute | solution.py:307
  77.4 10.2 %collective-permute-start.17 = (bf16[32,8192]{1,0:T(8,128)(2,1)S(1)}, bf16[32,8192]{1,0:T(8,128)(2,1)S(1)}, u32[]{:S(2)}, u32[]{:S(2)}) collective-permute-start(bf16[32,8192]{1,0:T(8,128)(2,1)S(1)} %get-tuple-element.27), channel_id=1, source_target_pairs={{0,1},{1,0},{2,3},{3,2},{4,5},{5,4},{6,7},{7,6},{8,9},{9,8},{10,11... | collective-permute-start | bytes 1572872 | tf_op jit(solution)/shard_map/ppermute | solution.py:307
  79.3 6.4 %collective-permute-start.20 = (bf16[16,8192]{1,0:T(8,128)(2,1)S(1)}, bf16[16,8192]{1,0:T(8,128)(2,1)S(1)}, u32[]{:S(2)}, u32[]{:S(2)}) collective-permute-start(bf16[16,8192]{1,0:T(8,128)(2,1)S(1)} %added.7), channel_id=1, source_target_pairs={{0,4},{1,3},{4,8},{5,1},{8,12},{9,5},{12,14},{13,9},{14,10},{15,13... | collective-permute-start | bytes 786440 | tf_op jit(solution)/shard_map/ppermute | solution.py:304
  81.2 7.4 %collective-permute-start.24 = (bf16[16,8192]{1,0:T(8,128)(2,1)S(1)}, bf16[16,8192]{1,0:T(8,128)(2,1)S(1)}, u32[]{:S(2)}, u32[]{:S(2)}) collective-permute-start(bf16[16,8192]{1,0:T(8,128)(2,1)S(1)} %added.11), channel_id=1, source_target_pairs={{0,4},{1,3},{4,8},{5,1},{8,12},{9,5},{12,14},{13,9},{14,10},{15,13... | collective-permute-start | bytes 786440 | tf_op jit(solution)/shard_map/ppermute | solution.py:304
  82.7 11.5 %collective-permute-start.16 = (bf16[32,8192]{1,0:T(8,128)(2,1)S(1)}, bf16[32,8192]{1,0:T(8,128)(2,1)S(1)}, u32[]{:S(2)}, u32[]{:S(2)}) collective-permute-start(bf16[32,8192]{1,0:T(8,128)(2,1)S(1)} %get-tuple-element.25), channel_id=1, source_target_pairs={{0,1},{1,0},{2,3},{3,2},{4,5},{5,4},{6,7},{7,6},{8,9},{9,8},{10,11... | collective-permute-start | bytes 1572872 | tf_op jit(solution)/shard_map/ppermute | solution.py:307
  85.8 6.4 %collective-permute-start.21 = (bf16[16,8192]{1,0:T(8,128)(2,1)S(1)}, bf16[16,8192]{1,0:T(8,128)(2,1)S(1)}, u32[]{:S(2)}, u32[]{:S(2)}) collective-permute-start(bf16[16,8192]{1,0:T(8,128)(2,1)S(1)} %added.8), channel_id=1, source_target_pairs={{0,4},{1,3},{4,8},{5,1},{8,12},{9,5},{12,14},{13,9},{14,10},{15,13... | collective-permute-start | bytes 786440 | tf_op jit(solution)/shard_map/ppermute | solution.py:304
  88.6 6.4 %collective-permute-start.25 = (bf16[16,8192]{1,0:T(8,128)(2,1)S(1)}, bf16[16,8192]{1,0:T(8,128)(2,1)S(1)}, u32[]{:S(2)}, u32[]{:S(2)}) collective-permute-start(bf16[16,8192]{1,0:T(8,128)(2,1)S(1)} %added.12), channel_id=1, source_target_pairs={{0,4},{1,3},{4,8},{5,1},{8,12},{9,5},{12,14},{13,9},{14,10},{15,13... | collective-permute-start | bytes 786440 | tf_op jit(solution)/shard_map/ppermute | solution.py:304
  92.3 6.4 %collective-permute-start.22 = (bf16[16,8192]{1,0:T(8,128)(2,1)S(1)}, bf16[16,8192]{1,0:T(8,128)(2,1)S(1)}, u32[]{:S(2)}, u32[]{:S(2)}) collective-permute-start(bf16[16,8192]{1,0:T(8,128)(2,1)S(1)} %added.9), channel_id=1, source_target_pairs={{0,4},{1,3},{4,8},{5,1},{8,12},{9,5},{12,14},{13,9},{14,10},{15,13... | collective-permute-start | bytes 786440 | tf_op jit(solution)/shard_map/ppermute | solution.py:304
  95.1 6.4 %collective-permute-start.26 = (bf16[16,8192]{1,0:T(8,128)(2,1)S(1)}, bf16[16,8192]{1,0:T(8,128)(2,1)S(1)}, u32[]{:S(2)}, u32[]{:S(2)}) collective-permute-start(bf16[16,8192]{1,0:T(8,128)(2,1)S(1)} %added.13), channel_id=1, source_target_pairs={{0,4},{1,3},{4,8},{5,1},{8,12},{9,5},{12,14},{13,9},{14,10},{15,13... | collective-permute-start | bytes 786440 | tf_op jit(solution)/shard_map/ppermute | solution.py:304
  96.9 4.6 %collective-permute-start.15 = (bf16[16,8192]{1,0:T(8,128)(2,1)S(1)}, bf16[16,8192]{1,0:T(8,128)(2,1)S(1)}, u32[]{:S(2)}, u32[]{:S(2)}) collective-permute-start(bf16[16,8192]{1,0:T(8,128)(2,1)S(1)} %get-tuple-element.23), channel_id=1, source_target_pairs={{0,1},{1,0},{2,3},{3,2},{4,5},{5,4},{6,7},{7,6},{8,9},{9,8},{10,11... | collective-permute-start | bytes 786440 | tf_op jit(solution)/shard_map/ppermute | solution.py:307
  98.9 6.4 %collective-permute-start.23 = (bf16[16,8192]{1,0:T(8,128)(2,1)S(1)}, bf16[16,8192]{1,0:T(8,128)(2,1)S(1)}, u32[]{:S(2)}, u32[]{:S(2)}) collective-permute-start(bf16[16,8192]{1,0:T(8,128)(2,1)S(1)} %added.10), channel_id=1, source_target_pairs={{0,4},{1,3},{4,8},{5,1},{8,12},{9,5},{12,14},{13,9},{14,10},{15,13... | collective-permute-start | bytes 786440 | tf_op jit(solution)/shard_map/ppermute | solution.py:304
  101.6 3.7 %collective-permute-start.27 = (bf16[16,8192]{1,0:T(8,128)(2,1)S(1)}, bf16[16,8192]{1,0:T(8,128)(2,1)S(1)}, u32[]{:S(2)}, u32[]{:S(2)}) collective-permute-start(bf16[16,8192]{1,0:T(8,128)(2,1)S(1)} %collective-permute-done.26), channel_id=1, source_target_pairs={{0,1},{1,0},{2,3},{3,2},{4,5},{5,4},{6,7},{7,6},{8,9},{9,8},{10,11... | collective-permute-start | bytes 786440 | tf_op jit(solution)/shard_map/ppermute | solution.py:307

commit v7 on v6

--- a/solution.py
+++ b/solution.py
@@ -80,12 +80,17 @@
     return [pl.BlockSpec(memory_space=pltpu.VMEM)] * count
 
 
-SCALARS = pl.BlockSpec(memory_space=pltpu.SMEM)
 FAR = pl.BlockSpec(memory_space=pl.ANY)
 
 
 def far(x):
     return pltpu.with_memory_space_constraint(x, pltpu.HBM)
+
+
+def picked(ref, index):
+    row = ref[...]
+    spots = lax.broadcasted_iota(jnp.int32, row.shape, 1)
+    return jnp.sum(jnp.where(spots == index, row, 0))
 
 
 def anchor_kernel(tokens_ref, passed_in, own_ref, passed_out, sem):
@@ -116,7 +121,7 @@
     block_rows = members * rows // blocks
     places = arrivals(lax.axis_index("tp"), members, rows)
     lhs = jnp.concatenate([piece[...] for piece in pieces], axis=0)
-    weights = jnp.concatenate([shrink_ref[ids_ref[b]] for b in range(blocks)], axis=0)
+    weights = jnp.concatenate([shrink_ref[picked(ids_ref, b)] for b in range(blocks)], axis=0)
     found = lax.dot_general(
         lhs, weights, (((1,), (1,)), ((), ())), preferred_element_type=F32
     )
@@ -131,11 +136,11 @@
 
 def rank_of(adapters, pieces, shrink):
     rows, model = pieces[0].shape
-    blocks, span = adapters.shape[0], shrink.shape[1]
+    blocks, span = adapters.shape[1], shrink.shape[1]
     total = rows * len(pieces)
     return pl.pallas_call(
         functools.partial(rank_kernel, blocks),
-        in_specs=[SCALARS] + whole(1 + len(pieces)),
+        in_specs=whole(2 + len(pieces)),
         out_specs=whole(1)[0],
         out_shape=jax.ShapeDtypeStruct((span, total), BF16),
         scratch_shapes=[pltpu.VMEM((total, 128), F32)],
@@ -175,14 +180,20 @@
     )(matrix, *pieces, after)
 
 
-def finish_kernel(blocks, ids_ref, gate_a, gate_b, up_a, up_b, rank_ref, expand_ref, hidden_ref):
+def finish_kernel(blocks, span, ids_ref, gate_a, gate_b, up_a, up_b, rank_ref, expand_ref, hidden_ref):
     ranks = rank_ref.shape[0]
-    rank = rank_ref[...].astype(F32).T.astype(BF16)
+    device = lax.axis_index("tp")
+    shape = (ranks, ranks)
+    want = lax.broadcasted_iota(jnp.int32, shape, 0)
+    have = lax.broadcasted_iota(jnp.int32, shape, 1)
+    origin = ((have // span) ^ device) * span + have % span
+    order = jnp.where(want == origin, 1.0, 0.0).astype(BF16)
+    rank = jnp.dot(order, rank_ref[...], preferred_element_type=F32).T.astype(BF16)
     half = ranks // 2
     rows = hidden_ref.shape[0] // blocks
     for b in range(blocks):
         part = slice(b * rows, (b + 1) * rows)
-        expand = expand_ref[ids_ref[b]]
+        expand = expand_ref[picked(ids_ref, b)]
         gate = jnp.dot(rank[part, :half], expand[:half], preferred_element_type=F32)
         up = jnp.dot(rank[part, half:], expand[half:], preferred_element_type=F32)
         gate += gate_a[part] + gate_b[part]
@@ -190,11 +201,11 @@
         hidden_ref[part] = (gate / (1.0 + jnp.exp(-gate)) * up).astype(BF16)
 
 
-def finish(adapters, products, rank, expand):
+def finish(adapters, products, rank, expand, span):
     total, width = products[0].shape
     return pl.pallas_call(
-        functools.partial(finish_kernel, adapters.shape[0]),
-        in_specs=[SCALARS] + whole(6),
+        functools.partial(finish_kernel, adapters.shape[1], span),
+        in_specs=whole(7),
         out_specs=whole(1)[0],
         out_shape=jax.ShapeDtypeStruct((total, width), BF16),
         compiler_params=params(),
@@ -202,13 +213,14 @@
     )(adapters, *products, rank, expand)
 
 
-def down_kernel(members, groups, rows, size, w_ref, hidden_ref, *refs):
+def down_kernel(members, groups, rows, first, size, w_ref, hidden_ref, *refs):
     outs, product_ref = refs[:-1], refs[-1]
     places = departures(lax.axis_index("tp"), members, rows)
     hidden = hidden_ref[...]
-    for start in range(0, w_ref.shape[1], size):
+    for start in range(0, outs[0].shape[1], size):
         columns = slice(start, start + size)
-        part = jnp.dot(hidden, w_ref[:, columns], preferred_element_type=F32)
+        weights = w_ref[:, first + start : first + start + size]
+        part = jnp.dot(hidden, weights, preferred_element_type=F32)
         product_ref[...] = part.astype(BF16)
         at = 0
         for out, group in zip(outs, groups, strict=True):
@@ -219,12 +231,12 @@
                 at += 1
 
 
-def down(hidden, down_matrix, groups, rows):
+def down(hidden, down_matrix, groups, rows, part, parts):
     total, depth = hidden.shape
-    columns = down_matrix.shape[1]
+    columns = down_matrix.shape[1] // parts
     size = min(1024, columns)
     return pl.pallas_call(
-        functools.partial(down_kernel, total // rows, groups, rows, size),
+        functools.partial(down_kernel, total // rows, groups, rows, part * columns, size),
         in_specs=whole(2),
         out_specs=whole(len(groups)),
         out_shape=[jax.ShapeDtypeStruct((group * rows, columns), BF16) for group in groups],
@@ -237,25 +249,32 @@
     )(down_matrix, hidden)
 
 
-def last_kernel(blocks, members, counts_ref, *refs):
-    out_ref = refs[-1]
+def last_kernel(blocks, members, parts, counts_ref, *refs):
+    terms, out_ref = refs[:-1], refs[-1]
     rows = out_ref.shape[0]
-    summed = refs[0][...].astype(F32)
-    for ref in refs[1:-1]:
-        summed += ref[...].astype(F32)
     first = lax.axis_index("tp") * rows
     block_rows = members * rows // blocks
-    live = counts_ref[first // block_rows] - first % block_rows
-    row = lax.broadcasted_iota(jnp.int32, summed.shape, 0)
-    out_ref[...] = jnp.where(row < live, summed, 0.0).astype(BF16)
-
-
-def last(members, counts, terms):
-    return pl.pallas_call(
-        functools.partial(last_kernel, counts.shape[0], members),
-        in_specs=[SCALARS] + whole(len(terms)),
-        out_specs=whole(1)[0],
-        out_shape=jax.ShapeDtypeStruct(terms[0].shape, BF16),
+    live = picked(counts_ref, first // block_rows) - first % block_rows
+    each = len(terms) // parts
+    columns = out_ref.shape[1] // parts
+    for part in range(parts):
+        summed = 0.0
+        for term in terms[part * each : (part + 1) * each]:
+            summed += term[...].astype(F32)
+        row = lax.broadcasted_iota(jnp.int32, summed.shape, 0)
+        out_ref[:, part * columns : (part + 1) * columns] = jnp.where(
+            row < live, summed, 0.0
+        ).astype(BF16)
+
+
+def last(members, counts, halves):
+    terms = [term for half in halves for term in half]
+    rows, columns = terms[0].shape
+    return pl.pallas_call(
+        functools.partial(last_kernel, counts.shape[1], members, len(halves)),
+        in_specs=whole(1 + len(terms)),
+        out_specs=whole(1)[0],
+        out_shape=jax.ShapeDtypeStruct((rows, columns * len(halves)), BF16),
         compiler_params=params(),
         name="last",
     )(counts, *terms)
@@ -319,29 +338,36 @@
             theirs.append(cross(second))
     pieces = pieces + mine + theirs
 
-    rank = rank_of(adapter_per_block, pieces, jnp.swapaxes(shrink_matrices, 1, 2))
-    everyone = lax.all_to_all(
-        jnp.broadcast_to(rank[None], (members,) + rank.shape), "tp", 0, 0, tiled=True
-    ).reshape(members * span, -1)
-    products = [
-        product(pieces, matrix, part, 2, rank)
-        for matrix in (gate_matrix, up_matrix)
-        for part in range(2)
-    ]
-    hidden = finish(adapter_per_block, products, everyone, expand_matrices)
+    adapters, counts = adapter_per_block[None], block_token_count[None]
+    rank = rank_of(adapters, pieces, jnp.swapaxes(shrink_matrices, 1, 2))
+    work = [(gate_matrix, 0), (gate_matrix, 1), (up_matrix, 0), (up_matrix, 1)]
+    products, after = [], rank
+    bit = 1
+    while bit < members or work:
+        if work:
+            matrix, part = work.pop(0)
+            products.append(product(pieces, matrix, part, 2, after))
+        if bit < members:
+            after = cross(rank, bit)
+            rank = jnp.concatenate([rank, after], axis=0)
+            bit *= 2
+    hidden = finish(adapters, products, rank, expand_matrices, span)
 
     slots = 2 * reach
     groups = [1] * slots + [1] + [2] * (reach - 1) + [1]
-    outs = down(hidden, down_matrix, groups, rows)
-    keep, give = outs[:slots], outs[slots:]
-    came = [cross(x) for x in give]
-    first = step(added(rows, (0, keep[0]), (0, came[0])))
-    second = None
-    for index in range(1, reach):
-        more = [] if second is None else [(0, second)]
-        second = step(added(rows, (0, keep[2 * index]), (rows, came[index]), *more))
-        first = step(added(rows, (0, keep[2 * index - 1]), (0, came[index]), (0, first)))
-    return last(members, block_token_count, [keep[-1], came[-1], first, cross(second)])
+    halves = []
+    for part in range(2):
+        outs = down(hidden, down_matrix, groups, rows, part, 2)
+        keep, give = outs[:slots], outs[slots:]
+        came = [cross(x) for x in give]
+        first = step(added(rows, (0, keep[0]), (0, came[0])))
+        second = None
+        for index in range(1, reach):
+            more = [] if second is None else [(0, second)]
+            second = step(added(rows, (0, keep[2 * index]), (rows, came[index]), *more))
+            first = step(added(rows, (0, keep[2 * index - 1]), (0, came[index]), (0, first)))
+        halves.append([keep[-1], came[-1], first, cross(second)])
+    return last(members, counts, halves)
 
 
 def solution(mesh):

time: 107 us -> 82.2 us (0.77)
  local copies, waits for them, and re-layouts: 24.5 us -> 0.09 us
  starting transfers between devices: 36 us -> 46.4 us
  waiting for transfers between devices: 25.6 us -> 15.7 us
    unnamed x48 -> x30, local copies, waits for them, and re-layouts: 23.9 us -> 0.08 us
    ppermute x14 -> x21, waiting for transfers between devices: 22.5 us -> 13.1 us  [step(): return lax.ppermute(x, 'tp', ring)]
    ppermute x14 -> x21, starting transfers between devices: 26.8 us -> 35.9 us  [step(): return lax.ppermute(x, 'tp', ring)]
    ppermute x14 -> x24, starting transfers between devices: 2.55 us -> 10.5 us  [cross(): return lax.ppermute(x, 'tp', crossing(members, bit))]
    all_to_all x1 -> x0, starting transfers between devices: 6.63 us -> none  [per_device(): lax.all_to_all(jnp.broadcast_to(rank[None], (members,) + rank.shape), 'tp...]
    pallas_call x3, Pallas kernels: 4.62 us -> 3.28 us  [the longest x1 1.58 us: rank_of(): pl.pallas_call(functools.partial(rank_kernel, blocks), in_specs=whole(2 +...]
    ppermute x14 -> x24, waiting for transfers between devices: 3.07 us -> 2.6 us  [cross(): return lax.ppermute(x, 'tp', crossing(members, bit))]
    pallas_call x1 -> x2, Pallas kernels: 4.63 us -> 5.01 us  [down(): pl.pallas_call(functools.partial(down_kernel, total // rows, groups, rows...]
  transfers between devices with their start and end apart: 29 -> 45, of which waited for: 16 -> 15; matrix products, arithmetic and copies ran while one was open for 0% -> 0% of each run, Pallas kernels for 10% -> 17%
where the time goes in v7:
time: 82.2 us; the launch traced here: 82.1 us
  starting transfers between devices  46.4 us (56%)
  Pallas kernels  19.5 us (24%)
  waiting for transfers between devices  15.7 us (19%)
    ppermute x21, starting transfers between devices, step(): return lax.ppermute(x, 'tp', ring)  35.9 us
    ppermute x21, waiting for transfers between devices, step(): return lax.ppermute(x, 'tp', ring)  13.1 us
    ppermute x24, starting transfers between devices, cross(): return lax.ppermute(x, 'tp', crossing(members, bit))  10.5 us
    pallas_call x4, Pallas kernels, product(): pl.pallas_call(functools.partial(product_kernel, part * depth), in_specs=...  9.43 us
    pallas_call x2, Pallas kernels, down(): pl.pallas_call(functools.partial(down_kernel, total // rows, groups, rows...  5.01 us
    ppermute x24, waiting for transfers between devices, cross(): return lax.ppermute(x, 'tp', crossing(members, bit))  2.6 us
  transfers between devices with their start and end apart: 45, of which 15 were waited for; matrix products, arithmetic and copies ran while one was open for 0% of the time, Pallas kernels for 17%

profile of v7, /device:TPU:0, one launch (start us, length us, event | category | flops | bytes accessed | tf_op | source)
XLA Modules:
  0.0 82.1 jit_solution(4078408917144643652)
XLA Ops:
  0.0 0.5 collective-permute-start
  0.5 2.6 %collective-permute-start.1 = (bf16[16,8192]{1,0:T(8,128)(2,1)}, bf16[16,8192]{1,0:T(8,128)(2,1)S(1)}, u32[]{:S(2)}, u32[]{:S(2)}) collective-permute-start(bf16[16,8192]{1,0:T(8,128)(2,1)} %tokens_ref.1), channel_id=1, source_target_pairs={{0,4},{1,3},{4,8},{5,1},{8,12},{9,5},{12,14},{13,9},{14,10},{15,13... | collective-permute-start | bytes 786440 | tf_op jit(solution)/shard_map/ppermute | solution.py:323
  3.1 1.1 %anchor.1 = (bf16[16,8192]{1,0:T(8,128)(2,1)S(1)}, bf16[16,8192]{1,0:T(8,128)(2,1)S(1)}) custom-call(bf16[16,8192]{1,0:T(8,128)(2,1)} %tokens_ref.1, bf16[16,8192]{1,0:T(8,128)(2,1)S(1)} %collective-permute-done.passed_in), custom_call_target="tpu_custom_call", output_to_operand_aliasing={{1}: (1, {})} | custom-call | flops 30000001024 | tf_op jit(solution)/shard_map/anchor/pallas_call | solution.py:103
  4.2 1.7 %collective-permute-start.2 = (bf16[16,8192]{1,0:T(8,128)(2,1)S(1)}, bf16[16,8192]{1,0:T(8,128)(2,1)S(1)}, u32[]{:S(2)}, u32[]{:S(2)}) collective-permute-start(bf16[16,8192]{1,0:T(8,128)(2,1)S(1)} %get-tuple-element.34.refs_1_), channel_id=1, source_target_pairs={{0,4},{1,3},{4,8},{5,1},{8,12},{9,5},{12,14},{13,9},{14,10},{15,13... | collective-permute-start | bytes 786440 | tf_op jit(solution)/shard_map/ppermute | solution.py:323
  5.9 1.6 %collective-permute-done.1.refs_2_ = bf16[16,8192]{1,0:T(8,128)(2,1)S(1)} collective-permute-done((bf16[16,8192]{1,0:T(8,128)(2,1)}, bf16[16,8192]{1,0:T(8,128)(2,1)S(1)}, u32[]{:S(2)}, u32[]{:S(2)}) %collective-permute-start.1) | collective-permute-done | bytes 262176 | tf_op jit(solution)/shard_map/ppermute | solution.py:323
  7.6 2.1 %collective-permute-start.3 = (bf16[16,8192]{1,0:T(8,128)(2,1)S(1)}, bf16[16,8192]{1,0:T(8,128)(2,1)S(1)}, u32[]{:S(2)}, u32[]{:S(2)}) collective-permute-start(bf16[16,8192]{1,0:T(8,128)(2,1)S(1)} %collective-permute-done.1.refs_2_), channel_id=1, source_target_pairs={{0,4},{1,3},{4,8},{5,1},{8,12},{9,5},{12,14},{13,9},{14,10},{15,13... | collective-permute-start | bytes 786440 | tf_op jit(solution)/shard_map/ppermute | solution.py:323
  9.7 1.0 %collective-permute-done.2.refs_3_ = bf16[16,8192]{1,0:T(8,128)(2,1)S(1)} collective-permute-done((bf16[16,8192]{1,0:T(8,128)(2,1)S(1)}, bf16[16,8192]{1,0:T(8,128)(2,1)S(1)}, u32[]{:S(2)}, u32[]{:S(2)}) %collective-permute-start.2) | collective-permute-done | bytes 262176 | tf_op jit(solution)/shard_map/ppermute | solution.py:323
  10.6 1.8 %collective-permute-start.4 = (bf16[16,8192]{1,0:T(8,128)(2,1)S(1)}, bf16[16,8192]{1,0:T(8,128)(2,1)S(1)}, u32[]{:S(2)}, u32[]{:S(2)}) collective-permute-start(bf16[16,8192]{1,0:T(8,128)(2,1)S(1)} %collective-permute-done.2.refs_3_), channel_id=1, source_target_pairs={{0,4},{1,3},{4,8},{5,1},{8,12},{9,5},{12,14},{13,9},{14,10},{15,13... | collective-permute-start | bytes 786440 | tf_op jit(solution)/shard_map/ppermute | solution.py:323
  12.5 1.5 %collective-permute-done.3.refs_4_ = bf16[16,8192]{1,0:T(8,128)(2,1)S(1)} collective-permute-done((bf16[16,8192]{1,0:T(8,128)(2,1)S(1)}, bf16[16,8192]{1,0:T(8,128)(2,1)S(1)}, u32[]{:S(2)}, u32[]{:S(2)}) %collective-permute-start.3) | collective-permute-done | bytes 262176 | tf_op jit(solution)/shard_map/ppermute | solution.py:323
  14.0 2.1 %collective-permute-start.5 = (bf16[16,8192]{1,0:T(8,128)(2,1)S(1)}, bf16[16,8192]{1,0:T(8,128)(2,1)S(1)}, u32[]{:S(2)}, u32[]{:S(2)}) collective-permute-start(bf16[16,8192]{1,0:T(8,128)(2,1)S(1)} %collective-permute-done.3.refs_4_), channel_id=1, source_target_pairs={{0,4},{1,3},{4,8},{5,1},{8,12},{9,5},{12,14},{13,9},{14,10},{15,13... | collective-permute-start | bytes 786440 | tf_op jit(solution)/shard_map/ppermute | solution.py:323
  16.0 0.5 collective-permute-start.9
  16.6 0.5 collective-permute-done.4.refs_5_
  17.0 1.8 %collective-permute-start.6 = (bf16[16,8192]{1,0:T(8,128)(2,1)S(1)}, bf16[16,8192]{1,0:T(8,128)(2,1)S(1)}, u32[]{:S(2)}, u32[]{:S(2)}) collective-permute-start(bf16[16,8192]{1,0:T(8,128)(2,1)S(1)} %collective-permute-done.4.refs_5_), channel_id=1, source_target_pairs={{0,4},{1,3},{4,8},{5,1},{8,12},{9,5},{12,14},{13,9},{14,10},{15,13... | collective-permute-start | bytes 786440 | tf_op jit(solution)/shard_map/ppermute | solution.py:323
  18.9 1.5 %collective-permute-done.5.refs_6_ = bf16[16,8192]{1,0:T(8,128)(2,1)S(1)} collective-permute-done((bf16[16,8192]{1,0:T(8,128)(2,1)S(1)}, bf16[16,8192]{1,0:T(8,128)(2,1)S(1)}, u32[]{:S(2)}, u32[]{:S(2)}) %collective-permute-start.5) | collective-permute-done | bytes 262176 | tf_op jit(solution)/shard_map/ppermute | solution.py:323
  20.3 2.1 %collective-permute-start.7 = (bf16[16,8192]{1,0:T(8,128)(2,1)S(1)}, bf16[16,8192]{1,0:T(8,128)(2,1)S(1)}, u32[]{:S(2)}, u32[]{:S(2)}) collective-permute-start(bf16[16,8192]{1,0:T(8,128)(2,1)S(1)} %collective-permute-done.5.refs_6_), channel_id=1, source_target_pairs={{0,4},{1,3},{4,8},{5,1},{8,12},{9,5},{12,14},{13,9},{14,10},{15,13... | collective-permute-start | bytes 786440 | tf_op jit(solution)/shard_map/ppermute | solution.py:323
  22.4 0.5 collective-permute-start.11
  22.9 0.1 collective-permute-start.12
  23.0 0.4 collective-permute-done.6.refs_7_
  23.4 0.1 collective-permute-start.13
  23.5 3.3 %collective-permute-done.7.refs_8_ = bf16[16,8192]{1,0:T(8,128)(2,1)S(1)} collective-permute-done((bf16[16,8192]{1,0:T(8,128)(2,1)S(1)}, bf16[16,8192]{1,0:T(8,128)(2,1)S(1)}, u32[]{:S(2)}, u32[]{:S(2)}) %collective-permute-start.7) | collective-permute-done | bytes 262176 | tf_op jit(solution)/shard_map/ppermute | solution.py:323
  26.7 1.5 %collective-permute-done.14.refs_15_ = bf16[16,8192]{1,0:T(8,128)(2,1)S(1)} collective-permute-done((bf16[16,8192]{1,0:T(8,128)(2,1)S(1)}, bf16[16,8192]{1,0:T(8,128)(2,1)S(1)}, u32[]{:S(2)}, u32[]{:S(2)}) %collective-permute-start.14) | collective-permute-done | bytes 262176 | tf_op jit(solution)/shard_map/ppermute | solution.py:326
  28.3 1.6 %rank.1.refs_16_ = bf16[8,256]{1,0:T(8,128)(2,1)S(1)} custom-call(s32[1,2]{1,0:T(1,128)S(1)} %bitcast.8, bf16[8,8,8192]{2,1,0:T(8,128)(2,1)S(1)} %bitcast.7, bf16[16,8192]{1,0:T(8,128)(2,1)S(1)} %get-tuple-element.33.refs_0_, bf16[16,8192]{1,0:T(8,128)(2,1)S(1)} %get-tuple-element.34.refs_1_, bf16[16,8192]{1,0:T(8,128)(2,1)S(1)} %collective-permute-done.1.refs_2_, ...), custom_call_target="tpu_custom_call" | custom-call | flops 67108864 | bytes 4194304 | tf_op jit(solution)/shard_map/rank/pallas_call | solution.py:141
  29.8 0.2 collective-permute-start.15
  30.0 2.4 %product.4.gate_a = f32[256,896]{1,0:T(8,128)S(1)} custom-call(bf16[8192,896]{1,0:T(8,128)(2,1)S(1)} %copy-done, bf16[16,8192]{1,0:T(8,128)(2,1)S(1)} %get-tuple-element.33.refs_0_, bf16[16,8192]{1,0:T(8,128)(2,1)S(1)} %get-tuple-element.34.refs_1_, bf16[16,8192]{1,0:T(8,128)(2,1)S(1)} %collective-permute-done.1.refs_2_, ...), custom_call_target="tpu_custom_call" | custom-call | flops 1879048192 | bytes 9437184 | tf_op jit(solution)/shard_map/product/pallas_call | solution.py:172
  32.5 2.1 %collective-permute-start.16 = (bf16[16,256]{1,0:T(8,128)(2,1)S(1)}, bf16[16,256]{1,0:T(8,128)(2,1)S(1)}, u32[]{:S(2)}, u32[]{:S(2)}) collective-permute-start(bf16[16,256]{1,0:T(8,128)(2,1)S(1)} %pad_maximum_fusion.2), channel_id=1, source_target_pairs={{0,2},{1,3},{2,0},{3,1},{4,6},{5,7},{6,4},{7,5},{8,10},{9,11},{10,... | collective-permute-start | bytes 24584 | tf_op jit(solution)/shard_map/ppermute | solution.py:326
  34.6 2.4 %product.5.gate_b = f32[256,896]{1,0:T(8,128)S(1)} custom-call(bf16[8192,896]{1,0:T(8,128)(2,1)S(1)} %copy-done, bf16[16,8192]{1,0:T(8,128)(2,1)S(1)} %get-tuple-element.33.refs_0_, bf16[16,8192]{1,0:T(8,128)(2,1)S(1)} %get-tuple-element.34.refs_1_, bf16[16,8192]{1,0:T(8,128)(2,1)S(1)} %collective-permute-done.1.refs_2_, ...), custom_call_target="tpu_custom_call" | custom-call | flops 1879048192 | bytes 9437184 | tf_op jit(solution)/shard_map/product/pallas_call | solution.py:172
  37.0 1.6 %collective-permute-start.17 = (bf16[32,256]{1,0:T(8,128)(2,1)S(1)}, bf16[32,256]{1,0:T(8,128)(2,1)S(1)}, u32[]{:S(2)}, u32[]{:S(2)}) collective-permute-start(bf16[32,256]{1,0:T(8,128)(2,1)S(1)} %pad_maximum_fusion.1), channel_id=1, source_target_pairs={{0,4},{1,5},{2,6},{3,7},{4,0},{5,1},{6,2},{7,3},{8,12},{9,13},{10,... | collective-permute-start | bytes 49160 | tf_op jit(solution)/shard_map/ppermute | solution.py:326
  38.7 2.3 %product.6.up_a = f32[256,896]{1,0:T(8,128)S(1)} custom-call(bf16[8192,896]{1,0:T(8,128)(2,1)S(1)} %bitcast.4, bf16[16,8192]{1,0:T(8,128)(2,1)S(1)} %get-tuple-element.33.refs_0_, bf16[16,8192]{1,0:T(8,128)(2,1)S(1)} %get-tuple-element.34.refs_1_, bf16[16,8192]{1,0:T(8,128)(2,1)S(1)} %collective-permute-done.1.refs_2_, ...), custom_call_target="tpu_custom_call" | custom-call | flops 1879048192 | bytes 9437184 | tf_op jit(solution)/shard_map/product/pallas_call | solution.py:172
  41.1 2.7 %collective-permute-start.18 = (bf16[64,256]{1,0:T(8,128)(2,1)S(1)}, bf16[64,256]{1,0:T(8,128)(2,1)S(1)}, u32[]{:S(2)}, u32[]{:S(2)}) collective-permute-start(bf16[64,256]{1,0:T(8,128)(2,1)S(1)} %pad_maximum_fusion), channel_id=1, source_target_pairs={{0,8},{1,9},{2,10},{3,11},{4,12},{5,13},{6,14},{7,15},{8,0},{9,1},... | collective-permute-start | bytes 98312 | tf_op jit(solution)/shard_map/ppermute | solution.py:326
  43.7 2.3 %product.7.up_b = f32[256,896]{1,0:T(8,128)S(1)} custom-call(bf16[8192,896]{1,0:T(8,128)(2,1)S(1)} %bitcast.4, bf16[16,8192]{1,0:T(8,128)(2,1)S(1)} %get-tuple-element.33.refs_0_, bf16[16,8192]{1,0:T(8,128)(2,1)S(1)} %get-tuple-element.34.refs_1_, bf16[16,8192]{1,0:T(8,128)(2,1)S(1)} %collective-permute-done.1.refs_2_, ...), custom_call_target="tpu_custom_call" | custom-call | flops 1879048192 | bytes 9437184 | tf_op jit(solution)/shard_map/product/pallas_call | solution.py:172
  46.1 0.7 finish.1.hidden_ref
  46.9 2.4 %down.2 = (bf16[16,4096]{1,0:T(8,128)(2,1)S(1)}, bf16[16,4096]{1,0:T(8,128)(2,1)S(1)}, bf16[16,4096]{1,0:T(8,128)(2,1)S(1)}, bf16[16,4096]{1,0:T(8,128)(2,1)S(1)...) custom-call(bf16[896,8192]{1,0:T(8,128)(2,1)S(1)} %bitcast.6, ...), custom_call_target="tpu_custom_call" | custom-call | flops 1879048192 | bytes 9437184 | tf_op jit(solution)/shard_map/down/pallas_call | solution.py:238
  49.4 0.1 collective-permute-start.22
  49.4 0.5 collective-permute-start.23
  49.9 2.6 %down.3 = (bf16[16,4096]{1,0:T(8,128)(2,1)S(1)}, bf16[16,4096]{1,0:T(8,128)(2,1)S(1)}, bf16[16,4096]{1,0:T(8,128)(2,1)S(1)}, bf16[16,4096]{1,0:T(8,128)(2,1)S(1)...) custom-call(bf16[896,8192]{1,0:T(8,128)(2,1)S(1)} %bitcast.6, ...), custom_call_target="tpu_custom_call" | custom-call | flops 1879048192 | bytes 9437184 | tf_op jit(solution)/shard_map/down/pallas_call | solution.py:238
  52.5 0.1 collective-permute-start.35
  52.7 0.4 collective-permute-start.21
  53.1 0.1 collective-permute-start.36
  53.2 0.4 collective-permute-start.34
  53.7 1.0 %collective-permute-done.36.refs_1_ = bf16[16,4096]{1,0:T(8,128)(2,1)S(1)} collective-permute-done((bf16[16,4096]{1,0:T(8,128)(2,1)S(1)}, bf16[16,4096]{1,0:T(8,128)(2,1)S(1)}, u32[]{:S(2)}, u32[]{:S(2)}) %collective-permute-start.36) | collective-permute-done | bytes 131104 | tf_op jit(solution)/shard_map/ppermute | solution.py:326
  54.7 1.3 %collective-permute-start.24 = (bf16[16,4096]{1,0:T(8,128)(2,1)S(1)}, bf16[16,4096]{1,0:T(8,128)(2,1)S(1)}, u32[]{:S(2)}, u32[]{:S(2)}) collective-permute-start(bf16[16,4096]{1,0:T(8,128)(2,1)S(1)} %added.14), channel_id=1, source_target_pairs={{0,4},{1,3},{4,8},{5,1},{8,12},{9,5},{12,14},{13,9},{14,10},{15,13... | collective-permute-start | bytes 393224 | tf_op jit(solution)/shard_map/ppermute | solution.py:323
  56.0 1.9 %collective-permute-start.37 = (bf16[16,4096]{1,0:T(8,128)(2,1)S(1)}, bf16[16,4096]{1,0:T(8,128)(2,1)S(1)}, u32[]{:S(2)}, u32[]{:S(2)}) collective-permute-start(bf16[16,4096]{1,0:T(8,128)(2,1)S(1)} %added.21), channel_id=1, source_target_pairs={{0,4},{1,3},{4,8},{5,1},{8,12},{9,5},{12,14},{13,9},{14,10},{15,13... | collective-permute-start | bytes 393224 | tf_op jit(solution)/shard_map/ppermute | solution.py:323
  57.9 1.6 %collective-permute-start.28 = (bf16[16,4096]{1,0:T(8,128)(2,1)S(1)}, bf16[16,4096]{1,0:T(8,128)(2,1)S(1)}, u32[]{:S(2)}, u32[]{:S(2)}) collective-permute-start(bf16[16,4096]{1,0:T(8,128)(2,1)S(1)} %added.18), channel_id=1, source_target_pairs={{0,4},{1,3},{4,8},{5,1},{8,12},{9,5},{12,14},{13,9},{14,10},{15,13... | collective-permute-start | bytes 393224 | tf_op jit(solution)/shard_map/ppermute | solution.py:323
  59.6 0.1 collective-permute-start.20
  59.7 1.3 %collective-permute-start.41 = (bf16[16,4096]{1,0:T(8,128)(2,1)S(1)}, bf16[16,4096]{1,0:T(8,128)(2,1)S(1)}, u32[]{:S(2)}, u32[]{:S(2)}) collective-permute-start(bf16[16,4096]{1,0:T(8,128)(2,1)S(1)} %added.25), channel_id=1, source_target_pairs={{0,4},{1,3},{4,8},{5,1},{8,12},{9,5},{12,14},{13,9},{14,10},{15,13... | collective-permute-start | bytes 393224 | tf_op jit(solution)/shard_map/ppermute | solution.py:323
  61.0 0.1 collective-permute-start.33
  61.1 1.9 %collective-permute-start.25 = (bf16[16,4096]{1,0:T(8,128)(2,1)S(1)}, bf16[16,4096]{1,0:T(8,128)(2,1)S(1)}, u32[]{:S(2)}, u32[]{:S(2)}) collective-permute-start(bf16[16,4096]{1,0:T(8,128)(2,1)S(1)} %added.15), channel_id=1, source_target_pairs={{0,4},{1,3},{4,8},{5,1},{8,12},{9,5},{12,14},{13,9},{14,10},{15,13... | collective-permute-start | bytes 393224 | tf_op jit(solution)/shard_map/ppermute | solution.py:323
  63.0 1.6 %collective-permute-start.38 = (bf16[16,4096]{1,0:T(8,128)(2,1)S(1)}, bf16[16,4096]{1,0:T(8,128)(2,1)S(1)}, u32[]{:S(2)}, u32[]{:S(2)}) collective-permute-start(bf16[16,4096]{1,0:T(8,128)(2,1)S(1)} %added.22), channel_id=1, source_target_pairs={{0,4},{1,3},{4,8},{5,1},{8,12},{9,5},{12,14},{13,9},{14,10},{15,13... | collective-permute-start | bytes 393224 | tf_op jit(solution)/shard_map/ppermute | solution.py:323
  64.7 1.3 %collective-permute-start.29 = (bf16[16,4096]{1,0:T(8,128)(2,1)S(1)}, bf16[16,4096]{1,0:T(8,128)(2,1)S(1)}, u32[]{:S(2)}, u32[]{:S(2)}) collective-permute-start(bf16[16,4096]{1,0:T(8,128)(2,1)S(1)} %added.19), channel_id=1, source_target_pairs={{0,4},{1,3},{4,8},{5,1},{8,12},{9,5},{12,14},{13,9},{14,10},{15,13... | collective-permute-start | bytes 393224 | tf_op jit(solution)/shard_map/ppermute | solution.py:323
  66.0 0.1 collective-permute-done.25.refs_2_
  66.1 1.8 %collective-permute-start.42 = (bf16[16,4096]{1,0:T(8,128)(2,1)S(1)}, bf16[16,4096]{1,0:T(8,128)(2,1)S(1)}, u32[]{:S(2)}, u32[]{:S(2)}) collective-permute-start(bf16[16,4096]{1,0:T(8,128)(2,1)S(1)} %added.26), channel_id=1, source_target_pairs={{0,4},{1,3},{4,8},{5,1},{8,12},{9,5},{12,14},{13,9},{14,10},{15,13... | collective-permute-start | bytes 393224 | tf_op jit(solution)/shard_map/ppermute | solution.py:323
  68.0 1.5 %collective-permute-start.26 = (bf16[16,4096]{1,0:T(8,128)(2,1)S(1)}, bf16[16,4096]{1,0:T(8,128)(2,1)S(1)}, u32[]{:S(2)}, u32[]{:S(2)}) collective-permute-start(bf16[16,4096]{1,0:T(8,128)(2,1)S(1)} %added.16), channel_id=1, source_target_pairs={{0,4},{1,3},{4,8},{5,1},{8,12},{9,5},{12,14},{13,9},{14,10},{15,13... | collective-permute-start | bytes 393224 | tf_op jit(solution)/shard_map/ppermute | solution.py:323
  69.6 0.1 collective-permute-start.19
  69.7 1.3 %collective-permute-start.39 = (bf16[16,4096]{1,0:T(8,128)(2,1)S(1)}, bf16[16,4096]{1,0:T(8,128)(2,1)S(1)}, u32[]{:S(2)}, u32[]{:S(2)}) collective-permute-start(bf16[16,4096]{1,0:T(8,128)(2,1)S(1)} %added.23), channel_id=1, source_target_pairs={{0,4},{1,3},{4,8},{5,1},{8,12},{9,5},{12,14},{13,9},{14,10},{15,13... | collective-permute-start | bytes 393224 | tf_op jit(solution)/shard_map/ppermute | solution.py:323
  71.1 1.7 %collective-permute-start.30 = (bf16[16,4096]{1,0:T(8,128)(2,1)S(1)}, bf16[16,4096]{1,0:T(8,128)(2,1)S(1)}, u32[]{:S(2)}, u32[]{:S(2)}) collective-permute-start(bf16[16,4096]{1,0:T(8,128)(2,1)S(1)} %added.20), channel_id=1, source_target_pairs={{0,4},{1,3},{4,8},{5,1},{8,12},{9,5},{12,14},{13,9},{14,10},{15,13... | collective-permute-start | bytes 393224 | tf_op jit(solution)/shard_map/ppermute | solution.py:323
  72.9 1.6 %collective-permute-start.43 = (bf16[16,4096]{1,0:T(8,128)(2,1)S(1)}, bf16[16,4096]{1,0:T(8,128)(2,1)S(1)}, u32[]{:S(2)}, u32[]{:S(2)}) collective-permute-start(bf16[16,4096]{1,0:T(8,128)(2,1)S(1)} %added.27), channel_id=1, source_target_pairs={{0,4},{1,3},{4,8},{5,1},{8,12},{9,5},{12,14},{13,9},{14,10},{15,13... | collective-permute-start | bytes 393224 | tf_op jit(solution)/shard_map/ppermute | solution.py:323
  74.5 0.2 collective-permute-done.39.refs_2_
  74.7 1.3 %collective-permute-start.27 = (bf16[16,4096]{1,0:T(8,128)(2,1)S(1)}, bf16[16,4096]{1,0:T(8,128)(2,1)S(1)}, u32[]{:S(2)}, u32[]{:S(2)}) collective-permute-start(bf16[16,4096]{1,0:T(8,128)(2,1)S(1)} %added.17), channel_id=1, source_target_pairs={{0,4},{1,3},{4,8},{5,1},{8,12},{9,5},{12,14},{13,9},{14,10},{15,13... | collective-permute-start | bytes 393224 | tf_op jit(solution)/shard_map/ppermute | solution.py:323
  76.1 1.7 %collective-permute-start.40 = (bf16[16,4096]{1,0:T(8,128)(2,1)S(1)}, bf16[16,4096]{1,0:T(8,128)(2,1)S(1)}, u32[]{:S(2)}, u32[]{:S(2)}) collective-permute-start(bf16[16,4096]{1,0:T(8,128)(2,1)S(1)} %added.24), channel_id=1, source_target_pairs={{0,4},{1,3},{4,8},{5,1},{8,12},{9,5},{12,14},{13,9},{14,10},{15,13... | collective-permute-start | bytes 393224 | tf_op jit(solution)/shard_map/ppermute | solution.py:323
  77.8 0.1 collective-permute-done.43
  77.9 0.4 collective-permute-start.44
  78.3 1.4 %collective-permute-done.27.refs_2_ = bf16[16,4096]{1,0:T(8,128)(2,1)S(1)} collective-permute-done((bf16[16,4096]{1,0:T(8,128)(2,1)S(1)}, bf16[16,4096]{1,0:T(8,128)(2,1)S(1)}, u32[]{:S(2)}, u32[]{:S(2)}) %collective-permute-start.27) | collective-permute-done | bytes 131104 | tf_op jit(solution)/shard_map/ppermute | solution.py:323
  79.7 1.4 %collective-permute-done.40.refs_6_ = bf16[16,4096]{1,0:T(8,128)(2,1)S(1)} collective-permute-done((bf16[16,4096]{1,0:T(8,128)(2,1)S(1)}, bf16[16,4096]{1,0:T(8,128)(2,1)S(1)}, u32[]{:S(2)}, u32[]{:S(2)}) %collective-permute-start.40) | collective-permute-done | bytes 131104 | tf_op jit(solution)/shard_map/ppermute | solution.py:323
  81.1 1.0 %last.1 = bf16[16,8192]{1,0:T(8,128)(2,1)} custom-call(s32[1,2]{1,0:T(1,128)S(1)} %bitcast.10, bf16[16,4096]{1,0:T(8,128)(2,1)S(1)} %get-tuple-element.35.refs_0_, bf16[16,4096]{1,0:T(8,128)(2,1)S(1)} %collective-permute-done.19.refs_1_, bf16[16,4096]{1,0:T(8,128)(2,1)S(1)} %collective-permute-done.27.refs_2_, ...), custom_call_target="tpu_custom_call" | custom-call | tf_op jit(solution)/shard_map/last/pallas_call | solution.py:273
  (86 shorter events, 0.9 us)
Async XLA Ops:
  0.0 28.3 %copy-start.3 = (s32[2]{0:T(128)S(1)}, s32[2]{0:T(128)}, u32[]{:S(2)}) copy-start(s32[2]{0:T(128)} %param.14) | copy-start | bytes 28
  0.0 28.3 %copy-start.2 = (bf16[8,8192,8]{1,2,0:T(8,128)(2,1)S(1)}, bf16[8,8192,8]{1,2,0:T(8,128)(2,1)}, u32[]{:S(2)}) copy-start(bf16[8,8192,8]{1,2,0:T(8,128)(2,1)} %param.12) | copy-start | bytes 3145732
  0.0 3.1 %collective-permute-start = (bf16[16,8192]{1,0:T(8,128)(2,1)}, bf16[16,8192]{1,0:T(8,128)(2,1)S(1)}, u32[]{:S(2)}, u32[]{:S(2)}) collective-permute-start(bf16[16,8192]{1,0:T(8,128)(2,1)} %tokens_ref.1), channel_id=1, source_target_pairs={{0,1},{1,0},{2,3},{3,2},{4,5},{5,4},{6,7},{7,6},{8,9},{9,8},{10,11... | collective-permute-start | bytes 786440 | tf_op jit(solution)/shard_map/ppermute | solution.py:326
  0.5 7.1 %collective-permute-start.1 = (bf16[16,8192]{1,0:T(8,128)(2,1)}, bf16[16,8192]{1,0:T(8,128)(2,1)S(1)}, u32[]{:S(2)}, u32[]{:S(2)}) collective-permute-start(bf16[16,8192]{1,0:T(8,128)(2,1)} %tokens_ref.1), channel_id=1, source_target_pairs={{0,4},{1,3},{4,8},{5,1},{8,12},{9,5},{12,14},{13,9},{14,10},{15,13... | collective-permute-start | bytes 786440 | tf_op jit(solution)/shard_map/ppermute | solution.py:323
  3.1 26.9 %copy-start = (bf16[8192,896]{1,0:T(8,128)(2,1)S(1)}, bf16[8192,896]{1,0:T(8,128)(2,1)}, u32[]{:S(2)}) copy-start(bf16[8192,896]{1,0:T(8,128)(2,1)} %w_ref.7) | copy-start | bytes 44040196
  4.2 6.4 %collective-permute-start.2 = (bf16[16,8192]{1,0:T(8,128)(2,1)S(1)}, bf16[16,8192]{1,0:T(8,128)(2,1)S(1)}, u32[]{:S(2)}, u32[]{:S(2)}) collective-permute-start(bf16[16,8192]{1,0:T(8,128)(2,1)S(1)} %get-tuple-element.34.refs_1_), channel_id=1, source_target_pairs={{0,4},{1,3},{4,8},{5,1},{8,12},{9,5},{12,14},{13,9},{14,10},{15,13... | collective-permute-start | bytes 786440 | tf_op jit(solution)/shard_map/ppermute | solution.py:323
  7.6 6.4 %collective-permute-start.3 = (bf16[16,8192]{1,0:T(8,128)(2,1)S(1)}, bf16[16,8192]{1,0:T(8,128)(2,1)S(1)}, u32[]{:S(2)}, u32[]{:S(2)}) collective-permute-start(bf16[16,8192]{1,0:T(8,128)(2,1)S(1)} %collective-permute-done.1.refs_2_), channel_id=1, source_target_pairs={{0,4},{1,3},{4,8},{5,1},{8,12},{9,5},{12,14},{13,9},{14,10},{15,13... | collective-permute-start | bytes 786440 | tf_op jit(solution)/shard_map/ppermute | solution.py:323
  10.6 6.4 %collective-permute-start.4 = (bf16[16,8192]{1,0:T(8,128)(2,1)S(1)}, bf16[16,8192]{1,0:T(8,128)(2,1)S(1)}, u32[]{:S(2)}, u32[]{:S(2)}) collective-permute-start(bf16[16,8192]{1,0:T(8,128)(2,1)S(1)} %collective-permute-done.2.refs_3_), channel_id=1, source_target_pairs={{0,4},{1,3},{4,8},{5,1},{8,12},{9,5},{12,14},{13,9},{14,10},{15,13... | collective-permute-start | bytes 786440 | tf_op jit(solution)/shard_map/ppermute | solution.py:323
  14.0 6.4 %collective-permute-start.5 = (bf16[16,8192]{1,0:T(8,128)(2,1)S(1)}, bf16[16,8192]{1,0:T(8,128)(2,1)S(1)}, u32[]{:S(2)}, u32[]{:S(2)}) collective-permute-start(bf16[16,8192]{1,0:T(8,128)(2,1)S(1)} %collective-permute-done.3.refs_4_), channel_id=1, source_target_pairs={{0,4},{1,3},{4,8},{5,1},{8,12},{9,5},{12,14},{13,9},{14,10},{15,13... | collective-permute-start | bytes 786440 | tf_op jit(solution)/shard_map/ppermute | solution.py:323
  16.0 6.4 %collective-permute-start.8 = (bf16[16,8192]{1,0:T(8,128)(2,1)S(1)}, bf16[16,8192]{1,0:T(8,128)(2,1)S(1)}, u32[]{:S(2)}, u32[]{:S(2)}) collective-permute-start(bf16[16,8192]{1,0:T(8,128)(2,1)S(1)} %collective-permute-done.1.refs_2_), channel_id=1, source_target_pairs={{0,1},{1,0},{2,3},{3,2},{4,5},{5,4},{6,7},{7,6},{8,9},{9,8},{10,11... | collective-permute-start | bytes 786440 | tf_op jit(solution)/shard_map/ppermute | solution.py:326
  16.0 6.9 %collective-permute-start.9 = (bf16[16,8192]{1,0:T(8,128)(2,1)S(1)}, bf16[16,8192]{1,0:T(8,128)(2,1)S(1)}, u32[]{:S(2)}, u32[]{:S(2)}) collective-permute-start(bf16[16,8192]{1,0:T(8,128)(2,1)S(1)} %collective-permute-done.2.refs_3_), channel_id=1, source_target_pairs={{0,1},{1,0},{2,3},{3,2},{4,5},{5,4},{6,7},{7,6},{8,9},{9,8},{10,11... | collective-permute-start | bytes 786440 | tf_op jit(solution)/shard_map/ppermute | solution.py:326
  17.0 6.4 %collective-permute-start.6 = (bf16[16,8192]{1,0:T(8,128)(2,1)S(1)}, bf16[16,8192]{1,0:T(8,128)(2,1)S(1)}, u32[]{:S(2)}, u32[]{:S(2)}) collective-permute-start(bf16[16,8192]{1,0:T(8,128)(2,1)S(1)} %collective-permute-done.4.refs_5_), channel_id=1, source_target_pairs={{0,4},{1,3},{4,8},{5,1},{8,12},{9,5},{12,14},{13,9},{14,10},{15,13... | collective-permute-start | bytes 786440 | tf_op jit(solution)/shard_map/ppermute | solution.py:323
  20.3 6.4 %collective-permute-start.7 = (bf16[16,8192]{1,0:T(8,128)(2,1)S(1)}, bf16[16,8192]{1,0:T(8,128)(2,1)S(1)}, u32[]{:S(2)}, u32[]{:S(2)}) collective-permute-start(bf16[16,8192]{1,0:T(8,128)(2,1)S(1)} %collective-permute-done.5.refs_6_), channel_id=1, source_target_pairs={{0,4},{1,3},{4,8},{5,1},{8,12},{9,5},{12,14},{13,9},{14,10},{15,13... | collective-permute-start | bytes 786440 | tf_op jit(solution)/shard_map/ppermute | solution.py:323
  22.4 4.3 %collective-permute-start.10 = (bf16[16,8192]{1,0:T(8,128)(2,1)S(1)}, bf16[16,8192]{1,0:T(8,128)(2,1)S(1)}, u32[]{:S(2)}, u32[]{:S(2)}) collective-permute-start(bf16[16,8192]{1,0:T(8,128)(2,1)S(1)} %collective-permute-done.3.refs_4_), channel_id=1, source_target_pairs={{0,1},{1,0},{2,3},{3,2},{4,5},{5,4},{6,7},{7,6},{8,9},{9,8},{10,11... | collective-permute-start | bytes 786440 | tf_op jit(solution)/shard_map/ppermute | solution.py:326
  22.4 4.3 %collective-permute-start.11 = (bf16[16,8192]{1,0:T(8,128)(2,1)S(1)}, bf16[16,8192]{1,0:T(8,128)(2,1)S(1)}, u32[]{:S(2)}, u32[]{:S(2)}) collective-permute-start(bf16[16,8192]{1,0:T(8,128)(2,1)S(1)} %collective-permute-done.4.refs_5_), channel_id=1, source_target_pairs={{0,1},{1,0},{2,3},{3,2},{4,5},{5,4},{6,7},{7,6},{8,9},{9,8},{10,11... | collective-permute-start | bytes 786440 | tf_op jit(solution)/shard_map/ppermute | solution.py:326
  22.9 3.8 %collective-permute-start.12 = (bf16[16,8192]{1,0:T(8,128)(2,1)S(1)}, bf16[16,8192]{1,0:T(8,128)(2,1)S(1)}, u32[]{:S(2)}, u32[]{:S(2)}) collective-permute-start(bf16[16,8192]{1,0:T(8,128)(2,1)S(1)} %collective-permute-done.5.refs_6_), channel_id=1, source_target_pairs={{0,1},{1,0},{2,3},{3,2},{4,5},{5,4},{6,7},{7,6},{8,9},{9,8},{10,11... | collective-permute-start | bytes 786440 | tf_op jit(solution)/shard_map/ppermute | solution.py:326
  23.4 3.4 %collective-permute-start.13 = (bf16[16,8192]{1,0:T(8,128)(2,1)S(1)}, bf16[16,8192]{1,0:T(8,128)(2,1)S(1)}, u32[]{:S(2)}, u32[]{:S(2)}) collective-permute-start(bf16[16,8192]{1,0:T(8,128)(2,1)S(1)} %collective-permute-done.6.refs_7_), channel_id=1, source_target_pairs={{0,1},{1,0},{2,3},{3,2},{4,5},{5,4},{6,7},{7,6},{8,9},{9,8},{10,11... | collective-permute-start | bytes 786440 | tf_op jit(solution)/shard_map/ppermute | solution.py:326
  26.7 1.5 %collective-permute-start.14 = (bf16[16,8192]{1,0:T(8,128)(2,1)S(1)}, bf16[16,8192]{1,0:T(8,128)(2,1)S(1)}, u32[]{:S(2)}, u32[]{:S(2)}) collective-permute-start(bf16[16,8192]{1,0:T(8,128)(2,1)S(1)} %collective-permute-done.7.refs_8_), channel_id=1, source_target_pairs={{0,1},{1,0},{2,3},{3,2},{4,5},{5,4},{6,7},{7,6},{8,9},{9,8},{10,11... | collective-permute-start | bytes 786440 | tf_op jit(solution)/shard_map/ppermute | solution.py:326
  29.8 2.6 %collective-permute-start.15 = (bf16[8,256]{1,0:T(8,128)(2,1)S(1)}, bf16[8,256]{1,0:T(8,128)(2,1)S(1)}, u32[]{:S(2)}, u32[]{:S(2)}) collective-permute-start(bf16[8,256]{1,0:T(8,128)(2,1)S(1)} %rank.1.refs_16_), channel_id=1, source_target_pairs={{0,1},{1,0},{2,3},{3,2},{4,5},{5,4},{6,7},{7,6},{8,9},{9,8},{10,11... | collective-permute-start | bytes 12296 | tf_op jit(solution)/shard_map/ppermute | solution.py:326
  30.0 8.6 %slice-start = ((s8[14680064]{0:T(1024)(128)(4,1)}), s8[2097152]{0:T(1024)(128)(4,1)S(1)}, s32[]{:S(2)}) async-start(s8[14680064]{0:T(1024)(128)(4,1)} %bitcast.3), calls=%async_computation | async-start | bytes 4194304
  30.0 8.6 %slice-start.1 = ((s8[14680064]{0:T(1024)(128)(4,1)}), s8[4194304]{0:T(1024)(128)(4,1)S(1)}, s32[]{:S(2)}) async-start(s8[14680064]{0:T(1024)(128)(4,1)} %bitcast.3), calls=%async_computation.1 | async-start | bytes 8388608
  32.4 6.2 %slice-start.2 = ((s8[14680064]{0:T(1024)(128)(4,1)}), s8[4194304]{0:T(1024)(128)(4,1)S(1)}, s32[]{:S(2)}) async-start(s8[14680064]{0:T(1024)(128)(4,1)} %bitcast.3), calls=%async_computation.2 | async-start | bytes 8388608
  32.4 6.2 %slice-start.3 = ((s8[14680064]{0:T(1024)(128)(4,1)}), s8[4194304]{0:T(1024)(128)(4,1)S(1)}, s32[]{:S(2)}) async-start(s8[14680064]{0:T(1024)(128)(4,1)} %bitcast.3), calls=%async_computation.3 | async-start | bytes 8388608
  32.5 4.5 %collective-permute-start.16 = (bf16[16,256]{1,0:T(8,128)(2,1)S(1)}, bf16[16,256]{1,0:T(8,128)(2,1)S(1)}, u32[]{:S(2)}, u32[]{:S(2)}) collective-permute-start(bf16[16,256]{1,0:T(8,128)(2,1)S(1)} %pad_maximum_fusion.2), channel_id=1, source_target_pairs={{0,2},{1,3},{2,0},{3,1},{4,6},{5,7},{6,4},{7,5},{8,10},{9,11},{10,... | collective-permute-start | bytes 24584 | tf_op jit(solution)/shard_map/ppermute | solution.py:326
  37.0 4.1 %collective-permute-start.17 = (bf16[32,256]{1,0:T(8,128)(2,1)S(1)}, bf16[32,256]{1,0:T(8,128)(2,1)S(1)}, u32[]{:S(2)}, u32[]{:S(2)}) collective-permute-start(bf16[32,256]{1,0:T(8,128)(2,1)S(1)} %pad_maximum_fusion.1), channel_id=1, source_target_pairs={{0,4},{1,5},{2,6},{3,7},{4,0},{5,1},{6,2},{7,3},{8,12},{9,13},{10,... | collective-permute-start | bytes 49160 | tf_op jit(solution)/shard_map/ppermute | solution.py:326
  38.6 8.2 %slice-start.4 = ((s8[14680064]{0:T(1024)(128)(4,1)}), s8[4194304]{0:T(1024)(128)(4,1)S(1)}, s32[]{:S(2)}) async-start(s8[14680064]{0:T(1024)(128)(4,1)} %bitcast.5), calls=%async_computation.4 | async-start | bytes 8388608
  38.6 8.2 %slice-start.5 = ((s8[14680064]{0:T(1024)(128)(4,1)}), s8[4194304]{0:T(1024)(128)(4,1)S(1)}, s32[]{:S(2)}) async-start(s8[14680064]{0:T(1024)(128)(4,1)} %bitcast.5), calls=%async_computation.5 | async-start | bytes 8388608
  41.0 5.1 %copy-start.1 = (bf16[8,128,896]{2,1,0:T(8,128)(2,1)S(1)}, bf16[8,128,896]{2,1,0:T(8,128)(2,1)}, u32[]{:S(2)}) copy-start(bf16[8,128,896]{2,1,0:T(8,128)(2,1)} %expand_ref.1) | copy-start | bytes 5505028
  41.1 5.8 %slice-start.6 = ((s8[14680064]{0:T(1024)(128)(4,1)}), s8[4194304]{0:T(1024)(128)(4,1)S(1)}, s32[]{:S(2)}) async-start(s8[14680064]{0:T(1024)(128)(4,1)} %bitcast.5), calls=%async_computation.6 | async-start | bytes 8388608
  41.1 5.8 %slice-start.7 = ((s8[14680064]{0:T(1024)(128)(4,1)}), s8[2097152]{0:T(1024)(128)(4,1)S(1)}, s32[]{:S(2)}) async-start(s8[14680064]{0:T(1024)(128)(4,1)} %bitcast.5), calls=%async_computation.7 | async-start | bytes 4194304
  41.1 5.0 %collective-permute-start.18 = (bf16[64,256]{1,0:T(8,128)(2,1)S(1)}, bf16[64,256]{1,0:T(8,128)(2,1)S(1)}, u32[]{:S(2)}, u32[]{:S(2)}) collective-permute-start(bf16[64,256]{1,0:T(8,128)(2,1)S(1)} %pad_maximum_fusion), channel_id=1, source_target_pairs={{0,8},{1,9},{2,10},{3,11},{4,12},{5,13},{6,14},{7,15},{8,0},{9,1},... | collective-permute-start | bytes 98312 | tf_op jit(solution)/shard_map/ppermute | solution.py:326
  49.3 31.8 %copy-start.4 = (s32[2]{0:T(128)S(1)}, s32[2]{0:T(128)}, u32[]{:S(2)}) copy-start(s32[2]{0:T(128)} %param.15) | copy-start | bytes 28
  49.4 6.7 %collective-permute-start.22 = (bf16[32,4096]{1,0:T(8,128)(2,1)S(1)}, bf16[32,4096]{1,0:T(8,128)(2,1)S(1)}, u32[]{:S(2)}, u32[]{:S(2)}) collective-permute-start(bf16[32,4096]{1,0:T(8,128)(2,1)S(1)} %get-tuple-element.42), channel_id=1, source_target_pairs={{0,1},{1,0},{2,3},{3,2},{4,5},{5,4},{6,7},{7,6},{8,9},{9,8},{10,11... | collective-permute-start | bytes 786440 | tf_op jit(solution)/shard_map/ppermute | solution.py:326
  49.4 3.8 %collective-permute-start.23 = (bf16[16,4096]{1,0:T(8,128)(2,1)S(1)}, bf16[16,4096]{1,0:T(8,128)(2,1)S(1)}, u32[]{:S(2)}, u32[]{:S(2)}) collective-permute-start(bf16[16,4096]{1,0:T(8,128)(2,1)S(1)} %get-tuple-element.44), channel_id=1, source_target_pairs={{0,1},{1,0},{2,3},{3,2},{4,5},{5,4},{6,7},{7,6},{8,9},{9,8},{10,11... | collective-permute-start | bytes 393224 | tf_op jit(solution)/shard_map/ppermute | solution.py:326
  52.5 5.4 %collective-permute-start.35 = (bf16[32,4096]{1,0:T(8,128)(2,1)S(1)}, bf16[32,4096]{1,0:T(8,128)(2,1)S(1)}, u32[]{:S(2)}, u32[]{:S(2)}) collective-permute-start(bf16[32,4096]{1,0:T(8,128)(2,1)S(1)} %get-tuple-element.55), channel_id=1, source_target_pairs={{0,1},{1,0},{2,3},{3,2},{4,5},{5,4},{6,7},{7,6},{8,9},{9,8},{10,11... | collective-permute-start | bytes 786440 | tf_op jit(solution)/shard_map/ppermute | solution.py:326
  52.7 6.9 %collective-permute-start.21 = (bf16[32,4096]{1,0:T(8,128)(2,1)S(1)}, bf16[32,4096]{1,0:T(8,128)(2,1)S(1)}, u32[]{:S(2)}, u32[]{:S(2)}) collective-permute-start(bf16[32,4096]{1,0:T(8,128)(2,1)S(1)} %get-tuple-element.40), channel_id=1, source_target_pairs={{0,1},{1,0},{2,3},{3,2},{4,5},{5,4},{6,7},{7,6},{8,9},{9,8},{10,11... | collective-permute-start | bytes 786440 | tf_op jit(solution)/shard_map/ppermute | solution.py:326
  53.1 1.6 %collective-permute-start.36 = (bf16[16,4096]{1,0:T(8,128)(2,1)S(1)}, bf16[16,4096]{1,0:T(8,128)(2,1)S(1)}, u32[]{:S(2)}, u32[]{:S(2)}) collective-permute-start(bf16[16,4096]{1,0:T(8,128)(2,1)S(1)} %get-tuple-element.57), channel_id=1, source_target_pairs={{0,1},{1,0},{2,3},{3,2},{4,5},{5,4},{6,7},{7,6},{8,9},{9,8},{10,11... | collective-permute-start | bytes 393224 | tf_op jit(solution)/shard_map/ppermute | solution.py:326
  53.2 7.8 %collective-permute-start.34 = (bf16[32,4096]{1,0:T(8,128)(2,1)S(1)}, bf16[32,4096]{1,0:T(8,128)(2,1)S(1)}, u32[]{:S(2)}, u32[]{:S(2)}) collective-permute-start(bf16[32,4096]{1,0:T(8,128)(2,1)S(1)} %get-tuple-element.53), channel_id=1, source_target_pairs={{0,1},{1,0},{2,3},{3,2},{4,5},{5,4},{6,7},{7,6},{8,9},{9,8},{10,11... | collective-permute-start | bytes 786440 | tf_op jit(solution)/shard_map/ppermute | solution.py:326
  54.7 5.0 %collective-permute-start.24 = (bf16[16,4096]{1,0:T(8,128)(2,1)S(1)}, bf16[16,4096]{1,0:T(8,128)(2,1)S(1)}, u32[]{:S(2)}, u32[]{:S(2)}) collective-permute-start(bf16[16,4096]{1,0:T(8,128)(2,1)S(1)} %added.14), channel_id=1, source_target_pairs={{0,4},{1,3},{4,8},{5,1},{8,12},{9,5},{12,14},{13,9},{14,10},{15,13... | collective-permute-start | bytes 393224 | tf_op jit(solution)/shard_map/ppermute | solution.py:323
  56.0 5.1 %collective-permute-start.37 = (bf16[16,4096]{1,0:T(8,128)(2,1)S(1)}, bf16[16,4096]{1,0:T(8,128)(2,1)S(1)}, u32[]{:S(2)}, u32[]{:S(2)}) collective-permute-start(bf16[16,4096]{1,0:T(8,128)(2,1)S(1)} %added.21), channel_id=1, source_target_pairs={{0,4},{1,3},{4,8},{5,1},{8,12},{9,5},{12,14},{13,9},{14,10},{15,13... | collective-permute-start | bytes 393224 | tf_op jit(solution)/shard_map/ppermute | solution.py:323
  57.9 5.1 %collective-permute-start.28 = (bf16[16,4096]{1,0:T(8,128)(2,1)S(1)}, bf16[16,4096]{1,0:T(8,128)(2,1)S(1)}, u32[]{:S(2)}, u32[]{:S(2)}) collective-permute-start(bf16[16,4096]{1,0:T(8,128)(2,1)S(1)} %added.18), channel_id=1, source_target_pairs={{0,4},{1,3},{4,8},{5,1},{8,12},{9,5},{12,14},{13,9},{14,10},{15,13... | collective-permute-start | bytes 393224 | tf_op jit(solution)/shard_map/ppermute | solution.py:323
  59.6 10.1 %collective-permute-start.20 = (bf16[32,4096]{1,0:T(8,128)(2,1)S(1)}, bf16[32,4096]{1,0:T(8,128)(2,1)S(1)}, u32[]{:S(2)}, u32[]{:S(2)}) collective-permute-start(bf16[32,4096]{1,0:T(8,128)(2,1)S(1)} %get-tuple-element.38), channel_id=1, source_target_pairs={{0,1},{1,0},{2,3},{3,2},{4,5},{5,4},{6,7},{7,6},{8,9},{9,8},{10,11... | collective-permute-start | bytes 786440 | tf_op jit(solution)/shard_map/ppermute | solution.py:326
  59.7 5.0 %collective-permute-start.41 = (bf16[16,4096]{1,0:T(8,128)(2,1)S(1)}, bf16[16,4096]{1,0:T(8,128)(2,1)S(1)}, u32[]{:S(2)}, u32[]{:S(2)}) collective-permute-start(bf16[16,4096]{1,0:T(8,128)(2,1)S(1)} %added.25), channel_id=1, source_target_pairs={{0,4},{1,3},{4,8},{5,1},{8,12},{9,5},{12,14},{13,9},{14,10},{15,13... | collective-permute-start | bytes 393224 | tf_op jit(solution)/shard_map/ppermute | solution.py:323
  61.0 10.1 %collective-permute-start.33 = (bf16[32,4096]{1,0:T(8,128)(2,1)S(1)}, bf16[32,4096]{1,0:T(8,128)(2,1)S(1)}, u32[]{:S(2)}, u32[]{:S(2)}) collective-permute-start(bf16[32,4096]{1,0:T(8,128)(2,1)S(1)} %get-tuple-element.51), channel_id=1, source_target_pairs={{0,1},{1,0},{2,3},{3,2},{4,5},{5,4},{6,7},{7,6},{8,9},{9,8},{10,11... | collective-permute-start | bytes 786440 | tf_op jit(solution)/shard_map/ppermute | solution.py:326
  61.1 5.0 %collective-permute-start.25 = (bf16[16,4096]{1,0:T(8,128)(2,1)S(1)}, bf16[16,4096]{1,0:T(8,128)(2,1)S(1)}, u32[]{:S(2)}, u32[]{:S(2)}) collective-permute-start(bf16[16,4096]{1,0:T(8,128)(2,1)S(1)} %added.15), channel_id=1, source_target_pairs={{0,4},{1,3},{4,8},{5,1},{8,12},{9,5},{12,14},{13,9},{14,10},{15,13... | collective-permute-start | bytes 393224 | tf_op jit(solution)/shard_map/ppermute | solution.py:323
  63.0 5.0 %collective-permute-start.38 = (bf16[16,4096]{1,0:T(8,128)(2,1)S(1)}, bf16[16,4096]{1,0:T(8,128)(2,1)S(1)}, u32[]{:S(2)}, u32[]{:S(2)}) collective-permute-start(bf16[16,4096]{1,0:T(8,128)(2,1)S(1)} %added.22), channel_id=1, source_target_pairs={{0,4},{1,3},{4,8},{5,1},{8,12},{9,5},{12,14},{13,9},{14,10},{15,13... | collective-permute-start | bytes 393224 | tf_op jit(solution)/shard_map/ppermute | solution.py:323
  64.7 5.0 %collective-permute-start.29 = (bf16[16,4096]{1,0:T(8,128)(2,1)S(1)}, bf16[16,4096]{1,0:T(8,128)(2,1)S(1)}, u32[]{:S(2)}, u32[]{:S(2)}) collective-permute-start(bf16[16,4096]{1,0:T(8,128)(2,1)S(1)} %added.19), channel_id=1, source_target_pairs={{0,4},{1,3},{4,8},{5,1},{8,12},{9,5},{12,14},{13,9},{14,10},{15,13... | collective-permute-start | bytes 393224 | tf_op jit(solution)/shard_map/ppermute | solution.py:323
  66.1 6.7 %collective-permute-start.42 = (bf16[16,4096]{1,0:T(8,128)(2,1)S(1)}, bf16[16,4096]{1,0:T(8,128)(2,1)S(1)}, u32[]{:S(2)}, u32[]{:S(2)}) collective-permute-start(bf16[16,4096]{1,0:T(8,128)(2,1)S(1)} %added.26), channel_id=1, source_target_pairs={{0,4},{1,3},{4,8},{5,1},{8,12},{9,5},{12,14},{13,9},{14,10},{15,13... | collective-permute-start | bytes 393224 | tf_op jit(solution)/shard_map/ppermute | solution.py:323
  68.0 6.4 %collective-permute-start.26 = (bf16[16,4096]{1,0:T(8,128)(2,1)S(1)}, bf16[16,4096]{1,0:T(8,128)(2,1)S(1)}, u32[]{:S(2)}, u32[]{:S(2)}) collective-permute-start(bf16[16,4096]{1,0:T(8,128)(2,1)S(1)} %added.16), channel_id=1, source_target_pairs={{0,4},{1,3},{4,8},{5,1},{8,12},{9,5},{12,14},{13,9},{14,10},{15,13... | collective-permute-start | bytes 393224 | tf_op jit(solution)/shard_map/ppermute | solution.py:323
  69.6 6.5 %collective-permute-start.19 = (bf16[16,4096]{1,0:T(8,128)(2,1)S(1)}, bf16[16,4096]{1,0:T(8,128)(2,1)S(1)}, u32[]{:S(2)}, u32[]{:S(2)}) collective-permute-start(bf16[16,4096]{1,0:T(8,128)(2,1)S(1)} %get-tuple-element.36), channel_id=1, source_target_pairs={{0,1},{1,0},{2,3},{3,2},{4,5},{5,4},{6,7},{7,6},{8,9},{9,8},{10,11... | collective-permute-start | bytes 393224 | tf_op jit(solution)/shard_map/ppermute | solution.py:326
  69.7 5.0 %collective-permute-start.39 = (bf16[16,4096]{1,0:T(8,128)(2,1)S(1)}, bf16[16,4096]{1,0:T(8,128)(2,1)S(1)}, u32[]{:S(2)}, u32[]{:S(2)}) collective-permute-start(bf16[16,4096]{1,0:T(8,128)(2,1)S(1)} %added.23), channel_id=1, source_target_pairs={{0,4},{1,3},{4,8},{5,1},{8,12},{9,5},{12,14},{13,9},{14,10},{15,13... | collective-permute-start | bytes 393224 | tf_op jit(solution)/shard_map/ppermute | solution.py:323
  71.1 6.6 %collective-permute-start.30 = (bf16[16,4096]{1,0:T(8,128)(2,1)S(1)}, bf16[16,4096]{1,0:T(8,128)(2,1)S(1)}, u32[]{:S(2)}, u32[]{:S(2)}) collective-permute-start(bf16[16,4096]{1,0:T(8,128)(2,1)S(1)} %added.20), channel_id=1, source_target_pairs={{0,4},{1,3},{4,8},{5,1},{8,12},{9,5},{12,14},{13,9},{14,10},{15,13... | collective-permute-start | bytes 393224 | tf_op jit(solution)/shard_map/ppermute | solution.py:323
  72.9 5.0 %collective-permute-start.43 = (bf16[16,4096]{1,0:T(8,128)(2,1)S(1)}, bf16[16,4096]{1,0:T(8,128)(2,1)S(1)}, u32[]{:S(2)}, u32[]{:S(2)}) collective-permute-start(bf16[16,4096]{1,0:T(8,128)(2,1)S(1)} %added.27), channel_id=1, source_target_pairs={{0,4},{1,3},{4,8},{5,1},{8,12},{9,5},{12,14},{13,9},{14,10},{15,13... | collective-permute-start | bytes 393224 | tf_op jit(solution)/shard_map/ppermute | solution.py:323
  74.4 3.8 %collective-permute-start.32 = (bf16[16,4096]{1,0:T(8,128)(2,1)S(1)}, bf16[16,4096]{1,0:T(8,128)(2,1)S(1)}, u32[]{:S(2)}, u32[]{:S(2)}) collective-permute-start(bf16[16,4096]{1,0:T(8,128)(2,1)S(1)} %get-tuple-element.49), channel_id=1, source_target_pairs={{0,1},{1,0},{2,3},{3,2},{4,5},{5,4},{6,7},{7,6},{8,9},{9,8},{10,11... | collective-permute-start | bytes 393224 | tf_op jit(solution)/shard_map/ppermute | solution.py:326
  74.7 5.0 %collective-permute-start.27 = (bf16[16,4096]{1,0:T(8,128)(2,1)S(1)}, bf16[16,4096]{1,0:T(8,128)(2,1)S(1)}, u32[]{:S(2)}, u32[]{:S(2)}) collective-permute-start(bf16[16,4096]{1,0:T(8,128)(2,1)S(1)} %added.17), channel_id=1, source_target_pairs={{0,4},{1,3},{4,8},{5,1},{8,12},{9,5},{12,14},{13,9},{14,10},{15,13... | collective-permute-start | bytes 393224 | tf_op jit(solution)/shard_map/ppermute | solution.py:323
  76.1 5.0 %collective-permute-start.40 = (bf16[16,4096]{1,0:T(8,128)(2,1)S(1)}, bf16[16,4096]{1,0:T(8,128)(2,1)S(1)}, u32[]{:S(2)}, u32[]{:S(2)}) collective-permute-start(bf16[16,4096]{1,0:T(8,128)(2,1)S(1)} %added.24), channel_id=1, source_target_pairs={{0,4},{1,3},{4,8},{5,1},{8,12},{9,5},{12,14},{13,9},{14,10},{15,13... | collective-permute-start | bytes 393224 | tf_op jit(solution)/shard_map/ppermute | solution.py:323
  77.8 3.3 %collective-permute-start.31 = (bf16[16,4096]{1,0:T(8,128)(2,1)S(1)}, bf16[16,4096]{1,0:T(8,128)(2,1)S(1)}, u32[]{:S(2)}, u32[]{:S(2)}) collective-permute-start(bf16[16,4096]{1,0:T(8,128)(2,1)S(1)} %collective-permute-done.30), channel_id=1, source_target_pairs={{0,1},{1,0},{2,3},{3,2},{4,5},{5,4},{6,7},{7,6},{8,9},{9,8},{10,11... | collective-permute-start | bytes 393224 | tf_op jit(solution)/shard_map/ppermute | solution.py:326
  77.9 3.2 %collective-permute-start.44 = (bf16[16,4096]{1,0:T(8,128)(2,1)S(1)}, bf16[16,4096]{1,0:T(8,128)(2,1)S(1)}, u32[]{:S(2)}, u32[]{:S(2)}) collective-permute-start(bf16[16,4096]{1,0:T(8,128)(2,1)S(1)} %collective-permute-done.43), channel_id=1, source_target_pairs={{0,1},{1,0},{2,3},{3,2},{4,5},{5,4},{6,7},{7,6},{8,9},{9,8},{10,11... | collective-permute-start | bytes 393224 | tf_op jit(solution)/shard_map/ppermute | solution.py:326

commit v8 on v7

--- a/solution.py
+++ b/solution.py
@@ -9,7 +9,7 @@
 
 F32 = jnp.float32
 BF16 = jnp.bfloat16
-VMEM_LIMIT = 20 * 1024 * 1024
+VMEM_LIMIT = 17 * 1024 * 1024
 
 
 def largest_tile(size, limit):
@@ -93,61 +93,111 @@
     return jnp.sum(jnp.where(spots == index, row, 0))
 
 
-def anchor_kernel(tokens_ref, passed_in, own_ref, passed_out, sem):
-    copy = pltpu.make_async_copy(tokens_ref, own_ref, sem)
-    copy.start()
-    copy.wait()
-
-
-def anchor(tokens, passed):
+def anchor_kernel(ids_ref, tokens_ref, shrink_ref, passed_in, own_ref, chosen_ref, passed_out, sems):
+    blocks = ids_ref.shape[1]
+    copies = [pltpu.make_async_copy(tokens_ref, own_ref, sems.at[blocks])]
+    for b in range(blocks):
+        source = shrink_ref.at[picked(ids_ref, b)]
+        copies.append(pltpu.make_async_copy(source, chosen_ref.at[b], sems.at[b]))
+    for copy in copies:
+        copy.start()
+    for copy in copies:
+        copy.wait()
+
+
+def anchor(adapters, tokens, shrink, passed):
+    blocks = adapters.shape[1]
     return pl.pallas_call(
         anchor_kernel,
-        in_specs=[FAR, FAR],
-        out_specs=whole(1) + [FAR],
-        out_shape=[jax.ShapeDtypeStruct(passed.shape, passed.dtype)] * 2,
-        input_output_aliases={1: 1},
-        scratch_shapes=[pltpu.SemaphoreType.DMA],
+        in_specs=whole(1) + [FAR] * 3,
+        out_specs=whole(2) + [FAR],
+        out_shape=[
+            jax.ShapeDtypeStruct(tokens.shape, BF16),
+            jax.ShapeDtypeStruct((blocks,) + shrink.shape[1:], BF16),
+            jax.ShapeDtypeStruct(passed.shape, BF16),
+        ],
+        input_output_aliases={3: 2},
+        scratch_shapes=[pltpu.SemaphoreType.DMA((blocks + 1,))],
         compiler_params=params(),
         cost_estimate=cost(30_000_000_000, 0),
         name="anchor",
-    )(far(tokens), passed)
-
-
-def rank_kernel(blocks, ids_ref, shrink_ref, *refs):
-    pieces, out_ref, scratch = refs[:-2], refs[-2], refs[-1]
-    members = len(pieces)
+    )(adapters, far(tokens), far(shrink), passed)
+
+
+def tie_kernel(x_ref, after_ref, out_ref):
+    del x_ref, after_ref, out_ref
+
+
+def tie(x, after):
+    return pl.pallas_call(
+        tie_kernel,
+        in_specs=[FAR, FAR],
+        out_specs=FAR,
+        out_shape=jax.ShapeDtypeStruct(x.shape, x.dtype),
+        input_output_aliases={0: 0},
+        compiler_params=params(),
+        name="tie",
+    )(x, after)
+
+
+def rank_kernel(members, numbers, ids_ref, expand_ref, own_ref, other_ref, *refs):
+    pieces, (out_ref, chosen_ref, scratch, sems) = refs[: len(numbers)], refs[-4:]
     rows = pieces[0].shape[0]
-    span = shrink_ref.shape[1]
+    blocks, span = ids_ref.shape[1], own_ref.shape[1]
     block_rows = members * rows // blocks
-    places = arrivals(lax.axis_index("tp"), members, rows)
+    device = lax.axis_index("tp")
+    places = arrivals(device, members, rows)
     lhs = jnp.concatenate([piece[...] for piece in pieces], axis=0)
-    weights = jnp.concatenate([shrink_ref[picked(ids_ref, b)] for b in range(blocks)], axis=0)
+    ids = [picked(ids_ref, b) for b in range(blocks)]
+    copies = [
+        pltpu.make_async_copy(expand_ref.at[ids[b]], chosen_ref.at[b], sems.at[b])
+        for b in range(blocks)
+    ]
+    for copy in copies:
+        copy.start()
+    weights = jnp.concatenate([ref[b] for ref in (own_ref, other_ref) for b in range(blocks)], axis=0)
     found = lax.dot_general(
         lhs, weights, (((1,), (1,)), ((), ())), preferred_element_type=F32
     )
-    for index, place in enumerate(places):
+    scratch[...] = jnp.zeros_like(scratch)
+    for index, number in enumerate(numbers):
         part = found[index * rows : (index + 1) * rows]
-        value = part[:, :span]
-        for b in range(1, blocks):
-            value = jnp.where(place // block_rows == b, part[:, b * span : (b + 1) * span], value)
-        scratch[pl.ds(place, rows), :span] = value
-    out_ref[...] = scratch[...].T[:span].astype(BF16)
-
-
-def rank_of(adapters, pieces, shrink):
+        for source in range(2):
+            first = source * blocks * span
+            value = part[:, first : first + span]
+            for b in range(1, blocks):
+                columns = part[:, first + b * span : first + (b + 1) * span]
+                value = jnp.where(places[number] // block_rows == b, columns, value)
+            scratch[source, pl.ds(places[number], rows), :span] = value
+    own, other = scratch[0].T[:span], scratch[1].T[:span]
+    lower = device % 2 == 0
+    out_ref[...] = jnp.concatenate(
+        [jnp.where(lower, own, other), jnp.where(lower, other, own)], axis=0
+    ).astype(BF16)
+    for copy in copies:
+        copy.wait()
+
+
+def rank_of(adapters, members, numbers, pieces, shrink, other, expand, after):
     rows, model = pieces[0].shape
-    blocks, span = adapters.shape[1], shrink.shape[1]
-    total = rows * len(pieces)
-    return pl.pallas_call(
-        functools.partial(rank_kernel, blocks),
-        in_specs=whole(2 + len(pieces)),
-        out_specs=whole(1)[0],
-        out_shape=jax.ShapeDtypeStruct((span, total), BF16),
-        scratch_shapes=[pltpu.VMEM((total, 128), F32)],
-        compiler_params=params(),
-        cost_estimate=cost(2 * total * model * span * blocks, 2 * total * model),
+    span = shrink.shape[1]
+    total = rows * members
+    return pl.pallas_call(
+        functools.partial(rank_kernel, members, numbers),
+        in_specs=whole(1) + [FAR] + whole(2 + len(pieces)) + [FAR] * len(after),
+        out_specs=whole(2),
+        out_shape=[
+            jax.ShapeDtypeStruct((2 * span, total), BF16),
+            jax.ShapeDtypeStruct((adapters.shape[1],) + expand.shape[1:], BF16),
+        ],
+        scratch_shapes=[
+            pltpu.VMEM((2, total, 128), F32),
+            pltpu.SemaphoreType.DMA((adapters.shape[1],)),
+        ],
+        compiler_params=params(),
+        cost_estimate=cost(2 * total * model * span * 2, 2 * total * model),
         name="rank",
-    )(adapters, shrink, *pieces)
+    )(adapters, far(expand), shrink, other, *pieces, *after)
 
 
 def product_kernel(first, w_ref, *refs):
@@ -180,20 +230,21 @@
     )(matrix, *pieces, after)
 
 
-def finish_kernel(blocks, span, ids_ref, gate_a, gate_b, up_a, up_b, rank_ref, expand_ref, hidden_ref):
+def finish_kernel(span, gate_a, gate_b, up_a, up_b, rank_ref, expand_ref, hidden_ref):
     ranks = rank_ref.shape[0]
-    device = lax.axis_index("tp")
+    chip = lax.axis_index("tp") // 2
     shape = (ranks, ranks)
     want = lax.broadcasted_iota(jnp.int32, shape, 0)
     have = lax.broadcasted_iota(jnp.int32, shape, 1)
-    origin = ((have // span) ^ device) * span + have % span
+    origin = ((have // span) ^ chip) * span + have % span
     order = jnp.where(want == origin, 1.0, 0.0).astype(BF16)
     rank = jnp.dot(order, rank_ref[...], preferred_element_type=F32).T.astype(BF16)
     half = ranks // 2
+    blocks = expand_ref.shape[0]
     rows = hidden_ref.shape[0] // blocks
     for b in range(blocks):
         part = slice(b * rows, (b + 1) * rows)
-        expand = expand_ref[picked(ids_ref, b)]
+        expand = expand_ref[b]
         gate = jnp.dot(rank[part, :half], expand[:half], preferred_element_type=F32)
         up = jnp.dot(rank[part, half:], expand[half:], preferred_element_type=F32)
         gate += gate_a[part] + gate_b[part]
@@ -201,26 +252,26 @@
         hidden_ref[part] = (gate / (1.0 + jnp.exp(-gate)) * up).astype(BF16)
 
 
-def finish(adapters, products, rank, expand, span):
+def finish(products, rank, expand, span):
     total, width = products[0].shape
     return pl.pallas_call(
-        functools.partial(finish_kernel, adapters.shape[1], span),
-        in_specs=whole(7),
+        functools.partial(finish_kernel, span),
+        in_specs=whole(6),
         out_specs=whole(1)[0],
         out_shape=jax.ShapeDtypeStruct((total, width), BF16),
         compiler_params=params(),
+        cost_estimate=cost(6_000_000_000, 0),
         name="finish",
-    )(adapters, *products, rank, expand)
-
-
-def down_kernel(members, groups, rows, first, size, w_ref, hidden_ref, *refs):
+    )(*products, rank, expand)
+
+
+def down_kernel(members, groups, rows, size, w_ref, hidden_ref, *refs):
     outs, product_ref = refs[:-1], refs[-1]
     places = departures(lax.axis_index("tp"), members, rows)
     hidden = hidden_ref[...]
-    for start in range(0, outs[0].shape[1], size):
+    for start in range(0, w_ref.shape[1], size):
         columns = slice(start, start + size)
-        weights = w_ref[:, first + start : first + start + size]
-        part = jnp.dot(hidden, weights, preferred_element_type=F32)
+        part = jnp.dot(hidden, w_ref[:, columns], preferred_element_type=F32)
         product_ref[...] = part.astype(BF16)
         at = 0
         for out, group in zip(outs, groups, strict=True):
@@ -231,12 +282,12 @@
                 at += 1
 
 
-def down(hidden, down_matrix, groups, rows, part, parts):
+def down(hidden, down_matrix, groups, rows):
     total, depth = hidden.shape
-    columns = down_matrix.shape[1] // parts
+    columns = down_matrix.shape[1]
     size = min(1024, columns)
     return pl.pallas_call(
-        functools.partial(down_kernel, total // rows, groups, rows, part * columns, size),
+        functools.partial(down_kernel, total // rows, groups, rows, size),
         in_specs=whole(2),
         out_specs=whole(len(groups)),
         out_shape=[jax.ShapeDtypeStruct((group * rows, columns), BF16) for group in groups],
@@ -326,7 +377,11 @@
         return lax.ppermute(x, "tp", crossing(members, bit))
 
     first = tokens
-    own, second = anchor(tokens, cross(tokens))
+    adapters, counts = adapter_per_block[None], block_token_count[None]
+    own, shrink, second = anchor(
+        adapters, tokens, jnp.swapaxes(shrink_matrices, 1, 2), cross(tokens)
+    )
+    other_shrink = cross(shrink)
     pieces, mine, theirs = [own, second], [], []
     for distance in range(1, reach + 1):
         first = step(first)
@@ -338,36 +393,42 @@
             theirs.append(cross(second))
     pieces = pieces + mine + theirs
 
-    adapters, counts = adapter_per_block[None], block_token_count[None]
-    rank = rank_of(adapters, pieces, jnp.swapaxes(shrink_matrices, 1, 2))
+    received = [0] + list(range(2, 2 + len(mine)))
+    rank, expand = rank_of(
+        adapters,
+        members,
+        received,
+        [pieces[i] for i in received],
+        shrink,
+        other_shrink,
+        expand_matrices,
+        theirs[:-1],
+    )
     work = [(gate_matrix, 0), (gate_matrix, 1), (up_matrix, 0), (up_matrix, 1)]
-    products, after = [], rank
-    bit = 1
+    products, after, bit = [], rank, 1
     while bit < members or work:
         if work:
             matrix, part = work.pop(0)
             products.append(product(pieces, matrix, part, 2, after))
         if bit < members:
             after = cross(rank, bit)
-            rank = jnp.concatenate([rank, after], axis=0)
+            rank = rank + after if bit == 1 else jnp.concatenate([rank, after], axis=0)
             bit *= 2
-    hidden = finish(adapters, products, rank, expand_matrices, span)
+    hidden = finish(products, rank, expand, 2 * span)
 
     slots = 2 * reach
     groups = [1] * slots + [1] + [2] * (reach - 1) + [1]
-    halves = []
-    for part in range(2):
-        outs = down(hidden, down_matrix, groups, rows, part, 2)
-        keep, give = outs[:slots], outs[slots:]
-        came = [cross(x) for x in give]
-        first = step(added(rows, (0, keep[0]), (0, came[0])))
-        second = None
-        for index in range(1, reach):
-            more = [] if second is None else [(0, second)]
-            second = step(added(rows, (0, keep[2 * index]), (rows, came[index]), *more))
-            first = step(added(rows, (0, keep[2 * index - 1]), (0, came[index]), (0, first)))
-        halves.append([keep[-1], came[-1], first, cross(second)])
-    return last(members, counts, halves)
+    outs = down(hidden, down_matrix, groups, rows)
+    keep, give = outs[:slots], outs[slots:]
+    came = [cross(give[0])]
+    came += [cross(tie(x, came[0])) for x in give[1:]]
+    first = step(added(rows, (0, keep[0]), (0, came[0])))
+    second = None
+    for index in range(1, reach):
+        more = [] if second is None else [(0, second)]
+        second = step(added(rows, (0, keep[2 * index]), (rows, came[index]), *more))
+        first = step(added(rows, (0, keep[2 * index - 1]), (0, came[index]), (0, first)))
+    return last(members, counts, [[keep[-1], came[-1], first, cross(second)]])
 
 
 def solution(mesh):

time: 82.2 us -> 83.3 us (1.013)
  starting transfers between devices: 46.4 us -> 31.7 us
  waiting for transfers between devices: 15.7 us -> 27.4 us
  local copies, waits for them, and re-layouts: 0.09 us -> 3.48 us
    ppermute x21 -> x14, starting transfers between devices: 35.9 us -> 23 us  [step(): return lax.ppermute(x, 'tp', ring)]
    ppermute x21 -> x14, waiting for transfers between devices: 13.1 us -> 25.8 us  [step(): return lax.ppermute(x, 'tp', ring)]
    unnamed x30 -> x28, local copies, waits for them, and re-layouts: 0.08 us -> 3.48 us
    ppermute x24 -> x19, starting transfers between devices: 10.5 us -> 8.75 us  [cross(): return lax.ppermute(x, 'tp', crossing(members, bit))]
    ppermute x24 -> x19, waiting for transfers between devices: 2.6 us -> 1.61 us  [cross(): return lax.ppermute(x, 'tp', crossing(members, bit))]
    pallas_call x3 -> x7, Pallas kernels: 3.42 us -> 4.17 us  [the longest x1 1.77 us: rank_of(): pl.pallas_call(functools.partial(rank_kernel, members, numbers), in_specs...]
    pallas_call x2 -> x1, Pallas kernels: 5.01 us -> 4.85 us  [down(): pl.pallas_call(functools.partial(down_kernel, total // rows, groups, rows...]
  transfers between devices with their start and end apart: 45 -> 33, of which waited for: 15 -> 15; matrix products, arithmetic and copies ran while one was open for 0% -> 0% of each run, Pallas kernels for 17% -> 16%
where the time goes in v8:
time: 83.3 us; the launch traced here: 83.1 us
  starting transfers between devices  31.7 us (38%)
  waiting for transfers between devices  27.4 us (33%)
  Pallas kernels  20.2 us (24%)
  local copies, waits for them, and re-layouts  3.48 us (4%)
    ppermute x14, waiting for transfers between devices, step(): return lax.ppermute(x, 'tp', ring)  25.8 us
    ppermute x14, starting transfers between devices, step(): return lax.ppermute(x, 'tp', ring)  23 us
    pallas_call x4, Pallas kernels, product(): pl.pallas_call(functools.partial(product_kernel, part * depth), in_specs=...  9.53 us
    ppermute x19, starting transfers between devices, cross(): return lax.ppermute(x, 'tp', crossing(members, bit))  8.75 us
    pallas_call x1, Pallas kernels, down(): pl.pallas_call(functools.partial(down_kernel, total // rows, groups, rows...  4.85 us
    unnamed x28, local copies, waits for them, and re-layouts  3.48 us
    pallas_call x1, Pallas kernels, rank_of(): pl.pallas_call(functools.partial(rank_kernel, members, numbers), in_specs...  1.77 us
  transfers between devices with their start and end apart: 33, of which 15 were waited for; matrix products, arithmetic and copies ran while one was open for 0% of the time, Pallas kernels for 16%

profile of v8, /device:TPU:0, one launch (start us, length us, event | category | flops | bytes accessed | tf_op | source)
XLA Modules:
  0.0 83.1 jit_solution(1548699332340400221)
XLA Ops:
  0.0 0.5 collective-permute-start
  0.5 2.6 %collective-permute-start.1 = (bf16[16,8192]{1,0:T(8,128)(2,1)}, bf16[16,8192]{1,0:T(8,128)(2,1)S(1)}, u32[]{:S(2)}, u32[]{:S(2)}) collective-permute-start(bf16[16,8192]{1,0:T(8,128)(2,1)} %tokens_ref.1), channel_id=1, source_target_pairs={{0,4},{1,3},{4,8},{5,1},{8,12},{9,5},{12,14},{13,9},{14,10},{15,13... | collective-permute-start | bytes 786440 | tf_op jit(solution)/shard_map/ppermute | solution.py:374
  3.0 0.8 copy-done
  3.8 1.6 %anchor.1 = (bf16[16,8192]{1,0:T(8,128)(2,1)S(1)}, bf16[2,8,8192]{2,1,0:T(8,128)(2,1)S(1)}, bf16[16,8192]{1,0:T(8,128)(2,1)S(1)}) custom-call(s32[1,2]{1,0:T(1,128)S(1)} %bitcast.9, bf16[16,8192]{1,0:T(8,128)(2,1)} %tokens_ref.1, bf16[8,8,8192]{2,1,0:T(8,128)(2,1)} %bitcast.12, ...), custom_call_target="tpu_custom_call", output_to_operand_aliasing={{2}: (3, {})} | custom-call | flops 30000001024 | tf_op jit(solution)/shard_map/anchor/pallas_call | solution.py:110
  5.4 1.8 %collective-permute-start.2 = (bf16[16,8192]{1,0:T(8,128)(2,1)S(1)}, bf16[16,8192]{1,0:T(8,128)(2,1)S(1)}, u32[]{:S(2)}, u32[]{:S(2)}) collective-permute-start(bf16[16,8192]{1,0:T(8,128)(2,1)S(1)} %get-tuple-element.24.refs_1_), channel_id=1, source_target_pairs={{0,4},{1,3},{4,8},{5,1},{8,12},{9,5},{12,14},{13,9},{14,10},{15,13... | collective-permute-start | bytes 786440 | tf_op jit(solution)/shard_map/ppermute | solution.py:374
  7.2 0.3 collective-permute-done.1.refs_1_.refs_2_
  7.5 2.1 %collective-permute-start.3 = (bf16[16,8192]{1,0:T(8,128)(2,1)S(1)}, bf16[16,8192]{1,0:T(8,128)(2,1)S(1)}, u32[]{:S(2)}, u32[]{:S(2)}) collective-permute-start(bf16[16,8192]{1,0:T(8,128)(2,1)S(1)} %collective-permute-done.1.refs_1_.refs_2_), channel_id=1, source_target_pairs={{0,4},{1,3},{4,8},{5,1},{8,12},{9,5},{12,14},{13,9},{14,10},{15,13... | collective-permute-start | bytes 786440 | tf_op jit(solution)/shard_map/ppermute | solution.py:374
  9.6 2.3 %collective-permute-done.2.refs_2_.refs_3_ = bf16[16,8192]{1,0:T(8,128)(2,1)S(1)} collective-permute-done((bf16[16,8192]{1,0:T(8,128)(2,1)S(1)}, bf16[16,8192]{1,0:T(8,128)(2,1)S(1)}, u32[]{:S(2)}, u32[]{:S(2)}) %collective-permute-start.2) | collective-permute-done | bytes 262176 | tf_op jit(solution)/shard_map/ppermute | solution.py:374
  11.9 1.7 %collective-permute-start.4 = (bf16[16,8192]{1,0:T(8,128)(2,1)S(1)}, bf16[16,8192]{1,0:T(8,128)(2,1)S(1)}, u32[]{:S(2)}, u32[]{:S(2)}) collective-permute-start(bf16[16,8192]{1,0:T(8,128)(2,1)S(1)} %collective-permute-done.2.refs_2_.refs_3_), channel_id=1, source_target_pairs={{0,4},{1,3},{4,8},{5,1},{8,12},{9,5},{12,14},{13,9},{14,10},{15,13... | collective-permute-start | bytes 786440 | tf_op jit(solution)/shard_map/ppermute | solution.py:374
  13.6 1.1 %collective-permute-done.3.refs_3_.refs_4_ = bf16[16,8192]{1,0:T(8,128)(2,1)S(1)} collective-permute-done((bf16[16,8192]{1,0:T(8,128)(2,1)S(1)}, bf16[16,8192]{1,0:T(8,128)(2,1)S(1)}, u32[]{:S(2)}, u32[]{:S(2)}) %collective-permute-start.3) | collective-permute-done | bytes 262176 | tf_op jit(solution)/shard_map/ppermute | solution.py:374
  14.7 1.7 %collective-permute-start.5 = (bf16[16,8192]{1,0:T(8,128)(2,1)S(1)}, bf16[16,8192]{1,0:T(8,128)(2,1)S(1)}, u32[]{:S(2)}, u32[]{:S(2)}) collective-permute-start(bf16[16,8192]{1,0:T(8,128)(2,1)S(1)} %collective-permute-done.3.refs_3_.refs_4_), channel_id=1, source_target_pairs={{0,4},{1,3},{4,8},{5,1},{8,12},{9,5},{12,14},{13,9},{14,10},{15,13... | collective-permute-start | bytes 786440 | tf_op jit(solution)/shard_map/ppermute | solution.py:374
  16.4 0.5 collective-permute-start.15
  16.9 1.3 %collective-permute-done.4.refs_4_.refs_5_ = bf16[16,8192]{1,0:T(8,128)(2,1)S(1)} collective-permute-done((bf16[16,8192]{1,0:T(8,128)(2,1)S(1)}, bf16[16,8192]{1,0:T(8,128)(2,1)S(1)}, u32[]{:S(2)}, u32[]{:S(2)}) %collective-permute-start.4) | collective-permute-done | bytes 262176 | tf_op jit(solution)/shard_map/ppermute | solution.py:374
  18.2 1.7 %collective-permute-start.6 = (bf16[16,8192]{1,0:T(8,128)(2,1)S(1)}, bf16[16,8192]{1,0:T(8,128)(2,1)S(1)}, u32[]{:S(2)}, u32[]{:S(2)}) collective-permute-start(bf16[16,8192]{1,0:T(8,128)(2,1)S(1)} %collective-permute-done.4.refs_4_.refs_5_), channel_id=1, source_target_pairs={{0,4},{1,3},{4,8},{5,1},{8,12},{9,5},{12,14},{13,9},{14,10},{15,13... | collective-permute-start | bytes 786440 | tf_op jit(solution)/shard_map/ppermute | solution.py:374
  20.0 1.1 %collective-permute-done.5.refs_5_.refs_6_ = bf16[16,8192]{1,0:T(8,128)(2,1)S(1)} collective-permute-done((bf16[16,8192]{1,0:T(8,128)(2,1)S(1)}, bf16[16,8192]{1,0:T(8,128)(2,1)S(1)}, u32[]{:S(2)}, u32[]{:S(2)}) %collective-permute-start.5) | collective-permute-done | bytes 262176 | tf_op jit(solution)/shard_map/ppermute | solution.py:374
  21.0 1.7 %collective-permute-start.7 = (bf16[16,8192]{1,0:T(8,128)(2,1)S(1)}, bf16[16,8192]{1,0:T(8,128)(2,1)S(1)}, u32[]{:S(2)}, u32[]{:S(2)}) collective-permute-start(bf16[16,8192]{1,0:T(8,128)(2,1)S(1)} %collective-permute-done.5.refs_5_.refs_6_), channel_id=1, source_target_pairs={{0,4},{1,3},{4,8},{5,1},{8,12},{9,5},{12,14},{13,9},{14,10},{15,13... | collective-permute-start | bytes 786440 | tf_op jit(solution)/shard_map/ppermute | solution.py:374
  22.8 0.5 collective-permute-start.11
  23.3 0.1 collective-permute-start.12
  23.4 1.2 %collective-permute-done.6.refs_6_.refs_7_ = bf16[16,8192]{1,0:T(8,128)(2,1)S(1)} collective-permute-done((bf16[16,8192]{1,0:T(8,128)(2,1)S(1)}, bf16[16,8192]{1,0:T(8,128)(2,1)S(1)}, u32[]{:S(2)}, u32[]{:S(2)}) %collective-permute-start.6) | collective-permute-done | bytes 262176 | tf_op jit(solution)/shard_map/ppermute | solution.py:374
  24.6 2.8 %collective-permute-done.7.refs_7_.refs_8_ = bf16[16,8192]{1,0:T(8,128)(2,1)S(1)} collective-permute-done((bf16[16,8192]{1,0:T(8,128)(2,1)S(1)}, bf16[16,8192]{1,0:T(8,128)(2,1)S(1)}, u32[]{:S(2)}, u32[]{:S(2)}) %collective-permute-start.7) | collective-permute-done | bytes 262176 | tf_op jit(solution)/shard_map/ppermute | solution.py:374
  27.5 1.8 %rank.1 = (bf16[16,256]{1,0:T(8,128)(2,1)S(1)}, bf16[2,128,896]{2,1,0:T(8,128)(2,1)S(1)}) custom-call(s32[1,2]{1,0:T(1,128)S(1)} %bitcast.10, bf16[8,128,896]{2,1,0:T(8,128)(2,1)} %expand_ref.1, bf16[2,8,8192]{2,1,0:T(8,128)(2,1)S(1)} %get-tuple-element.25.own_ref, bf16[2,8,8192]{2,1,0:T(8,128)(2,1)S(1)} %collective-permute-done.15.other_ref, ...), custom_call_target="tpu_custom_call" | custom-call | flops 67108864 | bytes 4194304 | tf_op jit(solution)/shard_map/rank/pallas_call | solution.py:185
  29.2 0.6 collective-permute-start.16
  29.8 0.0 slice-start.4
  29.8 0.0 slice-start.5
  29.9 2.4 %product.4.gate_a = f32[256,896]{1,0:T(8,128)S(1)} custom-call(bf16[8192,896]{1,0:T(8,128)(2,1)S(1)} %bitcast.4, bf16[16,8192]{1,0:T(8,128)(2,1)S(1)} %get-tuple-element.23.refs_0_, bf16[16,8192]{1,0:T(8,128)(2,1)S(1)} %get-tuple-element.24.refs_1_, bf16[16,8192]{1,0:T(8,128)(2,1)S(1)} %collective-permute-done.1.refs_1_.refs_2_, ...), custom_call_target="tpu_custom_call" | custom-call | flops 1879048192 | bytes 9437184 | tf_op jit(solution)/shard_map/product/pallas_call | solution.py:222
  32.3 0.0 slice-start.6
  32.3 1.7 %collective-permute-start.17 = (bf16[16,256]{1,0:T(8,128)(2,1)S(1)}, bf16[16,256]{1,0:T(8,128)(2,1)S(1)}, u32[]{:S(2)}, u32[]{:S(2)}) collective-permute-start(bf16[16,256]{1,0:T(8,128)(2,1)S(1)} %add.3), channel_id=1, source_target_pairs={{0,2},{1,3},{2,0},{3,1},{4,6},{5,7},{6,4},{7,5},{8,10},{9,11},{10,... | collective-permute-start | bytes 24584 | tf_op jit(solution)/shard_map/ppermute | solution.py:377
  34.0 2.4 %product.5.gate_b = f32[256,896]{1,0:T(8,128)S(1)} custom-call(bf16[8192,896]{1,0:T(8,128)(2,1)S(1)} %bitcast.4, bf16[16,8192]{1,0:T(8,128)(2,1)S(1)} %get-tuple-element.23.refs_0_, bf16[16,8192]{1,0:T(8,128)(2,1)S(1)} %get-tuple-element.24.refs_1_, bf16[16,8192]{1,0:T(8,128)(2,1)S(1)} %collective-permute-done.1.refs_1_.refs_2_, ...), custom_call_target="tpu_custom_call" | custom-call | flops 1879048192 | bytes 9437184 | tf_op jit(solution)/shard_map/product/pallas_call | solution.py:222
  36.5 1.6 %collective-permute-start.18 = (bf16[32,256]{1,0:T(8,128)(2,1)S(1)}, bf16[32,256]{1,0:T(8,128)(2,1)S(1)}, u32[]{:S(2)}, u32[]{:S(2)}) collective-permute-start(bf16[32,256]{1,0:T(8,128)(2,1)S(1)} %pad_maximum_fusion.2), channel_id=1, source_target_pairs={{0,4},{1,5},{2,6},{3,7},{4,0},{5,1},{6,2},{7,3},{8,12},{9,13},{10,... | collective-permute-start | bytes 49160 | tf_op jit(solution)/shard_map/ppermute | solution.py:377
  38.1 2.4 %product.6.up_a = f32[256,896]{1,0:T(8,128)S(1)} custom-call(bf16[8192,896]{1,0:T(8,128)(2,1)S(1)} %bitcast.6, bf16[16,8192]{1,0:T(8,128)(2,1)S(1)} %get-tuple-element.23.refs_0_, bf16[16,8192]{1,0:T(8,128)(2,1)S(1)} %get-tuple-element.24.refs_1_, bf16[16,8192]{1,0:T(8,128)(2,1)S(1)} %collective-permute-done.1.refs_1_.refs_2_, ...), custom_call_target="tpu_custom_call" | custom-call | flops 1879048192 | bytes 9437184 | tf_op jit(solution)/shard_map/product/pallas_call | solution.py:222
  40.5 2.7 %collective-permute-start.19 = (bf16[64,256]{1,0:T(8,128)(2,1)S(1)}, bf16[64,256]{1,0:T(8,128)(2,1)S(1)}, u32[]{:S(2)}, u32[]{:S(2)}) collective-permute-start(bf16[64,256]{1,0:T(8,128)(2,1)S(1)} %pad_maximum_fusion.1), channel_id=1, source_target_pairs={{0,8},{1,9},{2,10},{3,11},{4,12},{5,13},{6,14},{7,15},{8,0},{9,1},... | collective-permute-start | bytes 98312 | tf_op jit(solution)/shard_map/ppermute | solution.py:377
  43.2 2.4 %product.7.up_b = f32[256,896]{1,0:T(8,128)S(1)} custom-call(bf16[8192,896]{1,0:T(8,128)(2,1)S(1)} %bitcast.6, bf16[16,8192]{1,0:T(8,128)(2,1)S(1)} %get-tuple-element.23.refs_0_, bf16[16,8192]{1,0:T(8,128)(2,1)S(1)} %get-tuple-element.24.refs_1_, bf16[16,8192]{1,0:T(8,128)(2,1)S(1)} %collective-permute-done.1.refs_1_.refs_2_, ...), custom_call_target="tpu_custom_call" | custom-call | flops 1879048192 | bytes 9437184 | tf_op jit(solution)/shard_map/product/pallas_call | solution.py:222
  45.6 0.0 slice-start.10
  45.6 0.8 finish.1.hidden_ref
  46.5 1.4 %slice-done.10 = s8[4194304]{0:T(1024)(128)(4,1)S(1)} async-done(((s8[14680064]{0:T(1024)(128)(4,1)}), s8[4194304]{0:T(1024)(128)(4,1)S(1)}, s32[]{:S(2)}) %slice-start.10) | async-done | bytes 4194328
  47.9 1.2 %slice-done.11 = s8[4194304]{0:T(1024)(128)(4,1)S(1)} async-done(((s8[14680064]{0:T(1024)(128)(4,1)}), s8[4194304]{0:T(1024)(128)(4,1)S(1)}, s32[]{:S(2)}) %slice-start.11) | async-done | bytes 4194328
  49.1 4.8 %down.1 = (bf16[16,8192]{1,0:T(8,128)(2,1)S(1)}, bf16[16,8192]{1,0:T(8,128)(2,1)S(1)}, bf16[16,8192]{1,0:T(8,128)(2,1)S(1)}, bf16[16,8192]{1,0:T(8,128)(2,1)S(1)...) custom-call(bf16[896,8192]{1,0:T(8,128)(2,1)S(1)} %bitcast.8, ...), custom_call_target="tpu_custom_call" | custom-call | flops 3758096384 | bytes 18874368 | tf_op jit(solution)/shard_map/down/pallas_call | solution.py:289
  53.9 0.1 collective-permute-start.20
  54.0 1.5 %collective-permute-done.20.after_ref.refs_1_ = bf16[16,8192]{1,0:T(8,128)(2,1)S(1)} collective-permute-done((bf16[16,8192]{1,0:T(8,128)(2,1)S(1)}, bf16[16,8192]{1,0:T(8,128)(2,1)S(1)}, u32[]{:S(2)}, u32[]{:S(2)}) %collective-permute-start.20) | collective-permute-done | bytes 262176 | tf_op jit(solution)/shard_map/ppermute | solution.py:377
  55.5 0.1 collective-permute-start.24
  55.7 0.4 collective-permute-start.23
  56.1 0.1 added.7
  56.1 1.3 %collective-permute-start.25 = (bf16[16,8192]{1,0:T(8,128)(2,1)S(1)}, bf16[16,8192]{1,0:T(8,128)(2,1)S(1)}, u32[]{:S(2)}, u32[]{:S(2)}) collective-permute-start(bf16[16,8192]{1,0:T(8,128)(2,1)S(1)} %added.7), channel_id=1, source_target_pairs={{0,4},{1,3},{4,8},{5,1},{8,12},{9,5},{12,14},{13,9},{14,10},{15,13... | collective-permute-start | bytes 786440 | tf_op jit(solution)/shard_map/ppermute | solution.py:374
  57.4 0.0 collective-permute-done.24.refs_1_
  57.5 0.1 added.11
  57.5 1.8 %collective-permute-start.29 = (bf16[16,8192]{1,0:T(8,128)(2,1)S(1)}, bf16[16,8192]{1,0:T(8,128)(2,1)S(1)}, u32[]{:S(2)}, u32[]{:S(2)}) collective-permute-start(bf16[16,8192]{1,0:T(8,128)(2,1)S(1)} %added.11), channel_id=1, source_target_pairs={{0,4},{1,3},{4,8},{5,1},{8,12},{9,5},{12,14},{13,9},{14,10},{15,13... | collective-permute-start | bytes 786440 | tf_op jit(solution)/shard_map/ppermute | solution.py:374
  59.4 3.2 %collective-permute-done.25.refs_2_ = bf16[16,8192]{1,0:T(8,128)(2,1)S(1)} collective-permute-done((bf16[16,8192]{1,0:T(8,128)(2,1)S(1)}, bf16[16,8192]{1,0:T(8,128)(2,1)S(1)}, u32[]{:S(2)}, u32[]{:S(2)}) %collective-permute-start.25) | collective-permute-done | bytes 262176 | tf_op jit(solution)/shard_map/ppermute | solution.py:374
  62.6 0.1 added.8
  62.7 1.3 %collective-permute-start.26 = (bf16[16,8192]{1,0:T(8,128)(2,1)S(1)}, bf16[16,8192]{1,0:T(8,128)(2,1)S(1)}, u32[]{:S(2)}, u32[]{:S(2)}) collective-permute-start(bf16[16,8192]{1,0:T(8,128)(2,1)S(1)} %added.8), channel_id=1, source_target_pairs={{0,4},{1,3},{4,8},{5,1},{8,12},{9,5},{12,14},{13,9},{14,10},{15,13... | collective-permute-start | bytes 786440 | tf_op jit(solution)/shard_map/ppermute | solution.py:374
  63.9 1.4 %collective-permute-done.29.refs_2_ = bf16[16,8192]{1,0:T(8,128)(2,1)S(1)} collective-permute-done((bf16[16,8192]{1,0:T(8,128)(2,1)S(1)}, bf16[16,8192]{1,0:T(8,128)(2,1)S(1)}, u32[]{:S(2)}, u32[]{:S(2)}) %collective-permute-start.29) | collective-permute-done | bytes 262176 | tf_op jit(solution)/shard_map/ppermute | solution.py:374
  65.4 0.1 added.12
  65.5 1.3 %collective-permute-start.30 = (bf16[16,8192]{1,0:T(8,128)(2,1)S(1)}, bf16[16,8192]{1,0:T(8,128)(2,1)S(1)}, u32[]{:S(2)}, u32[]{:S(2)}) collective-permute-start(bf16[16,8192]{1,0:T(8,128)(2,1)S(1)} %added.12), channel_id=1, source_target_pairs={{0,4},{1,3},{4,8},{5,1},{8,12},{9,5},{12,14},{13,9},{14,10},{15,13... | collective-permute-start | bytes 786440 | tf_op jit(solution)/shard_map/ppermute | solution.py:374
  66.8 2.3 %collective-permute-done.26.refs_2_ = bf16[16,8192]{1,0:T(8,128)(2,1)S(1)} collective-permute-done((bf16[16,8192]{1,0:T(8,128)(2,1)S(1)}, bf16[16,8192]{1,0:T(8,128)(2,1)S(1)}, u32[]{:S(2)}, u32[]{:S(2)}) %collective-permute-start.26) | collective-permute-done | bytes 262176 | tf_op jit(solution)/shard_map/ppermute | solution.py:374
  69.1 0.1 added.9
  69.2 1.3 %collective-permute-start.27 = (bf16[16,8192]{1,0:T(8,128)(2,1)S(1)}, bf16[16,8192]{1,0:T(8,128)(2,1)S(1)}, u32[]{:S(2)}, u32[]{:S(2)}) collective-permute-start(bf16[16,8192]{1,0:T(8,128)(2,1)S(1)} %added.9), channel_id=1, source_target_pairs={{0,4},{1,3},{4,8},{5,1},{8,12},{9,5},{12,14},{13,9},{14,10},{15,13... | collective-permute-start | bytes 786440 | tf_op jit(solution)/shard_map/ppermute | solution.py:374
  70.5 1.4 %collective-permute-done.30.refs_2_ = bf16[16,8192]{1,0:T(8,128)(2,1)S(1)} collective-permute-done((bf16[16,8192]{1,0:T(8,128)(2,1)S(1)}, bf16[16,8192]{1,0:T(8,128)(2,1)S(1)}, u32[]{:S(2)}, u32[]{:S(2)}) %collective-permute-start.30) | collective-permute-done | bytes 262176 | tf_op jit(solution)/shard_map/ppermute | solution.py:374
  71.9 0.1 added.13
  72.0 1.3 %collective-permute-start.31 = (bf16[16,8192]{1,0:T(8,128)(2,1)S(1)}, bf16[16,8192]{1,0:T(8,128)(2,1)S(1)}, u32[]{:S(2)}, u32[]{:S(2)}) collective-permute-start(bf16[16,8192]{1,0:T(8,128)(2,1)S(1)} %added.13), channel_id=1, source_target_pairs={{0,4},{1,3},{4,8},{5,1},{8,12},{9,5},{12,14},{13,9},{14,10},{15,13... | collective-permute-start | bytes 786440 | tf_op jit(solution)/shard_map/ppermute | solution.py:374
  73.3 2.3 %collective-permute-done.27.refs_2_ = bf16[16,8192]{1,0:T(8,128)(2,1)S(1)} collective-permute-done((bf16[16,8192]{1,0:T(8,128)(2,1)S(1)}, bf16[16,8192]{1,0:T(8,128)(2,1)S(1)}, u32[]{:S(2)}, u32[]{:S(2)}) %collective-permute-start.27) | collective-permute-done | bytes 262176 | tf_op jit(solution)/shard_map/ppermute | solution.py:374
  75.6 0.1 added.10
  75.7 1.3 %collective-permute-start.28 = (bf16[16,8192]{1,0:T(8,128)(2,1)S(1)}, bf16[16,8192]{1,0:T(8,128)(2,1)S(1)}, u32[]{:S(2)}, u32[]{:S(2)}) collective-permute-start(bf16[16,8192]{1,0:T(8,128)(2,1)S(1)} %added.10), channel_id=1, source_target_pairs={{0,4},{1,3},{4,8},{5,1},{8,12},{9,5},{12,14},{13,9},{14,10},{15,13... | collective-permute-start | bytes 786440 | tf_op jit(solution)/shard_map/ppermute | solution.py:374
  77.0 1.4 %collective-permute-done.31 = bf16[16,8192]{1,0:T(8,128)(2,1)S(1)} collective-permute-done((bf16[16,8192]{1,0:T(8,128)(2,1)S(1)}, bf16[16,8192]{1,0:T(8,128)(2,1)S(1)}, u32[]{:S(2)}, u32[]{:S(2)}) %collective-permute-start.31) | collective-permute-done | bytes 262176 | tf_op jit(solution)/shard_map/ppermute | solution.py:374
  78.4 3.7 %collective-permute-done.28.refs_2_ = bf16[16,8192]{1,0:T(8,128)(2,1)S(1)} collective-permute-done((bf16[16,8192]{1,0:T(8,128)(2,1)S(1)}, bf16[16,8192]{1,0:T(8,128)(2,1)S(1)}, u32[]{:S(2)}, u32[]{:S(2)}) %collective-permute-start.28) | collective-permute-done | bytes 262176 | tf_op jit(solution)/shard_map/ppermute | solution.py:374
  82.1 1.0 %last.1 = bf16[16,8192]{1,0:T(8,128)(2,1)} custom-call(s32[1,2]{1,0:T(1,128)S(1)} %bitcast.11, bf16[16,8192]{1,0:T(8,128)(2,1)S(1)} %get-tuple-element.28.refs_0_, bf16[16,8192]{1,0:T(8,128)(2,1)S(1)} %collective-permute-done.21.refs_1_, bf16[16,8192]{1,0:T(8,128)(2,1)S(1)} %collective-permute-done.28.refs_2_, ...), custom_call_target="tpu_custom_call" | custom-call | tf_op jit(solution)/shard_map/last/pallas_call | solution.py:324
  (57 shorter events, 0.1 us)
Async XLA Ops:
  0.0 3.0 %collective-permute-start = (bf16[16,8192]{1,0:T(8,128)(2,1)}, bf16[16,8192]{1,0:T(8,128)(2,1)S(1)}, u32[]{:S(2)}, u32[]{:S(2)}) collective-permute-start(bf16[16,8192]{1,0:T(8,128)(2,1)} %tokens_ref.1), channel_id=1, source_target_pairs={{0,1},{1,0},{2,3},{3,2},{4,5},{5,4},{6,7},{7,6},{8,9},{9,8},{10,11... | collective-permute-start | bytes 786440 | tf_op jit(solution)/shard_map/ppermute | solution.py:377
  0.5 7.1 %collective-permute-start.1 = (bf16[16,8192]{1,0:T(8,128)(2,1)}, bf16[16,8192]{1,0:T(8,128)(2,1)S(1)}, u32[]{:S(2)}, u32[]{:S(2)}) collective-permute-start(bf16[16,8192]{1,0:T(8,128)(2,1)} %tokens_ref.1), channel_id=1, source_target_pairs={{0,4},{1,3},{4,8},{5,1},{8,12},{9,5},{12,14},{13,9},{14,10},{15,13... | collective-permute-start | bytes 786440 | tf_op jit(solution)/shard_map/ppermute | solution.py:374
  3.0 26.8 %slice-start = ((s8[14680064]{0:T(1024)(128)(4,1)}), s8[4194304]{0:T(1024)(128)(4,1)S(1)}, s32[]{:S(2)}) async-start(s8[14680064]{0:T(1024)(128)(4,1)} %bitcast.3), calls=%async_computation | async-start | bytes 8388608
  3.0 0.8 copy-start
  3.8 26.0 %slice-start.1 = ((s8[14680064]{0:T(1024)(128)(4,1)}), s8[4194304]{0:T(1024)(128)(4,1)S(1)}, s32[]{:S(2)}) async-start(s8[14680064]{0:T(1024)(128)(4,1)} %bitcast.3), calls=%async_computation.1 | async-start | bytes 8388608
  3.8 26.0 %slice-start.2 = ((s8[14680064]{0:T(1024)(128)(4,1)}), s8[4194304]{0:T(1024)(128)(4,1)S(1)}, s32[]{:S(2)}) async-start(s8[14680064]{0:T(1024)(128)(4,1)} %bitcast.3), calls=%async_computation.2 | async-start | bytes 8388608
  3.8 26.0 %slice-start.3 = ((s8[14680064]{0:T(1024)(128)(4,1)}), s8[2097152]{0:T(1024)(128)(4,1)S(1)}, s32[]{:S(2)}) async-start(s8[14680064]{0:T(1024)(128)(4,1)} %bitcast.3), calls=%async_computation.3 | async-start | bytes 4194304
  5.4 6.4 %collective-permute-start.2 = (bf16[16,8192]{1,0:T(8,128)(2,1)S(1)}, bf16[16,8192]{1,0:T(8,128)(2,1)S(1)}, u32[]{:S(2)}, u32[]{:S(2)}) collective-permute-start(bf16[16,8192]{1,0:T(8,128)(2,1)S(1)} %get-tuple-element.24.refs_1_), channel_id=1, source_target_pairs={{0,4},{1,3},{4,8},{5,1},{8,12},{9,5},{12,14},{13,9},{14,10},{15,13... | collective-permute-start | bytes 786440 | tf_op jit(solution)/shard_map/ppermute | solution.py:374
  7.5 7.1 %collective-permute-start.3 = (bf16[16,8192]{1,0:T(8,128)(2,1)S(1)}, bf16[16,8192]{1,0:T(8,128)(2,1)S(1)}, u32[]{:S(2)}, u32[]{:S(2)}) collective-permute-start(bf16[16,8192]{1,0:T(8,128)(2,1)S(1)} %collective-permute-done.1.refs_1_.refs_2_), channel_id=1, source_target_pairs={{0,4},{1,3},{4,8},{5,1},{8,12},{9,5},{12,14},{13,9},{14,10},{15,13... | collective-permute-start | bytes 786440 | tf_op jit(solution)/shard_map/ppermute | solution.py:374
  11.9 6.4 %collective-permute-start.4 = (bf16[16,8192]{1,0:T(8,128)(2,1)S(1)}, bf16[16,8192]{1,0:T(8,128)(2,1)S(1)}, u32[]{:S(2)}, u32[]{:S(2)}) collective-permute-start(bf16[16,8192]{1,0:T(8,128)(2,1)S(1)} %collective-permute-done.2.refs_2_.refs_3_), channel_id=1, source_target_pairs={{0,4},{1,3},{4,8},{5,1},{8,12},{9,5},{12,14},{13,9},{14,10},{15,13... | collective-permute-start | bytes 786440 | tf_op jit(solution)/shard_map/ppermute | solution.py:374
  14.7 6.4 %collective-permute-start.5 = (bf16[16,8192]{1,0:T(8,128)(2,1)S(1)}, bf16[16,8192]{1,0:T(8,128)(2,1)S(1)}, u32[]{:S(2)}, u32[]{:S(2)}) collective-permute-start(bf16[16,8192]{1,0:T(8,128)(2,1)S(1)} %collective-permute-done.3.refs_3_.refs_4_), channel_id=1, source_target_pairs={{0,4},{1,3},{4,8},{5,1},{8,12},{9,5},{12,14},{13,9},{14,10},{15,13... | collective-permute-start | bytes 786440 | tf_op jit(solution)/shard_map/ppermute | solution.py:374
  16.4 6.4 %collective-permute-start.8 = (bf16[16,8192]{1,0:T(8,128)(2,1)S(1)}, bf16[16,8192]{1,0:T(8,128)(2,1)S(1)}, u32[]{:S(2)}, u32[]{:S(2)}) collective-permute-start(bf16[16,8192]{1,0:T(8,128)(2,1)S(1)} %collective-permute-done.1.refs_1_.refs_2_), channel_id=1, source_target_pairs={{0,1},{1,0},{2,3},{3,2},{4,5},{5,4},{6,7},{7,6},{8,9},{9,8},{10,11... | collective-permute-start | bytes 786440 | tf_op jit(solution)/shard_map/ppermute | solution.py:377
  16.4 6.4 %collective-permute-start.15 = (bf16[2,8,8192]{2,1,0:T(8,128)(2,1)S(1)}, bf16[2,8,8192]{2,1,0:T(8,128)(2,1)S(1)}, u32[]{:S(2)}, u32[]{:S(2)}) collective-permute-start(bf16[2,8,8192]{2,1,0:T(8,128)(2,1)S(1)} %get-tuple-element.25.own_ref), channel_id=1, source_target_pairs={{0,1},{1,0},{2,3},{3,2},{4,5},{5,4},{6,7},{7,6},{8,9},{9,8},{10,11... | collective-permute-start | bytes 786440 | tf_op jit(solution)/shard_map/ppermute | solution.py:377
  16.9 6.4 %collective-permute-start.9 = (bf16[16,8192]{1,0:T(8,128)(2,1)S(1)}, bf16[16,8192]{1,0:T(8,128)(2,1)S(1)}, u32[]{:S(2)}, u32[]{:S(2)}) collective-permute-start(bf16[16,8192]{1,0:T(8,128)(2,1)S(1)} %collective-permute-done.2.refs_2_.refs_3_), channel_id=1, source_target_pairs={{0,1},{1,0},{2,3},{3,2},{4,5},{5,4},{6,7},{7,6},{8,9},{9,8},{10,11... | collective-permute-start | bytes 786440 | tf_op jit(solution)/shard_map/ppermute | solution.py:377
  18.2 6.4 %collective-permute-start.6 = (bf16[16,8192]{1,0:T(8,128)(2,1)S(1)}, bf16[16,8192]{1,0:T(8,128)(2,1)S(1)}, u32[]{:S(2)}, u32[]{:S(2)}) collective-permute-start(bf16[16,8192]{1,0:T(8,128)(2,1)S(1)} %collective-permute-done.4.refs_4_.refs_5_), channel_id=1, source_target_pairs={{0,4},{1,3},{4,8},{5,1},{8,12},{9,5},{12,14},{13,9},{14,10},{15,13... | collective-permute-start | bytes 786440 | tf_op jit(solution)/shard_map/ppermute | solution.py:374
  21.0 6.4 %collective-permute-start.7 = (bf16[16,8192]{1,0:T(8,128)(2,1)S(1)}, bf16[16,8192]{1,0:T(8,128)(2,1)S(1)}, u32[]{:S(2)}, u32[]{:S(2)}) collective-permute-start(bf16[16,8192]{1,0:T(8,128)(2,1)S(1)} %collective-permute-done.5.refs_5_.refs_6_), channel_id=1, source_target_pairs={{0,4},{1,3},{4,8},{5,1},{8,12},{9,5},{12,14},{13,9},{14,10},{15,13... | collective-permute-start | bytes 786440 | tf_op jit(solution)/shard_map/ppermute | solution.py:374
  22.8 4.6 %collective-permute-start.10 = (bf16[16,8192]{1,0:T(8,128)(2,1)S(1)}, bf16[16,8192]{1,0:T(8,128)(2,1)S(1)}, u32[]{:S(2)}, u32[]{:S(2)}) collective-permute-start(bf16[16,8192]{1,0:T(8,128)(2,1)S(1)} %collective-permute-done.3.refs_3_.refs_4_), channel_id=1, source_target_pairs={{0,1},{1,0},{2,3},{3,2},{4,5},{5,4},{6,7},{7,6},{8,9},{9,8},{10,11... | collective-permute-start | bytes 786440 | tf_op jit(solution)/shard_map/ppermute | solution.py:377
  22.8 4.6 %collective-permute-start.11 = (bf16[16,8192]{1,0:T(8,128)(2,1)S(1)}, bf16[16,8192]{1,0:T(8,128)(2,1)S(1)}, u32[]{:S(2)}, u32[]{:S(2)}) collective-permute-start(bf16[16,8192]{1,0:T(8,128)(2,1)S(1)} %collective-permute-done.4.refs_4_.refs_5_), channel_id=1, source_target_pairs={{0,1},{1,0},{2,3},{3,2},{4,5},{5,4},{6,7},{7,6},{8,9},{9,8},{10,11... | collective-permute-start | bytes 786440 | tf_op jit(solution)/shard_map/ppermute | solution.py:377
  23.3 4.1 %collective-permute-start.12 = (bf16[16,8192]{1,0:T(8,128)(2,1)S(1)}, bf16[16,8192]{1,0:T(8,128)(2,1)S(1)}, u32[]{:S(2)}, u32[]{:S(2)}) collective-permute-start(bf16[16,8192]{1,0:T(8,128)(2,1)S(1)} %collective-permute-done.5.refs_5_.refs_6_), channel_id=1, source_target_pairs={{0,1},{1,0},{2,3},{3,2},{4,5},{5,4},{6,7},{7,6},{8,9},{9,8},{10,11... | collective-permute-start | bytes 786440 | tf_op jit(solution)/shard_map/ppermute | solution.py:377
  24.6 2.8 %collective-permute-start.13 = (bf16[16,8192]{1,0:T(8,128)(2,1)S(1)}, bf16[16,8192]{1,0:T(8,128)(2,1)S(1)}, u32[]{:S(2)}, u32[]{:S(2)}) collective-permute-start(bf16[16,8192]{1,0:T(8,128)(2,1)S(1)} %collective-permute-done.6.refs_6_.refs_7_), channel_id=1, source_target_pairs={{0,1},{1,0},{2,3},{3,2},{4,5},{5,4},{6,7},{7,6},{8,9},{9,8},{10,11... | collective-permute-start | bytes 786440 | tf_op jit(solution)/shard_map/ppermute | solution.py:377
  27.4 2.4 %collective-permute-start.14 = (bf16[16,8192]{1,0:T(8,128)(2,1)S(1)}, bf16[16,8192]{1,0:T(8,128)(2,1)S(1)}, u32[]{:S(2)}, u32[]{:S(2)}) collective-permute-start(bf16[16,8192]{1,0:T(8,128)(2,1)S(1)} %collective-permute-done.7.refs_7_.refs_8_), channel_id=1, source_target_pairs={{0,1},{1,0},{2,3},{3,2},{4,5},{5,4},{6,7},{7,6},{8,9},{9,8},{10,11... | collective-permute-start | bytes 786440 | tf_op jit(solution)/shard_map/ppermute | solution.py:377
  29.2 3.0 %collective-permute-start.16 = (bf16[16,256]{1,0:T(8,128)(2,1)S(1)}, bf16[16,256]{1,0:T(8,128)(2,1)S(1)}, u32[]{:S(2)}, u32[]{:S(2)}) collective-permute-start(bf16[16,256]{1,0:T(8,128)(2,1)S(1)} %get-tuple-element.26.refs_16_), channel_id=1, source_target_pairs={{0,1},{1,0},{2,3},{3,2},{4,5},{5,4},{6,7},{7,6},{8,9},{9,8},{10,11... | collective-permute-start | bytes 24584 | tf_op jit(solution)/shard_map/ppermute | solution.py:377
  29.8 8.3 %slice-start.4 = ((s8[14680064]{0:T(1024)(128)(4,1)}), s8[4194304]{0:T(1024)(128)(4,1)S(1)}, s32[]{:S(2)}) async-start(s8[14680064]{0:T(1024)(128)(4,1)} %bitcast.5), calls=%async_computation.4 | async-start | bytes 8388608
  29.8 8.3 %slice-start.5 = ((s8[14680064]{0:T(1024)(128)(4,1)}), s8[4194304]{0:T(1024)(128)(4,1)S(1)}, s32[]{:S(2)}) async-start(s8[14680064]{0:T(1024)(128)(4,1)} %bitcast.5), calls=%async_computation.5 | async-start | bytes 8388608
  32.3 5.8 %slice-start.6 = ((s8[14680064]{0:T(1024)(128)(4,1)}), s8[4194304]{0:T(1024)(128)(4,1)S(1)}, s32[]{:S(2)}) async-start(s8[14680064]{0:T(1024)(128)(4,1)} %bitcast.5), calls=%async_computation.6 | async-start | bytes 8388608
  32.3 5.8 %slice-start.7 = ((s8[14680064]{0:T(1024)(128)(4,1)}), s8[2097152]{0:T(1024)(128)(4,1)S(1)}, s32[]{:S(2)}) async-start(s8[14680064]{0:T(1024)(128)(4,1)} %bitcast.5), calls=%async_computation.7 | async-start | bytes 4194304
  32.3 4.1 %collective-permute-start.17 = (bf16[16,256]{1,0:T(8,128)(2,1)S(1)}, bf16[16,256]{1,0:T(8,128)(2,1)S(1)}, u32[]{:S(2)}, u32[]{:S(2)}) collective-permute-start(bf16[16,256]{1,0:T(8,128)(2,1)S(1)} %add.3), channel_id=1, source_target_pairs={{0,2},{1,3},{2,0},{3,1},{4,6},{5,7},{6,4},{7,5},{8,10},{9,11},{10,... | collective-permute-start | bytes 24584 | tf_op jit(solution)/shard_map/ppermute | solution.py:377
  36.5 4.1 %collective-permute-start.18 = (bf16[32,256]{1,0:T(8,128)(2,1)S(1)}, bf16[32,256]{1,0:T(8,128)(2,1)S(1)}, u32[]{:S(2)}, u32[]{:S(2)}) collective-permute-start(bf16[32,256]{1,0:T(8,128)(2,1)S(1)} %pad_maximum_fusion.2), channel_id=1, source_target_pairs={{0,4},{1,5},{2,6},{3,7},{4,0},{5,1},{6,2},{7,3},{8,12},{9,13},{10,... | collective-permute-start | bytes 49160 | tf_op jit(solution)/shard_map/ppermute | solution.py:377
  40.5 5.0 %collective-permute-start.19 = (bf16[64,256]{1,0:T(8,128)(2,1)S(1)}, bf16[64,256]{1,0:T(8,128)(2,1)S(1)}, u32[]{:S(2)}, u32[]{:S(2)}) collective-permute-start(bf16[64,256]{1,0:T(8,128)(2,1)S(1)} %pad_maximum_fusion.1), channel_id=1, source_target_pairs={{0,8},{1,9},{2,10},{3,11},{4,12},{5,13},{6,14},{7,15},{8,0},{9,1},... | collective-permute-start | bytes 98312 | tf_op jit(solution)/shard_map/ppermute | solution.py:377
  43.2 3.3 %slice-start.8 = ((s8[14680064]{0:T(1024)(128)(4,1)}), s8[2097152]{0:T(1024)(128)(4,1)S(1)}, s32[]{:S(2)}) async-start(s8[14680064]{0:T(1024)(128)(4,1)} %bitcast.7), calls=%async_computation.8 | async-start | bytes 4194304
  43.2 3.3 %slice-start.9 = ((s8[14680064]{0:T(1024)(128)(4,1)}), s8[4194304]{0:T(1024)(128)(4,1)S(1)}, s32[]{:S(2)}) async-start(s8[14680064]{0:T(1024)(128)(4,1)} %bitcast.7), calls=%async_computation.9 | async-start | bytes 8388608
  45.6 2.3 %slice-start.10 = ((s8[14680064]{0:T(1024)(128)(4,1)}), s8[4194304]{0:T(1024)(128)(4,1)S(1)}, s32[]{:S(2)}) async-start(s8[14680064]{0:T(1024)(128)(4,1)} %bitcast.7), calls=%async_computation.10 | async-start | bytes 8388608
  45.6 3.5 %slice-start.11 = ((s8[14680064]{0:T(1024)(128)(4,1)}), s8[4194304]{0:T(1024)(128)(4,1)S(1)}, s32[]{:S(2)}) async-start(s8[14680064]{0:T(1024)(128)(4,1)} %bitcast.7), calls=%async_computation.11 | async-start | bytes 8388608
  49.1 33.0 %copy-start.1 = (s32[2]{0:T(128)S(1)}, s32[2]{0:T(128)}, u32[]{:S(2)}) copy-start(s32[2]{0:T(128)} %param.15) | copy-start | bytes 28
  53.9 1.6 %collective-permute-start.20 = (bf16[16,8192]{1,0:T(8,128)(2,1)S(1)}, bf16[16,8192]{1,0:T(8,128)(2,1)S(1)}, u32[]{:S(2)}, u32[]{:S(2)}) collective-permute-start(bf16[16,8192]{1,0:T(8,128)(2,1)S(1)} %get-tuple-element.30), channel_id=1, source_target_pairs={{0,1},{1,0},{2,3},{3,2},{4,5},{5,4},{6,7},{7,6},{8,9},{9,8},{10,11... | collective-permute-start | bytes 786440 | tf_op jit(solution)/shard_map/ppermute | solution.py:377
  55.5 1.9 %collective-permute-start.24 = (bf16[32,8192]{1,0:T(8,128)(2,1)S(1)}, bf16[32,8192]{1,0:T(8,128)(2,1)S(1)}, u32[]{:S(2)}, u32[]{:S(2)}) collective-permute-start(bf16[32,8192]{1,0:T(8,128)(2,1)S(1)} %tie.7), channel_id=1, source_target_pairs={{0,1},{1,0},{2,3},{3,2},{4,5},{5,4},{6,7},{7,6},{8,9},{9,8},{10,11... | collective-permute-start | bytes 1572872 | tf_op jit(solution)/shard_map/ppermute | solution.py:377
  55.7 8.3 %collective-permute-start.23 = (bf16[32,8192]{1,0:T(8,128)(2,1)S(1)}, bf16[32,8192]{1,0:T(8,128)(2,1)S(1)}, u32[]{:S(2)}, u32[]{:S(2)}) collective-permute-start(bf16[32,8192]{1,0:T(8,128)(2,1)S(1)} %tie.6), channel_id=1, source_target_pairs={{0,1},{1,0},{2,3},{3,2},{4,5},{5,4},{6,7},{7,6},{8,9},{9,8},{10,11... | collective-permute-start | bytes 1572872 | tf_op jit(solution)/shard_map/ppermute | solution.py:377
  56.1 6.4 %collective-permute-start.25 = (bf16[16,8192]{1,0:T(8,128)(2,1)S(1)}, bf16[16,8192]{1,0:T(8,128)(2,1)S(1)}, u32[]{:S(2)}, u32[]{:S(2)}) collective-permute-start(bf16[16,8192]{1,0:T(8,128)(2,1)S(1)} %added.7), channel_id=1, source_target_pairs={{0,4},{1,3},{4,8},{5,1},{8,12},{9,5},{12,14},{13,9},{14,10},{15,13... | collective-permute-start | bytes 786440 | tf_op jit(solution)/shard_map/ppermute | solution.py:374
  57.5 7.8 %collective-permute-start.29 = (bf16[16,8192]{1,0:T(8,128)(2,1)S(1)}, bf16[16,8192]{1,0:T(8,128)(2,1)S(1)}, u32[]{:S(2)}, u32[]{:S(2)}) collective-permute-start(bf16[16,8192]{1,0:T(8,128)(2,1)S(1)} %added.11), channel_id=1, source_target_pairs={{0,4},{1,3},{4,8},{5,1},{8,12},{9,5},{12,14},{13,9},{14,10},{15,13... | collective-permute-start | bytes 786440 | tf_op jit(solution)/shard_map/ppermute | solution.py:374
  59.4 11.1 %collective-permute-start.22 = (bf16[32,8192]{1,0:T(8,128)(2,1)S(1)}, bf16[32,8192]{1,0:T(8,128)(2,1)S(1)}, u32[]{:S(2)}, u32[]{:S(2)}) collective-permute-start(bf16[32,8192]{1,0:T(8,128)(2,1)S(1)} %tie.5), channel_id=1, source_target_pairs={{0,1},{1,0},{2,3},{3,2},{4,5},{5,4},{6,7},{7,6},{8,9},{9,8},{10,11... | collective-permute-start | bytes 1572872 | tf_op jit(solution)/shard_map/ppermute | solution.py:377
  62.7 6.4 %collective-permute-start.26 = (bf16[16,8192]{1,0:T(8,128)(2,1)S(1)}, bf16[16,8192]{1,0:T(8,128)(2,1)S(1)}, u32[]{:S(2)}, u32[]{:S(2)}) collective-permute-start(bf16[16,8192]{1,0:T(8,128)(2,1)S(1)} %added.8), channel_id=1, source_target_pairs={{0,4},{1,3},{4,8},{5,1},{8,12},{9,5},{12,14},{13,9},{14,10},{15,13... | collective-permute-start | bytes 786440 | tf_op jit(solution)/shard_map/ppermute | solution.py:374
  65.5 6.4 %collective-permute-start.30 = (bf16[16,8192]{1,0:T(8,128)(2,1)S(1)}, bf16[16,8192]{1,0:T(8,128)(2,1)S(1)}, u32[]{:S(2)}, u32[]{:S(2)}) collective-permute-start(bf16[16,8192]{1,0:T(8,128)(2,1)S(1)} %added.12), channel_id=1, source_target_pairs={{0,4},{1,3},{4,8},{5,1},{8,12},{9,5},{12,14},{13,9},{14,10},{15,13... | collective-permute-start | bytes 786440 | tf_op jit(solution)/shard_map/ppermute | solution.py:374
  69.2 6.4 %collective-permute-start.27 = (bf16[16,8192]{1,0:T(8,128)(2,1)S(1)}, bf16[16,8192]{1,0:T(8,128)(2,1)S(1)}, u32[]{:S(2)}, u32[]{:S(2)}) collective-permute-start(bf16[16,8192]{1,0:T(8,128)(2,1)S(1)} %added.9), channel_id=1, source_target_pairs={{0,4},{1,3},{4,8},{5,1},{8,12},{9,5},{12,14},{13,9},{14,10},{15,13... | collective-permute-start | bytes 786440 | tf_op jit(solution)/shard_map/ppermute | solution.py:374
  72.0 6.4 %collective-permute-start.31 = (bf16[16,8192]{1,0:T(8,128)(2,1)S(1)}, bf16[16,8192]{1,0:T(8,128)(2,1)S(1)}, u32[]{:S(2)}, u32[]{:S(2)}) collective-permute-start(bf16[16,8192]{1,0:T(8,128)(2,1)S(1)} %added.13), channel_id=1, source_target_pairs={{0,4},{1,3},{4,8},{5,1},{8,12},{9,5},{12,14},{13,9},{14,10},{15,13... | collective-permute-start | bytes 786440 | tf_op jit(solution)/shard_map/ppermute | solution.py:374
  73.3 5.1 %collective-permute-start.21 = (bf16[16,8192]{1,0:T(8,128)(2,1)S(1)}, bf16[16,8192]{1,0:T(8,128)(2,1)S(1)}, u32[]{:S(2)}, u32[]{:S(2)}) collective-permute-start(bf16[16,8192]{1,0:T(8,128)(2,1)S(1)} %tie.4), channel_id=1, source_target_pairs={{0,1},{1,0},{2,3},{3,2},{4,5},{5,4},{6,7},{7,6},{8,9},{9,8},{10,11... | collective-permute-start | bytes 786440 | tf_op jit(solution)/shard_map/ppermute | solution.py:377
  75.7 6.4 %collective-permute-start.28 = (bf16[16,8192]{1,0:T(8,128)(2,1)S(1)}, bf16[16,8192]{1,0:T(8,128)(2,1)S(1)}, u32[]{:S(2)}, u32[]{:S(2)}) collective-permute-start(bf16[16,8192]{1,0:T(8,128)(2,1)S(1)} %added.10), channel_id=1, source_target_pairs={{0,4},{1,3},{4,8},{5,1},{8,12},{9,5},{12,14},{13,9},{14,10},{15,13... | collective-permute-start | bytes 786440 | tf_op jit(solution)/shard_map/ppermute | solution.py:374
  78.4 3.7 %collective-permute-start.32 = (bf16[16,8192]{1,0:T(8,128)(2,1)S(1)}, bf16[16,8192]{1,0:T(8,128)(2,1)S(1)}, u32[]{:S(2)}, u32[]{:S(2)}) collective-permute-start(bf16[16,8192]{1,0:T(8,128)(2,1)S(1)} %collective-permute-done.31), channel_id=1, source_target_pairs={{0,1},{1,0},{2,3},{3,2},{4,5},{5,4},{6,7},{7,6},{8,9},{9,8},{10,11... | collective-permute-start | bytes 786440 | tf_op jit(solution)/shard_map/ppermute | solution.py:377

commit v9 on v8

--- a/solution.py
+++ b/solution.py
@@ -9,7 +9,8 @@
 
 F32 = jnp.float32
 BF16 = jnp.bfloat16
-VMEM_LIMIT = 17 * 1024 * 1024
+VMEM_LIMIT = 20 * 1024 * 1024
+WEIGHTS = (2, 2, 6, 6)
 
 
 def largest_tile(size, limit):
@@ -93,51 +94,24 @@
     return jnp.sum(jnp.where(spots == index, row, 0))
 
 
-def anchor_kernel(ids_ref, tokens_ref, shrink_ref, passed_in, own_ref, chosen_ref, passed_out, sems):
-    blocks = ids_ref.shape[1]
-    copies = [pltpu.make_async_copy(tokens_ref, own_ref, sems.at[blocks])]
-    for b in range(blocks):
-        source = shrink_ref.at[picked(ids_ref, b)]
-        copies.append(pltpu.make_async_copy(source, chosen_ref.at[b], sems.at[b]))
-    for copy in copies:
-        copy.start()
-    for copy in copies:
-        copy.wait()
-
-
-def anchor(adapters, tokens, shrink, passed):
-    blocks = adapters.shape[1]
+def anchor_kernel(tokens_ref, passed_in, own_ref, passed_out, sem):
+    copy = pltpu.make_async_copy(tokens_ref, own_ref, sem)
+    copy.start()
+    copy.wait()
+
+
+def anchor(tokens, passed):
     return pl.pallas_call(
         anchor_kernel,
-        in_specs=whole(1) + [FAR] * 3,
-        out_specs=whole(2) + [FAR],
-        out_shape=[
-            jax.ShapeDtypeStruct(tokens.shape, BF16),
-            jax.ShapeDtypeStruct((blocks,) + shrink.shape[1:], BF16),
-            jax.ShapeDtypeStruct(passed.shape, BF16),
-        ],
-        input_output_aliases={3: 2},
-        scratch_shapes=[pltpu.SemaphoreType.DMA((blocks + 1,))],
+        in_specs=[FAR, FAR],
+        out_specs=whole(1) + [FAR],
+        out_shape=[jax.ShapeDtypeStruct(passed.shape, passed.dtype)] * 2,
+        input_output_aliases={1: 1},
+        scratch_shapes=[pltpu.SemaphoreType.DMA],
         compiler_params=params(),
         cost_estimate=cost(30_000_000_000, 0),
         name="anchor",
-    )(adapters, far(tokens), far(shrink), passed)
-
-
-def tie_kernel(x_ref, after_ref, out_ref):
-    del x_ref, after_ref, out_ref
-
-
-def tie(x, after):
-    return pl.pallas_call(
-        tie_kernel,
-        in_specs=[FAR, FAR],
-        out_specs=FAR,
-        out_shape=jax.ShapeDtypeStruct(x.shape, x.dtype),
-        input_output_aliases={0: 0},
-        compiler_params=params(),
-        name="tie",
-    )(x, after)
+    )(far(tokens), passed)
 
 
 def rank_kernel(members, numbers, ids_ref, expand_ref, own_ref, other_ref, *refs):
@@ -155,7 +129,7 @@
     ]
     for copy in copies:
         copy.start()
-    weights = jnp.concatenate([ref[b] for ref in (own_ref, other_ref) for b in range(blocks)], axis=0)
+    weights = jnp.concatenate([ref[i] for ref in (own_ref, other_ref) for i in ids], axis=0)
     found = lax.dot_general(
         lhs, weights, (((1,), (1,)), ((), ())), preferred_element_type=F32
     )
@@ -214,7 +188,7 @@
         out_ref[pl.ds(place, rows), :] = part[index * rows : (index + 1) * rows]
 
 
-def product(pieces, matrix, part, parts, after):
+def product(pieces, matrix, part, parts, after, weight):
     rows, model = pieces[0].shape
     total = rows * len(pieces)
     width = matrix.shape[1]
@@ -225,7 +199,7 @@
         out_specs=whole(1)[0],
         out_shape=jax.ShapeDtypeStruct((total, width), F32),
         compiler_params=params(),
-        cost_estimate=cost(2 * total * depth * width, 2 * depth * (width + total)),
+        cost_estimate=cost(weight * total * depth * width, 2 * depth * (width + total)),
         name="product",
     )(matrix, *pieces, after)
 
@@ -260,7 +234,6 @@
         out_specs=whole(1)[0],
         out_shape=jax.ShapeDtypeStruct((total, width), BF16),
         compiler_params=params(),
-        cost_estimate=cost(6_000_000_000, 0),
         name="finish",
     )(*products, rank, expand)
 
@@ -377,10 +350,8 @@
         return lax.ppermute(x, "tp", crossing(members, bit))
 
     first = tokens
-    adapters, counts = adapter_per_block[None], block_token_count[None]
-    own, shrink, second = anchor(
-        adapters, tokens, jnp.swapaxes(shrink_matrices, 1, 2), cross(tokens)
-    )
+    own, second = anchor(tokens, cross(tokens))
+    shrink = jnp.swapaxes(shrink_matrices, 1, 2)
     other_shrink = cross(shrink)
     pieces, mine, theirs = [own, second], [], []
     for distance in range(1, reach + 1):
@@ -393,6 +364,7 @@
             theirs.append(cross(second))
     pieces = pieces + mine + theirs
 
+    adapters, counts = adapter_per_block[None], block_token_count[None]
     received = [0] + list(range(2, 2 + len(mine)))
     rank, expand = rank_of(
         adapters,
@@ -409,7 +381,7 @@
     while bit < members or work:
         if work:
             matrix, part = work.pop(0)
-            products.append(product(pieces, matrix, part, 2, after))
+            products.append(product(pieces, matrix, part, 2, after, WEIGHTS[len(products)]))
         if bit < members:
             after = cross(rank, bit)
             rank = rank + after if bit == 1 else jnp.concatenate([rank, after], axis=0)
@@ -420,8 +392,7 @@
     groups = [1] * slots + [1] + [2] * (reach - 1) + [1]
     outs = down(hidden, down_matrix, groups, rows)
     keep, give = outs[:slots], outs[slots:]
-    came = [cross(give[0])]
-    came += [cross(tie(x, came[0])) for x in give[1:]]
+    came = [cross(x) for x in give]
     first = step(added(rows, (0, keep[0]), (0, came[0])))
     second = None
     for index in range(1, reach):

time: 83.3 us -> 79.9 us (0.959)
  local copies, waits for them, and re-layouts: 3.48 us -> 0.06 us
  starting transfers between devices: 31.7 us -> 33.1 us
  Pallas kernels: 20.2 us -> 19 us
    unnamed x28 -> x24, local copies, waits for them, and re-layouts: 3.48 us -> 0.06 us
    ppermute x14, starting transfers between devices: 23 us -> 24 us  [step(): return lax.ppermute(x, 'tp', ring)]
where the time goes in v9:
time: 79.9 us; the launch traced here: 79.7 us
  starting transfers between devices  33.1 us (41%)
  waiting for transfers between devices  27.2 us (34%)
  Pallas kernels  19 us (24%)
    ppermute x14, waiting for transfers between devices, step(): return lax.ppermute(x, 'tp', ring)  25.4 us
    ppermute x14, starting transfers between devices, step(): return lax.ppermute(x, 'tp', ring)  24 us
    pallas_call x4, Pallas kernels, product(): pl.pallas_call(functools.partial(product_kernel, part * depth), in_specs=...  9.54 us
    ppermute x19, starting transfers between devices, cross(): return lax.ppermute(x, 'tp', crossing(members, bit))  9.08 us
    pallas_call x1, Pallas kernels, down(): pl.pallas_call(functools.partial(down_kernel, total // rows, groups, rows...  4.81 us
    ppermute x19, waiting for transfers between devices, cross(): return lax.ppermute(x, 'tp', crossing(members, bit))  1.74 us
  transfers between devices with their start and end apart: 33, of which 15 were waited for; matrix products, arithmetic and copies ran while one was open for 0% of the time, Pallas kernels for 16%

profile of v9, /device:TPU:0, one launch (start us, length us, event | category | flops | bytes accessed | tf_op | source)
XLA Modules:
  0.0 79.7 jit_solution(1643776947192255061)
XLA Ops:
  0.0 0.5 collective-permute-start
  0.5 2.6 %collective-permute-start.1 = (bf16[16,8192]{1,0:T(8,128)(2,1)}, bf16[16,8192]{1,0:T(8,128)(2,1)S(1)}, u32[]{:S(2)}, u32[]{:S(2)}) collective-permute-start(bf16[16,8192]{1,0:T(8,128)(2,1)} %tokens_ref.1), channel_id=1, source_target_pairs={{0,4},{1,3},{4,8},{5,1},{8,12},{9,5},{12,14},{13,9},{14,10},{15,13... | collective-permute-start | bytes 786440 | tf_op jit(solution)/shard_map/ppermute | solution.py:347
  3.1 0.0 collective-permute-done.passed_in
  3.1 1.1 %anchor.1 = (bf16[16,8192]{1,0:T(8,128)(2,1)S(1)}, bf16[16,8192]{1,0:T(8,128)(2,1)S(1)}) custom-call(bf16[16,8192]{1,0:T(8,128)(2,1)} %tokens_ref.1, bf16[16,8192]{1,0:T(8,128)(2,1)S(1)} %collective-permute-done.passed_in), custom_call_target="tpu_custom_call", output_to_operand_aliasing={{1}: (1, {})} | custom-call | flops 30000001024 | tf_op jit(solution)/shard_map/anchor/pallas_call | solution.py:104
  4.2 1.7 %collective-permute-start.2 = (bf16[16,8192]{1,0:T(8,128)(2,1)S(1)}, bf16[16,8192]{1,0:T(8,128)(2,1)S(1)}, u32[]{:S(2)}, u32[]{:S(2)}) collective-permute-start(bf16[16,8192]{1,0:T(8,128)(2,1)S(1)} %get-tuple-element.23.refs_1_), channel_id=1, source_target_pairs={{0,4},{1,3},{4,8},{5,1},{8,12},{9,5},{12,14},{13,9},{14,10},{15,13... | collective-permute-start | bytes 786440 | tf_op jit(solution)/shard_map/ppermute | solution.py:347
  6.0 1.6 %collective-permute-done.1.refs_1_.refs_2_ = bf16[16,8192]{1,0:T(8,128)(2,1)S(1)} collective-permute-done((bf16[16,8192]{1,0:T(8,128)(2,1)}, bf16[16,8192]{1,0:T(8,128)(2,1)S(1)}, u32[]{:S(2)}, u32[]{:S(2)}) %collective-permute-start.1) | collective-permute-done | bytes 262176 | tf_op jit(solution)/shard_map/ppermute | solution.py:347
  7.6 2.1 %collective-permute-start.3 = (bf16[16,8192]{1,0:T(8,128)(2,1)S(1)}, bf16[16,8192]{1,0:T(8,128)(2,1)S(1)}, u32[]{:S(2)}, u32[]{:S(2)}) collective-permute-start(bf16[16,8192]{1,0:T(8,128)(2,1)S(1)} %collective-permute-done.1.refs_1_.refs_2_), channel_id=1, source_target_pairs={{0,4},{1,3},{4,8},{5,1},{8,12},{9,5},{12,14},{13,9},{14,10},{15,13... | collective-permute-start | bytes 786440 | tf_op jit(solution)/shard_map/ppermute | solution.py:347
  9.7 0.0 collective-permute-start.8
  9.7 1.0 %collective-permute-done.2.refs_2_.refs_3_ = bf16[16,8192]{1,0:T(8,128)(2,1)S(1)} collective-permute-done((bf16[16,8192]{1,0:T(8,128)(2,1)S(1)}, bf16[16,8192]{1,0:T(8,128)(2,1)S(1)}, u32[]{:S(2)}, u32[]{:S(2)}) %collective-permute-start.2) | collective-permute-done | bytes 262176 | tf_op jit(solution)/shard_map/ppermute | solution.py:347
  10.6 1.8 %collective-permute-start.4 = (bf16[16,8192]{1,0:T(8,128)(2,1)S(1)}, bf16[16,8192]{1,0:T(8,128)(2,1)S(1)}, u32[]{:S(2)}, u32[]{:S(2)}) collective-permute-start(bf16[16,8192]{1,0:T(8,128)(2,1)S(1)} %collective-permute-done.2.refs_2_.refs_3_), channel_id=1, source_target_pairs={{0,4},{1,3},{4,8},{5,1},{8,12},{9,5},{12,14},{13,9},{14,10},{15,13... | collective-permute-start | bytes 786440 | tf_op jit(solution)/shard_map/ppermute | solution.py:347
  12.5 1.5 %collective-permute-done.3.refs_3_.refs_4_ = bf16[16,8192]{1,0:T(8,128)(2,1)S(1)} collective-permute-done((bf16[16,8192]{1,0:T(8,128)(2,1)S(1)}, bf16[16,8192]{1,0:T(8,128)(2,1)S(1)}, u32[]{:S(2)}, u32[]{:S(2)}) %collective-permute-start.3) | collective-permute-done | bytes 262176 | tf_op jit(solution)/shard_map/ppermute | solution.py:347
  14.0 2.1 %collective-permute-start.5 = (bf16[16,8192]{1,0:T(8,128)(2,1)S(1)}, bf16[16,8192]{1,0:T(8,128)(2,1)S(1)}, u32[]{:S(2)}, u32[]{:S(2)}) collective-permute-start(bf16[16,8192]{1,0:T(8,128)(2,1)S(1)} %collective-permute-done.3.refs_3_.refs_4_), channel_id=1, source_target_pairs={{0,4},{1,3},{4,8},{5,1},{8,12},{9,5},{12,14},{13,9},{14,10},{15,13... | collective-permute-start | bytes 786440 | tf_op jit(solution)/shard_map/ppermute | solution.py:347
  16.0 0.0 collective-permute-start.9
  16.1 0.5 collective-permute-start.10
  16.6 0.4 collective-permute-done.4.refs_4_.refs_5_
  17.0 1.8 %collective-permute-start.6 = (bf16[16,8192]{1,0:T(8,128)(2,1)S(1)}, bf16[16,8192]{1,0:T(8,128)(2,1)S(1)}, u32[]{:S(2)}, u32[]{:S(2)}) collective-permute-start(bf16[16,8192]{1,0:T(8,128)(2,1)S(1)} %collective-permute-done.4.refs_4_.refs_5_), channel_id=1, source_target_pairs={{0,4},{1,3},{4,8},{5,1},{8,12},{9,5},{12,14},{13,9},{14,10},{15,13... | collective-permute-start | bytes 786440 | tf_op jit(solution)/shard_map/ppermute | solution.py:347
  18.9 1.5 %collective-permute-done.5.refs_5_.refs_6_ = bf16[16,8192]{1,0:T(8,128)(2,1)S(1)} collective-permute-done((bf16[16,8192]{1,0:T(8,128)(2,1)S(1)}, bf16[16,8192]{1,0:T(8,128)(2,1)S(1)}, u32[]{:S(2)}, u32[]{:S(2)}) %collective-permute-start.5) | collective-permute-done | bytes 262176 | tf_op jit(solution)/shard_map/ppermute | solution.py:347
  20.3 2.1 %collective-permute-start.7 = (bf16[16,8192]{1,0:T(8,128)(2,1)S(1)}, bf16[16,8192]{1,0:T(8,128)(2,1)S(1)}, u32[]{:S(2)}, u32[]{:S(2)}) collective-permute-start(bf16[16,8192]{1,0:T(8,128)(2,1)S(1)} %collective-permute-done.5.refs_5_.refs_6_), channel_id=1, source_target_pairs={{0,4},{1,3},{4,8},{5,1},{8,12},{9,5},{12,14},{13,9},{14,10},{15,13... | collective-permute-start | bytes 786440 | tf_op jit(solution)/shard_map/ppermute | solution.py:347
  22.4 0.0 collective-permute-start.11
  22.4 0.5 collective-permute-start.12
  22.9 0.4 collective-permute-done.6.refs_6_.refs_7_
  23.4 3.3 %collective-permute-done.7.refs_7_.refs_8_ = bf16[16,8192]{1,0:T(8,128)(2,1)S(1)} collective-permute-done((bf16[16,8192]{1,0:T(8,128)(2,1)S(1)}, bf16[16,8192]{1,0:T(8,128)(2,1)S(1)}, u32[]{:S(2)}, u32[]{:S(2)}) %collective-permute-start.7) | collective-permute-done | bytes 262176 | tf_op jit(solution)/shard_map/ppermute | solution.py:347
  26.8 1.2 %rank.1 = (bf16[16,256]{1,0:T(8,128)(2,1)S(1)}, bf16[2,128,896]{2,1,0:T(8,128)(2,1)S(1)}) custom-call(s32[1,2]{1,0:T(1,128)S(1)} %bitcast.7, bf16[8,128,896]{2,1,0:T(8,128)(2,1)} %expand_ref.1, bf16[8,8,8192]{2,1,0:T(8,128)(2,1)S(1)} %bitcast.6, bf16[8,8,8192]{2,1,0:T(8,128)(2,1)S(1)} %collective-permute-done.15.other_ref, ...), custom_call_target="tpu_custom_call" | custom-call | flops 67108864 | bytes 4194304 | tf_op jit(solution)/shard_map/rank/pallas_call | solution.py:159
  28.0 0.6 collective-permute-start.16
  28.5 2.4 %product.4.gate_a = f32[256,896]{1,0:T(8,128)S(1)} custom-call(bf16[8192,896]{1,0:T(8,128)(2,1)S(1)} %copy-done, bf16[16,8192]{1,0:T(8,128)(2,1)S(1)} %get-tuple-element.22.refs_0_, bf16[16,8192]{1,0:T(8,128)(2,1)S(1)} %get-tuple-element.23.refs_1_, bf16[16,8192]{1,0:T(8,128)(2,1)S(1)} %collective-permute-done.1.refs_1_.refs_2_, ...), custom_call_target="tpu_custom_call" | custom-call | flops 1879048192 | bytes 9437184 | tf_op jit(solution)/shard_map/product/pallas_call | solution.py:196
  31.0 0.0 slice-start.6
  31.0 2.1 %collective-permute-start.17 = (bf16[16,256]{1,0:T(8,128)(2,1)S(1)}, bf16[16,256]{1,0:T(8,128)(2,1)S(1)}, u32[]{:S(2)}, u32[]{:S(2)}) collective-permute-start(bf16[16,256]{1,0:T(8,128)(2,1)S(1)} %add.3), channel_id=1, source_target_pairs={{0,2},{1,3},{2,0},{3,1},{4,6},{5,7},{6,4},{7,5},{8,10},{9,11},{10,... | collective-permute-start | bytes 24584 | tf_op jit(solution)/shard_map/ppermute | solution.py:350
  33.1 2.4 %product.5.gate_b = f32[256,896]{1,0:T(8,128)S(1)} custom-call(bf16[8192,896]{1,0:T(8,128)(2,1)S(1)} %copy-done, bf16[16,8192]{1,0:T(8,128)(2,1)S(1)} %get-tuple-element.22.refs_0_, bf16[16,8192]{1,0:T(8,128)(2,1)S(1)} %get-tuple-element.23.refs_1_, bf16[16,8192]{1,0:T(8,128)(2,1)S(1)} %collective-permute-done.1.refs_1_.refs_2_, ...), custom_call_target="tpu_custom_call" | custom-call | flops 1879048192 | bytes 9437184 | tf_op jit(solution)/shard_map/product/pallas_call | solution.py:196
  35.5 1.6 %collective-permute-start.18 = (bf16[32,256]{1,0:T(8,128)(2,1)S(1)}, bf16[32,256]{1,0:T(8,128)(2,1)S(1)}, u32[]{:S(2)}, u32[]{:S(2)}) collective-permute-start(bf16[32,256]{1,0:T(8,128)(2,1)S(1)} %pad_maximum_fusion.2), channel_id=1, source_target_pairs={{0,4},{1,5},{2,6},{3,7},{4,0},{5,1},{6,2},{7,3},{8,12},{9,13},{10,... | collective-permute-start | bytes 49160 | tf_op jit(solution)/shard_map/ppermute | solution.py:350
  37.2 0.0 slice-start
  37.2 0.0 slice-start.1
  37.2 2.4 %product.6.up_a = f32[256,896]{1,0:T(8,128)S(1)} custom-call(bf16[8192,896]{1,0:T(8,128)(2,1)S(1)} %bitcast.10, bf16[16,8192]{1,0:T(8,128)(2,1)S(1)} %get-tuple-element.22.refs_0_, bf16[16,8192]{1,0:T(8,128)(2,1)S(1)} %get-tuple-element.23.refs_1_, bf16[16,8192]{1,0:T(8,128)(2,1)S(1)} %collective-permute-done.1.refs_1_.refs_2_, ...), custom_call_target="tpu_custom_call" | custom-call | flops 5637144576 | bytes 9437184 | tf_op jit(solution)/shard_map/product/pallas_call | solution.py:196
  39.6 0.0 slice-start.2
  39.6 2.7 %collective-permute-start.19 = (bf16[64,256]{1,0:T(8,128)(2,1)S(1)}, bf16[64,256]{1,0:T(8,128)(2,1)S(1)}, u32[]{:S(2)}, u32[]{:S(2)}) collective-permute-start(bf16[64,256]{1,0:T(8,128)(2,1)S(1)} %pad_maximum_fusion.1), channel_id=1, source_target_pairs={{0,8},{1,9},{2,10},{3,11},{4,12},{5,13},{6,14},{7,15},{8,0},{9,1},... | collective-permute-start | bytes 98312 | tf_op jit(solution)/shard_map/ppermute | solution.py:350
  42.3 2.4 %product.7.up_b = f32[256,896]{1,0:T(8,128)S(1)} custom-call(bf16[8192,896]{1,0:T(8,128)(2,1)S(1)} %bitcast.10, bf16[16,8192]{1,0:T(8,128)(2,1)S(1)} %get-tuple-element.22.refs_0_, bf16[16,8192]{1,0:T(8,128)(2,1)S(1)} %get-tuple-element.23.refs_1_, bf16[16,8192]{1,0:T(8,128)(2,1)S(1)} %collective-permute-done.1.refs_1_.refs_2_, ...), custom_call_target="tpu_custom_call" | custom-call | flops 5637144576 | bytes 9437184 | tf_op jit(solution)/shard_map/product/pallas_call | solution.py:196
  44.7 0.0 copy-start.3
  44.7 0.7 finish.1.hidden_ref
  45.5 4.8 %down.1 = (bf16[16,8192]{1,0:T(8,128)(2,1)S(1)}, bf16[16,8192]{1,0:T(8,128)(2,1)S(1)}, bf16[16,8192]{1,0:T(8,128)(2,1)S(1)}, bf16[16,8192]{1,0:T(8,128)(2,1)S(1)...) custom-call(bf16[896,8192]{1,0:T(8,128)(2,1)S(1)} %bitcast.4, ...), custom_call_target="tpu_custom_call" | custom-call | flops 3758096384 | bytes 18874368 | tf_op jit(solution)/shard_map/down/pallas_call | solution.py:262
  50.3 0.1 collective-permute-start.23
  50.4 0.5 collective-permute-start.24
  50.9 0.1 collective-permute-start.22
  51.0 1.7 %collective-permute-done.24.refs_1_ = bf16[16,8192]{1,0:T(8,128)(2,1)S(1)} collective-permute-done((bf16[16,8192]{1,0:T(8,128)(2,1)S(1)}, bf16[16,8192]{1,0:T(8,128)(2,1)S(1)}, u32[]{:S(2)}, u32[]{:S(2)}) %collective-permute-start.24) | collective-permute-done | bytes 262176 | tf_op jit(solution)/shard_map/ppermute | solution.py:350
  52.7 0.1 added.7
  52.7 1.3 %collective-permute-start.25 = (bf16[16,8192]{1,0:T(8,128)(2,1)S(1)}, bf16[16,8192]{1,0:T(8,128)(2,1)S(1)}, u32[]{:S(2)}, u32[]{:S(2)}) collective-permute-start(bf16[16,8192]{1,0:T(8,128)(2,1)S(1)} %added.7), channel_id=1, source_target_pairs={{0,4},{1,3},{4,8},{5,1},{8,12},{9,5},{12,14},{13,9},{14,10},{15,13... | collective-permute-start | bytes 786440 | tf_op jit(solution)/shard_map/ppermute | solution.py:347
  54.0 0.1 added.11
  54.1 1.8 %collective-permute-start.29 = (bf16[16,8192]{1,0:T(8,128)(2,1)S(1)}, bf16[16,8192]{1,0:T(8,128)(2,1)S(1)}, u32[]{:S(2)}, u32[]{:S(2)}) collective-permute-start(bf16[16,8192]{1,0:T(8,128)(2,1)S(1)} %added.11), channel_id=1, source_target_pairs={{0,4},{1,3},{4,8},{5,1},{8,12},{9,5},{12,14},{13,9},{14,10},{15,13... | collective-permute-start | bytes 786440 | tf_op jit(solution)/shard_map/ppermute | solution.py:347
  55.9 3.2 %collective-permute-done.25.refs_2_ = bf16[16,8192]{1,0:T(8,128)(2,1)S(1)} collective-permute-done((bf16[16,8192]{1,0:T(8,128)(2,1)S(1)}, bf16[16,8192]{1,0:T(8,128)(2,1)S(1)}, u32[]{:S(2)}, u32[]{:S(2)}) %collective-permute-start.25) | collective-permute-done | bytes 262176 | tf_op jit(solution)/shard_map/ppermute | solution.py:347
  59.1 0.1 added.8
  59.2 1.3 %collective-permute-start.26 = (bf16[16,8192]{1,0:T(8,128)(2,1)S(1)}, bf16[16,8192]{1,0:T(8,128)(2,1)S(1)}, u32[]{:S(2)}, u32[]{:S(2)}) collective-permute-start(bf16[16,8192]{1,0:T(8,128)(2,1)S(1)} %added.8), channel_id=1, source_target_pairs={{0,4},{1,3},{4,8},{5,1},{8,12},{9,5},{12,14},{13,9},{14,10},{15,13... | collective-permute-start | bytes 786440 | tf_op jit(solution)/shard_map/ppermute | solution.py:347
  60.6 1.4 %collective-permute-done.29.refs_2_ = bf16[16,8192]{1,0:T(8,128)(2,1)S(1)} collective-permute-done((bf16[16,8192]{1,0:T(8,128)(2,1)S(1)}, bf16[16,8192]{1,0:T(8,128)(2,1)S(1)}, u32[]{:S(2)}, u32[]{:S(2)}) %collective-permute-start.29) | collective-permute-done | bytes 262176 | tf_op jit(solution)/shard_map/ppermute | solution.py:347
  62.0 0.1 added.12
  62.1 1.3 %collective-permute-start.30 = (bf16[16,8192]{1,0:T(8,128)(2,1)S(1)}, bf16[16,8192]{1,0:T(8,128)(2,1)S(1)}, u32[]{:S(2)}, u32[]{:S(2)}) collective-permute-start(bf16[16,8192]{1,0:T(8,128)(2,1)S(1)} %added.12), channel_id=1, source_target_pairs={{0,4},{1,3},{4,8},{5,1},{8,12},{9,5},{12,14},{13,9},{14,10},{15,13... | collective-permute-start | bytes 786440 | tf_op jit(solution)/shard_map/ppermute | solution.py:347
  63.4 2.3 %collective-permute-done.26.refs_2_ = bf16[16,8192]{1,0:T(8,128)(2,1)S(1)} collective-permute-done((bf16[16,8192]{1,0:T(8,128)(2,1)S(1)}, bf16[16,8192]{1,0:T(8,128)(2,1)S(1)}, u32[]{:S(2)}, u32[]{:S(2)}) %collective-permute-start.26) | collective-permute-done | bytes 262176 | tf_op jit(solution)/shard_map/ppermute | solution.py:347
  65.7 0.1 added.9
  65.8 1.3 %collective-permute-start.27 = (bf16[16,8192]{1,0:T(8,128)(2,1)S(1)}, bf16[16,8192]{1,0:T(8,128)(2,1)S(1)}, u32[]{:S(2)}, u32[]{:S(2)}) collective-permute-start(bf16[16,8192]{1,0:T(8,128)(2,1)S(1)} %added.9), channel_id=1, source_target_pairs={{0,4},{1,3},{4,8},{5,1},{8,12},{9,5},{12,14},{13,9},{14,10},{15,13... | collective-permute-start | bytes 786440 | tf_op jit(solution)/shard_map/ppermute | solution.py:347
  67.1 1.4 %collective-permute-done.30.refs_2_ = bf16[16,8192]{1,0:T(8,128)(2,1)S(1)} collective-permute-done((bf16[16,8192]{1,0:T(8,128)(2,1)S(1)}, bf16[16,8192]{1,0:T(8,128)(2,1)S(1)}, u32[]{:S(2)}, u32[]{:S(2)}) %collective-permute-start.30) | collective-permute-done | bytes 262176 | tf_op jit(solution)/shard_map/ppermute | solution.py:347
  68.5 0.1 added.13
  68.6 1.3 %collective-permute-start.31 = (bf16[16,8192]{1,0:T(8,128)(2,1)S(1)}, bf16[16,8192]{1,0:T(8,128)(2,1)S(1)}, u32[]{:S(2)}, u32[]{:S(2)}) collective-permute-start(bf16[16,8192]{1,0:T(8,128)(2,1)S(1)} %added.13), channel_id=1, source_target_pairs={{0,4},{1,3},{4,8},{5,1},{8,12},{9,5},{12,14},{13,9},{14,10},{15,13... | collective-permute-start | bytes 786440 | tf_op jit(solution)/shard_map/ppermute | solution.py:347
  69.9 2.3 %collective-permute-done.27.refs_2_ = bf16[16,8192]{1,0:T(8,128)(2,1)S(1)} collective-permute-done((bf16[16,8192]{1,0:T(8,128)(2,1)S(1)}, bf16[16,8192]{1,0:T(8,128)(2,1)S(1)}, u32[]{:S(2)}, u32[]{:S(2)}) %collective-permute-start.27) | collective-permute-done | bytes 262176 | tf_op jit(solution)/shard_map/ppermute | solution.py:347
  72.2 0.1 added.10
  72.3 1.3 %collective-permute-start.28 = (bf16[16,8192]{1,0:T(8,128)(2,1)S(1)}, bf16[16,8192]{1,0:T(8,128)(2,1)S(1)}, u32[]{:S(2)}, u32[]{:S(2)}) collective-permute-start(bf16[16,8192]{1,0:T(8,128)(2,1)S(1)} %added.10), channel_id=1, source_target_pairs={{0,4},{1,3},{4,8},{5,1},{8,12},{9,5},{12,14},{13,9},{14,10},{15,13... | collective-permute-start | bytes 786440 | tf_op jit(solution)/shard_map/ppermute | solution.py:347
  73.6 1.4 %collective-permute-done.31 = bf16[16,8192]{1,0:T(8,128)(2,1)S(1)} collective-permute-done((bf16[16,8192]{1,0:T(8,128)(2,1)S(1)}, bf16[16,8192]{1,0:T(8,128)(2,1)S(1)}, u32[]{:S(2)}, u32[]{:S(2)}) %collective-permute-start.31) | collective-permute-done | bytes 262176 | tf_op jit(solution)/shard_map/ppermute | solution.py:347
  75.0 3.7 %collective-permute-done.28.refs_2_ = bf16[16,8192]{1,0:T(8,128)(2,1)S(1)} collective-permute-done((bf16[16,8192]{1,0:T(8,128)(2,1)S(1)}, bf16[16,8192]{1,0:T(8,128)(2,1)S(1)}, u32[]{:S(2)}, u32[]{:S(2)}) %collective-permute-start.28) | collective-permute-done | bytes 262176 | tf_op jit(solution)/shard_map/ppermute | solution.py:347
  78.7 1.0 %last.1 = bf16[16,8192]{1,0:T(8,128)(2,1)} custom-call(s32[1,2]{1,0:T(1,128)S(1)} %bitcast.8, bf16[16,8192]{1,0:T(8,128)(2,1)S(1)} %get-tuple-element.26.refs_0_, bf16[16,8192]{1,0:T(8,128)(2,1)S(1)} %collective-permute-done.20.refs_1_, bf16[16,8192]{1,0:T(8,128)(2,1)S(1)} %collective-permute-done.28.refs_2_, ...), custom_call_target="tpu_custom_call" | custom-call | tf_op jit(solution)/shard_map/last/pallas_call | solution.py:297
  (48 shorter events, 0.1 us)
Async XLA Ops:
  0.0 5.9 %copy-start.1 = (bf16[8,8192,8]{1,2,0:T(8,128)(2,1)S(1)}, bf16[8,8192,8]{1,2,0:T(8,128)(2,1)}, u32[]{:S(2)}) copy-start(bf16[8,8192,8]{1,2,0:T(8,128)(2,1)} %param.12) | copy-start | bytes 3145732
  0.0 26.7 %copy-start.2 = (s32[2]{0:T(128)S(1)}, s32[2]{0:T(128)}, u32[]{:S(2)}) copy-start(s32[2]{0:T(128)} %param.14) | copy-start | bytes 28
  0.0 3.1 %collective-permute-start = (bf16[16,8192]{1,0:T(8,128)(2,1)}, bf16[16,8192]{1,0:T(8,128)(2,1)S(1)}, u32[]{:S(2)}, u32[]{:S(2)}) collective-permute-start(bf16[16,8192]{1,0:T(8,128)(2,1)} %tokens_ref.1), channel_id=1, source_target_pairs={{0,1},{1,0},{2,3},{3,2},{4,5},{5,4},{6,7},{7,6},{8,9},{9,8},{10,11... | collective-permute-start | bytes 786440 | tf_op jit(solution)/shard_map/ppermute | solution.py:350
  0.5 7.1 %collective-permute-start.1 = (bf16[16,8192]{1,0:T(8,128)(2,1)}, bf16[16,8192]{1,0:T(8,128)(2,1)S(1)}, u32[]{:S(2)}, u32[]{:S(2)}) collective-permute-start(bf16[16,8192]{1,0:T(8,128)(2,1)} %tokens_ref.1), channel_id=1, source_target_pairs={{0,4},{1,3},{4,8},{5,1},{8,12},{9,5},{12,14},{13,9},{14,10},{15,13... | collective-permute-start | bytes 786440 | tf_op jit(solution)/shard_map/ppermute | solution.py:347
  3.1 25.4 %copy-start = (bf16[8192,896]{1,0:T(8,128)(2,1)S(1)}, bf16[8192,896]{1,0:T(8,128)(2,1)}, u32[]{:S(2)}) copy-start(bf16[8192,896]{1,0:T(8,128)(2,1)} %w_ref.6) | copy-start | bytes 44040196
  4.2 6.4 %collective-permute-start.2 = (bf16[16,8192]{1,0:T(8,128)(2,1)S(1)}, bf16[16,8192]{1,0:T(8,128)(2,1)S(1)}, u32[]{:S(2)}, u32[]{:S(2)}) collective-permute-start(bf16[16,8192]{1,0:T(8,128)(2,1)S(1)} %get-tuple-element.23.refs_1_), channel_id=1, source_target_pairs={{0,4},{1,3},{4,8},{5,1},{8,12},{9,5},{12,14},{13,9},{14,10},{15,13... | collective-permute-start | bytes 786440 | tf_op jit(solution)/shard_map/ppermute | solution.py:347
  5.9 20.8 %collective-permute-start.15 = (bf16[8,8,8192]{2,1,0:T(8,128)(2,1)S(1)}, bf16[8,8,8192]{2,1,0:T(8,128)(2,1)S(1)}, u32[]{:S(2)}, u32[]{:S(2)}) collective-permute-start(bf16[8,8,8192]{2,1,0:T(8,128)(2,1)S(1)} %bitcast.5), channel_id=1, source_target_pairs={{0,1},{1,0},{2,3},{3,2},{4,5},{5,4},{6,7},{7,6},{8,9},{9,8},{10,11... | collective-permute-start | bytes 3145736 | tf_op jit(solution)/shard_map/ppermute | solution.py:350
  7.6 6.4 %collective-permute-start.3 = (bf16[16,8192]{1,0:T(8,128)(2,1)S(1)}, bf16[16,8192]{1,0:T(8,128)(2,1)S(1)}, u32[]{:S(2)}, u32[]{:S(2)}) collective-permute-start(bf16[16,8192]{1,0:T(8,128)(2,1)S(1)} %collective-permute-done.1.refs_1_.refs_2_), channel_id=1, source_target_pairs={{0,4},{1,3},{4,8},{5,1},{8,12},{9,5},{12,14},{13,9},{14,10},{15,13... | collective-permute-start | bytes 786440 | tf_op jit(solution)/shard_map/ppermute | solution.py:347
  9.7 6.4 %collective-permute-start.8 = (bf16[16,8192]{1,0:T(8,128)(2,1)S(1)}, bf16[16,8192]{1,0:T(8,128)(2,1)S(1)}, u32[]{:S(2)}, u32[]{:S(2)}) collective-permute-start(bf16[16,8192]{1,0:T(8,128)(2,1)S(1)} %collective-permute-done.1.refs_1_.refs_2_), channel_id=1, source_target_pairs={{0,1},{1,0},{2,3},{3,2},{4,5},{5,4},{6,7},{7,6},{8,9},{9,8},{10,11... | collective-permute-start | bytes 786440 | tf_op jit(solution)/shard_map/ppermute | solution.py:350
  10.6 6.4 %collective-permute-start.4 = (bf16[16,8192]{1,0:T(8,128)(2,1)S(1)}, bf16[16,8192]{1,0:T(8,128)(2,1)S(1)}, u32[]{:S(2)}, u32[]{:S(2)}) collective-permute-start(bf16[16,8192]{1,0:T(8,128)(2,1)S(1)} %collective-permute-done.2.refs_2_.refs_3_), channel_id=1, source_target_pairs={{0,4},{1,3},{4,8},{5,1},{8,12},{9,5},{12,14},{13,9},{14,10},{15,13... | collective-permute-start | bytes 786440 | tf_op jit(solution)/shard_map/ppermute | solution.py:347
  14.0 6.4 %collective-permute-start.5 = (bf16[16,8192]{1,0:T(8,128)(2,1)S(1)}, bf16[16,8192]{1,0:T(8,128)(2,1)S(1)}, u32[]{:S(2)}, u32[]{:S(2)}) collective-permute-start(bf16[16,8192]{1,0:T(8,128)(2,1)S(1)} %collective-permute-done.3.refs_3_.refs_4_), channel_id=1, source_target_pairs={{0,4},{1,3},{4,8},{5,1},{8,12},{9,5},{12,14},{13,9},{14,10},{15,13... | collective-permute-start | bytes 786440 | tf_op jit(solution)/shard_map/ppermute | solution.py:347
  16.0 6.4 %collective-permute-start.9 = (bf16[16,8192]{1,0:T(8,128)(2,1)S(1)}, bf16[16,8192]{1,0:T(8,128)(2,1)S(1)}, u32[]{:S(2)}, u32[]{:S(2)}) collective-permute-start(bf16[16,8192]{1,0:T(8,128)(2,1)S(1)} %collective-permute-done.2.refs_2_.refs_3_), channel_id=1, source_target_pairs={{0,1},{1,0},{2,3},{3,2},{4,5},{5,4},{6,7},{7,6},{8,9},{9,8},{10,11... | collective-permute-start | bytes 786440 | tf_op jit(solution)/shard_map/ppermute | solution.py:350
  16.1 6.4 %collective-permute-start.10 = (bf16[16,8192]{1,0:T(8,128)(2,1)S(1)}, bf16[16,8192]{1,0:T(8,128)(2,1)S(1)}, u32[]{:S(2)}, u32[]{:S(2)}) collective-permute-start(bf16[16,8192]{1,0:T(8,128)(2,1)S(1)} %collective-permute-done.3.refs_3_.refs_4_), channel_id=1, source_target_pairs={{0,1},{1,0},{2,3},{3,2},{4,5},{5,4},{6,7},{7,6},{8,9},{9,8},{10,11... | collective-permute-start | bytes 786440 | tf_op jit(solution)/shard_map/ppermute | solution.py:350
  17.0 6.4 %collective-permute-start.6 = (bf16[16,8192]{1,0:T(8,128)(2,1)S(1)}, bf16[16,8192]{1,0:T(8,128)(2,1)S(1)}, u32[]{:S(2)}, u32[]{:S(2)}) collective-permute-start(bf16[16,8192]{1,0:T(8,128)(2,1)S(1)} %collective-permute-done.4.refs_4_.refs_5_), channel_id=1, source_target_pairs={{0,4},{1,3},{4,8},{5,1},{8,12},{9,5},{12,14},{13,9},{14,10},{15,13... | collective-permute-start | bytes 786440 | tf_op jit(solution)/shard_map/ppermute | solution.py:347
  20.3 6.4 %collective-permute-start.7 = (bf16[16,8192]{1,0:T(8,128)(2,1)S(1)}, bf16[16,8192]{1,0:T(8,128)(2,1)S(1)}, u32[]{:S(2)}, u32[]{:S(2)}) collective-permute-start(bf16[16,8192]{1,0:T(8,128)(2,1)S(1)} %collective-permute-done.5.refs_5_.refs_6_), channel_id=1, source_target_pairs={{0,4},{1,3},{4,8},{5,1},{8,12},{9,5},{12,14},{13,9},{14,10},{15,13... | collective-permute-start | bytes 786440 | tf_op jit(solution)/shard_map/ppermute | solution.py:347
  22.4 4.3 %collective-permute-start.11 = (bf16[16,8192]{1,0:T(8,128)(2,1)S(1)}, bf16[16,8192]{1,0:T(8,128)(2,1)S(1)}, u32[]{:S(2)}, u32[]{:S(2)}) collective-permute-start(bf16[16,8192]{1,0:T(8,128)(2,1)S(1)} %collective-permute-done.4.refs_4_.refs_5_), channel_id=1, source_target_pairs={{0,1},{1,0},{2,3},{3,2},{4,5},{5,4},{6,7},{7,6},{8,9},{9,8},{10,11... | collective-permute-start | bytes 786440 | tf_op jit(solution)/shard_map/ppermute | solution.py:350
  22.4 4.3 %collective-permute-start.12 = (bf16[16,8192]{1,0:T(8,128)(2,1)S(1)}, bf16[16,8192]{1,0:T(8,128)(2,1)S(1)}, u32[]{:S(2)}, u32[]{:S(2)}) collective-permute-start(bf16[16,8192]{1,0:T(8,128)(2,1)S(1)} %collective-permute-done.5.refs_5_.refs_6_), channel_id=1, source_target_pairs={{0,1},{1,0},{2,3},{3,2},{4,5},{5,4},{6,7},{7,6},{8,9},{9,8},{10,11... | collective-permute-start | bytes 786440 | tf_op jit(solution)/shard_map/ppermute | solution.py:350
  23.4 3.4 %collective-permute-start.13 = (bf16[16,8192]{1,0:T(8,128)(2,1)S(1)}, bf16[16,8192]{1,0:T(8,128)(2,1)S(1)}, u32[]{:S(2)}, u32[]{:S(2)}) collective-permute-start(bf16[16,8192]{1,0:T(8,128)(2,1)S(1)} %collective-permute-done.6.refs_6_.refs_7_), channel_id=1, source_target_pairs={{0,1},{1,0},{2,3},{3,2},{4,5},{5,4},{6,7},{7,6},{8,9},{9,8},{10,11... | collective-permute-start | bytes 786440 | tf_op jit(solution)/shard_map/ppermute | solution.py:350
  26.7 1.8 %collective-permute-start.14 = (bf16[16,8192]{1,0:T(8,128)(2,1)S(1)}, bf16[16,8192]{1,0:T(8,128)(2,1)S(1)}, u32[]{:S(2)}, u32[]{:S(2)}) collective-permute-start(bf16[16,8192]{1,0:T(8,128)(2,1)S(1)} %collective-permute-done.7.refs_7_.refs_8_), channel_id=1, source_target_pairs={{0,1},{1,0},{2,3},{3,2},{4,5},{5,4},{6,7},{7,6},{8,9},{9,8},{10,11... | collective-permute-start | bytes 786440 | tf_op jit(solution)/shard_map/ppermute | solution.py:350
  28.0 3.0 %collective-permute-start.16 = (bf16[16,256]{1,0:T(8,128)(2,1)S(1)}, bf16[16,256]{1,0:T(8,128)(2,1)S(1)}, u32[]{:S(2)}, u32[]{:S(2)}) collective-permute-start(bf16[16,256]{1,0:T(8,128)(2,1)S(1)} %get-tuple-element.24.refs_16_), channel_id=1, source_target_pairs={{0,1},{1,0},{2,3},{3,2},{4,5},{5,4},{6,7},{7,6},{8,9},{9,8},{10,11... | collective-permute-start | bytes 24584 | tf_op jit(solution)/shard_map/ppermute | solution.py:350
  28.5 8.6 %slice-start.4 = ((s8[14680064]{0:T(1024)(128)(4,1)}), s8[2097152]{0:T(1024)(128)(4,1)S(1)}, s32[]{:S(2)}) async-start(s8[14680064]{0:T(1024)(128)(4,1)} %bitcast.9), calls=%async_computation.4 | async-start | bytes 4194304
  28.5 8.6 %slice-start.5 = ((s8[14680064]{0:T(1024)(128)(4,1)}), s8[4194304]{0:T(1024)(128)(4,1)S(1)}, s32[]{:S(2)}) async-start(s8[14680064]{0:T(1024)(128)(4,1)} %bitcast.9), calls=%async_computation.5 | async-start | bytes 8388608
  31.0 6.2 %slice-start.6 = ((s8[14680064]{0:T(1024)(128)(4,1)}), s8[4194304]{0:T(1024)(128)(4,1)S(1)}, s32[]{:S(2)}) async-start(s8[14680064]{0:T(1024)(128)(4,1)} %bitcast.9), calls=%async_computation.6 | async-start | bytes 8388608
  31.0 6.2 %slice-start.7 = ((s8[14680064]{0:T(1024)(128)(4,1)}), s8[4194304]{0:T(1024)(128)(4,1)S(1)}, s32[]{:S(2)}) async-start(s8[14680064]{0:T(1024)(128)(4,1)} %bitcast.9), calls=%async_computation.7 | async-start | bytes 8388608
  31.0 4.5 %collective-permute-start.17 = (bf16[16,256]{1,0:T(8,128)(2,1)S(1)}, bf16[16,256]{1,0:T(8,128)(2,1)S(1)}, u32[]{:S(2)}, u32[]{:S(2)}) collective-permute-start(bf16[16,256]{1,0:T(8,128)(2,1)S(1)} %add.3), channel_id=1, source_target_pairs={{0,2},{1,3},{2,0},{3,1},{4,6},{5,7},{6,4},{7,5},{8,10},{9,11},{10,... | collective-permute-start | bytes 24584 | tf_op jit(solution)/shard_map/ppermute | solution.py:350
  35.5 4.1 %collective-permute-start.18 = (bf16[32,256]{1,0:T(8,128)(2,1)S(1)}, bf16[32,256]{1,0:T(8,128)(2,1)S(1)}, u32[]{:S(2)}, u32[]{:S(2)}) collective-permute-start(bf16[32,256]{1,0:T(8,128)(2,1)S(1)} %pad_maximum_fusion.2), channel_id=1, source_target_pairs={{0,4},{1,5},{2,6},{3,7},{4,0},{5,1},{6,2},{7,3},{8,12},{9,13},{10,... | collective-permute-start | bytes 49160 | tf_op jit(solution)/shard_map/ppermute | solution.py:350
  37.2 8.3 %slice-start = ((s8[14680064]{0:T(1024)(128)(4,1)}), s8[4194304]{0:T(1024)(128)(4,1)S(1)}, s32[]{:S(2)}) async-start(s8[14680064]{0:T(1024)(128)(4,1)} %bitcast.3), calls=%async_computation | async-start | bytes 8388608
  37.2 8.3 %slice-start.1 = ((s8[14680064]{0:T(1024)(128)(4,1)}), s8[4194304]{0:T(1024)(128)(4,1)S(1)}, s32[]{:S(2)}) async-start(s8[14680064]{0:T(1024)(128)(4,1)} %bitcast.3), calls=%async_computation.1 | async-start | bytes 8388608
  39.6 5.9 %slice-start.2 = ((s8[14680064]{0:T(1024)(128)(4,1)}), s8[4194304]{0:T(1024)(128)(4,1)S(1)}, s32[]{:S(2)}) async-start(s8[14680064]{0:T(1024)(128)(4,1)} %bitcast.3), calls=%async_computation.2 | async-start | bytes 8388608
  39.6 5.9 %slice-start.3 = ((s8[14680064]{0:T(1024)(128)(4,1)}), s8[2097152]{0:T(1024)(128)(4,1)S(1)}, s32[]{:S(2)}) async-start(s8[14680064]{0:T(1024)(128)(4,1)} %bitcast.3), calls=%async_computation.3 | async-start | bytes 4194304
  39.6 5.1 %collective-permute-start.19 = (bf16[64,256]{1,0:T(8,128)(2,1)S(1)}, bf16[64,256]{1,0:T(8,128)(2,1)S(1)}, u32[]{:S(2)}, u32[]{:S(2)}) collective-permute-start(bf16[64,256]{1,0:T(8,128)(2,1)S(1)} %pad_maximum_fusion.1), channel_id=1, source_target_pairs={{0,8},{1,9},{2,10},{3,11},{4,12},{5,13},{6,14},{7,15},{8,0},{9,1},... | collective-permute-start | bytes 98312 | tf_op jit(solution)/shard_map/ppermute | solution.py:350
  44.7 34.1 %copy-start.3 = (s32[2]{0:T(128)S(1)}, s32[2]{0:T(128)}, u32[]{:S(2)}) copy-start(s32[2]{0:T(128)} %param.15) | copy-start | bytes 28
  50.3 3.7 %collective-permute-start.23 = (bf16[32,8192]{1,0:T(8,128)(2,1)S(1)}, bf16[32,8192]{1,0:T(8,128)(2,1)S(1)}, u32[]{:S(2)}, u32[]{:S(2)}) collective-permute-start(bf16[32,8192]{1,0:T(8,128)(2,1)S(1)} %get-tuple-element.33), channel_id=1, source_target_pairs={{0,1},{1,0},{2,3},{3,2},{4,5},{5,4},{6,7},{7,6},{8,9},{9,8},{10,11... | collective-permute-start | bytes 1572872 | tf_op jit(solution)/shard_map/ppermute | solution.py:350
  50.4 2.3 %collective-permute-start.24 = (bf16[16,8192]{1,0:T(8,128)(2,1)S(1)}, bf16[16,8192]{1,0:T(8,128)(2,1)S(1)}, u32[]{:S(2)}, u32[]{:S(2)}) collective-permute-start(bf16[16,8192]{1,0:T(8,128)(2,1)S(1)} %get-tuple-element.35), channel_id=1, source_target_pairs={{0,1},{1,0},{2,3},{3,2},{4,5},{5,4},{6,7},{7,6},{8,9},{9,8},{10,11... | collective-permute-start | bytes 786440 | tf_op jit(solution)/shard_map/ppermute | solution.py:350
  50.9 9.7 %collective-permute-start.22 = (bf16[32,8192]{1,0:T(8,128)(2,1)S(1)}, bf16[32,8192]{1,0:T(8,128)(2,1)S(1)}, u32[]{:S(2)}, u32[]{:S(2)}) collective-permute-start(bf16[32,8192]{1,0:T(8,128)(2,1)S(1)} %get-tuple-element.31), channel_id=1, source_target_pairs={{0,1},{1,0},{2,3},{3,2},{4,5},{5,4},{6,7},{7,6},{8,9},{9,8},{10,11... | collective-permute-start | bytes 1572872 | tf_op jit(solution)/shard_map/ppermute | solution.py:350
  52.7 6.4 %collective-permute-start.25 = (bf16[16,8192]{1,0:T(8,128)(2,1)S(1)}, bf16[16,8192]{1,0:T(8,128)(2,1)S(1)}, u32[]{:S(2)}, u32[]{:S(2)}) collective-permute-start(bf16[16,8192]{1,0:T(8,128)(2,1)S(1)} %added.7), channel_id=1, source_target_pairs={{0,4},{1,3},{4,8},{5,1},{8,12},{9,5},{12,14},{13,9},{14,10},{15,13... | collective-permute-start | bytes 786440 | tf_op jit(solution)/shard_map/ppermute | solution.py:347
  54.1 7.8 %collective-permute-start.29 = (bf16[16,8192]{1,0:T(8,128)(2,1)S(1)}, bf16[16,8192]{1,0:T(8,128)(2,1)S(1)}, u32[]{:S(2)}, u32[]{:S(2)}) collective-permute-start(bf16[16,8192]{1,0:T(8,128)(2,1)S(1)} %added.11), channel_id=1, source_target_pairs={{0,4},{1,3},{4,8},{5,1},{8,12},{9,5},{12,14},{13,9},{14,10},{15,13... | collective-permute-start | bytes 786440 | tf_op jit(solution)/shard_map/ppermute | solution.py:347
  55.9 11.1 %collective-permute-start.21 = (bf16[32,8192]{1,0:T(8,128)(2,1)S(1)}, bf16[32,8192]{1,0:T(8,128)(2,1)S(1)}, u32[]{:S(2)}, u32[]{:S(2)}) collective-permute-start(bf16[32,8192]{1,0:T(8,128)(2,1)S(1)} %get-tuple-element.29), channel_id=1, source_target_pairs={{0,1},{1,0},{2,3},{3,2},{4,5},{5,4},{6,7},{7,6},{8,9},{9,8},{10,11... | collective-permute-start | bytes 1572872 | tf_op jit(solution)/shard_map/ppermute | solution.py:350
  59.2 6.4 %collective-permute-start.26 = (bf16[16,8192]{1,0:T(8,128)(2,1)S(1)}, bf16[16,8192]{1,0:T(8,128)(2,1)S(1)}, u32[]{:S(2)}, u32[]{:S(2)}) collective-permute-start(bf16[16,8192]{1,0:T(8,128)(2,1)S(1)} %added.8), channel_id=1, source_target_pairs={{0,4},{1,3},{4,8},{5,1},{8,12},{9,5},{12,14},{13,9},{14,10},{15,13... | collective-permute-start | bytes 786440 | tf_op jit(solution)/shard_map/ppermute | solution.py:347
  62.1 6.4 %collective-permute-start.30 = (bf16[16,8192]{1,0:T(8,128)(2,1)S(1)}, bf16[16,8192]{1,0:T(8,128)(2,1)S(1)}, u32[]{:S(2)}, u32[]{:S(2)}) collective-permute-start(bf16[16,8192]{1,0:T(8,128)(2,1)S(1)} %added.12), channel_id=1, source_target_pairs={{0,4},{1,3},{4,8},{5,1},{8,12},{9,5},{12,14},{13,9},{14,10},{15,13... | collective-permute-start | bytes 786440 | tf_op jit(solution)/shard_map/ppermute | solution.py:347
  65.8 6.4 %collective-permute-start.27 = (bf16[16,8192]{1,0:T(8,128)(2,1)S(1)}, bf16[16,8192]{1,0:T(8,128)(2,1)S(1)}, u32[]{:S(2)}, u32[]{:S(2)}) collective-permute-start(bf16[16,8192]{1,0:T(8,128)(2,1)S(1)} %added.9), channel_id=1, source_target_pairs={{0,4},{1,3},{4,8},{5,1},{8,12},{9,5},{12,14},{13,9},{14,10},{15,13... | collective-permute-start | bytes 786440 | tf_op jit(solution)/shard_map/ppermute | solution.py:347
  68.6 6.4 %collective-permute-start.31 = (bf16[16,8192]{1,0:T(8,128)(2,1)S(1)}, bf16[16,8192]{1,0:T(8,128)(2,1)S(1)}, u32[]{:S(2)}, u32[]{:S(2)}) collective-permute-start(bf16[16,8192]{1,0:T(8,128)(2,1)S(1)} %added.13), channel_id=1, source_target_pairs={{0,4},{1,3},{4,8},{5,1},{8,12},{9,5},{12,14},{13,9},{14,10},{15,13... | collective-permute-start | bytes 786440 | tf_op jit(solution)/shard_map/ppermute | solution.py:347
  69.9 5.1 %collective-permute-start.20 = (bf16[16,8192]{1,0:T(8,128)(2,1)S(1)}, bf16[16,8192]{1,0:T(8,128)(2,1)S(1)}, u32[]{:S(2)}, u32[]{:S(2)}) collective-permute-start(bf16[16,8192]{1,0:T(8,128)(2,1)S(1)} %get-tuple-element.27), channel_id=1, source_target_pairs={{0,1},{1,0},{2,3},{3,2},{4,5},{5,4},{6,7},{7,6},{8,9},{9,8},{10,11... | collective-permute-start | bytes 786440 | tf_op jit(solution)/shard_map/ppermute | solution.py:350
  72.3 6.4 %collective-permute-start.28 = (bf16[16,8192]{1,0:T(8,128)(2,1)S(1)}, bf16[16,8192]{1,0:T(8,128)(2,1)S(1)}, u32[]{:S(2)}, u32[]{:S(2)}) collective-permute-start(bf16[16,8192]{1,0:T(8,128)(2,1)S(1)} %added.10), channel_id=1, source_target_pairs={{0,4},{1,3},{4,8},{5,1},{8,12},{9,5},{12,14},{13,9},{14,10},{15,13... | collective-permute-start | bytes 786440 | tf_op jit(solution)/shard_map/ppermute | solution.py:347
  75.0 3.7 %collective-permute-start.32 = (bf16[16,8192]{1,0:T(8,128)(2,1)S(1)}, bf16[16,8192]{1,0:T(8,128)(2,1)S(1)}, u32[]{:S(2)}, u32[]{:S(2)}) collective-permute-start(bf16[16,8192]{1,0:T(8,128)(2,1)S(1)} %collective-permute-done.31), channel_id=1, source_target_pairs={{0,1},{1,0},{2,3},{3,2},{4,5},{5,4},{6,7},{7,6},{8,9},{9,8},{10,11... | collective-permute-start | bytes 786440 | tf_op jit(solution)/shard_map/ppermute | solution.py:350

commit v10 on v9

--- a/solution.py
+++ b/solution.py
@@ -178,7 +178,7 @@
     pieces, out_ref = refs[:-2], refs[-1]
     rows = pieces[0].shape[0]
     depth = w_ref.shape[0] // 2
-    size = min(2048, depth)
+    size = depth
     places = arrivals(lax.axis_index("tp"), len(pieces), rows)
     part = 0.0
     for start in range(first, first + depth, size):
@@ -204,7 +204,7 @@
     )(matrix, *pieces, after)
 
 
-def finish_kernel(span, gate_a, gate_b, up_a, up_b, rank_ref, expand_ref, hidden_ref):
+def finish_kernel(span, piece_rows, gate_a, gate_b, up_a, up_b, rank_ref, expand_ref, out_ref, hidden_ref):
     ranks = rank_ref.shape[0]
     chip = lax.axis_index("tp") // 2
     shape = (ranks, ranks)
@@ -224,35 +224,35 @@
         gate += gate_a[part] + gate_b[part]
         up += up_a[part] + up_b[part]
         hidden_ref[part] = (gate / (1.0 + jnp.exp(-gate)) * up).astype(BF16)
-
-
-def finish(products, rank, expand, span):
+    members = hidden_ref.shape[0] // piece_rows
+    for index, place in enumerate(departures(lax.axis_index("tp"), members, piece_rows)):
+        out_ref[index * piece_rows : (index + 1) * piece_rows, :] = hidden_ref[
+            pl.ds(place, piece_rows), :
+        ]
+
+
+def finish(products, rank, expand, span, piece_rows):
     total, width = products[0].shape
     return pl.pallas_call(
-        functools.partial(finish_kernel, span),
+        functools.partial(finish_kernel, span, piece_rows),
         in_specs=whole(6),
         out_specs=whole(1)[0],
         out_shape=jax.ShapeDtypeStruct((total, width), BF16),
+        scratch_shapes=[pltpu.VMEM((total, width), BF16)],
         compiler_params=params(),
         name="finish",
     )(*products, rank, expand)
 
 
-def down_kernel(members, groups, rows, size, w_ref, hidden_ref, *refs):
-    outs, product_ref = refs[:-1], refs[-1]
-    places = departures(lax.axis_index("tp"), members, rows)
+def down_kernel(groups, rows, size, w_ref, hidden_ref, *outs):
     hidden = hidden_ref[...]
     for start in range(0, w_ref.shape[1], size):
         columns = slice(start, start + size)
         part = jnp.dot(hidden, w_ref[:, columns], preferred_element_type=F32)
-        product_ref[...] = part.astype(BF16)
         at = 0
         for out, group in zip(outs, groups, strict=True):
-            for index in range(group):
-                out[index * rows : (index + 1) * rows, columns] = product_ref[
-                    pl.ds(places[at], rows), :
-                ]
-                at += 1
+            out[:, columns] = part[at : at + group * rows].astype(BF16)
+            at += group * rows
 
 
 def down(hidden, down_matrix, groups, rows):
@@ -260,11 +260,10 @@
     columns = down_matrix.shape[1]
     size = min(1024, columns)
     return pl.pallas_call(
-        functools.partial(down_kernel, total // rows, groups, rows, size),
+        functools.partial(down_kernel, groups, rows, size),
         in_specs=whole(2),
         out_specs=whole(len(groups)),
         out_shape=[jax.ShapeDtypeStruct((group * rows, columns), BF16) for group in groups],
-        scratch_shapes=[pltpu.VMEM((total, size), BF16)],
         compiler_params=params(),
         cost_estimate=cost(
             2 * total * depth * columns, 2 * depth * columns + 2 * total * columns
@@ -386,7 +385,7 @@
             after = cross(rank, bit)
             rank = rank + after if bit == 1 else jnp.concatenate([rank, after], axis=0)
             bit *= 2
-    hidden = finish(products, rank, expand, 2 * span)
+    hidden = finish(products, rank, expand, 2 * span, rows)
 
     slots = 2 * reach
     groups = [1] * slots + [1] + [2] * (reach - 1) + [1]

time: 79.9 us -> 79.8 us (level)
  no operation moved by 1% of the time
where the time goes in v10:
time: 79.8 us; the launch traced here: 79.6 us
  starting transfers between devices  33.1 us (41%)
  waiting for transfers between devices  27.2 us (34%)
  Pallas kernels  18.9 us (24%)
    ppermute x14, waiting for transfers between devices, step(): return lax.ppermute(x, 'tp', ring)  25.4 us
    ppermute x14, starting transfers between devices, step(): return lax.ppermute(x, 'tp', ring)  24.1 us
    pallas_call x4, Pallas kernels, product(): pl.pallas_call(functools.partial(product_kernel, part * depth), in_specs=...  9.55 us
    ppermute x19, starting transfers between devices, cross(): return lax.ppermute(x, 'tp', crossing(members, bit))  9.08 us
    pallas_call x1, Pallas kernels, down(): pl.pallas_call(functools.partial(down_kernel, groups, rows, size), in_spe...  4.68 us
    ppermute x19, waiting for transfers between devices, cross(): return lax.ppermute(x, 'tp', crossing(members, bit))  1.74 us
  transfers between devices with their start and end apart: 33, of which 15 were waited for; matrix products, arithmetic and copies ran while one was open for 0% of the time, Pallas kernels for 16%

profile of v10, /device:TPU:0, one launch (start us, length us, event | category | flops | bytes accessed | tf_op | source)
XLA Modules:
  0.0 79.6 jit_solution(12209905471642980761)
XLA Ops:
  0.0 0.5 collective-permute-start
  0.5 2.6 %collective-permute-start.1 = (bf16[16,8192]{1,0:T(8,128)(2,1)}, bf16[16,8192]{1,0:T(8,128)(2,1)S(1)}, u32[]{:S(2)}, u32[]{:S(2)}) collective-permute-start(bf16[16,8192]{1,0:T(8,128)(2,1)} %tokens_ref.1), channel_id=1, source_target_pairs={{0,4},{1,3},{4,8},{5,1},{8,12},{9,5},{12,14},{13,9},{14,10},{15,13... | collective-permute-start | bytes 786440 | tf_op jit(solution)/shard_map/ppermute | solution.py:346
  3.1 0.0 collective-permute-done.passed_in
  3.1 1.1 %anchor.1 = (bf16[16,8192]{1,0:T(8,128)(2,1)S(1)}, bf16[16,8192]{1,0:T(8,128)(2,1)S(1)}) custom-call(bf16[16,8192]{1,0:T(8,128)(2,1)} %tokens_ref.1, bf16[16,8192]{1,0:T(8,128)(2,1)S(1)} %collective-permute-done.passed_in), custom_call_target="tpu_custom_call", output_to_operand_aliasing={{1}: (1, {})} | custom-call | flops 30000001024 | tf_op jit(solution)/shard_map/anchor/pallas_call | solution.py:104
  4.2 1.7 %collective-permute-start.2 = (bf16[16,8192]{1,0:T(8,128)(2,1)S(1)}, bf16[16,8192]{1,0:T(8,128)(2,1)S(1)}, u32[]{:S(2)}, u32[]{:S(2)}) collective-permute-start(bf16[16,8192]{1,0:T(8,128)(2,1)S(1)} %get-tuple-element.23.refs_1_), channel_id=1, source_target_pairs={{0,4},{1,3},{4,8},{5,1},{8,12},{9,5},{12,14},{13,9},{14,10},{15,13... | collective-permute-start | bytes 786440 | tf_op jit(solution)/shard_map/ppermute | solution.py:346
  5.9 0.0 collective-permute-start.15
  6.0 1.6 %collective-permute-done.1.refs_1_.refs_2_ = bf16[16,8192]{1,0:T(8,128)(2,1)S(1)} collective-permute-done((bf16[16,8192]{1,0:T(8,128)(2,1)}, bf16[16,8192]{1,0:T(8,128)(2,1)S(1)}, u32[]{:S(2)}, u32[]{:S(2)}) %collective-permute-start.1) | collective-permute-done | bytes 262176 | tf_op jit(solution)/shard_map/ppermute | solution.py:346
  7.6 2.1 %collective-permute-start.3 = (bf16[16,8192]{1,0:T(8,128)(2,1)S(1)}, bf16[16,8192]{1,0:T(8,128)(2,1)S(1)}, u32[]{:S(2)}, u32[]{:S(2)}) collective-permute-start(bf16[16,8192]{1,0:T(8,128)(2,1)S(1)} %collective-permute-done.1.refs_1_.refs_2_), channel_id=1, source_target_pairs={{0,4},{1,3},{4,8},{5,1},{8,12},{9,5},{12,14},{13,9},{14,10},{15,13... | collective-permute-start | bytes 786440 | tf_op jit(solution)/shard_map/ppermute | solution.py:346
  9.7 0.0 collective-permute-start.8
  9.7 1.0 %collective-permute-done.2.refs_2_.refs_3_ = bf16[16,8192]{1,0:T(8,128)(2,1)S(1)} collective-permute-done((bf16[16,8192]{1,0:T(8,128)(2,1)S(1)}, bf16[16,8192]{1,0:T(8,128)(2,1)S(1)}, u32[]{:S(2)}, u32[]{:S(2)}) %collective-permute-start.2) | collective-permute-done | bytes 262176 | tf_op jit(solution)/shard_map/ppermute | solution.py:346
  10.6 1.8 %collective-permute-start.4 = (bf16[16,8192]{1,0:T(8,128)(2,1)S(1)}, bf16[16,8192]{1,0:T(8,128)(2,1)S(1)}, u32[]{:S(2)}, u32[]{:S(2)}) collective-permute-start(bf16[16,8192]{1,0:T(8,128)(2,1)S(1)} %collective-permute-done.2.refs_2_.refs_3_), channel_id=1, source_target_pairs={{0,4},{1,3},{4,8},{5,1},{8,12},{9,5},{12,14},{13,9},{14,10},{15,13... | collective-permute-start | bytes 786440 | tf_op jit(solution)/shard_map/ppermute | solution.py:346
  12.5 1.5 %collective-permute-done.3.refs_3_.refs_4_ = bf16[16,8192]{1,0:T(8,128)(2,1)S(1)} collective-permute-done((bf16[16,8192]{1,0:T(8,128)(2,1)S(1)}, bf16[16,8192]{1,0:T(8,128)(2,1)S(1)}, u32[]{:S(2)}, u32[]{:S(2)}) %collective-permute-start.3) | collective-permute-done | bytes 262176 | tf_op jit(solution)/shard_map/ppermute | solution.py:346
  14.0 2.1 %collective-permute-start.5 = (bf16[16,8192]{1,0:T(8,128)(2,1)S(1)}, bf16[16,8192]{1,0:T(8,128)(2,1)S(1)}, u32[]{:S(2)}, u32[]{:S(2)}) collective-permute-start(bf16[16,8192]{1,0:T(8,128)(2,1)S(1)} %collective-permute-done.3.refs_3_.refs_4_), channel_id=1, source_target_pairs={{0,4},{1,3},{4,8},{5,1},{8,12},{9,5},{12,14},{13,9},{14,10},{15,13... | collective-permute-start | bytes 786440 | tf_op jit(solution)/shard_map/ppermute | solution.py:346
  16.0 0.0 collective-permute-done.8.refs_8_.refs_9_
  16.1 0.5 collective-permute-start.10
  16.6 0.4 collective-permute-done.4.refs_4_.refs_5_
  17.0 1.8 %collective-permute-start.6 = (bf16[16,8192]{1,0:T(8,128)(2,1)S(1)}, bf16[16,8192]{1,0:T(8,128)(2,1)S(1)}, u32[]{:S(2)}, u32[]{:S(2)}) collective-permute-start(bf16[16,8192]{1,0:T(8,128)(2,1)S(1)} %collective-permute-done.4.refs_4_.refs_5_), channel_id=1, source_target_pairs={{0,4},{1,3},{4,8},{5,1},{8,12},{9,5},{12,14},{13,9},{14,10},{15,13... | collective-permute-start | bytes 786440 | tf_op jit(solution)/shard_map/ppermute | solution.py:346
  18.9 1.5 %collective-permute-done.5.refs_5_.refs_6_ = bf16[16,8192]{1,0:T(8,128)(2,1)S(1)} collective-permute-done((bf16[16,8192]{1,0:T(8,128)(2,1)S(1)}, bf16[16,8192]{1,0:T(8,128)(2,1)S(1)}, u32[]{:S(2)}, u32[]{:S(2)}) %collective-permute-start.5) | collective-permute-done | bytes 262176 | tf_op jit(solution)/shard_map/ppermute | solution.py:346
  20.3 2.1 %collective-permute-start.7 = (bf16[16,8192]{1,0:T(8,128)(2,1)S(1)}, bf16[16,8192]{1,0:T(8,128)(2,1)S(1)}, u32[]{:S(2)}, u32[]{:S(2)}) collective-permute-start(bf16[16,8192]{1,0:T(8,128)(2,1)S(1)} %collective-permute-done.5.refs_5_.refs_6_), channel_id=1, source_target_pairs={{0,4},{1,3},{4,8},{5,1},{8,12},{9,5},{12,14},{13,9},{14,10},{15,13... | collective-permute-start | bytes 786440 | tf_op jit(solution)/shard_map/ppermute | solution.py:346
  22.4 0.5 collective-permute-start.12
  22.9 0.4 collective-permute-done.6.refs_6_.refs_7_
  23.4 3.3 %collective-permute-done.7.refs_7_.refs_8_ = bf16[16,8192]{1,0:T(8,128)(2,1)S(1)} collective-permute-done((bf16[16,8192]{1,0:T(8,128)(2,1)S(1)}, bf16[16,8192]{1,0:T(8,128)(2,1)S(1)}, u32[]{:S(2)}, u32[]{:S(2)}) %collective-permute-start.7) | collective-permute-done | bytes 262176 | tf_op jit(solution)/shard_map/ppermute | solution.py:346
  26.8 1.2 %rank.1 = (bf16[16,256]{1,0:T(8,128)(2,1)S(1)}, bf16[2,128,896]{2,1,0:T(8,128)(2,1)S(1)}) custom-call(s32[1,2]{1,0:T(1,128)S(1)} %bitcast.7, bf16[8,128,896]{2,1,0:T(8,128)(2,1)} %expand_ref.1, bf16[8,8,8192]{2,1,0:T(8,128)(2,1)S(1)} %bitcast.6, bf16[8,8,8192]{2,1,0:T(8,128)(2,1)S(1)} %collective-permute-done.15.other_ref, ...), custom_call_target="tpu_custom_call" | custom-call | flops 67108864 | bytes 4194304 | tf_op jit(solution)/shard_map/rank/pallas_call | solution.py:159
  28.0 0.6 collective-permute-start.16
  28.5 2.4 %product.4.gate_a = f32[256,896]{1,0:T(8,128)S(1)} custom-call(bf16[8192,896]{1,0:T(8,128)(2,1)S(1)} %copy-done, bf16[16,8192]{1,0:T(8,128)(2,1)S(1)} %get-tuple-element.22.refs_0_, bf16[16,8192]{1,0:T(8,128)(2,1)S(1)} %get-tuple-element.23.refs_1_, bf16[16,8192]{1,0:T(8,128)(2,1)S(1)} %collective-permute-done.1.refs_1_.refs_2_, ...), custom_call_target="tpu_custom_call" | custom-call | flops 1879048192 | bytes 9437184 | tf_op jit(solution)/shard_map/product/pallas_call | solution.py:196
  31.0 0.0 slice-start.6
  31.0 2.1 %collective-permute-start.17 = (bf16[16,256]{1,0:T(8,128)(2,1)S(1)}, bf16[16,256]{1,0:T(8,128)(2,1)S(1)}, u32[]{:S(2)}, u32[]{:S(2)}) collective-permute-start(bf16[16,256]{1,0:T(8,128)(2,1)S(1)} %add.3), channel_id=1, source_target_pairs={{0,2},{1,3},{2,0},{3,1},{4,6},{5,7},{6,4},{7,5},{8,10},{9,11},{10,... | collective-permute-start | bytes 24584 | tf_op jit(solution)/shard_map/ppermute | solution.py:349
  33.1 2.4 %product.5.gate_b = f32[256,896]{1,0:T(8,128)S(1)} custom-call(bf16[8192,896]{1,0:T(8,128)(2,1)S(1)} %copy-done, bf16[16,8192]{1,0:T(8,128)(2,1)S(1)} %get-tuple-element.22.refs_0_, bf16[16,8192]{1,0:T(8,128)(2,1)S(1)} %get-tuple-element.23.refs_1_, bf16[16,8192]{1,0:T(8,128)(2,1)S(1)} %collective-permute-done.1.refs_1_.refs_2_, ...), custom_call_target="tpu_custom_call" | custom-call | flops 1879048192 | bytes 9437184 | tf_op jit(solution)/shard_map/product/pallas_call | solution.py:196
  35.5 1.6 %collective-permute-start.18 = (bf16[32,256]{1,0:T(8,128)(2,1)S(1)}, bf16[32,256]{1,0:T(8,128)(2,1)S(1)}, u32[]{:S(2)}, u32[]{:S(2)}) collective-permute-start(bf16[32,256]{1,0:T(8,128)(2,1)S(1)} %pad_maximum_fusion.2), channel_id=1, source_target_pairs={{0,4},{1,5},{2,6},{3,7},{4,0},{5,1},{6,2},{7,3},{8,12},{9,13},{10,... | collective-permute-start | bytes 49160 | tf_op jit(solution)/shard_map/ppermute | solution.py:349
  37.2 0.0 slice-start
  37.2 0.0 slice-start.1
  37.2 2.4 %product.6.up_a = f32[256,896]{1,0:T(8,128)S(1)} custom-call(bf16[8192,896]{1,0:T(8,128)(2,1)S(1)} %bitcast.10, bf16[16,8192]{1,0:T(8,128)(2,1)S(1)} %get-tuple-element.22.refs_0_, bf16[16,8192]{1,0:T(8,128)(2,1)S(1)} %get-tuple-element.23.refs_1_, bf16[16,8192]{1,0:T(8,128)(2,1)S(1)} %collective-permute-done.1.refs_1_.refs_2_, ...), custom_call_target="tpu_custom_call" | custom-call | flops 5637144576 | bytes 9437184 | tf_op jit(solution)/shard_map/product/pallas_call | solution.py:196
  39.6 0.0 slice-start.2
  39.6 2.7 %collective-permute-start.19 = (bf16[64,256]{1,0:T(8,128)(2,1)S(1)}, bf16[64,256]{1,0:T(8,128)(2,1)S(1)}, u32[]{:S(2)}, u32[]{:S(2)}) collective-permute-start(bf16[64,256]{1,0:T(8,128)(2,1)S(1)} %pad_maximum_fusion.1), channel_id=1, source_target_pairs={{0,8},{1,9},{2,10},{3,11},{4,12},{5,13},{6,14},{7,15},{8,0},{9,1},... | collective-permute-start | bytes 98312 | tf_op jit(solution)/shard_map/ppermute | solution.py:349
  42.3 2.4 %product.7.up_b = f32[256,896]{1,0:T(8,128)S(1)} custom-call(bf16[8192,896]{1,0:T(8,128)(2,1)S(1)} %bitcast.10, bf16[16,8192]{1,0:T(8,128)(2,1)S(1)} %get-tuple-element.22.refs_0_, bf16[16,8192]{1,0:T(8,128)(2,1)S(1)} %get-tuple-element.23.refs_1_, bf16[16,8192]{1,0:T(8,128)(2,1)S(1)} %collective-permute-done.1.refs_1_.refs_2_, ...), custom_call_target="tpu_custom_call" | custom-call | flops 5637144576 | bytes 9437184 | tf_op jit(solution)/shard_map/product/pallas_call | solution.py:196
  44.7 0.0 copy-start.3
  44.7 0.8 finish.1.hidden_ref
  45.5 4.7 %down.1 = (bf16[16,8192]{1,0:T(8,128)(2,1)S(1)}, bf16[16,8192]{1,0:T(8,128)(2,1)S(1)}, bf16[16,8192]{1,0:T(8,128)(2,1)S(1)}, bf16[16,8192]{1,0:T(8,128)(2,1)S(1)...) custom-call(bf16[896,8192]{1,0:T(8,128)(2,1)S(1)} %bitcast.4, ...), custom_call_target="tpu_custom_call" | custom-call | flops 3758096384 | bytes 18874368 | tf_op jit(solution)/shard_map/down/pallas_call | solution.py:262
  50.2 0.1 collective-permute-start.23
  50.3 0.5 collective-permute-start.24
  50.8 0.1 collective-permute-start.22
  50.9 1.7 %collective-permute-done.24.refs_1_ = bf16[16,8192]{1,0:T(8,128)(2,1)S(1)} collective-permute-done((bf16[16,8192]{1,0:T(8,128)(2,1)S(1)}, bf16[16,8192]{1,0:T(8,128)(2,1)S(1)}, u32[]{:S(2)}, u32[]{:S(2)}) %collective-permute-start.24) | collective-permute-done | bytes 262176 | tf_op jit(solution)/shard_map/ppermute | solution.py:349
  52.6 0.1 added.7
  52.6 1.3 %collective-permute-start.25 = (bf16[16,8192]{1,0:T(8,128)(2,1)S(1)}, bf16[16,8192]{1,0:T(8,128)(2,1)S(1)}, u32[]{:S(2)}, u32[]{:S(2)}) collective-permute-start(bf16[16,8192]{1,0:T(8,128)(2,1)S(1)} %added.7), channel_id=1, source_target_pairs={{0,4},{1,3},{4,8},{5,1},{8,12},{9,5},{12,14},{13,9},{14,10},{15,13... | collective-permute-start | bytes 786440 | tf_op jit(solution)/shard_map/ppermute | solution.py:346
  54.0 0.1 added.11
  54.0 1.9 %collective-permute-start.29 = (bf16[16,8192]{1,0:T(8,128)(2,1)S(1)}, bf16[16,8192]{1,0:T(8,128)(2,1)S(1)}, u32[]{:S(2)}, u32[]{:S(2)}) collective-permute-start(bf16[16,8192]{1,0:T(8,128)(2,1)S(1)} %added.11), channel_id=1, source_target_pairs={{0,4},{1,3},{4,8},{5,1},{8,12},{9,5},{12,14},{13,9},{14,10},{15,13... | collective-permute-start | bytes 786440 | tf_op jit(solution)/shard_map/ppermute | solution.py:346
  55.9 3.2 %collective-permute-done.25.refs_2_ = bf16[16,8192]{1,0:T(8,128)(2,1)S(1)} collective-permute-done((bf16[16,8192]{1,0:T(8,128)(2,1)S(1)}, bf16[16,8192]{1,0:T(8,128)(2,1)S(1)}, u32[]{:S(2)}, u32[]{:S(2)}) %collective-permute-start.25) | collective-permute-done | bytes 262176 | tf_op jit(solution)/shard_map/ppermute | solution.py:346
  59.1 0.1 added.8
  59.2 1.3 %collective-permute-start.26 = (bf16[16,8192]{1,0:T(8,128)(2,1)S(1)}, bf16[16,8192]{1,0:T(8,128)(2,1)S(1)}, u32[]{:S(2)}, u32[]{:S(2)}) collective-permute-start(bf16[16,8192]{1,0:T(8,128)(2,1)S(1)} %added.8), channel_id=1, source_target_pairs={{0,4},{1,3},{4,8},{5,1},{8,12},{9,5},{12,14},{13,9},{14,10},{15,13... | collective-permute-start | bytes 786440 | tf_op jit(solution)/shard_map/ppermute | solution.py:346
  60.5 1.4 %collective-permute-done.29.refs_2_ = bf16[16,8192]{1,0:T(8,128)(2,1)S(1)} collective-permute-done((bf16[16,8192]{1,0:T(8,128)(2,1)S(1)}, bf16[16,8192]{1,0:T(8,128)(2,1)S(1)}, u32[]{:S(2)}, u32[]{:S(2)}) %collective-permute-start.29) | collective-permute-done | bytes 262176 | tf_op jit(solution)/shard_map/ppermute | solution.py:346
  61.9 0.1 added.12
  62.0 1.3 %collective-permute-start.30 = (bf16[16,8192]{1,0:T(8,128)(2,1)S(1)}, bf16[16,8192]{1,0:T(8,128)(2,1)S(1)}, u32[]{:S(2)}, u32[]{:S(2)}) collective-permute-start(bf16[16,8192]{1,0:T(8,128)(2,1)S(1)} %added.12), channel_id=1, source_target_pairs={{0,4},{1,3},{4,8},{5,1},{8,12},{9,5},{12,14},{13,9},{14,10},{15,13... | collective-permute-start | bytes 786440 | tf_op jit(solution)/shard_map/ppermute | solution.py:346
  63.3 2.3 %collective-permute-done.26.refs_2_ = bf16[16,8192]{1,0:T(8,128)(2,1)S(1)} collective-permute-done((bf16[16,8192]{1,0:T(8,128)(2,1)S(1)}, bf16[16,8192]{1,0:T(8,128)(2,1)S(1)}, u32[]{:S(2)}, u32[]{:S(2)}) %collective-permute-start.26) | collective-permute-done | bytes 262176 | tf_op jit(solution)/shard_map/ppermute | solution.py:346
  65.6 0.1 added.9
  65.7 1.3 %collective-permute-start.27 = (bf16[16,8192]{1,0:T(8,128)(2,1)S(1)}, bf16[16,8192]{1,0:T(8,128)(2,1)S(1)}, u32[]{:S(2)}, u32[]{:S(2)}) collective-permute-start(bf16[16,8192]{1,0:T(8,128)(2,1)S(1)} %added.9), channel_id=1, source_target_pairs={{0,4},{1,3},{4,8},{5,1},{8,12},{9,5},{12,14},{13,9},{14,10},{15,13... | collective-permute-start | bytes 786440 | tf_op jit(solution)/shard_map/ppermute | solution.py:346
  67.0 1.4 %collective-permute-done.30.refs_2_ = bf16[16,8192]{1,0:T(8,128)(2,1)S(1)} collective-permute-done((bf16[16,8192]{1,0:T(8,128)(2,1)S(1)}, bf16[16,8192]{1,0:T(8,128)(2,1)S(1)}, u32[]{:S(2)}, u32[]{:S(2)}) %collective-permute-start.30) | collective-permute-done | bytes 262176 | tf_op jit(solution)/shard_map/ppermute | solution.py:346
  68.4 0.1 added.13
  68.5 1.3 %collective-permute-start.31 = (bf16[16,8192]{1,0:T(8,128)(2,1)S(1)}, bf16[16,8192]{1,0:T(8,128)(2,1)S(1)}, u32[]{:S(2)}, u32[]{:S(2)}) collective-permute-start(bf16[16,8192]{1,0:T(8,128)(2,1)S(1)} %added.13), channel_id=1, source_target_pairs={{0,4},{1,3},{4,8},{5,1},{8,12},{9,5},{12,14},{13,9},{14,10},{15,13... | collective-permute-start | bytes 786440 | tf_op jit(solution)/shard_map/ppermute | solution.py:346
  69.8 2.3 %collective-permute-done.27.refs_2_ = bf16[16,8192]{1,0:T(8,128)(2,1)S(1)} collective-permute-done((bf16[16,8192]{1,0:T(8,128)(2,1)S(1)}, bf16[16,8192]{1,0:T(8,128)(2,1)S(1)}, u32[]{:S(2)}, u32[]{:S(2)}) %collective-permute-start.27) | collective-permute-done | bytes 262176 | tf_op jit(solution)/shard_map/ppermute | solution.py:346
  72.1 0.1 added.10
  72.2 1.3 %collective-permute-start.28 = (bf16[16,8192]{1,0:T(8,128)(2,1)S(1)}, bf16[16,8192]{1,0:T(8,128)(2,1)S(1)}, u32[]{:S(2)}, u32[]{:S(2)}) collective-permute-start(bf16[16,8192]{1,0:T(8,128)(2,1)S(1)} %added.10), channel_id=1, source_target_pairs={{0,4},{1,3},{4,8},{5,1},{8,12},{9,5},{12,14},{13,9},{14,10},{15,13... | collective-permute-start | bytes 786440 | tf_op jit(solution)/shard_map/ppermute | solution.py:346
  73.5 1.4 %collective-permute-done.31 = bf16[16,8192]{1,0:T(8,128)(2,1)S(1)} collective-permute-done((bf16[16,8192]{1,0:T(8,128)(2,1)S(1)}, bf16[16,8192]{1,0:T(8,128)(2,1)S(1)}, u32[]{:S(2)}, u32[]{:S(2)}) %collective-permute-start.31) | collective-permute-done | bytes 262176 | tf_op jit(solution)/shard_map/ppermute | solution.py:346
  74.9 3.7 %collective-permute-done.28.refs_2_ = bf16[16,8192]{1,0:T(8,128)(2,1)S(1)} collective-permute-done((bf16[16,8192]{1,0:T(8,128)(2,1)S(1)}, bf16[16,8192]{1,0:T(8,128)(2,1)S(1)}, u32[]{:S(2)}, u32[]{:S(2)}) %collective-permute-start.28) | collective-permute-done | bytes 262176 | tf_op jit(solution)/shard_map/ppermute | solution.py:346
  78.6 1.0 %last.1 = bf16[16,8192]{1,0:T(8,128)(2,1)} custom-call(s32[1,2]{1,0:T(1,128)S(1)} %bitcast.8, bf16[16,8192]{1,0:T(8,128)(2,1)S(1)} %get-tuple-element.26.refs_0_, bf16[16,8192]{1,0:T(8,128)(2,1)S(1)} %collective-permute-done.20.refs_1_, bf16[16,8192]{1,0:T(8,128)(2,1)S(1)} %collective-permute-done.28.refs_2_, ...), custom_call_target="tpu_custom_call" | custom-call | tf_op jit(solution)/shard_map/last/pallas_call | solution.py:296
  (48 shorter events, 0.1 us)
Async XLA Ops:
  0.0 5.9 %copy-start.1 = (bf16[8,8192,8]{1,2,0:T(8,128)(2,1)S(1)}, bf16[8,8192,8]{1,2,0:T(8,128)(2,1)}, u32[]{:S(2)}) copy-start(bf16[8,8192,8]{1,2,0:T(8,128)(2,1)} %param.12) | copy-start | bytes 3145732
  0.0 26.7 %copy-start.2 = (s32[2]{0:T(128)S(1)}, s32[2]{0:T(128)}, u32[]{:S(2)}) copy-start(s32[2]{0:T(128)} %param.14) | copy-start | bytes 28
  0.0 3.1 %collective-permute-start = (bf16[16,8192]{1,0:T(8,128)(2,1)}, bf16[16,8192]{1,0:T(8,128)(2,1)S(1)}, u32[]{:S(2)}, u32[]{:S(2)}) collective-permute-start(bf16[16,8192]{1,0:T(8,128)(2,1)} %tokens_ref.1), channel_id=1, source_target_pairs={{0,1},{1,0},{2,3},{3,2},{4,5},{5,4},{6,7},{7,6},{8,9},{9,8},{10,11... | collective-permute-start | bytes 786440 | tf_op jit(solution)/shard_map/ppermute | solution.py:349
  0.5 7.1 %collective-permute-start.1 = (bf16[16,8192]{1,0:T(8,128)(2,1)}, bf16[16,8192]{1,0:T(8,128)(2,1)S(1)}, u32[]{:S(2)}, u32[]{:S(2)}) collective-permute-start(bf16[16,8192]{1,0:T(8,128)(2,1)} %tokens_ref.1), channel_id=1, source_target_pairs={{0,4},{1,3},{4,8},{5,1},{8,12},{9,5},{12,14},{13,9},{14,10},{15,13... | collective-permute-start | bytes 786440 | tf_op jit(solution)/shard_map/ppermute | solution.py:346
  3.1 25.4 %copy-start = (bf16[8192,896]{1,0:T(8,128)(2,1)S(1)}, bf16[8192,896]{1,0:T(8,128)(2,1)}, u32[]{:S(2)}) copy-start(bf16[8192,896]{1,0:T(8,128)(2,1)} %w_ref.6) | copy-start | bytes 44040196
  4.2 6.4 %collective-permute-start.2 = (bf16[16,8192]{1,0:T(8,128)(2,1)S(1)}, bf16[16,8192]{1,0:T(8,128)(2,1)S(1)}, u32[]{:S(2)}, u32[]{:S(2)}) collective-permute-start(bf16[16,8192]{1,0:T(8,128)(2,1)S(1)} %get-tuple-element.23.refs_1_), channel_id=1, source_target_pairs={{0,4},{1,3},{4,8},{5,1},{8,12},{9,5},{12,14},{13,9},{14,10},{15,13... | collective-permute-start | bytes 786440 | tf_op jit(solution)/shard_map/ppermute | solution.py:346
  5.9 20.8 %collective-permute-start.15 = (bf16[8,8,8192]{2,1,0:T(8,128)(2,1)S(1)}, bf16[8,8,8192]{2,1,0:T(8,128)(2,1)S(1)}, u32[]{:S(2)}, u32[]{:S(2)}) collective-permute-start(bf16[8,8,8192]{2,1,0:T(8,128)(2,1)S(1)} %bitcast.5), channel_id=1, source_target_pairs={{0,1},{1,0},{2,3},{3,2},{4,5},{5,4},{6,7},{7,6},{8,9},{9,8},{10,11... | collective-permute-start | bytes 3145736 | tf_op jit(solution)/shard_map/ppermute | solution.py:349
  7.6 6.4 %collective-permute-start.3 = (bf16[16,8192]{1,0:T(8,128)(2,1)S(1)}, bf16[16,8192]{1,0:T(8,128)(2,1)S(1)}, u32[]{:S(2)}, u32[]{:S(2)}) collective-permute-start(bf16[16,8192]{1,0:T(8,128)(2,1)S(1)} %collective-permute-done.1.refs_1_.refs_2_), channel_id=1, source_target_pairs={{0,4},{1,3},{4,8},{5,1},{8,12},{9,5},{12,14},{13,9},{14,10},{15,13... | collective-permute-start | bytes 786440 | tf_op jit(solution)/shard_map/ppermute | solution.py:346
  9.7 6.4 %collective-permute-start.8 = (bf16[16,8192]{1,0:T(8,128)(2,1)S(1)}, bf16[16,8192]{1,0:T(8,128)(2,1)S(1)}, u32[]{:S(2)}, u32[]{:S(2)}) collective-permute-start(bf16[16,8192]{1,0:T(8,128)(2,1)S(1)} %collective-permute-done.1.refs_1_.refs_2_), channel_id=1, source_target_pairs={{0,1},{1,0},{2,3},{3,2},{4,5},{5,4},{6,7},{7,6},{8,9},{9,8},{10,11... | collective-permute-start | bytes 786440 | tf_op jit(solution)/shard_map/ppermute | solution.py:349
  10.6 6.4 %collective-permute-start.4 = (bf16[16,8192]{1,0:T(8,128)(2,1)S(1)}, bf16[16,8192]{1,0:T(8,128)(2,1)S(1)}, u32[]{:S(2)}, u32[]{:S(2)}) collective-permute-start(bf16[16,8192]{1,0:T(8,128)(2,1)S(1)} %collective-permute-done.2.refs_2_.refs_3_), channel_id=1, source_target_pairs={{0,4},{1,3},{4,8},{5,1},{8,12},{9,5},{12,14},{13,9},{14,10},{15,13... | collective-permute-start | bytes 786440 | tf_op jit(solution)/shard_map/ppermute | solution.py:346
  14.0 6.4 %collective-permute-start.5 = (bf16[16,8192]{1,0:T(8,128)(2,1)S(1)}, bf16[16,8192]{1,0:T(8,128)(2,1)S(1)}, u32[]{:S(2)}, u32[]{:S(2)}) collective-permute-start(bf16[16,8192]{1,0:T(8,128)(2,1)S(1)} %collective-permute-done.3.refs_3_.refs_4_), channel_id=1, source_target_pairs={{0,4},{1,3},{4,8},{5,1},{8,12},{9,5},{12,14},{13,9},{14,10},{15,13... | collective-permute-start | bytes 786440 | tf_op jit(solution)/shard_map/ppermute | solution.py:346
  16.0 6.4 %collective-permute-start.9 = (bf16[16,8192]{1,0:T(8,128)(2,1)S(1)}, bf16[16,8192]{1,0:T(8,128)(2,1)S(1)}, u32[]{:S(2)}, u32[]{:S(2)}) collective-permute-start(bf16[16,8192]{1,0:T(8,128)(2,1)S(1)} %collective-permute-done.2.refs_2_.refs_3_), channel_id=1, source_target_pairs={{0,1},{1,0},{2,3},{3,2},{4,5},{5,4},{6,7},{7,6},{8,9},{9,8},{10,11... | collective-permute-start | bytes 786440 | tf_op jit(solution)/shard_map/ppermute | solution.py:349
  16.1 6.4 %collective-permute-start.10 = (bf16[16,8192]{1,0:T(8,128)(2,1)S(1)}, bf16[16,8192]{1,0:T(8,128)(2,1)S(1)}, u32[]{:S(2)}, u32[]{:S(2)}) collective-permute-start(bf16[16,8192]{1,0:T(8,128)(2,1)S(1)} %collective-permute-done.3.refs_3_.refs_4_), channel_id=1, source_target_pairs={{0,1},{1,0},{2,3},{3,2},{4,5},{5,4},{6,7},{7,6},{8,9},{9,8},{10,11... | collective-permute-start | bytes 786440 | tf_op jit(solution)/shard_map/ppermute | solution.py:349
  17.0 6.4 %collective-permute-start.6 = (bf16[16,8192]{1,0:T(8,128)(2,1)S(1)}, bf16[16,8192]{1,0:T(8,128)(2,1)S(1)}, u32[]{:S(2)}, u32[]{:S(2)}) collective-permute-start(bf16[16,8192]{1,0:T(8,128)(2,1)S(1)} %collective-permute-done.4.refs_4_.refs_5_), channel_id=1, source_target_pairs={{0,4},{1,3},{4,8},{5,1},{8,12},{9,5},{12,14},{13,9},{14,10},{15,13... | collective-permute-start | bytes 786440 | tf_op jit(solution)/shard_map/ppermute | solution.py:346
  20.3 6.4 %collective-permute-start.7 = (bf16[16,8192]{1,0:T(8,128)(2,1)S(1)}, bf16[16,8192]{1,0:T(8,128)(2,1)S(1)}, u32[]{:S(2)}, u32[]{:S(2)}) collective-permute-start(bf16[16,8192]{1,0:T(8,128)(2,1)S(1)} %collective-permute-done.5.refs_5_.refs_6_), channel_id=1, source_target_pairs={{0,4},{1,3},{4,8},{5,1},{8,12},{9,5},{12,14},{13,9},{14,10},{15,13... | collective-permute-start | bytes 786440 | tf_op jit(solution)/shard_map/ppermute | solution.py:346
  22.4 4.3 %collective-permute-start.11 = (bf16[16,8192]{1,0:T(8,128)(2,1)S(1)}, bf16[16,8192]{1,0:T(8,128)(2,1)S(1)}, u32[]{:S(2)}, u32[]{:S(2)}) collective-permute-start(bf16[16,8192]{1,0:T(8,128)(2,1)S(1)} %collective-permute-done.4.refs_4_.refs_5_), channel_id=1, source_target_pairs={{0,1},{1,0},{2,3},{3,2},{4,5},{5,4},{6,7},{7,6},{8,9},{9,8},{10,11... | collective-permute-start | bytes 786440 | tf_op jit(solution)/shard_map/ppermute | solution.py:349
  22.4 4.3 %collective-permute-start.12 = (bf16[16,8192]{1,0:T(8,128)(2,1)S(1)}, bf16[16,8192]{1,0:T(8,128)(2,1)S(1)}, u32[]{:S(2)}, u32[]{:S(2)}) collective-permute-start(bf16[16,8192]{1,0:T(8,128)(2,1)S(1)} %collective-permute-done.5.refs_5_.refs_6_), channel_id=1, source_target_pairs={{0,1},{1,0},{2,3},{3,2},{4,5},{5,4},{6,7},{7,6},{8,9},{9,8},{10,11... | collective-permute-start | bytes 786440 | tf_op jit(solution)/shard_map/ppermute | solution.py:349
  23.4 3.4 %collective-permute-start.13 = (bf16[16,8192]{1,0:T(8,128)(2,1)S(1)}, bf16[16,8192]{1,0:T(8,128)(2,1)S(1)}, u32[]{:S(2)}, u32[]{:S(2)}) collective-permute-start(bf16[16,8192]{1,0:T(8,128)(2,1)S(1)} %collective-permute-done.6.refs_6_.refs_7_), channel_id=1, source_target_pairs={{0,1},{1,0},{2,3},{3,2},{4,5},{5,4},{6,7},{7,6},{8,9},{9,8},{10,11... | collective-permute-start | bytes 786440 | tf_op jit(solution)/shard_map/ppermute | solution.py:349
  26.7 1.8 %collective-permute-start.14 = (bf16[16,8192]{1,0:T(8,128)(2,1)S(1)}, bf16[16,8192]{1,0:T(8,128)(2,1)S(1)}, u32[]{:S(2)}, u32[]{:S(2)}) collective-permute-start(bf16[16,8192]{1,0:T(8,128)(2,1)S(1)} %collective-permute-done.7.refs_7_.refs_8_), channel_id=1, source_target_pairs={{0,1},{1,0},{2,3},{3,2},{4,5},{5,4},{6,7},{7,6},{8,9},{9,8},{10,11... | collective-permute-start | bytes 786440 | tf_op jit(solution)/shard_map/ppermute | solution.py:349
  28.0 3.0 %collective-permute-start.16 = (bf16[16,256]{1,0:T(8,128)(2,1)S(1)}, bf16[16,256]{1,0:T(8,128)(2,1)S(1)}, u32[]{:S(2)}, u32[]{:S(2)}) collective-permute-start(bf16[16,256]{1,0:T(8,128)(2,1)S(1)} %get-tuple-element.24.refs_16_), channel_id=1, source_target_pairs={{0,1},{1,0},{2,3},{3,2},{4,5},{5,4},{6,7},{7,6},{8,9},{9,8},{10,11... | collective-permute-start | bytes 24584 | tf_op jit(solution)/shard_map/ppermute | solution.py:349
  28.5 8.6 %slice-start.4 = ((s8[14680064]{0:T(1024)(128)(4,1)}), s8[2097152]{0:T(1024)(128)(4,1)S(1)}, s32[]{:S(2)}) async-start(s8[14680064]{0:T(1024)(128)(4,1)} %bitcast.9), calls=%async_computation.4 | async-start | bytes 4194304
  28.5 8.6 %slice-start.5 = ((s8[14680064]{0:T(1024)(128)(4,1)}), s8[4194304]{0:T(1024)(128)(4,1)S(1)}, s32[]{:S(2)}) async-start(s8[14680064]{0:T(1024)(128)(4,1)} %bitcast.9), calls=%async_computation.5 | async-start | bytes 8388608
  31.0 6.2 %slice-start.6 = ((s8[14680064]{0:T(1024)(128)(4,1)}), s8[4194304]{0:T(1024)(128)(4,1)S(1)}, s32[]{:S(2)}) async-start(s8[14680064]{0:T(1024)(128)(4,1)} %bitcast.9), calls=%async_computation.6 | async-start | bytes 8388608
  31.0 6.2 %slice-start.7 = ((s8[14680064]{0:T(1024)(128)(4,1)}), s8[4194304]{0:T(1024)(128)(4,1)S(1)}, s32[]{:S(2)}) async-start(s8[14680064]{0:T(1024)(128)(4,1)} %bitcast.9), calls=%async_computation.7 | async-start | bytes 8388608
  31.0 4.5 %collective-permute-start.17 = (bf16[16,256]{1,0:T(8,128)(2,1)S(1)}, bf16[16,256]{1,0:T(8,128)(2,1)S(1)}, u32[]{:S(2)}, u32[]{:S(2)}) collective-permute-start(bf16[16,256]{1,0:T(8,128)(2,1)S(1)} %add.3), channel_id=1, source_target_pairs={{0,2},{1,3},{2,0},{3,1},{4,6},{5,7},{6,4},{7,5},{8,10},{9,11},{10,... | collective-permute-start | bytes 24584 | tf_op jit(solution)/shard_map/ppermute | solution.py:349
  35.5 4.1 %collective-permute-start.18 = (bf16[32,256]{1,0:T(8,128)(2,1)S(1)}, bf16[32,256]{1,0:T(8,128)(2,1)S(1)}, u32[]{:S(2)}, u32[]{:S(2)}) collective-permute-start(bf16[32,256]{1,0:T(8,128)(2,1)S(1)} %pad_maximum_fusion.2), channel_id=1, source_target_pairs={{0,4},{1,5},{2,6},{3,7},{4,0},{5,1},{6,2},{7,3},{8,12},{9,13},{10,... | collective-permute-start | bytes 49160 | tf_op jit(solution)/shard_map/ppermute | solution.py:349
  37.2 8.3 %slice-start = ((s8[14680064]{0:T(1024)(128)(4,1)}), s8[4194304]{0:T(1024)(128)(4,1)S(1)}, s32[]{:S(2)}) async-start(s8[14680064]{0:T(1024)(128)(4,1)} %bitcast.3), calls=%async_computation | async-start | bytes 8388608
  37.2 8.3 %slice-start.1 = ((s8[14680064]{0:T(1024)(128)(4,1)}), s8[4194304]{0:T(1024)(128)(4,1)S(1)}, s32[]{:S(2)}) async-start(s8[14680064]{0:T(1024)(128)(4,1)} %bitcast.3), calls=%async_computation.1 | async-start | bytes 8388608
  39.6 5.9 %slice-start.2 = ((s8[14680064]{0:T(1024)(128)(4,1)}), s8[4194304]{0:T(1024)(128)(4,1)S(1)}, s32[]{:S(2)}) async-start(s8[14680064]{0:T(1024)(128)(4,1)} %bitcast.3), calls=%async_computation.2 | async-start | bytes 8388608
  39.6 5.9 %slice-start.3 = ((s8[14680064]{0:T(1024)(128)(4,1)}), s8[2097152]{0:T(1024)(128)(4,1)S(1)}, s32[]{:S(2)}) async-start(s8[14680064]{0:T(1024)(128)(4,1)} %bitcast.3), calls=%async_computation.3 | async-start | bytes 4194304
  39.6 5.1 %collective-permute-start.19 = (bf16[64,256]{1,0:T(8,128)(2,1)S(1)}, bf16[64,256]{1,0:T(8,128)(2,1)S(1)}, u32[]{:S(2)}, u32[]{:S(2)}) collective-permute-start(bf16[64,256]{1,0:T(8,128)(2,1)S(1)} %pad_maximum_fusion.1), channel_id=1, source_target_pairs={{0,8},{1,9},{2,10},{3,11},{4,12},{5,13},{6,14},{7,15},{8,0},{9,1},... | collective-permute-start | bytes 98312 | tf_op jit(solution)/shard_map/ppermute | solution.py:349
  44.7 34.0 %copy-start.3 = (s32[2]{0:T(128)S(1)}, s32[2]{0:T(128)}, u32[]{:S(2)}) copy-start(s32[2]{0:T(128)} %param.15) | copy-start | bytes 28
  50.2 3.7 %collective-permute-start.23 = (bf16[32,8192]{1,0:T(8,128)(2,1)S(1)}, bf16[32,8192]{1,0:T(8,128)(2,1)S(1)}, u32[]{:S(2)}, u32[]{:S(2)}) collective-permute-start(bf16[32,8192]{1,0:T(8,128)(2,1)S(1)} %get-tuple-element.33), channel_id=1, source_target_pairs={{0,1},{1,0},{2,3},{3,2},{4,5},{5,4},{6,7},{7,6},{8,9},{9,8},{10,11... | collective-permute-start | bytes 1572872 | tf_op jit(solution)/shard_map/ppermute | solution.py:349
  50.3 2.3 %collective-permute-start.24 = (bf16[16,8192]{1,0:T(8,128)(2,1)S(1)}, bf16[16,8192]{1,0:T(8,128)(2,1)S(1)}, u32[]{:S(2)}, u32[]{:S(2)}) collective-permute-start(bf16[16,8192]{1,0:T(8,128)(2,1)S(1)} %get-tuple-element.35), channel_id=1, source_target_pairs={{0,1},{1,0},{2,3},{3,2},{4,5},{5,4},{6,7},{7,6},{8,9},{9,8},{10,11... | collective-permute-start | bytes 786440 | tf_op jit(solution)/shard_map/ppermute | solution.py:349
  50.8 9.7 %collective-permute-start.22 = (bf16[32,8192]{1,0:T(8,128)(2,1)S(1)}, bf16[32,8192]{1,0:T(8,128)(2,1)S(1)}, u32[]{:S(2)}, u32[]{:S(2)}) collective-permute-start(bf16[32,8192]{1,0:T(8,128)(2,1)S(1)} %get-tuple-element.31), channel_id=1, source_target_pairs={{0,1},{1,0},{2,3},{3,2},{4,5},{5,4},{6,7},{7,6},{8,9},{9,8},{10,11... | collective-permute-start | bytes 1572872 | tf_op jit(solution)/shard_map/ppermute | solution.py:349
  52.6 6.4 %collective-permute-start.25 = (bf16[16,8192]{1,0:T(8,128)(2,1)S(1)}, bf16[16,8192]{1,0:T(8,128)(2,1)S(1)}, u32[]{:S(2)}, u32[]{:S(2)}) collective-permute-start(bf16[16,8192]{1,0:T(8,128)(2,1)S(1)} %added.7), channel_id=1, source_target_pairs={{0,4},{1,3},{4,8},{5,1},{8,12},{9,5},{12,14},{13,9},{14,10},{15,13... | collective-permute-start | bytes 786440 | tf_op jit(solution)/shard_map/ppermute | solution.py:346
  54.0 7.8 %collective-permute-start.29 = (bf16[16,8192]{1,0:T(8,128)(2,1)S(1)}, bf16[16,8192]{1,0:T(8,128)(2,1)S(1)}, u32[]{:S(2)}, u32[]{:S(2)}) collective-permute-start(bf16[16,8192]{1,0:T(8,128)(2,1)S(1)} %added.11), channel_id=1, source_target_pairs={{0,4},{1,3},{4,8},{5,1},{8,12},{9,5},{12,14},{13,9},{14,10},{15,13... | collective-permute-start | bytes 786440 | tf_op jit(solution)/shard_map/ppermute | solution.py:346
  55.9 11.1 %collective-permute-start.21 = (bf16[32,8192]{1,0:T(8,128)(2,1)S(1)}, bf16[32,8192]{1,0:T(8,128)(2,1)S(1)}, u32[]{:S(2)}, u32[]{:S(2)}) collective-permute-start(bf16[32,8192]{1,0:T(8,128)(2,1)S(1)} %get-tuple-element.29), channel_id=1, source_target_pairs={{0,1},{1,0},{2,3},{3,2},{4,5},{5,4},{6,7},{7,6},{8,9},{9,8},{10,11... | collective-permute-start | bytes 1572872 | tf_op jit(solution)/shard_map/ppermute | solution.py:349
  59.2 6.4 %collective-permute-start.26 = (bf16[16,8192]{1,0:T(8,128)(2,1)S(1)}, bf16[16,8192]{1,0:T(8,128)(2,1)S(1)}, u32[]{:S(2)}, u32[]{:S(2)}) collective-permute-start(bf16[16,8192]{1,0:T(8,128)(2,1)S(1)} %added.8), channel_id=1, source_target_pairs={{0,4},{1,3},{4,8},{5,1},{8,12},{9,5},{12,14},{13,9},{14,10},{15,13... | collective-permute-start | bytes 786440 | tf_op jit(solution)/shard_map/ppermute | solution.py:346
  62.0 6.4 %collective-permute-start.30 = (bf16[16,8192]{1,0:T(8,128)(2,1)S(1)}, bf16[16,8192]{1,0:T(8,128)(2,1)S(1)}, u32[]{:S(2)}, u32[]{:S(2)}) collective-permute-start(bf16[16,8192]{1,0:T(8,128)(2,1)S(1)} %added.12), channel_id=1, source_target_pairs={{0,4},{1,3},{4,8},{5,1},{8,12},{9,5},{12,14},{13,9},{14,10},{15,13... | collective-permute-start | bytes 786440 | tf_op jit(solution)/shard_map/ppermute | solution.py:346
  65.7 6.4 %collective-permute-start.27 = (bf16[16,8192]{1,0:T(8,128)(2,1)S(1)}, bf16[16,8192]{1,0:T(8,128)(2,1)S(1)}, u32[]{:S(2)}, u32[]{:S(2)}) collective-permute-start(bf16[16,8192]{1,0:T(8,128)(2,1)S(1)} %added.9), channel_id=1, source_target_pairs={{0,4},{1,3},{4,8},{5,1},{8,12},{9,5},{12,14},{13,9},{14,10},{15,13... | collective-permute-start | bytes 786440 | tf_op jit(solution)/shard_map/ppermute | solution.py:346
  68.5 6.4 %collective-permute-start.31 = (bf16[16,8192]{1,0:T(8,128)(2,1)S(1)}, bf16[16,8192]{1,0:T(8,128)(2,1)S(1)}, u32[]{:S(2)}, u32[]{:S(2)}) collective-permute-start(bf16[16,8192]{1,0:T(8,128)(2,1)S(1)} %added.13), channel_id=1, source_target_pairs={{0,4},{1,3},{4,8},{5,1},{8,12},{9,5},{12,14},{13,9},{14,10},{15,13... | collective-permute-start | bytes 786440 | tf_op jit(solution)/shard_map/ppermute | solution.py:346
  69.8 5.1 %collective-permute-start.20 = (bf16[16,8192]{1,0:T(8,128)(2,1)S(1)}, bf16[16,8192]{1,0:T(8,128)(2,1)S(1)}, u32[]{:S(2)}, u32[]{:S(2)}) collective-permute-start(bf16[16,8192]{1,0:T(8,128)(2,1)S(1)} %get-tuple-element.27), channel_id=1, source_target_pairs={{0,1},{1,0},{2,3},{3,2},{4,5},{5,4},{6,7},{7,6},{8,9},{9,8},{10,11... | collective-permute-start | bytes 786440 | tf_op jit(solution)/shard_map/ppermute | solution.py:349
  72.2 6.4 %collective-permute-start.28 = (bf16[16,8192]{1,0:T(8,128)(2,1)S(1)}, bf16[16,8192]{1,0:T(8,128)(2,1)S(1)}, u32[]{:S(2)}, u32[]{:S(2)}) collective-permute-start(bf16[16,8192]{1,0:T(8,128)(2,1)S(1)} %added.10), channel_id=1, source_target_pairs={{0,4},{1,3},{4,8},{5,1},{8,12},{9,5},{12,14},{13,9},{14,10},{15,13... | collective-permute-start | bytes 786440 | tf_op jit(solution)/shard_map/ppermute | solution.py:346
  74.9 3.7 %collective-permute-start.32 = (bf16[16,8192]{1,0:T(8,128)(2,1)S(1)}, bf16[16,8192]{1,0:T(8,128)(2,1)S(1)}, u32[]{:S(2)}, u32[]{:S(2)}) collective-permute-start(bf16[16,8192]{1,0:T(8,128)(2,1)S(1)} %collective-permute-done.31), channel_id=1, source_target_pairs={{0,1},{1,0},{2,3},{3,2},{4,5},{5,4},{6,7},{7,6},{8,9},{9,8},{10,11... | collective-permute-start | bytes 786440 | tf_op jit(solution)/shard_map/ppermute | solution.py:349

commit v11 on v10

--- a/solution.py
+++ b/solution.py
@@ -9,8 +9,8 @@
 
 F32 = jnp.float32
 BF16 = jnp.bfloat16
-VMEM_LIMIT = 20 * 1024 * 1024
-WEIGHTS = (2, 2, 6, 6)
+VMEM_LIMIT = 17 * 1024 * 1024
+WEIGHTS = (2, 2, 20, 20)
 
 
 def largest_tile(size, limit):
@@ -174,27 +174,22 @@
     )(adapters, far(expand), shrink, other, *pieces, *after)
 
 
-def product_kernel(first, w_ref, *refs):
+def product_kernel(first, depth, w_ref, *refs):
     pieces, out_ref = refs[:-2], refs[-1]
     rows = pieces[0].shape[0]
-    depth = w_ref.shape[0] // 2
-    size = depth
     places = arrivals(lax.axis_index("tp"), len(pieces), rows)
-    part = 0.0
-    for start in range(first, first + depth, size):
-        lhs = jnp.concatenate([piece[:, start : start + size] for piece in pieces], axis=0)
-        part += jnp.dot(lhs, w_ref[start : start + size, :], preferred_element_type=F32)
+    lhs = jnp.concatenate([piece[:, first : first + depth] for piece in pieces], axis=0)
+    part = jnp.dot(lhs, w_ref[first : first + depth, :], preferred_element_type=F32)
     for index, place in enumerate(places):
         out_ref[pl.ds(place, rows), :] = part[index * rows : (index + 1) * rows]
 
 
-def product(pieces, matrix, part, parts, after, weight):
-    rows, model = pieces[0].shape
+def product(pieces, matrix, first, depth, after, weight):
+    rows = pieces[0].shape[0]
     total = rows * len(pieces)
     width = matrix.shape[1]
-    depth = model // parts
-    return pl.pallas_call(
-        functools.partial(product_kernel, part * depth),
+    return pl.pallas_call(
+        functools.partial(product_kernel, first, depth),
         in_specs=whole(len(pieces) + 2),
         out_specs=whole(1)[0],
         out_shape=jax.ShapeDtypeStruct((total, width), F32),
@@ -375,15 +370,22 @@
         expand_matrices,
         theirs[:-1],
     )
-    work = [(gate_matrix, 0), (gate_matrix, 1), (up_matrix, 0), (up_matrix, 1)]
-    products, after, bit = [], rank, 1
+    rank = rank + cross(rank)
+    model = gate_matrix.shape[0]
+    cut = model * 2 // 3 // 256 * 256
+    rest = model - cut
+    work = [
+        [(gate_matrix, 0, cut)],
+        [(gate_matrix, cut, rest), (up_matrix, 0, rest)],
+        [(up_matrix, rest, cut)],
+    ]
+    products, after, bit = [], rank, 2
     while bit < members or work:
-        if work:
-            matrix, part = work.pop(0)
-            products.append(product(pieces, matrix, part, 2, after, WEIGHTS[len(products)]))
+        for part in work.pop(0) if work else []:
+            products.append(product(pieces, *part, after, WEIGHTS[len(products)]))
         if bit < members:
             after = cross(rank, bit)
-            rank = rank + after if bit == 1 else jnp.concatenate([rank, after], axis=0)
+            rank = jnp.concatenate([rank, after], axis=0)
             bit *= 2
     hidden = finish(products, rank, expand, 2 * span, rows)
 

time: 79.8 us -> 80.7 us (1.011)
  waiting for transfers between devices: 27.2 us -> 32.9 us
  starting transfers between devices: 33.1 us -> 28.2 us
    ppermute x14, starting transfers between devices: 24.1 us -> 19.1 us  [step(): return lax.ppermute(x, 'tp', ring)]
    ppermute x14, waiting for transfers between devices: 25.4 us -> 30.3 us  [step(): return lax.ppermute(x, 'tp', ring)]
    ppermute x19, waiting for transfers between devices: 1.74 us -> 2.57 us  [cross(): return lax.ppermute(x, 'tp', crossing(members, bit))]
  transfers between devices with their start and end apart: 33 -> 33, of which waited for: 15 -> 16; matrix products, arithmetic and copies ran while one was open for 0% -> 0% of each run, Pallas kernels for 16% -> 16%
where the time goes in v11:
time: 80.7 us; the launch traced here: 80.6 us
  waiting for transfers between devices  32.9 us (41%)
  starting transfers between devices  28.2 us (35%)
  Pallas kernels  19.1 us (24%)
    ppermute x14, waiting for transfers between devices, step(): return lax.ppermute(x, 'tp', ring)  30.3 us
    ppermute x14, starting transfers between devices, step(): return lax.ppermute(x, 'tp', ring)  19.1 us
    pallas_call x4, Pallas kernels, product(): pl.pallas_call(functools.partial(product_kernel, first, depth), in_specs=...  9.54 us
    ppermute x19, starting transfers between devices, cross(): return lax.ppermute(x, 'tp', crossing(members, bit))  9.08 us
    pallas_call x1, Pallas kernels, down(): pl.pallas_call(functools.partial(down_kernel, groups, rows, size), in_spe...  4.7 us
    ppermute x19, waiting for transfers between devices, cross(): return lax.ppermute(x, 'tp', crossing(members, bit))  2.57 us
  transfers between devices with their start and end apart: 33, of which 16 were waited for; matrix products, arithmetic and copies ran while one was open for 0% of the time, Pallas kernels for 16%

profile of v11, /device:TPU:0, one launch (start us, length us, event | category | flops | bytes accessed | tf_op | source)
XLA Modules:
  0.0 80.6 jit_solution(14137451824086134565)
XLA Ops:
  0.0 0.5 collective-permute-start
  0.5 2.6 %collective-permute-start.1 = (bf16[16,8192]{1,0:T(8,128)(2,1)}, bf16[16,8192]{1,0:T(8,128)(2,1)S(1)}, u32[]{:S(2)}, u32[]{:S(2)}) collective-permute-start(bf16[16,8192]{1,0:T(8,128)(2,1)} %tokens_ref.1), channel_id=1, source_target_pairs={{0,4},{1,3},{4,8},{5,1},{8,12},{9,5},{12,14},{13,9},{14,10},{15,13... | collective-permute-start | bytes 786440 | tf_op jit(solution)/shard_map/ppermute | solution.py:341
  3.1 0.0 collective-permute-done.passed_in
  3.1 1.1 %anchor.1 = (bf16[16,8192]{1,0:T(8,128)(2,1)S(1)}, bf16[16,8192]{1,0:T(8,128)(2,1)S(1)}) custom-call(bf16[16,8192]{1,0:T(8,128)(2,1)} %tokens_ref.1, bf16[16,8192]{1,0:T(8,128)(2,1)S(1)} %collective-permute-done.passed_in), custom_call_target="tpu_custom_call", output_to_operand_aliasing={{1}: (1, {})} | custom-call | flops 30000001024 | tf_op jit(solution)/shard_map/anchor/pallas_call | solution.py:104
  4.2 0.0 slice-start.4
  4.2 1.7 %collective-permute-start.2 = (bf16[16,8192]{1,0:T(8,128)(2,1)S(1)}, bf16[16,8192]{1,0:T(8,128)(2,1)S(1)}, u32[]{:S(2)}, u32[]{:S(2)}) collective-permute-start(bf16[16,8192]{1,0:T(8,128)(2,1)S(1)} %get-tuple-element.23.refs_1_), channel_id=1, source_target_pairs={{0,4},{1,3},{4,8},{5,1},{8,12},{9,5},{12,14},{13,9},{14,10},{15,13... | collective-permute-start | bytes 786440 | tf_op jit(solution)/shard_map/ppermute | solution.py:341
  6.0 1.6 %collective-permute-done.1.refs_1_.refs_2_ = bf16[16,8192]{1,0:T(8,128)(2,1)S(1)} collective-permute-done((bf16[16,8192]{1,0:T(8,128)(2,1)}, bf16[16,8192]{1,0:T(8,128)(2,1)S(1)}, u32[]{:S(2)}, u32[]{:S(2)}) %collective-permute-start.1) | collective-permute-done | bytes 262176 | tf_op jit(solution)/shard_map/ppermute | solution.py:341
  7.6 2.1 %collective-permute-start.3 = (bf16[16,8192]{1,0:T(8,128)(2,1)S(1)}, bf16[16,8192]{1,0:T(8,128)(2,1)S(1)}, u32[]{:S(2)}, u32[]{:S(2)}) collective-permute-start(bf16[16,8192]{1,0:T(8,128)(2,1)S(1)} %collective-permute-done.1.refs_1_.refs_2_), channel_id=1, source_target_pairs={{0,4},{1,3},{4,8},{5,1},{8,12},{9,5},{12,14},{13,9},{14,10},{15,13... | collective-permute-start | bytes 786440 | tf_op jit(solution)/shard_map/ppermute | solution.py:341
  9.7 0.0 collective-permute-start.8
  9.7 1.0 %collective-permute-done.2.refs_2_.refs_3_ = bf16[16,8192]{1,0:T(8,128)(2,1)S(1)} collective-permute-done((bf16[16,8192]{1,0:T(8,128)(2,1)S(1)}, bf16[16,8192]{1,0:T(8,128)(2,1)S(1)}, u32[]{:S(2)}, u32[]{:S(2)}) %collective-permute-start.2) | collective-permute-done | bytes 262176 | tf_op jit(solution)/shard_map/ppermute | solution.py:341
  10.6 1.8 %collective-permute-start.4 = (bf16[16,8192]{1,0:T(8,128)(2,1)S(1)}, bf16[16,8192]{1,0:T(8,128)(2,1)S(1)}, u32[]{:S(2)}, u32[]{:S(2)}) collective-permute-start(bf16[16,8192]{1,0:T(8,128)(2,1)S(1)} %collective-permute-done.2.refs_2_.refs_3_), channel_id=1, source_target_pairs={{0,4},{1,3},{4,8},{5,1},{8,12},{9,5},{12,14},{13,9},{14,10},{15,13... | collective-permute-start | bytes 786440 | tf_op jit(solution)/shard_map/ppermute | solution.py:341
  12.5 1.5 %collective-permute-done.3.refs_3_.refs_4_ = bf16[16,8192]{1,0:T(8,128)(2,1)S(1)} collective-permute-done((bf16[16,8192]{1,0:T(8,128)(2,1)S(1)}, bf16[16,8192]{1,0:T(8,128)(2,1)S(1)}, u32[]{:S(2)}, u32[]{:S(2)}) %collective-permute-start.3) | collective-permute-done | bytes 262176 | tf_op jit(solution)/shard_map/ppermute | solution.py:341
  14.0 2.1 %collective-permute-start.5 = (bf16[16,8192]{1,0:T(8,128)(2,1)S(1)}, bf16[16,8192]{1,0:T(8,128)(2,1)S(1)}, u32[]{:S(2)}, u32[]{:S(2)}) collective-permute-start(bf16[16,8192]{1,0:T(8,128)(2,1)S(1)} %collective-permute-done.3.refs_3_.refs_4_), channel_id=1, source_target_pairs={{0,4},{1,3},{4,8},{5,1},{8,12},{9,5},{12,14},{13,9},{14,10},{15,13... | collective-permute-start | bytes 786440 | tf_op jit(solution)/shard_map/ppermute | solution.py:341
  16.0 0.0 collective-permute-done.8.refs_8_.refs_9_
  16.1 0.5 collective-permute-start.10
  16.6 0.5 collective-permute-done.4.refs_4_.refs_5_
  17.0 1.8 %collective-permute-start.6 = (bf16[16,8192]{1,0:T(8,128)(2,1)S(1)}, bf16[16,8192]{1,0:T(8,128)(2,1)S(1)}, u32[]{:S(2)}, u32[]{:S(2)}) collective-permute-start(bf16[16,8192]{1,0:T(8,128)(2,1)S(1)} %collective-permute-done.4.refs_4_.refs_5_), channel_id=1, source_target_pairs={{0,4},{1,3},{4,8},{5,1},{8,12},{9,5},{12,14},{13,9},{14,10},{15,13... | collective-permute-start | bytes 786440 | tf_op jit(solution)/shard_map/ppermute | solution.py:341
  18.9 1.5 %collective-permute-done.5.refs_5_.refs_6_ = bf16[16,8192]{1,0:T(8,128)(2,1)S(1)} collective-permute-done((bf16[16,8192]{1,0:T(8,128)(2,1)S(1)}, bf16[16,8192]{1,0:T(8,128)(2,1)S(1)}, u32[]{:S(2)}, u32[]{:S(2)}) %collective-permute-start.5) | collective-permute-done | bytes 262176 | tf_op jit(solution)/shard_map/ppermute | solution.py:341
  20.3 2.1 %collective-permute-start.7 = (bf16[16,8192]{1,0:T(8,128)(2,1)S(1)}, bf16[16,8192]{1,0:T(8,128)(2,1)S(1)}, u32[]{:S(2)}, u32[]{:S(2)}) collective-permute-start(bf16[16,8192]{1,0:T(8,128)(2,1)S(1)} %collective-permute-done.5.refs_5_.refs_6_), channel_id=1, source_target_pairs={{0,4},{1,3},{4,8},{5,1},{8,12},{9,5},{12,14},{13,9},{14,10},{15,13... | collective-permute-start | bytes 786440 | tf_op jit(solution)/shard_map/ppermute | solution.py:341
  22.4 0.5 collective-permute-start.12
  22.9 0.5 collective-permute-done.6.refs_6_.refs_7_
  23.4 3.3 %collective-permute-done.7.refs_7_.refs_8_ = bf16[16,8192]{1,0:T(8,128)(2,1)S(1)} collective-permute-done((bf16[16,8192]{1,0:T(8,128)(2,1)S(1)}, bf16[16,8192]{1,0:T(8,128)(2,1)S(1)}, u32[]{:S(2)}, u32[]{:S(2)}) %collective-permute-start.7) | collective-permute-done | bytes 262176 | tf_op jit(solution)/shard_map/ppermute | solution.py:341
  26.8 0.0 slice-start.5
  26.8 1.3 %rank.1 = (bf16[16,256]{1,0:T(8,128)(2,1)S(1)}, bf16[2,128,896]{2,1,0:T(8,128)(2,1)S(1)}) custom-call(s32[1,2]{1,0:T(1,128)S(1)} %bitcast.7, bf16[8,128,896]{2,1,0:T(8,128)(2,1)} %expand_ref.1, bf16[8,8,8192]{2,1,0:T(8,128)(2,1)S(1)} %bitcast.6, bf16[8,8,8192]{2,1,0:T(8,128)(2,1)S(1)} %collective-permute-done.15.other_ref, ...), custom_call_target="tpu_custom_call" | custom-call | flops 67108864 | bytes 4194304 | tf_op jit(solution)/shard_map/rank/pallas_call | solution.py:159
  28.1 0.6 collective-permute-start.16
  28.7 0.8 %collective-permute-done.16 = bf16[16,256]{1,0:T(8,128)(2,1)S(1)} collective-permute-done((bf16[16,256]{1,0:T(8,128)(2,1)S(1)}, bf16[16,256]{1,0:T(8,128)(2,1)S(1)}, u32[]{:S(2)}, u32[]{:S(2)}) %collective-permute-start.16) | collective-permute-done | bytes 8224 | tf_op jit(solution)/shard_map/ppermute | solution.py:344
  29.5 2.1 %collective-permute-start.17 = (bf16[16,256]{1,0:T(8,128)(2,1)S(1)}, bf16[16,256]{1,0:T(8,128)(2,1)S(1)}, u32[]{:S(2)}, u32[]{:S(2)}) collective-permute-start(bf16[16,256]{1,0:T(8,128)(2,1)S(1)} %add.3.refs_16_), channel_id=1, source_target_pairs={{0,2},{1,3},{2,0},{3,1},{4,6},{5,7},{6,4},{7,5},{8,10},{9,11},{10,... | collective-permute-start | bytes 24584 | tf_op jit(solution)/shard_map/ppermute | solution.py:344
  31.6 3.1 %product.4.gate_a = f32[256,896]{1,0:T(8,128)S(1)} custom-call(bf16[8192,896]{1,0:T(8,128)(2,1)S(1)} %copy-done, bf16[16,8192]{1,0:T(8,128)(2,1)S(1)} %get-tuple-element.22.refs_0_, bf16[16,8192]{1,0:T(8,128)(2,1)S(1)} %get-tuple-element.23.refs_1_, bf16[16,8192]{1,0:T(8,128)(2,1)S(1)} %collective-permute-done.1.refs_1_.refs_2_, ...), custom_call_target="tpu_custom_call" | custom-call | flops 2466250752 | bytes 12386304 | tf_op jit(solution)/shard_map/product/pallas_call | solution.py:191
  34.7 1.6 %collective-permute-start.18 = (bf16[32,256]{1,0:T(8,128)(2,1)S(1)}, bf16[32,256]{1,0:T(8,128)(2,1)S(1)}, u32[]{:S(2)}, u32[]{:S(2)}) collective-permute-start(bf16[32,256]{1,0:T(8,128)(2,1)S(1)} %pad_maximum_fusion.2), channel_id=1, source_target_pairs={{0,4},{1,5},{2,6},{3,7},{4,0},{5,1},{6,2},{7,3},{8,12},{9,13},{10,... | collective-permute-start | bytes 49160 | tf_op jit(solution)/shard_map/ppermute | solution.py:344
  36.4 1.7 %product.6.up_a = f32[256,896]{1,0:T(8,128)S(1)} custom-call(bf16[8192,896]{1,0:T(8,128)(2,1)S(1)} %bitcast.10, bf16[16,8192]{1,0:T(8,128)(2,1)S(1)} %get-tuple-element.22.refs_0_, bf16[16,8192]{1,0:T(8,128)(2,1)S(1)} %get-tuple-element.23.refs_1_, bf16[16,8192]{1,0:T(8,128)(2,1)S(1)} %collective-permute-done.1.refs_1_.refs_2_, ...), custom_call_target="tpu_custom_call" | custom-call | flops 12918456320 | bytes 6488064 | tf_op jit(solution)/shard_map/product/pallas_call | solution.py:191
  38.1 1.7 %product.5.gate_b = f32[256,896]{1,0:T(8,128)S(1)} custom-call(bf16[8192,896]{1,0:T(8,128)(2,1)S(1)} %copy-done, bf16[16,8192]{1,0:T(8,128)(2,1)S(1)} %get-tuple-element.22.refs_0_, bf16[16,8192]{1,0:T(8,128)(2,1)S(1)} %get-tuple-element.23.refs_1_, bf16[16,8192]{1,0:T(8,128)(2,1)S(1)} %collective-permute-done.1.refs_1_.refs_2_, ...), custom_call_target="tpu_custom_call" | custom-call | flops 1291845632 | bytes 6488064 | tf_op jit(solution)/shard_map/product/pallas_call | solution.py:191
  39.8 0.0 slice-start
  39.8 0.0 slice-start.1
  39.9 2.7 %collective-permute-start.19 = (bf16[64,256]{1,0:T(8,128)(2,1)S(1)}, bf16[64,256]{1,0:T(8,128)(2,1)S(1)}, u32[]{:S(2)}, u32[]{:S(2)}) collective-permute-start(bf16[64,256]{1,0:T(8,128)(2,1)S(1)} %pad_maximum_fusion.1), channel_id=1, source_target_pairs={{0,8},{1,9},{2,10},{3,11},{4,12},{5,13},{6,14},{7,15},{8,0},{9,1},... | collective-permute-start | bytes 98312 | tf_op jit(solution)/shard_map/ppermute | solution.py:344
  42.5 3.1 %product.7.up_b = f32[256,896]{1,0:T(8,128)S(1)} custom-call(bf16[8192,896]{1,0:T(8,128)(2,1)S(1)} %bitcast.10, bf16[16,8192]{1,0:T(8,128)(2,1)S(1)} %get-tuple-element.22.refs_0_, bf16[16,8192]{1,0:T(8,128)(2,1)S(1)} %get-tuple-element.23.refs_1_, bf16[16,8192]{1,0:T(8,128)(2,1)S(1)} %collective-permute-done.1.refs_1_.refs_2_, ...), custom_call_target="tpu_custom_call" | custom-call | flops 24662507520 | bytes 12386304 | tf_op jit(solution)/shard_map/product/pallas_call | solution.py:191
  45.6 0.0 copy-start.3
  45.6 0.8 finish.1.hidden_ref
  46.5 4.7 %down.1 = (bf16[16,8192]{1,0:T(8,128)(2,1)S(1)}, bf16[16,8192]{1,0:T(8,128)(2,1)S(1)}, bf16[16,8192]{1,0:T(8,128)(2,1)S(1)}, bf16[16,8192]{1,0:T(8,128)(2,1)S(1)...) custom-call(bf16[896,8192]{1,0:T(8,128)(2,1)S(1)} %bitcast.4, ...), custom_call_target="tpu_custom_call" | custom-call | flops 3758096384 | bytes 18874368 | tf_op jit(solution)/shard_map/down/pallas_call | solution.py:257
  51.2 0.1 collective-permute-start.23
  51.3 0.5 collective-permute-start.24
  51.7 0.1 collective-permute-start.22
  51.8 1.7 %collective-permute-done.24.refs_1_ = bf16[16,8192]{1,0:T(8,128)(2,1)S(1)} collective-permute-done((bf16[16,8192]{1,0:T(8,128)(2,1)S(1)}, bf16[16,8192]{1,0:T(8,128)(2,1)S(1)}, u32[]{:S(2)}, u32[]{:S(2)}) %collective-permute-start.24) | collective-permute-done | bytes 262176 | tf_op jit(solution)/shard_map/ppermute | solution.py:344
  53.5 0.1 added.7
  53.6 0.5 collective-permute-start.25
  54.1 0.1 added.11
  54.2 1.9 %collective-permute-start.29 = (bf16[16,8192]{1,0:T(8,128)(2,1)S(1)}, bf16[16,8192]{1,0:T(8,128)(2,1)S(1)}, u32[]{:S(2)}, u32[]{:S(2)}) collective-permute-start(bf16[16,8192]{1,0:T(8,128)(2,1)S(1)} %added.11), channel_id=1, source_target_pairs={{0,4},{1,3},{4,8},{5,1},{8,12},{9,5},{12,14},{13,9},{14,10},{15,13... | collective-permute-start | bytes 786440 | tf_op jit(solution)/shard_map/ppermute | solution.py:341
  56.0 4.0 %collective-permute-done.25.refs_2_ = bf16[16,8192]{1,0:T(8,128)(2,1)S(1)} collective-permute-done((bf16[16,8192]{1,0:T(8,128)(2,1)S(1)}, bf16[16,8192]{1,0:T(8,128)(2,1)S(1)}, u32[]{:S(2)}, u32[]{:S(2)}) %collective-permute-start.25) | collective-permute-done | bytes 262176 | tf_op jit(solution)/shard_map/ppermute | solution.py:341
  60.0 0.1 added.8
  60.1 0.5 collective-permute-start.26
  60.6 2.2 %collective-permute-done.29.refs_2_ = bf16[16,8192]{1,0:T(8,128)(2,1)S(1)} collective-permute-done((bf16[16,8192]{1,0:T(8,128)(2,1)S(1)}, bf16[16,8192]{1,0:T(8,128)(2,1)S(1)}, u32[]{:S(2)}, u32[]{:S(2)}) %collective-permute-start.29) | collective-permute-done | bytes 262176 | tf_op jit(solution)/shard_map/ppermute | solution.py:341
  62.8 0.1 added.12
  62.9 0.5 collective-permute-start.30
  63.4 3.1 %collective-permute-done.26.refs_2_ = bf16[16,8192]{1,0:T(8,128)(2,1)S(1)} collective-permute-done((bf16[16,8192]{1,0:T(8,128)(2,1)S(1)}, bf16[16,8192]{1,0:T(8,128)(2,1)S(1)}, u32[]{:S(2)}, u32[]{:S(2)}) %collective-permute-start.26) | collective-permute-done | bytes 262176 | tf_op jit(solution)/shard_map/ppermute | solution.py:341
  66.5 0.1 added.9
  66.6 0.5 collective-permute-start.27
  67.1 2.2 %collective-permute-done.30.refs_2_ = bf16[16,8192]{1,0:T(8,128)(2,1)S(1)} collective-permute-done((bf16[16,8192]{1,0:T(8,128)(2,1)S(1)}, bf16[16,8192]{1,0:T(8,128)(2,1)S(1)}, u32[]{:S(2)}, u32[]{:S(2)}) %collective-permute-start.30) | collective-permute-done | bytes 262176 | tf_op jit(solution)/shard_map/ppermute | solution.py:341
  69.3 0.1 added.13
  69.4 0.5 collective-permute-start.31
  70.0 3.1 %collective-permute-done.27.refs_2_ = bf16[16,8192]{1,0:T(8,128)(2,1)S(1)} collective-permute-done((bf16[16,8192]{1,0:T(8,128)(2,1)S(1)}, bf16[16,8192]{1,0:T(8,128)(2,1)S(1)}, u32[]{:S(2)}, u32[]{:S(2)}) %collective-permute-start.27) | collective-permute-done | bytes 262176 | tf_op jit(solution)/shard_map/ppermute | solution.py:341
  73.1 0.1 added.10
  73.2 0.5 collective-permute-start.28
  73.7 2.2 %collective-permute-done.31 = bf16[16,8192]{1,0:T(8,128)(2,1)S(1)} collective-permute-done((bf16[16,8192]{1,0:T(8,128)(2,1)S(1)}, bf16[16,8192]{1,0:T(8,128)(2,1)S(1)}, u32[]{:S(2)}, u32[]{:S(2)}) %collective-permute-start.31) | collective-permute-done | bytes 262176 | tf_op jit(solution)/shard_map/ppermute | solution.py:341
  75.9 3.7 %collective-permute-done.28.refs_2_ = bf16[16,8192]{1,0:T(8,128)(2,1)S(1)} collective-permute-done((bf16[16,8192]{1,0:T(8,128)(2,1)S(1)}, bf16[16,8192]{1,0:T(8,128)(2,1)S(1)}, u32[]{:S(2)}, u32[]{:S(2)}) %collective-permute-start.28) | collective-permute-done | bytes 262176 | tf_op jit(solution)/shard_map/ppermute | solution.py:341
  79.6 1.0 %last.1 = bf16[16,8192]{1,0:T(8,128)(2,1)} custom-call(s32[1,2]{1,0:T(1,128)S(1)} %bitcast.8, bf16[16,8192]{1,0:T(8,128)(2,1)S(1)} %get-tuple-element.26.refs_0_, bf16[16,8192]{1,0:T(8,128)(2,1)S(1)} %collective-permute-done.20.refs_1_, bf16[16,8192]{1,0:T(8,128)(2,1)S(1)} %collective-permute-done.28.refs_2_, ...), custom_call_target="tpu_custom_call" | custom-call | tf_op jit(solution)/shard_map/last/pallas_call | solution.py:291
  (48 shorter events, 0.1 us)
Async XLA Ops:
  0.0 6.0 %copy-start.1 = (bf16[8,8192,8]{1,2,0:T(8,128)(2,1)S(1)}, bf16[8,8192,8]{1,2,0:T(8,128)(2,1)}, u32[]{:S(2)}) copy-start(bf16[8,8192,8]{1,2,0:T(8,128)(2,1)} %param.12) | copy-start | bytes 3145732
  0.0 26.7 %copy-start.2 = (s32[2]{0:T(128)S(1)}, s32[2]{0:T(128)}, u32[]{:S(2)}) copy-start(s32[2]{0:T(128)} %param.14) | copy-start | bytes 28
  0.0 3.1 %collective-permute-start = (bf16[16,8192]{1,0:T(8,128)(2,1)}, bf16[16,8192]{1,0:T(8,128)(2,1)S(1)}, u32[]{:S(2)}, u32[]{:S(2)}) collective-permute-start(bf16[16,8192]{1,0:T(8,128)(2,1)} %tokens_ref.1), channel_id=1, source_target_pairs={{0,1},{1,0},{2,3},{3,2},{4,5},{5,4},{6,7},{7,6},{8,9},{9,8},{10,11... | collective-permute-start | bytes 786440 | tf_op jit(solution)/shard_map/ppermute | solution.py:344
  0.5 7.1 %collective-permute-start.1 = (bf16[16,8192]{1,0:T(8,128)(2,1)}, bf16[16,8192]{1,0:T(8,128)(2,1)S(1)}, u32[]{:S(2)}, u32[]{:S(2)}) collective-permute-start(bf16[16,8192]{1,0:T(8,128)(2,1)} %tokens_ref.1), channel_id=1, source_target_pairs={{0,4},{1,3},{4,8},{5,1},{8,12},{9,5},{12,14},{13,9},{14,10},{15,13... | collective-permute-start | bytes 786440 | tf_op jit(solution)/shard_map/ppermute | solution.py:341
  3.1 28.5 %copy-start = (bf16[8192,896]{1,0:T(8,128)(2,1)S(1)}, bf16[8192,896]{1,0:T(8,128)(2,1)}, u32[]{:S(2)}) copy-start(bf16[8192,896]{1,0:T(8,128)(2,1)} %w_ref.6) | copy-start | bytes 44040196
  4.2 32.2 %slice-start.4 = ((s8[14680064]{0:T(1024)(128)(4,1)}), s8[2097152]{0:T(1024)(128)(4,1)S(1)}, s32[]{:S(2)}) async-start(s8[14680064]{0:T(1024)(128)(4,1)} %bitcast.9), calls=%async_computation.4 | async-start | bytes 4194304
  4.2 6.4 %collective-permute-start.2 = (bf16[16,8192]{1,0:T(8,128)(2,1)S(1)}, bf16[16,8192]{1,0:T(8,128)(2,1)S(1)}, u32[]{:S(2)}, u32[]{:S(2)}) collective-permute-start(bf16[16,8192]{1,0:T(8,128)(2,1)S(1)} %get-tuple-element.23.refs_1_), channel_id=1, source_target_pairs={{0,4},{1,3},{4,8},{5,1},{8,12},{9,5},{12,14},{13,9},{14,10},{15,13... | collective-permute-start | bytes 786440 | tf_op jit(solution)/shard_map/ppermute | solution.py:341
  6.0 20.8 %collective-permute-start.15 = (bf16[8,8,8192]{2,1,0:T(8,128)(2,1)S(1)}, bf16[8,8,8192]{2,1,0:T(8,128)(2,1)S(1)}, u32[]{:S(2)}, u32[]{:S(2)}) collective-permute-start(bf16[8,8,8192]{2,1,0:T(8,128)(2,1)S(1)} %bitcast.5), channel_id=1, source_target_pairs={{0,1},{1,0},{2,3},{3,2},{4,5},{5,4},{6,7},{7,6},{8,9},{9,8},{10,11... | collective-permute-start | bytes 3145736 | tf_op jit(solution)/shard_map/ppermute | solution.py:344
  7.6 6.4 %collective-permute-start.3 = (bf16[16,8192]{1,0:T(8,128)(2,1)S(1)}, bf16[16,8192]{1,0:T(8,128)(2,1)S(1)}, u32[]{:S(2)}, u32[]{:S(2)}) collective-permute-start(bf16[16,8192]{1,0:T(8,128)(2,1)S(1)} %collective-permute-done.1.refs_1_.refs_2_), channel_id=1, source_target_pairs={{0,4},{1,3},{4,8},{5,1},{8,12},{9,5},{12,14},{13,9},{14,10},{15,13... | collective-permute-start | bytes 786440 | tf_op jit(solution)/shard_map/ppermute | solution.py:341
  9.7 6.4 %collective-permute-start.8 = (bf16[16,8192]{1,0:T(8,128)(2,1)S(1)}, bf16[16,8192]{1,0:T(8,128)(2,1)S(1)}, u32[]{:S(2)}, u32[]{:S(2)}) collective-permute-start(bf16[16,8192]{1,0:T(8,128)(2,1)S(1)} %collective-permute-done.1.refs_1_.refs_2_), channel_id=1, source_target_pairs={{0,1},{1,0},{2,3},{3,2},{4,5},{5,4},{6,7},{7,6},{8,9},{9,8},{10,11... | collective-permute-start | bytes 786440 | tf_op jit(solution)/shard_map/ppermute | solution.py:344
  10.6 6.4 %collective-permute-start.4 = (bf16[16,8192]{1,0:T(8,128)(2,1)S(1)}, bf16[16,8192]{1,0:T(8,128)(2,1)S(1)}, u32[]{:S(2)}, u32[]{:S(2)}) collective-permute-start(bf16[16,8192]{1,0:T(8,128)(2,1)S(1)} %collective-permute-done.2.refs_2_.refs_3_), channel_id=1, source_target_pairs={{0,4},{1,3},{4,8},{5,1},{8,12},{9,5},{12,14},{13,9},{14,10},{15,13... | collective-permute-start | bytes 786440 | tf_op jit(solution)/shard_map/ppermute | solution.py:341
  14.0 6.4 %collective-permute-start.5 = (bf16[16,8192]{1,0:T(8,128)(2,1)S(1)}, bf16[16,8192]{1,0:T(8,128)(2,1)S(1)}, u32[]{:S(2)}, u32[]{:S(2)}) collective-permute-start(bf16[16,8192]{1,0:T(8,128)(2,1)S(1)} %collective-permute-done.3.refs_3_.refs_4_), channel_id=1, source_target_pairs={{0,4},{1,3},{4,8},{5,1},{8,12},{9,5},{12,14},{13,9},{14,10},{15,13... | collective-permute-start | bytes 786440 | tf_op jit(solution)/shard_map/ppermute | solution.py:341
  16.0 6.4 %collective-permute-start.9 = (bf16[16,8192]{1,0:T(8,128)(2,1)S(1)}, bf16[16,8192]{1,0:T(8,128)(2,1)S(1)}, u32[]{:S(2)}, u32[]{:S(2)}) collective-permute-start(bf16[16,8192]{1,0:T(8,128)(2,1)S(1)} %collective-permute-done.2.refs_2_.refs_3_), channel_id=1, source_target_pairs={{0,1},{1,0},{2,3},{3,2},{4,5},{5,4},{6,7},{7,6},{8,9},{9,8},{10,11... | collective-permute-start | bytes 786440 | tf_op jit(solution)/shard_map/ppermute | solution.py:344
  16.1 6.4 %collective-permute-start.10 = (bf16[16,8192]{1,0:T(8,128)(2,1)S(1)}, bf16[16,8192]{1,0:T(8,128)(2,1)S(1)}, u32[]{:S(2)}, u32[]{:S(2)}) collective-permute-start(bf16[16,8192]{1,0:T(8,128)(2,1)S(1)} %collective-permute-done.3.refs_3_.refs_4_), channel_id=1, source_target_pairs={{0,1},{1,0},{2,3},{3,2},{4,5},{5,4},{6,7},{7,6},{8,9},{9,8},{10,11... | collective-permute-start | bytes 786440 | tf_op jit(solution)/shard_map/ppermute | solution.py:344
  17.0 6.4 %collective-permute-start.6 = (bf16[16,8192]{1,0:T(8,128)(2,1)S(1)}, bf16[16,8192]{1,0:T(8,128)(2,1)S(1)}, u32[]{:S(2)}, u32[]{:S(2)}) collective-permute-start(bf16[16,8192]{1,0:T(8,128)(2,1)S(1)} %collective-permute-done.4.refs_4_.refs_5_), channel_id=1, source_target_pairs={{0,4},{1,3},{4,8},{5,1},{8,12},{9,5},{12,14},{13,9},{14,10},{15,13... | collective-permute-start | bytes 786440 | tf_op jit(solution)/shard_map/ppermute | solution.py:341
  20.3 6.4 %collective-permute-start.7 = (bf16[16,8192]{1,0:T(8,128)(2,1)S(1)}, bf16[16,8192]{1,0:T(8,128)(2,1)S(1)}, u32[]{:S(2)}, u32[]{:S(2)}) collective-permute-start(bf16[16,8192]{1,0:T(8,128)(2,1)S(1)} %collective-permute-done.5.refs_5_.refs_6_), channel_id=1, source_target_pairs={{0,4},{1,3},{4,8},{5,1},{8,12},{9,5},{12,14},{13,9},{14,10},{15,13... | collective-permute-start | bytes 786440 | tf_op jit(solution)/shard_map/ppermute | solution.py:341
  22.4 4.3 %collective-permute-start.11 = (bf16[16,8192]{1,0:T(8,128)(2,1)S(1)}, bf16[16,8192]{1,0:T(8,128)(2,1)S(1)}, u32[]{:S(2)}, u32[]{:S(2)}) collective-permute-start(bf16[16,8192]{1,0:T(8,128)(2,1)S(1)} %collective-permute-done.4.refs_4_.refs_5_), channel_id=1, source_target_pairs={{0,1},{1,0},{2,3},{3,2},{4,5},{5,4},{6,7},{7,6},{8,9},{9,8},{10,11... | collective-permute-start | bytes 786440 | tf_op jit(solution)/shard_map/ppermute | solution.py:344
  22.4 4.3 %collective-permute-start.12 = (bf16[16,8192]{1,0:T(8,128)(2,1)S(1)}, bf16[16,8192]{1,0:T(8,128)(2,1)S(1)}, u32[]{:S(2)}, u32[]{:S(2)}) collective-permute-start(bf16[16,8192]{1,0:T(8,128)(2,1)S(1)} %collective-permute-done.5.refs_5_.refs_6_), channel_id=1, source_target_pairs={{0,1},{1,0},{2,3},{3,2},{4,5},{5,4},{6,7},{7,6},{8,9},{9,8},{10,11... | collective-permute-start | bytes 786440 | tf_op jit(solution)/shard_map/ppermute | solution.py:344
  23.4 3.3 %collective-permute-start.13 = (bf16[16,8192]{1,0:T(8,128)(2,1)S(1)}, bf16[16,8192]{1,0:T(8,128)(2,1)S(1)}, u32[]{:S(2)}, u32[]{:S(2)}) collective-permute-start(bf16[16,8192]{1,0:T(8,128)(2,1)S(1)} %collective-permute-done.6.refs_6_.refs_7_), channel_id=1, source_target_pairs={{0,1},{1,0},{2,3},{3,2},{4,5},{5,4},{6,7},{7,6},{8,9},{9,8},{10,11... | collective-permute-start | bytes 786440 | tf_op jit(solution)/shard_map/ppermute | solution.py:344
  26.7 4.9 %collective-permute-start.14 = (bf16[16,8192]{1,0:T(8,128)(2,1)S(1)}, bf16[16,8192]{1,0:T(8,128)(2,1)S(1)}, u32[]{:S(2)}, u32[]{:S(2)}) collective-permute-start(bf16[16,8192]{1,0:T(8,128)(2,1)S(1)} %collective-permute-done.7.refs_7_.refs_8_), channel_id=1, source_target_pairs={{0,1},{1,0},{2,3},{3,2},{4,5},{5,4},{6,7},{7,6},{8,9},{9,8},{10,11... | collective-permute-start | bytes 786440 | tf_op jit(solution)/shard_map/ppermute | solution.py:344
  26.8 9.6 %slice-start.5 = ((s8[14680064]{0:T(1024)(128)(4,1)}), s8[4194304]{0:T(1024)(128)(4,1)S(1)}, s32[]{:S(2)}) async-start(s8[14680064]{0:T(1024)(128)(4,1)} %bitcast.9), calls=%async_computation.5 | async-start | bytes 8388608
  28.1 1.4 %collective-permute-start.16 = (bf16[16,256]{1,0:T(8,128)(2,1)S(1)}, bf16[16,256]{1,0:T(8,128)(2,1)S(1)}, u32[]{:S(2)}, u32[]{:S(2)}) collective-permute-start(bf16[16,256]{1,0:T(8,128)(2,1)S(1)} %get-tuple-element.24), channel_id=1, source_target_pairs={{0,1},{1,0},{2,3},{3,2},{4,5},{5,4},{6,7},{7,6},{8,9},{9,8},{10,11... | collective-permute-start | bytes 24584 | tf_op jit(solution)/shard_map/ppermute | solution.py:344
  29.5 6.9 %slice-start.6 = ((s8[14680064]{0:T(1024)(128)(4,1)}), s8[4194304]{0:T(1024)(128)(4,1)S(1)}, s32[]{:S(2)}) async-start(s8[14680064]{0:T(1024)(128)(4,1)} %bitcast.9), calls=%async_computation.6 | async-start | bytes 8388608
  29.5 6.9 %slice-start.7 = ((s8[14680064]{0:T(1024)(128)(4,1)}), s8[4194304]{0:T(1024)(128)(4,1)S(1)}, s32[]{:S(2)}) async-start(s8[14680064]{0:T(1024)(128)(4,1)} %bitcast.9), calls=%async_computation.7 | async-start | bytes 8388608
  29.5 5.2 %collective-permute-start.17 = (bf16[16,256]{1,0:T(8,128)(2,1)S(1)}, bf16[16,256]{1,0:T(8,128)(2,1)S(1)}, u32[]{:S(2)}, u32[]{:S(2)}) collective-permute-start(bf16[16,256]{1,0:T(8,128)(2,1)S(1)} %add.3.refs_16_), channel_id=1, source_target_pairs={{0,2},{1,3},{2,0},{3,1},{4,6},{5,7},{6,4},{7,5},{8,10},{9,11},{10,... | collective-permute-start | bytes 24584 | tf_op jit(solution)/shard_map/ppermute | solution.py:344
  34.7 5.1 %collective-permute-start.18 = (bf16[32,256]{1,0:T(8,128)(2,1)S(1)}, bf16[32,256]{1,0:T(8,128)(2,1)S(1)}, u32[]{:S(2)}, u32[]{:S(2)}) collective-permute-start(bf16[32,256]{1,0:T(8,128)(2,1)S(1)} %pad_maximum_fusion.2), channel_id=1, source_target_pairs={{0,4},{1,5},{2,6},{3,7},{4,0},{5,1},{6,2},{7,3},{8,12},{9,13},{10,... | collective-permute-start | bytes 49160 | tf_op jit(solution)/shard_map/ppermute | solution.py:344
  39.8 6.6 %slice-start = ((s8[14680064]{0:T(1024)(128)(4,1)}), s8[4194304]{0:T(1024)(128)(4,1)S(1)}, s32[]{:S(2)}) async-start(s8[14680064]{0:T(1024)(128)(4,1)} %bitcast.3), calls=%async_computation | async-start | bytes 8388608
  39.8 6.6 %slice-start.1 = ((s8[14680064]{0:T(1024)(128)(4,1)}), s8[4194304]{0:T(1024)(128)(4,1)S(1)}, s32[]{:S(2)}) async-start(s8[14680064]{0:T(1024)(128)(4,1)} %bitcast.3), calls=%async_computation.1 | async-start | bytes 8388608
  39.9 6.6 %slice-start.2 = ((s8[14680064]{0:T(1024)(128)(4,1)}), s8[4194304]{0:T(1024)(128)(4,1)S(1)}, s32[]{:S(2)}) async-start(s8[14680064]{0:T(1024)(128)(4,1)} %bitcast.3), calls=%async_computation.2 | async-start | bytes 8388608
  39.9 6.6 %slice-start.3 = ((s8[14680064]{0:T(1024)(128)(4,1)}), s8[2097152]{0:T(1024)(128)(4,1)S(1)}, s32[]{:S(2)}) async-start(s8[14680064]{0:T(1024)(128)(4,1)} %bitcast.3), calls=%async_computation.3 | async-start | bytes 4194304
  39.9 5.7 %collective-permute-start.19 = (bf16[64,256]{1,0:T(8,128)(2,1)S(1)}, bf16[64,256]{1,0:T(8,128)(2,1)S(1)}, u32[]{:S(2)}, u32[]{:S(2)}) collective-permute-start(bf16[64,256]{1,0:T(8,128)(2,1)S(1)} %pad_maximum_fusion.1), channel_id=1, source_target_pairs={{0,8},{1,9},{2,10},{3,11},{4,12},{5,13},{6,14},{7,15},{8,0},{9,1},... | collective-permute-start | bytes 98312 | tf_op jit(solution)/shard_map/ppermute | solution.py:344
  45.6 34.0 %copy-start.3 = (s32[2]{0:T(128)S(1)}, s32[2]{0:T(128)}, u32[]{:S(2)}) copy-start(s32[2]{0:T(128)} %param.15) | copy-start | bytes 28
  51.2 2.9 %collective-permute-start.23 = (bf16[32,8192]{1,0:T(8,128)(2,1)S(1)}, bf16[32,8192]{1,0:T(8,128)(2,1)S(1)}, u32[]{:S(2)}, u32[]{:S(2)}) collective-permute-start(bf16[32,8192]{1,0:T(8,128)(2,1)S(1)} %get-tuple-element.33), channel_id=1, source_target_pairs={{0,1},{1,0},{2,3},{3,2},{4,5},{5,4},{6,7},{7,6},{8,9},{9,8},{10,11... | collective-permute-start | bytes 1572872 | tf_op jit(solution)/shard_map/ppermute | solution.py:344
  51.3 2.3 %collective-permute-start.24 = (bf16[16,8192]{1,0:T(8,128)(2,1)S(1)}, bf16[16,8192]{1,0:T(8,128)(2,1)S(1)}, u32[]{:S(2)}, u32[]{:S(2)}) collective-permute-start(bf16[16,8192]{1,0:T(8,128)(2,1)S(1)} %get-tuple-element.35), channel_id=1, source_target_pairs={{0,1},{1,0},{2,3},{3,2},{4,5},{5,4},{6,7},{7,6},{8,9},{9,8},{10,11... | collective-permute-start | bytes 786440 | tf_op jit(solution)/shard_map/ppermute | solution.py:344
  51.7 8.9 %collective-permute-start.22 = (bf16[32,8192]{1,0:T(8,128)(2,1)S(1)}, bf16[32,8192]{1,0:T(8,128)(2,1)S(1)}, u32[]{:S(2)}, u32[]{:S(2)}) collective-permute-start(bf16[32,8192]{1,0:T(8,128)(2,1)S(1)} %get-tuple-element.31), channel_id=1, source_target_pairs={{0,1},{1,0},{2,3},{3,2},{4,5},{5,4},{6,7},{7,6},{8,9},{9,8},{10,11... | collective-permute-start | bytes 1572872 | tf_op jit(solution)/shard_map/ppermute | solution.py:344
  53.6 6.4 %collective-permute-start.25 = (bf16[16,8192]{1,0:T(8,128)(2,1)S(1)}, bf16[16,8192]{1,0:T(8,128)(2,1)S(1)}, u32[]{:S(2)}, u32[]{:S(2)}) collective-permute-start(bf16[16,8192]{1,0:T(8,128)(2,1)S(1)} %added.7), channel_id=1, source_target_pairs={{0,4},{1,3},{4,8},{5,1},{8,12},{9,5},{12,14},{13,9},{14,10},{15,13... | collective-permute-start | bytes 786440 | tf_op jit(solution)/shard_map/ppermute | solution.py:341
  54.2 8.7 %collective-permute-start.29 = (bf16[16,8192]{1,0:T(8,128)(2,1)S(1)}, bf16[16,8192]{1,0:T(8,128)(2,1)S(1)}, u32[]{:S(2)}, u32[]{:S(2)}) collective-permute-start(bf16[16,8192]{1,0:T(8,128)(2,1)S(1)} %added.11), channel_id=1, source_target_pairs={{0,4},{1,3},{4,8},{5,1},{8,12},{9,5},{12,14},{13,9},{14,10},{15,13... | collective-permute-start | bytes 786440 | tf_op jit(solution)/shard_map/ppermute | solution.py:341
  56.0 11.1 %collective-permute-start.21 = (bf16[32,8192]{1,0:T(8,128)(2,1)S(1)}, bf16[32,8192]{1,0:T(8,128)(2,1)S(1)}, u32[]{:S(2)}, u32[]{:S(2)}) collective-permute-start(bf16[32,8192]{1,0:T(8,128)(2,1)S(1)} %get-tuple-element.29), channel_id=1, source_target_pairs={{0,1},{1,0},{2,3},{3,2},{4,5},{5,4},{6,7},{7,6},{8,9},{9,8},{10,11... | collective-permute-start | bytes 1572872 | tf_op jit(solution)/shard_map/ppermute | solution.py:344
  60.1 6.4 %collective-permute-start.26 = (bf16[16,8192]{1,0:T(8,128)(2,1)S(1)}, bf16[16,8192]{1,0:T(8,128)(2,1)S(1)}, u32[]{:S(2)}, u32[]{:S(2)}) collective-permute-start(bf16[16,8192]{1,0:T(8,128)(2,1)S(1)} %added.8), channel_id=1, source_target_pairs={{0,4},{1,3},{4,8},{5,1},{8,12},{9,5},{12,14},{13,9},{14,10},{15,13... | collective-permute-start | bytes 786440 | tf_op jit(solution)/shard_map/ppermute | solution.py:341
  62.9 6.4 %collective-permute-start.30 = (bf16[16,8192]{1,0:T(8,128)(2,1)S(1)}, bf16[16,8192]{1,0:T(8,128)(2,1)S(1)}, u32[]{:S(2)}, u32[]{:S(2)}) collective-permute-start(bf16[16,8192]{1,0:T(8,128)(2,1)S(1)} %added.12), channel_id=1, source_target_pairs={{0,4},{1,3},{4,8},{5,1},{8,12},{9,5},{12,14},{13,9},{14,10},{15,13... | collective-permute-start | bytes 786440 | tf_op jit(solution)/shard_map/ppermute | solution.py:341
  66.6 6.4 %collective-permute-start.27 = (bf16[16,8192]{1,0:T(8,128)(2,1)S(1)}, bf16[16,8192]{1,0:T(8,128)(2,1)S(1)}, u32[]{:S(2)}, u32[]{:S(2)}) collective-permute-start(bf16[16,8192]{1,0:T(8,128)(2,1)S(1)} %added.9), channel_id=1, source_target_pairs={{0,4},{1,3},{4,8},{5,1},{8,12},{9,5},{12,14},{13,9},{14,10},{15,13... | collective-permute-start | bytes 786440 | tf_op jit(solution)/shard_map/ppermute | solution.py:341
  69.4 6.4 %collective-permute-start.31 = (bf16[16,8192]{1,0:T(8,128)(2,1)S(1)}, bf16[16,8192]{1,0:T(8,128)(2,1)S(1)}, u32[]{:S(2)}, u32[]{:S(2)}) collective-permute-start(bf16[16,8192]{1,0:T(8,128)(2,1)S(1)} %added.13), channel_id=1, source_target_pairs={{0,4},{1,3},{4,8},{5,1},{8,12},{9,5},{12,14},{13,9},{14,10},{15,13... | collective-permute-start | bytes 786440 | tf_op jit(solution)/shard_map/ppermute | solution.py:341
  69.9 5.9 %collective-permute-start.20 = (bf16[16,8192]{1,0:T(8,128)(2,1)S(1)}, bf16[16,8192]{1,0:T(8,128)(2,1)S(1)}, u32[]{:S(2)}, u32[]{:S(2)}) collective-permute-start(bf16[16,8192]{1,0:T(8,128)(2,1)S(1)} %get-tuple-element.27), channel_id=1, source_target_pairs={{0,1},{1,0},{2,3},{3,2},{4,5},{5,4},{6,7},{7,6},{8,9},{9,8},{10,11... | collective-permute-start | bytes 786440 | tf_op jit(solution)/shard_map/ppermute | solution.py:344
  73.2 6.4 %collective-permute-start.28 = (bf16[16,8192]{1,0:T(8,128)(2,1)S(1)}, bf16[16,8192]{1,0:T(8,128)(2,1)S(1)}, u32[]{:S(2)}, u32[]{:S(2)}) collective-permute-start(bf16[16,8192]{1,0:T(8,128)(2,1)S(1)} %added.10), channel_id=1, source_target_pairs={{0,4},{1,3},{4,8},{5,1},{8,12},{9,5},{12,14},{13,9},{14,10},{15,13... | collective-permute-start | bytes 786440 | tf_op jit(solution)/shard_map/ppermute | solution.py:341
  75.9 3.7 %collective-permute-start.32 = (bf16[16,8192]{1,0:T(8,128)(2,1)S(1)}, bf16[16,8192]{1,0:T(8,128)(2,1)S(1)}, u32[]{:S(2)}, u32[]{:S(2)}) collective-permute-start(bf16[16,8192]{1,0:T(8,128)(2,1)S(1)} %collective-permute-done.31), channel_id=1, source_target_pairs={{0,1},{1,0},{2,3},{3,2},{4,5},{5,4},{6,7},{7,6},{8,9},{9,8},{10,11... | collective-permute-start | bytes 786440 | tf_op jit(solution)/shard_map/ppermute | solution.py:344

commit v12 on v10

--- a/solution.py
+++ b/solution.py
@@ -9,8 +9,8 @@
 
 F32 = jnp.float32
 BF16 = jnp.bfloat16
-VMEM_LIMIT = 20 * 1024 * 1024
-WEIGHTS = (2, 2, 6, 6)
+VMEM_LIMIT = 8 * 1024 * 1024
+WEIGHTS = (6, 6, 6, 6)
 
 
 def largest_tile(size, limit):
@@ -174,37 +174,56 @@
     )(adapters, far(expand), shrink, other, *pieces, *after)
 
 
-def product_kernel(first, w_ref, *refs):
-    pieces, out_ref = refs[:-2], refs[-1]
+def product_kernel(first, depth, main, role, w_ref, *refs):
+    outs = 1 if role is None else 2
+    refs, outs = refs[:-outs], refs[-outs:]
+    aside, pieces = (refs[:1], refs[1:-1]) if role == 1 else ((), refs[:-1])
     rows = pieces[0].shape[0]
-    depth = w_ref.shape[0] // 2
-    size = depth
     places = arrivals(lax.axis_index("tp"), len(pieces), rows)
-    part = 0.0
-    for start in range(first, first + depth, size):
-        lhs = jnp.concatenate([piece[:, start : start + size] for piece in pieces], axis=0)
-        part += jnp.dot(lhs, w_ref[start : start + size, :], preferred_element_type=F32)
-    for index, place in enumerate(places):
-        out_ref[pl.ds(place, rows), :] = part[index * rows : (index + 1) * rows]
-
-
-def product(pieces, matrix, part, parts, after, weight):
-    rows, model = pieces[0].shape
+    lhs = jnp.concatenate([piece[:, first : first + depth] for piece in pieces], axis=0)
+    span = slice(first, first + depth)
+
+    def store(out_ref, weights):
+        part = jnp.dot(lhs, weights, preferred_element_type=F32)
+        for index, place in enumerate(places):
+            out_ref[pl.ds(place, rows), :] = part[index * rows : (index + 1) * rows]
+
+    store(outs[0], w_ref[span, :main])
+    if role == 0:
+        outs[1][...] = w_ref[span, main:]
+    elif role == 1:
+        store(outs[1], jnp.concatenate([w_ref[span, main:], aside[0][...]], axis=1))
+
+
+def product(pieces, matrix, part, parts, after, weight, aside):
+    rows = pieces[0].shape[0]
     total = rows * len(pieces)
-    width = matrix.shape[1]
+    model, width = matrix.shape
     depth = model // parts
-    return pl.pallas_call(
-        functools.partial(product_kernel, part * depth),
-        in_specs=whole(len(pieces) + 2),
-        out_specs=whole(1)[0],
-        out_shape=jax.ShapeDtypeStruct((total, width), F32),
+    tail = 128 if width % 256 == 128 else 0
+    main = width - tail
+    out_shape = [jax.ShapeDtypeStruct((total, main), F32)]
+    role, extra = None, []
+    if tail and isinstance(aside, int):
+        role = 0
+        out_shape.append(jax.ShapeDtypeStruct((depth, tail), BF16))
+    elif tail:
+        role, extra = 1, [aside]
+        out_shape.append(jax.ShapeDtypeStruct((total, 2 * tail), F32))
+    return pl.pallas_call(
+        functools.partial(product_kernel, part * depth, depth, main, role),
+        in_specs=whole(len(pieces) + 2 + len(extra)),
+        out_specs=whole(len(out_shape)),
+        out_shape=out_shape,
         compiler_params=params(),
         cost_estimate=cost(weight * total * depth * width, 2 * depth * (width + total)),
         name="product",
-    )(matrix, *pieces, after)
-
-
-def finish_kernel(span, piece_rows, gate_a, gate_b, up_a, up_b, rank_ref, expand_ref, out_ref, hidden_ref):
+    )(matrix, *extra, *pieces, after)
+
+
+def finish_kernel(span, piece_rows, *refs):
+    *products, rank_ref, expand_ref, out_ref, hidden_ref = refs
+    gate_a, gate_b, up_a, up_b, *tails = products
     ranks = rank_ref.shape[0]
     chip = lax.axis_index("tp") // 2
     shape = (ranks, ranks)
@@ -216,14 +235,24 @@
     half = ranks // 2
     blocks = expand_ref.shape[0]
     rows = hidden_ref.shape[0] // blocks
+    main = gate_a.shape[1]
+    tail = hidden_ref.shape[1] - main
     for b in range(blocks):
         part = slice(b * rows, (b + 1) * rows)
         expand = expand_ref[b]
         gate = jnp.dot(rank[part, :half], expand[:half], preferred_element_type=F32)
         up = jnp.dot(rank[part, half:], expand[half:], preferred_element_type=F32)
-        gate += gate_a[part] + gate_b[part]
-        up += up_a[part] + up_b[part]
-        hidden_ref[part] = (gate / (1.0 + jnp.exp(-gate)) * up).astype(BF16)
+        gates = [gate[:, :main] + gate_a[part] + gate_b[part]]
+        ups = [up[:, :main] + up_a[part] + up_b[part]]
+        if tail:
+            both = tails[0][part] + tails[1][part]
+            gates.append(gate[:, main:] + both[:, tail:])
+            ups.append(up[:, main:] + both[:, :tail])
+        column = 0
+        for gate, up in zip(gates, ups, strict=True):
+            hidden = (gate / (1.0 + jnp.exp(-gate)) * up).astype(BF16)
+            hidden_ref[part, column : column + gate.shape[1]] = hidden
+            column += gate.shape[1]
     members = hidden_ref.shape[0] // piece_rows
     for index, place in enumerate(departures(lax.axis_index("tp"), members, piece_rows)):
         out_ref[index * piece_rows : (index + 1) * piece_rows, :] = hidden_ref[
@@ -232,10 +261,10 @@
 
 
 def finish(products, rank, expand, span, piece_rows):
-    total, width = products[0].shape
+    total, width = products[0].shape[0], expand.shape[2]
     return pl.pallas_call(
         functools.partial(finish_kernel, span, piece_rows),
-        in_specs=whole(6),
+        in_specs=whole(len(products) + 2),
         out_specs=whole(1)[0],
         out_shape=jax.ShapeDtypeStruct((total, width), BF16),
         scratch_shapes=[pltpu.VMEM((total, width), BF16)],
@@ -376,15 +405,20 @@
         theirs[:-1],
     )
     work = [(gate_matrix, 0), (gate_matrix, 1), (up_matrix, 0), (up_matrix, 1)]
-    products, after, bit = [], rank, 1
+    products, aside, after, bit = [], [0, 0], rank, 1
     while bit < members or work:
         if work:
             matrix, part = work.pop(0)
-            products.append(product(pieces, matrix, part, 2, after, WEIGHTS[len(products)]))
+            result, *left = product(
+                pieces, matrix, part, 2, after, WEIGHTS[len(products)], aside[part]
+            )
+            aside[part] = left[0] if left else None
+            products.append(result)
         if bit < members:
             after = cross(rank, bit)
             rank = rank + after if bit == 1 else jnp.concatenate([rank, after], axis=0)
             bit *= 2
+    products += [x for x in aside if x is not None]
     hidden = finish(products, rank, expand, 2 * span, rows)
 
     slots = 2 * reach

time: 79.8 us -> 78.8 us (0.987)
    pallas_call x4, Pallas kernels: 9.55 us -> 8.55 us  [product(): pl.pallas_call(functools.partial(product_kernel, part * depth, depth, mai...]
  transfers between devices with their start and end apart: 33 -> 33, of which waited for: 15 -> 15; matrix products, arithmetic and copies ran while one was open for 0% -> 0% of each run, Pallas kernels for 16% -> 15%
where the time goes in v12:
time: 78.8 us; the launch traced here: 78.6 us
  starting transfers between devices  32.7 us (41%)
  waiting for transfers between devices  27.2 us (35%)
  Pallas kernels  18.4 us (23%)
    ppermute x14, waiting for transfers between devices, step(): return lax.ppermute(x, 'tp', ring)  25.4 us
    ppermute x14, starting transfers between devices, step(): return lax.ppermute(x, 'tp', ring)  23.5 us
    ppermute x19, starting transfers between devices, cross(): return lax.ppermute(x, 'tp', crossing(members, bit))  9.17 us
    pallas_call x4, Pallas kernels, product(): pl.pallas_call(functools.partial(product_kernel, part * depth, depth, mai...  8.55 us
    pallas_call x1, Pallas kernels, down(): pl.pallas_call(functools.partial(down_kernel, groups, rows, size), in_spe...  4.5 us
    ppermute x19, waiting for transfers between devices, cross(): return lax.ppermute(x, 'tp', crossing(members, bit))  1.74 us
    pallas_call x1, Pallas kernels, anchor(): pl.pallas_call(anchor_kernel, in_specs=[FAR, FAR], out_specs=whole(1) + [...  1.71 us
  transfers between devices with their start and end apart: 33, of which 15 were waited for; matrix products, arithmetic and copies ran while one was open for 0% of the time, Pallas kernels for 15%

profile of v12, /device:TPU:0, one launch (start us, length us, event | category | flops | bytes accessed | tf_op | source)
XLA Modules:
  0.0 78.6 jit_solution(13314367502785061375)
XLA Ops:
  0.0 0.5 collective-permute-start
  0.5 2.6 %collective-permute-start.1 = (bf16[16,8192]{1,0:T(8,128)(2,1)}, bf16[16,8192]{1,0:T(8,128)(2,1)S(1)}, u32[]{:S(2)}, u32[]{:S(2)}) collective-permute-start(bf16[16,8192]{1,0:T(8,128)(2,1)} %tokens_ref.1), channel_id=1, source_target_pairs={{0,4},{1,3},{4,8},{5,1},{8,12},{9,5},{12,14},{13,9},{14,10},{15,13... | collective-permute-start | bytes 786440 | tf_op jit(solution)/shard_map/ppermute | solution.py:375
  3.2 0.0 collective-permute-done.passed_in
  3.2 1.7 %anchor.1 = (bf16[16,8192]{1,0:T(8,128)(2,1)S(1)}, bf16[16,8192]{1,0:T(8,128)(2,1)S(1)}) custom-call(bf16[16,8192]{1,0:T(8,128)(2,1)} %tokens_ref.1, bf16[16,8192]{1,0:T(8,128)(2,1)S(1)} %collective-permute-done.passed_in), custom_call_target="tpu_custom_call", output_to_operand_aliasing={{1}: (1, {})} | custom-call | flops 30000001024 | tf_op jit(solution)/shard_map/anchor/pallas_call | solution.py:104
  4.9 1.7 %collective-permute-start.2 = (bf16[16,8192]{1,0:T(8,128)(2,1)S(1)}, bf16[16,8192]{1,0:T(8,128)(2,1)S(1)}, u32[]{:S(2)}, u32[]{:S(2)}) collective-permute-start(bf16[16,8192]{1,0:T(8,128)(2,1)S(1)} %get-tuple-element.31.refs_1_.refs_2_), channel_id=1, source_target_pairs={{0,4},{1,3},{4,8},{5,1},{8,12},{9,5},{12,14},{13,9},{14,10},{15,13... | collective-permute-start | bytes 786440 | tf_op jit(solution)/shard_map/ppermute | solution.py:375
  6.6 0.0 collective-permute-start.15
  6.6 1.1 %collective-permute-done.1.refs_1_.refs_2_.refs_3_ = bf16[16,8192]{1,0:T(8,128)(2,1)S(1)} collective-permute-done((bf16[16,8192]{1,0:T(8,128)(2,1)}, bf16[16,8192]{1,0:T(8,128)(2,1)S(1)}, u32[]{:S(2)}, u32[]{:S(2)}) %collective-permute-start.1) | collective-permute-done | bytes 262176 | tf_op jit(solution)/shard_map/ppermute | solution.py:375
  7.7 2.1 %collective-permute-start.3 = (bf16[16,8192]{1,0:T(8,128)(2,1)S(1)}, bf16[16,8192]{1,0:T(8,128)(2,1)S(1)}, u32[]{:S(2)}, u32[]{:S(2)}) collective-permute-start(bf16[16,8192]{1,0:T(8,128)(2,1)S(1)} %collective-permute-done.1.refs_1_.refs_2_.refs_3_), channel_id=1, source_target_pairs={{0,4},{1,3},{4,8},{5,1},{8,12},{9,5},{12,14},{13,9},{14,10},{15,13... | collective-permute-start | bytes 786440 | tf_op jit(solution)/shard_map/ppermute | solution.py:375
  9.7 0.0 collective-permute-start.8
  9.8 1.6 %collective-permute-done.2.refs_2_.refs_3_.refs_4_ = bf16[16,8192]{1,0:T(8,128)(2,1)S(1)} collective-permute-done((bf16[16,8192]{1,0:T(8,128)(2,1)S(1)}, bf16[16,8192]{1,0:T(8,128)(2,1)S(1)}, u32[]{:S(2)}, u32[]{:S(2)}) %collective-permute-start.2) | collective-permute-done | bytes 262176 | tf_op jit(solution)/shard_map/ppermute | solution.py:375
  11.3 1.7 %collective-permute-start.4 = (bf16[16,8192]{1,0:T(8,128)(2,1)S(1)}, bf16[16,8192]{1,0:T(8,128)(2,1)S(1)}, u32[]{:S(2)}, u32[]{:S(2)}) collective-permute-start(bf16[16,8192]{1,0:T(8,128)(2,1)S(1)} %collective-permute-done.2.refs_2_.refs_3_.refs_4_), channel_id=1, source_target_pairs={{0,4},{1,3},{4,8},{5,1},{8,12},{9,5},{12,14},{13,9},{14,10},{15,13... | collective-permute-start | bytes 786440 | tf_op jit(solution)/shard_map/ppermute | solution.py:375
  13.0 1.1 %collective-permute-done.3.refs_3_.refs_4_.refs_5_ = bf16[16,8192]{1,0:T(8,128)(2,1)S(1)} collective-permute-done((bf16[16,8192]{1,0:T(8,128)(2,1)S(1)}, bf16[16,8192]{1,0:T(8,128)(2,1)S(1)}, u32[]{:S(2)}, u32[]{:S(2)}) %collective-permute-start.3) | collective-permute-done | bytes 262176 | tf_op jit(solution)/shard_map/ppermute | solution.py:375
  14.1 2.0 %collective-permute-start.5 = (bf16[16,8192]{1,0:T(8,128)(2,1)S(1)}, bf16[16,8192]{1,0:T(8,128)(2,1)S(1)}, u32[]{:S(2)}, u32[]{:S(2)}) collective-permute-start(bf16[16,8192]{1,0:T(8,128)(2,1)S(1)} %collective-permute-done.3.refs_3_.refs_4_.refs_5_), channel_id=1, source_target_pairs={{0,4},{1,3},{4,8},{5,1},{8,12},{9,5},{12,14},{13,9},{14,10},{15,13... | collective-permute-start | bytes 786440 | tf_op jit(solution)/shard_map/ppermute | solution.py:375
  16.1 0.5 collective-permute-start.10
  16.6 1.1 %collective-permute-done.4.refs_4_.refs_5_.refs_6_ = bf16[16,8192]{1,0:T(8,128)(2,1)S(1)} collective-permute-done((bf16[16,8192]{1,0:T(8,128)(2,1)S(1)}, bf16[16,8192]{1,0:T(8,128)(2,1)S(1)}, u32[]{:S(2)}, u32[]{:S(2)}) %collective-permute-start.4) | collective-permute-done | bytes 262176 | tf_op jit(solution)/shard_map/ppermute | solution.py:375
  17.7 1.7 %collective-permute-start.6 = (bf16[16,8192]{1,0:T(8,128)(2,1)S(1)}, bf16[16,8192]{1,0:T(8,128)(2,1)S(1)}, u32[]{:S(2)}, u32[]{:S(2)}) collective-permute-start(bf16[16,8192]{1,0:T(8,128)(2,1)S(1)} %collective-permute-done.4.refs_4_.refs_5_.refs_6_), channel_id=1, source_target_pairs={{0,4},{1,3},{4,8},{5,1},{8,12},{9,5},{12,14},{13,9},{14,10},{15,13... | collective-permute-start | bytes 786440 | tf_op jit(solution)/shard_map/ppermute | solution.py:375
  19.4 1.1 %collective-permute-done.5.refs_5_.refs_6_.refs_7_ = bf16[16,8192]{1,0:T(8,128)(2,1)S(1)} collective-permute-done((bf16[16,8192]{1,0:T(8,128)(2,1)S(1)}, bf16[16,8192]{1,0:T(8,128)(2,1)S(1)}, u32[]{:S(2)}, u32[]{:S(2)}) %collective-permute-start.5) | collective-permute-done | bytes 262176 | tf_op jit(solution)/shard_map/ppermute | solution.py:375
  20.5 2.0 %collective-permute-start.7 = (bf16[16,8192]{1,0:T(8,128)(2,1)S(1)}, bf16[16,8192]{1,0:T(8,128)(2,1)S(1)}, u32[]{:S(2)}, u32[]{:S(2)}) collective-permute-start(bf16[16,8192]{1,0:T(8,128)(2,1)S(1)} %collective-permute-done.5.refs_5_.refs_6_.refs_7_), channel_id=1, source_target_pairs={{0,4},{1,3},{4,8},{5,1},{8,12},{9,5},{12,14},{13,9},{14,10},{15,13... | collective-permute-start | bytes 786440 | tf_op jit(solution)/shard_map/ppermute | solution.py:375
  22.5 0.0 collective-permute-done.9.refs_9_.refs_10_.refs_11_
  22.5 0.0 collective-permute-start.11
  22.5 0.5 collective-permute-start.12
  23.0 1.0 %collective-permute-done.6.refs_6_.refs_7_.refs_8_ = bf16[16,8192]{1,0:T(8,128)(2,1)S(1)} collective-permute-done((bf16[16,8192]{1,0:T(8,128)(2,1)S(1)}, bf16[16,8192]{1,0:T(8,128)(2,1)S(1)}, u32[]{:S(2)}, u32[]{:S(2)}) %collective-permute-start.6) | collective-permute-done | bytes 262176 | tf_op jit(solution)/shard_map/ppermute | solution.py:375
  24.1 2.8 %collective-permute-done.7.refs_7_.refs_8_.refs_9_ = bf16[16,8192]{1,0:T(8,128)(2,1)S(1)} collective-permute-done((bf16[16,8192]{1,0:T(8,128)(2,1)S(1)}, bf16[16,8192]{1,0:T(8,128)(2,1)S(1)}, u32[]{:S(2)}, u32[]{:S(2)}) %collective-permute-start.7) | collective-permute-done | bytes 262176 | tf_op jit(solution)/shard_map/ppermute | solution.py:375
  26.9 1.2 %rank.1 = (bf16[16,256]{1,0:T(8,128)(2,1)S(1)}, bf16[2,128,896]{2,1,0:T(8,128)(2,1)S(1)}) custom-call(s32[1,2]{1,0:T(1,128)S(1)} %bitcast.7, bf16[8,128,896]{2,1,0:T(8,128)(2,1)} %expand_ref.1, bf16[8,8,8192]{2,1,0:T(8,128)(2,1)S(1)} %bitcast.6, bf16[8,8,8192]{2,1,0:T(8,128)(2,1)S(1)} %collective-permute-done.15.other_ref, ...), custom_call_target="tpu_custom_call" | custom-call | flops 67108864 | bytes 4194304 | tf_op jit(solution)/shard_map/rank/pallas_call | solution.py:159
  28.1 0.6 collective-permute-start.16
  28.7 2.0 %product.4 = (f32[256,768]{1,0:T(8,128)S(1)}, bf16[4096,128]{1,0:T(8,128)(2,1)S(1)}) custom-call(bf16[8192,896]{1,0:T(8,128)(2,1)S(1)} %copy-done.3, bf16[16,8192]{1,0:T(8,128)(2,1)S(1)} %get-tuple-element.30.refs_0_.refs_1_, bf16[16,8192]{1,0:T(8,128)(2,1)S(1)} %get-tuple-element.31.refs_1_.refs_2_, ...), custom_call_target="tpu_custom_call" | custom-call | flops 5637144576 | bytes 9437184 | tf_op jit(solution)/shard_map/product/pallas_call | solution.py:213
  30.7 0.0 slice-start.6
  30.7 2.0 %collective-permute-start.17 = (bf16[16,256]{1,0:T(8,128)(2,1)S(1)}, bf16[16,256]{1,0:T(8,128)(2,1)S(1)}, u32[]{:S(2)}, u32[]{:S(2)}) collective-permute-start(bf16[16,256]{1,0:T(8,128)(2,1)S(1)} %add.3), channel_id=1, source_target_pairs={{0,2},{1,3},{2,0},{3,1},{4,6},{5,7},{6,4},{7,5},{8,10},{9,11},{10,... | collective-permute-start | bytes 24584 | tf_op jit(solution)/shard_map/ppermute | solution.py:378
  32.7 1.9 %product.5 = (f32[256,768]{1,0:T(8,128)S(1)}, bf16[4096,128]{1,0:T(8,128)(2,1)S(1)}) custom-call(bf16[8192,896]{1,0:T(8,128)(2,1)S(1)} %copy-done.3, bf16[16,8192]{1,0:T(8,128)(2,1)S(1)} %get-tuple-element.30.refs_0_.refs_1_, bf16[16,8192]{1,0:T(8,128)(2,1)S(1)} %get-tuple-element.31.refs_1_.refs_2_, ...), custom_call_target="tpu_custom_call" | custom-call | flops 5637144576 | bytes 9437184 | tf_op jit(solution)/shard_map/product/pallas_call | solution.py:213
  34.7 1.7 %collective-permute-start.18 = (bf16[32,256]{1,0:T(8,128)(2,1)S(1)}, bf16[32,256]{1,0:T(8,128)(2,1)S(1)}, u32[]{:S(2)}, u32[]{:S(2)}) collective-permute-start(bf16[32,256]{1,0:T(8,128)(2,1)S(1)} %pad_maximum_fusion.2), channel_id=1, source_target_pairs={{0,4},{1,5},{2,6},{3,7},{4,0},{5,1},{6,2},{7,3},{8,12},{9,13},{10,... | collective-permute-start | bytes 49160 | tf_op jit(solution)/shard_map/ppermute | solution.py:378
  36.4 0.0 slice-start
  36.5 0.0 slice-start.1
  36.5 2.3 %product.6 = (f32[256,768]{1,0:T(8,128)S(1)}, f32[256,256]{1,0:T(8,128)S(1)}) custom-call(bf16[8192,896]{1,0:T(8,128)(2,1)S(1)} %bitcast.10, bf16[4096,128]{1,0:T(8,128)(2,1)S(1)} %get-tuple-element.35.refs_0_, bf16[16,8192]{1,0:T(8,128)(2,1)S(1)} %get-tuple-element.30.refs_0_.refs_1_, bf16[16,8192]{1,0:T(8,128)(2,1)S(1)} %get-tuple-element.31.refs_1_.refs_2_, ...), custom_call_target="tpu_custom_call" | custom-call | flops 5637144576 | bytes 9437184 | tf_op jit(solution)/shard_map/product/pallas_call | solution.py:213
  38.8 2.7 %collective-permute-start.19 = (bf16[64,256]{1,0:T(8,128)(2,1)S(1)}, bf16[64,256]{1,0:T(8,128)(2,1)S(1)}, u32[]{:S(2)}, u32[]{:S(2)}) collective-permute-start(bf16[64,256]{1,0:T(8,128)(2,1)S(1)} %pad_maximum_fusion.1), channel_id=1, source_target_pairs={{0,8},{1,9},{2,10},{3,11},{4,12},{5,13},{6,14},{7,15},{8,0},{9,1},... | collective-permute-start | bytes 98312 | tf_op jit(solution)/shard_map/ppermute | solution.py:378
  41.5 2.3 %product.7 = (f32[256,768]{1,0:T(8,128)S(1)}, f32[256,256]{1,0:T(8,128)S(1)}) custom-call(bf16[8192,896]{1,0:T(8,128)(2,1)S(1)} %bitcast.10, bf16[4096,128]{1,0:T(8,128)(2,1)S(1)} %get-tuple-element.37.refs_0_, bf16[16,8192]{1,0:T(8,128)(2,1)S(1)} %get-tuple-element.30.refs_0_.refs_1_, bf16[16,8192]{1,0:T(8,128)(2,1)S(1)} %get-tuple-element.31.refs_1_.refs_2_, ...), custom_call_target="tpu_custom_call" | custom-call | flops 5637144576 | bytes 9437184 | tf_op jit(solution)/shard_map/product/pallas_call | solution.py:213
  43.8 0.0 copy-start.2
  43.9 0.8 %finish.1.hidden_ref = bf16[256,896]{1,0:T(8,128)(2,1)S(1)} custom-call(f32[256,768]{1,0:T(8,128)S(1)} %get-tuple-element.33.refs_0_, f32[256,768]{1,0:T(8,128)S(1)} %get-tuple-element.34.refs_1_, f32[256,768]{1,0:T(8,128)S(1)} %get-tuple-element.36.refs_2_, f32[256,768]{1,0:T(8,128)S(1)} %get-tuple-element.38.refs_3_, ...), custom_call_target="tpu_custom_call" | custom-call | tf_op jit(solution)/shard_map/finish/pallas_call | solution.py:265
  44.7 4.5 %down.1 = (bf16[16,8192]{1,0:T(8,128)(2,1)S(1)}, bf16[16,8192]{1,0:T(8,128)(2,1)S(1)}, bf16[16,8192]{1,0:T(8,128)(2,1)S(1)}, bf16[16,8192]{1,0:T(8,128)(2,1)S(1)...) custom-call(bf16[896,8192]{1,0:T(8,128)(2,1)S(1)} %bitcast.4, ...), custom_call_target="tpu_custom_call" | custom-call | flops 3758096384 | bytes 18874368 | tf_op jit(solution)/shard_map/down/pallas_call | solution.py:291
  49.2 0.1 collective-permute-start.23
  49.3 0.5 collective-permute-start.24
  49.8 0.1 collective-permute-start.22
  49.9 1.7 %collective-permute-done.24.refs_1_ = bf16[16,8192]{1,0:T(8,128)(2,1)S(1)} collective-permute-done((bf16[16,8192]{1,0:T(8,128)(2,1)S(1)}, bf16[16,8192]{1,0:T(8,128)(2,1)S(1)}, u32[]{:S(2)}, u32[]{:S(2)}) %collective-permute-start.24) | collective-permute-done | bytes 262176 | tf_op jit(solution)/shard_map/ppermute | solution.py:378
  51.6 0.1 added.7
  51.6 1.3 %collective-permute-start.25 = (bf16[16,8192]{1,0:T(8,128)(2,1)S(1)}, bf16[16,8192]{1,0:T(8,128)(2,1)S(1)}, u32[]{:S(2)}, u32[]{:S(2)}) collective-permute-start(bf16[16,8192]{1,0:T(8,128)(2,1)S(1)} %added.7), channel_id=1, source_target_pairs={{0,4},{1,3},{4,8},{5,1},{8,12},{9,5},{12,14},{13,9},{14,10},{15,13... | collective-permute-start | bytes 786440 | tf_op jit(solution)/shard_map/ppermute | solution.py:375
  52.9 0.1 added.11
  53.0 1.9 %collective-permute-start.29 = (bf16[16,8192]{1,0:T(8,128)(2,1)S(1)}, bf16[16,8192]{1,0:T(8,128)(2,1)S(1)}, u32[]{:S(2)}, u32[]{:S(2)}) collective-permute-start(bf16[16,8192]{1,0:T(8,128)(2,1)S(1)} %added.11), channel_id=1, source_target_pairs={{0,4},{1,3},{4,8},{5,1},{8,12},{9,5},{12,14},{13,9},{14,10},{15,13... | collective-permute-start | bytes 786440 | tf_op jit(solution)/shard_map/ppermute | solution.py:375
  54.9 3.1 %collective-permute-done.25.refs_2_ = bf16[16,8192]{1,0:T(8,128)(2,1)S(1)} collective-permute-done((bf16[16,8192]{1,0:T(8,128)(2,1)S(1)}, bf16[16,8192]{1,0:T(8,128)(2,1)S(1)}, u32[]{:S(2)}, u32[]{:S(2)}) %collective-permute-start.25) | collective-permute-done | bytes 262176 | tf_op jit(solution)/shard_map/ppermute | solution.py:375
  58.1 0.1 added.8
  58.2 1.3 %collective-permute-start.26 = (bf16[16,8192]{1,0:T(8,128)(2,1)S(1)}, bf16[16,8192]{1,0:T(8,128)(2,1)S(1)}, u32[]{:S(2)}, u32[]{:S(2)}) collective-permute-start(bf16[16,8192]{1,0:T(8,128)(2,1)S(1)} %added.8), channel_id=1, source_target_pairs={{0,4},{1,3},{4,8},{5,1},{8,12},{9,5},{12,14},{13,9},{14,10},{15,13... | collective-permute-start | bytes 786440 | tf_op jit(solution)/shard_map/ppermute | solution.py:375
  59.5 1.4 %collective-permute-done.29.refs_2_ = bf16[16,8192]{1,0:T(8,128)(2,1)S(1)} collective-permute-done((bf16[16,8192]{1,0:T(8,128)(2,1)S(1)}, bf16[16,8192]{1,0:T(8,128)(2,1)S(1)}, u32[]{:S(2)}, u32[]{:S(2)}) %collective-permute-start.29) | collective-permute-done | bytes 262176 | tf_op jit(solution)/shard_map/ppermute | solution.py:375
  60.9 0.1 added.12
  61.0 1.3 %collective-permute-start.30 = (bf16[16,8192]{1,0:T(8,128)(2,1)S(1)}, bf16[16,8192]{1,0:T(8,128)(2,1)S(1)}, u32[]{:S(2)}, u32[]{:S(2)}) collective-permute-start(bf16[16,8192]{1,0:T(8,128)(2,1)S(1)} %added.12), channel_id=1, source_target_pairs={{0,4},{1,3},{4,8},{5,1},{8,12},{9,5},{12,14},{13,9},{14,10},{15,13... | collective-permute-start | bytes 786440 | tf_op jit(solution)/shard_map/ppermute | solution.py:375
  62.3 2.3 %collective-permute-done.26.refs_2_ = bf16[16,8192]{1,0:T(8,128)(2,1)S(1)} collective-permute-done((bf16[16,8192]{1,0:T(8,128)(2,1)S(1)}, bf16[16,8192]{1,0:T(8,128)(2,1)S(1)}, u32[]{:S(2)}, u32[]{:S(2)}) %collective-permute-start.26) | collective-permute-done | bytes 262176 | tf_op jit(solution)/shard_map/ppermute | solution.py:375
  64.6 0.1 added.9
  64.7 1.3 %collective-permute-start.27 = (bf16[16,8192]{1,0:T(8,128)(2,1)S(1)}, bf16[16,8192]{1,0:T(8,128)(2,1)S(1)}, u32[]{:S(2)}, u32[]{:S(2)}) collective-permute-start(bf16[16,8192]{1,0:T(8,128)(2,1)S(1)} %added.9), channel_id=1, source_target_pairs={{0,4},{1,3},{4,8},{5,1},{8,12},{9,5},{12,14},{13,9},{14,10},{15,13... | collective-permute-start | bytes 786440 | tf_op jit(solution)/shard_map/ppermute | solution.py:375
  66.0 1.4 %collective-permute-done.30.refs_2_ = bf16[16,8192]{1,0:T(8,128)(2,1)S(1)} collective-permute-done((bf16[16,8192]{1,0:T(8,128)(2,1)S(1)}, bf16[16,8192]{1,0:T(8,128)(2,1)S(1)}, u32[]{:S(2)}, u32[]{:S(2)}) %collective-permute-start.30) | collective-permute-done | bytes 262176 | tf_op jit(solution)/shard_map/ppermute | solution.py:375
  67.4 0.1 added.13
  67.5 1.3 %collective-permute-start.31 = (bf16[16,8192]{1,0:T(8,128)(2,1)S(1)}, bf16[16,8192]{1,0:T(8,128)(2,1)S(1)}, u32[]{:S(2)}, u32[]{:S(2)}) collective-permute-start(bf16[16,8192]{1,0:T(8,128)(2,1)S(1)} %added.13), channel_id=1, source_target_pairs={{0,4},{1,3},{4,8},{5,1},{8,12},{9,5},{12,14},{13,9},{14,10},{15,13... | collective-permute-start | bytes 786440 | tf_op jit(solution)/shard_map/ppermute | solution.py:375
  68.8 2.3 %collective-permute-done.27.refs_2_ = bf16[16,8192]{1,0:T(8,128)(2,1)S(1)} collective-permute-done((bf16[16,8192]{1,0:T(8,128)(2,1)S(1)}, bf16[16,8192]{1,0:T(8,128)(2,1)S(1)}, u32[]{:S(2)}, u32[]{:S(2)}) %collective-permute-start.27) | collective-permute-done | bytes 262176 | tf_op jit(solution)/shard_map/ppermute | solution.py:375
  71.1 0.1 added.10
  71.2 1.3 %collective-permute-start.28 = (bf16[16,8192]{1,0:T(8,128)(2,1)S(1)}, bf16[16,8192]{1,0:T(8,128)(2,1)S(1)}, u32[]{:S(2)}, u32[]{:S(2)}) collective-permute-start(bf16[16,8192]{1,0:T(8,128)(2,1)S(1)} %added.10), channel_id=1, source_target_pairs={{0,4},{1,3},{4,8},{5,1},{8,12},{9,5},{12,14},{13,9},{14,10},{15,13... | collective-permute-start | bytes 786440 | tf_op jit(solution)/shard_map/ppermute | solution.py:375
  72.5 1.4 %collective-permute-done.31 = bf16[16,8192]{1,0:T(8,128)(2,1)S(1)} collective-permute-done((bf16[16,8192]{1,0:T(8,128)(2,1)S(1)}, bf16[16,8192]{1,0:T(8,128)(2,1)S(1)}, u32[]{:S(2)}, u32[]{:S(2)}) %collective-permute-start.31) | collective-permute-done | bytes 262176 | tf_op jit(solution)/shard_map/ppermute | solution.py:375
  73.9 3.7 %collective-permute-done.28.refs_2_ = bf16[16,8192]{1,0:T(8,128)(2,1)S(1)} collective-permute-done((bf16[16,8192]{1,0:T(8,128)(2,1)S(1)}, bf16[16,8192]{1,0:T(8,128)(2,1)S(1)}, u32[]{:S(2)}, u32[]{:S(2)}) %collective-permute-start.28) | collective-permute-done | bytes 262176 | tf_op jit(solution)/shard_map/ppermute | solution.py:375
  77.6 1.0 %last.1 = bf16[16,8192]{1,0:T(8,128)(2,1)} custom-call(s32[1,2]{1,0:T(1,128)S(1)} %bitcast.8, bf16[16,8192]{1,0:T(8,128)(2,1)S(1)} %get-tuple-element.42.refs_0_, bf16[16,8192]{1,0:T(8,128)(2,1)S(1)} %collective-permute-done.20.refs_1_, bf16[16,8192]{1,0:T(8,128)(2,1)S(1)} %collective-permute-done.28.refs_2_, ...), custom_call_target="tpu_custom_call" | custom-call | tf_op jit(solution)/shard_map/last/pallas_call | solution.py:325
  (48 shorter events, 0.1 us)
Async XLA Ops:
  0.0 6.6 %copy-start = (bf16[8,8192,8]{1,2,0:T(8,128)(2,1)S(1)}, bf16[8,8192,8]{1,2,0:T(8,128)(2,1)}, u32[]{:S(2)}) copy-start(bf16[8,8192,8]{1,2,0:T(8,128)(2,1)} %param.12) | copy-start | bytes 3145732
  0.0 26.9 %copy-start.1 = (s32[2]{0:T(128)S(1)}, s32[2]{0:T(128)}, u32[]{:S(2)}) copy-start(s32[2]{0:T(128)} %param.14) | copy-start | bytes 28
  0.0 28.7 %copy-start.3 = (bf16[8192,896]{1,0:T(8,128)(2,1)S(1)}, bf16[8192,896]{1,0:T(8,128)(2,1)}, u32[]{:S(2)}) copy-start(bf16[8192,896]{1,0:T(8,128)(2,1)} %w_ref.6) | copy-start | bytes 44040196
  0.0 3.2 %collective-permute-start = (bf16[16,8192]{1,0:T(8,128)(2,1)}, bf16[16,8192]{1,0:T(8,128)(2,1)S(1)}, u32[]{:S(2)}, u32[]{:S(2)}) collective-permute-start(bf16[16,8192]{1,0:T(8,128)(2,1)} %tokens_ref.1), channel_id=1, source_target_pairs={{0,1},{1,0},{2,3},{3,2},{4,5},{5,4},{6,7},{7,6},{8,9},{9,8},{10,11... | collective-permute-start | bytes 786440 | tf_op jit(solution)/shard_map/ppermute | solution.py:378
  0.5 7.1 %collective-permute-start.1 = (bf16[16,8192]{1,0:T(8,128)(2,1)}, bf16[16,8192]{1,0:T(8,128)(2,1)S(1)}, u32[]{:S(2)}, u32[]{:S(2)}) collective-permute-start(bf16[16,8192]{1,0:T(8,128)(2,1)} %tokens_ref.1), channel_id=1, source_target_pairs={{0,4},{1,3},{4,8},{5,1},{8,12},{9,5},{12,14},{13,9},{14,10},{15,13... | collective-permute-start | bytes 786440 | tf_op jit(solution)/shard_map/ppermute | solution.py:375
  4.9 6.4 %collective-permute-start.2 = (bf16[16,8192]{1,0:T(8,128)(2,1)S(1)}, bf16[16,8192]{1,0:T(8,128)(2,1)S(1)}, u32[]{:S(2)}, u32[]{:S(2)}) collective-permute-start(bf16[16,8192]{1,0:T(8,128)(2,1)S(1)} %get-tuple-element.31.refs_1_.refs_2_), channel_id=1, source_target_pairs={{0,4},{1,3},{4,8},{5,1},{8,12},{9,5},{12,14},{13,9},{14,10},{15,13... | collective-permute-start | bytes 786440 | tf_op jit(solution)/shard_map/ppermute | solution.py:375
  6.6 20.3 %collective-permute-start.15 = (bf16[8,8,8192]{2,1,0:T(8,128)(2,1)S(1)}, bf16[8,8,8192]{2,1,0:T(8,128)(2,1)S(1)}, u32[]{:S(2)}, u32[]{:S(2)}) collective-permute-start(bf16[8,8,8192]{2,1,0:T(8,128)(2,1)S(1)} %bitcast.5), channel_id=1, source_target_pairs={{0,1},{1,0},{2,3},{3,2},{4,5},{5,4},{6,7},{7,6},{8,9},{9,8},{10,11... | collective-permute-start | bytes 3145736 | tf_op jit(solution)/shard_map/ppermute | solution.py:378
  7.7 6.5 %collective-permute-start.3 = (bf16[16,8192]{1,0:T(8,128)(2,1)S(1)}, bf16[16,8192]{1,0:T(8,128)(2,1)S(1)}, u32[]{:S(2)}, u32[]{:S(2)}) collective-permute-start(bf16[16,8192]{1,0:T(8,128)(2,1)S(1)} %collective-permute-done.1.refs_1_.refs_2_.refs_3_), channel_id=1, source_target_pairs={{0,4},{1,3},{4,8},{5,1},{8,12},{9,5},{12,14},{13,9},{14,10},{15,13... | collective-permute-start | bytes 786440 | tf_op jit(solution)/shard_map/ppermute | solution.py:375
  9.7 6.4 %collective-permute-start.8 = (bf16[16,8192]{1,0:T(8,128)(2,1)S(1)}, bf16[16,8192]{1,0:T(8,128)(2,1)S(1)}, u32[]{:S(2)}, u32[]{:S(2)}) collective-permute-start(bf16[16,8192]{1,0:T(8,128)(2,1)S(1)} %collective-permute-done.1.refs_1_.refs_2_.refs_3_), channel_id=1, source_target_pairs={{0,1},{1,0},{2,3},{3,2},{4,5},{5,4},{6,7},{7,6},{8,9},{9,8},{10,11... | collective-permute-start | bytes 786440 | tf_op jit(solution)/shard_map/ppermute | solution.py:378
  11.3 6.4 %collective-permute-start.4 = (bf16[16,8192]{1,0:T(8,128)(2,1)S(1)}, bf16[16,8192]{1,0:T(8,128)(2,1)S(1)}, u32[]{:S(2)}, u32[]{:S(2)}) collective-permute-start(bf16[16,8192]{1,0:T(8,128)(2,1)S(1)} %collective-permute-done.2.refs_2_.refs_3_.refs_4_), channel_id=1, source_target_pairs={{0,4},{1,3},{4,8},{5,1},{8,12},{9,5},{12,14},{13,9},{14,10},{15,13... | collective-permute-start | bytes 786440 | tf_op jit(solution)/shard_map/ppermute | solution.py:375
  14.1 6.4 %collective-permute-start.5 = (bf16[16,8192]{1,0:T(8,128)(2,1)S(1)}, bf16[16,8192]{1,0:T(8,128)(2,1)S(1)}, u32[]{:S(2)}, u32[]{:S(2)}) collective-permute-start(bf16[16,8192]{1,0:T(8,128)(2,1)S(1)} %collective-permute-done.3.refs_3_.refs_4_.refs_5_), channel_id=1, source_target_pairs={{0,4},{1,3},{4,8},{5,1},{8,12},{9,5},{12,14},{13,9},{14,10},{15,13... | collective-permute-start | bytes 786440 | tf_op jit(solution)/shard_map/ppermute | solution.py:375
  16.1 6.4 %collective-permute-start.9 = (bf16[16,8192]{1,0:T(8,128)(2,1)S(1)}, bf16[16,8192]{1,0:T(8,128)(2,1)S(1)}, u32[]{:S(2)}, u32[]{:S(2)}) collective-permute-start(bf16[16,8192]{1,0:T(8,128)(2,1)S(1)} %collective-permute-done.2.refs_2_.refs_3_.refs_4_), channel_id=1, source_target_pairs={{0,1},{1,0},{2,3},{3,2},{4,5},{5,4},{6,7},{7,6},{8,9},{9,8},{10,11... | collective-permute-start | bytes 786440 | tf_op jit(solution)/shard_map/ppermute | solution.py:378
  16.1 6.4 %collective-permute-start.10 = (bf16[16,8192]{1,0:T(8,128)(2,1)S(1)}, bf16[16,8192]{1,0:T(8,128)(2,1)S(1)}, u32[]{:S(2)}, u32[]{:S(2)}) collective-permute-start(bf16[16,8192]{1,0:T(8,128)(2,1)S(1)} %collective-permute-done.3.refs_3_.refs_4_.refs_5_), channel_id=1, source_target_pairs={{0,1},{1,0},{2,3},{3,2},{4,5},{5,4},{6,7},{7,6},{8,9},{9,8},{10,11... | collective-permute-start | bytes 786440 | tf_op jit(solution)/shard_map/ppermute | solution.py:378
  17.7 6.4 %collective-permute-start.6 = (bf16[16,8192]{1,0:T(8,128)(2,1)S(1)}, bf16[16,8192]{1,0:T(8,128)(2,1)S(1)}, u32[]{:S(2)}, u32[]{:S(2)}) collective-permute-start(bf16[16,8192]{1,0:T(8,128)(2,1)S(1)} %collective-permute-done.4.refs_4_.refs_5_.refs_6_), channel_id=1, source_target_pairs={{0,4},{1,3},{4,8},{5,1},{8,12},{9,5},{12,14},{13,9},{14,10},{15,13... | collective-permute-start | bytes 786440 | tf_op jit(solution)/shard_map/ppermute | solution.py:375
  20.5 6.4 %collective-permute-start.7 = (bf16[16,8192]{1,0:T(8,128)(2,1)S(1)}, bf16[16,8192]{1,0:T(8,128)(2,1)S(1)}, u32[]{:S(2)}, u32[]{:S(2)}) collective-permute-start(bf16[16,8192]{1,0:T(8,128)(2,1)S(1)} %collective-permute-done.5.refs_5_.refs_6_.refs_7_), channel_id=1, source_target_pairs={{0,4},{1,3},{4,8},{5,1},{8,12},{9,5},{12,14},{13,9},{14,10},{15,13... | collective-permute-start | bytes 786440 | tf_op jit(solution)/shard_map/ppermute | solution.py:375
  22.5 4.4 %collective-permute-start.11 = (bf16[16,8192]{1,0:T(8,128)(2,1)S(1)}, bf16[16,8192]{1,0:T(8,128)(2,1)S(1)}, u32[]{:S(2)}, u32[]{:S(2)}) collective-permute-start(bf16[16,8192]{1,0:T(8,128)(2,1)S(1)} %collective-permute-done.4.refs_4_.refs_5_.refs_6_), channel_id=1, source_target_pairs={{0,1},{1,0},{2,3},{3,2},{4,5},{5,4},{6,7},{7,6},{8,9},{9,8},{10,11... | collective-permute-start | bytes 786440 | tf_op jit(solution)/shard_map/ppermute | solution.py:378
  22.5 4.4 %collective-permute-start.12 = (bf16[16,8192]{1,0:T(8,128)(2,1)S(1)}, bf16[16,8192]{1,0:T(8,128)(2,1)S(1)}, u32[]{:S(2)}, u32[]{:S(2)}) collective-permute-start(bf16[16,8192]{1,0:T(8,128)(2,1)S(1)} %collective-permute-done.5.refs_5_.refs_6_.refs_7_), channel_id=1, source_target_pairs={{0,1},{1,0},{2,3},{3,2},{4,5},{5,4},{6,7},{7,6},{8,9},{9,8},{10,11... | collective-permute-start | bytes 786440 | tf_op jit(solution)/shard_map/ppermute | solution.py:378
  24.1 2.8 %collective-permute-start.13 = (bf16[16,8192]{1,0:T(8,128)(2,1)S(1)}, bf16[16,8192]{1,0:T(8,128)(2,1)S(1)}, u32[]{:S(2)}, u32[]{:S(2)}) collective-permute-start(bf16[16,8192]{1,0:T(8,128)(2,1)S(1)} %collective-permute-done.6.refs_6_.refs_7_.refs_8_), channel_id=1, source_target_pairs={{0,1},{1,0},{2,3},{3,2},{4,5},{5,4},{6,7},{7,6},{8,9},{9,8},{10,11... | collective-permute-start | bytes 786440 | tf_op jit(solution)/shard_map/ppermute | solution.py:378
  26.9 1.8 %collective-permute-start.14 = (bf16[16,8192]{1,0:T(8,128)(2,1)S(1)}, bf16[16,8192]{1,0:T(8,128)(2,1)S(1)}, u32[]{:S(2)}, u32[]{:S(2)}) collective-permute-start(bf16[16,8192]{1,0:T(8,128)(2,1)S(1)} %collective-permute-done.7.refs_7_.refs_8_.refs_9_), channel_id=1, source_target_pairs={{0,1},{1,0},{2,3},{3,2},{4,5},{5,4},{6,7},{7,6},{8,9},{9,8},{10,11... | collective-permute-start | bytes 786440 | tf_op jit(solution)/shard_map/ppermute | solution.py:378
  28.1 2.5 %collective-permute-start.16 = (bf16[16,256]{1,0:T(8,128)(2,1)S(1)}, bf16[16,256]{1,0:T(8,128)(2,1)S(1)}, u32[]{:S(2)}, u32[]{:S(2)}) collective-permute-start(bf16[16,256]{1,0:T(8,128)(2,1)S(1)} %get-tuple-element.32.refs_16_), channel_id=1, source_target_pairs={{0,1},{1,0},{2,3},{3,2},{4,5},{5,4},{6,7},{7,6},{8,9},{9,8},{10,11... | collective-permute-start | bytes 24584 | tf_op jit(solution)/shard_map/ppermute | solution.py:378
  28.7 7.7 %slice-start.4 = ((s8[14680064]{0:T(1024)(128)(4,1)}), s8[4194304]{0:T(1024)(128)(4,1)S(1)}, s32[]{:S(2)}) async-start(s8[14680064]{0:T(1024)(128)(4,1)} %bitcast.9), calls=%async_computation.4 | async-start | bytes 8388608
  28.7 7.7 %slice-start.5 = ((s8[14680064]{0:T(1024)(128)(4,1)}), s8[4194304]{0:T(1024)(128)(4,1)S(1)}, s32[]{:S(2)}) async-start(s8[14680064]{0:T(1024)(128)(4,1)} %bitcast.9), calls=%async_computation.5 | async-start | bytes 8388608
  30.7 5.7 %slice-start.6 = ((s8[14680064]{0:T(1024)(128)(4,1)}), s8[4194304]{0:T(1024)(128)(4,1)S(1)}, s32[]{:S(2)}) async-start(s8[14680064]{0:T(1024)(128)(4,1)} %bitcast.9), calls=%async_computation.6 | async-start | bytes 8388608
  30.7 5.7 %slice-start.7 = ((s8[14680064]{0:T(1024)(128)(4,1)}), s8[2097152]{0:T(1024)(128)(4,1)S(1)}, s32[]{:S(2)}) async-start(s8[14680064]{0:T(1024)(128)(4,1)} %bitcast.9), calls=%async_computation.7 | async-start | bytes 4194304
  30.7 4.0 %collective-permute-start.17 = (bf16[16,256]{1,0:T(8,128)(2,1)S(1)}, bf16[16,256]{1,0:T(8,128)(2,1)S(1)}, u32[]{:S(2)}, u32[]{:S(2)}) collective-permute-start(bf16[16,256]{1,0:T(8,128)(2,1)S(1)} %add.3), channel_id=1, source_target_pairs={{0,2},{1,3},{2,0},{3,1},{4,6},{5,7},{6,4},{7,5},{8,10},{9,11},{10,... | collective-permute-start | bytes 24584 | tf_op jit(solution)/shard_map/ppermute | solution.py:378
  34.7 4.1 %collective-permute-start.18 = (bf16[32,256]{1,0:T(8,128)(2,1)S(1)}, bf16[32,256]{1,0:T(8,128)(2,1)S(1)}, u32[]{:S(2)}, u32[]{:S(2)}) collective-permute-start(bf16[32,256]{1,0:T(8,128)(2,1)S(1)} %pad_maximum_fusion.2), channel_id=1, source_target_pairs={{0,4},{1,5},{2,6},{3,7},{4,0},{5,1},{6,2},{7,3},{8,12},{9,13},{10,... | collective-permute-start | bytes 49160 | tf_op jit(solution)/shard_map/ppermute | solution.py:378
  36.4 8.2 %slice-start = ((s8[14680064]{0:T(1024)(128)(4,1)}), s8[4194304]{0:T(1024)(128)(4,1)S(1)}, s32[]{:S(2)}) async-start(s8[14680064]{0:T(1024)(128)(4,1)} %bitcast.3), calls=%async_computation | async-start | bytes 8388608
  36.5 8.2 %slice-start.1 = ((s8[14680064]{0:T(1024)(128)(4,1)}), s8[4194304]{0:T(1024)(128)(4,1)S(1)}, s32[]{:S(2)}) async-start(s8[14680064]{0:T(1024)(128)(4,1)} %bitcast.3), calls=%async_computation.1 | async-start | bytes 8388608
  38.8 5.0 %collective-permute-start.19 = (bf16[64,256]{1,0:T(8,128)(2,1)S(1)}, bf16[64,256]{1,0:T(8,128)(2,1)S(1)}, u32[]{:S(2)}, u32[]{:S(2)}) collective-permute-start(bf16[64,256]{1,0:T(8,128)(2,1)S(1)} %pad_maximum_fusion.1), channel_id=1, source_target_pairs={{0,8},{1,9},{2,10},{3,11},{4,12},{5,13},{6,14},{7,15},{8,0},{9,1},... | collective-permute-start | bytes 98312 | tf_op jit(solution)/shard_map/ppermute | solution.py:378
  41.5 3.2 %slice-start.2 = ((s8[14680064]{0:T(1024)(128)(4,1)}), s8[4194304]{0:T(1024)(128)(4,1)S(1)}, s32[]{:S(2)}) async-start(s8[14680064]{0:T(1024)(128)(4,1)} %bitcast.3), calls=%async_computation.2 | async-start | bytes 8388608
  41.5 3.2 %slice-start.3 = ((s8[14680064]{0:T(1024)(128)(4,1)}), s8[2097152]{0:T(1024)(128)(4,1)S(1)}, s32[]{:S(2)}) async-start(s8[14680064]{0:T(1024)(128)(4,1)} %bitcast.3), calls=%async_computation.3 | async-start | bytes 4194304
  43.8 33.8 %copy-start.2 = (s32[2]{0:T(128)S(1)}, s32[2]{0:T(128)}, u32[]{:S(2)}) copy-start(s32[2]{0:T(128)} %param.15) | copy-start | bytes 28
  49.2 3.7 %collective-permute-start.23 = (bf16[32,8192]{1,0:T(8,128)(2,1)S(1)}, bf16[32,8192]{1,0:T(8,128)(2,1)S(1)}, u32[]{:S(2)}, u32[]{:S(2)}) collective-permute-start(bf16[32,8192]{1,0:T(8,128)(2,1)S(1)} %get-tuple-element.49), channel_id=1, source_target_pairs={{0,1},{1,0},{2,3},{3,2},{4,5},{5,4},{6,7},{7,6},{8,9},{9,8},{10,11... | collective-permute-start | bytes 1572872 | tf_op jit(solution)/shard_map/ppermute | solution.py:378
  49.3 2.3 %collective-permute-start.24 = (bf16[16,8192]{1,0:T(8,128)(2,1)S(1)}, bf16[16,8192]{1,0:T(8,128)(2,1)S(1)}, u32[]{:S(2)}, u32[]{:S(2)}) collective-permute-start(bf16[16,8192]{1,0:T(8,128)(2,1)S(1)} %get-tuple-element.51), channel_id=1, source_target_pairs={{0,1},{1,0},{2,3},{3,2},{4,5},{5,4},{6,7},{7,6},{8,9},{9,8},{10,11... | collective-permute-start | bytes 786440 | tf_op jit(solution)/shard_map/ppermute | solution.py:378
  49.8 9.7 %collective-permute-start.22 = (bf16[32,8192]{1,0:T(8,128)(2,1)S(1)}, bf16[32,8192]{1,0:T(8,128)(2,1)S(1)}, u32[]{:S(2)}, u32[]{:S(2)}) collective-permute-start(bf16[32,8192]{1,0:T(8,128)(2,1)S(1)} %get-tuple-element.47), channel_id=1, source_target_pairs={{0,1},{1,0},{2,3},{3,2},{4,5},{5,4},{6,7},{7,6},{8,9},{9,8},{10,11... | collective-permute-start | bytes 1572872 | tf_op jit(solution)/shard_map/ppermute | solution.py:378
  51.6 6.4 %collective-permute-start.25 = (bf16[16,8192]{1,0:T(8,128)(2,1)S(1)}, bf16[16,8192]{1,0:T(8,128)(2,1)S(1)}, u32[]{:S(2)}, u32[]{:S(2)}) collective-permute-start(bf16[16,8192]{1,0:T(8,128)(2,1)S(1)} %added.7), channel_id=1, source_target_pairs={{0,4},{1,3},{4,8},{5,1},{8,12},{9,5},{12,14},{13,9},{14,10},{15,13... | collective-permute-start | bytes 786440 | tf_op jit(solution)/shard_map/ppermute | solution.py:375
  53.0 7.9 %collective-permute-start.29 = (bf16[16,8192]{1,0:T(8,128)(2,1)S(1)}, bf16[16,8192]{1,0:T(8,128)(2,1)S(1)}, u32[]{:S(2)}, u32[]{:S(2)}) collective-permute-start(bf16[16,8192]{1,0:T(8,128)(2,1)S(1)} %added.11), channel_id=1, source_target_pairs={{0,4},{1,3},{4,8},{5,1},{8,12},{9,5},{12,14},{13,9},{14,10},{15,13... | collective-permute-start | bytes 786440 | tf_op jit(solution)/shard_map/ppermute | solution.py:375
  54.9 11.1 %collective-permute-start.21 = (bf16[32,8192]{1,0:T(8,128)(2,1)S(1)}, bf16[32,8192]{1,0:T(8,128)(2,1)S(1)}, u32[]{:S(2)}, u32[]{:S(2)}) collective-permute-start(bf16[32,8192]{1,0:T(8,128)(2,1)S(1)} %get-tuple-element.45), channel_id=1, source_target_pairs={{0,1},{1,0},{2,3},{3,2},{4,5},{5,4},{6,7},{7,6},{8,9},{9,8},{10,11... | collective-permute-start | bytes 1572872 | tf_op jit(solution)/shard_map/ppermute | solution.py:378
  58.2 6.4 %collective-permute-start.26 = (bf16[16,8192]{1,0:T(8,128)(2,1)S(1)}, bf16[16,8192]{1,0:T(8,128)(2,1)S(1)}, u32[]{:S(2)}, u32[]{:S(2)}) collective-permute-start(bf16[16,8192]{1,0:T(8,128)(2,1)S(1)} %added.8), channel_id=1, source_target_pairs={{0,4},{1,3},{4,8},{5,1},{8,12},{9,5},{12,14},{13,9},{14,10},{15,13... | collective-permute-start | bytes 786440 | tf_op jit(solution)/shard_map/ppermute | solution.py:375
  61.0 6.4 %collective-permute-start.30 = (bf16[16,8192]{1,0:T(8,128)(2,1)S(1)}, bf16[16,8192]{1,0:T(8,128)(2,1)S(1)}, u32[]{:S(2)}, u32[]{:S(2)}) collective-permute-start(bf16[16,8192]{1,0:T(8,128)(2,1)S(1)} %added.12), channel_id=1, source_target_pairs={{0,4},{1,3},{4,8},{5,1},{8,12},{9,5},{12,14},{13,9},{14,10},{15,13... | collective-permute-start | bytes 786440 | tf_op jit(solution)/shard_map/ppermute | solution.py:375
  64.7 6.4 %collective-permute-start.27 = (bf16[16,8192]{1,0:T(8,128)(2,1)S(1)}, bf16[16,8192]{1,0:T(8,128)(2,1)S(1)}, u32[]{:S(2)}, u32[]{:S(2)}) collective-permute-start(bf16[16,8192]{1,0:T(8,128)(2,1)S(1)} %added.9), channel_id=1, source_target_pairs={{0,4},{1,3},{4,8},{5,1},{8,12},{9,5},{12,14},{13,9},{14,10},{15,13... | collective-permute-start | bytes 786440 | tf_op jit(solution)/shard_map/ppermute | solution.py:375
  67.5 6.4 %collective-permute-start.31 = (bf16[16,8192]{1,0:T(8,128)(2,1)S(1)}, bf16[16,8192]{1,0:T(8,128)(2,1)S(1)}, u32[]{:S(2)}, u32[]{:S(2)}) collective-permute-start(bf16[16,8192]{1,0:T(8,128)(2,1)S(1)} %added.13), channel_id=1, source_target_pairs={{0,4},{1,3},{4,8},{5,1},{8,12},{9,5},{12,14},{13,9},{14,10},{15,13... | collective-permute-start | bytes 786440 | tf_op jit(solution)/shard_map/ppermute | solution.py:375
  68.8 5.1 %collective-permute-start.20 = (bf16[16,8192]{1,0:T(8,128)(2,1)S(1)}, bf16[16,8192]{1,0:T(8,128)(2,1)S(1)}, u32[]{:S(2)}, u32[]{:S(2)}) collective-permute-start(bf16[16,8192]{1,0:T(8,128)(2,1)S(1)} %get-tuple-element.43), channel_id=1, source_target_pairs={{0,1},{1,0},{2,3},{3,2},{4,5},{5,4},{6,7},{7,6},{8,9},{9,8},{10,11... | collective-permute-start | bytes 786440 | tf_op jit(solution)/shard_map/ppermute | solution.py:378
  71.2 6.4 %collective-permute-start.28 = (bf16[16,8192]{1,0:T(8,128)(2,1)S(1)}, bf16[16,8192]{1,0:T(8,128)(2,1)S(1)}, u32[]{:S(2)}, u32[]{:S(2)}) collective-permute-start(bf16[16,8192]{1,0:T(8,128)(2,1)S(1)} %added.10), channel_id=1, source_target_pairs={{0,4},{1,3},{4,8},{5,1},{8,12},{9,5},{12,14},{13,9},{14,10},{15,13... | collective-permute-start | bytes 786440 | tf_op jit(solution)/shard_map/ppermute | solution.py:375
  73.9 3.7 %collective-permute-start.32 = (bf16[16,8192]{1,0:T(8,128)(2,1)S(1)}, bf16[16,8192]{1,0:T(8,128)(2,1)S(1)}, u32[]{:S(2)}, u32[]{:S(2)}) collective-permute-start(bf16[16,8192]{1,0:T(8,128)(2,1)S(1)} %collective-permute-done.31), channel_id=1, source_target_pairs={{0,1},{1,0},{2,3},{3,2},{4,5},{5,4},{6,7},{7,6},{8,9},{9,8},{10,11... | collective-permute-start | bytes 786440 | tf_op jit(solution)/shard_map/ppermute | solution.py:378

commit v13 on v12

--- a/solution.py
+++ b/solution.py
@@ -121,7 +121,6 @@
     block_rows = members * rows // blocks
     device = lax.axis_index("tp")
     places = arrivals(device, members, rows)
-    lhs = jnp.concatenate([piece[...] for piece in pieces], axis=0)
     ids = [picked(ids_ref, b) for b in range(blocks)]
     copies = [
         pltpu.make_async_copy(expand_ref.at[ids[b]], chosen_ref.at[b], sems.at[b])
@@ -130,9 +129,17 @@
     for copy in copies:
         copy.start()
     weights = jnp.concatenate([ref[i] for ref in (own_ref, other_ref) for i in ids], axis=0)
-    found = lax.dot_general(
-        lhs, weights, (((1,), (1,)), ((), ())), preferred_element_type=F32
-    )
+    wanted = weights.shape[0]
+    slices = max(1, 256 // wanted)
+    depth = weights.shape[1] // slices
+    spans = [slice(i * depth, (i + 1) * depth) for i in range(slices)]
+    lhs = jnp.concatenate([piece[:, cut] for cut in spans for piece in pieces], axis=0)
+    rhs = jnp.concatenate([weights[:, cut] for cut in spans], axis=0)
+    squares = lax.dot_general(lhs, rhs, (((1,), (1,)), ((), ())), preferred_element_type=F32)
+    height = len(pieces) * rows
+    found = 0.0
+    for i in range(slices):
+        found += squares[i * height : (i + 1) * height, i * wanted : (i + 1) * wanted]
     scratch[...] = jnp.zeros_like(scratch)
     for index, number in enumerate(numbers):
         part = found[index * rows : (index + 1) * rows]
@@ -287,7 +294,7 @@
 def down(hidden, down_matrix, groups, rows):
     total, depth = hidden.shape
     columns = down_matrix.shape[1]
-    size = min(1024, columns)
+    size = min(2048, columns)
     return pl.pallas_call(
         functools.partial(down_kernel, groups, rows, size),
         in_specs=whole(2),

time: 78.8 us -> 78.8 us (level)
  no operation moved by 1% of the time
where the time goes in v13:
time: 78.8 us; the launch traced here: 78.6 us
  starting transfers between devices  32.7 us (41%)
  waiting for transfers between devices  27.2 us (35%)
  Pallas kernels  18.4 us (23%)
    ppermute x14, waiting for transfers between devices, step(): return lax.ppermute(x, 'tp', ring)  25.4 us
    ppermute x14, starting transfers between devices, step(): return lax.ppermute(x, 'tp', ring)  23.6 us
    ppermute x19, starting transfers between devices, cross(): return lax.ppermute(x, 'tp', crossing(members, bit))  9.17 us
    pallas_call x4, Pallas kernels, product(): pl.pallas_call(functools.partial(product_kernel, part * depth, depth, mai...  8.55 us
    pallas_call x1, Pallas kernels, down(): pl.pallas_call(functools.partial(down_kernel, groups, rows, size), in_spe...  4.5 us
    ppermute x19, waiting for transfers between devices, cross(): return lax.ppermute(x, 'tp', crossing(members, bit))  1.74 us
    pallas_call x1, Pallas kernels, anchor(): pl.pallas_call(anchor_kernel, in_specs=[FAR, FAR], out_specs=whole(1) + [...  1.71 us
  transfers between devices with their start and end apart: 33, of which 15 were waited for; matrix products, arithmetic and copies ran while one was open for 0% of the time, Pallas kernels for 15%

profile of v13, /device:TPU:0, one launch (start us, length us, event | category | flops | bytes accessed | tf_op | source)
XLA Modules:
  0.0 78.6 jit_solution(8784999251553196646)
XLA Ops:
  0.0 0.5 collective-permute-start
  0.5 2.6 %collective-permute-start.1 = (bf16[16,8192]{1,0:T(8,128)(2,1)}, bf16[16,8192]{1,0:T(8,128)(2,1)S(1)}, u32[]{:S(2)}, u32[]{:S(2)}) collective-permute-start(bf16[16,8192]{1,0:T(8,128)(2,1)} %tokens_ref.1), channel_id=1, source_target_pairs={{0,4},{1,3},{4,8},{5,1},{8,12},{9,5},{12,14},{13,9},{14,10},{15,13... | collective-permute-start | bytes 786440 | tf_op jit(solution)/shard_map/ppermute | solution.py:382
  3.2 1.7 %anchor.1 = (bf16[16,8192]{1,0:T(8,128)(2,1)S(1)}, bf16[16,8192]{1,0:T(8,128)(2,1)S(1)}) custom-call(bf16[16,8192]{1,0:T(8,128)(2,1)} %tokens_ref.1, bf16[16,8192]{1,0:T(8,128)(2,1)S(1)} %collective-permute-done.passed_in), custom_call_target="tpu_custom_call", output_to_operand_aliasing={{1}: (1, {})} | custom-call | flops 30000001024 | tf_op jit(solution)/shard_map/anchor/pallas_call | solution.py:104
  4.9 1.7 %collective-permute-start.2 = (bf16[16,8192]{1,0:T(8,128)(2,1)S(1)}, bf16[16,8192]{1,0:T(8,128)(2,1)S(1)}, u32[]{:S(2)}, u32[]{:S(2)}) collective-permute-start(bf16[16,8192]{1,0:T(8,128)(2,1)S(1)} %get-tuple-element.31.refs_1_.refs_2_), channel_id=1, source_target_pairs={{0,4},{1,3},{4,8},{5,1},{8,12},{9,5},{12,14},{13,9},{14,10},{15,13... | collective-permute-start | bytes 786440 | tf_op jit(solution)/shard_map/ppermute | solution.py:382
  6.6 1.1 %collective-permute-done.1.refs_1_.refs_2_.refs_3_ = bf16[16,8192]{1,0:T(8,128)(2,1)S(1)} collective-permute-done((bf16[16,8192]{1,0:T(8,128)(2,1)}, bf16[16,8192]{1,0:T(8,128)(2,1)S(1)}, u32[]{:S(2)}, u32[]{:S(2)}) %collective-permute-start.1) | collective-permute-done | bytes 262176 | tf_op jit(solution)/shard_map/ppermute | solution.py:382
  7.7 2.1 %collective-permute-start.3 = (bf16[16,8192]{1,0:T(8,128)(2,1)S(1)}, bf16[16,8192]{1,0:T(8,128)(2,1)S(1)}, u32[]{:S(2)}, u32[]{:S(2)}) collective-permute-start(bf16[16,8192]{1,0:T(8,128)(2,1)S(1)} %collective-permute-done.1.refs_1_.refs_2_.refs_3_), channel_id=1, source_target_pairs={{0,4},{1,3},{4,8},{5,1},{8,12},{9,5},{12,14},{13,9},{14,10},{15,13... | collective-permute-start | bytes 786440 | tf_op jit(solution)/shard_map/ppermute | solution.py:382
  9.8 1.6 %collective-permute-done.2.refs_2_.refs_3_.refs_4_ = bf16[16,8192]{1,0:T(8,128)(2,1)S(1)} collective-permute-done((bf16[16,8192]{1,0:T(8,128)(2,1)S(1)}, bf16[16,8192]{1,0:T(8,128)(2,1)S(1)}, u32[]{:S(2)}, u32[]{:S(2)}) %collective-permute-start.2) | collective-permute-done | bytes 262176 | tf_op jit(solution)/shard_map/ppermute | solution.py:382
  11.3 1.7 %collective-permute-start.4 = (bf16[16,8192]{1,0:T(8,128)(2,1)S(1)}, bf16[16,8192]{1,0:T(8,128)(2,1)S(1)}, u32[]{:S(2)}, u32[]{:S(2)}) collective-permute-start(bf16[16,8192]{1,0:T(8,128)(2,1)S(1)} %collective-permute-done.2.refs_2_.refs_3_.refs_4_), channel_id=1, source_target_pairs={{0,4},{1,3},{4,8},{5,1},{8,12},{9,5},{12,14},{13,9},{14,10},{15,13... | collective-permute-start | bytes 786440 | tf_op jit(solution)/shard_map/ppermute | solution.py:382
  13.0 1.1 %collective-permute-done.3.refs_3_.refs_4_.refs_5_ = bf16[16,8192]{1,0:T(8,128)(2,1)S(1)} collective-permute-done((bf16[16,8192]{1,0:T(8,128)(2,1)S(1)}, bf16[16,8192]{1,0:T(8,128)(2,1)S(1)}, u32[]{:S(2)}, u32[]{:S(2)}) %collective-permute-start.3) | collective-permute-done | bytes 262176 | tf_op jit(solution)/shard_map/ppermute | solution.py:382
  14.1 2.0 %collective-permute-start.5 = (bf16[16,8192]{1,0:T(8,128)(2,1)S(1)}, bf16[16,8192]{1,0:T(8,128)(2,1)S(1)}, u32[]{:S(2)}, u32[]{:S(2)}) collective-permute-start(bf16[16,8192]{1,0:T(8,128)(2,1)S(1)} %collective-permute-done.3.refs_3_.refs_4_.refs_5_), channel_id=1, source_target_pairs={{0,4},{1,3},{4,8},{5,1},{8,12},{9,5},{12,14},{13,9},{14,10},{15,13... | collective-permute-start | bytes 786440 | tf_op jit(solution)/shard_map/ppermute | solution.py:382
  16.1 0.0 collective-permute-start.9
  16.1 0.0 collective-permute-done.8.refs_8_.refs_9_.refs_10_
  16.1 0.5 collective-permute-start.10
  16.6 1.1 %collective-permute-done.4.refs_4_.refs_5_.refs_6_ = bf16[16,8192]{1,0:T(8,128)(2,1)S(1)} collective-permute-done((bf16[16,8192]{1,0:T(8,128)(2,1)S(1)}, bf16[16,8192]{1,0:T(8,128)(2,1)S(1)}, u32[]{:S(2)}, u32[]{:S(2)}) %collective-permute-start.4) | collective-permute-done | bytes 262176 | tf_op jit(solution)/shard_map/ppermute | solution.py:382
  17.7 1.7 %collective-permute-start.6 = (bf16[16,8192]{1,0:T(8,128)(2,1)S(1)}, bf16[16,8192]{1,0:T(8,128)(2,1)S(1)}, u32[]{:S(2)}, u32[]{:S(2)}) collective-permute-start(bf16[16,8192]{1,0:T(8,128)(2,1)S(1)} %collective-permute-done.4.refs_4_.refs_5_.refs_6_), channel_id=1, source_target_pairs={{0,4},{1,3},{4,8},{5,1},{8,12},{9,5},{12,14},{13,9},{14,10},{15,13... | collective-permute-start | bytes 786440 | tf_op jit(solution)/shard_map/ppermute | solution.py:382
  19.4 1.1 %collective-permute-done.5.refs_5_.refs_6_.refs_7_ = bf16[16,8192]{1,0:T(8,128)(2,1)S(1)} collective-permute-done((bf16[16,8192]{1,0:T(8,128)(2,1)S(1)}, bf16[16,8192]{1,0:T(8,128)(2,1)S(1)}, u32[]{:S(2)}, u32[]{:S(2)}) %collective-permute-start.5) | collective-permute-done | bytes 262176 | tf_op jit(solution)/shard_map/ppermute | solution.py:382
  20.5 2.0 %collective-permute-start.7 = (bf16[16,8192]{1,0:T(8,128)(2,1)S(1)}, bf16[16,8192]{1,0:T(8,128)(2,1)S(1)}, u32[]{:S(2)}, u32[]{:S(2)}) collective-permute-start(bf16[16,8192]{1,0:T(8,128)(2,1)S(1)} %collective-permute-done.5.refs_5_.refs_6_.refs_7_), channel_id=1, source_target_pairs={{0,4},{1,3},{4,8},{5,1},{8,12},{9,5},{12,14},{13,9},{14,10},{15,13... | collective-permute-start | bytes 786440 | tf_op jit(solution)/shard_map/ppermute | solution.py:382
  22.5 0.5 collective-permute-start.12
  23.0 1.0 %collective-permute-done.6.refs_6_.refs_7_.refs_8_ = bf16[16,8192]{1,0:T(8,128)(2,1)S(1)} collective-permute-done((bf16[16,8192]{1,0:T(8,128)(2,1)S(1)}, bf16[16,8192]{1,0:T(8,128)(2,1)S(1)}, u32[]{:S(2)}, u32[]{:S(2)}) %collective-permute-start.6) | collective-permute-done | bytes 262176 | tf_op jit(solution)/shard_map/ppermute | solution.py:382
  24.1 0.0 collective-permute-start.13
  24.1 2.8 %collective-permute-done.7.refs_7_.refs_8_.refs_9_ = bf16[16,8192]{1,0:T(8,128)(2,1)S(1)} collective-permute-done((bf16[16,8192]{1,0:T(8,128)(2,1)S(1)}, bf16[16,8192]{1,0:T(8,128)(2,1)S(1)}, u32[]{:S(2)}, u32[]{:S(2)}) %collective-permute-start.7) | collective-permute-done | bytes 262176 | tf_op jit(solution)/shard_map/ppermute | solution.py:382
  26.9 0.0 collective-permute-done.11.refs_11_.refs_12_.refs_13_
  26.9 0.0 collective-permute-done.12.refs_12_.refs_13_.refs_14_
  26.9 1.2 %rank.1 = (bf16[16,256]{1,0:T(8,128)(2,1)S(1)}, bf16[2,128,896]{2,1,0:T(8,128)(2,1)S(1)}) custom-call(s32[1,2]{1,0:T(1,128)S(1)} %bitcast.7, bf16[8,128,896]{2,1,0:T(8,128)(2,1)} %expand_ref.1, bf16[8,8,8192]{2,1,0:T(8,128)(2,1)S(1)} %bitcast.6, bf16[8,8,8192]{2,1,0:T(8,128)(2,1)S(1)} %collective-permute-done.15.other_ref, ...), custom_call_target="tpu_custom_call" | custom-call | flops 67108864 | bytes 4194304 | tf_op jit(solution)/shard_map/rank/pallas_call | solution.py:166
  28.1 0.6 collective-permute-start.16
  28.7 1.9 %product.4 = (f32[256,768]{1,0:T(8,128)S(1)}, bf16[4096,128]{1,0:T(8,128)(2,1)S(1)}) custom-call(bf16[8192,896]{1,0:T(8,128)(2,1)S(1)} %copy-done.3, bf16[16,8192]{1,0:T(8,128)(2,1)S(1)} %get-tuple-element.30.refs_0_.refs_1_, bf16[16,8192]{1,0:T(8,128)(2,1)S(1)} %get-tuple-element.31.refs_1_.refs_2_, ...), custom_call_target="tpu_custom_call" | custom-call | flops 5637144576 | bytes 9437184 | tf_op jit(solution)/shard_map/product/pallas_call | solution.py:220
  30.7 0.0 slice-start.6
  30.7 2.0 %collective-permute-start.17 = (bf16[16,256]{1,0:T(8,128)(2,1)S(1)}, bf16[16,256]{1,0:T(8,128)(2,1)S(1)}, u32[]{:S(2)}, u32[]{:S(2)}) collective-permute-start(bf16[16,256]{1,0:T(8,128)(2,1)S(1)} %add.3), channel_id=1, source_target_pairs={{0,2},{1,3},{2,0},{3,1},{4,6},{5,7},{6,4},{7,5},{8,10},{9,11},{10,... | collective-permute-start | bytes 24584 | tf_op jit(solution)/shard_map/ppermute | solution.py:385
  32.7 1.9 %product.5 = (f32[256,768]{1,0:T(8,128)S(1)}, bf16[4096,128]{1,0:T(8,128)(2,1)S(1)}) custom-call(bf16[8192,896]{1,0:T(8,128)(2,1)S(1)} %copy-done.3, bf16[16,8192]{1,0:T(8,128)(2,1)S(1)} %get-tuple-element.30.refs_0_.refs_1_, bf16[16,8192]{1,0:T(8,128)(2,1)S(1)} %get-tuple-element.31.refs_1_.refs_2_, ...), custom_call_target="tpu_custom_call" | custom-call | flops 5637144576 | bytes 9437184 | tf_op jit(solution)/shard_map/product/pallas_call | solution.py:220
  34.7 1.7 %collective-permute-start.18 = (bf16[32,256]{1,0:T(8,128)(2,1)S(1)}, bf16[32,256]{1,0:T(8,128)(2,1)S(1)}, u32[]{:S(2)}, u32[]{:S(2)}) collective-permute-start(bf16[32,256]{1,0:T(8,128)(2,1)S(1)} %pad_maximum_fusion.2), channel_id=1, source_target_pairs={{0,4},{1,5},{2,6},{3,7},{4,0},{5,1},{6,2},{7,3},{8,12},{9,13},{10,... | collective-permute-start | bytes 49160 | tf_op jit(solution)/shard_map/ppermute | solution.py:385
  36.4 0.0 slice-start
  36.5 0.0 slice-start.1
  36.5 2.3 %product.6 = (f32[256,768]{1,0:T(8,128)S(1)}, f32[256,256]{1,0:T(8,128)S(1)}) custom-call(bf16[8192,896]{1,0:T(8,128)(2,1)S(1)} %bitcast.10, bf16[4096,128]{1,0:T(8,128)(2,1)S(1)} %get-tuple-element.35.refs_0_, bf16[16,8192]{1,0:T(8,128)(2,1)S(1)} %get-tuple-element.30.refs_0_.refs_1_, bf16[16,8192]{1,0:T(8,128)(2,1)S(1)} %get-tuple-element.31.refs_1_.refs_2_, ...), custom_call_target="tpu_custom_call" | custom-call | flops 5637144576 | bytes 9437184 | tf_op jit(solution)/shard_map/product/pallas_call | solution.py:220
  38.8 2.7 %collective-permute-start.19 = (bf16[64,256]{1,0:T(8,128)(2,1)S(1)}, bf16[64,256]{1,0:T(8,128)(2,1)S(1)}, u32[]{:S(2)}, u32[]{:S(2)}) collective-permute-start(bf16[64,256]{1,0:T(8,128)(2,1)S(1)} %pad_maximum_fusion.1), channel_id=1, source_target_pairs={{0,8},{1,9},{2,10},{3,11},{4,12},{5,13},{6,14},{7,15},{8,0},{9,1},... | collective-permute-start | bytes 98312 | tf_op jit(solution)/shard_map/ppermute | solution.py:385
  41.5 2.3 %product.7 = (f32[256,768]{1,0:T(8,128)S(1)}, f32[256,256]{1,0:T(8,128)S(1)}) custom-call(bf16[8192,896]{1,0:T(8,128)(2,1)S(1)} %bitcast.10, bf16[4096,128]{1,0:T(8,128)(2,1)S(1)} %get-tuple-element.37.refs_0_, bf16[16,8192]{1,0:T(8,128)(2,1)S(1)} %get-tuple-element.30.refs_0_.refs_1_, bf16[16,8192]{1,0:T(8,128)(2,1)S(1)} %get-tuple-element.31.refs_1_.refs_2_, ...), custom_call_target="tpu_custom_call" | custom-call | flops 5637144576 | bytes 9437184 | tf_op jit(solution)/shard_map/product/pallas_call | solution.py:220
  43.8 0.0 copy-start.2
  43.9 0.8 finish.1.hidden_ref
  44.7 4.5 %down.1 = (bf16[16,8192]{1,0:T(8,128)(2,1)S(1)}, bf16[16,8192]{1,0:T(8,128)(2,1)S(1)}, bf16[16,8192]{1,0:T(8,128)(2,1)S(1)}, bf16[16,8192]{1,0:T(8,128)(2,1)S(1)...) custom-call(bf16[896,8192]{1,0:T(8,128)(2,1)S(1)} %bitcast.4, ...), custom_call_target="tpu_custom_call" | custom-call | flops 3758096384 | bytes 18874368 | tf_op jit(solution)/shard_map/down/pallas_call | solution.py:298
  49.2 0.1 collective-permute-start.23
  49.3 0.5 collective-permute-start.24
  49.8 0.1 collective-permute-start.22
  49.9 1.7 %collective-permute-done.24.refs_1_ = bf16[16,8192]{1,0:T(8,128)(2,1)S(1)} collective-permute-done((bf16[16,8192]{1,0:T(8,128)(2,1)S(1)}, bf16[16,8192]{1,0:T(8,128)(2,1)S(1)}, u32[]{:S(2)}, u32[]{:S(2)}) %collective-permute-start.24) | collective-permute-done | bytes 262176 | tf_op jit(solution)/shard_map/ppermute | solution.py:385
  51.6 0.1 added.7
  51.6 1.3 %collective-permute-start.25 = (bf16[16,8192]{1,0:T(8,128)(2,1)S(1)}, bf16[16,8192]{1,0:T(8,128)(2,1)S(1)}, u32[]{:S(2)}, u32[]{:S(2)}) collective-permute-start(bf16[16,8192]{1,0:T(8,128)(2,1)S(1)} %added.7), channel_id=1, source_target_pairs={{0,4},{1,3},{4,8},{5,1},{8,12},{9,5},{12,14},{13,9},{14,10},{15,13... | collective-permute-start | bytes 786440 | tf_op jit(solution)/shard_map/ppermute | solution.py:382
  52.9 0.1 added.11
  53.0 1.9 %collective-permute-start.29 = (bf16[16,8192]{1,0:T(8,128)(2,1)S(1)}, bf16[16,8192]{1,0:T(8,128)(2,1)S(1)}, u32[]{:S(2)}, u32[]{:S(2)}) collective-permute-start(bf16[16,8192]{1,0:T(8,128)(2,1)S(1)} %added.11), channel_id=1, source_target_pairs={{0,4},{1,3},{4,8},{5,1},{8,12},{9,5},{12,14},{13,9},{14,10},{15,13... | collective-permute-start | bytes 786440 | tf_op jit(solution)/shard_map/ppermute | solution.py:382
  54.9 3.1 %collective-permute-done.25.refs_2_ = bf16[16,8192]{1,0:T(8,128)(2,1)S(1)} collective-permute-done((bf16[16,8192]{1,0:T(8,128)(2,1)S(1)}, bf16[16,8192]{1,0:T(8,128)(2,1)S(1)}, u32[]{:S(2)}, u32[]{:S(2)}) %collective-permute-start.25) | collective-permute-done | bytes 262176 | tf_op jit(solution)/shard_map/ppermute | solution.py:382
  58.1 0.1 added.8
  58.2 1.3 %collective-permute-start.26 = (bf16[16,8192]{1,0:T(8,128)(2,1)S(1)}, bf16[16,8192]{1,0:T(8,128)(2,1)S(1)}, u32[]{:S(2)}, u32[]{:S(2)}) collective-permute-start(bf16[16,8192]{1,0:T(8,128)(2,1)S(1)} %added.8), channel_id=1, source_target_pairs={{0,4},{1,3},{4,8},{5,1},{8,12},{9,5},{12,14},{13,9},{14,10},{15,13... | collective-permute-start | bytes 786440 | tf_op jit(solution)/shard_map/ppermute | solution.py:382
  59.5 1.4 %collective-permute-done.29.refs_2_ = bf16[16,8192]{1,0:T(8,128)(2,1)S(1)} collective-permute-done((bf16[16,8192]{1,0:T(8,128)(2,1)S(1)}, bf16[16,8192]{1,0:T(8,128)(2,1)S(1)}, u32[]{:S(2)}, u32[]{:S(2)}) %collective-permute-start.29) | collective-permute-done | bytes 262176 | tf_op jit(solution)/shard_map/ppermute | solution.py:382
  60.9 0.1 added.12
  61.0 1.3 %collective-permute-start.30 = (bf16[16,8192]{1,0:T(8,128)(2,1)S(1)}, bf16[16,8192]{1,0:T(8,128)(2,1)S(1)}, u32[]{:S(2)}, u32[]{:S(2)}) collective-permute-start(bf16[16,8192]{1,0:T(8,128)(2,1)S(1)} %added.12), channel_id=1, source_target_pairs={{0,4},{1,3},{4,8},{5,1},{8,12},{9,5},{12,14},{13,9},{14,10},{15,13... | collective-permute-start | bytes 786440 | tf_op jit(solution)/shard_map/ppermute | solution.py:382
  62.3 2.3 %collective-permute-done.26.refs_2_ = bf16[16,8192]{1,0:T(8,128)(2,1)S(1)} collective-permute-done((bf16[16,8192]{1,0:T(8,128)(2,1)S(1)}, bf16[16,8192]{1,0:T(8,128)(2,1)S(1)}, u32[]{:S(2)}, u32[]{:S(2)}) %collective-permute-start.26) | collective-permute-done | bytes 262176 | tf_op jit(solution)/shard_map/ppermute | solution.py:382
  64.6 0.1 added.9
  64.7 1.3 %collective-permute-start.27 = (bf16[16,8192]{1,0:T(8,128)(2,1)S(1)}, bf16[16,8192]{1,0:T(8,128)(2,1)S(1)}, u32[]{:S(2)}, u32[]{:S(2)}) collective-permute-start(bf16[16,8192]{1,0:T(8,128)(2,1)S(1)} %added.9), channel_id=1, source_target_pairs={{0,4},{1,3},{4,8},{5,1},{8,12},{9,5},{12,14},{13,9},{14,10},{15,13... | collective-permute-start | bytes 786440 | tf_op jit(solution)/shard_map/ppermute | solution.py:382
  66.0 1.4 %collective-permute-done.30.refs_2_ = bf16[16,8192]{1,0:T(8,128)(2,1)S(1)} collective-permute-done((bf16[16,8192]{1,0:T(8,128)(2,1)S(1)}, bf16[16,8192]{1,0:T(8,128)(2,1)S(1)}, u32[]{:S(2)}, u32[]{:S(2)}) %collective-permute-start.30) | collective-permute-done | bytes 262176 | tf_op jit(solution)/shard_map/ppermute | solution.py:382
  67.4 0.1 added.13
  67.5 1.3 %collective-permute-start.31 = (bf16[16,8192]{1,0:T(8,128)(2,1)S(1)}, bf16[16,8192]{1,0:T(8,128)(2,1)S(1)}, u32[]{:S(2)}, u32[]{:S(2)}) collective-permute-start(bf16[16,8192]{1,0:T(8,128)(2,1)S(1)} %added.13), channel_id=1, source_target_pairs={{0,4},{1,3},{4,8},{5,1},{8,12},{9,5},{12,14},{13,9},{14,10},{15,13... | collective-permute-start | bytes 786440 | tf_op jit(solution)/shard_map/ppermute | solution.py:382
  68.8 2.3 %collective-permute-done.27.refs_2_ = bf16[16,8192]{1,0:T(8,128)(2,1)S(1)} collective-permute-done((bf16[16,8192]{1,0:T(8,128)(2,1)S(1)}, bf16[16,8192]{1,0:T(8,128)(2,1)S(1)}, u32[]{:S(2)}, u32[]{:S(2)}) %collective-permute-start.27) | collective-permute-done | bytes 262176 | tf_op jit(solution)/shard_map/ppermute | solution.py:382
  71.1 0.1 added.10
  71.2 1.3 %collective-permute-start.28 = (bf16[16,8192]{1,0:T(8,128)(2,1)S(1)}, bf16[16,8192]{1,0:T(8,128)(2,1)S(1)}, u32[]{:S(2)}, u32[]{:S(2)}) collective-permute-start(bf16[16,8192]{1,0:T(8,128)(2,1)S(1)} %added.10), channel_id=1, source_target_pairs={{0,4},{1,3},{4,8},{5,1},{8,12},{9,5},{12,14},{13,9},{14,10},{15,13... | collective-permute-start | bytes 786440 | tf_op jit(solution)/shard_map/ppermute | solution.py:382
  72.5 1.4 %collective-permute-done.31 = bf16[16,8192]{1,0:T(8,128)(2,1)S(1)} collective-permute-done((bf16[16,8192]{1,0:T(8,128)(2,1)S(1)}, bf16[16,8192]{1,0:T(8,128)(2,1)S(1)}, u32[]{:S(2)}, u32[]{:S(2)}) %collective-permute-start.31) | collective-permute-done | bytes 262176 | tf_op jit(solution)/shard_map/ppermute | solution.py:382
  73.9 3.7 %collective-permute-done.28.refs_2_ = bf16[16,8192]{1,0:T(8,128)(2,1)S(1)} collective-permute-done((bf16[16,8192]{1,0:T(8,128)(2,1)S(1)}, bf16[16,8192]{1,0:T(8,128)(2,1)S(1)}, u32[]{:S(2)}, u32[]{:S(2)}) %collective-permute-start.28) | collective-permute-done | bytes 262176 | tf_op jit(solution)/shard_map/ppermute | solution.py:382
  77.6 1.0 %last.1 = bf16[16,8192]{1,0:T(8,128)(2,1)} custom-call(s32[1,2]{1,0:T(1,128)S(1)} %bitcast.8, bf16[16,8192]{1,0:T(8,128)(2,1)S(1)} %get-tuple-element.42.refs_0_, bf16[16,8192]{1,0:T(8,128)(2,1)S(1)} %collective-permute-done.20.refs_1_, bf16[16,8192]{1,0:T(8,128)(2,1)S(1)} %collective-permute-done.28.refs_2_, ...), custom_call_target="tpu_custom_call" | custom-call | tf_op jit(solution)/shard_map/last/pallas_call | solution.py:332
  (48 shorter events, 0.1 us)
Async XLA Ops:
  0.0 6.6 %copy-start = (bf16[8,8192,8]{1,2,0:T(8,128)(2,1)S(1)}, bf16[8,8192,8]{1,2,0:T(8,128)(2,1)}, u32[]{:S(2)}) copy-start(bf16[8,8192,8]{1,2,0:T(8,128)(2,1)} %param.12) | copy-start | bytes 3145732
  0.0 26.9 %copy-start.1 = (s32[2]{0:T(128)S(1)}, s32[2]{0:T(128)}, u32[]{:S(2)}) copy-start(s32[2]{0:T(128)} %param.14) | copy-start | bytes 28
  0.0 28.7 %copy-start.3 = (bf16[8192,896]{1,0:T(8,128)(2,1)S(1)}, bf16[8192,896]{1,0:T(8,128)(2,1)}, u32[]{:S(2)}) copy-start(bf16[8192,896]{1,0:T(8,128)(2,1)} %w_ref.6) | copy-start | bytes 44040196
  0.0 3.2 %collective-permute-start = (bf16[16,8192]{1,0:T(8,128)(2,1)}, bf16[16,8192]{1,0:T(8,128)(2,1)S(1)}, u32[]{:S(2)}, u32[]{:S(2)}) collective-permute-start(bf16[16,8192]{1,0:T(8,128)(2,1)} %tokens_ref.1), channel_id=1, source_target_pairs={{0,1},{1,0},{2,3},{3,2},{4,5},{5,4},{6,7},{7,6},{8,9},{9,8},{10,11... | collective-permute-start | bytes 786440 | tf_op jit(solution)/shard_map/ppermute | solution.py:385
  0.5 7.1 %collective-permute-start.1 = (bf16[16,8192]{1,0:T(8,128)(2,1)}, bf16[16,8192]{1,0:T(8,128)(2,1)S(1)}, u32[]{:S(2)}, u32[]{:S(2)}) collective-permute-start(bf16[16,8192]{1,0:T(8,128)(2,1)} %tokens_ref.1), channel_id=1, source_target_pairs={{0,4},{1,3},{4,8},{5,1},{8,12},{9,5},{12,14},{13,9},{14,10},{15,13... | collective-permute-start | bytes 786440 | tf_op jit(solution)/shard_map/ppermute | solution.py:382
  4.9 6.4 %collective-permute-start.2 = (bf16[16,8192]{1,0:T(8,128)(2,1)S(1)}, bf16[16,8192]{1,0:T(8,128)(2,1)S(1)}, u32[]{:S(2)}, u32[]{:S(2)}) collective-permute-start(bf16[16,8192]{1,0:T(8,128)(2,1)S(1)} %get-tuple-element.31.refs_1_.refs_2_), channel_id=1, source_target_pairs={{0,4},{1,3},{4,8},{5,1},{8,12},{9,5},{12,14},{13,9},{14,10},{15,13... | collective-permute-start | bytes 786440 | tf_op jit(solution)/shard_map/ppermute | solution.py:382
  6.6 20.3 %collective-permute-start.15 = (bf16[8,8,8192]{2,1,0:T(8,128)(2,1)S(1)}, bf16[8,8,8192]{2,1,0:T(8,128)(2,1)S(1)}, u32[]{:S(2)}, u32[]{:S(2)}) collective-permute-start(bf16[8,8,8192]{2,1,0:T(8,128)(2,1)S(1)} %bitcast.5), channel_id=1, source_target_pairs={{0,1},{1,0},{2,3},{3,2},{4,5},{5,4},{6,7},{7,6},{8,9},{9,8},{10,11... | collective-permute-start | bytes 3145736 | tf_op jit(solution)/shard_map/ppermute | solution.py:385
  7.7 6.5 %collective-permute-start.3 = (bf16[16,8192]{1,0:T(8,128)(2,1)S(1)}, bf16[16,8192]{1,0:T(8,128)(2,1)S(1)}, u32[]{:S(2)}, u32[]{:S(2)}) collective-permute-start(bf16[16,8192]{1,0:T(8,128)(2,1)S(1)} %collective-permute-done.1.refs_1_.refs_2_.refs_3_), channel_id=1, source_target_pairs={{0,4},{1,3},{4,8},{5,1},{8,12},{9,5},{12,14},{13,9},{14,10},{15,13... | collective-permute-start | bytes 786440 | tf_op jit(solution)/shard_map/ppermute | solution.py:382
  9.7 6.4 %collective-permute-start.8 = (bf16[16,8192]{1,0:T(8,128)(2,1)S(1)}, bf16[16,8192]{1,0:T(8,128)(2,1)S(1)}, u32[]{:S(2)}, u32[]{:S(2)}) collective-permute-start(bf16[16,8192]{1,0:T(8,128)(2,1)S(1)} %collective-permute-done.1.refs_1_.refs_2_.refs_3_), channel_id=1, source_target_pairs={{0,1},{1,0},{2,3},{3,2},{4,5},{5,4},{6,7},{7,6},{8,9},{9,8},{10,11... | collective-permute-start | bytes 786440 | tf_op jit(solution)/shard_map/ppermute | solution.py:385
  11.3 6.4 %collective-permute-start.4 = (bf16[16,8192]{1,0:T(8,128)(2,1)S(1)}, bf16[16,8192]{1,0:T(8,128)(2,1)S(1)}, u32[]{:S(2)}, u32[]{:S(2)}) collective-permute-start(bf16[16,8192]{1,0:T(8,128)(2,1)S(1)} %collective-permute-done.2.refs_2_.refs_3_.refs_4_), channel_id=1, source_target_pairs={{0,4},{1,3},{4,8},{5,1},{8,12},{9,5},{12,14},{13,9},{14,10},{15,13... | collective-permute-start | bytes 786440 | tf_op jit(solution)/shard_map/ppermute | solution.py:382
  14.1 6.4 %collective-permute-start.5 = (bf16[16,8192]{1,0:T(8,128)(2,1)S(1)}, bf16[16,8192]{1,0:T(8,128)(2,1)S(1)}, u32[]{:S(2)}, u32[]{:S(2)}) collective-permute-start(bf16[16,8192]{1,0:T(8,128)(2,1)S(1)} %collective-permute-done.3.refs_3_.refs_4_.refs_5_), channel_id=1, source_target_pairs={{0,4},{1,3},{4,8},{5,1},{8,12},{9,5},{12,14},{13,9},{14,10},{15,13... | collective-permute-start | bytes 786440 | tf_op jit(solution)/shard_map/ppermute | solution.py:382
  16.1 6.4 %collective-permute-start.9 = (bf16[16,8192]{1,0:T(8,128)(2,1)S(1)}, bf16[16,8192]{1,0:T(8,128)(2,1)S(1)}, u32[]{:S(2)}, u32[]{:S(2)}) collective-permute-start(bf16[16,8192]{1,0:T(8,128)(2,1)S(1)} %collective-permute-done.2.refs_2_.refs_3_.refs_4_), channel_id=1, source_target_pairs={{0,1},{1,0},{2,3},{3,2},{4,5},{5,4},{6,7},{7,6},{8,9},{9,8},{10,11... | collective-permute-start | bytes 786440 | tf_op jit(solution)/shard_map/ppermute | solution.py:385
  16.1 6.4 %collective-permute-start.10 = (bf16[16,8192]{1,0:T(8,128)(2,1)S(1)}, bf16[16,8192]{1,0:T(8,128)(2,1)S(1)}, u32[]{:S(2)}, u32[]{:S(2)}) collective-permute-start(bf16[16,8192]{1,0:T(8,128)(2,1)S(1)} %collective-permute-done.3.refs_3_.refs_4_.refs_5_), channel_id=1, source_target_pairs={{0,1},{1,0},{2,3},{3,2},{4,5},{5,4},{6,7},{7,6},{8,9},{9,8},{10,11... | collective-permute-start | bytes 786440 | tf_op jit(solution)/shard_map/ppermute | solution.py:385
  17.7 6.4 %collective-permute-start.6 = (bf16[16,8192]{1,0:T(8,128)(2,1)S(1)}, bf16[16,8192]{1,0:T(8,128)(2,1)S(1)}, u32[]{:S(2)}, u32[]{:S(2)}) collective-permute-start(bf16[16,8192]{1,0:T(8,128)(2,1)S(1)} %collective-permute-done.4.refs_4_.refs_5_.refs_6_), channel_id=1, source_target_pairs={{0,4},{1,3},{4,8},{5,1},{8,12},{9,5},{12,14},{13,9},{14,10},{15,13... | collective-permute-start | bytes 786440 | tf_op jit(solution)/shard_map/ppermute | solution.py:382
  20.5 6.4 %collective-permute-start.7 = (bf16[16,8192]{1,0:T(8,128)(2,1)S(1)}, bf16[16,8192]{1,0:T(8,128)(2,1)S(1)}, u32[]{:S(2)}, u32[]{:S(2)}) collective-permute-start(bf16[16,8192]{1,0:T(8,128)(2,1)S(1)} %collective-permute-done.5.refs_5_.refs_6_.refs_7_), channel_id=1, source_target_pairs={{0,4},{1,3},{4,8},{5,1},{8,12},{9,5},{12,14},{13,9},{14,10},{15,13... | collective-permute-start | bytes 786440 | tf_op jit(solution)/shard_map/ppermute | solution.py:382
  22.5 4.4 %collective-permute-start.11 = (bf16[16,8192]{1,0:T(8,128)(2,1)S(1)}, bf16[16,8192]{1,0:T(8,128)(2,1)S(1)}, u32[]{:S(2)}, u32[]{:S(2)}) collective-permute-start(bf16[16,8192]{1,0:T(8,128)(2,1)S(1)} %collective-permute-done.4.refs_4_.refs_5_.refs_6_), channel_id=1, source_target_pairs={{0,1},{1,0},{2,3},{3,2},{4,5},{5,4},{6,7},{7,6},{8,9},{9,8},{10,11... | collective-permute-start | bytes 786440 | tf_op jit(solution)/shard_map/ppermute | solution.py:385
  22.5 4.4 %collective-permute-start.12 = (bf16[16,8192]{1,0:T(8,128)(2,1)S(1)}, bf16[16,8192]{1,0:T(8,128)(2,1)S(1)}, u32[]{:S(2)}, u32[]{:S(2)}) collective-permute-start(bf16[16,8192]{1,0:T(8,128)(2,1)S(1)} %collective-permute-done.5.refs_5_.refs_6_.refs_7_), channel_id=1, source_target_pairs={{0,1},{1,0},{2,3},{3,2},{4,5},{5,4},{6,7},{7,6},{8,9},{9,8},{10,11... | collective-permute-start | bytes 786440 | tf_op jit(solution)/shard_map/ppermute | solution.py:385
  24.1 2.8 %collective-permute-start.13 = (bf16[16,8192]{1,0:T(8,128)(2,1)S(1)}, bf16[16,8192]{1,0:T(8,128)(2,1)S(1)}, u32[]{:S(2)}, u32[]{:S(2)}) collective-permute-start(bf16[16,8192]{1,0:T(8,128)(2,1)S(1)} %collective-permute-done.6.refs_6_.refs_7_.refs_8_), channel_id=1, source_target_pairs={{0,1},{1,0},{2,3},{3,2},{4,5},{5,4},{6,7},{7,6},{8,9},{9,8},{10,11... | collective-permute-start | bytes 786440 | tf_op jit(solution)/shard_map/ppermute | solution.py:385
  26.9 1.8 %collective-permute-start.14 = (bf16[16,8192]{1,0:T(8,128)(2,1)S(1)}, bf16[16,8192]{1,0:T(8,128)(2,1)S(1)}, u32[]{:S(2)}, u32[]{:S(2)}) collective-permute-start(bf16[16,8192]{1,0:T(8,128)(2,1)S(1)} %collective-permute-done.7.refs_7_.refs_8_.refs_9_), channel_id=1, source_target_pairs={{0,1},{1,0},{2,3},{3,2},{4,5},{5,4},{6,7},{7,6},{8,9},{9,8},{10,11... | collective-permute-start | bytes 786440 | tf_op jit(solution)/shard_map/ppermute | solution.py:385
  28.1 2.5 %collective-permute-start.16 = (bf16[16,256]{1,0:T(8,128)(2,1)S(1)}, bf16[16,256]{1,0:T(8,128)(2,1)S(1)}, u32[]{:S(2)}, u32[]{:S(2)}) collective-permute-start(bf16[16,256]{1,0:T(8,128)(2,1)S(1)} %get-tuple-element.32.refs_16_), channel_id=1, source_target_pairs={{0,1},{1,0},{2,3},{3,2},{4,5},{5,4},{6,7},{7,6},{8,9},{9,8},{10,11... | collective-permute-start | bytes 24584 | tf_op jit(solution)/shard_map/ppermute | solution.py:385
  28.7 7.7 %slice-start.4 = ((s8[14680064]{0:T(1024)(128)(4,1)}), s8[4194304]{0:T(1024)(128)(4,1)S(1)}, s32[]{:S(2)}) async-start(s8[14680064]{0:T(1024)(128)(4,1)} %bitcast.9), calls=%async_computation.4 | async-start | bytes 8388608
  28.7 7.7 %slice-start.5 = ((s8[14680064]{0:T(1024)(128)(4,1)}), s8[4194304]{0:T(1024)(128)(4,1)S(1)}, s32[]{:S(2)}) async-start(s8[14680064]{0:T(1024)(128)(4,1)} %bitcast.9), calls=%async_computation.5 | async-start | bytes 8388608
  30.7 5.7 %slice-start.6 = ((s8[14680064]{0:T(1024)(128)(4,1)}), s8[4194304]{0:T(1024)(128)(4,1)S(1)}, s32[]{:S(2)}) async-start(s8[14680064]{0:T(1024)(128)(4,1)} %bitcast.9), calls=%async_computation.6 | async-start | bytes 8388608
  30.7 5.7 %slice-start.7 = ((s8[14680064]{0:T(1024)(128)(4,1)}), s8[2097152]{0:T(1024)(128)(4,1)S(1)}, s32[]{:S(2)}) async-start(s8[14680064]{0:T(1024)(128)(4,1)} %bitcast.9), calls=%async_computation.7 | async-start | bytes 4194304
  30.7 4.0 %collective-permute-start.17 = (bf16[16,256]{1,0:T(8,128)(2,1)S(1)}, bf16[16,256]{1,0:T(8,128)(2,1)S(1)}, u32[]{:S(2)}, u32[]{:S(2)}) collective-permute-start(bf16[16,256]{1,0:T(8,128)(2,1)S(1)} %add.3), channel_id=1, source_target_pairs={{0,2},{1,3},{2,0},{3,1},{4,6},{5,7},{6,4},{7,5},{8,10},{9,11},{10,... | collective-permute-start | bytes 24584 | tf_op jit(solution)/shard_map/ppermute | solution.py:385
  34.7 4.1 %collective-permute-start.18 = (bf16[32,256]{1,0:T(8,128)(2,1)S(1)}, bf16[32,256]{1,0:T(8,128)(2,1)S(1)}, u32[]{:S(2)}, u32[]{:S(2)}) collective-permute-start(bf16[32,256]{1,0:T(8,128)(2,1)S(1)} %pad_maximum_fusion.2), channel_id=1, source_target_pairs={{0,4},{1,5},{2,6},{3,7},{4,0},{5,1},{6,2},{7,3},{8,12},{9,13},{10,... | collective-permute-start | bytes 49160 | tf_op jit(solution)/shard_map/ppermute | solution.py:385
  36.4 8.2 %slice-start = ((s8[14680064]{0:T(1024)(128)(4,1)}), s8[4194304]{0:T(1024)(128)(4,1)S(1)}, s32[]{:S(2)}) async-start(s8[14680064]{0:T(1024)(128)(4,1)} %bitcast.3), calls=%async_computation | async-start | bytes 8388608
  36.5 8.2 %slice-start.1 = ((s8[14680064]{0:T(1024)(128)(4,1)}), s8[4194304]{0:T(1024)(128)(4,1)S(1)}, s32[]{:S(2)}) async-start(s8[14680064]{0:T(1024)(128)(4,1)} %bitcast.3), calls=%async_computation.1 | async-start | bytes 8388608
  38.8 5.0 %collective-permute-start.19 = (bf16[64,256]{1,0:T(8,128)(2,1)S(1)}, bf16[64,256]{1,0:T(8,128)(2,1)S(1)}, u32[]{:S(2)}, u32[]{:S(2)}) collective-permute-start(bf16[64,256]{1,0:T(8,128)(2,1)S(1)} %pad_maximum_fusion.1), channel_id=1, source_target_pairs={{0,8},{1,9},{2,10},{3,11},{4,12},{5,13},{6,14},{7,15},{8,0},{9,1},... | collective-permute-start | bytes 98312 | tf_op jit(solution)/shard_map/ppermute | solution.py:385
  41.5 3.2 %slice-start.2 = ((s8[14680064]{0:T(1024)(128)(4,1)}), s8[4194304]{0:T(1024)(128)(4,1)S(1)}, s32[]{:S(2)}) async-start(s8[14680064]{0:T(1024)(128)(4,1)} %bitcast.3), calls=%async_computation.2 | async-start | bytes 8388608
  41.5 3.2 %slice-start.3 = ((s8[14680064]{0:T(1024)(128)(4,1)}), s8[2097152]{0:T(1024)(128)(4,1)S(1)}, s32[]{:S(2)}) async-start(s8[14680064]{0:T(1024)(128)(4,1)} %bitcast.3), calls=%async_computation.3 | async-start | bytes 4194304
  43.8 33.8 %copy-start.2 = (s32[2]{0:T(128)S(1)}, s32[2]{0:T(128)}, u32[]{:S(2)}) copy-start(s32[2]{0:T(128)} %param.15) | copy-start | bytes 28
  49.2 3.7 %collective-permute-start.23 = (bf16[32,8192]{1,0:T(8,128)(2,1)S(1)}, bf16[32,8192]{1,0:T(8,128)(2,1)S(1)}, u32[]{:S(2)}, u32[]{:S(2)}) collective-permute-start(bf16[32,8192]{1,0:T(8,128)(2,1)S(1)} %get-tuple-element.49), channel_id=1, source_target_pairs={{0,1},{1,0},{2,3},{3,2},{4,5},{5,4},{6,7},{7,6},{8,9},{9,8},{10,11... | collective-permute-start | bytes 1572872 | tf_op jit(solution)/shard_map/ppermute | solution.py:385
  49.3 2.3 %collective-permute-start.24 = (bf16[16,8192]{1,0:T(8,128)(2,1)S(1)}, bf16[16,8192]{1,0:T(8,128)(2,1)S(1)}, u32[]{:S(2)}, u32[]{:S(2)}) collective-permute-start(bf16[16,8192]{1,0:T(8,128)(2,1)S(1)} %get-tuple-element.51), channel_id=1, source_target_pairs={{0,1},{1,0},{2,3},{3,2},{4,5},{5,4},{6,7},{7,6},{8,9},{9,8},{10,11... | collective-permute-start | bytes 786440 | tf_op jit(solution)/shard_map/ppermute | solution.py:385
  49.8 9.7 %collective-permute-start.22 = (bf16[32,8192]{1,0:T(8,128)(2,1)S(1)}, bf16[32,8192]{1,0:T(8,128)(2,1)S(1)}, u32[]{:S(2)}, u32[]{:S(2)}) collective-permute-start(bf16[32,8192]{1,0:T(8,128)(2,1)S(1)} %get-tuple-element.47), channel_id=1, source_target_pairs={{0,1},{1,0},{2,3},{3,2},{4,5},{5,4},{6,7},{7,6},{8,9},{9,8},{10,11... | collective-permute-start | bytes 1572872 | tf_op jit(solution)/shard_map/ppermute | solution.py:385
  51.6 6.4 %collective-permute-start.25 = (bf16[16,8192]{1,0:T(8,128)(2,1)S(1)}, bf16[16,8192]{1,0:T(8,128)(2,1)S(1)}, u32[]{:S(2)}, u32[]{:S(2)}) collective-permute-start(bf16[16,8192]{1,0:T(8,128)(2,1)S(1)} %added.7), channel_id=1, source_target_pairs={{0,4},{1,3},{4,8},{5,1},{8,12},{9,5},{12,14},{13,9},{14,10},{15,13... | collective-permute-start | bytes 786440 | tf_op jit(solution)/shard_map/ppermute | solution.py:382
  53.0 7.8 %collective-permute-start.29 = (bf16[16,8192]{1,0:T(8,128)(2,1)S(1)}, bf16[16,8192]{1,0:T(8,128)(2,1)S(1)}, u32[]{:S(2)}, u32[]{:S(2)}) collective-permute-start(bf16[16,8192]{1,0:T(8,128)(2,1)S(1)} %added.11), channel_id=1, source_target_pairs={{0,4},{1,3},{4,8},{5,1},{8,12},{9,5},{12,14},{13,9},{14,10},{15,13... | collective-permute-start | bytes 786440 | tf_op jit(solution)/shard_map/ppermute | solution.py:382
  54.9 11.1 %collective-permute-start.21 = (bf16[32,8192]{1,0:T(8,128)(2,1)S(1)}, bf16[32,8192]{1,0:T(8,128)(2,1)S(1)}, u32[]{:S(2)}, u32[]{:S(2)}) collective-permute-start(bf16[32,8192]{1,0:T(8,128)(2,1)S(1)} %get-tuple-element.45), channel_id=1, source_target_pairs={{0,1},{1,0},{2,3},{3,2},{4,5},{5,4},{6,7},{7,6},{8,9},{9,8},{10,11... | collective-permute-start | bytes 1572872 | tf_op jit(solution)/shard_map/ppermute | solution.py:385
  58.2 6.4 %collective-permute-start.26 = (bf16[16,8192]{1,0:T(8,128)(2,1)S(1)}, bf16[16,8192]{1,0:T(8,128)(2,1)S(1)}, u32[]{:S(2)}, u32[]{:S(2)}) collective-permute-start(bf16[16,8192]{1,0:T(8,128)(2,1)S(1)} %added.8), channel_id=1, source_target_pairs={{0,4},{1,3},{4,8},{5,1},{8,12},{9,5},{12,14},{13,9},{14,10},{15,13... | collective-permute-start | bytes 786440 | tf_op jit(solution)/shard_map/ppermute | solution.py:382
  61.0 6.4 %collective-permute-start.30 = (bf16[16,8192]{1,0:T(8,128)(2,1)S(1)}, bf16[16,8192]{1,0:T(8,128)(2,1)S(1)}, u32[]{:S(2)}, u32[]{:S(2)}) collective-permute-start(bf16[16,8192]{1,0:T(8,128)(2,1)S(1)} %added.12), channel_id=1, source_target_pairs={{0,4},{1,3},{4,8},{5,1},{8,12},{9,5},{12,14},{13,9},{14,10},{15,13... | collective-permute-start | bytes 786440 | tf_op jit(solution)/shard_map/ppermute | solution.py:382
  64.7 6.4 %collective-permute-start.27 = (bf16[16,8192]{1,0:T(8,128)(2,1)S(1)}, bf16[16,8192]{1,0:T(8,128)(2,1)S(1)}, u32[]{:S(2)}, u32[]{:S(2)}) collective-permute-start(bf16[16,8192]{1,0:T(8,128)(2,1)S(1)} %added.9), channel_id=1, source_target_pairs={{0,4},{1,3},{4,8},{5,1},{8,12},{9,5},{12,14},{13,9},{14,10},{15,13... | collective-permute-start | bytes 786440 | tf_op jit(solution)/shard_map/ppermute | solution.py:382
  67.5 6.4 %collective-permute-start.31 = (bf16[16,8192]{1,0:T(8,128)(2,1)S(1)}, bf16[16,8192]{1,0:T(8,128)(2,1)S(1)}, u32[]{:S(2)}, u32[]{:S(2)}) collective-permute-start(bf16[16,8192]{1,0:T(8,128)(2,1)S(1)} %added.13), channel_id=1, source_target_pairs={{0,4},{1,3},{4,8},{5,1},{8,12},{9,5},{12,14},{13,9},{14,10},{15,13... | collective-permute-start | bytes 786440 | tf_op jit(solution)/shard_map/ppermute | solution.py:382
  68.8 5.1 %collective-permute-start.20 = (bf16[16,8192]{1,0:T(8,128)(2,1)S(1)}, bf16[16,8192]{1,0:T(8,128)(2,1)S(1)}, u32[]{:S(2)}, u32[]{:S(2)}) collective-permute-start(bf16[16,8192]{1,0:T(8,128)(2,1)S(1)} %get-tuple-element.43), channel_id=1, source_target_pairs={{0,1},{1,0},{2,3},{3,2},{4,5},{5,4},{6,7},{7,6},{8,9},{9,8},{10,11... | collective-permute-start | bytes 786440 | tf_op jit(solution)/shard_map/ppermute | solution.py:385
  71.2 6.4 %collective-permute-start.28 = (bf16[16,8192]{1,0:T(8,128)(2,1)S(1)}, bf16[16,8192]{1,0:T(8,128)(2,1)S(1)}, u32[]{:S(2)}, u32[]{:S(2)}) collective-permute-start(bf16[16,8192]{1,0:T(8,128)(2,1)S(1)} %added.10), channel_id=1, source_target_pairs={{0,4},{1,3},{4,8},{5,1},{8,12},{9,5},{12,14},{13,9},{14,10},{15,13... | collective-permute-start | bytes 786440 | tf_op jit(solution)/shard_map/ppermute | solution.py:382
  73.9 3.7 %collective-permute-start.32 = (bf16[16,8192]{1,0:T(8,128)(2,1)S(1)}, bf16[16,8192]{1,0:T(8,128)(2,1)S(1)}, u32[]{:S(2)}, u32[]{:S(2)}) collective-permute-start(bf16[16,8192]{1,0:T(8,128)(2,1)S(1)} %collective-permute-done.31), channel_id=1, source_target_pairs={{0,1},{1,0},{2,3},{3,2},{4,5},{5,4},{6,7},{7,6},{8,9},{9,8},{10,11... | collective-permute-start | bytes 786440 | tf_op jit(solution)/shard_map/ppermute | solution.py:385

commit v14 on v13

--- a/solution.py
+++ b/solution.py
@@ -114,20 +114,14 @@
     )(far(tokens), passed)
 
 
-def rank_kernel(members, numbers, ids_ref, expand_ref, own_ref, other_ref, *refs):
-    pieces, (out_ref, chosen_ref, scratch, sems) = refs[: len(numbers)], refs[-4:]
+def rank_kernel(members, numbers, ids_ref, own_ref, other_ref, *refs):
+    pieces, (out_ref, scratch) = refs[: len(numbers)], refs[-2:]
     rows = pieces[0].shape[0]
     blocks, span = ids_ref.shape[1], own_ref.shape[1]
     block_rows = members * rows // blocks
     device = lax.axis_index("tp")
     places = arrivals(device, members, rows)
     ids = [picked(ids_ref, b) for b in range(blocks)]
-    copies = [
-        pltpu.make_async_copy(expand_ref.at[ids[b]], chosen_ref.at[b], sems.at[b])
-        for b in range(blocks)
-    ]
-    for copy in copies:
-        copy.start()
     weights = jnp.concatenate([ref[i] for ref in (own_ref, other_ref) for i in ids], axis=0)
     wanted = weights.shape[0]
     slices = max(1, 256 // wanted)
@@ -155,36 +149,36 @@
     out_ref[...] = jnp.concatenate(
         [jnp.where(lower, own, other), jnp.where(lower, other, own)], axis=0
     ).astype(BF16)
-    for copy in copies:
-        copy.wait()
-
-
-def rank_of(adapters, members, numbers, pieces, shrink, other, expand, after):
+
+
+def rank_of(adapters, members, numbers, pieces, shrink, other, after):
     rows, model = pieces[0].shape
     span = shrink.shape[1]
     total = rows * members
     return pl.pallas_call(
         functools.partial(rank_kernel, members, numbers),
-        in_specs=whole(1) + [FAR] + whole(2 + len(pieces)) + [FAR] * len(after),
-        out_specs=whole(2),
-        out_shape=[
-            jax.ShapeDtypeStruct((2 * span, total), BF16),
-            jax.ShapeDtypeStruct((adapters.shape[1],) + expand.shape[1:], BF16),
-        ],
-        scratch_shapes=[
-            pltpu.VMEM((2, total, 128), F32),
-            pltpu.SemaphoreType.DMA((adapters.shape[1],)),
-        ],
+        in_specs=whole(3 + len(pieces)) + [FAR] * len(after),
+        out_specs=whole(1)[0],
+        out_shape=jax.ShapeDtypeStruct((2 * span, total), BF16),
+        scratch_shapes=[pltpu.VMEM((2, total, 128), F32)],
         compiler_params=params(),
         cost_estimate=cost(2 * total * model * span * 2, 2 * total * model),
         name="rank",
-    )(adapters, far(expand), shrink, other, *pieces, *after)
-
-
-def product_kernel(first, depth, main, role, w_ref, *refs):
-    outs = 1 if role is None else 2
-    refs, outs = refs[:-outs], refs[-outs:]
-    aside, pieces = (refs[:1], refs[1:-1]) if role == 1 else ((), refs[:-1])
+    )(adapters, shrink, other, *pieces, *after)
+
+
+def product_kernel(first, depth, main, role, count, fetch, w_ref, *refs):
+    aside, refs = refs[: role or 0], refs[role or 0 :]
+    pieces, refs = refs[:count], refs[count + 1 :]
+    copies = []
+    if fetch:
+        ids_ref, expand_ref, *refs, chosen_ref, sems = refs
+        for b in range(ids_ref.shape[1]):
+            source = expand_ref.at[picked(ids_ref, b)]
+            copies.append(pltpu.make_async_copy(source, chosen_ref.at[b], sems.at[b]))
+    for copy in copies:
+        copy.start()
+    outs = refs
     rows = pieces[0].shape[0]
     places = arrivals(lax.axis_index("tp"), len(pieces), rows)
     lhs = jnp.concatenate([piece[:, first : first + depth] for piece in pieces], axis=0)
@@ -200,9 +194,11 @@
         outs[1][...] = w_ref[span, main:]
     elif role == 1:
         store(outs[1], jnp.concatenate([w_ref[span, main:], aside[0][...]], axis=1))
-
-
-def product(pieces, matrix, part, parts, after, weight, aside):
+    for copy in copies:
+        copy.wait()
+
+
+def product(pieces, matrix, part, parts, after, weight, aside, fetch=None):
     rows = pieces[0].shape[0]
     total = rows * len(pieces)
     model, width = matrix.shape
@@ -217,15 +213,26 @@
     elif tail:
         role, extra = 1, [aside]
         out_shape.append(jax.ShapeDtypeStruct((total, 2 * tail), F32))
-    return pl.pallas_call(
-        functools.partial(product_kernel, part * depth, depth, main, role),
-        in_specs=whole(len(pieces) + 2 + len(extra)),
+    specs, scratch, fetched = whole(len(pieces) + 2 + len(extra)), [], []
+    if fetch is not None:
+        adapters, expand = fetch
+        blocks = adapters.shape[1]
+        fetched = [adapters, far(expand)]
+        specs += whole(1) + [FAR]
+        out_shape.append(jax.ShapeDtypeStruct((blocks,) + expand.shape[1:], BF16))
+        scratch.append(pltpu.SemaphoreType.DMA((blocks,)))
+    return pl.pallas_call(
+        functools.partial(
+            product_kernel, part * depth, depth, main, role, len(pieces), fetch is not None
+        ),
+        in_specs=specs,
         out_specs=whole(len(out_shape)),
         out_shape=out_shape,
+        scratch_shapes=scratch,
         compiler_params=params(),
         cost_estimate=cost(weight * total * depth * width, 2 * depth * (width + total)),
         name="product",
-    )(matrix, *extra, *pieces, after)
+    )(matrix, *extra, *pieces, after, *fetched)
 
 
 def finish_kernel(span, piece_rows, *refs):
@@ -401,14 +408,13 @@
 
     adapters, counts = adapter_per_block[None], block_token_count[None]
     received = [0] + list(range(2, 2 + len(mine)))
-    rank, expand = rank_of(
+    rank = rank_of(
         adapters,
         members,
         received,
         [pieces[i] for i in received],
         shrink,
         other_shrink,
-        expand_matrices,
         theirs[:-1],
     )
     work = [(gate_matrix, 0), (gate_matrix, 1), (up_matrix, 0), (up_matrix, 1)]
@@ -416,9 +422,12 @@
     while bit < members or work:
         if work:
             matrix, part = work.pop(0)
+            fetch = None if products else (adapters, expand_matrices)
             result, *left = product(
-                pieces, matrix, part, 2, after, WEIGHTS[len(products)], aside[part]
+                pieces, matrix, part, 2, after, WEIGHTS[len(products)], aside[part], fetch
             )
+            if fetch is not None:
+                expand = left.pop()
             aside[part] = left[0] if left else None
             products.append(result)
         if bit < members:

time: 78.8 us -> 80.3 us (1.019)
  Pallas kernels: 18.4 us -> 19.9 us
    pallas_call x4, Pallas kernels: 8.55 us -> 10.1 us  [product(): pl.pallas_call(functools.partial(product_kernel, part * depth, depth, mai...]
  transfers between devices with their start and end apart: 33 -> 33, of which waited for: 15 -> 15; matrix products, arithmetic and copies ran while one was open for 0% -> 0% of each run, Pallas kernels for 15% -> 17%
where the time goes in v14:
time: 80.3 us; the launch traced here: 80.1 us
  starting transfers between devices  32.7 us (41%)
  waiting for transfers between devices  27.2 us (34%)
  Pallas kernels  19.9 us (25%)
    ppermute x14, waiting for transfers between devices, step(): return lax.ppermute(x, 'tp', ring)  25.4 us
    ppermute x14, starting transfers between devices, step(): return lax.ppermute(x, 'tp', ring)  23.5 us
    pallas_call x4, Pallas kernels, product(): pl.pallas_call(functools.partial(product_kernel, part * depth, depth, mai...  10.1 us
    ppermute x19, starting transfers between devices, cross(): return lax.ppermute(x, 'tp', crossing(members, bit))  9.17 us
    pallas_call x1, Pallas kernels, down(): pl.pallas_call(functools.partial(down_kernel, groups, rows, size), in_spe...  4.5 us
    ppermute x19, waiting for transfers between devices, cross(): return lax.ppermute(x, 'tp', crossing(members, bit))  1.74 us
    pallas_call x1, Pallas kernels, anchor(): pl.pallas_call(anchor_kernel, in_specs=[FAR, FAR], out_specs=whole(1) + [...  1.71 us
  transfers between devices with their start and end apart: 33, of which 15 were waited for; matrix products, arithmetic and copies ran while one was open for 0% of the time, Pallas kernels for 17%

profile of v14, /device:TPU:0, one launch (start us, length us, event | category | flops | bytes accessed | tf_op | source)
XLA Modules:
  0.0 80.1 jit_solution(17276850688824529176)
XLA Ops:
  0.0 0.5 collective-permute-start
  0.5 2.6 %collective-permute-start.1 = (bf16[16,8192]{1,0:T(8,128)(2,1)}, bf16[16,8192]{1,0:T(8,128)(2,1)S(1)}, u32[]{:S(2)}, u32[]{:S(2)}) collective-permute-start(bf16[16,8192]{1,0:T(8,128)(2,1)} %tokens_ref.1), channel_id=1, source_target_pairs={{0,4},{1,3},{4,8},{5,1},{8,12},{9,5},{12,14},{13,9},{14,10},{15,13... | collective-permute-start | bytes 786440 | tf_op jit(solution)/shard_map/ppermute | solution.py:389
  3.2 0.0 collective-permute-done.passed_in
  3.2 1.7 %anchor.1 = (bf16[16,8192]{1,0:T(8,128)(2,1)S(1)}, bf16[16,8192]{1,0:T(8,128)(2,1)S(1)}) custom-call(bf16[16,8192]{1,0:T(8,128)(2,1)} %tokens_ref.1, bf16[16,8192]{1,0:T(8,128)(2,1)S(1)} %collective-permute-done.passed_in), custom_call_target="tpu_custom_call", output_to_operand_aliasing={{1}: (1, {})} | custom-call | flops 30000001024 | tf_op jit(solution)/shard_map/anchor/pallas_call | solution.py:104
  4.9 1.7 %collective-permute-start.2 = (bf16[16,8192]{1,0:T(8,128)(2,1)S(1)}, bf16[16,8192]{1,0:T(8,128)(2,1)S(1)}, u32[]{:S(2)}, u32[]{:S(2)}) collective-permute-start(bf16[16,8192]{1,0:T(8,128)(2,1)S(1)} %get-tuple-element.30.refs_1_.refs_2_), channel_id=1, source_target_pairs={{0,4},{1,3},{4,8},{5,1},{8,12},{9,5},{12,14},{13,9},{14,10},{15,13... | collective-permute-start | bytes 786440 | tf_op jit(solution)/shard_map/ppermute | solution.py:389
  6.6 0.0 collective-permute-start.15
  6.6 1.1 %collective-permute-done.1.refs_1_.refs_2_.refs_3_ = bf16[16,8192]{1,0:T(8,128)(2,1)S(1)} collective-permute-done((bf16[16,8192]{1,0:T(8,128)(2,1)}, bf16[16,8192]{1,0:T(8,128)(2,1)S(1)}, u32[]{:S(2)}, u32[]{:S(2)}) %collective-permute-start.1) | collective-permute-done | bytes 262176 | tf_op jit(solution)/shard_map/ppermute | solution.py:389
  7.7 2.1 %collective-permute-start.3 = (bf16[16,8192]{1,0:T(8,128)(2,1)S(1)}, bf16[16,8192]{1,0:T(8,128)(2,1)S(1)}, u32[]{:S(2)}, u32[]{:S(2)}) collective-permute-start(bf16[16,8192]{1,0:T(8,128)(2,1)S(1)} %collective-permute-done.1.refs_1_.refs_2_.refs_3_), channel_id=1, source_target_pairs={{0,4},{1,3},{4,8},{5,1},{8,12},{9,5},{12,14},{13,9},{14,10},{15,13... | collective-permute-start | bytes 786440 | tf_op jit(solution)/shard_map/ppermute | solution.py:389
  9.8 1.6 %collective-permute-done.2.refs_2_.refs_3_.refs_4_ = bf16[16,8192]{1,0:T(8,128)(2,1)S(1)} collective-permute-done((bf16[16,8192]{1,0:T(8,128)(2,1)S(1)}, bf16[16,8192]{1,0:T(8,128)(2,1)S(1)}, u32[]{:S(2)}, u32[]{:S(2)}) %collective-permute-start.2) | collective-permute-done | bytes 262176 | tf_op jit(solution)/shard_map/ppermute | solution.py:389
  11.3 1.7 %collective-permute-start.4 = (bf16[16,8192]{1,0:T(8,128)(2,1)S(1)}, bf16[16,8192]{1,0:T(8,128)(2,1)S(1)}, u32[]{:S(2)}, u32[]{:S(2)}) collective-permute-start(bf16[16,8192]{1,0:T(8,128)(2,1)S(1)} %collective-permute-done.2.refs_2_.refs_3_.refs_4_), channel_id=1, source_target_pairs={{0,4},{1,3},{4,8},{5,1},{8,12},{9,5},{12,14},{13,9},{14,10},{15,13... | collective-permute-start | bytes 786440 | tf_op jit(solution)/shard_map/ppermute | solution.py:389
  13.0 1.1 %collective-permute-done.3.refs_3_.refs_4_.refs_5_ = bf16[16,8192]{1,0:T(8,128)(2,1)S(1)} collective-permute-done((bf16[16,8192]{1,0:T(8,128)(2,1)S(1)}, bf16[16,8192]{1,0:T(8,128)(2,1)S(1)}, u32[]{:S(2)}, u32[]{:S(2)}) %collective-permute-start.3) | collective-permute-done | bytes 262176 | tf_op jit(solution)/shard_map/ppermute | solution.py:389
  14.1 2.0 %collective-permute-start.5 = (bf16[16,8192]{1,0:T(8,128)(2,1)S(1)}, bf16[16,8192]{1,0:T(8,128)(2,1)S(1)}, u32[]{:S(2)}, u32[]{:S(2)}) collective-permute-start(bf16[16,8192]{1,0:T(8,128)(2,1)S(1)} %collective-permute-done.3.refs_3_.refs_4_.refs_5_), channel_id=1, source_target_pairs={{0,4},{1,3},{4,8},{5,1},{8,12},{9,5},{12,14},{13,9},{14,10},{15,13... | collective-permute-start | bytes 786440 | tf_op jit(solution)/shard_map/ppermute | solution.py:389
  16.1 0.0 collective-permute-start.9
  16.1 0.0 collective-permute-done.8.refs_8_.refs_9_.refs_10_
  16.1 0.5 collective-permute-start.10
  16.6 1.1 %collective-permute-done.4.refs_4_.refs_5_.refs_6_ = bf16[16,8192]{1,0:T(8,128)(2,1)S(1)} collective-permute-done((bf16[16,8192]{1,0:T(8,128)(2,1)S(1)}, bf16[16,8192]{1,0:T(8,128)(2,1)S(1)}, u32[]{:S(2)}, u32[]{:S(2)}) %collective-permute-start.4) | collective-permute-done | bytes 262176 | tf_op jit(solution)/shard_map/ppermute | solution.py:389
  17.7 1.7 %collective-permute-start.6 = (bf16[16,8192]{1,0:T(8,128)(2,1)S(1)}, bf16[16,8192]{1,0:T(8,128)(2,1)S(1)}, u32[]{:S(2)}, u32[]{:S(2)}) collective-permute-start(bf16[16,8192]{1,0:T(8,128)(2,1)S(1)} %collective-permute-done.4.refs_4_.refs_5_.refs_6_), channel_id=1, source_target_pairs={{0,4},{1,3},{4,8},{5,1},{8,12},{9,5},{12,14},{13,9},{14,10},{15,13... | collective-permute-start | bytes 786440 | tf_op jit(solution)/shard_map/ppermute | solution.py:389
  19.4 1.1 %collective-permute-done.5.refs_5_.refs_6_.refs_7_ = bf16[16,8192]{1,0:T(8,128)(2,1)S(1)} collective-permute-done((bf16[16,8192]{1,0:T(8,128)(2,1)S(1)}, bf16[16,8192]{1,0:T(8,128)(2,1)S(1)}, u32[]{:S(2)}, u32[]{:S(2)}) %collective-permute-start.5) | collective-permute-done | bytes 262176 | tf_op jit(solution)/shard_map/ppermute | solution.py:389
  20.5 2.0 %collective-permute-start.7 = (bf16[16,8192]{1,0:T(8,128)(2,1)S(1)}, bf16[16,8192]{1,0:T(8,128)(2,1)S(1)}, u32[]{:S(2)}, u32[]{:S(2)}) collective-permute-start(bf16[16,8192]{1,0:T(8,128)(2,1)S(1)} %collective-permute-done.5.refs_5_.refs_6_.refs_7_), channel_id=1, source_target_pairs={{0,4},{1,3},{4,8},{5,1},{8,12},{9,5},{12,14},{13,9},{14,10},{15,13... | collective-permute-start | bytes 786440 | tf_op jit(solution)/shard_map/ppermute | solution.py:389
  22.5 0.0 collective-permute-done.9.refs_9_.refs_10_.refs_11_
  22.5 0.5 collective-permute-start.12
  23.0 1.0 %collective-permute-done.6.refs_6_.refs_7_.refs_8_ = bf16[16,8192]{1,0:T(8,128)(2,1)S(1)} collective-permute-done((bf16[16,8192]{1,0:T(8,128)(2,1)S(1)}, bf16[16,8192]{1,0:T(8,128)(2,1)S(1)}, u32[]{:S(2)}, u32[]{:S(2)}) %collective-permute-start.6) | collective-permute-done | bytes 262176 | tf_op jit(solution)/shard_map/ppermute | solution.py:389
  24.1 2.8 %collective-permute-done.7.refs_7_.refs_8_.refs_9_ = bf16[16,8192]{1,0:T(8,128)(2,1)S(1)} collective-permute-done((bf16[16,8192]{1,0:T(8,128)(2,1)S(1)}, bf16[16,8192]{1,0:T(8,128)(2,1)S(1)}, u32[]{:S(2)}, u32[]{:S(2)}) %collective-permute-start.7) | collective-permute-done | bytes 262176 | tf_op jit(solution)/shard_map/ppermute | solution.py:389
  26.9 1.2 %rank.1.refs_16_ = bf16[16,256]{1,0:T(8,128)(2,1)S(1)} custom-call(s32[1,2]{1,0:T(1,128)S(1)} %bitcast.7, bf16[8,8,8192]{2,1,0:T(8,128)(2,1)S(1)} %bitcast.6, bf16[8,8,8192]{2,1,0:T(8,128)(2,1)S(1)} %collective-permute-done.15.other_ref, bf16[16,8192]{1,0:T(8,128)(2,1)S(1)} %get-tuple-element.29.refs_0_.refs_1_, ...), custom_call_target="tpu_custom_call" | custom-call | flops 67108864 | bytes 4194304 | tf_op jit(solution)/shard_map/rank/pallas_call | solution.py:158
  28.1 0.5 collective-permute-start.16
  28.6 3.5 %product.4 = (f32[256,768]{1,0:T(8,128)S(1)}, bf16[4096,128]{1,0:T(8,128)(2,1)S(1)}, bf16[2,128,896]{2,1,0:T(8,128)(2,1)S(1)}) custom-call(bf16[8192,896]{1,0:T(8,128)(2,1)S(1)} %copy-done.3, bf16[16,8192]{1,0:T(8,128)(2,1)S(1)} %get-tuple-element.29.refs_0_.refs_1_, bf16[16,8192]{1,0:T(8,128)(2,1)S(1)} %get-tuple-element.30.refs_1_.refs_2_, ...), custom_call_target="tpu_custom_call" | custom-call | flops 5637144576 | bytes 9437184 | tf_op jit(solution)/shard_map/product/pallas_call | solution.py:224
  32.2 0.0 slice-start.6
  32.2 2.0 %collective-permute-start.17 = (bf16[16,256]{1,0:T(8,128)(2,1)S(1)}, bf16[16,256]{1,0:T(8,128)(2,1)S(1)}, u32[]{:S(2)}, u32[]{:S(2)}) collective-permute-start(bf16[16,256]{1,0:T(8,128)(2,1)S(1)} %add.3), channel_id=1, source_target_pairs={{0,2},{1,3},{2,0},{3,1},{4,6},{5,7},{6,4},{7,5},{8,10},{9,11},{10,... | collective-permute-start | bytes 24584 | tf_op jit(solution)/shard_map/ppermute | solution.py:392
  34.2 1.9 %product.5 = (f32[256,768]{1,0:T(8,128)S(1)}, bf16[4096,128]{1,0:T(8,128)(2,1)S(1)}) custom-call(bf16[8192,896]{1,0:T(8,128)(2,1)S(1)} %copy-done.3, bf16[16,8192]{1,0:T(8,128)(2,1)S(1)} %get-tuple-element.29.refs_0_.refs_1_, bf16[16,8192]{1,0:T(8,128)(2,1)S(1)} %get-tuple-element.30.refs_1_.refs_2_, ...), custom_call_target="tpu_custom_call" | custom-call | flops 5637144576 | bytes 9437184 | tf_op jit(solution)/shard_map/product/pallas_call | solution.py:224
  36.1 1.8 %collective-permute-start.18 = (bf16[32,256]{1,0:T(8,128)(2,1)S(1)}, bf16[32,256]{1,0:T(8,128)(2,1)S(1)}, u32[]{:S(2)}, u32[]{:S(2)}) collective-permute-start(bf16[32,256]{1,0:T(8,128)(2,1)S(1)} %pad_maximum_fusion.2), channel_id=1, source_target_pairs={{0,4},{1,5},{2,6},{3,7},{4,0},{5,1},{6,2},{7,3},{8,12},{9,13},{10,... | collective-permute-start | bytes 49160 | tf_op jit(solution)/shard_map/ppermute | solution.py:392
  37.9 0.0 slice-start
  37.9 0.0 slice-start.1
  38.0 2.3 %product.6 = (f32[256,768]{1,0:T(8,128)S(1)}, f32[256,256]{1,0:T(8,128)S(1)}) custom-call(bf16[8192,896]{1,0:T(8,128)(2,1)S(1)} %bitcast.11, bf16[4096,128]{1,0:T(8,128)(2,1)S(1)} %get-tuple-element.33.refs_0_, bf16[16,8192]{1,0:T(8,128)(2,1)S(1)} %get-tuple-element.29.refs_0_.refs_1_, bf16[16,8192]{1,0:T(8,128)(2,1)S(1)} %get-tuple-element.30.refs_1_.refs_2_, ...), custom_call_target="tpu_custom_call" | custom-call | flops 5637144576 | bytes 9437184 | tf_op jit(solution)/shard_map/product/pallas_call | solution.py:224
  40.3 2.7 %collective-permute-start.19 = (bf16[64,256]{1,0:T(8,128)(2,1)S(1)}, bf16[64,256]{1,0:T(8,128)(2,1)S(1)}, u32[]{:S(2)}, u32[]{:S(2)}) collective-permute-start(bf16[64,256]{1,0:T(8,128)(2,1)S(1)} %pad_maximum_fusion.1), channel_id=1, source_target_pairs={{0,8},{1,9},{2,10},{3,11},{4,12},{5,13},{6,14},{7,15},{8,0},{9,1},... | collective-permute-start | bytes 98312 | tf_op jit(solution)/shard_map/ppermute | solution.py:392
  43.0 2.3 %product.7 = (f32[256,768]{1,0:T(8,128)S(1)}, f32[256,256]{1,0:T(8,128)S(1)}) custom-call(bf16[8192,896]{1,0:T(8,128)(2,1)S(1)} %bitcast.11, bf16[4096,128]{1,0:T(8,128)(2,1)S(1)} %get-tuple-element.35.refs_0_, bf16[16,8192]{1,0:T(8,128)(2,1)S(1)} %get-tuple-element.29.refs_0_.refs_1_, bf16[16,8192]{1,0:T(8,128)(2,1)S(1)} %get-tuple-element.30.refs_1_.refs_2_, ...), custom_call_target="tpu_custom_call" | custom-call | flops 5637144576 | bytes 9437184 | tf_op jit(solution)/shard_map/product/pallas_call | solution.py:224
  45.3 0.0 copy-start.2
  45.3 0.8 finish.1.hidden_ref
  46.2 4.5 %down.1 = (bf16[16,8192]{1,0:T(8,128)(2,1)S(1)}, bf16[16,8192]{1,0:T(8,128)(2,1)S(1)}, bf16[16,8192]{1,0:T(8,128)(2,1)S(1)}, bf16[16,8192]{1,0:T(8,128)(2,1)S(1)...) custom-call(bf16[896,8192]{1,0:T(8,128)(2,1)S(1)} %bitcast.4, ...), custom_call_target="tpu_custom_call" | custom-call | flops 3758096384 | bytes 18874368 | tf_op jit(solution)/shard_map/down/pallas_call | solution.py:305
  50.7 0.1 collective-permute-start.23
  50.8 0.5 collective-permute-start.24
  51.3 0.1 collective-permute-start.22
  51.4 1.7 %collective-permute-done.24.refs_1_ = bf16[16,8192]{1,0:T(8,128)(2,1)S(1)} collective-permute-done((bf16[16,8192]{1,0:T(8,128)(2,1)S(1)}, bf16[16,8192]{1,0:T(8,128)(2,1)S(1)}, u32[]{:S(2)}, u32[]{:S(2)}) %collective-permute-start.24) | collective-permute-done | bytes 262176 | tf_op jit(solution)/shard_map/ppermute | solution.py:392
  53.1 0.1 added.7
  53.1 1.3 %collective-permute-start.25 = (bf16[16,8192]{1,0:T(8,128)(2,1)S(1)}, bf16[16,8192]{1,0:T(8,128)(2,1)S(1)}, u32[]{:S(2)}, u32[]{:S(2)}) collective-permute-start(bf16[16,8192]{1,0:T(8,128)(2,1)S(1)} %added.7), channel_id=1, source_target_pairs={{0,4},{1,3},{4,8},{5,1},{8,12},{9,5},{12,14},{13,9},{14,10},{15,13... | collective-permute-start | bytes 786440 | tf_op jit(solution)/shard_map/ppermute | solution.py:389
  54.4 0.1 added.11
  54.5 1.9 %collective-permute-start.29 = (bf16[16,8192]{1,0:T(8,128)(2,1)S(1)}, bf16[16,8192]{1,0:T(8,128)(2,1)S(1)}, u32[]{:S(2)}, u32[]{:S(2)}) collective-permute-start(bf16[16,8192]{1,0:T(8,128)(2,1)S(1)} %added.11), channel_id=1, source_target_pairs={{0,4},{1,3},{4,8},{5,1},{8,12},{9,5},{12,14},{13,9},{14,10},{15,13... | collective-permute-start | bytes 786440 | tf_op jit(solution)/shard_map/ppermute | solution.py:389
  56.4 3.1 %collective-permute-done.25.refs_2_ = bf16[16,8192]{1,0:T(8,128)(2,1)S(1)} collective-permute-done((bf16[16,8192]{1,0:T(8,128)(2,1)S(1)}, bf16[16,8192]{1,0:T(8,128)(2,1)S(1)}, u32[]{:S(2)}, u32[]{:S(2)}) %collective-permute-start.25) | collective-permute-done | bytes 262176 | tf_op jit(solution)/shard_map/ppermute | solution.py:389
  59.5 0.1 added.8
  59.6 1.3 %collective-permute-start.26 = (bf16[16,8192]{1,0:T(8,128)(2,1)S(1)}, bf16[16,8192]{1,0:T(8,128)(2,1)S(1)}, u32[]{:S(2)}, u32[]{:S(2)}) collective-permute-start(bf16[16,8192]{1,0:T(8,128)(2,1)S(1)} %added.8), channel_id=1, source_target_pairs={{0,4},{1,3},{4,8},{5,1},{8,12},{9,5},{12,14},{13,9},{14,10},{15,13... | collective-permute-start | bytes 786440 | tf_op jit(solution)/shard_map/ppermute | solution.py:389
  61.0 1.4 %collective-permute-done.29.refs_2_ = bf16[16,8192]{1,0:T(8,128)(2,1)S(1)} collective-permute-done((bf16[16,8192]{1,0:T(8,128)(2,1)S(1)}, bf16[16,8192]{1,0:T(8,128)(2,1)S(1)}, u32[]{:S(2)}, u32[]{:S(2)}) %collective-permute-start.29) | collective-permute-done | bytes 262176 | tf_op jit(solution)/shard_map/ppermute | solution.py:389
  62.4 0.1 added.12
  62.5 1.3 %collective-permute-start.30 = (bf16[16,8192]{1,0:T(8,128)(2,1)S(1)}, bf16[16,8192]{1,0:T(8,128)(2,1)S(1)}, u32[]{:S(2)}, u32[]{:S(2)}) collective-permute-start(bf16[16,8192]{1,0:T(8,128)(2,1)S(1)} %added.12), channel_id=1, source_target_pairs={{0,4},{1,3},{4,8},{5,1},{8,12},{9,5},{12,14},{13,9},{14,10},{15,13... | collective-permute-start | bytes 786440 | tf_op jit(solution)/shard_map/ppermute | solution.py:389
  63.8 2.3 %collective-permute-done.26.refs_2_ = bf16[16,8192]{1,0:T(8,128)(2,1)S(1)} collective-permute-done((bf16[16,8192]{1,0:T(8,128)(2,1)S(1)}, bf16[16,8192]{1,0:T(8,128)(2,1)S(1)}, u32[]{:S(2)}, u32[]{:S(2)}) %collective-permute-start.26) | collective-permute-done | bytes 262176 | tf_op jit(solution)/shard_map/ppermute | solution.py:389
  66.1 0.1 added.9
  66.2 1.3 %collective-permute-start.27 = (bf16[16,8192]{1,0:T(8,128)(2,1)S(1)}, bf16[16,8192]{1,0:T(8,128)(2,1)S(1)}, u32[]{:S(2)}, u32[]{:S(2)}) collective-permute-start(bf16[16,8192]{1,0:T(8,128)(2,1)S(1)} %added.9), channel_id=1, source_target_pairs={{0,4},{1,3},{4,8},{5,1},{8,12},{9,5},{12,14},{13,9},{14,10},{15,13... | collective-permute-start | bytes 786440 | tf_op jit(solution)/shard_map/ppermute | solution.py:389
  67.5 1.4 %collective-permute-done.30.refs_2_ = bf16[16,8192]{1,0:T(8,128)(2,1)S(1)} collective-permute-done((bf16[16,8192]{1,0:T(8,128)(2,1)S(1)}, bf16[16,8192]{1,0:T(8,128)(2,1)S(1)}, u32[]{:S(2)}, u32[]{:S(2)}) %collective-permute-start.30) | collective-permute-done | bytes 262176 | tf_op jit(solution)/shard_map/ppermute | solution.py:389
  68.9 0.1 added.13
  69.0 1.3 %collective-permute-start.31 = (bf16[16,8192]{1,0:T(8,128)(2,1)S(1)}, bf16[16,8192]{1,0:T(8,128)(2,1)S(1)}, u32[]{:S(2)}, u32[]{:S(2)}) collective-permute-start(bf16[16,8192]{1,0:T(8,128)(2,1)S(1)} %added.13), channel_id=1, source_target_pairs={{0,4},{1,3},{4,8},{5,1},{8,12},{9,5},{12,14},{13,9},{14,10},{15,13... | collective-permute-start | bytes 786440 | tf_op jit(solution)/shard_map/ppermute | solution.py:389
  70.3 2.3 %collective-permute-done.27.refs_2_ = bf16[16,8192]{1,0:T(8,128)(2,1)S(1)} collective-permute-done((bf16[16,8192]{1,0:T(8,128)(2,1)S(1)}, bf16[16,8192]{1,0:T(8,128)(2,1)S(1)}, u32[]{:S(2)}, u32[]{:S(2)}) %collective-permute-start.27) | collective-permute-done | bytes 262176 | tf_op jit(solution)/shard_map/ppermute | solution.py:389
  72.6 0.1 added.10
  72.7 1.3 %collective-permute-start.28 = (bf16[16,8192]{1,0:T(8,128)(2,1)S(1)}, bf16[16,8192]{1,0:T(8,128)(2,1)S(1)}, u32[]{:S(2)}, u32[]{:S(2)}) collective-permute-start(bf16[16,8192]{1,0:T(8,128)(2,1)S(1)} %added.10), channel_id=1, source_target_pairs={{0,4},{1,3},{4,8},{5,1},{8,12},{9,5},{12,14},{13,9},{14,10},{15,13... | collective-permute-start | bytes 786440 | tf_op jit(solution)/shard_map/ppermute | solution.py:389
  74.0 1.4 %collective-permute-done.31 = bf16[16,8192]{1,0:T(8,128)(2,1)S(1)} collective-permute-done((bf16[16,8192]{1,0:T(8,128)(2,1)S(1)}, bf16[16,8192]{1,0:T(8,128)(2,1)S(1)}, u32[]{:S(2)}, u32[]{:S(2)}) %collective-permute-start.31) | collective-permute-done | bytes 262176 | tf_op jit(solution)/shard_map/ppermute | solution.py:389
  75.4 3.7 %collective-permute-done.28.refs_2_ = bf16[16,8192]{1,0:T(8,128)(2,1)S(1)} collective-permute-done((bf16[16,8192]{1,0:T(8,128)(2,1)S(1)}, bf16[16,8192]{1,0:T(8,128)(2,1)S(1)}, u32[]{:S(2)}, u32[]{:S(2)}) %collective-permute-start.28) | collective-permute-done | bytes 262176 | tf_op jit(solution)/shard_map/ppermute | solution.py:389
  79.1 1.0 %last.1 = bf16[16,8192]{1,0:T(8,128)(2,1)} custom-call(s32[1,2]{1,0:T(1,128)S(1)} %bitcast.9, bf16[16,8192]{1,0:T(8,128)(2,1)S(1)} %get-tuple-element.40.refs_0_, bf16[16,8192]{1,0:T(8,128)(2,1)S(1)} %collective-permute-done.20.refs_1_, bf16[16,8192]{1,0:T(8,128)(2,1)S(1)} %collective-permute-done.28.refs_2_, ...), custom_call_target="tpu_custom_call" | custom-call | tf_op jit(solution)/shard_map/last/pallas_call | solution.py:339
  (48 shorter events, 0.1 us)
Async XLA Ops:
  0.0 6.6 %copy-start = (bf16[8,8192,8]{1,2,0:T(8,128)(2,1)S(1)}, bf16[8,8192,8]{1,2,0:T(8,128)(2,1)}, u32[]{:S(2)}) copy-start(bf16[8,8192,8]{1,2,0:T(8,128)(2,1)} %param.12) | copy-start | bytes 3145732
  0.0 26.9 %copy-start.1 = (s32[2]{0:T(128)S(1)}, s32[2]{0:T(128)}, u32[]{:S(2)}) copy-start(s32[2]{0:T(128)} %param.14) | copy-start | bytes 28
  0.0 28.6 %copy-start.3 = (bf16[8192,896]{1,0:T(8,128)(2,1)S(1)}, bf16[8192,896]{1,0:T(8,128)(2,1)}, u32[]{:S(2)}) copy-start(bf16[8192,896]{1,0:T(8,128)(2,1)} %w_ref.6) | copy-start | bytes 44040196
  0.0 3.2 %collective-permute-start = (bf16[16,8192]{1,0:T(8,128)(2,1)}, bf16[16,8192]{1,0:T(8,128)(2,1)S(1)}, u32[]{:S(2)}, u32[]{:S(2)}) collective-permute-start(bf16[16,8192]{1,0:T(8,128)(2,1)} %tokens_ref.1), channel_id=1, source_target_pairs={{0,1},{1,0},{2,3},{3,2},{4,5},{5,4},{6,7},{7,6},{8,9},{9,8},{10,11... | collective-permute-start | bytes 786440 | tf_op jit(solution)/shard_map/ppermute | solution.py:392
  0.5 7.1 %collective-permute-start.1 = (bf16[16,8192]{1,0:T(8,128)(2,1)}, bf16[16,8192]{1,0:T(8,128)(2,1)S(1)}, u32[]{:S(2)}, u32[]{:S(2)}) collective-permute-start(bf16[16,8192]{1,0:T(8,128)(2,1)} %tokens_ref.1), channel_id=1, source_target_pairs={{0,4},{1,3},{4,8},{5,1},{8,12},{9,5},{12,14},{13,9},{14,10},{15,13... | collective-permute-start | bytes 786440 | tf_op jit(solution)/shard_map/ppermute | solution.py:389
  4.9 6.4 %collective-permute-start.2 = (bf16[16,8192]{1,0:T(8,128)(2,1)S(1)}, bf16[16,8192]{1,0:T(8,128)(2,1)S(1)}, u32[]{:S(2)}, u32[]{:S(2)}) collective-permute-start(bf16[16,8192]{1,0:T(8,128)(2,1)S(1)} %get-tuple-element.30.refs_1_.refs_2_), channel_id=1, source_target_pairs={{0,4},{1,3},{4,8},{5,1},{8,12},{9,5},{12,14},{13,9},{14,10},{15,13... | collective-permute-start | bytes 786440 | tf_op jit(solution)/shard_map/ppermute | solution.py:389
  6.6 20.3 %collective-permute-start.15 = (bf16[8,8,8192]{2,1,0:T(8,128)(2,1)S(1)}, bf16[8,8,8192]{2,1,0:T(8,128)(2,1)S(1)}, u32[]{:S(2)}, u32[]{:S(2)}) collective-permute-start(bf16[8,8,8192]{2,1,0:T(8,128)(2,1)S(1)} %bitcast.5), channel_id=1, source_target_pairs={{0,1},{1,0},{2,3},{3,2},{4,5},{5,4},{6,7},{7,6},{8,9},{9,8},{10,11... | collective-permute-start | bytes 3145736 | tf_op jit(solution)/shard_map/ppermute | solution.py:392
  7.7 6.5 %collective-permute-start.3 = (bf16[16,8192]{1,0:T(8,128)(2,1)S(1)}, bf16[16,8192]{1,0:T(8,128)(2,1)S(1)}, u32[]{:S(2)}, u32[]{:S(2)}) collective-permute-start(bf16[16,8192]{1,0:T(8,128)(2,1)S(1)} %collective-permute-done.1.refs_1_.refs_2_.refs_3_), channel_id=1, source_target_pairs={{0,4},{1,3},{4,8},{5,1},{8,12},{9,5},{12,14},{13,9},{14,10},{15,13... | collective-permute-start | bytes 786440 | tf_op jit(solution)/shard_map/ppermute | solution.py:389
  9.7 6.4 %collective-permute-start.8 = (bf16[16,8192]{1,0:T(8,128)(2,1)S(1)}, bf16[16,8192]{1,0:T(8,128)(2,1)S(1)}, u32[]{:S(2)}, u32[]{:S(2)}) collective-permute-start(bf16[16,8192]{1,0:T(8,128)(2,1)S(1)} %collective-permute-done.1.refs_1_.refs_2_.refs_3_), channel_id=1, source_target_pairs={{0,1},{1,0},{2,3},{3,2},{4,5},{5,4},{6,7},{7,6},{8,9},{9,8},{10,11... | collective-permute-start | bytes 786440 | tf_op jit(solution)/shard_map/ppermute | solution.py:392
  11.3 6.4 %collective-permute-start.4 = (bf16[16,8192]{1,0:T(8,128)(2,1)S(1)}, bf16[16,8192]{1,0:T(8,128)(2,1)S(1)}, u32[]{:S(2)}, u32[]{:S(2)}) collective-permute-start(bf16[16,8192]{1,0:T(8,128)(2,1)S(1)} %collective-permute-done.2.refs_2_.refs_3_.refs_4_), channel_id=1, source_target_pairs={{0,4},{1,3},{4,8},{5,1},{8,12},{9,5},{12,14},{13,9},{14,10},{15,13... | collective-permute-start | bytes 786440 | tf_op jit(solution)/shard_map/ppermute | solution.py:389
  14.1 6.4 %collective-permute-start.5 = (bf16[16,8192]{1,0:T(8,128)(2,1)S(1)}, bf16[16,8192]{1,0:T(8,128)(2,1)S(1)}, u32[]{:S(2)}, u32[]{:S(2)}) collective-permute-start(bf16[16,8192]{1,0:T(8,128)(2,1)S(1)} %collective-permute-done.3.refs_3_.refs_4_.refs_5_), channel_id=1, source_target_pairs={{0,4},{1,3},{4,8},{5,1},{8,12},{9,5},{12,14},{13,9},{14,10},{15,13... | collective-permute-start | bytes 786440 | tf_op jit(solution)/shard_map/ppermute | solution.py:389
  16.1 6.4 %collective-permute-start.9 = (bf16[16,8192]{1,0:T(8,128)(2,1)S(1)}, bf16[16,8192]{1,0:T(8,128)(2,1)S(1)}, u32[]{:S(2)}, u32[]{:S(2)}) collective-permute-start(bf16[16,8192]{1,0:T(8,128)(2,1)S(1)} %collective-permute-done.2.refs_2_.refs_3_.refs_4_), channel_id=1, source_target_pairs={{0,1},{1,0},{2,3},{3,2},{4,5},{5,4},{6,7},{7,6},{8,9},{9,8},{10,11... | collective-permute-start | bytes 786440 | tf_op jit(solution)/shard_map/ppermute | solution.py:392
  16.1 6.4 %collective-permute-start.10 = (bf16[16,8192]{1,0:T(8,128)(2,1)S(1)}, bf16[16,8192]{1,0:T(8,128)(2,1)S(1)}, u32[]{:S(2)}, u32[]{:S(2)}) collective-permute-start(bf16[16,8192]{1,0:T(8,128)(2,1)S(1)} %collective-permute-done.3.refs_3_.refs_4_.refs_5_), channel_id=1, source_target_pairs={{0,1},{1,0},{2,3},{3,2},{4,5},{5,4},{6,7},{7,6},{8,9},{9,8},{10,11... | collective-permute-start | bytes 786440 | tf_op jit(solution)/shard_map/ppermute | solution.py:392
  17.7 6.4 %collective-permute-start.6 = (bf16[16,8192]{1,0:T(8,128)(2,1)S(1)}, bf16[16,8192]{1,0:T(8,128)(2,1)S(1)}, u32[]{:S(2)}, u32[]{:S(2)}) collective-permute-start(bf16[16,8192]{1,0:T(8,128)(2,1)S(1)} %collective-permute-done.4.refs_4_.refs_5_.refs_6_), channel_id=1, source_target_pairs={{0,4},{1,3},{4,8},{5,1},{8,12},{9,5},{12,14},{13,9},{14,10},{15,13... | collective-permute-start | bytes 786440 | tf_op jit(solution)/shard_map/ppermute | solution.py:389
  20.5 6.4 %collective-permute-start.7 = (bf16[16,8192]{1,0:T(8,128)(2,1)S(1)}, bf16[16,8192]{1,0:T(8,128)(2,1)S(1)}, u32[]{:S(2)}, u32[]{:S(2)}) collective-permute-start(bf16[16,8192]{1,0:T(8,128)(2,1)S(1)} %collective-permute-done.5.refs_5_.refs_6_.refs_7_), channel_id=1, source_target_pairs={{0,4},{1,3},{4,8},{5,1},{8,12},{9,5},{12,14},{13,9},{14,10},{15,13... | collective-permute-start | bytes 786440 | tf_op jit(solution)/shard_map/ppermute | solution.py:389
  22.5 4.4 %collective-permute-start.11 = (bf16[16,8192]{1,0:T(8,128)(2,1)S(1)}, bf16[16,8192]{1,0:T(8,128)(2,1)S(1)}, u32[]{:S(2)}, u32[]{:S(2)}) collective-permute-start(bf16[16,8192]{1,0:T(8,128)(2,1)S(1)} %collective-permute-done.4.refs_4_.refs_5_.refs_6_), channel_id=1, source_target_pairs={{0,1},{1,0},{2,3},{3,2},{4,5},{5,4},{6,7},{7,6},{8,9},{9,8},{10,11... | collective-permute-start | bytes 786440 | tf_op jit(solution)/shard_map/ppermute | solution.py:392
  22.5 4.4 %collective-permute-start.12 = (bf16[16,8192]{1,0:T(8,128)(2,1)S(1)}, bf16[16,8192]{1,0:T(8,128)(2,1)S(1)}, u32[]{:S(2)}, u32[]{:S(2)}) collective-permute-start(bf16[16,8192]{1,0:T(8,128)(2,1)S(1)} %collective-permute-done.5.refs_5_.refs_6_.refs_7_), channel_id=1, source_target_pairs={{0,1},{1,0},{2,3},{3,2},{4,5},{5,4},{6,7},{7,6},{8,9},{9,8},{10,11... | collective-permute-start | bytes 786440 | tf_op jit(solution)/shard_map/ppermute | solution.py:392
  24.1 2.8 %collective-permute-start.13 = (bf16[16,8192]{1,0:T(8,128)(2,1)S(1)}, bf16[16,8192]{1,0:T(8,128)(2,1)S(1)}, u32[]{:S(2)}, u32[]{:S(2)}) collective-permute-start(bf16[16,8192]{1,0:T(8,128)(2,1)S(1)} %collective-permute-done.6.refs_6_.refs_7_.refs_8_), channel_id=1, source_target_pairs={{0,1},{1,0},{2,3},{3,2},{4,5},{5,4},{6,7},{7,6},{8,9},{9,8},{10,11... | collective-permute-start | bytes 786440 | tf_op jit(solution)/shard_map/ppermute | solution.py:392
  26.9 1.7 %collective-permute-start.14 = (bf16[16,8192]{1,0:T(8,128)(2,1)S(1)}, bf16[16,8192]{1,0:T(8,128)(2,1)S(1)}, u32[]{:S(2)}, u32[]{:S(2)}) collective-permute-start(bf16[16,8192]{1,0:T(8,128)(2,1)S(1)} %collective-permute-done.7.refs_7_.refs_8_.refs_9_), channel_id=1, source_target_pairs={{0,1},{1,0},{2,3},{3,2},{4,5},{5,4},{6,7},{7,6},{8,9},{9,8},{10,11... | collective-permute-start | bytes 786440 | tf_op jit(solution)/shard_map/ppermute | solution.py:392
  28.1 4.1 %collective-permute-start.16 = (bf16[16,256]{1,0:T(8,128)(2,1)S(1)}, bf16[16,256]{1,0:T(8,128)(2,1)S(1)}, u32[]{:S(2)}, u32[]{:S(2)}) collective-permute-start(bf16[16,256]{1,0:T(8,128)(2,1)S(1)} %rank.1.refs_16_), channel_id=1, source_target_pairs={{0,1},{1,0},{2,3},{3,2},{4,5},{5,4},{6,7},{7,6},{8,9},{9,8},{10,11... | collective-permute-start | bytes 24584 | tf_op jit(solution)/shard_map/ppermute | solution.py:392
  28.6 9.3 %slice-start.4 = ((s8[14680064]{0:T(1024)(128)(4,1)}), s8[4194304]{0:T(1024)(128)(4,1)S(1)}, s32[]{:S(2)}) async-start(s8[14680064]{0:T(1024)(128)(4,1)} %bitcast.10), calls=%async_computation.4 | async-start | bytes 8388608
  28.6 9.3 %slice-start.5 = ((s8[14680064]{0:T(1024)(128)(4,1)}), s8[4194304]{0:T(1024)(128)(4,1)S(1)}, s32[]{:S(2)}) async-start(s8[14680064]{0:T(1024)(128)(4,1)} %bitcast.10), calls=%async_computation.5 | async-start | bytes 8388608
  32.2 5.7 %slice-start.6 = ((s8[14680064]{0:T(1024)(128)(4,1)}), s8[4194304]{0:T(1024)(128)(4,1)S(1)}, s32[]{:S(2)}) async-start(s8[14680064]{0:T(1024)(128)(4,1)} %bitcast.10), calls=%async_computation.6 | async-start | bytes 8388608
  32.2 5.7 %slice-start.7 = ((s8[14680064]{0:T(1024)(128)(4,1)}), s8[2097152]{0:T(1024)(128)(4,1)S(1)}, s32[]{:S(2)}) async-start(s8[14680064]{0:T(1024)(128)(4,1)} %bitcast.10), calls=%async_computation.7 | async-start | bytes 4194304
  32.2 3.9 %collective-permute-start.17 = (bf16[16,256]{1,0:T(8,128)(2,1)S(1)}, bf16[16,256]{1,0:T(8,128)(2,1)S(1)}, u32[]{:S(2)}, u32[]{:S(2)}) collective-permute-start(bf16[16,256]{1,0:T(8,128)(2,1)S(1)} %add.3), channel_id=1, source_target_pairs={{0,2},{1,3},{2,0},{3,1},{4,6},{5,7},{6,4},{7,5},{8,10},{9,11},{10,... | collective-permute-start | bytes 24584 | tf_op jit(solution)/shard_map/ppermute | solution.py:392
  36.1 4.2 %collective-permute-start.18 = (bf16[32,256]{1,0:T(8,128)(2,1)S(1)}, bf16[32,256]{1,0:T(8,128)(2,1)S(1)}, u32[]{:S(2)}, u32[]{:S(2)}) collective-permute-start(bf16[32,256]{1,0:T(8,128)(2,1)S(1)} %pad_maximum_fusion.2), channel_id=1, source_target_pairs={{0,4},{1,5},{2,6},{3,7},{4,0},{5,1},{6,2},{7,3},{8,12},{9,13},{10,... | collective-permute-start | bytes 49160 | tf_op jit(solution)/shard_map/ppermute | solution.py:392
  37.9 8.2 %slice-start = ((s8[14680064]{0:T(1024)(128)(4,1)}), s8[4194304]{0:T(1024)(128)(4,1)S(1)}, s32[]{:S(2)}) async-start(s8[14680064]{0:T(1024)(128)(4,1)} %bitcast.3), calls=%async_computation | async-start | bytes 8388608
  37.9 8.2 %slice-start.1 = ((s8[14680064]{0:T(1024)(128)(4,1)}), s8[4194304]{0:T(1024)(128)(4,1)S(1)}, s32[]{:S(2)}) async-start(s8[14680064]{0:T(1024)(128)(4,1)} %bitcast.3), calls=%async_computation.1 | async-start | bytes 8388608
  40.3 5.0 %collective-permute-start.19 = (bf16[64,256]{1,0:T(8,128)(2,1)S(1)}, bf16[64,256]{1,0:T(8,128)(2,1)S(1)}, u32[]{:S(2)}, u32[]{:S(2)}) collective-permute-start(bf16[64,256]{1,0:T(8,128)(2,1)S(1)} %pad_maximum_fusion.1), channel_id=1, source_target_pairs={{0,8},{1,9},{2,10},{3,11},{4,12},{5,13},{6,14},{7,15},{8,0},{9,1},... | collective-permute-start | bytes 98312 | tf_op jit(solution)/shard_map/ppermute | solution.py:392
  43.0 3.2 %slice-start.2 = ((s8[14680064]{0:T(1024)(128)(4,1)}), s8[4194304]{0:T(1024)(128)(4,1)S(1)}, s32[]{:S(2)}) async-start(s8[14680064]{0:T(1024)(128)(4,1)} %bitcast.3), calls=%async_computation.2 | async-start | bytes 8388608
  43.0 3.2 %slice-start.3 = ((s8[14680064]{0:T(1024)(128)(4,1)}), s8[2097152]{0:T(1024)(128)(4,1)S(1)}, s32[]{:S(2)}) async-start(s8[14680064]{0:T(1024)(128)(4,1)} %bitcast.3), calls=%async_computation.3 | async-start | bytes 4194304
  45.3 33.8 %copy-start.2 = (s32[2]{0:T(128)S(1)}, s32[2]{0:T(128)}, u32[]{:S(2)}) copy-start(s32[2]{0:T(128)} %param.15) | copy-start | bytes 28
  50.7 3.7 %collective-permute-start.23 = (bf16[32,8192]{1,0:T(8,128)(2,1)S(1)}, bf16[32,8192]{1,0:T(8,128)(2,1)S(1)}, u32[]{:S(2)}, u32[]{:S(2)}) collective-permute-start(bf16[32,8192]{1,0:T(8,128)(2,1)S(1)} %get-tuple-element.47), channel_id=1, source_target_pairs={{0,1},{1,0},{2,3},{3,2},{4,5},{5,4},{6,7},{7,6},{8,9},{9,8},{10,11... | collective-permute-start | bytes 1572872 | tf_op jit(solution)/shard_map/ppermute | solution.py:392
  50.8 2.3 %collective-permute-start.24 = (bf16[16,8192]{1,0:T(8,128)(2,1)S(1)}, bf16[16,8192]{1,0:T(8,128)(2,1)S(1)}, u32[]{:S(2)}, u32[]{:S(2)}) collective-permute-start(bf16[16,8192]{1,0:T(8,128)(2,1)S(1)} %get-tuple-element.49), channel_id=1, source_target_pairs={{0,1},{1,0},{2,3},{3,2},{4,5},{5,4},{6,7},{7,6},{8,9},{9,8},{10,11... | collective-permute-start | bytes 786440 | tf_op jit(solution)/shard_map/ppermute | solution.py:392
  51.3 9.7 %collective-permute-start.22 = (bf16[32,8192]{1,0:T(8,128)(2,1)S(1)}, bf16[32,8192]{1,0:T(8,128)(2,1)S(1)}, u32[]{:S(2)}, u32[]{:S(2)}) collective-permute-start(bf16[32,8192]{1,0:T(8,128)(2,1)S(1)} %get-tuple-element.45), channel_id=1, source_target_pairs={{0,1},{1,0},{2,3},{3,2},{4,5},{5,4},{6,7},{7,6},{8,9},{9,8},{10,11... | collective-permute-start | bytes 1572872 | tf_op jit(solution)/shard_map/ppermute | solution.py:392
  53.1 6.4 %collective-permute-start.25 = (bf16[16,8192]{1,0:T(8,128)(2,1)S(1)}, bf16[16,8192]{1,0:T(8,128)(2,1)S(1)}, u32[]{:S(2)}, u32[]{:S(2)}) collective-permute-start(bf16[16,8192]{1,0:T(8,128)(2,1)S(1)} %added.7), channel_id=1, source_target_pairs={{0,4},{1,3},{4,8},{5,1},{8,12},{9,5},{12,14},{13,9},{14,10},{15,13... | collective-permute-start | bytes 786440 | tf_op jit(solution)/shard_map/ppermute | solution.py:389
  54.5 7.8 %collective-permute-start.29 = (bf16[16,8192]{1,0:T(8,128)(2,1)S(1)}, bf16[16,8192]{1,0:T(8,128)(2,1)S(1)}, u32[]{:S(2)}, u32[]{:S(2)}) collective-permute-start(bf16[16,8192]{1,0:T(8,128)(2,1)S(1)} %added.11), channel_id=1, source_target_pairs={{0,4},{1,3},{4,8},{5,1},{8,12},{9,5},{12,14},{13,9},{14,10},{15,13... | collective-permute-start | bytes 786440 | tf_op jit(solution)/shard_map/ppermute | solution.py:389
  56.4 11.1 %collective-permute-start.21 = (bf16[32,8192]{1,0:T(8,128)(2,1)S(1)}, bf16[32,8192]{1,0:T(8,128)(2,1)S(1)}, u32[]{:S(2)}, u32[]{:S(2)}) collective-permute-start(bf16[32,8192]{1,0:T(8,128)(2,1)S(1)} %get-tuple-element.43), channel_id=1, source_target_pairs={{0,1},{1,0},{2,3},{3,2},{4,5},{5,4},{6,7},{7,6},{8,9},{9,8},{10,11... | collective-permute-start | bytes 1572872 | tf_op jit(solution)/shard_map/ppermute | solution.py:392
  59.6 6.4 %collective-permute-start.26 = (bf16[16,8192]{1,0:T(8,128)(2,1)S(1)}, bf16[16,8192]{1,0:T(8,128)(2,1)S(1)}, u32[]{:S(2)}, u32[]{:S(2)}) collective-permute-start(bf16[16,8192]{1,0:T(8,128)(2,1)S(1)} %added.8), channel_id=1, source_target_pairs={{0,4},{1,3},{4,8},{5,1},{8,12},{9,5},{12,14},{13,9},{14,10},{15,13... | collective-permute-start | bytes 786440 | tf_op jit(solution)/shard_map/ppermute | solution.py:389
  62.5 6.4 %collective-permute-start.30 = (bf16[16,8192]{1,0:T(8,128)(2,1)S(1)}, bf16[16,8192]{1,0:T(8,128)(2,1)S(1)}, u32[]{:S(2)}, u32[]{:S(2)}) collective-permute-start(bf16[16,8192]{1,0:T(8,128)(2,1)S(1)} %added.12), channel_id=1, source_target_pairs={{0,4},{1,3},{4,8},{5,1},{8,12},{9,5},{12,14},{13,9},{14,10},{15,13... | collective-permute-start | bytes 786440 | tf_op jit(solution)/shard_map/ppermute | solution.py:389
  66.2 6.4 %collective-permute-start.27 = (bf16[16,8192]{1,0:T(8,128)(2,1)S(1)}, bf16[16,8192]{1,0:T(8,128)(2,1)S(1)}, u32[]{:S(2)}, u32[]{:S(2)}) collective-permute-start(bf16[16,8192]{1,0:T(8,128)(2,1)S(1)} %added.9), channel_id=1, source_target_pairs={{0,4},{1,3},{4,8},{5,1},{8,12},{9,5},{12,14},{13,9},{14,10},{15,13... | collective-permute-start | bytes 786440 | tf_op jit(solution)/shard_map/ppermute | solution.py:389
  69.0 6.4 %collective-permute-start.31 = (bf16[16,8192]{1,0:T(8,128)(2,1)S(1)}, bf16[16,8192]{1,0:T(8,128)(2,1)S(1)}, u32[]{:S(2)}, u32[]{:S(2)}) collective-permute-start(bf16[16,8192]{1,0:T(8,128)(2,1)S(1)} %added.13), channel_id=1, source_target_pairs={{0,4},{1,3},{4,8},{5,1},{8,12},{9,5},{12,14},{13,9},{14,10},{15,13... | collective-permute-start | bytes 786440 | tf_op jit(solution)/shard_map/ppermute | solution.py:389
  70.3 5.1 %collective-permute-start.20 = (bf16[16,8192]{1,0:T(8,128)(2,1)S(1)}, bf16[16,8192]{1,0:T(8,128)(2,1)S(1)}, u32[]{:S(2)}, u32[]{:S(2)}) collective-permute-start(bf16[16,8192]{1,0:T(8,128)(2,1)S(1)} %get-tuple-element.41), channel_id=1, source_target_pairs={{0,1},{1,0},{2,3},{3,2},{4,5},{5,4},{6,7},{7,6},{8,9},{9,8},{10,11... | collective-permute-start | bytes 786440 | tf_op jit(solution)/shard_map/ppermute | solution.py:392
  72.7 6.4 %collective-permute-start.28 = (bf16[16,8192]{1,0:T(8,128)(2,1)S(1)}, bf16[16,8192]{1,0:T(8,128)(2,1)S(1)}, u32[]{:S(2)}, u32[]{:S(2)}) collective-permute-start(bf16[16,8192]{1,0:T(8,128)(2,1)S(1)} %added.10), channel_id=1, source_target_pairs={{0,4},{1,3},{4,8},{5,1},{8,12},{9,5},{12,14},{13,9},{14,10},{15,13... | collective-permute-start | bytes 786440 | tf_op jit(solution)/shard_map/ppermute | solution.py:389
  75.4 3.7 %collective-permute-start.32 = (bf16[16,8192]{1,0:T(8,128)(2,1)S(1)}, bf16[16,8192]{1,0:T(8,128)(2,1)S(1)}, u32[]{:S(2)}, u32[]{:S(2)}) collective-permute-start(bf16[16,8192]{1,0:T(8,128)(2,1)S(1)} %collective-permute-done.31), channel_id=1, source_target_pairs={{0,1},{1,0},{2,3},{3,2},{4,5},{5,4},{6,7},{7,6},{8,9},{9,8},{10,11... | collective-permute-start | bytes 786440 | tf_op jit(solution)/shard_map/ppermute | solution.py:392

commit v15 on v13

--- a/solution.py
+++ b/solution.py
@@ -112,6 +112,22 @@
         cost_estimate=cost(30_000_000_000, 0),
         name="anchor",
     )(far(tokens), passed)
+
+
+def tie_kernel(x_ref, after_ref, out_ref):
+    del x_ref, after_ref, out_ref
+
+
+def tie(x, after):
+    return pl.pallas_call(
+        tie_kernel,
+        in_specs=[FAR, FAR],
+        out_specs=FAR,
+        out_shape=jax.ShapeDtypeStruct(x.shape, x.dtype),
+        input_output_aliases={0: 0},
+        compiler_params=params(),
+        name="tie",
+    )(x, after)
 
 
 def rank_kernel(members, numbers, ids_ref, expand_ref, own_ref, other_ref, *refs):
@@ -313,7 +329,11 @@
     rows = out_ref.shape[0]
     first = lax.axis_index("tp") * rows
     block_rows = members * rows // blocks
-    live = picked(counts_ref, first // block_rows) - first % block_rows
+    counts = counts_ref[...]
+    spots = lax.broadcasted_iota(jnp.int32, counts.shape, 1)
+    live = jnp.sum(
+        jnp.where(spots == first // block_rows, counts, 0), axis=1, keepdims=True
+    ) - first % block_rows
     each = len(terms) // parts
     columns = out_ref.shape[1] // parts
     for part in range(parts):
@@ -432,7 +452,8 @@
     groups = [1] * slots + [1] + [2] * (reach - 1) + [1]
     outs = down(hidden, down_matrix, groups, rows)
     keep, give = outs[:slots], outs[slots:]
-    came = [cross(x) for x in give]
+    came = [cross(give[0])]
+    came += [cross(tie(x, came[0])) for x in give[1:]]
     first = step(added(rows, (0, keep[0]), (0, came[0])))
     second = None
     for index in range(1, reach):

time: 78.8 us -> 78.5 us (level)
  no operation moved by 1% of the time
where the time goes in v15:
time: 78.5 us; the launch traced here: 78.3 us
  starting transfers between devices  32.7 us (42%)
  waiting for transfers between devices  27 us (34%)
  Pallas kernels  18.3 us (23%)
    ppermute x14, waiting for transfers between devices, step(): return lax.ppermute(x, 'tp', ring)  25.4 us
    ppermute x14, starting transfers between devices, step(): return lax.ppermute(x, 'tp', ring)  23.6 us
    ppermute x19, starting transfers between devices, cross(): return lax.ppermute(x, 'tp', crossing(members, bit))  9.1 us
    pallas_call x4, Pallas kernels, product(): pl.pallas_call(functools.partial(product_kernel, part * depth, depth, mai...  8.55 us
    pallas_call x1, Pallas kernels, down(): pl.pallas_call(functools.partial(down_kernel, groups, rows, size), in_spe...  4.5 us
    pallas_call x1, Pallas kernels, anchor(): pl.pallas_call(anchor_kernel, in_specs=[FAR, FAR], out_specs=whole(1) + [...  1.71 us
    ppermute x19, waiting for transfers between devices, cross(): return lax.ppermute(x, 'tp', crossing(members, bit))  1.58 us
  transfers between devices with their start and end apart: 33, of which 15 were waited for; matrix products, arithmetic and copies ran while one was open for 0% of the time, Pallas kernels for 15%

profile of v15, /device:TPU:0, one launch (start us, length us, event | category | flops | bytes accessed | tf_op | source)
XLA Modules:
  0.0 78.3 jit_solution(17497271873915358287)
XLA Ops:
  0.0 0.5 collective-permute-start
  0.5 2.6 %collective-permute-start.1 = (bf16[16,8192]{1,0:T(8,128)(2,1)}, bf16[16,8192]{1,0:T(8,128)(2,1)S(1)}, u32[]{:S(2)}, u32[]{:S(2)}) collective-permute-start(bf16[16,8192]{1,0:T(8,128)(2,1)} %tokens_ref.1), channel_id=1, source_target_pairs={{0,4},{1,3},{4,8},{5,1},{8,12},{9,5},{12,14},{13,9},{14,10},{15,13... | collective-permute-start | bytes 786440 | tf_op jit(solution)/shard_map/ppermute | solution.py:402
  3.2 0.0 collective-permute-done.passed_in
  3.2 1.7 %anchor.1 = (bf16[16,8192]{1,0:T(8,128)(2,1)S(1)}, bf16[16,8192]{1,0:T(8,128)(2,1)S(1)}) custom-call(bf16[16,8192]{1,0:T(8,128)(2,1)} %tokens_ref.1, bf16[16,8192]{1,0:T(8,128)(2,1)S(1)} %collective-permute-done.passed_in), custom_call_target="tpu_custom_call", output_to_operand_aliasing={{1}: (1, {})} | custom-call | flops 30000001024 | tf_op jit(solution)/shard_map/anchor/pallas_call | solution.py:104
  4.9 1.7 %collective-permute-start.2 = (bf16[16,8192]{1,0:T(8,128)(2,1)S(1)}, bf16[16,8192]{1,0:T(8,128)(2,1)S(1)}, u32[]{:S(2)}, u32[]{:S(2)}) collective-permute-start(bf16[16,8192]{1,0:T(8,128)(2,1)S(1)} %get-tuple-element.31.refs_1_.refs_2_), channel_id=1, source_target_pairs={{0,4},{1,3},{4,8},{5,1},{8,12},{9,5},{12,14},{13,9},{14,10},{15,13... | collective-permute-start | bytes 786440 | tf_op jit(solution)/shard_map/ppermute | solution.py:402
  6.6 0.0 collective-permute-start.15
  6.6 1.1 %collective-permute-done.1.refs_1_.refs_2_.refs_3_ = bf16[16,8192]{1,0:T(8,128)(2,1)S(1)} collective-permute-done((bf16[16,8192]{1,0:T(8,128)(2,1)}, bf16[16,8192]{1,0:T(8,128)(2,1)S(1)}, u32[]{:S(2)}, u32[]{:S(2)}) %collective-permute-start.1) | collective-permute-done | bytes 262176 | tf_op jit(solution)/shard_map/ppermute | solution.py:402
  7.7 2.1 %collective-permute-start.3 = (bf16[16,8192]{1,0:T(8,128)(2,1)S(1)}, bf16[16,8192]{1,0:T(8,128)(2,1)S(1)}, u32[]{:S(2)}, u32[]{:S(2)}) collective-permute-start(bf16[16,8192]{1,0:T(8,128)(2,1)S(1)} %collective-permute-done.1.refs_1_.refs_2_.refs_3_), channel_id=1, source_target_pairs={{0,4},{1,3},{4,8},{5,1},{8,12},{9,5},{12,14},{13,9},{14,10},{15,13... | collective-permute-start | bytes 786440 | tf_op jit(solution)/shard_map/ppermute | solution.py:402
  9.8 1.6 %collective-permute-done.2.refs_2_.refs_3_.refs_4_ = bf16[16,8192]{1,0:T(8,128)(2,1)S(1)} collective-permute-done((bf16[16,8192]{1,0:T(8,128)(2,1)S(1)}, bf16[16,8192]{1,0:T(8,128)(2,1)S(1)}, u32[]{:S(2)}, u32[]{:S(2)}) %collective-permute-start.2) | collective-permute-done | bytes 262176 | tf_op jit(solution)/shard_map/ppermute | solution.py:402
  11.3 1.7 %collective-permute-start.4 = (bf16[16,8192]{1,0:T(8,128)(2,1)S(1)}, bf16[16,8192]{1,0:T(8,128)(2,1)S(1)}, u32[]{:S(2)}, u32[]{:S(2)}) collective-permute-start(bf16[16,8192]{1,0:T(8,128)(2,1)S(1)} %collective-permute-done.2.refs_2_.refs_3_.refs_4_), channel_id=1, source_target_pairs={{0,4},{1,3},{4,8},{5,1},{8,12},{9,5},{12,14},{13,9},{14,10},{15,13... | collective-permute-start | bytes 786440 | tf_op jit(solution)/shard_map/ppermute | solution.py:402
  13.0 1.1 %collective-permute-done.3.refs_3_.refs_4_.refs_5_ = bf16[16,8192]{1,0:T(8,128)(2,1)S(1)} collective-permute-done((bf16[16,8192]{1,0:T(8,128)(2,1)S(1)}, bf16[16,8192]{1,0:T(8,128)(2,1)S(1)}, u32[]{:S(2)}, u32[]{:S(2)}) %collective-permute-start.3) | collective-permute-done | bytes 262176 | tf_op jit(solution)/shard_map/ppermute | solution.py:402
  14.1 2.0 %collective-permute-start.5 = (bf16[16,8192]{1,0:T(8,128)(2,1)S(1)}, bf16[16,8192]{1,0:T(8,128)(2,1)S(1)}, u32[]{:S(2)}, u32[]{:S(2)}) collective-permute-start(bf16[16,8192]{1,0:T(8,128)(2,1)S(1)} %collective-permute-done.3.refs_3_.refs_4_.refs_5_), channel_id=1, source_target_pairs={{0,4},{1,3},{4,8},{5,1},{8,12},{9,5},{12,14},{13,9},{14,10},{15,13... | collective-permute-start | bytes 786440 | tf_op jit(solution)/shard_map/ppermute | solution.py:402
  16.1 0.0 collective-permute-start.9
  16.1 0.0 collective-permute-done.8.refs_8_.refs_9_.refs_10_
  16.1 0.5 collective-permute-start.10
  16.6 1.1 %collective-permute-done.4.refs_4_.refs_5_.refs_6_ = bf16[16,8192]{1,0:T(8,128)(2,1)S(1)} collective-permute-done((bf16[16,8192]{1,0:T(8,128)(2,1)S(1)}, bf16[16,8192]{1,0:T(8,128)(2,1)S(1)}, u32[]{:S(2)}, u32[]{:S(2)}) %collective-permute-start.4) | collective-permute-done | bytes 262176 | tf_op jit(solution)/shard_map/ppermute | solution.py:402
  17.7 1.7 %collective-permute-start.6 = (bf16[16,8192]{1,0:T(8,128)(2,1)S(1)}, bf16[16,8192]{1,0:T(8,128)(2,1)S(1)}, u32[]{:S(2)}, u32[]{:S(2)}) collective-permute-start(bf16[16,8192]{1,0:T(8,128)(2,1)S(1)} %collective-permute-done.4.refs_4_.refs_5_.refs_6_), channel_id=1, source_target_pairs={{0,4},{1,3},{4,8},{5,1},{8,12},{9,5},{12,14},{13,9},{14,10},{15,13... | collective-permute-start | bytes 786440 | tf_op jit(solution)/shard_map/ppermute | solution.py:402
  19.4 1.1 %collective-permute-done.5.refs_5_.refs_6_.refs_7_ = bf16[16,8192]{1,0:T(8,128)(2,1)S(1)} collective-permute-done((bf16[16,8192]{1,0:T(8,128)(2,1)S(1)}, bf16[16,8192]{1,0:T(8,128)(2,1)S(1)}, u32[]{:S(2)}, u32[]{:S(2)}) %collective-permute-start.5) | collective-permute-done | bytes 262176 | tf_op jit(solution)/shard_map/ppermute | solution.py:402
  20.5 2.0 %collective-permute-start.7 = (bf16[16,8192]{1,0:T(8,128)(2,1)S(1)}, bf16[16,8192]{1,0:T(8,128)(2,1)S(1)}, u32[]{:S(2)}, u32[]{:S(2)}) collective-permute-start(bf16[16,8192]{1,0:T(8,128)(2,1)S(1)} %collective-permute-done.5.refs_5_.refs_6_.refs_7_), channel_id=1, source_target_pairs={{0,4},{1,3},{4,8},{5,1},{8,12},{9,5},{12,14},{13,9},{14,10},{15,13... | collective-permute-start | bytes 786440 | tf_op jit(solution)/shard_map/ppermute | solution.py:402
  22.5 0.5 collective-permute-start.12
  23.0 1.0 %collective-permute-done.6.refs_6_.refs_7_.refs_8_ = bf16[16,8192]{1,0:T(8,128)(2,1)S(1)} collective-permute-done((bf16[16,8192]{1,0:T(8,128)(2,1)S(1)}, bf16[16,8192]{1,0:T(8,128)(2,1)S(1)}, u32[]{:S(2)}, u32[]{:S(2)}) %collective-permute-start.6) | collective-permute-done | bytes 262176 | tf_op jit(solution)/shard_map/ppermute | solution.py:402
  24.1 2.8 %collective-permute-done.7.refs_7_.refs_8_.refs_9_ = bf16[16,8192]{1,0:T(8,128)(2,1)S(1)} collective-permute-done((bf16[16,8192]{1,0:T(8,128)(2,1)S(1)}, bf16[16,8192]{1,0:T(8,128)(2,1)S(1)}, u32[]{:S(2)}, u32[]{:S(2)}) %collective-permute-start.7) | collective-permute-done | bytes 262176 | tf_op jit(solution)/shard_map/ppermute | solution.py:402
  26.9 1.2 %rank.1 = (bf16[16,256]{1,0:T(8,128)(2,1)S(1)}, bf16[2,128,896]{2,1,0:T(8,128)(2,1)S(1)}) custom-call(s32[1,2]{1,0:T(1,128)S(1)} %bitcast.7, bf16[8,128,896]{2,1,0:T(8,128)(2,1)} %expand_ref.1, bf16[8,8,8192]{2,1,0:T(8,128)(2,1)S(1)} %bitcast.6, bf16[8,8,8192]{2,1,0:T(8,128)(2,1)S(1)} %collective-permute-done.15.other_ref, ...), custom_call_target="tpu_custom_call" | custom-call | flops 67108864 | bytes 4194304 | tf_op jit(solution)/shard_map/rank/pallas_call | solution.py:182
  28.1 0.6 collective-permute-start.16
  28.7 1.9 %product.4 = (f32[256,768]{1,0:T(8,128)S(1)}, bf16[4096,128]{1,0:T(8,128)(2,1)S(1)}) custom-call(bf16[8192,896]{1,0:T(8,128)(2,1)S(1)} %copy-done.3, bf16[16,8192]{1,0:T(8,128)(2,1)S(1)} %get-tuple-element.30.refs_0_.refs_1_, bf16[16,8192]{1,0:T(8,128)(2,1)S(1)} %get-tuple-element.31.refs_1_.refs_2_, ...), custom_call_target="tpu_custom_call" | custom-call | flops 5637144576 | bytes 9437184 | tf_op jit(solution)/shard_map/product/pallas_call | solution.py:236
  30.7 0.0 slice-start.6
  30.7 2.0 %collective-permute-start.17 = (bf16[16,256]{1,0:T(8,128)(2,1)S(1)}, bf16[16,256]{1,0:T(8,128)(2,1)S(1)}, u32[]{:S(2)}, u32[]{:S(2)}) collective-permute-start(bf16[16,256]{1,0:T(8,128)(2,1)S(1)} %add.3), channel_id=1, source_target_pairs={{0,2},{1,3},{2,0},{3,1},{4,6},{5,7},{6,4},{7,5},{8,10},{9,11},{10,... | collective-permute-start | bytes 24584 | tf_op jit(solution)/shard_map/ppermute | solution.py:405
  32.7 1.9 %product.5 = (f32[256,768]{1,0:T(8,128)S(1)}, bf16[4096,128]{1,0:T(8,128)(2,1)S(1)}) custom-call(bf16[8192,896]{1,0:T(8,128)(2,1)S(1)} %copy-done.3, bf16[16,8192]{1,0:T(8,128)(2,1)S(1)} %get-tuple-element.30.refs_0_.refs_1_, bf16[16,8192]{1,0:T(8,128)(2,1)S(1)} %get-tuple-element.31.refs_1_.refs_2_, ...), custom_call_target="tpu_custom_call" | custom-call | flops 5637144576 | bytes 9437184 | tf_op jit(solution)/shard_map/product/pallas_call | solution.py:236
  34.7 1.7 %collective-permute-start.18 = (bf16[32,256]{1,0:T(8,128)(2,1)S(1)}, bf16[32,256]{1,0:T(8,128)(2,1)S(1)}, u32[]{:S(2)}, u32[]{:S(2)}) collective-permute-start(bf16[32,256]{1,0:T(8,128)(2,1)S(1)} %pad_maximum_fusion.2), channel_id=1, source_target_pairs={{0,4},{1,5},{2,6},{3,7},{4,0},{5,1},{6,2},{7,3},{8,12},{9,13},{10,... | collective-permute-start | bytes 49160 | tf_op jit(solution)/shard_map/ppermute | solution.py:405
  36.4 0.0 slice-start
  36.5 0.0 slice-start.1
  36.5 2.3 %product.6 = (f32[256,768]{1,0:T(8,128)S(1)}, f32[256,256]{1,0:T(8,128)S(1)}) custom-call(bf16[8192,896]{1,0:T(8,128)(2,1)S(1)} %bitcast.10, bf16[4096,128]{1,0:T(8,128)(2,1)S(1)} %get-tuple-element.35.refs_0_, bf16[16,8192]{1,0:T(8,128)(2,1)S(1)} %get-tuple-element.30.refs_0_.refs_1_, bf16[16,8192]{1,0:T(8,128)(2,1)S(1)} %get-tuple-element.31.refs_1_.refs_2_, ...), custom_call_target="tpu_custom_call" | custom-call | flops 5637144576 | bytes 9437184 | tf_op jit(solution)/shard_map/product/pallas_call | solution.py:236
  38.8 2.7 %collective-permute-start.19 = (bf16[64,256]{1,0:T(8,128)(2,1)S(1)}, bf16[64,256]{1,0:T(8,128)(2,1)S(1)}, u32[]{:S(2)}, u32[]{:S(2)}) collective-permute-start(bf16[64,256]{1,0:T(8,128)(2,1)S(1)} %pad_maximum_fusion.1), channel_id=1, source_target_pairs={{0,8},{1,9},{2,10},{3,11},{4,12},{5,13},{6,14},{7,15},{8,0},{9,1},... | collective-permute-start | bytes 98312 | tf_op jit(solution)/shard_map/ppermute | solution.py:405
  41.5 2.3 %product.7 = (f32[256,768]{1,0:T(8,128)S(1)}, f32[256,256]{1,0:T(8,128)S(1)}) custom-call(bf16[8192,896]{1,0:T(8,128)(2,1)S(1)} %bitcast.10, bf16[4096,128]{1,0:T(8,128)(2,1)S(1)} %get-tuple-element.37.refs_0_, bf16[16,8192]{1,0:T(8,128)(2,1)S(1)} %get-tuple-element.30.refs_0_.refs_1_, bf16[16,8192]{1,0:T(8,128)(2,1)S(1)} %get-tuple-element.31.refs_1_.refs_2_, ...), custom_call_target="tpu_custom_call" | custom-call | flops 5637144576 | bytes 9437184 | tf_op jit(solution)/shard_map/product/pallas_call | solution.py:236
  43.8 0.8 %finish.1.hidden_ref = bf16[256,896]{1,0:T(8,128)(2,1)S(1)} custom-call(f32[256,768]{1,0:T(8,128)S(1)} %get-tuple-element.33.refs_0_, f32[256,768]{1,0:T(8,128)S(1)} %get-tuple-element.34.refs_1_, f32[256,768]{1,0:T(8,128)S(1)} %get-tuple-element.36.refs_2_, f32[256,768]{1,0:T(8,128)S(1)} %get-tuple-element.38.refs_3_, ...), custom_call_target="tpu_custom_call" | custom-call | tf_op jit(solution)/shard_map/finish/pallas_call | solution.py:288
  44.7 0.0 copy-start.2
  44.7 4.5 %down.1 = (bf16[16,8192]{1,0:T(8,128)(2,1)S(1)}, bf16[16,8192]{1,0:T(8,128)(2,1)S(1)}, bf16[16,8192]{1,0:T(8,128)(2,1)S(1)}, bf16[16,8192]{1,0:T(8,128)(2,1)S(1)...) custom-call(bf16[896,8192]{1,0:T(8,128)(2,1)S(1)} %bitcast.4, ...), custom_call_target="tpu_custom_call" | custom-call | flops 3758096384 | bytes 18874368 | tf_op jit(solution)/shard_map/down/pallas_call | solution.py:314
  49.2 0.1 collective-permute-start.20
  49.3 1.5 %collective-permute-done.20.after_ref.refs_1_ = bf16[16,8192]{1,0:T(8,128)(2,1)S(1)} collective-permute-done((bf16[16,8192]{1,0:T(8,128)(2,1)S(1)}, bf16[16,8192]{1,0:T(8,128)(2,1)S(1)}, u32[]{:S(2)}, u32[]{:S(2)}) %collective-permute-start.20) | collective-permute-done | bytes 262176 | tf_op jit(solution)/shard_map/ppermute | solution.py:405
  50.8 0.1 collective-permute-start.24
  51.0 0.4 collective-permute-start.23
  51.3 0.1 added.7
  51.4 1.3 %collective-permute-start.25 = (bf16[16,8192]{1,0:T(8,128)(2,1)S(1)}, bf16[16,8192]{1,0:T(8,128)(2,1)S(1)}, u32[]{:S(2)}, u32[]{:S(2)}) collective-permute-start(bf16[16,8192]{1,0:T(8,128)(2,1)S(1)} %added.7), channel_id=1, source_target_pairs={{0,4},{1,3},{4,8},{5,1},{8,12},{9,5},{12,14},{13,9},{14,10},{15,13... | collective-permute-start | bytes 786440 | tf_op jit(solution)/shard_map/ppermute | solution.py:402
  52.7 0.0 collective-permute-done.24.refs_1_
  52.7 0.1 added.11
  52.8 1.9 %collective-permute-start.29 = (bf16[16,8192]{1,0:T(8,128)(2,1)S(1)}, bf16[16,8192]{1,0:T(8,128)(2,1)S(1)}, u32[]{:S(2)}, u32[]{:S(2)}) collective-permute-start(bf16[16,8192]{1,0:T(8,128)(2,1)S(1)} %added.11), channel_id=1, source_target_pairs={{0,4},{1,3},{4,8},{5,1},{8,12},{9,5},{12,14},{13,9},{14,10},{15,13... | collective-permute-start | bytes 786440 | tf_op jit(solution)/shard_map/ppermute | solution.py:402
  54.7 3.1 %collective-permute-done.25.refs_2_ = bf16[16,8192]{1,0:T(8,128)(2,1)S(1)} collective-permute-done((bf16[16,8192]{1,0:T(8,128)(2,1)S(1)}, bf16[16,8192]{1,0:T(8,128)(2,1)S(1)}, u32[]{:S(2)}, u32[]{:S(2)}) %collective-permute-start.25) | collective-permute-done | bytes 262176 | tf_op jit(solution)/shard_map/ppermute | solution.py:402
  57.8 0.1 added.8
  57.9 1.3 %collective-permute-start.26 = (bf16[16,8192]{1,0:T(8,128)(2,1)S(1)}, bf16[16,8192]{1,0:T(8,128)(2,1)S(1)}, u32[]{:S(2)}, u32[]{:S(2)}) collective-permute-start(bf16[16,8192]{1,0:T(8,128)(2,1)S(1)} %added.8), channel_id=1, source_target_pairs={{0,4},{1,3},{4,8},{5,1},{8,12},{9,5},{12,14},{13,9},{14,10},{15,13... | collective-permute-start | bytes 786440 | tf_op jit(solution)/shard_map/ppermute | solution.py:402
  59.2 1.4 %collective-permute-done.29.refs_2_ = bf16[16,8192]{1,0:T(8,128)(2,1)S(1)} collective-permute-done((bf16[16,8192]{1,0:T(8,128)(2,1)S(1)}, bf16[16,8192]{1,0:T(8,128)(2,1)S(1)}, u32[]{:S(2)}, u32[]{:S(2)}) %collective-permute-start.29) | collective-permute-done | bytes 262176 | tf_op jit(solution)/shard_map/ppermute | solution.py:402
  60.6 0.1 added.12
  60.7 1.3 %collective-permute-start.30 = (bf16[16,8192]{1,0:T(8,128)(2,1)S(1)}, bf16[16,8192]{1,0:T(8,128)(2,1)S(1)}, u32[]{:S(2)}, u32[]{:S(2)}) collective-permute-start(bf16[16,8192]{1,0:T(8,128)(2,1)S(1)} %added.12), channel_id=1, source_target_pairs={{0,4},{1,3},{4,8},{5,1},{8,12},{9,5},{12,14},{13,9},{14,10},{15,13... | collective-permute-start | bytes 786440 | tf_op jit(solution)/shard_map/ppermute | solution.py:402
  62.0 2.3 %collective-permute-done.26.refs_2_ = bf16[16,8192]{1,0:T(8,128)(2,1)S(1)} collective-permute-done((bf16[16,8192]{1,0:T(8,128)(2,1)S(1)}, bf16[16,8192]{1,0:T(8,128)(2,1)S(1)}, u32[]{:S(2)}, u32[]{:S(2)}) %collective-permute-start.26) | collective-permute-done | bytes 262176 | tf_op jit(solution)/shard_map/ppermute | solution.py:402
  64.3 0.1 added.9
  64.4 1.3 %collective-permute-start.27 = (bf16[16,8192]{1,0:T(8,128)(2,1)S(1)}, bf16[16,8192]{1,0:T(8,128)(2,1)S(1)}, u32[]{:S(2)}, u32[]{:S(2)}) collective-permute-start(bf16[16,8192]{1,0:T(8,128)(2,1)S(1)} %added.9), channel_id=1, source_target_pairs={{0,4},{1,3},{4,8},{5,1},{8,12},{9,5},{12,14},{13,9},{14,10},{15,13... | collective-permute-start | bytes 786440 | tf_op jit(solution)/shard_map/ppermute | solution.py:402
  65.8 1.4 %collective-permute-done.30.refs_2_ = bf16[16,8192]{1,0:T(8,128)(2,1)S(1)} collective-permute-done((bf16[16,8192]{1,0:T(8,128)(2,1)S(1)}, bf16[16,8192]{1,0:T(8,128)(2,1)S(1)}, u32[]{:S(2)}, u32[]{:S(2)}) %collective-permute-start.30) | collective-permute-done | bytes 262176 | tf_op jit(solution)/shard_map/ppermute | solution.py:402
  67.2 0.1 added.13
  67.3 1.3 %collective-permute-start.31 = (bf16[16,8192]{1,0:T(8,128)(2,1)S(1)}, bf16[16,8192]{1,0:T(8,128)(2,1)S(1)}, u32[]{:S(2)}, u32[]{:S(2)}) collective-permute-start(bf16[16,8192]{1,0:T(8,128)(2,1)S(1)} %added.13), channel_id=1, source_target_pairs={{0,4},{1,3},{4,8},{5,1},{8,12},{9,5},{12,14},{13,9},{14,10},{15,13... | collective-permute-start | bytes 786440 | tf_op jit(solution)/shard_map/ppermute | solution.py:402
  68.6 2.3 %collective-permute-done.27.refs_2_ = bf16[16,8192]{1,0:T(8,128)(2,1)S(1)} collective-permute-done((bf16[16,8192]{1,0:T(8,128)(2,1)S(1)}, bf16[16,8192]{1,0:T(8,128)(2,1)S(1)}, u32[]{:S(2)}, u32[]{:S(2)}) %collective-permute-start.27) | collective-permute-done | bytes 262176 | tf_op jit(solution)/shard_map/ppermute | solution.py:402
  70.9 0.1 added.10
  71.0 1.3 %collective-permute-start.28 = (bf16[16,8192]{1,0:T(8,128)(2,1)S(1)}, bf16[16,8192]{1,0:T(8,128)(2,1)S(1)}, u32[]{:S(2)}, u32[]{:S(2)}) collective-permute-start(bf16[16,8192]{1,0:T(8,128)(2,1)S(1)} %added.10), channel_id=1, source_target_pairs={{0,4},{1,3},{4,8},{5,1},{8,12},{9,5},{12,14},{13,9},{14,10},{15,13... | collective-permute-start | bytes 786440 | tf_op jit(solution)/shard_map/ppermute | solution.py:402
  72.3 1.4 %collective-permute-done.31 = bf16[16,8192]{1,0:T(8,128)(2,1)S(1)} collective-permute-done((bf16[16,8192]{1,0:T(8,128)(2,1)S(1)}, bf16[16,8192]{1,0:T(8,128)(2,1)S(1)}, u32[]{:S(2)}, u32[]{:S(2)}) %collective-permute-start.31) | collective-permute-done | bytes 262176 | tf_op jit(solution)/shard_map/ppermute | solution.py:402
  73.7 3.7 %collective-permute-done.28.refs_2_ = bf16[16,8192]{1,0:T(8,128)(2,1)S(1)} collective-permute-done((bf16[16,8192]{1,0:T(8,128)(2,1)S(1)}, bf16[16,8192]{1,0:T(8,128)(2,1)S(1)}, u32[]{:S(2)}, u32[]{:S(2)}) %collective-permute-start.28) | collective-permute-done | bytes 262176 | tf_op jit(solution)/shard_map/ppermute | solution.py:402
  77.4 0.9 %last.1 = bf16[16,8192]{1,0:T(8,128)(2,1)} custom-call(s32[1,2]{1,0:T(1,128)S(1)} %bitcast.8, bf16[16,8192]{1,0:T(8,128)(2,1)S(1)} %get-tuple-element.42.refs_0_, bf16[16,8192]{1,0:T(8,128)(2,1)S(1)} %collective-permute-done.21.refs_1_, bf16[16,8192]{1,0:T(8,128)(2,1)S(1)} %collective-permute-done.28.refs_2_, ...), custom_call_target="tpu_custom_call" | custom-call | tf_op jit(solution)/shard_map/last/pallas_call | solution.py:352
  (52 shorter events, 0.1 us)
Async XLA Ops:
  0.0 6.6 %copy-start = (bf16[8,8192,8]{1,2,0:T(8,128)(2,1)S(1)}, bf16[8,8192,8]{1,2,0:T(8,128)(2,1)}, u32[]{:S(2)}) copy-start(bf16[8,8192,8]{1,2,0:T(8,128)(2,1)} %param.12) | copy-start | bytes 3145732
  0.0 26.9 %copy-start.1 = (s32[2]{0:T(128)S(1)}, s32[2]{0:T(128)}, u32[]{:S(2)}) copy-start(s32[2]{0:T(128)} %param.14) | copy-start | bytes 28
  0.0 28.7 %copy-start.3 = (bf16[8192,896]{1,0:T(8,128)(2,1)S(1)}, bf16[8192,896]{1,0:T(8,128)(2,1)}, u32[]{:S(2)}) copy-start(bf16[8192,896]{1,0:T(8,128)(2,1)} %w_ref.6) | copy-start | bytes 44040196
  0.0 3.2 %collective-permute-start = (bf16[16,8192]{1,0:T(8,128)(2,1)}, bf16[16,8192]{1,0:T(8,128)(2,1)S(1)}, u32[]{:S(2)}, u32[]{:S(2)}) collective-permute-start(bf16[16,8192]{1,0:T(8,128)(2,1)} %tokens_ref.1), channel_id=1, source_target_pairs={{0,1},{1,0},{2,3},{3,2},{4,5},{5,4},{6,7},{7,6},{8,9},{9,8},{10,11... | collective-permute-start | bytes 786440 | tf_op jit(solution)/shard_map/ppermute | solution.py:405
  0.5 7.1 %collective-permute-start.1 = (bf16[16,8192]{1,0:T(8,128)(2,1)}, bf16[16,8192]{1,0:T(8,128)(2,1)S(1)}, u32[]{:S(2)}, u32[]{:S(2)}) collective-permute-start(bf16[16,8192]{1,0:T(8,128)(2,1)} %tokens_ref.1), channel_id=1, source_target_pairs={{0,4},{1,3},{4,8},{5,1},{8,12},{9,5},{12,14},{13,9},{14,10},{15,13... | collective-permute-start | bytes 786440 | tf_op jit(solution)/shard_map/ppermute | solution.py:402
  4.9 6.4 %collective-permute-start.2 = (bf16[16,8192]{1,0:T(8,128)(2,1)S(1)}, bf16[16,8192]{1,0:T(8,128)(2,1)S(1)}, u32[]{:S(2)}, u32[]{:S(2)}) collective-permute-start(bf16[16,8192]{1,0:T(8,128)(2,1)S(1)} %get-tuple-element.31.refs_1_.refs_2_), channel_id=1, source_target_pairs={{0,4},{1,3},{4,8},{5,1},{8,12},{9,5},{12,14},{13,9},{14,10},{15,13... | collective-permute-start | bytes 786440 | tf_op jit(solution)/shard_map/ppermute | solution.py:402
  6.6 20.3 %collective-permute-start.15 = (bf16[8,8,8192]{2,1,0:T(8,128)(2,1)S(1)}, bf16[8,8,8192]{2,1,0:T(8,128)(2,1)S(1)}, u32[]{:S(2)}, u32[]{:S(2)}) collective-permute-start(bf16[8,8,8192]{2,1,0:T(8,128)(2,1)S(1)} %bitcast.5), channel_id=1, source_target_pairs={{0,1},{1,0},{2,3},{3,2},{4,5},{5,4},{6,7},{7,6},{8,9},{9,8},{10,11... | collective-permute-start | bytes 3145736 | tf_op jit(solution)/shard_map/ppermute | solution.py:405
  7.7 6.5 %collective-permute-start.3 = (bf16[16,8192]{1,0:T(8,128)(2,1)S(1)}, bf16[16,8192]{1,0:T(8,128)(2,1)S(1)}, u32[]{:S(2)}, u32[]{:S(2)}) collective-permute-start(bf16[16,8192]{1,0:T(8,128)(2,1)S(1)} %collective-permute-done.1.refs_1_.refs_2_.refs_3_), channel_id=1, source_target_pairs={{0,4},{1,3},{4,8},{5,1},{8,12},{9,5},{12,14},{13,9},{14,10},{15,13... | collective-permute-start | bytes 786440 | tf_op jit(solution)/shard_map/ppermute | solution.py:402
  9.7 6.4 %collective-permute-start.8 = (bf16[16,8192]{1,0:T(8,128)(2,1)S(1)}, bf16[16,8192]{1,0:T(8,128)(2,1)S(1)}, u32[]{:S(2)}, u32[]{:S(2)}) collective-permute-start(bf16[16,8192]{1,0:T(8,128)(2,1)S(1)} %collective-permute-done.1.refs_1_.refs_2_.refs_3_), channel_id=1, source_target_pairs={{0,1},{1,0},{2,3},{3,2},{4,5},{5,4},{6,7},{7,6},{8,9},{9,8},{10,11... | collective-permute-start | bytes 786440 | tf_op jit(solution)/shard_map/ppermute | solution.py:405
  11.3 6.4 %collective-permute-start.4 = (bf16[16,8192]{1,0:T(8,128)(2,1)S(1)}, bf16[16,8192]{1,0:T(8,128)(2,1)S(1)}, u32[]{:S(2)}, u32[]{:S(2)}) collective-permute-start(bf16[16,8192]{1,0:T(8,128)(2,1)S(1)} %collective-permute-done.2.refs_2_.refs_3_.refs_4_), channel_id=1, source_target_pairs={{0,4},{1,3},{4,8},{5,1},{8,12},{9,5},{12,14},{13,9},{14,10},{15,13... | collective-permute-start | bytes 786440 | tf_op jit(solution)/shard_map/ppermute | solution.py:402
  14.1 6.4 %collective-permute-start.5 = (bf16[16,8192]{1,0:T(8,128)(2,1)S(1)}, bf16[16,8192]{1,0:T(8,128)(2,1)S(1)}, u32[]{:S(2)}, u32[]{:S(2)}) collective-permute-start(bf16[16,8192]{1,0:T(8,128)(2,1)S(1)} %collective-permute-done.3.refs_3_.refs_4_.refs_5_), channel_id=1, source_target_pairs={{0,4},{1,3},{4,8},{5,1},{8,12},{9,5},{12,14},{13,9},{14,10},{15,13... | collective-permute-start | bytes 786440 | tf_op jit(solution)/shard_map/ppermute | solution.py:402
  16.1 6.4 %collective-permute-start.9 = (bf16[16,8192]{1,0:T(8,128)(2,1)S(1)}, bf16[16,8192]{1,0:T(8,128)(2,1)S(1)}, u32[]{:S(2)}, u32[]{:S(2)}) collective-permute-start(bf16[16,8192]{1,0:T(8,128)(2,1)S(1)} %collective-permute-done.2.refs_2_.refs_3_.refs_4_), channel_id=1, source_target_pairs={{0,1},{1,0},{2,3},{3,2},{4,5},{5,4},{6,7},{7,6},{8,9},{9,8},{10,11... | collective-permute-start | bytes 786440 | tf_op jit(solution)/shard_map/ppermute | solution.py:405
  16.1 6.4 %collective-permute-start.10 = (bf16[16,8192]{1,0:T(8,128)(2,1)S(1)}, bf16[16,8192]{1,0:T(8,128)(2,1)S(1)}, u32[]{:S(2)}, u32[]{:S(2)}) collective-permute-start(bf16[16,8192]{1,0:T(8,128)(2,1)S(1)} %collective-permute-done.3.refs_3_.refs_4_.refs_5_), channel_id=1, source_target_pairs={{0,1},{1,0},{2,3},{3,2},{4,5},{5,4},{6,7},{7,6},{8,9},{9,8},{10,11... | collective-permute-start | bytes 786440 | tf_op jit(solution)/shard_map/ppermute | solution.py:405
  17.7 6.4 %collective-permute-start.6 = (bf16[16,8192]{1,0:T(8,128)(2,1)S(1)}, bf16[16,8192]{1,0:T(8,128)(2,1)S(1)}, u32[]{:S(2)}, u32[]{:S(2)}) collective-permute-start(bf16[16,8192]{1,0:T(8,128)(2,1)S(1)} %collective-permute-done.4.refs_4_.refs_5_.refs_6_), channel_id=1, source_target_pairs={{0,4},{1,3},{4,8},{5,1},{8,12},{9,5},{12,14},{13,9},{14,10},{15,13... | collective-permute-start | bytes 786440 | tf_op jit(solution)/shard_map/ppermute | solution.py:402
  20.5 6.4 %collective-permute-start.7 = (bf16[16,8192]{1,0:T(8,128)(2,1)S(1)}, bf16[16,8192]{1,0:T(8,128)(2,1)S(1)}, u32[]{:S(2)}, u32[]{:S(2)}) collective-permute-start(bf16[16,8192]{1,0:T(8,128)(2,1)S(1)} %collective-permute-done.5.refs_5_.refs_6_.refs_7_), channel_id=1, source_target_pairs={{0,4},{1,3},{4,8},{5,1},{8,12},{9,5},{12,14},{13,9},{14,10},{15,13... | collective-permute-start | bytes 786440 | tf_op jit(solution)/shard_map/ppermute | solution.py:402
  22.5 4.4 %collective-permute-start.11 = (bf16[16,8192]{1,0:T(8,128)(2,1)S(1)}, bf16[16,8192]{1,0:T(8,128)(2,1)S(1)}, u32[]{:S(2)}, u32[]{:S(2)}) collective-permute-start(bf16[16,8192]{1,0:T(8,128)(2,1)S(1)} %collective-permute-done.4.refs_4_.refs_5_.refs_6_), channel_id=1, source_target_pairs={{0,1},{1,0},{2,3},{3,2},{4,5},{5,4},{6,7},{7,6},{8,9},{9,8},{10,11... | collective-permute-start | bytes 786440 | tf_op jit(solution)/shard_map/ppermute | solution.py:405
  22.5 4.4 %collective-permute-start.12 = (bf16[16,8192]{1,0:T(8,128)(2,1)S(1)}, bf16[16,8192]{1,0:T(8,128)(2,1)S(1)}, u32[]{:S(2)}, u32[]{:S(2)}) collective-permute-start(bf16[16,8192]{1,0:T(8,128)(2,1)S(1)} %collective-permute-done.5.refs_5_.refs_6_.refs_7_), channel_id=1, source_target_pairs={{0,1},{1,0},{2,3},{3,2},{4,5},{5,4},{6,7},{7,6},{8,9},{9,8},{10,11... | collective-permute-start | bytes 786440 | tf_op jit(solution)/shard_map/ppermute | solution.py:405
  24.1 2.8 %collective-permute-start.13 = (bf16[16,8192]{1,0:T(8,128)(2,1)S(1)}, bf16[16,8192]{1,0:T(8,128)(2,1)S(1)}, u32[]{:S(2)}, u32[]{:S(2)}) collective-permute-start(bf16[16,8192]{1,0:T(8,128)(2,1)S(1)} %collective-permute-done.6.refs_6_.refs_7_.refs_8_), channel_id=1, source_target_pairs={{0,1},{1,0},{2,3},{3,2},{4,5},{5,4},{6,7},{7,6},{8,9},{9,8},{10,11... | collective-permute-start | bytes 786440 | tf_op jit(solution)/shard_map/ppermute | solution.py:405
  26.9 1.8 %collective-permute-start.14 = (bf16[16,8192]{1,0:T(8,128)(2,1)S(1)}, bf16[16,8192]{1,0:T(8,128)(2,1)S(1)}, u32[]{:S(2)}, u32[]{:S(2)}) collective-permute-start(bf16[16,8192]{1,0:T(8,128)(2,1)S(1)} %collective-permute-done.7.refs_7_.refs_8_.refs_9_), channel_id=1, source_target_pairs={{0,1},{1,0},{2,3},{3,2},{4,5},{5,4},{6,7},{7,6},{8,9},{9,8},{10,11... | collective-permute-start | bytes 786440 | tf_op jit(solution)/shard_map/ppermute | solution.py:405
  28.1 2.5 %collective-permute-start.16 = (bf16[16,256]{1,0:T(8,128)(2,1)S(1)}, bf16[16,256]{1,0:T(8,128)(2,1)S(1)}, u32[]{:S(2)}, u32[]{:S(2)}) collective-permute-start(bf16[16,256]{1,0:T(8,128)(2,1)S(1)} %get-tuple-element.32.refs_16_), channel_id=1, source_target_pairs={{0,1},{1,0},{2,3},{3,2},{4,5},{5,4},{6,7},{7,6},{8,9},{9,8},{10,11... | collective-permute-start | bytes 24584 | tf_op jit(solution)/shard_map/ppermute | solution.py:405
  28.7 7.7 %slice-start.4 = ((s8[14680064]{0:T(1024)(128)(4,1)}), s8[4194304]{0:T(1024)(128)(4,1)S(1)}, s32[]{:S(2)}) async-start(s8[14680064]{0:T(1024)(128)(4,1)} %bitcast.9), calls=%async_computation.4 | async-start | bytes 8388608
  28.7 7.7 %slice-start.5 = ((s8[14680064]{0:T(1024)(128)(4,1)}), s8[4194304]{0:T(1024)(128)(4,1)S(1)}, s32[]{:S(2)}) async-start(s8[14680064]{0:T(1024)(128)(4,1)} %bitcast.9), calls=%async_computation.5 | async-start | bytes 8388608
  30.7 5.7 %slice-start.6 = ((s8[14680064]{0:T(1024)(128)(4,1)}), s8[4194304]{0:T(1024)(128)(4,1)S(1)}, s32[]{:S(2)}) async-start(s8[14680064]{0:T(1024)(128)(4,1)} %bitcast.9), calls=%async_computation.6 | async-start | bytes 8388608
  30.7 5.7 %slice-start.7 = ((s8[14680064]{0:T(1024)(128)(4,1)}), s8[2097152]{0:T(1024)(128)(4,1)S(1)}, s32[]{:S(2)}) async-start(s8[14680064]{0:T(1024)(128)(4,1)} %bitcast.9), calls=%async_computation.7 | async-start | bytes 4194304
  30.7 4.0 %collective-permute-start.17 = (bf16[16,256]{1,0:T(8,128)(2,1)S(1)}, bf16[16,256]{1,0:T(8,128)(2,1)S(1)}, u32[]{:S(2)}, u32[]{:S(2)}) collective-permute-start(bf16[16,256]{1,0:T(8,128)(2,1)S(1)} %add.3), channel_id=1, source_target_pairs={{0,2},{1,3},{2,0},{3,1},{4,6},{5,7},{6,4},{7,5},{8,10},{9,11},{10,... | collective-permute-start | bytes 24584 | tf_op jit(solution)/shard_map/ppermute | solution.py:405
  34.7 4.1 %collective-permute-start.18 = (bf16[32,256]{1,0:T(8,128)(2,1)S(1)}, bf16[32,256]{1,0:T(8,128)(2,1)S(1)}, u32[]{:S(2)}, u32[]{:S(2)}) collective-permute-start(bf16[32,256]{1,0:T(8,128)(2,1)S(1)} %pad_maximum_fusion.2), channel_id=1, source_target_pairs={{0,4},{1,5},{2,6},{3,7},{4,0},{5,1},{6,2},{7,3},{8,12},{9,13},{10,... | collective-permute-start | bytes 49160 | tf_op jit(solution)/shard_map/ppermute | solution.py:405
  36.4 8.2 %slice-start = ((s8[14680064]{0:T(1024)(128)(4,1)}), s8[4194304]{0:T(1024)(128)(4,1)S(1)}, s32[]{:S(2)}) async-start(s8[14680064]{0:T(1024)(128)(4,1)} %bitcast.3), calls=%async_computation | async-start | bytes 8388608
  36.5 8.2 %slice-start.1 = ((s8[14680064]{0:T(1024)(128)(4,1)}), s8[4194304]{0:T(1024)(128)(4,1)S(1)}, s32[]{:S(2)}) async-start(s8[14680064]{0:T(1024)(128)(4,1)} %bitcast.3), calls=%async_computation.1 | async-start | bytes 8388608
  38.8 5.0 %collective-permute-start.19 = (bf16[64,256]{1,0:T(8,128)(2,1)S(1)}, bf16[64,256]{1,0:T(8,128)(2,1)S(1)}, u32[]{:S(2)}, u32[]{:S(2)}) collective-permute-start(bf16[64,256]{1,0:T(8,128)(2,1)S(1)} %pad_maximum_fusion.1), channel_id=1, source_target_pairs={{0,8},{1,9},{2,10},{3,11},{4,12},{5,13},{6,14},{7,15},{8,0},{9,1},... | collective-permute-start | bytes 98312 | tf_op jit(solution)/shard_map/ppermute | solution.py:405
  41.5 3.2 %slice-start.2 = ((s8[14680064]{0:T(1024)(128)(4,1)}), s8[4194304]{0:T(1024)(128)(4,1)S(1)}, s32[]{:S(2)}) async-start(s8[14680064]{0:T(1024)(128)(4,1)} %bitcast.3), calls=%async_computation.2 | async-start | bytes 8388608
  41.5 3.2 %slice-start.3 = ((s8[14680064]{0:T(1024)(128)(4,1)}), s8[2097152]{0:T(1024)(128)(4,1)S(1)}, s32[]{:S(2)}) async-start(s8[14680064]{0:T(1024)(128)(4,1)} %bitcast.3), calls=%async_computation.3 | async-start | bytes 4194304
  44.7 32.7 %copy-start.2 = (s32[2]{0:T(128)S(1)}, s32[2]{0:T(128)}, u32[]{:S(2)}) copy-start(s32[2]{0:T(128)} %param.15) | copy-start | bytes 28
  49.2 1.6 %collective-permute-start.20 = (bf16[16,8192]{1,0:T(8,128)(2,1)S(1)}, bf16[16,8192]{1,0:T(8,128)(2,1)S(1)}, u32[]{:S(2)}, u32[]{:S(2)}) collective-permute-start(bf16[16,8192]{1,0:T(8,128)(2,1)S(1)} %get-tuple-element.44), channel_id=1, source_target_pairs={{0,1},{1,0},{2,3},{3,2},{4,5},{5,4},{6,7},{7,6},{8,9},{9,8},{10,11... | collective-permute-start | bytes 786440 | tf_op jit(solution)/shard_map/ppermute | solution.py:405
  50.8 1.9 %collective-permute-start.24 = (bf16[32,8192]{1,0:T(8,128)(2,1)S(1)}, bf16[32,8192]{1,0:T(8,128)(2,1)S(1)}, u32[]{:S(2)}, u32[]{:S(2)}) collective-permute-start(bf16[32,8192]{1,0:T(8,128)(2,1)S(1)} %tie.7), channel_id=1, source_target_pairs={{0,1},{1,0},{2,3},{3,2},{4,5},{5,4},{6,7},{7,6},{8,9},{9,8},{10,11... | collective-permute-start | bytes 1572872 | tf_op jit(solution)/shard_map/ppermute | solution.py:405
  51.0 8.3 %collective-permute-start.23 = (bf16[32,8192]{1,0:T(8,128)(2,1)S(1)}, bf16[32,8192]{1,0:T(8,128)(2,1)S(1)}, u32[]{:S(2)}, u32[]{:S(2)}) collective-permute-start(bf16[32,8192]{1,0:T(8,128)(2,1)S(1)} %tie.6), channel_id=1, source_target_pairs={{0,1},{1,0},{2,3},{3,2},{4,5},{5,4},{6,7},{7,6},{8,9},{9,8},{10,11... | collective-permute-start | bytes 1572872 | tf_op jit(solution)/shard_map/ppermute | solution.py:405
  51.4 6.4 %collective-permute-start.25 = (bf16[16,8192]{1,0:T(8,128)(2,1)S(1)}, bf16[16,8192]{1,0:T(8,128)(2,1)S(1)}, u32[]{:S(2)}, u32[]{:S(2)}) collective-permute-start(bf16[16,8192]{1,0:T(8,128)(2,1)S(1)} %added.7), channel_id=1, source_target_pairs={{0,4},{1,3},{4,8},{5,1},{8,12},{9,5},{12,14},{13,9},{14,10},{15,13... | collective-permute-start | bytes 786440 | tf_op jit(solution)/shard_map/ppermute | solution.py:402
  52.8 7.8 %collective-permute-start.29 = (bf16[16,8192]{1,0:T(8,128)(2,1)S(1)}, bf16[16,8192]{1,0:T(8,128)(2,1)S(1)}, u32[]{:S(2)}, u32[]{:S(2)}) collective-permute-start(bf16[16,8192]{1,0:T(8,128)(2,1)S(1)} %added.11), channel_id=1, source_target_pairs={{0,4},{1,3},{4,8},{5,1},{8,12},{9,5},{12,14},{13,9},{14,10},{15,13... | collective-permute-start | bytes 786440 | tf_op jit(solution)/shard_map/ppermute | solution.py:402
  54.7 11.1 %collective-permute-start.22 = (bf16[32,8192]{1,0:T(8,128)(2,1)S(1)}, bf16[32,8192]{1,0:T(8,128)(2,1)S(1)}, u32[]{:S(2)}, u32[]{:S(2)}) collective-permute-start(bf16[32,8192]{1,0:T(8,128)(2,1)S(1)} %tie.5), channel_id=1, source_target_pairs={{0,1},{1,0},{2,3},{3,2},{4,5},{5,4},{6,7},{7,6},{8,9},{9,8},{10,11... | collective-permute-start | bytes 1572872 | tf_op jit(solution)/shard_map/ppermute | solution.py:405
  57.9 6.4 %collective-permute-start.26 = (bf16[16,8192]{1,0:T(8,128)(2,1)S(1)}, bf16[16,8192]{1,0:T(8,128)(2,1)S(1)}, u32[]{:S(2)}, u32[]{:S(2)}) collective-permute-start(bf16[16,8192]{1,0:T(8,128)(2,1)S(1)} %added.8), channel_id=1, source_target_pairs={{0,4},{1,3},{4,8},{5,1},{8,12},{9,5},{12,14},{13,9},{14,10},{15,13... | collective-permute-start | bytes 786440 | tf_op jit(solution)/shard_map/ppermute | solution.py:402
  60.7 6.4 %collective-permute-start.30 = (bf16[16,8192]{1,0:T(8,128)(2,1)S(1)}, bf16[16,8192]{1,0:T(8,128)(2,1)S(1)}, u32[]{:S(2)}, u32[]{:S(2)}) collective-permute-start(bf16[16,8192]{1,0:T(8,128)(2,1)S(1)} %added.12), channel_id=1, source_target_pairs={{0,4},{1,3},{4,8},{5,1},{8,12},{9,5},{12,14},{13,9},{14,10},{15,13... | collective-permute-start | bytes 786440 | tf_op jit(solution)/shard_map/ppermute | solution.py:402
  64.4 6.4 %collective-permute-start.27 = (bf16[16,8192]{1,0:T(8,128)(2,1)S(1)}, bf16[16,8192]{1,0:T(8,128)(2,1)S(1)}, u32[]{:S(2)}, u32[]{:S(2)}) collective-permute-start(bf16[16,8192]{1,0:T(8,128)(2,1)S(1)} %added.9), channel_id=1, source_target_pairs={{0,4},{1,3},{4,8},{5,1},{8,12},{9,5},{12,14},{13,9},{14,10},{15,13... | collective-permute-start | bytes 786440 | tf_op jit(solution)/shard_map/ppermute | solution.py:402
  67.3 6.4 %collective-permute-start.31 = (bf16[16,8192]{1,0:T(8,128)(2,1)S(1)}, bf16[16,8192]{1,0:T(8,128)(2,1)S(1)}, u32[]{:S(2)}, u32[]{:S(2)}) collective-permute-start(bf16[16,8192]{1,0:T(8,128)(2,1)S(1)} %added.13), channel_id=1, source_target_pairs={{0,4},{1,3},{4,8},{5,1},{8,12},{9,5},{12,14},{13,9},{14,10},{15,13... | collective-permute-start | bytes 786440 | tf_op jit(solution)/shard_map/ppermute | solution.py:402
  68.6 5.1 %collective-permute-start.21 = (bf16[16,8192]{1,0:T(8,128)(2,1)S(1)}, bf16[16,8192]{1,0:T(8,128)(2,1)S(1)}, u32[]{:S(2)}, u32[]{:S(2)}) collective-permute-start(bf16[16,8192]{1,0:T(8,128)(2,1)S(1)} %tie.4), channel_id=1, source_target_pairs={{0,1},{1,0},{2,3},{3,2},{4,5},{5,4},{6,7},{7,6},{8,9},{9,8},{10,11... | collective-permute-start | bytes 786440 | tf_op jit(solution)/shard_map/ppermute | solution.py:405
  71.0 6.4 %collective-permute-start.28 = (bf16[16,8192]{1,0:T(8,128)(2,1)S(1)}, bf16[16,8192]{1,0:T(8,128)(2,1)S(1)}, u32[]{:S(2)}, u32[]{:S(2)}) collective-permute-start(bf16[16,8192]{1,0:T(8,128)(2,1)S(1)} %added.10), channel_id=1, source_target_pairs={{0,4},{1,3},{4,8},{5,1},{8,12},{9,5},{12,14},{13,9},{14,10},{15,13... | collective-permute-start | bytes 786440 | tf_op jit(solution)/shard_map/ppermute | solution.py:402
  73.7 3.7 %collective-permute-start.32 = (bf16[16,8192]{1,0:T(8,128)(2,1)S(1)}, bf16[16,8192]{1,0:T(8,128)(2,1)S(1)}, u32[]{:S(2)}, u32[]{:S(2)}) collective-permute-start(bf16[16,8192]{1,0:T(8,128)(2,1)S(1)} %collective-permute-done.31), channel_id=1, source_target_pairs={{0,1},{1,0},{2,3},{3,2},{4,5},{5,4},{6,7},{7,6},{8,9},{9,8},{10,11... | collective-permute-start | bytes 786440 | tf_op jit(solution)/shard_map/ppermute | solution.py:405

commit v16 on v15

--- a/solution.py
+++ b/solution.py
@@ -157,20 +157,21 @@
     for i in range(slices):
         found += squares[i * height : (i + 1) * height, i * wanted : (i + 1) * wanted]
     scratch[...] = jnp.zeros_like(scratch)
+    lower = device % 2 == 0
     for index, number in enumerate(numbers):
         part = found[index * rows : (index + 1) * rows]
+        values = []
         for source in range(2):
             first = source * blocks * span
             value = part[:, first : first + span]
             for b in range(1, blocks):
                 columns = part[:, first + b * span : first + (b + 1) * span]
                 value = jnp.where(places[number] // block_rows == b, columns, value)
-            scratch[source, pl.ds(places[number], rows), :span] = value
-    own, other = scratch[0].T[:span], scratch[1].T[:span]
-    lower = device % 2 == 0
-    out_ref[...] = jnp.concatenate(
-        [jnp.where(lower, own, other), jnp.where(lower, other, own)], axis=0
-    ).astype(BF16)
+            values.append(value)
+        own, other = values
+        both = [jnp.where(lower, own, other), jnp.where(lower, other, own)]
+        scratch[pl.ds(places[number], rows), : 2 * span] = jnp.concatenate(both, axis=1)
+    out_ref[...] = scratch[...].T[: 2 * span].astype(BF16)
     for copy in copies:
         copy.wait()
 
@@ -188,7 +189,7 @@
             jax.ShapeDtypeStruct((adapters.shape[1],) + expand.shape[1:], BF16),
         ],
         scratch_shapes=[
-            pltpu.VMEM((2, total, 128), F32),
+            pltpu.VMEM((total, 128), F32),
             pltpu.SemaphoreType.DMA((adapters.shape[1],)),
         ],
         compiler_params=params(),

time: 78.5 us -> 78.5 us (level)
  no operation moved by 1% of the time
where the time goes in v16:
time: 78.5 us; the launch traced here: 78.4 us
  starting transfers between devices  32.7 us (42%)
  waiting for transfers between devices  27 us (34%)
  Pallas kernels  18.4 us (23%)
    ppermute x14, waiting for transfers between devices, step(): return lax.ppermute(x, 'tp', ring)  25.4 us
    ppermute x14, starting transfers between devices, step(): return lax.ppermute(x, 'tp', ring)  23.6 us
    ppermute x19, starting transfers between devices, cross(): return lax.ppermute(x, 'tp', crossing(members, bit))  9.11 us
    pallas_call x4, Pallas kernels, product(): pl.pallas_call(functools.partial(product_kernel, part * depth, depth, mai...  8.55 us
    pallas_call x1, Pallas kernels, down(): pl.pallas_call(functools.partial(down_kernel, groups, rows, size), in_spe...  4.5 us
    pallas_call x1, Pallas kernels, anchor(): pl.pallas_call(anchor_kernel, in_specs=[FAR, FAR], out_specs=whole(1) + [...  1.71 us
    ppermute x19, waiting for transfers between devices, cross(): return lax.ppermute(x, 'tp', crossing(members, bit))  1.58 us
  transfers between devices with their start and end apart: 33, of which 15 were waited for; matrix products, arithmetic and copies ran while one was open for 0% of the time, Pallas kernels for 15%

profile of v16, /device:TPU:0, one launch (start us, length us, event | category | flops | bytes accessed | tf_op | source)
XLA Modules:
  0.0 78.4 jit_solution(422930526771800072)
XLA Ops:
  0.0 0.5 collective-permute-start
  0.5 2.6 %collective-permute-start.1 = (bf16[16,8192]{1,0:T(8,128)(2,1)}, bf16[16,8192]{1,0:T(8,128)(2,1)S(1)}, u32[]{:S(2)}, u32[]{:S(2)}) collective-permute-start(bf16[16,8192]{1,0:T(8,128)(2,1)} %tokens_ref.1), channel_id=1, source_target_pairs={{0,4},{1,3},{4,8},{5,1},{8,12},{9,5},{12,14},{13,9},{14,10},{15,13... | collective-permute-start | bytes 786440 | tf_op jit(solution)/shard_map/ppermute | solution.py:403
  3.2 0.0 collective-permute-done.passed_in
  3.2 1.7 %anchor.1 = (bf16[16,8192]{1,0:T(8,128)(2,1)S(1)}, bf16[16,8192]{1,0:T(8,128)(2,1)S(1)}) custom-call(bf16[16,8192]{1,0:T(8,128)(2,1)} %tokens_ref.1, bf16[16,8192]{1,0:T(8,128)(2,1)S(1)} %collective-permute-done.passed_in), custom_call_target="tpu_custom_call", output_to_operand_aliasing={{1}: (1, {})} | custom-call | flops 30000001024 | tf_op jit(solution)/shard_map/anchor/pallas_call | solution.py:104
  4.9 1.7 %collective-permute-start.2 = (bf16[16,8192]{1,0:T(8,128)(2,1)S(1)}, bf16[16,8192]{1,0:T(8,128)(2,1)S(1)}, u32[]{:S(2)}, u32[]{:S(2)}) collective-permute-start(bf16[16,8192]{1,0:T(8,128)(2,1)S(1)} %get-tuple-element.31.refs_1_.refs_2_), channel_id=1, source_target_pairs={{0,4},{1,3},{4,8},{5,1},{8,12},{9,5},{12,14},{13,9},{14,10},{15,13... | collective-permute-start | bytes 786440 | tf_op jit(solution)/shard_map/ppermute | solution.py:403
  6.6 0.0 collective-permute-start.15
  6.6 1.1 %collective-permute-done.1.refs_1_.refs_2_.refs_3_ = bf16[16,8192]{1,0:T(8,128)(2,1)S(1)} collective-permute-done((bf16[16,8192]{1,0:T(8,128)(2,1)}, bf16[16,8192]{1,0:T(8,128)(2,1)S(1)}, u32[]{:S(2)}, u32[]{:S(2)}) %collective-permute-start.1) | collective-permute-done | bytes 262176 | tf_op jit(solution)/shard_map/ppermute | solution.py:403
  7.7 2.1 %collective-permute-start.3 = (bf16[16,8192]{1,0:T(8,128)(2,1)S(1)}, bf16[16,8192]{1,0:T(8,128)(2,1)S(1)}, u32[]{:S(2)}, u32[]{:S(2)}) collective-permute-start(bf16[16,8192]{1,0:T(8,128)(2,1)S(1)} %collective-permute-done.1.refs_1_.refs_2_.refs_3_), channel_id=1, source_target_pairs={{0,4},{1,3},{4,8},{5,1},{8,12},{9,5},{12,14},{13,9},{14,10},{15,13... | collective-permute-start | bytes 786440 | tf_op jit(solution)/shard_map/ppermute | solution.py:403
  9.7 0.0 collective-permute-start.8
  9.8 1.6 %collective-permute-done.2.refs_2_.refs_3_.refs_4_ = bf16[16,8192]{1,0:T(8,128)(2,1)S(1)} collective-permute-done((bf16[16,8192]{1,0:T(8,128)(2,1)S(1)}, bf16[16,8192]{1,0:T(8,128)(2,1)S(1)}, u32[]{:S(2)}, u32[]{:S(2)}) %collective-permute-start.2) | collective-permute-done | bytes 262176 | tf_op jit(solution)/shard_map/ppermute | solution.py:403
  11.3 1.7 %collective-permute-start.4 = (bf16[16,8192]{1,0:T(8,128)(2,1)S(1)}, bf16[16,8192]{1,0:T(8,128)(2,1)S(1)}, u32[]{:S(2)}, u32[]{:S(2)}) collective-permute-start(bf16[16,8192]{1,0:T(8,128)(2,1)S(1)} %collective-permute-done.2.refs_2_.refs_3_.refs_4_), channel_id=1, source_target_pairs={{0,4},{1,3},{4,8},{5,1},{8,12},{9,5},{12,14},{13,9},{14,10},{15,13... | collective-permute-start | bytes 786440 | tf_op jit(solution)/shard_map/ppermute | solution.py:403
  13.0 1.1 %collective-permute-done.3.refs_3_.refs_4_.refs_5_ = bf16[16,8192]{1,0:T(8,128)(2,1)S(1)} collective-permute-done((bf16[16,8192]{1,0:T(8,128)(2,1)S(1)}, bf16[16,8192]{1,0:T(8,128)(2,1)S(1)}, u32[]{:S(2)}, u32[]{:S(2)}) %collective-permute-start.3) | collective-permute-done | bytes 262176 | tf_op jit(solution)/shard_map/ppermute | solution.py:403
  14.1 2.0 %collective-permute-start.5 = (bf16[16,8192]{1,0:T(8,128)(2,1)S(1)}, bf16[16,8192]{1,0:T(8,128)(2,1)S(1)}, u32[]{:S(2)}, u32[]{:S(2)}) collective-permute-start(bf16[16,8192]{1,0:T(8,128)(2,1)S(1)} %collective-permute-done.3.refs_3_.refs_4_.refs_5_), channel_id=1, source_target_pairs={{0,4},{1,3},{4,8},{5,1},{8,12},{9,5},{12,14},{13,9},{14,10},{15,13... | collective-permute-start | bytes 786440 | tf_op jit(solution)/shard_map/ppermute | solution.py:403
  16.1 0.5 collective-permute-start.10
  16.6 1.1 %collective-permute-done.4.refs_4_.refs_5_.refs_6_ = bf16[16,8192]{1,0:T(8,128)(2,1)S(1)} collective-permute-done((bf16[16,8192]{1,0:T(8,128)(2,1)S(1)}, bf16[16,8192]{1,0:T(8,128)(2,1)S(1)}, u32[]{:S(2)}, u32[]{:S(2)}) %collective-permute-start.4) | collective-permute-done | bytes 262176 | tf_op jit(solution)/shard_map/ppermute | solution.py:403
  17.7 1.7 %collective-permute-start.6 = (bf16[16,8192]{1,0:T(8,128)(2,1)S(1)}, bf16[16,8192]{1,0:T(8,128)(2,1)S(1)}, u32[]{:S(2)}, u32[]{:S(2)}) collective-permute-start(bf16[16,8192]{1,0:T(8,128)(2,1)S(1)} %collective-permute-done.4.refs_4_.refs_5_.refs_6_), channel_id=1, source_target_pairs={{0,4},{1,3},{4,8},{5,1},{8,12},{9,5},{12,14},{13,9},{14,10},{15,13... | collective-permute-start | bytes 786440 | tf_op jit(solution)/shard_map/ppermute | solution.py:403
  19.4 1.1 %collective-permute-done.5.refs_5_.refs_6_.refs_7_ = bf16[16,8192]{1,0:T(8,128)(2,1)S(1)} collective-permute-done((bf16[16,8192]{1,0:T(8,128)(2,1)S(1)}, bf16[16,8192]{1,0:T(8,128)(2,1)S(1)}, u32[]{:S(2)}, u32[]{:S(2)}) %collective-permute-start.5) | collective-permute-done | bytes 262176 | tf_op jit(solution)/shard_map/ppermute | solution.py:403
  20.5 2.0 %collective-permute-start.7 = (bf16[16,8192]{1,0:T(8,128)(2,1)S(1)}, bf16[16,8192]{1,0:T(8,128)(2,1)S(1)}, u32[]{:S(2)}, u32[]{:S(2)}) collective-permute-start(bf16[16,8192]{1,0:T(8,128)(2,1)S(1)} %collective-permute-done.5.refs_5_.refs_6_.refs_7_), channel_id=1, source_target_pairs={{0,4},{1,3},{4,8},{5,1},{8,12},{9,5},{12,14},{13,9},{14,10},{15,13... | collective-permute-start | bytes 786440 | tf_op jit(solution)/shard_map/ppermute | solution.py:403
  22.5 0.0 collective-permute-done.9.refs_9_.refs_10_.refs_11_
  22.5 0.5 collective-permute-start.12
  23.0 1.0 %collective-permute-done.6.refs_6_.refs_7_.refs_8_ = bf16[16,8192]{1,0:T(8,128)(2,1)S(1)} collective-permute-done((bf16[16,8192]{1,0:T(8,128)(2,1)S(1)}, bf16[16,8192]{1,0:T(8,128)(2,1)S(1)}, u32[]{:S(2)}, u32[]{:S(2)}) %collective-permute-start.6) | collective-permute-done | bytes 262176 | tf_op jit(solution)/shard_map/ppermute | solution.py:403
  24.1 2.8 %collective-permute-done.7.refs_7_.refs_8_.refs_9_ = bf16[16,8192]{1,0:T(8,128)(2,1)S(1)} collective-permute-done((bf16[16,8192]{1,0:T(8,128)(2,1)S(1)}, bf16[16,8192]{1,0:T(8,128)(2,1)S(1)}, u32[]{:S(2)}, u32[]{:S(2)}) %collective-permute-start.7) | collective-permute-done | bytes 262176 | tf_op jit(solution)/shard_map/ppermute | solution.py:403
  26.9 1.3 %rank.1 = (bf16[16,256]{1,0:T(8,128)(2,1)S(1)}, bf16[2,128,896]{2,1,0:T(8,128)(2,1)S(1)}) custom-call(s32[1,2]{1,0:T(1,128)S(1)} %bitcast.7, bf16[8,128,896]{2,1,0:T(8,128)(2,1)} %expand_ref.1, bf16[8,8,8192]{2,1,0:T(8,128)(2,1)S(1)} %bitcast.6, bf16[8,8,8192]{2,1,0:T(8,128)(2,1)S(1)} %collective-permute-done.15.other_ref, ...), custom_call_target="tpu_custom_call" | custom-call | flops 67108864 | bytes 4194304 | tf_op jit(solution)/shard_map/rank/pallas_call | solution.py:183
  28.2 0.6 collective-permute-start.16
  28.8 2.0 %product.4 = (f32[256,768]{1,0:T(8,128)S(1)}, bf16[4096,128]{1,0:T(8,128)(2,1)S(1)}) custom-call(bf16[8192,896]{1,0:T(8,128)(2,1)S(1)} %copy-done.3, bf16[16,8192]{1,0:T(8,128)(2,1)S(1)} %get-tuple-element.30.refs_0_.refs_1_, bf16[16,8192]{1,0:T(8,128)(2,1)S(1)} %get-tuple-element.31.refs_1_.refs_2_, ...), custom_call_target="tpu_custom_call" | custom-call | flops 5637144576 | bytes 9437184 | tf_op jit(solution)/shard_map/product/pallas_call | solution.py:237
  30.7 0.0 slice-start.6
  30.8 2.0 %collective-permute-start.17 = (bf16[16,256]{1,0:T(8,128)(2,1)S(1)}, bf16[16,256]{1,0:T(8,128)(2,1)S(1)}, u32[]{:S(2)}, u32[]{:S(2)}) collective-permute-start(bf16[16,256]{1,0:T(8,128)(2,1)S(1)} %add.3), channel_id=1, source_target_pairs={{0,2},{1,3},{2,0},{3,1},{4,6},{5,7},{6,4},{7,5},{8,10},{9,11},{10,... | collective-permute-start | bytes 24584 | tf_op jit(solution)/shard_map/ppermute | solution.py:406
  32.8 1.9 %product.5 = (f32[256,768]{1,0:T(8,128)S(1)}, bf16[4096,128]{1,0:T(8,128)(2,1)S(1)}) custom-call(bf16[8192,896]{1,0:T(8,128)(2,1)S(1)} %copy-done.3, bf16[16,8192]{1,0:T(8,128)(2,1)S(1)} %get-tuple-element.30.refs_0_.refs_1_, bf16[16,8192]{1,0:T(8,128)(2,1)S(1)} %get-tuple-element.31.refs_1_.refs_2_, ...), custom_call_target="tpu_custom_call" | custom-call | flops 5637144576 | bytes 9437184 | tf_op jit(solution)/shard_map/product/pallas_call | solution.py:237
  34.7 1.8 %collective-permute-start.18 = (bf16[32,256]{1,0:T(8,128)(2,1)S(1)}, bf16[32,256]{1,0:T(8,128)(2,1)S(1)}, u32[]{:S(2)}, u32[]{:S(2)}) collective-permute-start(bf16[32,256]{1,0:T(8,128)(2,1)S(1)} %pad_maximum_fusion.2), channel_id=1, source_target_pairs={{0,4},{1,5},{2,6},{3,7},{4,0},{5,1},{6,2},{7,3},{8,12},{9,13},{10,... | collective-permute-start | bytes 49160 | tf_op jit(solution)/shard_map/ppermute | solution.py:406
  36.5 0.0 slice-start
  36.5 0.0 slice-start.1
  36.5 2.3 %product.6 = (f32[256,768]{1,0:T(8,128)S(1)}, f32[256,256]{1,0:T(8,128)S(1)}) custom-call(bf16[8192,896]{1,0:T(8,128)(2,1)S(1)} %bitcast.10, bf16[4096,128]{1,0:T(8,128)(2,1)S(1)} %get-tuple-element.35.refs_0_, bf16[16,8192]{1,0:T(8,128)(2,1)S(1)} %get-tuple-element.30.refs_0_.refs_1_, bf16[16,8192]{1,0:T(8,128)(2,1)S(1)} %get-tuple-element.31.refs_1_.refs_2_, ...), custom_call_target="tpu_custom_call" | custom-call | flops 5637144576 | bytes 9437184 | tf_op jit(solution)/shard_map/product/pallas_call | solution.py:237
  38.9 2.6 %collective-permute-start.19 = (bf16[64,256]{1,0:T(8,128)(2,1)S(1)}, bf16[64,256]{1,0:T(8,128)(2,1)S(1)}, u32[]{:S(2)}, u32[]{:S(2)}) collective-permute-start(bf16[64,256]{1,0:T(8,128)(2,1)S(1)} %pad_maximum_fusion.1), channel_id=1, source_target_pairs={{0,8},{1,9},{2,10},{3,11},{4,12},{5,13},{6,14},{7,15},{8,0},{9,1},... | collective-permute-start | bytes 98312 | tf_op jit(solution)/shard_map/ppermute | solution.py:406
  41.6 2.3 %product.7 = (f32[256,768]{1,0:T(8,128)S(1)}, f32[256,256]{1,0:T(8,128)S(1)}) custom-call(bf16[8192,896]{1,0:T(8,128)(2,1)S(1)} %bitcast.10, bf16[4096,128]{1,0:T(8,128)(2,1)S(1)} %get-tuple-element.37.refs_0_, bf16[16,8192]{1,0:T(8,128)(2,1)S(1)} %get-tuple-element.30.refs_0_.refs_1_, bf16[16,8192]{1,0:T(8,128)(2,1)S(1)} %get-tuple-element.31.refs_1_.refs_2_, ...), custom_call_target="tpu_custom_call" | custom-call | flops 5637144576 | bytes 9437184 | tf_op jit(solution)/shard_map/product/pallas_call | solution.py:237
  43.9 0.8 %finish.1.hidden_ref = bf16[256,896]{1,0:T(8,128)(2,1)S(1)} custom-call(f32[256,768]{1,0:T(8,128)S(1)} %get-tuple-element.33.refs_0_, f32[256,768]{1,0:T(8,128)S(1)} %get-tuple-element.34.refs_1_, f32[256,768]{1,0:T(8,128)S(1)} %get-tuple-element.36.refs_2_, f32[256,768]{1,0:T(8,128)S(1)} %get-tuple-element.38.refs_3_, ...), custom_call_target="tpu_custom_call" | custom-call | tf_op jit(solution)/shard_map/finish/pallas_call | solution.py:289
  44.8 0.0 copy-start.2
  44.8 4.5 %down.1 = (bf16[16,8192]{1,0:T(8,128)(2,1)S(1)}, bf16[16,8192]{1,0:T(8,128)(2,1)S(1)}, bf16[16,8192]{1,0:T(8,128)(2,1)S(1)}, bf16[16,8192]{1,0:T(8,128)(2,1)S(1)...) custom-call(bf16[896,8192]{1,0:T(8,128)(2,1)S(1)} %bitcast.4, ...), custom_call_target="tpu_custom_call" | custom-call | flops 3758096384 | bytes 18874368 | tf_op jit(solution)/shard_map/down/pallas_call | solution.py:315
  49.3 0.1 collective-permute-start.20
  49.4 1.5 %collective-permute-done.20.after_ref.refs_1_ = bf16[16,8192]{1,0:T(8,128)(2,1)S(1)} collective-permute-done((bf16[16,8192]{1,0:T(8,128)(2,1)S(1)}, bf16[16,8192]{1,0:T(8,128)(2,1)S(1)}, u32[]{:S(2)}, u32[]{:S(2)}) %collective-permute-start.20) | collective-permute-done | bytes 262176 | tf_op jit(solution)/shard_map/ppermute | solution.py:406
  50.9 0.1 collective-permute-start.24
  51.0 0.4 collective-permute-start.23
  51.4 0.1 added.7
  51.5 1.3 %collective-permute-start.25 = (bf16[16,8192]{1,0:T(8,128)(2,1)S(1)}, bf16[16,8192]{1,0:T(8,128)(2,1)S(1)}, u32[]{:S(2)}, u32[]{:S(2)}) collective-permute-start(bf16[16,8192]{1,0:T(8,128)(2,1)S(1)} %added.7), channel_id=1, source_target_pairs={{0,4},{1,3},{4,8},{5,1},{8,12},{9,5},{12,14},{13,9},{14,10},{15,13... | collective-permute-start | bytes 786440 | tf_op jit(solution)/shard_map/ppermute | solution.py:403
  52.8 0.0 collective-permute-done.24.refs_1_
  52.8 0.1 added.11
  52.9 1.9 %collective-permute-start.29 = (bf16[16,8192]{1,0:T(8,128)(2,1)S(1)}, bf16[16,8192]{1,0:T(8,128)(2,1)S(1)}, u32[]{:S(2)}, u32[]{:S(2)}) collective-permute-start(bf16[16,8192]{1,0:T(8,128)(2,1)S(1)} %added.11), channel_id=1, source_target_pairs={{0,4},{1,3},{4,8},{5,1},{8,12},{9,5},{12,14},{13,9},{14,10},{15,13... | collective-permute-start | bytes 786440 | tf_op jit(solution)/shard_map/ppermute | solution.py:403
  54.8 3.1 %collective-permute-done.25.refs_2_ = bf16[16,8192]{1,0:T(8,128)(2,1)S(1)} collective-permute-done((bf16[16,8192]{1,0:T(8,128)(2,1)S(1)}, bf16[16,8192]{1,0:T(8,128)(2,1)S(1)}, u32[]{:S(2)}, u32[]{:S(2)}) %collective-permute-start.25) | collective-permute-done | bytes 262176 | tf_op jit(solution)/shard_map/ppermute | solution.py:403
  57.9 0.1 added.8
  58.0 1.3 %collective-permute-start.26 = (bf16[16,8192]{1,0:T(8,128)(2,1)S(1)}, bf16[16,8192]{1,0:T(8,128)(2,1)S(1)}, u32[]{:S(2)}, u32[]{:S(2)}) collective-permute-start(bf16[16,8192]{1,0:T(8,128)(2,1)S(1)} %added.8), channel_id=1, source_target_pairs={{0,4},{1,3},{4,8},{5,1},{8,12},{9,5},{12,14},{13,9},{14,10},{15,13... | collective-permute-start | bytes 786440 | tf_op jit(solution)/shard_map/ppermute | solution.py:403
  59.3 1.4 %collective-permute-done.29.refs_2_ = bf16[16,8192]{1,0:T(8,128)(2,1)S(1)} collective-permute-done((bf16[16,8192]{1,0:T(8,128)(2,1)S(1)}, bf16[16,8192]{1,0:T(8,128)(2,1)S(1)}, u32[]{:S(2)}, u32[]{:S(2)}) %collective-permute-start.29) | collective-permute-done | bytes 262176 | tf_op jit(solution)/shard_map/ppermute | solution.py:403
  60.7 0.1 added.12
  60.8 1.3 %collective-permute-start.30 = (bf16[16,8192]{1,0:T(8,128)(2,1)S(1)}, bf16[16,8192]{1,0:T(8,128)(2,1)S(1)}, u32[]{:S(2)}, u32[]{:S(2)}) collective-permute-start(bf16[16,8192]{1,0:T(8,128)(2,1)S(1)} %added.12), channel_id=1, source_target_pairs={{0,4},{1,3},{4,8},{5,1},{8,12},{9,5},{12,14},{13,9},{14,10},{15,13... | collective-permute-start | bytes 786440 | tf_op jit(solution)/shard_map/ppermute | solution.py:403
  62.1 2.3 %collective-permute-done.26.refs_2_ = bf16[16,8192]{1,0:T(8,128)(2,1)S(1)} collective-permute-done((bf16[16,8192]{1,0:T(8,128)(2,1)S(1)}, bf16[16,8192]{1,0:T(8,128)(2,1)S(1)}, u32[]{:S(2)}, u32[]{:S(2)}) %collective-permute-start.26) | collective-permute-done | bytes 262176 | tf_op jit(solution)/shard_map/ppermute | solution.py:403
  64.4 0.1 added.9
  64.5 1.3 %collective-permute-start.27 = (bf16[16,8192]{1,0:T(8,128)(2,1)S(1)}, bf16[16,8192]{1,0:T(8,128)(2,1)S(1)}, u32[]{:S(2)}, u32[]{:S(2)}) collective-permute-start(bf16[16,8192]{1,0:T(8,128)(2,1)S(1)} %added.9), channel_id=1, source_target_pairs={{0,4},{1,3},{4,8},{5,1},{8,12},{9,5},{12,14},{13,9},{14,10},{15,13... | collective-permute-start | bytes 786440 | tf_op jit(solution)/shard_map/ppermute | solution.py:403
  65.8 1.4 %collective-permute-done.30.refs_2_ = bf16[16,8192]{1,0:T(8,128)(2,1)S(1)} collective-permute-done((bf16[16,8192]{1,0:T(8,128)(2,1)S(1)}, bf16[16,8192]{1,0:T(8,128)(2,1)S(1)}, u32[]{:S(2)}, u32[]{:S(2)}) %collective-permute-start.30) | collective-permute-done | bytes 262176 | tf_op jit(solution)/shard_map/ppermute | solution.py:403
  67.2 0.1 added.13
  67.3 1.3 %collective-permute-start.31 = (bf16[16,8192]{1,0:T(8,128)(2,1)S(1)}, bf16[16,8192]{1,0:T(8,128)(2,1)S(1)}, u32[]{:S(2)}, u32[]{:S(2)}) collective-permute-start(bf16[16,8192]{1,0:T(8,128)(2,1)S(1)} %added.13), channel_id=1, source_target_pairs={{0,4},{1,3},{4,8},{5,1},{8,12},{9,5},{12,14},{13,9},{14,10},{15,13... | collective-permute-start | bytes 786440 | tf_op jit(solution)/shard_map/ppermute | solution.py:403
  68.6 2.3 %collective-permute-done.27.refs_2_ = bf16[16,8192]{1,0:T(8,128)(2,1)S(1)} collective-permute-done((bf16[16,8192]{1,0:T(8,128)(2,1)S(1)}, bf16[16,8192]{1,0:T(8,128)(2,1)S(1)}, u32[]{:S(2)}, u32[]{:S(2)}) %collective-permute-start.27) | collective-permute-done | bytes 262176 | tf_op jit(solution)/shard_map/ppermute | solution.py:403
  70.9 0.1 added.10
  71.0 1.3 %collective-permute-start.28 = (bf16[16,8192]{1,0:T(8,128)(2,1)S(1)}, bf16[16,8192]{1,0:T(8,128)(2,1)S(1)}, u32[]{:S(2)}, u32[]{:S(2)}) collective-permute-start(bf16[16,8192]{1,0:T(8,128)(2,1)S(1)} %added.10), channel_id=1, source_target_pairs={{0,4},{1,3},{4,8},{5,1},{8,12},{9,5},{12,14},{13,9},{14,10},{15,13... | collective-permute-start | bytes 786440 | tf_op jit(solution)/shard_map/ppermute | solution.py:403
  72.4 1.4 %collective-permute-done.31 = bf16[16,8192]{1,0:T(8,128)(2,1)S(1)} collective-permute-done((bf16[16,8192]{1,0:T(8,128)(2,1)S(1)}, bf16[16,8192]{1,0:T(8,128)(2,1)S(1)}, u32[]{:S(2)}, u32[]{:S(2)}) %collective-permute-start.31) | collective-permute-done | bytes 262176 | tf_op jit(solution)/shard_map/ppermute | solution.py:403
  73.7 3.7 %collective-permute-done.28.refs_2_ = bf16[16,8192]{1,0:T(8,128)(2,1)S(1)} collective-permute-done((bf16[16,8192]{1,0:T(8,128)(2,1)S(1)}, bf16[16,8192]{1,0:T(8,128)(2,1)S(1)}, u32[]{:S(2)}, u32[]{:S(2)}) %collective-permute-start.28) | collective-permute-done | bytes 262176 | tf_op jit(solution)/shard_map/ppermute | solution.py:403
  77.5 0.9 %last.1 = bf16[16,8192]{1,0:T(8,128)(2,1)} custom-call(s32[1,2]{1,0:T(1,128)S(1)} %bitcast.8, bf16[16,8192]{1,0:T(8,128)(2,1)S(1)} %get-tuple-element.42.refs_0_, bf16[16,8192]{1,0:T(8,128)(2,1)S(1)} %collective-permute-done.21.refs_1_, bf16[16,8192]{1,0:T(8,128)(2,1)S(1)} %collective-permute-done.28.refs_2_, ...), custom_call_target="tpu_custom_call" | custom-call | tf_op jit(solution)/shard_map/last/pallas_call | solution.py:353
  (52 shorter events, 0.1 us)
Async XLA Ops:
  0.0 6.6 %copy-start = (bf16[8,8192,8]{1,2,0:T(8,128)(2,1)S(1)}, bf16[8,8192,8]{1,2,0:T(8,128)(2,1)}, u32[]{:S(2)}) copy-start(bf16[8,8192,8]{1,2,0:T(8,128)(2,1)} %param.12) | copy-start | bytes 3145732
  0.0 26.9 %copy-start.1 = (s32[2]{0:T(128)S(1)}, s32[2]{0:T(128)}, u32[]{:S(2)}) copy-start(s32[2]{0:T(128)} %param.14) | copy-start | bytes 28
  0.0 28.7 %copy-start.3 = (bf16[8192,896]{1,0:T(8,128)(2,1)S(1)}, bf16[8192,896]{1,0:T(8,128)(2,1)}, u32[]{:S(2)}) copy-start(bf16[8192,896]{1,0:T(8,128)(2,1)} %w_ref.6) | copy-start | bytes 44040196
  0.0 3.2 %collective-permute-start = (bf16[16,8192]{1,0:T(8,128)(2,1)}, bf16[16,8192]{1,0:T(8,128)(2,1)S(1)}, u32[]{:S(2)}, u32[]{:S(2)}) collective-permute-start(bf16[16,8192]{1,0:T(8,128)(2,1)} %tokens_ref.1), channel_id=1, source_target_pairs={{0,1},{1,0},{2,3},{3,2},{4,5},{5,4},{6,7},{7,6},{8,9},{9,8},{10,11... | collective-permute-start | bytes 786440 | tf_op jit(solution)/shard_map/ppermute | solution.py:406
  0.5 7.1 %collective-permute-start.1 = (bf16[16,8192]{1,0:T(8,128)(2,1)}, bf16[16,8192]{1,0:T(8,128)(2,1)S(1)}, u32[]{:S(2)}, u32[]{:S(2)}) collective-permute-start(bf16[16,8192]{1,0:T(8,128)(2,1)} %tokens_ref.1), channel_id=1, source_target_pairs={{0,4},{1,3},{4,8},{5,1},{8,12},{9,5},{12,14},{13,9},{14,10},{15,13... | collective-permute-start | bytes 786440 | tf_op jit(solution)/shard_map/ppermute | solution.py:403
  4.9 6.4 %collective-permute-start.2 = (bf16[16,8192]{1,0:T(8,128)(2,1)S(1)}, bf16[16,8192]{1,0:T(8,128)(2,1)S(1)}, u32[]{:S(2)}, u32[]{:S(2)}) collective-permute-start(bf16[16,8192]{1,0:T(8,128)(2,1)S(1)} %get-tuple-element.31.refs_1_.refs_2_), channel_id=1, source_target_pairs={{0,4},{1,3},{4,8},{5,1},{8,12},{9,5},{12,14},{13,9},{14,10},{15,13... | collective-permute-start | bytes 786440 | tf_op jit(solution)/shard_map/ppermute | solution.py:403
  6.6 20.3 %collective-permute-start.15 = (bf16[8,8,8192]{2,1,0:T(8,128)(2,1)S(1)}, bf16[8,8,8192]{2,1,0:T(8,128)(2,1)S(1)}, u32[]{:S(2)}, u32[]{:S(2)}) collective-permute-start(bf16[8,8,8192]{2,1,0:T(8,128)(2,1)S(1)} %bitcast.5), channel_id=1, source_target_pairs={{0,1},{1,0},{2,3},{3,2},{4,5},{5,4},{6,7},{7,6},{8,9},{9,8},{10,11... | collective-permute-start | bytes 3145736 | tf_op jit(solution)/shard_map/ppermute | solution.py:406
  7.7 6.5 %collective-permute-start.3 = (bf16[16,8192]{1,0:T(8,128)(2,1)S(1)}, bf16[16,8192]{1,0:T(8,128)(2,1)S(1)}, u32[]{:S(2)}, u32[]{:S(2)}) collective-permute-start(bf16[16,8192]{1,0:T(8,128)(2,1)S(1)} %collective-permute-done.1.refs_1_.refs_2_.refs_3_), channel_id=1, source_target_pairs={{0,4},{1,3},{4,8},{5,1},{8,12},{9,5},{12,14},{13,9},{14,10},{15,13... | collective-permute-start | bytes 786440 | tf_op jit(solution)/shard_map/ppermute | solution.py:403
  9.7 6.4 %collective-permute-start.8 = (bf16[16,8192]{1,0:T(8,128)(2,1)S(1)}, bf16[16,8192]{1,0:T(8,128)(2,1)S(1)}, u32[]{:S(2)}, u32[]{:S(2)}) collective-permute-start(bf16[16,8192]{1,0:T(8,128)(2,1)S(1)} %collective-permute-done.1.refs_1_.refs_2_.refs_3_), channel_id=1, source_target_pairs={{0,1},{1,0},{2,3},{3,2},{4,5},{5,4},{6,7},{7,6},{8,9},{9,8},{10,11... | collective-permute-start | bytes 786440 | tf_op jit(solution)/shard_map/ppermute | solution.py:406
  11.3 6.4 %collective-permute-start.4 = (bf16[16,8192]{1,0:T(8,128)(2,1)S(1)}, bf16[16,8192]{1,0:T(8,128)(2,1)S(1)}, u32[]{:S(2)}, u32[]{:S(2)}) collective-permute-start(bf16[16,8192]{1,0:T(8,128)(2,1)S(1)} %collective-permute-done.2.refs_2_.refs_3_.refs_4_), channel_id=1, source_target_pairs={{0,4},{1,3},{4,8},{5,1},{8,12},{9,5},{12,14},{13,9},{14,10},{15,13... | collective-permute-start | bytes 786440 | tf_op jit(solution)/shard_map/ppermute | solution.py:403
  14.1 6.4 %collective-permute-start.5 = (bf16[16,8192]{1,0:T(8,128)(2,1)S(1)}, bf16[16,8192]{1,0:T(8,128)(2,1)S(1)}, u32[]{:S(2)}, u32[]{:S(2)}) collective-permute-start(bf16[16,8192]{1,0:T(8,128)(2,1)S(1)} %collective-permute-done.3.refs_3_.refs_4_.refs_5_), channel_id=1, source_target_pairs={{0,4},{1,3},{4,8},{5,1},{8,12},{9,5},{12,14},{13,9},{14,10},{15,13... | collective-permute-start | bytes 786440 | tf_op jit(solution)/shard_map/ppermute | solution.py:403
  16.1 6.4 %collective-permute-start.9 = (bf16[16,8192]{1,0:T(8,128)(2,1)S(1)}, bf16[16,8192]{1,0:T(8,128)(2,1)S(1)}, u32[]{:S(2)}, u32[]{:S(2)}) collective-permute-start(bf16[16,8192]{1,0:T(8,128)(2,1)S(1)} %collective-permute-done.2.refs_2_.refs_3_.refs_4_), channel_id=1, source_target_pairs={{0,1},{1,0},{2,3},{3,2},{4,5},{5,4},{6,7},{7,6},{8,9},{9,8},{10,11... | collective-permute-start | bytes 786440 | tf_op jit(solution)/shard_map/ppermute | solution.py:406
  16.1 6.4 %collective-permute-start.10 = (bf16[16,8192]{1,0:T(8,128)(2,1)S(1)}, bf16[16,8192]{1,0:T(8,128)(2,1)S(1)}, u32[]{:S(2)}, u32[]{:S(2)}) collective-permute-start(bf16[16,8192]{1,0:T(8,128)(2,1)S(1)} %collective-permute-done.3.refs_3_.refs_4_.refs_5_), channel_id=1, source_target_pairs={{0,1},{1,0},{2,3},{3,2},{4,5},{5,4},{6,7},{7,6},{8,9},{9,8},{10,11... | collective-permute-start | bytes 786440 | tf_op jit(solution)/shard_map/ppermute | solution.py:406
  17.7 6.4 %collective-permute-start.6 = (bf16[16,8192]{1,0:T(8,128)(2,1)S(1)}, bf16[16,8192]{1,0:T(8,128)(2,1)S(1)}, u32[]{:S(2)}, u32[]{:S(2)}) collective-permute-start(bf16[16,8192]{1,0:T(8,128)(2,1)S(1)} %collective-permute-done.4.refs_4_.refs_5_.refs_6_), channel_id=1, source_target_pairs={{0,4},{1,3},{4,8},{5,1},{8,12},{9,5},{12,14},{13,9},{14,10},{15,13... | collective-permute-start | bytes 786440 | tf_op jit(solution)/shard_map/ppermute | solution.py:403
  20.5 6.4 %collective-permute-start.7 = (bf16[16,8192]{1,0:T(8,128)(2,1)S(1)}, bf16[16,8192]{1,0:T(8,128)(2,1)S(1)}, u32[]{:S(2)}, u32[]{:S(2)}) collective-permute-start(bf16[16,8192]{1,0:T(8,128)(2,1)S(1)} %collective-permute-done.5.refs_5_.refs_6_.refs_7_), channel_id=1, source_target_pairs={{0,4},{1,3},{4,8},{5,1},{8,12},{9,5},{12,14},{13,9},{14,10},{15,13... | collective-permute-start | bytes 786440 | tf_op jit(solution)/shard_map/ppermute | solution.py:403
  22.5 4.4 %collective-permute-start.11 = (bf16[16,8192]{1,0:T(8,128)(2,1)S(1)}, bf16[16,8192]{1,0:T(8,128)(2,1)S(1)}, u32[]{:S(2)}, u32[]{:S(2)}) collective-permute-start(bf16[16,8192]{1,0:T(8,128)(2,1)S(1)} %collective-permute-done.4.refs_4_.refs_5_.refs_6_), channel_id=1, source_target_pairs={{0,1},{1,0},{2,3},{3,2},{4,5},{5,4},{6,7},{7,6},{8,9},{9,8},{10,11... | collective-permute-start | bytes 786440 | tf_op jit(solution)/shard_map/ppermute | solution.py:406
  22.5 4.4 %collective-permute-start.12 = (bf16[16,8192]{1,0:T(8,128)(2,1)S(1)}, bf16[16,8192]{1,0:T(8,128)(2,1)S(1)}, u32[]{:S(2)}, u32[]{:S(2)}) collective-permute-start(bf16[16,8192]{1,0:T(8,128)(2,1)S(1)} %collective-permute-done.5.refs_5_.refs_6_.refs_7_), channel_id=1, source_target_pairs={{0,1},{1,0},{2,3},{3,2},{4,5},{5,4},{6,7},{7,6},{8,9},{9,8},{10,11... | collective-permute-start | bytes 786440 | tf_op jit(solution)/shard_map/ppermute | solution.py:406
  24.1 2.8 %collective-permute-start.13 = (bf16[16,8192]{1,0:T(8,128)(2,1)S(1)}, bf16[16,8192]{1,0:T(8,128)(2,1)S(1)}, u32[]{:S(2)}, u32[]{:S(2)}) collective-permute-start(bf16[16,8192]{1,0:T(8,128)(2,1)S(1)} %collective-permute-done.6.refs_6_.refs_7_.refs_8_), channel_id=1, source_target_pairs={{0,1},{1,0},{2,3},{3,2},{4,5},{5,4},{6,7},{7,6},{8,9},{9,8},{10,11... | collective-permute-start | bytes 786440 | tf_op jit(solution)/shard_map/ppermute | solution.py:406
  26.9 1.9 %collective-permute-start.14 = (bf16[16,8192]{1,0:T(8,128)(2,1)S(1)}, bf16[16,8192]{1,0:T(8,128)(2,1)S(1)}, u32[]{:S(2)}, u32[]{:S(2)}) collective-permute-start(bf16[16,8192]{1,0:T(8,128)(2,1)S(1)} %collective-permute-done.7.refs_7_.refs_8_.refs_9_), channel_id=1, source_target_pairs={{0,1},{1,0},{2,3},{3,2},{4,5},{5,4},{6,7},{7,6},{8,9},{9,8},{10,11... | collective-permute-start | bytes 786440 | tf_op jit(solution)/shard_map/ppermute | solution.py:406
  28.2 2.5 %collective-permute-start.16 = (bf16[16,256]{1,0:T(8,128)(2,1)S(1)}, bf16[16,256]{1,0:T(8,128)(2,1)S(1)}, u32[]{:S(2)}, u32[]{:S(2)}) collective-permute-start(bf16[16,256]{1,0:T(8,128)(2,1)S(1)} %get-tuple-element.32.refs_16_), channel_id=1, source_target_pairs={{0,1},{1,0},{2,3},{3,2},{4,5},{5,4},{6,7},{7,6},{8,9},{9,8},{10,11... | collective-permute-start | bytes 24584 | tf_op jit(solution)/shard_map/ppermute | solution.py:406
  28.7 7.7 %slice-start.4 = ((s8[14680064]{0:T(1024)(128)(4,1)}), s8[4194304]{0:T(1024)(128)(4,1)S(1)}, s32[]{:S(2)}) async-start(s8[14680064]{0:T(1024)(128)(4,1)} %bitcast.9), calls=%async_computation.4 | async-start | bytes 8388608
  28.7 7.7 %slice-start.5 = ((s8[14680064]{0:T(1024)(128)(4,1)}), s8[4194304]{0:T(1024)(128)(4,1)S(1)}, s32[]{:S(2)}) async-start(s8[14680064]{0:T(1024)(128)(4,1)} %bitcast.9), calls=%async_computation.5 | async-start | bytes 8388608
  30.7 5.8 %slice-start.6 = ((s8[14680064]{0:T(1024)(128)(4,1)}), s8[4194304]{0:T(1024)(128)(4,1)S(1)}, s32[]{:S(2)}) async-start(s8[14680064]{0:T(1024)(128)(4,1)} %bitcast.9), calls=%async_computation.6 | async-start | bytes 8388608
  30.8 5.7 %slice-start.7 = ((s8[14680064]{0:T(1024)(128)(4,1)}), s8[2097152]{0:T(1024)(128)(4,1)S(1)}, s32[]{:S(2)}) async-start(s8[14680064]{0:T(1024)(128)(4,1)} %bitcast.9), calls=%async_computation.7 | async-start | bytes 4194304
  30.8 4.0 %collective-permute-start.17 = (bf16[16,256]{1,0:T(8,128)(2,1)S(1)}, bf16[16,256]{1,0:T(8,128)(2,1)S(1)}, u32[]{:S(2)}, u32[]{:S(2)}) collective-permute-start(bf16[16,256]{1,0:T(8,128)(2,1)S(1)} %add.3), channel_id=1, source_target_pairs={{0,2},{1,3},{2,0},{3,1},{4,6},{5,7},{6,4},{7,5},{8,10},{9,11},{10,... | collective-permute-start | bytes 24584 | tf_op jit(solution)/shard_map/ppermute | solution.py:406
  34.7 4.1 %collective-permute-start.18 = (bf16[32,256]{1,0:T(8,128)(2,1)S(1)}, bf16[32,256]{1,0:T(8,128)(2,1)S(1)}, u32[]{:S(2)}, u32[]{:S(2)}) collective-permute-start(bf16[32,256]{1,0:T(8,128)(2,1)S(1)} %pad_maximum_fusion.2), channel_id=1, source_target_pairs={{0,4},{1,5},{2,6},{3,7},{4,0},{5,1},{6,2},{7,3},{8,12},{9,13},{10,... | collective-permute-start | bytes 49160 | tf_op jit(solution)/shard_map/ppermute | solution.py:406
  36.5 8.2 %slice-start = ((s8[14680064]{0:T(1024)(128)(4,1)}), s8[4194304]{0:T(1024)(128)(4,1)S(1)}, s32[]{:S(2)}) async-start(s8[14680064]{0:T(1024)(128)(4,1)} %bitcast.3), calls=%async_computation | async-start | bytes 8388608
  36.5 8.2 %slice-start.1 = ((s8[14680064]{0:T(1024)(128)(4,1)}), s8[4194304]{0:T(1024)(128)(4,1)S(1)}, s32[]{:S(2)}) async-start(s8[14680064]{0:T(1024)(128)(4,1)} %bitcast.3), calls=%async_computation.1 | async-start | bytes 8388608
  38.9 5.0 %collective-permute-start.19 = (bf16[64,256]{1,0:T(8,128)(2,1)S(1)}, bf16[64,256]{1,0:T(8,128)(2,1)S(1)}, u32[]{:S(2)}, u32[]{:S(2)}) collective-permute-start(bf16[64,256]{1,0:T(8,128)(2,1)S(1)} %pad_maximum_fusion.1), channel_id=1, source_target_pairs={{0,8},{1,9},{2,10},{3,11},{4,12},{5,13},{6,14},{7,15},{8,0},{9,1},... | collective-permute-start | bytes 98312 | tf_op jit(solution)/shard_map/ppermute | solution.py:406
  41.5 3.2 %slice-start.2 = ((s8[14680064]{0:T(1024)(128)(4,1)}), s8[4194304]{0:T(1024)(128)(4,1)S(1)}, s32[]{:S(2)}) async-start(s8[14680064]{0:T(1024)(128)(4,1)} %bitcast.3), calls=%async_computation.2 | async-start | bytes 8388608
  41.6 3.2 %slice-start.3 = ((s8[14680064]{0:T(1024)(128)(4,1)}), s8[2097152]{0:T(1024)(128)(4,1)S(1)}, s32[]{:S(2)}) async-start(s8[14680064]{0:T(1024)(128)(4,1)} %bitcast.3), calls=%async_computation.3 | async-start | bytes 4194304
  44.8 32.7 %copy-start.2 = (s32[2]{0:T(128)S(1)}, s32[2]{0:T(128)}, u32[]{:S(2)}) copy-start(s32[2]{0:T(128)} %param.15) | copy-start | bytes 28
  49.3 1.6 %collective-permute-start.20 = (bf16[16,8192]{1,0:T(8,128)(2,1)S(1)}, bf16[16,8192]{1,0:T(8,128)(2,1)S(1)}, u32[]{:S(2)}, u32[]{:S(2)}) collective-permute-start(bf16[16,8192]{1,0:T(8,128)(2,1)S(1)} %get-tuple-element.44), channel_id=1, source_target_pairs={{0,1},{1,0},{2,3},{3,2},{4,5},{5,4},{6,7},{7,6},{8,9},{9,8},{10,11... | collective-permute-start | bytes 786440 | tf_op jit(solution)/shard_map/ppermute | solution.py:406
  50.9 1.9 %collective-permute-start.24 = (bf16[32,8192]{1,0:T(8,128)(2,1)S(1)}, bf16[32,8192]{1,0:T(8,128)(2,1)S(1)}, u32[]{:S(2)}, u32[]{:S(2)}) collective-permute-start(bf16[32,8192]{1,0:T(8,128)(2,1)S(1)} %tie.7), channel_id=1, source_target_pairs={{0,1},{1,0},{2,3},{3,2},{4,5},{5,4},{6,7},{7,6},{8,9},{9,8},{10,11... | collective-permute-start | bytes 1572872 | tf_op jit(solution)/shard_map/ppermute | solution.py:406
  51.0 8.3 %collective-permute-start.23 = (bf16[32,8192]{1,0:T(8,128)(2,1)S(1)}, bf16[32,8192]{1,0:T(8,128)(2,1)S(1)}, u32[]{:S(2)}, u32[]{:S(2)}) collective-permute-start(bf16[32,8192]{1,0:T(8,128)(2,1)S(1)} %tie.6), channel_id=1, source_target_pairs={{0,1},{1,0},{2,3},{3,2},{4,5},{5,4},{6,7},{7,6},{8,9},{9,8},{10,11... | collective-permute-start | bytes 1572872 | tf_op jit(solution)/shard_map/ppermute | solution.py:406
  51.5 6.4 %collective-permute-start.25 = (bf16[16,8192]{1,0:T(8,128)(2,1)S(1)}, bf16[16,8192]{1,0:T(8,128)(2,1)S(1)}, u32[]{:S(2)}, u32[]{:S(2)}) collective-permute-start(bf16[16,8192]{1,0:T(8,128)(2,1)S(1)} %added.7), channel_id=1, source_target_pairs={{0,4},{1,3},{4,8},{5,1},{8,12},{9,5},{12,14},{13,9},{14,10},{15,13... | collective-permute-start | bytes 786440 | tf_op jit(solution)/shard_map/ppermute | solution.py:403
  52.9 7.8 %collective-permute-start.29 = (bf16[16,8192]{1,0:T(8,128)(2,1)S(1)}, bf16[16,8192]{1,0:T(8,128)(2,1)S(1)}, u32[]{:S(2)}, u32[]{:S(2)}) collective-permute-start(bf16[16,8192]{1,0:T(8,128)(2,1)S(1)} %added.11), channel_id=1, source_target_pairs={{0,4},{1,3},{4,8},{5,1},{8,12},{9,5},{12,14},{13,9},{14,10},{15,13... | collective-permute-start | bytes 786440 | tf_op jit(solution)/shard_map/ppermute | solution.py:403
  54.8 11.1 %collective-permute-start.22 = (bf16[32,8192]{1,0:T(8,128)(2,1)S(1)}, bf16[32,8192]{1,0:T(8,128)(2,1)S(1)}, u32[]{:S(2)}, u32[]{:S(2)}) collective-permute-start(bf16[32,8192]{1,0:T(8,128)(2,1)S(1)} %tie.5), channel_id=1, source_target_pairs={{0,1},{1,0},{2,3},{3,2},{4,5},{5,4},{6,7},{7,6},{8,9},{9,8},{10,11... | collective-permute-start | bytes 1572872 | tf_op jit(solution)/shard_map/ppermute | solution.py:406
  58.0 6.4 %collective-permute-start.26 = (bf16[16,8192]{1,0:T(8,128)(2,1)S(1)}, bf16[16,8192]{1,0:T(8,128)(2,1)S(1)}, u32[]{:S(2)}, u32[]{:S(2)}) collective-permute-start(bf16[16,8192]{1,0:T(8,128)(2,1)S(1)} %added.8), channel_id=1, source_target_pairs={{0,4},{1,3},{4,8},{5,1},{8,12},{9,5},{12,14},{13,9},{14,10},{15,13... | collective-permute-start | bytes 786440 | tf_op jit(solution)/shard_map/ppermute | solution.py:403
  60.8 6.4 %collective-permute-start.30 = (bf16[16,8192]{1,0:T(8,128)(2,1)S(1)}, bf16[16,8192]{1,0:T(8,128)(2,1)S(1)}, u32[]{:S(2)}, u32[]{:S(2)}) collective-permute-start(bf16[16,8192]{1,0:T(8,128)(2,1)S(1)} %added.12), channel_id=1, source_target_pairs={{0,4},{1,3},{4,8},{5,1},{8,12},{9,5},{12,14},{13,9},{14,10},{15,13... | collective-permute-start | bytes 786440 | tf_op jit(solution)/shard_map/ppermute | solution.py:403
  64.5 6.4 %collective-permute-start.27 = (bf16[16,8192]{1,0:T(8,128)(2,1)S(1)}, bf16[16,8192]{1,0:T(8,128)(2,1)S(1)}, u32[]{:S(2)}, u32[]{:S(2)}) collective-permute-start(bf16[16,8192]{1,0:T(8,128)(2,1)S(1)} %added.9), channel_id=1, source_target_pairs={{0,4},{1,3},{4,8},{5,1},{8,12},{9,5},{12,14},{13,9},{14,10},{15,13... | collective-permute-start | bytes 786440 | tf_op jit(solution)/shard_map/ppermute | solution.py:403
  67.3 6.4 %collective-permute-start.31 = (bf16[16,8192]{1,0:T(8,128)(2,1)S(1)}, bf16[16,8192]{1,0:T(8,128)(2,1)S(1)}, u32[]{:S(2)}, u32[]{:S(2)}) collective-permute-start(bf16[16,8192]{1,0:T(8,128)(2,1)S(1)} %added.13), channel_id=1, source_target_pairs={{0,4},{1,3},{4,8},{5,1},{8,12},{9,5},{12,14},{13,9},{14,10},{15,13... | collective-permute-start | bytes 786440 | tf_op jit(solution)/shard_map/ppermute | solution.py:403
  68.6 5.1 %collective-permute-start.21 = (bf16[16,8192]{1,0:T(8,128)(2,1)S(1)}, bf16[16,8192]{1,0:T(8,128)(2,1)S(1)}, u32[]{:S(2)}, u32[]{:S(2)}) collective-permute-start(bf16[16,8192]{1,0:T(8,128)(2,1)S(1)} %tie.4), channel_id=1, source_target_pairs={{0,1},{1,0},{2,3},{3,2},{4,5},{5,4},{6,7},{7,6},{8,9},{9,8},{10,11... | collective-permute-start | bytes 786440 | tf_op jit(solution)/shard_map/ppermute | solution.py:406
  71.0 6.4 %collective-permute-start.28 = (bf16[16,8192]{1,0:T(8,128)(2,1)S(1)}, bf16[16,8192]{1,0:T(8,128)(2,1)S(1)}, u32[]{:S(2)}, u32[]{:S(2)}) collective-permute-start(bf16[16,8192]{1,0:T(8,128)(2,1)S(1)} %added.10), channel_id=1, source_target_pairs={{0,4},{1,3},{4,8},{5,1},{8,12},{9,5},{12,14},{13,9},{14,10},{15,13... | collective-permute-start | bytes 786440 | tf_op jit(solution)/shard_map/ppermute | solution.py:403
  73.7 3.7 %collective-permute-start.32 = (bf16[16,8192]{1,0:T(8,128)(2,1)S(1)}, bf16[16,8192]{1,0:T(8,128)(2,1)S(1)}, u32[]{:S(2)}, u32[]{:S(2)}) collective-permute-start(bf16[16,8192]{1,0:T(8,128)(2,1)S(1)} %collective-permute-done.31), channel_id=1, source_target_pairs={{0,1},{1,0},{2,3},{3,2},{4,5},{5,4},{6,7},{7,6},{8,9},{9,8},{10,11... | collective-permute-start | bytes 786440 | tf_op jit(solution)/shard_map/ppermute | solution.py:406

commit v17 on v15

--- a/solution.py
+++ b/solution.py
@@ -244,7 +244,7 @@
     )(matrix, *extra, *pieces, after)
 
 
-def finish_kernel(span, piece_rows, *refs):
+def finish_kernel(span, piece_rows, steps, *refs):
     *products, rank_ref, expand_ref, out_ref, hidden_ref = refs
     gate_a, gate_b, up_a, up_b, *tails = products
     ranks = rank_ref.shape[0]
@@ -252,7 +252,10 @@
     shape = (ranks, ranks)
     want = lax.broadcasted_iota(jnp.int32, shape, 0)
     have = lax.broadcasted_iota(jnp.int32, shape, 1)
-    origin = ((have // span) ^ chip) * span + have % span
+    away = 0
+    for place, step in enumerate(steps):
+        away += ((have // span) >> place) % 2 * step
+    origin = (away ^ chip) * span + have % span
     order = jnp.where(want == origin, 1.0, 0.0).astype(BF16)
     rank = jnp.dot(order, rank_ref[...], preferred_element_type=F32).T.astype(BF16)
     half = ranks // 2
@@ -283,10 +286,10 @@
         ]
 
 
-def finish(products, rank, expand, span, piece_rows):
+def finish(products, rank, expand, span, piece_rows, steps):
     total, width = products[0].shape[0], expand.shape[2]
     return pl.pallas_call(
-        functools.partial(finish_kernel, span, piece_rows),
+        functools.partial(finish_kernel, span, piece_rows, steps),
         in_specs=whole(len(products) + 2),
         out_specs=whole(1)[0],
         out_shape=jax.ShapeDtypeStruct((total, width), BF16),
@@ -432,8 +435,9 @@
         theirs[:-1],
     )
     work = [(gate_matrix, 0), (gate_matrix, 1), (up_matrix, 0), (up_matrix, 1)]
-    products, aside, after, bit = [], [0, 0], rank, 1
-    while bit < members or work:
+    rounds = [1] + [1 << i for i in range(members.bit_length() - 2, 0, -1)]
+    products, aside, after, left_over = [], [0, 0], rank, list(rounds)
+    while left_over or work:
         if work:
             matrix, part = work.pop(0)
             result, *left = product(
@@ -441,12 +445,12 @@
             )
             aside[part] = left[0] if left else None
             products.append(result)
-        if bit < members:
+        if left_over:
+            bit = left_over.pop(0)
             after = cross(rank, bit)
             rank = rank + after if bit == 1 else jnp.concatenate([rank, after], axis=0)
-            bit *= 2
     products += [x for x in aside if x is not None]
-    hidden = finish(products, rank, expand, 2 * span, rows)
+    hidden = finish(products, rank, expand, 2 * span, rows, [bit // 2 for bit in rounds[1:]])
 
     slots = 2 * reach
     groups = [1] * slots + [1] + [2] * (reach - 1) + [1]

time: 78.5 us -> 78.4 us (level)
  no operation moved by 1% of the time
where the time goes in v17:
time: 78.4 us; the launch traced here: 78.3 us
  starting transfers between devices  32.5 us (41%)
  waiting for transfers between devices  27.1 us (35%)
  Pallas kernels  18.3 us (23%)
    ppermute x14, waiting for transfers between devices, step(): return lax.ppermute(x, 'tp', ring)  25.5 us
    ppermute x14, starting transfers between devices, step(): return lax.ppermute(x, 'tp', ring)  23.5 us
    ppermute x19, starting transfers between devices, cross(): return lax.ppermute(x, 'tp', crossing(members, bit))  9.01 us
    pallas_call x4, Pallas kernels, product(): pl.pallas_call(functools.partial(product_kernel, part * depth, depth, mai...  8.56 us
    pallas_call x1, Pallas kernels, down(): pl.pallas_call(functools.partial(down_kernel, groups, rows, size), in_spe...  4.5 us
    pallas_call x1, Pallas kernels, anchor(): pl.pallas_call(anchor_kernel, in_specs=[FAR, FAR], out_specs=whole(1) + [...  1.71 us
    ppermute x19, waiting for transfers between devices, cross(): return lax.ppermute(x, 'tp', crossing(members, bit))  1.63 us
  transfers between devices with their start and end apart: 33, of which 15 were waited for; matrix products, arithmetic and copies ran while one was open for 0% of the time, Pallas kernels for 15%

profile of v17, /device:TPU:0, one launch (start us, length us, event | category | flops | bytes accessed | tf_op | source)
XLA Modules:
  0.0 78.3 jit_solution(1189474481512250830)
XLA Ops:
  0.0 0.5 collective-permute-start
  0.5 2.6 %collective-permute-start.1 = (bf16[16,8192]{1,0:T(8,128)(2,1)}, bf16[16,8192]{1,0:T(8,128)(2,1)S(1)}, u32[]{:S(2)}, u32[]{:S(2)}) collective-permute-start(bf16[16,8192]{1,0:T(8,128)(2,1)} %tokens_ref.1), channel_id=1, source_target_pairs={{0,4},{1,3},{4,8},{5,1},{8,12},{9,5},{12,14},{13,9},{14,10},{15,13... | collective-permute-start | bytes 786440 | tf_op jit(solution)/shard_map/ppermute | solution.py:405
  3.2 1.7 %anchor.1 = (bf16[16,8192]{1,0:T(8,128)(2,1)S(1)}, bf16[16,8192]{1,0:T(8,128)(2,1)S(1)}) custom-call(bf16[16,8192]{1,0:T(8,128)(2,1)} %tokens_ref.1, bf16[16,8192]{1,0:T(8,128)(2,1)S(1)} %collective-permute-done.passed_in), custom_call_target="tpu_custom_call", output_to_operand_aliasing={{1}: (1, {})} | custom-call | flops 30000001024 | tf_op jit(solution)/shard_map/anchor/pallas_call | solution.py:104
  4.9 1.7 %collective-permute-start.2 = (bf16[16,8192]{1,0:T(8,128)(2,1)S(1)}, bf16[16,8192]{1,0:T(8,128)(2,1)S(1)}, u32[]{:S(2)}, u32[]{:S(2)}) collective-permute-start(bf16[16,8192]{1,0:T(8,128)(2,1)S(1)} %get-tuple-element.31.refs_1_.refs_2_), channel_id=1, source_target_pairs={{0,4},{1,3},{4,8},{5,1},{8,12},{9,5},{12,14},{13,9},{14,10},{15,13... | collective-permute-start | bytes 786440 | tf_op jit(solution)/shard_map/ppermute | solution.py:405
  6.6 1.1 %collective-permute-done.1.refs_1_.refs_2_.refs_3_ = bf16[16,8192]{1,0:T(8,128)(2,1)S(1)} collective-permute-done((bf16[16,8192]{1,0:T(8,128)(2,1)}, bf16[16,8192]{1,0:T(8,128)(2,1)S(1)}, u32[]{:S(2)}, u32[]{:S(2)}) %collective-permute-start.1) | collective-permute-done | bytes 262176 | tf_op jit(solution)/shard_map/ppermute | solution.py:405
  7.7 2.1 %collective-permute-start.3 = (bf16[16,8192]{1,0:T(8,128)(2,1)S(1)}, bf16[16,8192]{1,0:T(8,128)(2,1)S(1)}, u32[]{:S(2)}, u32[]{:S(2)}) collective-permute-start(bf16[16,8192]{1,0:T(8,128)(2,1)S(1)} %collective-permute-done.1.refs_1_.refs_2_.refs_3_), channel_id=1, source_target_pairs={{0,4},{1,3},{4,8},{5,1},{8,12},{9,5},{12,14},{13,9},{14,10},{15,13... | collective-permute-start | bytes 786440 | tf_op jit(solution)/shard_map/ppermute | solution.py:405
  9.7 0.0 collective-permute-start.8
  9.8 1.6 %collective-permute-done.2.refs_2_.refs_3_.refs_4_ = bf16[16,8192]{1,0:T(8,128)(2,1)S(1)} collective-permute-done((bf16[16,8192]{1,0:T(8,128)(2,1)S(1)}, bf16[16,8192]{1,0:T(8,128)(2,1)S(1)}, u32[]{:S(2)}, u32[]{:S(2)}) %collective-permute-start.2) | collective-permute-done | bytes 262176 | tf_op jit(solution)/shard_map/ppermute | solution.py:405
  11.3 1.7 %collective-permute-start.4 = (bf16[16,8192]{1,0:T(8,128)(2,1)S(1)}, bf16[16,8192]{1,0:T(8,128)(2,1)S(1)}, u32[]{:S(2)}, u32[]{:S(2)}) collective-permute-start(bf16[16,8192]{1,0:T(8,128)(2,1)S(1)} %collective-permute-done.2.refs_2_.refs_3_.refs_4_), channel_id=1, source_target_pairs={{0,4},{1,3},{4,8},{5,1},{8,12},{9,5},{12,14},{13,9},{14,10},{15,13... | collective-permute-start | bytes 786440 | tf_op jit(solution)/shard_map/ppermute | solution.py:405
  13.0 1.1 %collective-permute-done.3.refs_3_.refs_4_.refs_5_ = bf16[16,8192]{1,0:T(8,128)(2,1)S(1)} collective-permute-done((bf16[16,8192]{1,0:T(8,128)(2,1)S(1)}, bf16[16,8192]{1,0:T(8,128)(2,1)S(1)}, u32[]{:S(2)}, u32[]{:S(2)}) %collective-permute-start.3) | collective-permute-done | bytes 262176 | tf_op jit(solution)/shard_map/ppermute | solution.py:405
  14.1 2.0 %collective-permute-start.5 = (bf16[16,8192]{1,0:T(8,128)(2,1)S(1)}, bf16[16,8192]{1,0:T(8,128)(2,1)S(1)}, u32[]{:S(2)}, u32[]{:S(2)}) collective-permute-start(bf16[16,8192]{1,0:T(8,128)(2,1)S(1)} %collective-permute-done.3.refs_3_.refs_4_.refs_5_), channel_id=1, source_target_pairs={{0,4},{1,3},{4,8},{5,1},{8,12},{9,5},{12,14},{13,9},{14,10},{15,13... | collective-permute-start | bytes 786440 | tf_op jit(solution)/shard_map/ppermute | solution.py:405
  16.1 0.0 collective-permute-start.9
  16.1 0.5 collective-permute-start.10
  16.6 1.1 %collective-permute-done.4.refs_4_.refs_5_.refs_6_ = bf16[16,8192]{1,0:T(8,128)(2,1)S(1)} collective-permute-done((bf16[16,8192]{1,0:T(8,128)(2,1)S(1)}, bf16[16,8192]{1,0:T(8,128)(2,1)S(1)}, u32[]{:S(2)}, u32[]{:S(2)}) %collective-permute-start.4) | collective-permute-done | bytes 262176 | tf_op jit(solution)/shard_map/ppermute | solution.py:405
  17.7 1.7 %collective-permute-start.6 = (bf16[16,8192]{1,0:T(8,128)(2,1)S(1)}, bf16[16,8192]{1,0:T(8,128)(2,1)S(1)}, u32[]{:S(2)}, u32[]{:S(2)}) collective-permute-start(bf16[16,8192]{1,0:T(8,128)(2,1)S(1)} %collective-permute-done.4.refs_4_.refs_5_.refs_6_), channel_id=1, source_target_pairs={{0,4},{1,3},{4,8},{5,1},{8,12},{9,5},{12,14},{13,9},{14,10},{15,13... | collective-permute-start | bytes 786440 | tf_op jit(solution)/shard_map/ppermute | solution.py:405
  19.4 1.1 %collective-permute-done.5.refs_5_.refs_6_.refs_7_ = bf16[16,8192]{1,0:T(8,128)(2,1)S(1)} collective-permute-done((bf16[16,8192]{1,0:T(8,128)(2,1)S(1)}, bf16[16,8192]{1,0:T(8,128)(2,1)S(1)}, u32[]{:S(2)}, u32[]{:S(2)}) %collective-permute-start.5) | collective-permute-done | bytes 262176 | tf_op jit(solution)/shard_map/ppermute | solution.py:405
  20.5 2.0 %collective-permute-start.7 = (bf16[16,8192]{1,0:T(8,128)(2,1)S(1)}, bf16[16,8192]{1,0:T(8,128)(2,1)S(1)}, u32[]{:S(2)}, u32[]{:S(2)}) collective-permute-start(bf16[16,8192]{1,0:T(8,128)(2,1)S(1)} %collective-permute-done.5.refs_5_.refs_6_.refs_7_), channel_id=1, source_target_pairs={{0,4},{1,3},{4,8},{5,1},{8,12},{9,5},{12,14},{13,9},{14,10},{15,13... | collective-permute-start | bytes 786440 | tf_op jit(solution)/shard_map/ppermute | solution.py:405
  22.5 0.0 collective-permute-start.11
  22.5 0.5 collective-permute-start.12
  23.0 1.0 %collective-permute-done.6.refs_6_.refs_7_.refs_8_ = bf16[16,8192]{1,0:T(8,128)(2,1)S(1)} collective-permute-done((bf16[16,8192]{1,0:T(8,128)(2,1)S(1)}, bf16[16,8192]{1,0:T(8,128)(2,1)S(1)}, u32[]{:S(2)}, u32[]{:S(2)}) %collective-permute-start.6) | collective-permute-done | bytes 262176 | tf_op jit(solution)/shard_map/ppermute | solution.py:405
  24.1 2.8 %collective-permute-done.7.refs_7_.refs_8_.refs_9_ = bf16[16,8192]{1,0:T(8,128)(2,1)S(1)} collective-permute-done((bf16[16,8192]{1,0:T(8,128)(2,1)S(1)}, bf16[16,8192]{1,0:T(8,128)(2,1)S(1)}, u32[]{:S(2)}, u32[]{:S(2)}) %collective-permute-start.7) | collective-permute-done | bytes 262176 | tf_op jit(solution)/shard_map/ppermute | solution.py:405
  26.9 1.2 %rank.1 = (bf16[16,256]{1,0:T(8,128)(2,1)S(1)}, bf16[2,128,896]{2,1,0:T(8,128)(2,1)S(1)}) custom-call(s32[1,2]{1,0:T(1,128)S(1)} %bitcast.7, bf16[8,128,896]{2,1,0:T(8,128)(2,1)} %expand_ref.1, bf16[8,8,8192]{2,1,0:T(8,128)(2,1)S(1)} %bitcast.6, bf16[8,8,8192]{2,1,0:T(8,128)(2,1)S(1)} %collective-permute-done.15.other_ref, ...), custom_call_target="tpu_custom_call" | custom-call | flops 67108864 | bytes 4194304 | tf_op jit(solution)/shard_map/rank/pallas_call | solution.py:182
  28.1 0.6 collective-permute-start.16
  28.7 1.9 %product.4 = (f32[256,768]{1,0:T(8,128)S(1)}, bf16[4096,128]{1,0:T(8,128)(2,1)S(1)}) custom-call(bf16[8192,896]{1,0:T(8,128)(2,1)S(1)} %copy-done.3, bf16[16,8192]{1,0:T(8,128)(2,1)S(1)} %get-tuple-element.30.refs_0_.refs_1_, bf16[16,8192]{1,0:T(8,128)(2,1)S(1)} %get-tuple-element.31.refs_1_.refs_2_, ...), custom_call_target="tpu_custom_call" | custom-call | flops 5637144576 | bytes 9437184 | tf_op jit(solution)/shard_map/product/pallas_call | solution.py:236
  30.7 0.0 slice-start.6
  30.7 3.1 %collective-permute-start.17 = (bf16[16,256]{1,0:T(8,128)(2,1)S(1)}, bf16[16,256]{1,0:T(8,128)(2,1)S(1)}, u32[]{:S(2)}, u32[]{:S(2)}) collective-permute-start(bf16[16,256]{1,0:T(8,128)(2,1)S(1)} %add.3), channel_id=1, source_target_pairs={{0,8},{1,9},{2,10},{3,11},{4,12},{5,13},{6,14},{7,15},{8,0},{9,1},... | collective-permute-start | bytes 24584 | tf_op jit(solution)/shard_map/ppermute | solution.py:408
  33.8 1.9 %product.5 = (f32[256,768]{1,0:T(8,128)S(1)}, bf16[4096,128]{1,0:T(8,128)(2,1)S(1)}) custom-call(bf16[8192,896]{1,0:T(8,128)(2,1)S(1)} %copy-done.3, bf16[16,8192]{1,0:T(8,128)(2,1)S(1)} %get-tuple-element.30.refs_0_.refs_1_, bf16[16,8192]{1,0:T(8,128)(2,1)S(1)} %get-tuple-element.31.refs_1_.refs_2_, ...), custom_call_target="tpu_custom_call" | custom-call | flops 5637144576 | bytes 9437184 | tf_op jit(solution)/shard_map/product/pallas_call | solution.py:236
  35.8 1.6 %collective-permute-start.18 = (bf16[32,256]{1,0:T(8,128)(2,1)S(1)}, bf16[32,256]{1,0:T(8,128)(2,1)S(1)}, u32[]{:S(2)}, u32[]{:S(2)}) collective-permute-start(bf16[32,256]{1,0:T(8,128)(2,1)S(1)} %pad_maximum_fusion.2), channel_id=1, source_target_pairs={{0,4},{1,5},{2,6},{3,7},{4,0},{5,1},{6,2},{7,3},{8,12},{9,13},{10,... | collective-permute-start | bytes 49160 | tf_op jit(solution)/shard_map/ppermute | solution.py:408
  37.4 0.0 slice-start
  37.4 0.0 slice-start.1
  37.4 2.3 %product.6 = (f32[256,768]{1,0:T(8,128)S(1)}, f32[256,256]{1,0:T(8,128)S(1)}) custom-call(bf16[8192,896]{1,0:T(8,128)(2,1)S(1)} %bitcast.10, bf16[4096,128]{1,0:T(8,128)(2,1)S(1)} %get-tuple-element.35.refs_0_, bf16[16,8192]{1,0:T(8,128)(2,1)S(1)} %get-tuple-element.30.refs_0_.refs_1_, bf16[16,8192]{1,0:T(8,128)(2,1)S(1)} %get-tuple-element.31.refs_1_.refs_2_, ...), custom_call_target="tpu_custom_call" | custom-call | flops 5637144576 | bytes 9437184 | tf_op jit(solution)/shard_map/product/pallas_call | solution.py:236
  39.8 1.6 %collective-permute-start.19 = (bf16[64,256]{1,0:T(8,128)(2,1)S(1)}, bf16[64,256]{1,0:T(8,128)(2,1)S(1)}, u32[]{:S(2)}, u32[]{:S(2)}) collective-permute-start(bf16[64,256]{1,0:T(8,128)(2,1)S(1)} %pad_maximum_fusion.1), channel_id=1, source_target_pairs={{0,2},{1,3},{2,0},{3,1},{4,6},{5,7},{6,4},{7,5},{8,10},{9,11},{10,... | collective-permute-start | bytes 98312 | tf_op jit(solution)/shard_map/ppermute | solution.py:408
  41.4 2.3 %product.7 = (f32[256,768]{1,0:T(8,128)S(1)}, f32[256,256]{1,0:T(8,128)S(1)}) custom-call(bf16[8192,896]{1,0:T(8,128)(2,1)S(1)} %bitcast.10, bf16[4096,128]{1,0:T(8,128)(2,1)S(1)} %get-tuple-element.37.refs_0_, bf16[16,8192]{1,0:T(8,128)(2,1)S(1)} %get-tuple-element.30.refs_0_.refs_1_, bf16[16,8192]{1,0:T(8,128)(2,1)S(1)} %get-tuple-element.31.refs_1_.refs_2_, ...), custom_call_target="tpu_custom_call" | custom-call | flops 5637144576 | bytes 9437184 | tf_op jit(solution)/shard_map/product/pallas_call | solution.py:236
  43.7 0.0 collective-permute-done.19
  43.8 0.8 %finish.1.hidden_ref = bf16[256,896]{1,0:T(8,128)(2,1)S(1)} custom-call(f32[256,768]{1,0:T(8,128)S(1)} %get-tuple-element.33.refs_0_, f32[256,768]{1,0:T(8,128)S(1)} %get-tuple-element.34.refs_1_, f32[256,768]{1,0:T(8,128)S(1)} %get-tuple-element.36.refs_2_, f32[256,768]{1,0:T(8,128)S(1)} %get-tuple-element.38.refs_3_, ...), custom_call_target="tpu_custom_call" | custom-call | tf_op jit(solution)/shard_map/finish/pallas_call | solution.py:291
  44.6 0.0 copy-start.2
  44.6 4.5 %down.1 = (bf16[16,8192]{1,0:T(8,128)(2,1)S(1)}, bf16[16,8192]{1,0:T(8,128)(2,1)S(1)}, bf16[16,8192]{1,0:T(8,128)(2,1)S(1)}, bf16[16,8192]{1,0:T(8,128)(2,1)S(1)...) custom-call(bf16[896,8192]{1,0:T(8,128)(2,1)S(1)} %bitcast.4, ...), custom_call_target="tpu_custom_call" | custom-call | flops 3758096384 | bytes 18874368 | tf_op jit(solution)/shard_map/down/pallas_call | solution.py:317
  49.2 0.1 collective-permute-start.20
  49.2 1.5 %collective-permute-done.20.after_ref.refs_1_ = bf16[16,8192]{1,0:T(8,128)(2,1)S(1)} collective-permute-done((bf16[16,8192]{1,0:T(8,128)(2,1)S(1)}, bf16[16,8192]{1,0:T(8,128)(2,1)S(1)}, u32[]{:S(2)}, u32[]{:S(2)}) %collective-permute-start.20) | collective-permute-done | bytes 262176 | tf_op jit(solution)/shard_map/ppermute | solution.py:408
  50.8 0.1 collective-permute-start.24
  50.9 0.4 collective-permute-start.23
  51.3 0.1 added.7
  51.3 1.3 %collective-permute-start.25 = (bf16[16,8192]{1,0:T(8,128)(2,1)S(1)}, bf16[16,8192]{1,0:T(8,128)(2,1)S(1)}, u32[]{:S(2)}, u32[]{:S(2)}) collective-permute-start(bf16[16,8192]{1,0:T(8,128)(2,1)S(1)} %added.7), channel_id=1, source_target_pairs={{0,4},{1,3},{4,8},{5,1},{8,12},{9,5},{12,14},{13,9},{14,10},{15,13... | collective-permute-start | bytes 786440 | tf_op jit(solution)/shard_map/ppermute | solution.py:405
  52.6 0.0 collective-permute-done.24.refs_1_
  52.7 0.1 added.11
  52.7 1.9 %collective-permute-start.29 = (bf16[16,8192]{1,0:T(8,128)(2,1)S(1)}, bf16[16,8192]{1,0:T(8,128)(2,1)S(1)}, u32[]{:S(2)}, u32[]{:S(2)}) collective-permute-start(bf16[16,8192]{1,0:T(8,128)(2,1)S(1)} %added.11), channel_id=1, source_target_pairs={{0,4},{1,3},{4,8},{5,1},{8,12},{9,5},{12,14},{13,9},{14,10},{15,13... | collective-permute-start | bytes 786440 | tf_op jit(solution)/shard_map/ppermute | solution.py:405
  54.6 3.2 %collective-permute-done.25.refs_2_ = bf16[16,8192]{1,0:T(8,128)(2,1)S(1)} collective-permute-done((bf16[16,8192]{1,0:T(8,128)(2,1)S(1)}, bf16[16,8192]{1,0:T(8,128)(2,1)S(1)}, u32[]{:S(2)}, u32[]{:S(2)}) %collective-permute-start.25) | collective-permute-done | bytes 262176 | tf_op jit(solution)/shard_map/ppermute | solution.py:405
  57.8 0.1 added.8
  57.9 1.3 %collective-permute-start.26 = (bf16[16,8192]{1,0:T(8,128)(2,1)S(1)}, bf16[16,8192]{1,0:T(8,128)(2,1)S(1)}, u32[]{:S(2)}, u32[]{:S(2)}) collective-permute-start(bf16[16,8192]{1,0:T(8,128)(2,1)S(1)} %added.8), channel_id=1, source_target_pairs={{0,4},{1,3},{4,8},{5,1},{8,12},{9,5},{12,14},{13,9},{14,10},{15,13... | collective-permute-start | bytes 786440 | tf_op jit(solution)/shard_map/ppermute | solution.py:405
  59.2 1.4 %collective-permute-done.29.refs_2_ = bf16[16,8192]{1,0:T(8,128)(2,1)S(1)} collective-permute-done((bf16[16,8192]{1,0:T(8,128)(2,1)S(1)}, bf16[16,8192]{1,0:T(8,128)(2,1)S(1)}, u32[]{:S(2)}, u32[]{:S(2)}) %collective-permute-start.29) | collective-permute-done | bytes 262176 | tf_op jit(solution)/shard_map/ppermute | solution.py:405
  60.6 0.1 added.12
  60.7 1.3 %collective-permute-start.30 = (bf16[16,8192]{1,0:T(8,128)(2,1)S(1)}, bf16[16,8192]{1,0:T(8,128)(2,1)S(1)}, u32[]{:S(2)}, u32[]{:S(2)}) collective-permute-start(bf16[16,8192]{1,0:T(8,128)(2,1)S(1)} %added.12), channel_id=1, source_target_pairs={{0,4},{1,3},{4,8},{5,1},{8,12},{9,5},{12,14},{13,9},{14,10},{15,13... | collective-permute-start | bytes 786440 | tf_op jit(solution)/shard_map/ppermute | solution.py:405
  62.0 2.3 %collective-permute-done.26.refs_2_ = bf16[16,8192]{1,0:T(8,128)(2,1)S(1)} collective-permute-done((bf16[16,8192]{1,0:T(8,128)(2,1)S(1)}, bf16[16,8192]{1,0:T(8,128)(2,1)S(1)}, u32[]{:S(2)}, u32[]{:S(2)}) %collective-permute-start.26) | collective-permute-done | bytes 262176 | tf_op jit(solution)/shard_map/ppermute | solution.py:405
  64.3 0.1 added.9
  64.4 1.3 %collective-permute-start.27 = (bf16[16,8192]{1,0:T(8,128)(2,1)S(1)}, bf16[16,8192]{1,0:T(8,128)(2,1)S(1)}, u32[]{:S(2)}, u32[]{:S(2)}) collective-permute-start(bf16[16,8192]{1,0:T(8,128)(2,1)S(1)} %added.9), channel_id=1, source_target_pairs={{0,4},{1,3},{4,8},{5,1},{8,12},{9,5},{12,14},{13,9},{14,10},{15,13... | collective-permute-start | bytes 786440 | tf_op jit(solution)/shard_map/ppermute | solution.py:405
  65.7 1.4 %collective-permute-done.30.refs_2_ = bf16[16,8192]{1,0:T(8,128)(2,1)S(1)} collective-permute-done((bf16[16,8192]{1,0:T(8,128)(2,1)S(1)}, bf16[16,8192]{1,0:T(8,128)(2,1)S(1)}, u32[]{:S(2)}, u32[]{:S(2)}) %collective-permute-start.30) | collective-permute-done | bytes 262176 | tf_op jit(solution)/shard_map/ppermute | solution.py:405
  67.1 0.1 added.13
  67.2 1.3 %collective-permute-start.31 = (bf16[16,8192]{1,0:T(8,128)(2,1)S(1)}, bf16[16,8192]{1,0:T(8,128)(2,1)S(1)}, u32[]{:S(2)}, u32[]{:S(2)}) collective-permute-start(bf16[16,8192]{1,0:T(8,128)(2,1)S(1)} %added.13), channel_id=1, source_target_pairs={{0,4},{1,3},{4,8},{5,1},{8,12},{9,5},{12,14},{13,9},{14,10},{15,13... | collective-permute-start | bytes 786440 | tf_op jit(solution)/shard_map/ppermute | solution.py:405
  68.5 2.3 %collective-permute-done.27.refs_2_ = bf16[16,8192]{1,0:T(8,128)(2,1)S(1)} collective-permute-done((bf16[16,8192]{1,0:T(8,128)(2,1)S(1)}, bf16[16,8192]{1,0:T(8,128)(2,1)S(1)}, u32[]{:S(2)}, u32[]{:S(2)}) %collective-permute-start.27) | collective-permute-done | bytes 262176 | tf_op jit(solution)/shard_map/ppermute | solution.py:405
  70.8 0.1 added.10
  70.9 1.3 %collective-permute-start.28 = (bf16[16,8192]{1,0:T(8,128)(2,1)S(1)}, bf16[16,8192]{1,0:T(8,128)(2,1)S(1)}, u32[]{:S(2)}, u32[]{:S(2)}) collective-permute-start(bf16[16,8192]{1,0:T(8,128)(2,1)S(1)} %added.10), channel_id=1, source_target_pairs={{0,4},{1,3},{4,8},{5,1},{8,12},{9,5},{12,14},{13,9},{14,10},{15,13... | collective-permute-start | bytes 786440 | tf_op jit(solution)/shard_map/ppermute | solution.py:405
  72.2 1.4 %collective-permute-done.31 = bf16[16,8192]{1,0:T(8,128)(2,1)S(1)} collective-permute-done((bf16[16,8192]{1,0:T(8,128)(2,1)S(1)}, bf16[16,8192]{1,0:T(8,128)(2,1)S(1)}, u32[]{:S(2)}, u32[]{:S(2)}) %collective-permute-start.31) | collective-permute-done | bytes 262176 | tf_op jit(solution)/shard_map/ppermute | solution.py:405
  73.6 3.7 %collective-permute-done.28.refs_2_ = bf16[16,8192]{1,0:T(8,128)(2,1)S(1)} collective-permute-done((bf16[16,8192]{1,0:T(8,128)(2,1)S(1)}, bf16[16,8192]{1,0:T(8,128)(2,1)S(1)}, u32[]{:S(2)}, u32[]{:S(2)}) %collective-permute-start.28) | collective-permute-done | bytes 262176 | tf_op jit(solution)/shard_map/ppermute | solution.py:405
  77.3 0.9 %last.1 = bf16[16,8192]{1,0:T(8,128)(2,1)} custom-call(s32[1,2]{1,0:T(1,128)S(1)} %bitcast.8, bf16[16,8192]{1,0:T(8,128)(2,1)S(1)} %get-tuple-element.42.refs_0_, bf16[16,8192]{1,0:T(8,128)(2,1)S(1)} %collective-permute-done.21.refs_1_, bf16[16,8192]{1,0:T(8,128)(2,1)S(1)} %collective-permute-done.28.refs_2_, ...), custom_call_target="tpu_custom_call" | custom-call | tf_op jit(solution)/shard_map/last/pallas_call | solution.py:355
  (52 shorter events, 0.1 us)
Async XLA Ops:
  0.0 6.6 %copy-start = (bf16[8,8192,8]{1,2,0:T(8,128)(2,1)S(1)}, bf16[8,8192,8]{1,2,0:T(8,128)(2,1)}, u32[]{:S(2)}) copy-start(bf16[8,8192,8]{1,2,0:T(8,128)(2,1)} %param.12) | copy-start | bytes 3145732
  0.0 26.9 %copy-start.1 = (s32[2]{0:T(128)S(1)}, s32[2]{0:T(128)}, u32[]{:S(2)}) copy-start(s32[2]{0:T(128)} %param.14) | copy-start | bytes 28
  0.0 28.7 %copy-start.3 = (bf16[8192,896]{1,0:T(8,128)(2,1)S(1)}, bf16[8192,896]{1,0:T(8,128)(2,1)}, u32[]{:S(2)}) copy-start(bf16[8192,896]{1,0:T(8,128)(2,1)} %w_ref.6) | copy-start | bytes 44040196
  0.0 3.2 %collective-permute-start = (bf16[16,8192]{1,0:T(8,128)(2,1)}, bf16[16,8192]{1,0:T(8,128)(2,1)S(1)}, u32[]{:S(2)}, u32[]{:S(2)}) collective-permute-start(bf16[16,8192]{1,0:T(8,128)(2,1)} %tokens_ref.1), channel_id=1, source_target_pairs={{0,1},{1,0},{2,3},{3,2},{4,5},{5,4},{6,7},{7,6},{8,9},{9,8},{10,11... | collective-permute-start | bytes 786440 | tf_op jit(solution)/shard_map/ppermute | solution.py:408
  0.5 7.1 %collective-permute-start.1 = (bf16[16,8192]{1,0:T(8,128)(2,1)}, bf16[16,8192]{1,0:T(8,128)(2,1)S(1)}, u32[]{:S(2)}, u32[]{:S(2)}) collective-permute-start(bf16[16,8192]{1,0:T(8,128)(2,1)} %tokens_ref.1), channel_id=1, source_target_pairs={{0,4},{1,3},{4,8},{5,1},{8,12},{9,5},{12,14},{13,9},{14,10},{15,13... | collective-permute-start | bytes 786440 | tf_op jit(solution)/shard_map/ppermute | solution.py:405
  4.9 6.4 %collective-permute-start.2 = (bf16[16,8192]{1,0:T(8,128)(2,1)S(1)}, bf16[16,8192]{1,0:T(8,128)(2,1)S(1)}, u32[]{:S(2)}, u32[]{:S(2)}) collective-permute-start(bf16[16,8192]{1,0:T(8,128)(2,1)S(1)} %get-tuple-element.31.refs_1_.refs_2_), channel_id=1, source_target_pairs={{0,4},{1,3},{4,8},{5,1},{8,12},{9,5},{12,14},{13,9},{14,10},{15,13... | collective-permute-start | bytes 786440 | tf_op jit(solution)/shard_map/ppermute | solution.py:405
  6.6 20.3 %collective-permute-start.15 = (bf16[8,8,8192]{2,1,0:T(8,128)(2,1)S(1)}, bf16[8,8,8192]{2,1,0:T(8,128)(2,1)S(1)}, u32[]{:S(2)}, u32[]{:S(2)}) collective-permute-start(bf16[8,8,8192]{2,1,0:T(8,128)(2,1)S(1)} %bitcast.5), channel_id=1, source_target_pairs={{0,1},{1,0},{2,3},{3,2},{4,5},{5,4},{6,7},{7,6},{8,9},{9,8},{10,11... | collective-permute-start | bytes 3145736 | tf_op jit(solution)/shard_map/ppermute | solution.py:408
  7.7 6.5 %collective-permute-start.3 = (bf16[16,8192]{1,0:T(8,128)(2,1)S(1)}, bf16[16,8192]{1,0:T(8,128)(2,1)S(1)}, u32[]{:S(2)}, u32[]{:S(2)}) collective-permute-start(bf16[16,8192]{1,0:T(8,128)(2,1)S(1)} %collective-permute-done.1.refs_1_.refs_2_.refs_3_), channel_id=1, source_target_pairs={{0,4},{1,3},{4,8},{5,1},{8,12},{9,5},{12,14},{13,9},{14,10},{15,13... | collective-permute-start | bytes 786440 | tf_op jit(solution)/shard_map/ppermute | solution.py:405
  9.7 6.4 %collective-permute-start.8 = (bf16[16,8192]{1,0:T(8,128)(2,1)S(1)}, bf16[16,8192]{1,0:T(8,128)(2,1)S(1)}, u32[]{:S(2)}, u32[]{:S(2)}) collective-permute-start(bf16[16,8192]{1,0:T(8,128)(2,1)S(1)} %collective-permute-done.1.refs_1_.refs_2_.refs_3_), channel_id=1, source_target_pairs={{0,1},{1,0},{2,3},{3,2},{4,5},{5,4},{6,7},{7,6},{8,9},{9,8},{10,11... | collective-permute-start | bytes 786440 | tf_op jit(solution)/shard_map/ppermute | solution.py:408
  11.3 6.4 %collective-permute-start.4 = (bf16[16,8192]{1,0:T(8,128)(2,1)S(1)}, bf16[16,8192]{1,0:T(8,128)(2,1)S(1)}, u32[]{:S(2)}, u32[]{:S(2)}) collective-permute-start(bf16[16,8192]{1,0:T(8,128)(2,1)S(1)} %collective-permute-done.2.refs_2_.refs_3_.refs_4_), channel_id=1, source_target_pairs={{0,4},{1,3},{4,8},{5,1},{8,12},{9,5},{12,14},{13,9},{14,10},{15,13... | collective-permute-start | bytes 786440 | tf_op jit(solution)/shard_map/ppermute | solution.py:405
  14.1 6.4 %collective-permute-start.5 = (bf16[16,8192]{1,0:T(8,128)(2,1)S(1)}, bf16[16,8192]{1,0:T(8,128)(2,1)S(1)}, u32[]{:S(2)}, u32[]{:S(2)}) collective-permute-start(bf16[16,8192]{1,0:T(8,128)(2,1)S(1)} %collective-permute-done.3.refs_3_.refs_4_.refs_5_), channel_id=1, source_target_pairs={{0,4},{1,3},{4,8},{5,1},{8,12},{9,5},{12,14},{13,9},{14,10},{15,13... | collective-permute-start | bytes 786440 | tf_op jit(solution)/shard_map/ppermute | solution.py:405
  16.1 6.4 %collective-permute-start.9 = (bf16[16,8192]{1,0:T(8,128)(2,1)S(1)}, bf16[16,8192]{1,0:T(8,128)(2,1)S(1)}, u32[]{:S(2)}, u32[]{:S(2)}) collective-permute-start(bf16[16,8192]{1,0:T(8,128)(2,1)S(1)} %collective-permute-done.2.refs_2_.refs_3_.refs_4_), channel_id=1, source_target_pairs={{0,1},{1,0},{2,3},{3,2},{4,5},{5,4},{6,7},{7,6},{8,9},{9,8},{10,11... | collective-permute-start | bytes 786440 | tf_op jit(solution)/shard_map/ppermute | solution.py:408
  16.1 6.4 %collective-permute-start.10 = (bf16[16,8192]{1,0:T(8,128)(2,1)S(1)}, bf16[16,8192]{1,0:T(8,128)(2,1)S(1)}, u32[]{:S(2)}, u32[]{:S(2)}) collective-permute-start(bf16[16,8192]{1,0:T(8,128)(2,1)S(1)} %collective-permute-done.3.refs_3_.refs_4_.refs_5_), channel_id=1, source_target_pairs={{0,1},{1,0},{2,3},{3,2},{4,5},{5,4},{6,7},{7,6},{8,9},{9,8},{10,11... | collective-permute-start | bytes 786440 | tf_op jit(solution)/shard_map/ppermute | solution.py:408
  17.7 6.4 %collective-permute-start.6 = (bf16[16,8192]{1,0:T(8,128)(2,1)S(1)}, bf16[16,8192]{1,0:T(8,128)(2,1)S(1)}, u32[]{:S(2)}, u32[]{:S(2)}) collective-permute-start(bf16[16,8192]{1,0:T(8,128)(2,1)S(1)} %collective-permute-done.4.refs_4_.refs_5_.refs_6_), channel_id=1, source_target_pairs={{0,4},{1,3},{4,8},{5,1},{8,12},{9,5},{12,14},{13,9},{14,10},{15,13... | collective-permute-start | bytes 786440 | tf_op jit(solution)/shard_map/ppermute | solution.py:405
  20.5 6.4 %collective-permute-start.7 = (bf16[16,8192]{1,0:T(8,128)(2,1)S(1)}, bf16[16,8192]{1,0:T(8,128)(2,1)S(1)}, u32[]{:S(2)}, u32[]{:S(2)}) collective-permute-start(bf16[16,8192]{1,0:T(8,128)(2,1)S(1)} %collective-permute-done.5.refs_5_.refs_6_.refs_7_), channel_id=1, source_target_pairs={{0,4},{1,3},{4,8},{5,1},{8,12},{9,5},{12,14},{13,9},{14,10},{15,13... | collective-permute-start | bytes 786440 | tf_op jit(solution)/shard_map/ppermute | solution.py:405
  22.5 4.4 %collective-permute-start.11 = (bf16[16,8192]{1,0:T(8,128)(2,1)S(1)}, bf16[16,8192]{1,0:T(8,128)(2,1)S(1)}, u32[]{:S(2)}, u32[]{:S(2)}) collective-permute-start(bf16[16,8192]{1,0:T(8,128)(2,1)S(1)} %collective-permute-done.4.refs_4_.refs_5_.refs_6_), channel_id=1, source_target_pairs={{0,1},{1,0},{2,3},{3,2},{4,5},{5,4},{6,7},{7,6},{8,9},{9,8},{10,11... | collective-permute-start | bytes 786440 | tf_op jit(solution)/shard_map/ppermute | solution.py:408
  22.5 4.4 %collective-permute-start.12 = (bf16[16,8192]{1,0:T(8,128)(2,1)S(1)}, bf16[16,8192]{1,0:T(8,128)(2,1)S(1)}, u32[]{:S(2)}, u32[]{:S(2)}) collective-permute-start(bf16[16,8192]{1,0:T(8,128)(2,1)S(1)} %collective-permute-done.5.refs_5_.refs_6_.refs_7_), channel_id=1, source_target_pairs={{0,1},{1,0},{2,3},{3,2},{4,5},{5,4},{6,7},{7,6},{8,9},{9,8},{10,11... | collective-permute-start | bytes 786440 | tf_op jit(solution)/shard_map/ppermute | solution.py:408
  24.1 2.8 %collective-permute-start.13 = (bf16[16,8192]{1,0:T(8,128)(2,1)S(1)}, bf16[16,8192]{1,0:T(8,128)(2,1)S(1)}, u32[]{:S(2)}, u32[]{:S(2)}) collective-permute-start(bf16[16,8192]{1,0:T(8,128)(2,1)S(1)} %collective-permute-done.6.refs_6_.refs_7_.refs_8_), channel_id=1, source_target_pairs={{0,1},{1,0},{2,3},{3,2},{4,5},{5,4},{6,7},{7,6},{8,9},{9,8},{10,11... | collective-permute-start | bytes 786440 | tf_op jit(solution)/shard_map/ppermute | solution.py:408
  26.9 1.8 %collective-permute-start.14 = (bf16[16,8192]{1,0:T(8,128)(2,1)S(1)}, bf16[16,8192]{1,0:T(8,128)(2,1)S(1)}, u32[]{:S(2)}, u32[]{:S(2)}) collective-permute-start(bf16[16,8192]{1,0:T(8,128)(2,1)S(1)} %collective-permute-done.7.refs_7_.refs_8_.refs_9_), channel_id=1, source_target_pairs={{0,1},{1,0},{2,3},{3,2},{4,5},{5,4},{6,7},{7,6},{8,9},{9,8},{10,11... | collective-permute-start | bytes 786440 | tf_op jit(solution)/shard_map/ppermute | solution.py:408
  28.1 2.5 %collective-permute-start.16 = (bf16[16,256]{1,0:T(8,128)(2,1)S(1)}, bf16[16,256]{1,0:T(8,128)(2,1)S(1)}, u32[]{:S(2)}, u32[]{:S(2)}) collective-permute-start(bf16[16,256]{1,0:T(8,128)(2,1)S(1)} %get-tuple-element.32.refs_16_), channel_id=1, source_target_pairs={{0,1},{1,0},{2,3},{3,2},{4,5},{5,4},{6,7},{7,6},{8,9},{9,8},{10,11... | collective-permute-start | bytes 24584 | tf_op jit(solution)/shard_map/ppermute | solution.py:408
  28.7 8.7 %slice-start.4 = ((s8[14680064]{0:T(1024)(128)(4,1)}), s8[4194304]{0:T(1024)(128)(4,1)S(1)}, s32[]{:S(2)}) async-start(s8[14680064]{0:T(1024)(128)(4,1)} %bitcast.9), calls=%async_computation.4 | async-start | bytes 8388608
  28.7 8.7 %slice-start.5 = ((s8[14680064]{0:T(1024)(128)(4,1)}), s8[4194304]{0:T(1024)(128)(4,1)S(1)}, s32[]{:S(2)}) async-start(s8[14680064]{0:T(1024)(128)(4,1)} %bitcast.9), calls=%async_computation.5 | async-start | bytes 8388608
  30.7 6.7 %slice-start.6 = ((s8[14680064]{0:T(1024)(128)(4,1)}), s8[4194304]{0:T(1024)(128)(4,1)S(1)}, s32[]{:S(2)}) async-start(s8[14680064]{0:T(1024)(128)(4,1)} %bitcast.9), calls=%async_computation.6 | async-start | bytes 8388608
  30.7 6.7 %slice-start.7 = ((s8[14680064]{0:T(1024)(128)(4,1)}), s8[2097152]{0:T(1024)(128)(4,1)S(1)}, s32[]{:S(2)}) async-start(s8[14680064]{0:T(1024)(128)(4,1)} %bitcast.9), calls=%async_computation.7 | async-start | bytes 4194304
  30.7 5.0 %collective-permute-start.17 = (bf16[16,256]{1,0:T(8,128)(2,1)S(1)}, bf16[16,256]{1,0:T(8,128)(2,1)S(1)}, u32[]{:S(2)}, u32[]{:S(2)}) collective-permute-start(bf16[16,256]{1,0:T(8,128)(2,1)S(1)} %add.3), channel_id=1, source_target_pairs={{0,8},{1,9},{2,10},{3,11},{4,12},{5,13},{6,14},{7,15},{8,0},{9,1},... | collective-permute-start | bytes 24584 | tf_op jit(solution)/shard_map/ppermute | solution.py:408
  35.8 4.0 %collective-permute-start.18 = (bf16[32,256]{1,0:T(8,128)(2,1)S(1)}, bf16[32,256]{1,0:T(8,128)(2,1)S(1)}, u32[]{:S(2)}, u32[]{:S(2)}) collective-permute-start(bf16[32,256]{1,0:T(8,128)(2,1)S(1)} %pad_maximum_fusion.2), channel_id=1, source_target_pairs={{0,4},{1,5},{2,6},{3,7},{4,0},{5,1},{6,2},{7,3},{8,12},{9,13},{10,... | collective-permute-start | bytes 49160 | tf_op jit(solution)/shard_map/ppermute | solution.py:408
  37.4 7.2 %slice-start = ((s8[14680064]{0:T(1024)(128)(4,1)}), s8[4194304]{0:T(1024)(128)(4,1)S(1)}, s32[]{:S(2)}) async-start(s8[14680064]{0:T(1024)(128)(4,1)} %bitcast.3), calls=%async_computation | async-start | bytes 8388608
  37.4 7.2 %slice-start.1 = ((s8[14680064]{0:T(1024)(128)(4,1)}), s8[4194304]{0:T(1024)(128)(4,1)S(1)}, s32[]{:S(2)}) async-start(s8[14680064]{0:T(1024)(128)(4,1)} %bitcast.3), calls=%async_computation.1 | async-start | bytes 8388608
  39.8 4.0 %collective-permute-start.19 = (bf16[64,256]{1,0:T(8,128)(2,1)S(1)}, bf16[64,256]{1,0:T(8,128)(2,1)S(1)}, u32[]{:S(2)}, u32[]{:S(2)}) collective-permute-start(bf16[64,256]{1,0:T(8,128)(2,1)S(1)} %pad_maximum_fusion.1), channel_id=1, source_target_pairs={{0,2},{1,3},{2,0},{3,1},{4,6},{5,7},{6,4},{7,5},{8,10},{9,11},{10,... | collective-permute-start | bytes 98312 | tf_op jit(solution)/shard_map/ppermute | solution.py:408
  41.4 3.2 %slice-start.2 = ((s8[14680064]{0:T(1024)(128)(4,1)}), s8[4194304]{0:T(1024)(128)(4,1)S(1)}, s32[]{:S(2)}) async-start(s8[14680064]{0:T(1024)(128)(4,1)} %bitcast.3), calls=%async_computation.2 | async-start | bytes 8388608
  41.4 3.2 %slice-start.3 = ((s8[14680064]{0:T(1024)(128)(4,1)}), s8[2097152]{0:T(1024)(128)(4,1)S(1)}, s32[]{:S(2)}) async-start(s8[14680064]{0:T(1024)(128)(4,1)} %bitcast.3), calls=%async_computation.3 | async-start | bytes 4194304
  44.6 32.7 %copy-start.2 = (s32[2]{0:T(128)S(1)}, s32[2]{0:T(128)}, u32[]{:S(2)}) copy-start(s32[2]{0:T(128)} %param.15) | copy-start | bytes 28
  49.2 1.6 %collective-permute-start.20 = (bf16[16,8192]{1,0:T(8,128)(2,1)S(1)}, bf16[16,8192]{1,0:T(8,128)(2,1)S(1)}, u32[]{:S(2)}, u32[]{:S(2)}) collective-permute-start(bf16[16,8192]{1,0:T(8,128)(2,1)S(1)} %get-tuple-element.44), channel_id=1, source_target_pairs={{0,1},{1,0},{2,3},{3,2},{4,5},{5,4},{6,7},{7,6},{8,9},{9,8},{10,11... | collective-permute-start | bytes 786440 | tf_op jit(solution)/shard_map/ppermute | solution.py:408
  50.8 1.9 %collective-permute-start.24 = (bf16[32,8192]{1,0:T(8,128)(2,1)S(1)}, bf16[32,8192]{1,0:T(8,128)(2,1)S(1)}, u32[]{:S(2)}, u32[]{:S(2)}) collective-permute-start(bf16[32,8192]{1,0:T(8,128)(2,1)S(1)} %tie.7), channel_id=1, source_target_pairs={{0,1},{1,0},{2,3},{3,2},{4,5},{5,4},{6,7},{7,6},{8,9},{9,8},{10,11... | collective-permute-start | bytes 1572872 | tf_op jit(solution)/shard_map/ppermute | solution.py:408
  50.9 8.3 %collective-permute-start.23 = (bf16[32,8192]{1,0:T(8,128)(2,1)S(1)}, bf16[32,8192]{1,0:T(8,128)(2,1)S(1)}, u32[]{:S(2)}, u32[]{:S(2)}) collective-permute-start(bf16[32,8192]{1,0:T(8,128)(2,1)S(1)} %tie.6), channel_id=1, source_target_pairs={{0,1},{1,0},{2,3},{3,2},{4,5},{5,4},{6,7},{7,6},{8,9},{9,8},{10,11... | collective-permute-start | bytes 1572872 | tf_op jit(solution)/shard_map/ppermute | solution.py:408
  51.3 6.4 %collective-permute-start.25 = (bf16[16,8192]{1,0:T(8,128)(2,1)S(1)}, bf16[16,8192]{1,0:T(8,128)(2,1)S(1)}, u32[]{:S(2)}, u32[]{:S(2)}) collective-permute-start(bf16[16,8192]{1,0:T(8,128)(2,1)S(1)} %added.7), channel_id=1, source_target_pairs={{0,4},{1,3},{4,8},{5,1},{8,12},{9,5},{12,14},{13,9},{14,10},{15,13... | collective-permute-start | bytes 786440 | tf_op jit(solution)/shard_map/ppermute | solution.py:405
  52.7 7.8 %collective-permute-start.29 = (bf16[16,8192]{1,0:T(8,128)(2,1)S(1)}, bf16[16,8192]{1,0:T(8,128)(2,1)S(1)}, u32[]{:S(2)}, u32[]{:S(2)}) collective-permute-start(bf16[16,8192]{1,0:T(8,128)(2,1)S(1)} %added.11), channel_id=1, source_target_pairs={{0,4},{1,3},{4,8},{5,1},{8,12},{9,5},{12,14},{13,9},{14,10},{15,13... | collective-permute-start | bytes 786440 | tf_op jit(solution)/shard_map/ppermute | solution.py:405
  54.6 11.1 %collective-permute-start.22 = (bf16[32,8192]{1,0:T(8,128)(2,1)S(1)}, bf16[32,8192]{1,0:T(8,128)(2,1)S(1)}, u32[]{:S(2)}, u32[]{:S(2)}) collective-permute-start(bf16[32,8192]{1,0:T(8,128)(2,1)S(1)} %tie.5), channel_id=1, source_target_pairs={{0,1},{1,0},{2,3},{3,2},{4,5},{5,4},{6,7},{7,6},{8,9},{9,8},{10,11... | collective-permute-start | bytes 1572872 | tf_op jit(solution)/shard_map/ppermute | solution.py:408
  57.9 6.4 %collective-permute-start.26 = (bf16[16,8192]{1,0:T(8,128)(2,1)S(1)}, bf16[16,8192]{1,0:T(8,128)(2,1)S(1)}, u32[]{:S(2)}, u32[]{:S(2)}) collective-permute-start(bf16[16,8192]{1,0:T(8,128)(2,1)S(1)} %added.8), channel_id=1, source_target_pairs={{0,4},{1,3},{4,8},{5,1},{8,12},{9,5},{12,14},{13,9},{14,10},{15,13... | collective-permute-start | bytes 786440 | tf_op jit(solution)/shard_map/ppermute | solution.py:405
  60.7 6.4 %collective-permute-start.30 = (bf16[16,8192]{1,0:T(8,128)(2,1)S(1)}, bf16[16,8192]{1,0:T(8,128)(2,1)S(1)}, u32[]{:S(2)}, u32[]{:S(2)}) collective-permute-start(bf16[16,8192]{1,0:T(8,128)(2,1)S(1)} %added.12), channel_id=1, source_target_pairs={{0,4},{1,3},{4,8},{5,1},{8,12},{9,5},{12,14},{13,9},{14,10},{15,13... | collective-permute-start | bytes 786440 | tf_op jit(solution)/shard_map/ppermute | solution.py:405
  64.4 6.4 %collective-permute-start.27 = (bf16[16,8192]{1,0:T(8,128)(2,1)S(1)}, bf16[16,8192]{1,0:T(8,128)(2,1)S(1)}, u32[]{:S(2)}, u32[]{:S(2)}) collective-permute-start(bf16[16,8192]{1,0:T(8,128)(2,1)S(1)} %added.9), channel_id=1, source_target_pairs={{0,4},{1,3},{4,8},{5,1},{8,12},{9,5},{12,14},{13,9},{14,10},{15,13... | collective-permute-start | bytes 786440 | tf_op jit(solution)/shard_map/ppermute | solution.py:405
  67.2 6.4 %collective-permute-start.31 = (bf16[16,8192]{1,0:T(8,128)(2,1)S(1)}, bf16[16,8192]{1,0:T(8,128)(2,1)S(1)}, u32[]{:S(2)}, u32[]{:S(2)}) collective-permute-start(bf16[16,8192]{1,0:T(8,128)(2,1)S(1)} %added.13), channel_id=1, source_target_pairs={{0,4},{1,3},{4,8},{5,1},{8,12},{9,5},{12,14},{13,9},{14,10},{15,13... | collective-permute-start | bytes 786440 | tf_op jit(solution)/shard_map/ppermute | solution.py:405
  68.5 5.1 %collective-permute-start.21 = (bf16[16,8192]{1,0:T(8,128)(2,1)S(1)}, bf16[16,8192]{1,0:T(8,128)(2,1)S(1)}, u32[]{:S(2)}, u32[]{:S(2)}) collective-permute-start(bf16[16,8192]{1,0:T(8,128)(2,1)S(1)} %tie.4), channel_id=1, source_target_pairs={{0,1},{1,0},{2,3},{3,2},{4,5},{5,4},{6,7},{7,6},{8,9},{9,8},{10,11... | collective-permute-start | bytes 786440 | tf_op jit(solution)/shard_map/ppermute | solution.py:408
  70.9 6.4 %collective-permute-start.28 = (bf16[16,8192]{1,0:T(8,128)(2,1)S(1)}, bf16[16,8192]{1,0:T(8,128)(2,1)S(1)}, u32[]{:S(2)}, u32[]{:S(2)}) collective-permute-start(bf16[16,8192]{1,0:T(8,128)(2,1)S(1)} %added.10), channel_id=1, source_target_pairs={{0,4},{1,3},{4,8},{5,1},{8,12},{9,5},{12,14},{13,9},{14,10},{15,13... | collective-permute-start | bytes 786440 | tf_op jit(solution)/shard_map/ppermute | solution.py:405
  73.6 3.7 %collective-permute-start.32 = (bf16[16,8192]{1,0:T(8,128)(2,1)S(1)}, bf16[16,8192]{1,0:T(8,128)(2,1)S(1)}, u32[]{:S(2)}, u32[]{:S(2)}) collective-permute-start(bf16[16,8192]{1,0:T(8,128)(2,1)S(1)} %collective-permute-done.31), channel_id=1, source_target_pairs={{0,1},{1,0},{2,3},{3,2},{4,5},{5,4},{6,7},{7,6},{8,9},{9,8},{10,11... | collective-permute-start | bytes 786440 | tf_op jit(solution)/shard_map/ppermute | solution.py:408
